TPU v7x, 32 devices: a whole 2x2x4 slice. The times are simulated.
32 devices in a mesh: fsdp: 8 (over z, x), seq: 4 (over y, core).
Axes of the slice: x: 2, y: 2, z: 4, core: 2. Of those that a mesh axis runs over, the one named last changes fastest.
Arguments:
- tokens: bfloat16 [8, 512, 3584], P('fsdp', 'seq'), may hold values from -6 to 6
- queries: bfloat16 [8, 512, 3584], P('fsdp', 'seq'), may hold values from -21 to 21
- cotangent: bfloat16 [8, 512, 3584], P('fsdp', 'seq'), may hold values from -6 to 6
- modality: int32 [8, 512], P('fsdp', 'seq'), may hold values from 0 to 1, as said below
- block_ids: int32 [8, 512], P('fsdp', 'seq'), may hold values from 0 to 511, as said below
- kv_weight: bfloat16 [2, 3584, 1024], P(None, 'fsdp', 'seq'), may hold values from -0.09375 to 0.09375
Outputs:
- attended: bfloat16 [8, 512, 3584], P('fsdp', 'seq')
- grad_queries: bfloat16 [8, 512, 3584], P('fsdp', 'seq')
- grad_tokens: bfloat16 [8, 512, 3584], P('fsdp', 'seq')
- grad_kv_weight: float32 [2, 3584, 1024], P(None, 'fsdp', 'seq')
Inputs may be any that keep to these rules, and one draw needn't show every extreme that they name: `modality`: the first 32 tokens of a sequence are text; video tokens come in whole frames of 32 tokens starting at multiples of 32. `block_ids`: a text token's id is its position in its sequence; a video token's id is the position of the last token of its frame.
All inputs are finite; a program needn't handle non-finite values.
Results may differ from a plain program's by a relative error of at most 0.015.
The roundings to bfloat16 on the way count: a program that leaves them out, or rounds other values in their place, can miss the bound.
Values may be sent and summed in bfloat16 or wider, within the bound.
No kernel may reach another device: no remote copies, remote signals or barrier semaphores. Data moves between devices by JAX's collectives and lax.ppermute only.
A program may use at most 128 MiB of HBM per device.

v0:
```python
import jax
import jax.numpy as jnp
from jax import lax
from jax.sharding import PartitionSpec as P

HEAD_DIM = 128
GROUP = 7


def attend(query_rows, key_value, query_blocks, key_blocks):
    count = query_rows.shape[0]
    length = key_value.shape[0]
    groups = key_value.shape[1] // (2 * HEAD_DIM)
    split_kv = key_value.reshape(length, groups, 2, HEAD_DIM)
    keys = split_kv[:, :, 0]
    values = split_kv[:, :, 1]
    heads = query_rows.reshape(count, groups, GROUP, HEAD_DIM)
    scores = jnp.einsum("rgjd,lgd->gjrl", heads, keys) * HEAD_DIM ** (-0.5)
    visible = key_blocks[None, :] <= query_blocks[:, None]
    scores = jnp.where(visible, scores, -1e30)
    top = jnp.max(scores, axis=-1, keepdims=True)
    expo = jnp.exp(scores - top)
    probs = expo / jnp.sum(expo, axis=-1, keepdims=True)
    rounded = lax.optimization_barrier(probs.astype(jnp.bfloat16)).astype(jnp.float32)
    result = jnp.einsum("gjrl,lgd->rgjd", rounded, values)
    return result.reshape(count, groups * GROUP * HEAD_DIM)


def per_device(tokens, queries, cotangent, modality, block_ids, kv_weight):
    gathered, whole_modal, whole_blocks = (
        lax.all_gather(tokens, "seq", axis=1, tiled=True),
        lax.all_gather(modality, "seq", axis=1, tiled=True),
        lax.all_gather(block_ids, "seq", axis=1, tiled=True),
    )
    hidden = gathered[0]
    modal_all = whole_modal[0]
    blocks_all = whole_blocks[0]
    weight = lax.all_gather(kv_weight, "fsdp", axis=1, tiled=True)
    text_part = jnp.dot(hidden, weight[0], preferred_element_type=jnp.float32)
    video_part = jnp.dot(hidden, weight[1], preferred_element_type=jnp.float32)
    key_value = jnp.where(modal_all[:, None] == 1, video_part, text_part).astype(jnp.bfloat16)
    kv_float = lax.optimization_barrier(key_value).astype(jnp.float32)
    head_query, head_upstream = (
        lax.all_to_all(queries[0], "seq", split_axis=1, concat_axis=0, tiled=True),
        lax.all_to_all(cotangent[0], "seq", split_axis=1, concat_axis=0, tiled=True),
    )

    def head_attend(query_float, kv_in):
        return attend(query_float, kv_in, blocks_all, blocks_all)

    result, pullback = jax.vjp(head_attend, head_query.astype(jnp.float32), kv_float)
    grad_head, grad_kv = pullback(head_upstream.astype(jnp.float32))
    attended, grad_query = (
        lax.all_to_all(result.astype(jnp.bfloat16), "seq", split_axis=0, concat_axis=1, tiled=True),
        lax.all_to_all(
            grad_head.astype(jnp.bfloat16), "seq", split_axis=0, concat_axis=1, tiled=True
        ),
    )
    grad_kv_b = grad_kv.astype(jnp.bfloat16)
    zeros = jnp.zeros_like(grad_kv_b)
    text_grad = jnp.where(modal_all[:, None] == 0, grad_kv_b, zeros)
    video_grad = jnp.where(modal_all[:, None] == 1, grad_kv_b, zeros)
    weight_term = jnp.stack(
        [
            jnp.einsum("ld,lc->dc", hidden, text_grad, preferred_element_type=jnp.float32),
            jnp.einsum("ld,lc->dc", hidden, video_grad, preferred_element_type=jnp.float32),
        ]
    )
    grad_weight = lax.psum_scatter(weight_term, "fsdp", scatter_dimension=1, tiled=True)
    grad_hidden = lax.psum_scatter(
        jnp.einsum("rc,dc->rd", text_grad, weight[0], preferred_element_type=jnp.float32)
        + jnp.einsum("rc,dc->rd", video_grad, weight[1], preferred_element_type=jnp.float32),
        "seq",
        scatter_dimension=0,
        tiled=True,
    )
    return (attended[None], grad_query[None], grad_hidden.astype(jnp.bfloat16)[None], grad_weight)


def solution(mesh):
    placed = (
        P("fsdp", "seq", None),
        P("fsdp", "seq", None),
        P("fsdp", "seq", None),
        P("fsdp", "seq"),
        P("fsdp", "seq"),
        P(None, "fsdp", "seq"),
    )
    return jax.shard_map(
        per_device,
        mesh=mesh,
        in_specs=placed,
        out_specs=(
            P("fsdp", "seq", None),
            P("fsdp", "seq", None),
            P("fsdp", "seq", None),
            P(None, "fsdp", "seq"),
        ),
        check_vma=False,
    )
```

profile of v0, /device:TPU:0, one launch (start us, length us, event | category | flops | bytes accessed | tf_op | source)
XLA Modules:
  0.0 487.7 jit_solution(4097683201329522287)
XLA Ops:
  8.7 2.2 copy.48
  10.9 4.2 all-to-all-start
  15.1 2.2 copy.53
  17.3 17.0 %all-to-all-done = bf16[128,4,896]{0,2,1:T(8,128)(2,1)S(1)} async-done(((bf16[128,4,896]{0,2,1:T(8,128)(2,1)}), bf16[128,4,896]{0,2,1:T(8,128)(2,1)S(1)}, u32[]{:S(2)}, u32[]{:S(2)}) %all-to-all-start) | async-done | bytes 917536 | tf_op jit(solution)/shard_map/all_to_all | solution.py:44
  34.4 3.5 all-to-all-start.2
  37.9 20.6 %all_gather.12 = s32[1,512]{1,0:T(1,128)S(1)} all-gather(s32[1,128]{1,0:T(1,128)S(1)} %copy-done.9), channel_id=1, replica_groups=mesh['fsdp'=8,'seq'=4] {'seq'}, dimensions={1}, use_global_device_ids=true | all-gather | bytes 2560 | tf_op jit(solution)/shard_map/all_gather | solution.py:32
  58.6 5.0 %all_gather.15 = s32[1,512]{1,0:T(1,128)S(1)} all-gather(s32[1,128]{1,0:T(1,128)S(1)} %copy-done.10), channel_id=1, replica_groups=mesh['fsdp'=8,'seq'=4] {'seq'}, dimensions={1}, use_global_device_ids=true | all-gather | bytes 2560 | tf_op jit(solution)/shard_map/all_gather | solution.py:33
  63.8 1.6 copy.49
  65.5 1.8 reshape.179
  67.3 1.6 copy.54
  68.9 1.7 reshape.181
  70.7 54.7 %all-gather.5.cloned.1.call-done = bf16[2,3584,256]{2,1,0:T(8,128)(2,1)} async-done(((bf16[2,448,256]{2,1,0:T(8,128)(2,1)}), bf16[2,3584,256]{2,1,0:T(8,128)(2,1)}) %all-gather.5.cloned.1.call-update) | async-done | bytes 3670032 | tf_op jit(solution)/shard_map/all_gather | solution.py:38
  125.3 3.9 fusion.16
  129.2 0.9 copy-done.5
  130.1 1.1 fusion.42
  131.7 1.4 fusion.9
  133.1 2.9 copy-done
  136.0 1.6 fusion.28
  137.7 1.1 convert_bitcast_fusion
  138.9 5.9 %convert_reduce_fusion = (f32[7,512]{1,0:T(8,128)S(1)}, pred[1,7,512,512]{2,3,1,0:T(32,128)(4,1)S(1)}, f32[7,512]{1,0:T(8,128)S(1)}) fusion(f32[7,512]{1,0:T(8,128)S(1)} %get-tuple-element.32, f32[512,512,7]{1,0,2:T(8,128)} %copy-done, pred[512,512]{0,1:T(8,128)(4,1)S(1)} %broadcast_compare_fusion, f32[7,512]{1,0:T(8,128)S(1)} %multiply_divide_fusion, ...), kind=kLoop, calls=%fused_computation.13 | loop fusion | flops 18342912 | bytes 13164544 | tf_op jit(solution)/shard_map/jvp()/reduce_sum | solution.py:21
  144.9 3.2 fusion.60
  148.1 1.3 fusion.45
  149.4 2.3 fusion.48
  151.7 1.2 copy-done.4
  153.0 1.0 copy-done.2
  154.0 1.1 convolution_bitcast_fusion
  155.1 1.1 convolution_bitcast_fusion.1
  156.2 3.4 pad_maximum_fusion
  159.6 11.7 %copy.60 = f32[2,3584,256]{2,0,1:T(2,128)} copy(f32[2,3584,256]{1,2,0:T(8,128)} %pad_maximum_fusion) | data formatting | bytes 14680064 | tf_op jit(solution)/shard_map/stack | solution.py:63
  171.4 2.8 fusion.29
  174.2 4.2 convolution_add_fusion
  178.5 1.5 copy-done.8
  179.9 6.7 %fusion.33 = bf16[512,7,128]{2,0,1:T(8,128)(2,1)} fusion(f32[1,7,512,512]{2,3,1,0:T(8,128)} %copy-done.4, pred[1,7,512,512]{2,3,1,0:T(32,128)(4,1)S(1)} %copy-done.8, f32[7,512]{1,0:T(8,128)S(1)} %negate_divide_fusion, pred[512,512]{0,1:T(8,128)(4,1)S(1)} %broadcast_compare_fusion, bf16[512,1,1,128]{3,2,0,1:T(2,128)(2,1)S(1)} %get-tuple-element.31), kind=kOutput, calls=%fused_computation.45 | convolution fusion | flops 477560832 | bytes 10500096 | tf_op jit(solution)/shard_map/transpose(jvp(rgjd,lgd->gjrl))/dot_general | solution.py:18
  186.6 1.5 copy.57
  188.3 1.0 copy.58
  189.3 3.5 all-to-all-start.3
  192.9 2.7 fusion.36
  195.8 1.0 copy.52
  196.9 9.0 %all-to-all-done.3 = bf16[4,128,896]{1,2,0:T(8,128)(2,1)S(1)} async-done(((bf16[4,128,896]{1,2,0:T(8,128)(2,1)}), bf16[4,128,896]{1,2,0:T(8,128)(2,1)S(1)}, u32[]{:S(2)}, u32[]{:S(2)}) %all-to-all-start.3) | async-done | bytes 917536 | tf_op jit(solution)/shard_map/all_to_all | solution.py:55
  205.9 3.5 all-to-all-start.1
  210.7 1.3 copy.62
  211.9 10.5 %all-to-all-done.1 = bf16[4,128,896]{1,2,0:T(8,128)(2,1)S(1)} async-done(((bf16[4,128,896]{1,2,0:T(8,128)(2,1)}), bf16[4,128,896]{1,2,0:T(8,128)(2,1)S(1)}, u32[]{:S(2)}, u32[]{:S(2)}) %all-to-all-start.1) | async-done | bytes 917536 | tf_op jit(solution)/shard_map/all_to_all | solution.py:54
  222.4 1.3 copy.61
  223.7 187.8 %all-reduce.5.cloned.1.call-done = f32[2,3584,256]{2,0,1:T(2,128)} async-done(((f32[2,3584,256]{2,0,1:T(2,128)}), f32[2,3584,256]{2,0,1:T(2,128)}) %all-reduce.5.cloned.1.call-update) | async-done | bytes 7340048
  411.5 1.5 constant_dynamic-slice_fusion
  413.0 1.0 copy.63
  414.0 64.6 %reduce-scatter.2.cloned.1.call-done = f32[128,3584]{1,0:T(8,128)} async-done(((f32[512,3584]{1,0:T(8,128)}), f32[128,3584]{1,0:T(8,128)}) %reduce-scatter.2.cloned.1.call-update) | async-done | bytes 1835024 | tf_op jit(solution)/shard_map/reduce_scatter | solution.py:70
  478.7 2.5 convert_bitcast_fusion.1
  (46 shorter events, 3.5 us)
Async XLA Ops:
  7.2 30.8 %copy-start.9 = (s32[1,128]{1,0:T(1,128)S(1)}, s32[1,128]{1,0:T(1,128)}, u32[]{:S(2)}) copy-start(s32[1,128]{1,0:T(1,128)} %param.9) | copy-start | bytes 1540
  7.2 51.4 %copy-start.10 = (s32[1,128]{1,0:T(1,128)S(1)}, s32[1,128]{1,0:T(1,128)}, u32[]{:S(2)}) copy-start(s32[1,128]{1,0:T(1,128)} %param.10) | copy-start | bytes 1540
  7.2 63.5 %all-gather.3.cloned.1.call-start = ((), (), s32[]{:S(2)}) async-start(), calls=%async_computation.5 | async-start | bytes 4587520 | tf_op jit(solution)/shard_map/all_gather | solution.py:31
  7.9 117.4 %all-gather.5.cloned.1.call-start = ((), (), s32[]{:S(2)}) async-start(), calls=%async_computation.6 | async-start | bytes 4128768 | tf_op jit(solution)/shard_map/all_gather | solution.py:38
  10.9 23.5 %all-to-all-start = ((bf16[128,4,896]{0,2,1:T(8,128)(2,1)}), bf16[128,4,896]{0,2,1:T(8,128)(2,1)S(1)}, u32[]{:S(2)}, u32[]{:S(2)}) async-start(bf16[128,4,896]{0,2,1:T(8,128)(2,1)} %bitcast.8), calls=%async_computation | async-start | bytes 1835008 | tf_op jit(solution)/shard_map/all_to_all | solution.py:44
  34.4 32.9 %all-to-all-start.2 = ((bf16[128,4,896]{0,2,1:T(8,128)(2,1)}), bf16[128,4,896]{0,2,1:T(8,128)(2,1)S(1)}, u32[]{:S(2)}, u32[]{:S(2)}) async-start(bf16[128,4,896]{0,2,1:T(8,128)(2,1)} %bitcast.18), calls=%async_computation.2 | async-start | bytes 1835008 | tf_op jit(solution)/shard_map/all_to_all | solution.py:45
  37.9 373.7 %all-reduce.5.cloned.1.call-start = ((), (), s32[]{:S(2)}) async-start(), calls=%async_computation.8 | async-start | bytes 14680064
  125.3 3.9 copy-start.1
  125.3 4.8 copy-start.5
  133.1 2.9 copy-start
  137.7 7.1 %slice-start = ((s8[7340032]{0:T(1024)(128)(4,1)}), s8[4194304]{0:T(1024)(128)(4,1)S(1)}, s32[]{:S(2)}) async-start(s8[7340032]{0:T(1024)(128)(4,1)} %bitcast.152), calls=%async_computation.9 | async-start | bytes 8388608
  138.9 6.0 %slice-start.1 = ((s8[7340032]{0:T(1024)(128)(4,1)}), s8[3145728]{0:T(1024)(128)(4,1)S(1)}, s32[]{:S(2)}) async-start(s8[7340032]{0:T(1024)(128)(4,1)} %bitcast.152), calls=%async_computation.10 | async-start | bytes 6291456
  144.8 4.6 copy-start.7
  148.1 3.6 copy-start.3
  148.1 4.9 copy-start.4
  149.4 4.6 copy-start.2
  171.3 307.3 %reduce-scatter.2.cloned.1.call-start = ((), (), s32[]{:S(2)}) async-start(), calls=%async_computation.7 | async-start | bytes 9175040 | tf_op jit(solution)/shard_map/reduce_scatter | solution.py:70
  171.4 2.8 copy-start.6
  178.4 1.5 copy-start.8
  188.3 21.1 %copy-start.11 = (u32[32]{0:T(128)S(1)}, u32[32]{0:T(128)}, u32[]{:S(2)}) copy-start(u32[32]{0:T(128)} %constant.30) | copy-start | bytes 388
  189.3 16.5 %all-to-all-start.3 = ((bf16[4,128,896]{1,2,0:T(8,128)(2,1)}), bf16[4,128,896]{1,2,0:T(8,128)(2,1)S(1)}, u32[]{:S(2)}, u32[]{:S(2)}) async-start(bf16[4,128,896]{1,2,0:T(8,128)(2,1)} %copy.58), calls=%async_computation.3 | async-start | bytes 1835008 | tf_op jit(solution)/shard_map/all_to_all | solution.py:55
  205.9 16.5 %all-to-all-start.1 = ((bf16[4,128,896]{1,2,0:T(8,128)(2,1)}), bf16[4,128,896]{1,2,0:T(8,128)(2,1)S(1)}, u32[]{:S(2)}, u32[]{:S(2)}) async-start(bf16[4,128,896]{1,2,0:T(8,128)(2,1)} %copy.52), calls=%async_computation.1 | async-start | bytes 1835008 | tf_op jit(solution)/shard_map/all_to_all | solution.py:54
Sparse Core Ops, SparseCore 0:
  9.6 46.4 all-gather.2
  58.2 67.0 all-gather.4
  171.5 240.0 all-reduce.4
  414.1 64.5 reduce-scatter.1
where the time goes:
time: 489 us; the launch traced here: 488 us
  waiting for transfers between devices  345 us (71%)
  local copies, waits for them, and re-layouts  40.6 us (8%)
  matrix products  29.7 us (6%)
  blocking collectives  25.7 us (5%)
  other arithmetic  16.9 us (3%)
  starting transfers between devices  14.9 us (3%)
  between operations  14.8 us (3%)
    unnamed x5, waiting for transfers between devices  189 us
    reduce_scatter x1, waiting for transfers between devices, per_device(): lax.psum_scatter(jnp.einsum('rc,dc->rd', text_grad, weight[0], preferred_...  64.6 us
    all_gather x1, waiting for transfers between devices, per_device(): weight = lax.all_gather(kv_weight, 'fsdp', axis=1, tiled=True)  54.7 us
    all_gather x1, blocking collectives, per_device(): lax.all_gather(modality, 'seq', axis=1, tiled=True)  20.6 us
    unnamed x36, local copies, waits for them, and re-layouts  17.8 us
    all_to_all x1, waiting for transfers between devices, per_device(): lax.all_to_all(queries[0], 'seq', split_axis=1, concat_axis=0, tiled=True)  17 us
    another operation x1, local copies, waits for them, and re-layouts, per_device(): jnp.stack([jnp.einsum('ld,lc->dc', hidden, text_grad, preferred_element_t...  11.7 us
    all_to_all x1, waiting for transfers between devices, per_device(): lax.all_to_all(result.astype(jnp.bfloat16), 'seq', split_axis=0, concat_a...  10.5 us
  transfers between devices with their start and end apart: 8, of which 6 were waited for; matrix products, arithmetic and copies ran while one was open for 8% of the time, Pallas kernels for 0%

commit v1 on v0

v1 whole, which is shorter than its diff:
```python
import functools

import jax
import jax.numpy as jnp
from jax import lax
from jax.experimental import pallas as pl
from jax.experimental.pallas import tpu as pltpu
from jax.sharding import PartitionSpec as P

HEAD_DIM = 128
GROUP = 7
SPAN = GROUP * HEAD_DIM
PAIR = 2 * HEAD_DIM
SCALE = HEAD_DIM ** (-0.5)
LOG2E = 1.4426950408889634
HIDDEN = -1e30
DIGIT = 16
F32 = jnp.float32
BF16 = jnp.bfloat16
ANYWHERE = pl.BlockSpec(memory_space=pl.ANY)
CYCLE = (0, 2, 4, 6, 7, 5, 3, 1)


def contract(a, b, da, db):
    return lax.dot_general(a, b, (((da,), (db,)), ((), ())), preferred_element_type=F32)


def shaped(shape, dtype):
    return jax.ShapeDtypeStruct(shape, dtype)


def constant_block(shape):
    return pl.BlockSpec(shape, lambda i, *prefetched: (0,) * len(shape))


def call(body, grid, prefetched, operands, in_specs, out_specs, out_shape, flops, scratch=(), aliases=None, mib=32):
    moved = sum(x.size * x.dtype.itemsize for x in operands)
    return pl.pallas_call(
        body,
        grid_spec=pltpu.PrefetchScalarGridSpec(
            num_scalar_prefetch=len(prefetched),
            grid=(grid,),
            in_specs=in_specs,
            out_specs=out_specs,
            scratch_shapes=scratch,
        ),
        out_shape=out_shape,
        input_output_aliases=aliases or {},
        compiler_params=pltpu.CompilerParams(vmem_limit_bytes=mib * 1024 * 1024),
        cost_estimate=pl.CostEstimate(flops=flops, bytes_accessed=moved, transcendentals=0),
    )(*prefetched, *operands)


def after(x, *others):
    return pl.pallas_call(
        lambda *refs: None,
        in_specs=[ANYWHERE] * (1 + len(others)),
        out_specs=ANYWHERE,
        out_shape=shaped(x.shape, x.dtype),
        input_output_aliases={0: 0},
        cost_estimate=pl.CostEstimate(flops=0, bytes_accessed=0, transcendentals=0),
    )(x, *others)


def blocks_kernel(depth, tok_ref, kind_ref, ids_ref, out_ref):
    count, rows, lanes = out_ref.shape
    base = lanes - 128
    lane = lax.broadcasted_iota(jnp.int32, (rows, 128), 1) - (depth - base)
    ids = ids_ref[...]
    marks = (kind_ref[...], lax.div(ids, DIGIT), lax.rem(ids, DIGIT))
    for j in range(count):
        out_ref[j, :, :depth] = tok_ref[:, j * depth : (j + 1) * depth]
        last = out_ref[j, :, base:].astype(F32)
        last = jnp.where(lane >= 0, 0.0, last)
        for i, mark in enumerate(marks):
            last = jnp.where(lane == i, mark.astype(F32), last)
        out_ref[j, :, base:] = last.astype(BF16)


def token_blocks(tokens, kinds, ids, count):
    rows, width = tokens.shape
    depth = width // count
    lanes = -(-(depth + 3) // 128) * 128
    return call(
        functools.partial(blocks_kernel, depth),
        1,
        (),
        (tokens, kinds, ids),
        [constant_block((rows, width)), constant_block((rows, 1)), constant_block((rows, 1))],
        constant_block((count, rows, lanes)),
        shaped((count, rows, lanes), BF16),
        0,
    )


def read_marks(block, depth):
    mark = [block[:, depth + i : depth + i + 1].astype(F32) for i in range(3)]
    return mark[0], mark[1] * DIGIT + mark[2]


def pack_kernel(heads_ref, q_ref, up_ref, out_ref):
    out_ref[0, 0] = q_ref[...]
    out_ref[0, 1] = up_ref[...]


def pack_heads(heads, queries, upstream):
    rows = queries.shape[0]
    by_head = pl.BlockSpec((rows, SPAN), lambda i, heads: (0, heads[i]))
    return call(
        pack_kernel,
        2,
        (heads,),
        (queries, upstream),
        [by_head, by_head],
        pl.BlockSpec((1, 2, rows, SPAN), lambda i, heads: (i, 0, 0, 0)),
        shaped((2, 2, rows, SPAN), BF16),
        0,
    )


def place_kernel(heads_ref, near_ref, far_ref, att_in, gq_in, att_ref, gq_ref):
    step = pl.program_id(0)
    for i, ref in enumerate((near_ref, far_ref)):

        @pl.when(step == i)
        def _():
            att_ref[...] = ref[0]
            gq_ref[...] = ref[1]


def place_heads(heads, near, far, attended, grad_queries):
    rows = attended.shape[0]
    by_head = pl.BlockSpec((rows, SPAN), lambda i, heads: (0, heads[i]))
    return call(
        place_kernel,
        2,
        (heads,),
        (near, far, attended, grad_queries),
        [constant_block(near.shape)] * 2 + [ANYWHERE] * 2,
        [by_head, by_head],
        [shaped(attended.shape, BF16)] * 2,
        0,
        aliases={3: 0, 4: 1},
    )


def project_kernel(depth, count, halves, first, last, quarters_ref, owners_ref, *refs):
    parts, refs = refs[: 4 * count], refs[4 * count :]
    weights, refs = refs[: count + halves], refs[count + halves :]
    rows, lanes = parts[0].shape[1:]
    sums = [0.0, 0.0]
    for b in range(count):
        left = jnp.concatenate([ref[0][:, :depth] for ref in parts[4 * b : 4 * b + 4]], axis=0)
        for e in range(2):
            right = jnp.concatenate([ref[e] for ref in weights], axis=0) if halves else weights[b][e]
            sums[e] = sums[e] + contract(left, right, 1, 0)
    if not first:
        sums = [s + refs[0][:, e * PAIR : (e + 1) * PAIR] for e, s in enumerate(sums)]
        refs = refs[1:]
    if not last:
        for e in range(2):
            refs[0][:, e * PAIR : (e + 1) * PAIR] = sums[e]
        return
    kv_ref, kind_ref, ids_ref, ids_row_ref = refs
    for r in range(4):
        here = pl.ds(pl.multiple_of(quarters_ref[r] * rows, rows), rows)
        kind, ids = read_marks(parts[r][0], depth)
        mine = slice(r * rows, (r + 1) * rows)
        kv_ref[here, :] = jnp.where(kind == 1.0, sums[1][mine], sums[0][mine]).astype(BF16)
        kind_ref[here, :] = kind
        ids_ref[here, :] = ids
    ids_row_ref[...] = jnp.broadcast_to(ids_ref[...], (4 * rows, 128)).T[:1]


def project(quarters, owners, parts, weights, total, depth, last, halves):
    rows, lanes = parts[0].shape[1:]
    count = 1 if halves else len(weights)
    length = 4 * rows
    part_specs = [
        pl.BlockSpec((1, rows, lanes), functools.partial(lambda b, i, q, o: (o[b], 0, 0), b))
        for b in range(count)
        for _ in range(4)
    ]
    full = (length, 2 * PAIR)
    before = [] if total is None else [total]
    if last:
        outs = [(length, PAIR), (length, 1), (length, 1), (1, length)]
        out_specs = [constant_block(shape) for shape in outs]
        out_shape = [shaped(shape, BF16 if i == 0 else F32) for i, shape in enumerate(outs)]
    else:
        out_specs, out_shape = constant_block(full), shaped(full, F32)
    operands = (*(list(parts) * count), *weights, *before)
    return call(
        functools.partial(project_kernel, depth, count, int(halves), total is None, last),
        1,
        (quarters, owners),
        operands,
        part_specs + [constant_block(w.shape) for w in weights] + [constant_block(full)] * len(before),
        out_specs,
        out_shape,
        4 * length * depth * PAIR * count,
        aliases={1 + len(operands): 0} if before and not last else None,
    )


def attend_kernel(spot, where_ref, q_ref, up_ref, pack_ref, kv_ref, ids_ref, ids_row_ref, *refs):
    att_ref, gq_ref, other_ref, gkv_ref, bias, scores_all, dp_all, pbs, his, los = refs[-10:]
    rows = q_ref.shape[0]
    heads = [slice(h * HEAD_DIM, (h + 1) * HEAD_DIM) for h in range(GROUP)]
    for i in range(2):
        here = pl.ds(pl.multiple_of(where_ref[1 + i] * rows, rows), rows)
        bias[i * rows : (i + 1) * rows, :] = jnp.where(ids_row_ref[...] <= ids_ref[here, :], 0.0, HIDDEN)
    keys = kv_ref[:, :HEAD_DIM]
    values = kv_ref[:, HEAD_DIM:]
    q = jnp.concatenate([q_ref[:, cols] for cols in heads] + [pack_ref[0, 0, :, cols] for cols in heads], axis=0)
    up = jnp.concatenate([up_ref[:, cols] for cols in heads] + [pack_ref[0, 1, :, cols] for cols in heads], axis=0)
    scores_all[...] = contract(q, keys, 1, 1)
    dp_all[...] = contract(up, values, 1, 1).astype(BF16)
    for h in range(2 * GROUP):
        here = slice(h * rows, (h + 1) * rows)
        side = h // GROUP
        scores = scores_all[here, :] * (SCALE * LOG2E) + bias[side * rows : (side + 1) * rows, :]
        expo = jnp.exp2(scores - jnp.max(scores, axis=-1, keepdims=True))
        probs = expo * (1.0 / jnp.sum(expo, axis=-1, keepdims=True))
        pbs[here, :] = probs.astype(BF16)
        dp = dp_all[here, :].astype(F32)
        ds = probs * (dp - jnp.sum(probs * dp, axis=-1, keepdims=True))
        hi = ds.astype(BF16)
        his[here, :] = hi
        los[here, :] = (ds - hi.astype(F32)).astype(BF16)
    att = contract(pbs[...], values, 1, 0).astype(BF16)
    gq = ((contract(his[...], keys, 1, 0) + contract(los[...], keys, 1, 0)) * SCALE).astype(BF16)
    for h, cols in enumerate(heads):
        here = slice(h * rows, (h + 1) * rows)
        there = slice((GROUP + h) * rows, (GROUP + h + 1) * rows)
        att_ref[:, cols] = att[here]
        gq_ref[:, cols] = gq[here]
        other_ref[0, :, cols] = att[there]
        other_ref[1, :, cols] = gq[there]
    dk = (contract(q, his[...], 0, 0) + contract(q, los[...], 0, 0)) * SCALE
    dv = contract(up, pbs[...], 0, 0)
    gkv_ref[:, :HEAD_DIM] = dk.T
    gkv_ref[:, HEAD_DIM:] = dv.T


def attend(where, spot, queries, upstream, pack, kv, ids, ids_row, before=()):
    rows, width = queries.shape
    length = kv.shape[0]
    by_head = pl.BlockSpec((rows, SPAN), lambda i, where: (0, where[0]))
    stacked = (2 * GROUP * rows, length)
    operands = (queries, upstream, pack, kv, ids, ids_row, *before)
    return call(
        functools.partial(attend_kernel, spot),
        1,
        (where,),
        operands,
        [
            by_head,
            by_head,
            pl.BlockSpec((1, 2, rows, SPAN), lambda i, where: (spot, 0, 0, 0)),
            constant_block((length, PAIR)),
            constant_block((length, 1)),
            constant_block((1, length)),
        ]
        + [ANYWHERE] * len(before),
        [by_head, by_head, constant_block((2, rows, SPAN)), constant_block((length, PAIR))],
        [
            shaped((rows, width), BF16),
            shaped((rows, width), BF16),
            shaped((2, rows, SPAN), BF16),
            shaped((length, PAIR), F32),
        ],
        16 * 2 * GROUP * rows * length * HEAD_DIM,
        scratch=[pltpu.VMEM((2 * rows, length), F32), pltpu.VMEM(stacked, F32)] + [pltpu.VMEM(stacked, BF16)] * 4,
        aliases={7 + i: i for i in range(len(before))},
        mib=40,
    )


def by_expert(kind, x):
    return [jnp.where(kind == float(e), x, 0.0).astype(BF16) for e in range(2)]


def hidden_kernel(quarters_ref, kind_ref, g_ref, gc_ref, w_ref, wc_ref, mine_ref, away_ref, masked):
    rows = mine_ref.shape[0]

    @pl.when(pl.program_id(0) == 0)
    def _():
        for i in range(2):
            here = pl.ds(pl.multiple_of(quarters_ref[i] * rows, rows), rows)
            for k, ref in enumerate((g_ref, gc_ref)):
                for e, part in enumerate(by_expert(kind_ref[here, :], ref[here, :].astype(F32))):
                    masked[2 * k + e, i * rows : (i + 1) * rows, :] = part

    total = 0.0
    for k, ref in enumerate((w_ref, wc_ref)):
        for e in range(2):
            total = total + contract(masked[2 * k + e], ref[:, e].reshape(-1, PAIR), 1, 1)
    mine_ref[...] = total[:rows]
    away_ref[...] = total[rows:].astype(BF16)


def hidden_grad(quarters, kind, grad, grad_c, weight, weight_c, rows):
    count, _, depth, _ = weight.shape
    length = grad.shape[0]
    group = count // 4
    by_tile = pl.BlockSpec((group, 2, depth, PAIR), lambda i, q: (i, 0, 0, 0))
    out = pl.BlockSpec((rows, group * depth), lambda i, q: (0, i))
    width = count * depth
    return call(
        hidden_kernel,
        4,
        (quarters,),
        (kind, grad, grad_c, weight, weight_c),
        [constant_block((length, 1)), constant_block((length, PAIR)), constant_block((length, PAIR)), by_tile, by_tile],
        [out, out],
        [shaped((rows, width), F32), shaped((rows, width), BF16)],
        16 * rows * width * PAIR,
        scratch=[pltpu.VMEM((4, 2 * rows, PAIR), BF16)],
    )


def weight_kernel(depth, count, halves, first, last, quarters_ref, owners_ref, *refs):
    parts, refs = refs[: 4 * count], refs[4 * count :]
    grads, refs = refs[: count + halves], refs[count + halves :]
    rows, lanes = parts[0].shape[1:]
    size = grads[0].shape[0]
    total = 0.0
    for b in range(count):
        left = jnp.concatenate([ref[0] for ref in parts[4 * b : 4 * b + 4]], axis=0)
        quarter = []
        for r in range(4):
            start = quarters_ref[r] * rows
            if halves:
                inner = pl.ds(pl.multiple_of(lax.rem(start, size), rows), rows)
                quarter.append(jnp.where(start < size, grads[0][inner, :].astype(F32), grads[1][inner, :].astype(F32)))
            else:
                quarter.append(grads[b][pl.ds(pl.multiple_of(start, rows), rows), :].astype(F32))
        kind = left[:, depth : depth + 1].astype(F32)
        right = jnp.concatenate(by_expert(kind, jnp.concatenate(quarter, axis=0)), axis=-1)
        total = total + contract(left, right, 0, 0)
    if not first:
        total = total + refs[0][...]
        refs = refs[1:]
    if not last:
        refs[0][...] = total
        return
    for e in range(2):
        refs[0][e] = total[:depth, e * PAIR : (e + 1) * PAIR]


def weight_grad(quarters, owners, parts, grads, total, depth, last, halves):
    rows, lanes = parts[0].shape[1:]
    count = 1 if halves else len(grads)
    part_specs = [
        pl.BlockSpec((1, rows, lanes), functools.partial(lambda b, i, q, o: (o[b], 0, 0), b))
        for b in range(count)
        for _ in range(4)
    ]
    full = (lanes, 2 * PAIR)
    out = (2, depth, PAIR) if last else full
    before = [] if total is None else [total]
    operands = (*(list(parts) * count), *grads, *before)
    return call(
        functools.partial(weight_kernel, depth, count, int(halves), total is None, last),
        1,
        (quarters, owners),
        operands,
        part_specs + [constant_block(g.shape) for g in grads] + [constant_block(full)] * len(before),
        constant_block(out),
        shaped(out, F32),
        16 * rows * lanes * PAIR * count,
        aliases={1 + len(operands): 0} if before and not last else None,
    )


def in_order(parts, quarters):
    count, rows, lanes = parts[0].shape
    whole = jnp.stack(parts, axis=1)
    return jnp.take(whole, quarters, axis=1).reshape(count, 4 * rows, lanes)


def project_plain(quarters, parts, weights, depth):
    tokens = in_order(parts, quarters)
    kind, ids = read_marks(tokens[0], depth)
    sums = jnp.einsum("jmk,jekn->emn", tokens[:, :, :depth], weights, preferred_element_type=F32)
    return jnp.where(kind == 1.0, sums[1], sums[0]).astype(BF16), kind, ids, ids.reshape(1, -1)


def weight_plain(quarters, parts, grads, depth):
    tokens = in_order(parts, quarters)
    kind = tokens[:, :, depth : depth + 1].astype(F32)
    sums = [
        jnp.einsum("jmk,jmn->kn", tokens[:, :, :depth], g, preferred_element_type=F32)
        for g in by_expert(kind, grads.astype(F32))
    ]
    return jnp.stack(sums)


def per_device(fsdp, seq, tokens, queries, cotangent, modality, block_ids, kv_weight):
    tokens, queries, cotangent = tokens[0], queries[0], cotangent[0]
    me_f = lax.axis_index("fsdp")
    me_s = lax.axis_index("seq")
    rows, width = tokens.shape
    depth = kv_weight.shape[1]
    near_link = fsdp == len(CYCLE)

    def swap(x, bit):
        return lax.ppermute(x, "seq", [(i, i ^ bit) for i in range(seq)])

    def over_seq(x):
        across = swap(x, 2)
        return [x, swap(x, 1), across, swap(across, 1)]

    def turn(x, by):
        return lax.ppermute(x, "fsdp", [(CYCLE[i], CYCLE[(i + by) % fsdp]) for i in range(fsdp)])

    if near_link:
        spot = jnp.array([CYCLE.index(i) for i in range(fsdp)], jnp.int32)[me_f]
        order = jnp.array(CYCLE, jnp.int32)
        around = [order[lax.rem(spot + fsdp + by, fsdp)] for by in (0, -1, 1, -2, 2, -3, 3, 4)]

    def round_cycle(x, cut, hold=None):
        ups, downs = x, x
        found = [x]
        for step in range(1, 5):
            if step == 4:
                size = x.shape[cut] // 2
                ups = lax.slice_in_dim(ups, 0, size, axis=cut)
                downs = lax.slice_in_dim(downs, size, 2 * size, axis=cut)
            if step == 2 and hold is not None:
                ups, downs = after(ups, hold), after(downs, hold)
            ups, downs = turn(ups, 1), turn(downs, -1)
            found += [ups, downs]
        return found

    quarters = me_s ^ jnp.arange(seq, dtype=jnp.int32)
    if near_link:
        weights = round_cycle(kv_weight, 1)
    else:
        weight = lax.all_gather(kv_weight, "fsdp", axis=0)

    own_blocks = token_blocks(tokens, modality.reshape(rows, 1), block_ids.reshape(rows, 1), fsdp)
    parts = over_seq(own_blocks)
    pack = swap(pack_heads(me_s ^ jnp.array([1, 3], jnp.int32), queries, cotangent), 1)
    columns = over_seq(lax.all_to_all(own_blocks, "fsdp", split_axis=0, concat_axis=0, tiled=True))

    if near_link:
        groups = ((0, 5), (5, 7), (7, 8))
        owners = [jnp.stack(around[a:b]) for a, b in groups]
        total = project(quarters, owners[0], parts, weights[:5], None, depth, False, False)
        total = project(quarters, owners[1], parts, weights[5:7], total, depth, False, False)
        kv, kind, ids, ids_row = project(quarters, owners[2], parts, weights[7:], total, depth, True, True)
        weight = jnp.zeros((fsdp, *kv_weight.shape), BF16)
        for owner, block in zip(around, weights[:7]):
            weight = lax.dynamic_update_index_in_dim(weight, block, owner, 0)
        for i, block in enumerate(weights[7:]):
            weight = lax.dynamic_update_slice(weight, block[None], (around[7], 0, i * (depth // 2), 0))
    else:
        kv, kind, ids, ids_row = project_plain(quarters, parts, weight, depth)
    weight_c = swap(weight, 1)

    where_near = jnp.stack([me_s, me_s, me_s ^ 1])
    where_far = jnp.stack([me_s ^ 2, me_s, me_s ^ 1])
    kv_far = swap(kv, 2)
    attended, grad_queries, other_near, near = attend(where_near, 0, queries, cotangent, pack, kv, ids, ids_row)
    attended, grad_queries, other_far, far = attend(
        where_far, 1, queries, cotangent, pack, kv_far, ids, ids_row, (attended, grad_queries)
    )
    grad_kv = (near + swap(far, 2)).astype(BF16)
    attended, grad_queries = place_heads(
        me_s ^ jnp.array([1, 3], jnp.int32), swap(other_near, 1), swap(other_far, 1), attended, grad_queries
    )

    mine, away = hidden_grad(
        jnp.stack([me_s, me_s ^ 2]), kind, grad_kv, swap(grad_kv, 1), weight, weight_c, rows
    )
    if near_link:
        grads = round_cycle(grad_kv, 0, away)
        total = weight_grad(quarters, owners[0], columns, grads[:5], None, depth, False, False)
        total = weight_grad(quarters, owners[1], columns, grads[5:7], total, depth, False, False)
        grad_weight = weight_grad(quarters, owners[2], columns, grads[7:], total, depth, True, True)
    else:
        grad_weight = weight_plain(quarters, columns, lax.all_gather(grad_kv, "fsdp", axis=0), depth)
    grad_tokens = (mine + swap(away, 2).astype(F32)).astype(BF16)
    return attended[None], grad_queries[None], grad_tokens[None], grad_weight


def solution(mesh):
    split = P("fsdp", "seq", None)
    weights = P(None, "fsdp", "seq")
    return jax.shard_map(
        functools.partial(per_device, mesh.shape["fsdp"], mesh.shape["seq"]),
        mesh=mesh,
        in_specs=(split, split, split, P("fsdp", "seq"), P("fsdp", "seq"), weights),
        out_specs=(split, split, split, weights),
        check_vma=False,
    )
```

time: 489 us -> 193 us (0.39)
  waiting for transfers between devices: 345 us -> 57.1 us
  Pallas kernels: 0 us -> 43.6 us
  matrix products: 29.7 us -> 0 us
  blocking collectives: 25.7 us -> 0 us
  starting transfers between devices: 14.9 us -> 30.9 us
  other arithmetic: 16.9 us -> 3.86 us
  between operations: 14.8 us -> 21.2 us
  local copies, waits for them, and re-layouts: 40.6 us -> 35 us
    unnamed x5 -> x0, waiting for transfers between devices: 189 us -> none
    reduce_scatter x1 -> x0, waiting for transfers between devices: 64.6 us -> none  [per_device(): lax.psum_scatter(jnp.einsum('rc,dc->rd', text_grad, weight[0], preferred_...]
    ppermute x0 -> x30, waiting for transfers between devices: none -> 56.2 us  [the longest x16 32.8 us: turn(): lax.ppermute(x, 'fsdp', [(CYCLE[i], CYCLE[(i + by) % fsdp]) for i in rang...]
    all_gather x2 -> x0, waiting for transfers between devices: 54.7 us -> none  [the longest x1 54.7 us: per_device(): weight = lax.all_gather(kv_weight, 'fsdp', axis=1, tiled=True)]
    pallas_call x0 -> x14, Pallas kernels: none -> 43.6 us  [the longest x12 43.6 us: call(): pl.pallas_call(body, grid_spec=pltpu.PrefetchScalarGridSpec(num_scalar_pr...]
    all_to_all x4 -> x1, waiting for transfers between devices: 36.5 us -> 0.87 us  [per_device(): lax.all_to_all(own_blocks, 'fsdp', split_axis=0, concat_axis=0, tiled=True)]
    dot_general x12 -> x0, matrix products: 29.7 us -> none  [the longest x3 10.3 us: attend(): scores = jnp.einsum('rgjd,lgd->gjrl', heads, keys) * HEAD_DIM ** (-0.5)]
    ppermute x0 -> x30, starting transfers between devices: none -> 26 us  [the longest x16 19.5 us: turn(): lax.ppermute(x, 'fsdp', [(CYCLE[i], CYCLE[(i + by) % fsdp]) for i in rang...]
  transfers between devices with their start and end apart: 8 -> 31, of which waited for: 6 -> 9; matrix products, arithmetic and copies ran while one was open for 8% -> 10% of each run, Pallas kernels for 0% -> 23%
where the time goes in v1:
time: 193 us; the launch traced here: 192 us
  waiting for transfers between devices  57.1 us (30%)
  Pallas kernels  43.6 us (23%)
  local copies, waits for them, and re-layouts  35 us (18%)
  starting transfers between devices  30.9 us (16%)
  between operations  21.2 us (11%)
  other arithmetic  3.86 us (2%)
    pallas_call x12, Pallas kernels, call(): pl.pallas_call(body, grid_spec=pltpu.PrefetchScalarGridSpec(num_scalar_pr...  43.6 us
    ppermute x16, waiting for transfers between devices, turn(): lax.ppermute(x, 'fsdp', [(CYCLE[i], CYCLE[(i + by) % fsdp]) for i in rang...  32.8 us
    ppermute x14, waiting for transfers between devices, swap(): return lax.ppermute(x, 'seq', [(i, i ^ bit) for i in range(seq)])  23.4 us
    ppermute x16, starting transfers between devices, turn(): lax.ppermute(x, 'fsdp', [(CYCLE[i], CYCLE[(i + by) % fsdp]) for i in rang...  19.5 us
    unnamed x68, local copies, waits for them, and re-layouts  18 us
    ppermute x14, starting transfers between devices, swap(): return lax.ppermute(x, 'seq', [(i, i ^ bit) for i in range(seq)])  6.49 us
    dynamic_update_slice x7, local copies, waits for them, and re-layouts, per_device(): weight = lax.dynamic_update_index_in_dim(weight, block, owner, 0)  5.68 us
    all_to_all x1, starting transfers between devices, per_device(): lax.all_to_all(own_blocks, 'fsdp', split_axis=0, concat_axis=0, tiled=True)  4.92 us
  transfers between devices with their start and end apart: 31, of which 9 were waited for; matrix products, arithmetic and copies ran while one was open for 10% of the time, Pallas kernels for 23%

profile of v1, /device:TPU:0, one launch (start us, length us, event | category | flops | bytes accessed | tf_op | source)
XLA Modules:
  0.0 191.8 jit_solution(13269060204925062437)
XLA Ops:
  0.6 3.1 %collective-permute-start.4 = (bf16[2,448,256]{2,1,0:T(8,128)(2,1)}, bf16[2,448,256]{2,1,0:T(8,128)(2,1)S(1)}, u32[]{:S(2)}, u32[]{:S(2)}) collective-permute-start(bf16[2,448,256]{2,1,0:T(8,128)(2,1)} %refs_20_.1), channel_id=1, source_target_pairs={{0,8},{8,16},{16,24},{24,28},{28,20},{20,12},{12,4},{4,0},{1,9},{9... | collective-permute-start | bytes 1376264 | tf_op jit(solution)/shard_map/ppermute | solution.py:416
  5.3 1.2 copy-done.20
  6.4 1.4 shard_map.130.refs_0_.refs_4_.refs_8_.refs_12_.refs_16_
  7.8 2.0 %collective-permute-start.2 = (bf16[8,128,512]{2,1,0:T(8,128)(2,1)}, bf16[8,128,512]{2,1,0:T(8,128)(2,1)S(1)}, u32[]{:S(2)}, u32[]{:S(2)}) collective-permute-start(bf16[8,128,512]{2,1,0:T(8,128)(2,1)} %shard_map.130.refs_0_.refs_4_.refs_8_.refs_12_.refs_16_), channel_id=1, source_target_pairs={{0,2},{1,3},{2,0},{3,1},{4,6},{5,7},{6,4},{7,5},{8,10},{9,11},{10,... | collective-permute-start | bytes 3145736 | tf_op jit(solution)/shard_map/ppermute | solution.py:409
  9.8 1.2 dynamic_slice.27
  16.2 1.6 fusion.1
  33.0 2.2 %broadcast_in_dim.42 = bf16[8,2,448,256]{3,2,1,0:T(8,128)(2,1)} broadcast(bf16[]{:T(256)} %constant.86.clone.1), dimensions={} | broadcast | bytes 3670018 | tf_op jit(solution)/shard_map/broadcast_in_dim | solution.py:454
  36.0 1.6 collective-permute-start.5
  39.7 7.8 %collective-permute-done.5.refs_23_ = bf16[2,448,256]{2,1,0:T(8,128)(2,1)S(1)} collective-permute-done((bf16[2,448,256]{2,1,0:T(8,128)(2,1)S(1)}, bf16[2,448,256]{2,1,0:T(8,128)(2,1)S(1)}, u32[]{:S(2)}, u32[]{:S(2)}) %collective-permute-start.5) | collective-permute-done | bytes 458784 | tf_op jit(solution)/shard_map/ppermute | solution.py:416
  47.5 1.6 collective-permute-start.6
  51.1 6.9 %collective-permute-done.6.refs_8_ = bf16[2,448,256]{2,1,0:T(8,128)(2,1)S(1)} collective-permute-done((bf16[2,448,256]{2,1,0:T(8,128)(2,1)S(1)}, bf16[2,448,256]{2,1,0:T(8,128)(2,1)S(1)}, u32[]{:S(2)}, u32[]{:S(2)}) %collective-permute-start.6) | collective-permute-done | bytes 458784 | tf_op jit(solution)/shard_map/ppermute | solution.py:416
  58.1 1.6 collective-permute-start.7
  61.9 2.3 %collective-permute-done.7.refs_4_ = bf16[2,224,256]{2,1,0:T(8,128)(2,1)S(1)} collective-permute-done((bf16[2,224,256]{2,1,0:T(8,128)(2,1)S(1)}, bf16[2,224,256]{2,1,0:T(8,128)(2,1)S(1)}, u32[]{:S(2)}, u32[]{:S(2)}) %collective-permute-start.7) | collective-permute-done | bytes 229408 | tf_op jit(solution)/shard_map/ppermute | solution.py:416
  66.6 4.9 %all-to-all-start = ((bf16[8,128,512]{2,1,0:T(8,128)(2,1)}), bf16[8,128,512]{2,1,0:T(8,128)(2,1)S(1)}, u32[]{:S(2)}, u32[]{:S(2)}) async-start(bf16[8,128,512]{2,1,0:T(8,128)(2,1)} %shard_map.130.refs_0_.refs_4_.refs_8_.refs_12_.refs_16_), calls=%async_computation | async-start | bytes 2097152 | tf_op jit(solution)/shard_map/all_to_all | solution.py:446
  72.0 1.2 copy-done.21
  73.2 1.2 copy-done.23
  74.4 1.6 shard_map.129
  76.2 3.2 %stack.33.owners_ref = s32[5]{0:T(128)S(1)} concatenate(s32[1]{0:T(128)} %get-tuple-element.39, s32[1]{0:T(128)} %get-tuple-element.38, s32[1]{0:T(128)} %get-tuple-element.37, s32[1]{0:T(128)} %get-tuple-element.43, s32[1]{0:T(128)} %get-tuple-element.36), dimensions={0} | concatenate | bytes 40 | tf_op jit(solution)/shard_map/stack | solution.py:450
  79.4 1.4 pad_add_fusion.owners_ref
  80.8 1.1 copy-done.7
  81.9 1.0 copy-done.9
  82.9 1.0 copy-done.11
  84.0 1.0 copy-done.13
  85.0 1.0 copy-done.15
  86.0 3.4 %shard_map.131.refs_10_ = f32[512,512]{1,0:T(8,128)S(1)} custom-call(s32[4]{0:T(128)S(1)} %iota_xor_fusion.quarters_ref, s32[5]{0:T(128)S(1)} %stack.33.owners_ref, bf16[8,128,512]{2,1,0:T(8,128)(2,1)} %shard_map.130.refs_0_.refs_4_.refs_8_.refs_12_.refs_16_, bf16[8,128,512]{2,1,0:T(8,128)(2,1)S(1)} %collective-permute-done.1.refs_1_.refs_5_.refs_9_.refs_13_.refs_17_, ...), custom_call_target="tpu_custom_call" | custom-call | flops 1174405120 | bytes 23265280 | tf_op jit(solution)/shard_map/pallas_call | solution.py:38
  89.4 2.4 %shard_map.132.refs_6_ = f32[512,512]{1,0:T(8,128)S(1)} custom-call(s32[4]{0:T(128)S(1)} %iota_xor_fusion.quarters_ref, s32[2]{0:T(128)S(1)} %pad_add_fusion.owners_ref, bf16[8,128,512]{2,1,0:T(8,128)(2,1)} %shard_map.130.refs_0_.refs_4_.refs_8_.refs_12_.refs_16_, ...), custom_call_target="tpu_custom_call", output_to_operand_aliasing={{}: (12, {})} | custom-call | flops 469762048 | bytes 10354688 | tf_op jit(solution)/shard_map/pallas_call | solution.py:38
  91.8 3.3 %shard_map.133 = (bf16[512,256]{1,0:T(8,128)(2,1)}, f32[512,1]{1,0:T(8,128)S(1)}, f32[512,1]{1,0:T(8,128)S(1)}, f32[1,512]{1,0:T(1,128)S(1)}) custom-call(s32[4]{0:T(128)S(1)} %iota_xor_fusion.quarters_ref, s32[1]{0:T(128)} %get-tuple-element.42.owners_ref, bf16[8,128,512]{2,1,0:T(8,128)(2,1)} %shard_map.130.refs_0_.refs_4_.refs_8_.refs_12_.refs_16_, ...), custom_call_target="tpu_custom_call" | custom-call | flops 234881024 | bytes 5701632 | tf_op jit(solution)/shard_map/pallas_call | solution.py:38
  98.6 1.2 copy-done.22
  99.8 1.2 copy-done.24
  101.9 6.2 %shard_map.134 = (bf16[128,3584]{1,0:T(8,128)(2,1)}, bf16[128,3584]{1,0:T(8,128)(2,1)}, bf16[2,128,896]{2,1,0:T(8,128)(2,1)}, f32[512,256]{1,0:T(8,128)S(1)}) custom-call(s32[3]{0:T(128)S(1)} %get-tuple-element.44.where_ref, bf16[128,3584]{1,0:T(8,128)(2,1)S(1)} %bitcast.48, bf16[128,3584]{1,0:T(8,128)(2,1)S(1)} %bitcast.51, ...), custom_call_target="tpu_custom_call" | custom-call | flops 1879048192 | bytes 3018752 | tf_op jit(solution)/shard_map/pallas_call | solution.py:38
  108.1 6.1 %shard_map.135 = (bf16[128,3584]{1,0:T(8,128)(2,1)}, bf16[128,3584]{1,0:T(8,128)(2,1)}, bf16[2,128,896]{2,1,0:T(8,128)(2,1)}, f32[512,256]{1,0:T(8,128)S(1)}) custom-call(s32[3]{0:T(128)S(1)} %get-tuple-element.45.where_ref, bf16[128,3584]{1,0:T(8,128)(2,1)S(1)} %bitcast.49, ...), custom_call_target="tpu_custom_call", output_to_operand_aliasing={{0}: (7, {}), {1}: (8, {})} | custom-call | flops 1879048192 | bytes 4853760 | tf_op jit(solution)/shard_map/pallas_call | solution.py:38
  114.1 1.4 collective-permute-start.15
  115.5 23.4 %collective-permute-done.15 = f32[512,256]{1,0:T(8,128)S(1)} collective-permute-done((f32[512,256]{1,0:T(8,128)S(1)}, f32[512,256]{1,0:T(8,128)S(1)}, u32[]{:S(2)}, u32[]{:S(2)}) %collective-permute-start.15) | collective-permute-done | bytes 524320 | tf_op jit(solution)/shard_map/ppermute | solution.py:409
  139.1 2.1 %collective-permute-start.22 = (bf16[512,256]{1,0:T(8,128)(2,1)S(1)}, bf16[512,256]{1,0:T(8,128)(2,1)S(1)}, u32[]{:S(2)}, u32[]{:S(2)}) collective-permute-start(bf16[512,256]{1,0:T(8,128)(2,1)S(1)} %add_convert_fusion.1.g_ref.refs_20_), channel_id=1, source_target_pairs={{0,8},{8,16},{16,24},{24,28},{28,20},{20,12},{12,4},{4,0},{1,9},{9... | collective-permute-start | bytes 786440 | tf_op jit(solution)/shard_map/ppermute | solution.py:416
  141.8 6.2 %collective-permute-done.22.refs_21_ = bf16[512,256]{1,0:T(8,128)(2,1)S(1)} collective-permute-done((bf16[512,256]{1,0:T(8,128)(2,1)S(1)}, bf16[512,256]{1,0:T(8,128)(2,1)S(1)}, u32[]{:S(2)}, u32[]{:S(2)}) %collective-permute-start.22) | collective-permute-done | bytes 262176 | tf_op jit(solution)/shard_map/ppermute | solution.py:416
  148.1 2.0 %collective-permute-start.26 = (bf16[512,256]{1,0:T(8,128)(2,1)S(1)}, bf16[512,256]{1,0:T(8,128)(2,1)S(1)}, u32[]{:S(2)}, u32[]{:S(2)}) collective-permute-start(bf16[512,256]{1,0:T(8,128)(2,1)S(1)} %add_convert_fusion.1.g_ref.refs_20_), channel_id=1, source_target_pairs={{0,4},{8,0},{16,8},{24,16},{28,24},{20,28},{12,20},{4,12},{1,5},{9... | collective-permute-start | bytes 786440 | tf_op jit(solution)/shard_map/ppermute | solution.py:416
  150.2 6.9 %shard_map.137 = (f32[128,3584]{1,0:T(8,128)S(1)}, bf16[128,3584]{1,0:T(8,128)(2,1)}) custom-call(s32[2]{0:T(128)S(1)} %pad_add_fusion.1.quarters_ref, f32[512,1]{1,0:T(8,128)S(1)} %copy-done.28, bf16[512,256]{1,0:T(8,128)(2,1)S(1)} %add_convert_fusion.1.g_ref.refs_20_, bf16[512,256]{1,0:T(8,128)(2,1)S(1)} %collective-permute-done.16.gc_ref, ...), custom_call_target="tpu_custom_call" | custom-call | flops 1879048192 | bytes 7866368 | tf_op jit(solution)/shard_map/pallas_call | solution.py:38
  157.0 1.3 copy-done.4
  160.5 1.7 collective-permute-start.27
  162.3 6.2 %collective-permute-done.23.refs_23_ = bf16[512,256]{1,0:T(8,128)(2,1)} collective-permute-done((bf16[512,256]{1,0:T(8,128)(2,1)}, bf16[512,256]{1,0:T(8,128)(2,1)}, u32[]{:S(2)}, u32[]{:S(2)}) %collective-permute-start.23) | collective-permute-done | bytes 262176 | tf_op jit(solution)/shard_map/ppermute | solution.py:416
  168.7 1.7 collective-permute-start.28
  170.5 2.7 %shard_map.136 = (bf16[128,3584]{1,0:T(8,128)(2,1)}, bf16[128,3584]{1,0:T(8,128)(2,1)}) custom-call(s32[2]{0:T(128)S(1)} %broadcast_xor_fusion.heads_ref, bf16[2,128,896]{2,1,0:T(8,128)(2,1)} %collective-permute-done.12.near_ref, bf16[2,128,896]{2,1,0:T(8,128)(2,1)} %collective-permute-done.14.far_ref, ...), custom_call_target="tpu_custom_call", output_to_operand_aliasing={{0}: (3, {}), {1}: (4, {})} | custom-call | bytes 2752512 | tf_op jit(solution)/shard_map/pallas_call | solution.py:38
  173.1 2.5 %collective-permute-done.24.refs_8_ = bf16[512,256]{1,0:T(8,128)(2,1)S(1)} collective-permute-done((bf16[512,256]{1,0:T(8,128)(2,1)}, bf16[512,256]{1,0:T(8,128)(2,1)S(1)}, u32[]{:S(2)}, u32[]{:S(2)}) %collective-permute-start.24) | collective-permute-done | bytes 262176 | tf_op jit(solution)/shard_map/ppermute | solution.py:416
  176.0 1.8 collective-permute-start.29
  179.7 3.7 %shard_map.140.refs_10_ = f32[512,512]{1,0:T(8,128)S(1)} custom-call(s32[4]{0:T(128)S(1)} %iota_xor_fusion.quarters_ref, s32[5]{0:T(128)S(1)} %stack.33.owners_ref, bf16[8,128,512]{2,1,0:T(8,128)(2,1)S(1)} %all-to-all-done.refs_0_.refs_4_.refs_8_.refs_12_.refs_16_, bf16[8,128,512]{2,1,0:T(8,128)(2,1)S(1)} %collective-permute-done.19.refs_1_.refs_5_.refs_9_.refs_13_.refs_17_, ...), custom_call_target="tpu_custom_call" | custom-call | flops 1342177280 | bytes 22282240 | tf_op jit(solution)/shard_map/pallas_call | solution.py:38
  183.3 2.4 %shard_map.141.refs_6_ = f32[512,512]{1,0:T(8,128)S(1)} custom-call(s32[4]{0:T(128)S(1)} %iota_xor_fusion.quarters_ref, s32[2]{0:T(128)S(1)} %pad_add_fusion.owners_ref, bf16[8,128,512]{2,1,0:T(8,128)(2,1)S(1)} %all-to-all-done.refs_0_.refs_4_.refs_8_.refs_12_.refs_16_, ...), custom_call_target="tpu_custom_call", output_to_operand_aliasing={{}: (12, {})} | custom-call | flops 536870912 | bytes 9961472 | tf_op jit(solution)/shard_map/pallas_call | solution.py:38
  185.8 3.7 %shard_map.142 = f32[2,448,256]{2,1,0:T(8,128)} custom-call(s32[4]{0:T(128)S(1)} %iota_xor_fusion.quarters_ref, s32[1]{0:T(128)} %get-tuple-element.42.owners_ref, bf16[8,128,512]{2,1,0:T(8,128)(2,1)S(1)} %all-to-all-done.refs_0_.refs_4_.refs_8_.refs_12_.refs_16_, bf16[8,128,512]{2,1,0:T(8,128)(2,1)S(1)} %collective-permute-done.19.refs_1_.refs_5_.refs_9_.refs_13_.refs_17_, ...), custom_call_target="tpu_custom_call" | custom-call | flops 268435456 | bytes 5505024 | tf_op jit(solution)/shard_map/pallas_call | solution.py:38
  189.5 2.3 %fusion = bf16[1,128,3584]{2,1,0:T(8,128)(2,1)} fusion(f32[128,3584]{1,0:T(8,128)S(1)} %copy-done.5, bf16[128,3584]{1,0:T(8,128)(2,1)} %collective-permute-done.18), kind=kLoop, calls=%fused_computation.1 | loop fusion | flops 1376256 | bytes 3670016 | tf_op jit(solution)/shard_map/broadcast_in_dim | solution.py:486
  (122 shorter events, 22.1 us)
Async XLA Ops:
  0.6 34.6 %copy-start.6 = (bf16[2,448,256]{2,1,0:T(8,128)(2,1)S(1)}, bf16[2,448,256]{2,1,0:T(8,128)(2,1)}, u32[]{:S(2)}) copy-start(bf16[2,448,256]{2,1,0:T(8,128)(2,1)} %refs_20_.1) | copy-start | bytes 1376260
  0.6 35.4 %collective-permute-start.4 = (bf16[2,448,256]{2,1,0:T(8,128)(2,1)}, bf16[2,448,256]{2,1,0:T(8,128)(2,1)S(1)}, u32[]{:S(2)}, u32[]{:S(2)}) collective-permute-start(bf16[2,448,256]{2,1,0:T(8,128)(2,1)} %refs_20_.1), channel_id=1, source_target_pairs={{0,8},{8,16},{16,24},{24,28},{28,20},{20,12},{12,4},{4,0},{1,9},{9... | collective-permute-start | bytes 1376264 | tf_op jit(solution)/shard_map/ppermute | solution.py:416
  3.7 33.9 %collective-permute-start.8 = (bf16[2,448,256]{2,1,0:T(8,128)(2,1)}, bf16[2,448,256]{2,1,0:T(8,128)(2,1)S(1)}, u32[]{:S(2)}, u32[]{:S(2)}) collective-permute-start(bf16[2,448,256]{2,1,0:T(8,128)(2,1)} %refs_20_.1), channel_id=1, source_target_pairs={{0,4},{8,0},{16,8},{24,16},{28,24},{20,28},{12,20},{4,12},{1,5},{9... | collective-permute-start | bytes 1376264 | tf_op jit(solution)/shard_map/ppermute | solution.py:416
  7.8 63.9 %collective-permute-start.2 = (bf16[8,128,512]{2,1,0:T(8,128)(2,1)}, bf16[8,128,512]{2,1,0:T(8,128)(2,1)S(1)}, u32[]{:S(2)}, u32[]{:S(2)}) collective-permute-start(bf16[8,128,512]{2,1,0:T(8,128)(2,1)} %shard_map.130.refs_0_.refs_4_.refs_8_.refs_12_.refs_16_), channel_id=1, source_target_pairs={{0,2},{1,3},{2,0},{3,1},{4,6},{5,7},{6,4},{7,5},{8,10},{9,11},{10,... | collective-permute-start | bytes 3145736 | tf_op jit(solution)/shard_map/ppermute | solution.py:409
  36.0 30.5 %copy-start.8 = (bf16[2,448,256]{2,1,0:T(8,128)(2,1)}, bf16[2,448,256]{2,1,0:T(8,128)(2,1)S(1)}, u32[]{:S(2)}) copy-start(bf16[2,448,256]{2,1,0:T(8,128)(2,1)S(1)} %collective-permute-done.4.refs_21_) | copy-start | bytes 1376260
  36.0 11.4 %collective-permute-start.5 = (bf16[2,448,256]{2,1,0:T(8,128)(2,1)S(1)}, bf16[2,448,256]{2,1,0:T(8,128)(2,1)S(1)}, u32[]{:S(2)}, u32[]{:S(2)}) collective-permute-start(bf16[2,448,256]{2,1,0:T(8,128)(2,1)S(1)} %collective-permute-done.4.refs_21_), channel_id=1, source_target_pairs={{0,8},{8,16},{16,24},{24,28},{28,20},{20,12},{12,4},{4,0},{1,9},{9... | collective-permute-start | bytes 1376264 | tf_op jit(solution)/shard_map/ppermute | solution.py:416
  37.6 29.0 %copy-start.10 = (bf16[2,448,256]{2,1,0:T(8,128)(2,1)}, bf16[2,448,256]{2,1,0:T(8,128)(2,1)S(1)}, u32[]{:S(2)}) copy-start(bf16[2,448,256]{2,1,0:T(8,128)(2,1)S(1)} %collective-permute-done.8.refs_22_) | copy-start | bytes 1376260
  37.6 11.4 %collective-permute-start.9 = (bf16[2,448,256]{2,1,0:T(8,128)(2,1)S(1)}, bf16[2,448,256]{2,1,0:T(8,128)(2,1)S(1)}, u32[]{:S(2)}, u32[]{:S(2)}) collective-permute-start(bf16[2,448,256]{2,1,0:T(8,128)(2,1)S(1)} %collective-permute-done.8.refs_22_), channel_id=1, source_target_pairs={{0,4},{8,0},{16,8},{24,16},{28,24},{20,28},{12,20},{4,12},{1,5},{9... | collective-permute-start | bytes 1376264 | tf_op jit(solution)/shard_map/ppermute | solution.py:416
  39.7 32.3 %copy-start.32 = (s32[2]{0:T(128)S(1)}, s32[2]{0:T(128)}, u32[]{:S(2)}) copy-start(s32[2]{0:T(128)} %constant.90.clone) | copy-start | bytes 28
  47.5 14.4 %copy-start.12 = (bf16[2,448,256]{2,1,0:T(8,128)(2,1)}, bf16[2,448,256]{2,1,0:T(8,128)(2,1)S(1)}, u32[]{:S(2)}) copy-start(bf16[2,448,256]{2,1,0:T(8,128)(2,1)S(1)} %collective-permute-done.5.refs_23_) | copy-start | bytes 1376260
  47.5 10.6 %collective-permute-start.6 = (bf16[2,448,256]{2,1,0:T(8,128)(2,1)S(1)}, bf16[2,448,256]{2,1,0:T(8,128)(2,1)S(1)}, u32[]{:S(2)}, u32[]{:S(2)}) collective-permute-start(bf16[2,448,256]{2,1,0:T(8,128)(2,1)S(1)} %collective-permute-done.5.refs_23_), channel_id=1, source_target_pairs={{0,8},{8,16},{16,24},{24,28},{28,20},{20,12},{12,4},{4,0},{1,9},{9... | collective-permute-start | bytes 1376264 | tf_op jit(solution)/shard_map/ppermute | solution.py:416
  49.0 15.1 %copy-start.14 = (bf16[2,448,256]{2,1,0:T(8,128)(2,1)}, bf16[2,448,256]{2,1,0:T(8,128)(2,1)S(1)}, u32[]{:S(2)}) copy-start(bf16[2,448,256]{2,1,0:T(8,128)(2,1)S(1)} %collective-permute-done.9.refs_24_) | copy-start | bytes 1376260
  49.0 10.7 %collective-permute-start.10 = (bf16[2,448,256]{2,1,0:T(8,128)(2,1)S(1)}, bf16[2,448,256]{2,1,0:T(8,128)(2,1)S(1)}, u32[]{:S(2)}, u32[]{:S(2)}) collective-permute-start(bf16[2,448,256]{2,1,0:T(8,128)(2,1)S(1)} %collective-permute-done.9.refs_24_), channel_id=1, source_target_pairs={{0,4},{8,0},{16,8},{24,16},{28,24},{20,28},{12,20},{4,12},{1,5},{9... | collective-permute-start | bytes 1376264 | tf_op jit(solution)/shard_map/ppermute | solution.py:416
  58.1 2.2 %copy-start = (bf16[2,448,256]{2,1,0:T(8,128)(2,1)}, bf16[2,448,256]{2,1,0:T(8,128)(2,1)S(1)}, u32[]{:S(2)}) copy-start(bf16[2,448,256]{2,1,0:T(8,128)(2,1)S(1)} %collective-permute-done.6.refs_8_) | copy-start | bytes 1376260
  58.1 6.1 %collective-permute-start.7 = (bf16[2,224,256]{2,1,0:T(8,128)(2,1)S(1)}, bf16[2,224,256]{2,1,0:T(8,128)(2,1)S(1)}, u32[]{:S(2)}, u32[]{:S(2)}) collective-permute-start(bf16[2,224,256]{2,1,0:T(8,128)(2,1)S(1)} %slice.16), channel_id=1, source_target_pairs={{0,8},{8,16},{16,24},{24,28},{28,20},{20,12},{12,4},{4,0},{1,9},{9... | collective-permute-start | bytes 688136 | tf_op jit(solution)/shard_map/ppermute | solution.py:416
  59.7 1.4 copy-start.2
  59.7 6.1 %collective-permute-start.11 = (bf16[2,224,256]{2,1,0:T(8,128)(2,1)S(1)}, bf16[2,224,256]{2,1,0:T(8,128)(2,1)S(1)}, u32[]{:S(2)}, u32[]{:S(2)}) collective-permute-start(bf16[2,224,256]{2,1,0:T(8,128)(2,1)S(1)} %slice.17), channel_id=1, source_target_pairs={{0,4},{8,0},{16,8},{24,16},{28,24},{20,28},{12,20},{4,12},{1,5},{9... | collective-permute-start | bytes 688136 | tf_op jit(solution)/shard_map/ppermute | solution.py:416
  66.6 81.5 %collective-permute-start.17 = (bf16[8,2,448,256]{3,2,1,0:T(8,128)(2,1)}, bf16[8,2,448,256]{3,2,1,0:T(8,128)(2,1)}, u32[]{:S(2)}, u32[]{:S(2)}) collective-permute-start(bf16[8,2,448,256]{3,2,1,0:T(8,128)(2,1)} %bitcast_dynamic-update-slice_fusion.7.w_ref), channel_id=1, source_target_pairs={{0,1},{1,0},{2,3},{3,2},{4,5},{5,4},{6,7},{7,6},{8,9},{9,8},{10,11... | collective-permute-start | bytes 11010056 | tf_op jit(solution)/shard_map/ppermute | solution.py:409
  66.6 31.3 %all-to-all-start = ((bf16[8,128,512]{2,1,0:T(8,128)(2,1)}), bf16[8,128,512]{2,1,0:T(8,128)(2,1)S(1)}, u32[]{:S(2)}, u32[]{:S(2)}) async-start(bf16[8,128,512]{2,1,0:T(8,128)(2,1)} %shard_map.130.refs_0_.refs_4_.refs_8_.refs_12_.refs_16_), calls=%async_computation | async-start | bytes 2097152 | tf_op jit(solution)/shard_map/all_to_all | solution.py:446
  71.5 9.3 %collective-permute-start.1 = (bf16[8,128,512]{2,1,0:T(8,128)(2,1)}, bf16[8,128,512]{2,1,0:T(8,128)(2,1)S(1)}, u32[]{:S(2)}, u32[]{:S(2)}) collective-permute-start(bf16[8,128,512]{2,1,0:T(8,128)(2,1)} %shard_map.130.refs_0_.refs_4_.refs_8_.refs_12_.refs_16_), channel_id=1, source_target_pairs={{0,1},{1,0},{2,3},{3,2},{4,5},{5,4},{6,7},{7,6},{8,9},{9,8},{10,11... | collective-permute-start | bytes 3145736 | tf_op jit(solution)/shard_map/ppermute | solution.py:409
  71.7 9.1 %collective-permute-start.3 = (bf16[8,128,512]{2,1,0:T(8,128)(2,1)S(1)}, bf16[8,128,512]{2,1,0:T(8,128)(2,1)}, u32[]{:S(2)}, u32[]{:S(2)}) collective-permute-start(bf16[8,128,512]{2,1,0:T(8,128)(2,1)S(1)} %collective-permute-done.2.refs_2_.refs_6_.refs_10_.refs_14_.refs_18_), channel_id=1, source_target_pairs={{0,1},{1,0},{2,3},{3,2},{4,5},{5,4},{6,7},{7,6},{8,9},{9,8},{10,11... | collective-permute-start | bytes 3145736 | tf_op jit(solution)/shard_map/ppermute | solution.py:409
  76.0 22.6 %collective-permute-start = (bf16[2,2,128,896]{3,2,1,0:T(8,128)(2,1)}, bf16[2,2,128,896]{3,2,1,0:T(8,128)(2,1)}, u32[]{:S(2)}, u32[]{:S(2)}) collective-permute-start(bf16[2,2,128,896]{3,2,1,0:T(8,128)(2,1)} %shard_map.129), channel_id=1, source_target_pairs={{0,1},{1,0},{2,3},{3,2},{4,5},{5,4},{6,7},{7,6},{8,9},{9,8},{10,11... | collective-permute-start | bytes 2752520 | tf_op jit(solution)/shard_map/ppermute | solution.py:409
  80.8 8.6 %copy-start.1 = (bf16[2,448,256]{2,1,0:T(8,128)(2,1)S(1)}, bf16[2,448,256]{2,1,0:T(8,128)(2,1)}, u32[]{:S(2)}) copy-start(bf16[2,448,256]{2,1,0:T(8,128)(2,1)} %copy-done) | copy-start | bytes 1376260
  80.8 8.6 %copy-start.3 = (bf16[2,448,256]{2,1,0:T(8,128)(2,1)S(1)}, bf16[2,448,256]{2,1,0:T(8,128)(2,1)}, u32[]{:S(2)}) copy-start(bf16[2,448,256]{2,1,0:T(8,128)(2,1)} %copy-done.2) | copy-start | bytes 1376260
  89.4 2.4 %copy-start.26 = (bf16[2,224,256]{2,1,0:T(8,128)(2,1)S(1)}, bf16[2,224,256]{2,1,0:T(8,128)(2,1)}, u32[]{:S(2)}) copy-start(bf16[2,224,256]{2,1,0:T(8,128)(2,1)} %copy-done.25) | copy-start | bytes 688132
  96.5 11.6 %collective-permute-start.13 = (bf16[512,256]{1,0:T(8,128)(2,1)}, bf16[512,256]{1,0:T(8,128)(2,1)S(1)}, u32[]{:S(2)}, u32[]{:S(2)}) collective-permute-start(bf16[512,256]{1,0:T(8,128)(2,1)} %get-tuple-element.20.kv_ref), channel_id=1, source_target_pairs={{0,2},{1,3},{2,0},{3,1},{4,6},{5,7},{6,4},{7,5},{8,10},{9,11},{10,... | collective-permute-start | bytes 786440 | tf_op jit(solution)/shard_map/ppermute | solution.py:409
  97.9 43.4 %collective-permute-start.20 = (bf16[8,128,512]{2,1,0:T(8,128)(2,1)S(1)}, bf16[8,128,512]{2,1,0:T(8,128)(2,1)S(1)}, u32[]{:S(2)}, u32[]{:S(2)}) collective-permute-start(bf16[8,128,512]{2,1,0:T(8,128)(2,1)S(1)} %all-to-all-done.refs_0_.refs_4_.refs_8_.refs_12_.refs_16_), channel_id=1, source_target_pairs={{0,2},{1,3},{2,0},{3,1},{4,6},{5,7},{6,4},{7,5},{8,10},{9,11},{10,... | collective-permute-start | bytes 3145736 | tf_op jit(solution)/shard_map/ppermute | solution.py:409
  101.9 6.2 %copy-start.31 = (f32[512,1]{1,0:T(8,128)S(1)}, f32[512,1]{1,0:T(8,128)}, u32[]{:S(2)}) copy-start(f32[512,1]{1,0:T(8,128)} %copy-done.29) | copy-start | bytes 6148
  108.1 42.1 %copy-start.28 = (f32[512,1]{1,0:T(8,128)S(1)}, f32[512,1]{1,0:T(8,128)}, u32[]{:S(2)}) copy-start(f32[512,1]{1,0:T(8,128)} %copy-done.27) | copy-start | bytes 6148
  114.1 24.8 %collective-permute-start.15 = (f32[512,256]{1,0:T(8,128)S(1)}, f32[512,256]{1,0:T(8,128)S(1)}, u32[]{:S(2)}, u32[]{:S(2)}) collective-permute-start(f32[512,256]{1,0:T(8,128)S(1)} %get-tuple-element.33), channel_id=1, source_target_pairs={{0,2},{1,3},{2,0},{3,1},{4,6},{5,7},{6,4},{7,5},{8,10},{9,11},{10,... | collective-permute-start | bytes 1572872 | tf_op jit(solution)/shard_map/ppermute | solution.py:409
  139.0 2.7 %collective-permute-start.16 = (bf16[512,256]{1,0:T(8,128)(2,1)S(1)}, bf16[512,256]{1,0:T(8,128)(2,1)S(1)}, u32[]{:S(2)}, u32[]{:S(2)}) collective-permute-start(bf16[512,256]{1,0:T(8,128)(2,1)S(1)} %add_convert_fusion.1.g_ref.refs_20_), channel_id=1, source_target_pairs={{0,1},{1,0},{2,3},{3,2},{4,5},{5,4},{6,7},{7,6},{8,9},{9,8},{10,11... | collective-permute-start | bytes 786440 | tf_op jit(solution)/shard_map/ppermute | solution.py:409
  139.1 9.0 %collective-permute-start.22 = (bf16[512,256]{1,0:T(8,128)(2,1)S(1)}, bf16[512,256]{1,0:T(8,128)(2,1)S(1)}, u32[]{:S(2)}, u32[]{:S(2)}) collective-permute-start(bf16[512,256]{1,0:T(8,128)(2,1)S(1)} %add_convert_fusion.1.g_ref.refs_20_), channel_id=1, source_target_pairs={{0,8},{8,16},{16,24},{24,28},{28,20},{20,12},{12,4},{4,0},{1,9},{9... | collective-permute-start | bytes 786440 | tf_op jit(solution)/shard_map/ppermute | solution.py:416
  141.1 36.6 %collective-permute-start.19 = (bf16[8,128,512]{2,1,0:T(8,128)(2,1)S(1)}, bf16[8,128,512]{2,1,0:T(8,128)(2,1)S(1)}, u32[]{:S(2)}, u32[]{:S(2)}) collective-permute-start(bf16[8,128,512]{2,1,0:T(8,128)(2,1)S(1)} %all-to-all-done.refs_0_.refs_4_.refs_8_.refs_12_.refs_16_), channel_id=1, source_target_pairs={{0,1},{1,0},{2,3},{3,2},{4,5},{5,4},{6,7},{7,6},{8,9},{9,8},{10,11... | collective-permute-start | bytes 3145736 | tf_op jit(solution)/shard_map/ppermute | solution.py:409
  141.3 36.5 %collective-permute-start.21 = (bf16[8,128,512]{2,1,0:T(8,128)(2,1)S(1)}, bf16[8,128,512]{2,1,0:T(8,128)(2,1)}, u32[]{:S(2)}, u32[]{:S(2)}) collective-permute-start(bf16[8,128,512]{2,1,0:T(8,128)(2,1)S(1)} %collective-permute-done.20.refs_2_.refs_6_.refs_10_.refs_14_.refs_18_), channel_id=1, source_target_pairs={{0,1},{1,0},{2,3},{3,2},{4,5},{5,4},{6,7},{7,6},{8,9},{9,8},{10,11... | collective-permute-start | bytes 3145736 | tf_op jit(solution)/shard_map/ppermute | solution.py:409
  141.7 18.6 %collective-permute-start.12 = (bf16[2,128,896]{2,1,0:T(8,128)(2,1)}, bf16[2,128,896]{2,1,0:T(8,128)(2,1)}, u32[]{:S(2)}, u32[]{:S(2)}) collective-permute-start(bf16[2,128,896]{2,1,0:T(8,128)(2,1)} %get-tuple-element.23), channel_id=1, source_target_pairs={{0,1},{1,0},{2,3},{3,2},{4,5},{5,4},{6,7},{7,6},{8,9},{9,8},{10,11... | collective-permute-start | bytes 1376264 | tf_op jit(solution)/shard_map/ppermute | solution.py:409
  148.0 10.8 %copy-start.16 = (bf16[512,256]{1,0:T(8,128)(2,1)}, bf16[512,256]{1,0:T(8,128)(2,1)S(1)}, u32[]{:S(2)}) copy-start(bf16[512,256]{1,0:T(8,128)(2,1)S(1)} %collective-permute-done.22.refs_21_) | copy-start | bytes 786436
  148.0 12.5 %collective-permute-start.14 = (bf16[2,128,896]{2,1,0:T(8,128)(2,1)}, bf16[2,128,896]{2,1,0:T(8,128)(2,1)}, u32[]{:S(2)}, u32[]{:S(2)}) collective-permute-start(bf16[2,128,896]{2,1,0:T(8,128)(2,1)} %get-tuple-element.26), channel_id=1, source_target_pairs={{0,1},{1,0},{2,3},{3,2},{4,5},{5,4},{6,7},{7,6},{8,9},{9,8},{10,11... | collective-permute-start | bytes 1376264 | tf_op jit(solution)/shard_map/ppermute | solution.py:409
  148.1 10.2 %collective-permute-start.26 = (bf16[512,256]{1,0:T(8,128)(2,1)S(1)}, bf16[512,256]{1,0:T(8,128)(2,1)S(1)}, u32[]{:S(2)}, u32[]{:S(2)}) collective-permute-start(bf16[512,256]{1,0:T(8,128)(2,1)S(1)} %add_convert_fusion.1.g_ref.refs_20_), channel_id=1, source_target_pairs={{0,4},{8,0},{16,8},{24,16},{28,24},{20,28},{12,20},{4,12},{1,5},{9... | collective-permute-start | bytes 786440 | tf_op jit(solution)/shard_map/ppermute | solution.py:416
  157.0 1.3 copy-start.4
  158.3 1.2 copy-start.18
  158.3 31.2 %collective-permute-start.18 = (bf16[128,3584]{1,0:T(8,128)(2,1)}, bf16[128,3584]{1,0:T(8,128)(2,1)}, u32[]{:S(2)}, u32[]{:S(2)}) collective-permute-start(bf16[128,3584]{1,0:T(8,128)(2,1)} %get-tuple-element.35.refs_1_), channel_id=1, source_target_pairs={{0,2},{1,3},{2,0},{3,1},{4,6},{5,7},{6,4},{7,5},{8,10},{9,11},{10,... | collective-permute-start | bytes 2752520 | tf_op jit(solution)/shard_map/ppermute | solution.py:409
  160.2 8.2 %collective-permute-start.23 = (bf16[512,256]{1,0:T(8,128)(2,1)}, bf16[512,256]{1,0:T(8,128)(2,1)}, u32[]{:S(2)}, u32[]{:S(2)}) collective-permute-start(bf16[512,256]{1,0:T(8,128)(2,1)} %shard_map.138), channel_id=1, source_target_pairs={{0,8},{8,16},{16,24},{24,28},{28,20},{20,12},{12,4},{4,0},{1,9},{9... | collective-permute-start | bytes 786440 | tf_op jit(solution)/shard_map/ppermute | solution.py:416
  160.5 8.2 %collective-permute-start.27 = (bf16[512,256]{1,0:T(8,128)(2,1)}, bf16[512,256]{1,0:T(8,128)(2,1)S(1)}, u32[]{:S(2)}, u32[]{:S(2)}) collective-permute-start(bf16[512,256]{1,0:T(8,128)(2,1)} %shard_map.139), channel_id=1, source_target_pairs={{0,4},{8,0},{16,8},{24,16},{28,24},{20,28},{12,20},{4,12},{1,5},{9... | collective-permute-start | bytes 786440 | tf_op jit(solution)/shard_map/ppermute | solution.py:416
  168.4 7.2 %collective-permute-start.24 = (bf16[512,256]{1,0:T(8,128)(2,1)}, bf16[512,256]{1,0:T(8,128)(2,1)S(1)}, u32[]{:S(2)}, u32[]{:S(2)}) collective-permute-start(bf16[512,256]{1,0:T(8,128)(2,1)} %collective-permute-done.23.refs_23_), channel_id=1, source_target_pairs={{0,8},{8,16},{16,24},{24,28},{28,20},{20,12},{12,4},{4,0},{1,9},{9... | collective-permute-start | bytes 786440 | tf_op jit(solution)/shard_map/ppermute | solution.py:416
  168.7 7.3 %collective-permute-start.28 = (bf16[512,256]{1,0:T(8,128)(2,1)S(1)}, bf16[512,256]{1,0:T(8,128)(2,1)S(1)}, u32[]{:S(2)}, u32[]{:S(2)}) collective-permute-start(bf16[512,256]{1,0:T(8,128)(2,1)S(1)} %collective-permute-done.27.refs_24_), channel_id=1, source_target_pairs={{0,4},{8,0},{16,8},{24,16},{28,24},{20,28},{12,20},{4,12},{1,5},{9... | collective-permute-start | bytes 786440 | tf_op jit(solution)/shard_map/ppermute | solution.py:416
  175.6 10.2 %collective-permute-start.25 = (bf16[256,256]{1,0:T(8,128)(2,1)S(1)}, bf16[256,256]{1,0:T(8,128)(2,1)S(1)}, u32[]{:S(2)}, u32[]{:S(2)}) collective-permute-start(bf16[256,256]{1,0:T(8,128)(2,1)S(1)} %slice.18), channel_id=1, source_target_pairs={{0,8},{8,16},{16,24},{24,28},{28,20},{20,12},{12,4},{4,0},{1,9},{9... | collective-permute-start | bytes 393224 | tf_op jit(solution)/shard_map/ppermute | solution.py:416
  176.0 9.8 %collective-permute-start.29 = (bf16[256,256]{1,0:T(8,128)(2,1)S(1)}, bf16[256,256]{1,0:T(8,128)(2,1)S(1)}, u32[]{:S(2)}, u32[]{:S(2)}) collective-permute-start(bf16[256,256]{1,0:T(8,128)(2,1)S(1)} %slice.19), channel_id=1, source_target_pairs={{0,4},{8,0},{16,8},{24,16},{28,24},{20,28},{12,20},{4,12},{1,5},{9... | collective-permute-start | bytes 393224 | tf_op jit(solution)/shard_map/ppermute | solution.py:416
  185.8 3.7 %copy-start.5 = (f32[128,3584]{1,0:T(8,128)S(1)}, f32[128,3584]{1,0:T(8,128)}, u32[]{:S(2)}) copy-start(f32[128,3584]{1,0:T(8,128)} %copy-done.4) | copy-start | bytes 5505028
  (16 other events, 16.1 us)

commit v2 on v1

--- a/solution.py
+++ b/solution.py
@@ -19,6 +19,7 @@
 BF16 = jnp.bfloat16
 ANYWHERE = pl.BlockSpec(memory_space=pl.ANY)
 CYCLE = (0, 2, 4, 6, 7, 5, 3, 1)
+STEPS = (0, -1, 1, -2, 2, -3, 3, 4)
 
 
 def contract(a, b, da, db):
@@ -33,7 +34,7 @@
     return pl.BlockSpec(shape, lambda i, *prefetched: (0,) * len(shape))
 
 
-def call(body, grid, prefetched, operands, in_specs, out_specs, out_shape, flops, scratch=(), aliases=None, mib=32):
+def call(body, grid, prefetched, operands, in_specs, out_specs, out_shape, flops, scratch=(), aliases=None):
     moved = sum(x.size * x.dtype.itemsize for x in operands)
     return pl.pallas_call(
         body,
@@ -46,9 +47,18 @@
         ),
         out_shape=out_shape,
         input_output_aliases=aliases or {},
-        compiler_params=pltpu.CompilerParams(vmem_limit_bytes=mib * 1024 * 1024),
+        compiler_params=pltpu.CompilerParams(vmem_limit_bytes=56 * 1024 * 1024),
         cost_estimate=pl.CostEstimate(flops=flops, bytes_accessed=moved, transcendentals=0),
     )(*prefetched, *operands)
+
+
+def owner_at(me_f, by):
+    size = len(CYCLE)
+    half = size // 2
+    line, side = lax.div(me_f, 2), lax.rem(me_f, 2)
+    spot = jnp.where(side == 1, size - 1 - line, line)
+    spot = lax.rem(spot + (size + by), size)
+    return jnp.where(spot < half, 2 * spot, 2 * (size - 1 - spot) + 1)
 
 
 def after(x, *others):
@@ -98,27 +108,27 @@
     return mark[0], mark[1] * DIGIT + mark[2]
 
 
-def pack_kernel(heads_ref, q_ref, up_ref, out_ref):
+def pack_kernel(me_ref, q_ref, up_ref, out_ref):
     out_ref[0, 0] = q_ref[...]
     out_ref[0, 1] = up_ref[...]
 
 
-def pack_heads(heads, queries, upstream):
+def pack_heads(me, queries, upstream):
     rows = queries.shape[0]
-    by_head = pl.BlockSpec((rows, SPAN), lambda i, heads: (0, heads[i]))
+    by_head = pl.BlockSpec((rows, SPAN), lambda i, me: (0, me[0] ^ (1 + 2 * i)))
     return call(
         pack_kernel,
         2,
-        (heads,),
+        (me,),
         (queries, upstream),
         [by_head, by_head],
-        pl.BlockSpec((1, 2, rows, SPAN), lambda i, heads: (i, 0, 0, 0)),
+        pl.BlockSpec((1, 2, rows, SPAN), lambda i, me: (i, 0, 0, 0)),
         shaped((2, 2, rows, SPAN), BF16),
         0,
     )
 
 
-def place_kernel(heads_ref, near_ref, far_ref, att_in, gq_in, att_ref, gq_ref):
+def place_kernel(me_ref, near_ref, far_ref, att_in, gq_in, att_ref, gq_ref):
     step = pl.program_id(0)
     for i, ref in enumerate((near_ref, far_ref)):
 
@@ -128,13 +138,13 @@
             gq_ref[...] = ref[1]
 
 
-def place_heads(heads, near, far, attended, grad_queries):
+def place_heads(me, near, far, attended, grad_queries):
     rows = attended.shape[0]
-    by_head = pl.BlockSpec((rows, SPAN), lambda i, heads: (0, heads[i]))
+    by_head = pl.BlockSpec((rows, SPAN), lambda i, me: (0, me[0] ^ (1 + 2 * i)))
     return call(
         place_kernel,
         2,
-        (heads,),
+        (me,),
         (near, far, attended, grad_queries),
         [constant_block(near.shape)] * 2 + [ANYWHERE] * 2,
         [by_head, by_head],
@@ -144,7 +154,7 @@
     )
 
 
-def project_kernel(depth, count, halves, first, last, quarters_ref, owners_ref, *refs):
+def project_kernel(depth, count, halves, first, last, me_ref, *refs):
     parts, refs = refs[: 4 * count], refs[4 * count :]
     weights, refs = refs[: count + halves], refs[count + halves :]
     rows, lanes = parts[0].shape[1:]
@@ -163,7 +173,7 @@
         return
     kv_ref, kind_ref, ids_ref, ids_row_ref = refs
     for r in range(4):
-        here = pl.ds(pl.multiple_of(quarters_ref[r] * rows, rows), rows)
+        here = pl.ds(pl.multiple_of((me_ref[0] ^ r) * rows, rows), rows)
         kind, ids = read_marks(parts[r][0], depth)
         mine = slice(r * rows, (r + 1) * rows)
         kv_ref[here, :] = jnp.where(kind == 1.0, sums[1][mine], sums[0][mine]).astype(BF16)
@@ -172,13 +182,13 @@
     ids_row_ref[...] = jnp.broadcast_to(ids_ref[...], (4 * rows, 128)).T[:1]
 
 
-def project(quarters, owners, parts, weights, total, depth, last, halves):
+def project(me, steps, parts, weights, total, depth, last, halves):
     rows, lanes = parts[0].shape[1:]
     count = 1 if halves else len(weights)
     length = 4 * rows
     part_specs = [
-        pl.BlockSpec((1, rows, lanes), functools.partial(lambda b, i, q, o: (o[b], 0, 0), b))
-        for b in range(count)
+        pl.BlockSpec((1, rows, lanes), functools.partial(lambda by, i, me: (owner_at(me[1], by), 0, 0), by))
+        for by in steps
         for _ in range(4)
     ]
     full = (length, 2 * PAIR)
@@ -193,22 +203,22 @@
     return call(
         functools.partial(project_kernel, depth, count, int(halves), total is None, last),
         1,
-        (quarters, owners),
+        (me,),
         operands,
         part_specs + [constant_block(w.shape) for w in weights] + [constant_block(full)] * len(before),
         out_specs,
         out_shape,
         4 * length * depth * PAIR * count,
-        aliases={1 + len(operands): 0} if before and not last else None,
-    )
-
-
-def attend_kernel(spot, where_ref, q_ref, up_ref, pack_ref, kv_ref, ids_ref, ids_row_ref, *refs):
+        aliases={len(operands): 0} if before and not last else None,
+    )
+
+
+def attend_kernel(spot, me_ref, q_ref, up_ref, pack_ref, kv_ref, ids_ref, ids_row_ref, *refs):
     att_ref, gq_ref, other_ref, gkv_ref, bias, scores_all, dp_all, pbs, his, los = refs[-10:]
     rows = q_ref.shape[0]
     heads = [slice(h * HEAD_DIM, (h + 1) * HEAD_DIM) for h in range(GROUP)]
     for i in range(2):
-        here = pl.ds(pl.multiple_of(where_ref[1 + i] * rows, rows), rows)
+        here = pl.ds(pl.multiple_of((me_ref[0] ^ i) * rows, rows), rows)
         bias[i * rows : (i + 1) * rows, :] = jnp.where(ids_row_ref[...] <= ids_ref[here, :], 0.0, HIDDEN)
     keys = kv_ref[:, :HEAD_DIM]
     values = kv_ref[:, HEAD_DIM:]
@@ -243,21 +253,21 @@
     gkv_ref[:, HEAD_DIM:] = dv.T
 
 
-def attend(where, spot, queries, upstream, pack, kv, ids, ids_row, before=()):
+def attend(me, spot, queries, upstream, pack, kv, ids, ids_row, before=()):
     rows, width = queries.shape
     length = kv.shape[0]
-    by_head = pl.BlockSpec((rows, SPAN), lambda i, where: (0, where[0]))
+    by_head = pl.BlockSpec((rows, SPAN), lambda i, me: (0, me[0] ^ (2 * spot)))
     stacked = (2 * GROUP * rows, length)
     operands = (queries, upstream, pack, kv, ids, ids_row, *before)
     return call(
         functools.partial(attend_kernel, spot),
         1,
-        (where,),
+        (me,),
         operands,
         [
             by_head,
             by_head,
-            pl.BlockSpec((1, 2, rows, SPAN), lambda i, where: (spot, 0, 0, 0)),
+            pl.BlockSpec((1, 2, rows, SPAN), lambda i, me: (spot, 0, 0, 0)),
             constant_block((length, PAIR)),
             constant_block((length, 1)),
             constant_block((1, length)),
@@ -273,7 +283,6 @@
         16 * 2 * GROUP * rows * length * HEAD_DIM,
         scratch=[pltpu.VMEM((2 * rows, length), F32), pltpu.VMEM(stacked, F32)] + [pltpu.VMEM(stacked, BF16)] * 4,
         aliases={7 + i: i for i in range(len(before))},
-        mib=40,
     )
 
 
@@ -281,13 +290,13 @@
     return [jnp.where(kind == float(e), x, 0.0).astype(BF16) for e in range(2)]
 
 
-def hidden_kernel(quarters_ref, kind_ref, g_ref, gc_ref, w_ref, wc_ref, mine_ref, away_ref, masked):
+def hidden_kernel(me_ref, kind_ref, g_ref, gc_ref, w_ref, wc_ref, mine_ref, away_ref, masked):
     rows = mine_ref.shape[0]
 
     @pl.when(pl.program_id(0) == 0)
     def _():
         for i in range(2):
-            here = pl.ds(pl.multiple_of(quarters_ref[i] * rows, rows), rows)
+            here = pl.ds(pl.multiple_of((me_ref[0] ^ (2 * i)) * rows, rows), rows)
             for k, ref in enumerate((g_ref, gc_ref)):
                 for e, part in enumerate(by_expert(kind_ref[here, :], ref[here, :].astype(F32))):
                     masked[2 * k + e, i * rows : (i + 1) * rows, :] = part
@@ -295,12 +304,13 @@
     total = 0.0
     for k, ref in enumerate((w_ref, wc_ref)):
         for e in range(2):
-            total = total + contract(masked[2 * k + e], ref[:, e].reshape(-1, PAIR), 1, 1)
+            total = total + contract(ref[:, e].reshape(-1, PAIR), masked[2 * k + e], 1, 1)
+    total = total.T
     mine_ref[...] = total[:rows]
     away_ref[...] = total[rows:].astype(BF16)
 
 
-def hidden_grad(quarters, kind, grad, grad_c, weight, weight_c, rows):
+def hidden_grad(me, kind, grad, grad_c, weight, weight_c, rows):
     count, _, depth, _ = weight.shape
     length = grad.shape[0]
     group = count // 4
@@ -310,7 +320,7 @@
     return call(
         hidden_kernel,
         4,
-        (quarters,),
+        (me,),
         (kind, grad, grad_c, weight, weight_c),
         [constant_block((length, 1)), constant_block((length, PAIR)), constant_block((length, PAIR)), by_tile, by_tile],
         [out, out],
@@ -320,7 +330,7 @@
     )
 
 
-def weight_kernel(depth, count, halves, first, last, quarters_ref, owners_ref, *refs):
+def weight_kernel(depth, count, halves, first, last, me_ref, *refs):
     parts, refs = refs[: 4 * count], refs[4 * count :]
     grads, refs = refs[: count + halves], refs[count + halves :]
     rows, lanes = parts[0].shape[1:]
@@ -330,7 +340,7 @@
         left = jnp.concatenate([ref[0] for ref in parts[4 * b : 4 * b + 4]], axis=0)
         quarter = []
         for r in range(4):
-            start = quarters_ref[r] * rows
+            start = (me_ref[0] ^ r) * rows
             if halves:
                 inner = pl.ds(pl.multiple_of(lax.rem(start, size), rows), rows)
                 quarter.append(jnp.where(start < size, grads[0][inner, :].astype(F32), grads[1][inner, :].astype(F32)))
@@ -349,12 +359,12 @@
         refs[0][e] = total[:depth, e * PAIR : (e + 1) * PAIR]
 
 
-def weight_grad(quarters, owners, parts, grads, total, depth, last, halves):
+def weight_grad(me, steps, parts, grads, total, depth, last, halves):
     rows, lanes = parts[0].shape[1:]
     count = 1 if halves else len(grads)
     part_specs = [
-        pl.BlockSpec((1, rows, lanes), functools.partial(lambda b, i, q, o: (o[b], 0, 0), b))
-        for b in range(count)
+        pl.BlockSpec((1, rows, lanes), functools.partial(lambda by, i, me: (owner_at(me[1], by), 0, 0), by))
+        for by in steps
         for _ in range(4)
     ]
     full = (lanes, 2 * PAIR)
@@ -364,13 +374,43 @@
     return call(
         functools.partial(weight_kernel, depth, count, int(halves), total is None, last),
         1,
-        (quarters, owners),
+        (me,),
         operands,
         part_specs + [constant_block(g.shape) for g in grads] + [constant_block(full)] * len(before),
         constant_block(out),
         shaped(out, F32),
         16 * rows * lanes * PAIR * count,
-        aliases={1 + len(operands): 0} if before and not last else None,
+        aliases={len(operands): 0} if before and not last else None,
+    )
+
+
+def gather_kernel(me_ref, *refs):
+    blocks, whole_ref, sems = refs[:-2], refs[-2], refs[-1]
+    size = blocks[-1].shape[1]
+    copies = []
+    for i, block in enumerate(blocks):
+        owner = owner_at(me_ref[1], STEPS[min(i, len(STEPS) - 1)])
+        there = whole_ref.at[owner]
+        if i >= len(STEPS) - 1:
+            there = whole_ref.at[owner, :, pl.ds((i - len(STEPS) + 1) * size, size), :]
+        copies.append(pltpu.make_async_copy(block, there, sems.at[i]))
+    for copy in copies:
+        copy.start()
+    for copy in copies:
+        copy.wait()
+
+
+def gather_blocks(me, blocks):
+    return call(
+        gather_kernel,
+        1,
+        (me,),
+        tuple(blocks),
+        [ANYWHERE] * len(blocks),
+        ANYWHERE,
+        shaped((len(CYCLE), *blocks[0].shape), blocks[0].dtype),
+        0,
+        scratch=[pltpu.SemaphoreType.DMA((len(blocks),))],
     )
 
 
@@ -408,78 +448,66 @@
     def swap(x, bit):
         return lax.ppermute(x, "seq", [(i, i ^ bit) for i in range(seq)])
 
-    def over_seq(x):
-        across = swap(x, 2)
-        return [x, swap(x, 1), across, swap(across, 1)]
-
     def turn(x, by):
         return lax.ppermute(x, "fsdp", [(CYCLE[i], CYCLE[(i + by) % fsdp]) for i in range(fsdp)])
 
-    if near_link:
-        spot = jnp.array([CYCLE.index(i) for i in range(fsdp)], jnp.int32)[me_f]
-        order = jnp.array(CYCLE, jnp.int32)
-        around = [order[lax.rem(spot + fsdp + by, fsdp)] for by in (0, -1, 1, -2, 2, -3, 3, 4)]
-
-    def round_cycle(x, cut, hold=None):
-        ups, downs = x, x
-        found = [x]
-        for step in range(1, 5):
-            if step == 4:
-                size = x.shape[cut] // 2
-                ups = lax.slice_in_dim(ups, 0, size, axis=cut)
-                downs = lax.slice_in_dim(downs, size, 2 * size, axis=cut)
-            if step == 2 and hold is not None:
-                ups, downs = after(ups, hold), after(downs, hold)
-            ups, downs = turn(ups, 1), turn(downs, -1)
-            found += [ups, downs]
-        return found
-
+    def both_ways(ups, downs):
+        return turn(ups, 1), turn(downs, -1)
+
+    def halves(ups, downs, axis):
+        size = ups.shape[axis] // 2
+        return lax.slice_in_dim(ups, 0, size, axis=axis), lax.slice_in_dim(downs, size, 2 * size, axis=axis)
+
+    def exchange_columns(x):
+        return lax.all_to_all(x, "fsdp", split_axis=0, concat_axis=0, tiled=True)
+
+    me = jnp.stack([me_s, me_f])
     quarters = me_s ^ jnp.arange(seq, dtype=jnp.int32)
     if near_link:
-        weights = round_cycle(kv_weight, 1)
+        weights = [kv_weight, *both_ways(kv_weight, kv_weight)]
     else:
         weight = lax.all_gather(kv_weight, "fsdp", axis=0)
 
-    own_blocks = token_blocks(tokens, modality.reshape(rows, 1), block_ids.reshape(rows, 1), fsdp)
-    parts = over_seq(own_blocks)
-    pack = swap(pack_heads(me_s ^ jnp.array([1, 3], jnp.int32), queries, cotangent), 1)
-    columns = over_seq(lax.all_to_all(own_blocks, "fsdp", split_axis=0, concat_axis=0, tiled=True))
+    blocks = token_blocks(tokens, modality.reshape(rows, 1), block_ids.reshape(rows, 1), fsdp)
+    across = swap(blocks, 2)
+    parts = [blocks, swap(blocks, 1), across, swap(across, 1)]
+    pack = swap(pack_heads(me, queries, cotangent), 1)
+    columns = exchange_columns(blocks)
+    columns_across = exchange_columns(across)
 
     if near_link:
-        groups = ((0, 5), (5, 7), (7, 8))
-        owners = [jnp.stack(around[a:b]) for a, b in groups]
-        total = project(quarters, owners[0], parts, weights[:5], None, depth, False, False)
-        total = project(quarters, owners[1], parts, weights[5:7], total, depth, False, False)
-        kv, kind, ids, ids_row = project(quarters, owners[2], parts, weights[7:], total, depth, True, True)
-        weight = jnp.zeros((fsdp, *kv_weight.shape), BF16)
-        for owner, block in zip(around, weights[:7]):
-            weight = lax.dynamic_update_index_in_dim(weight, block, owner, 0)
-        for i, block in enumerate(weights[7:]):
-            weight = lax.dynamic_update_slice(weight, block[None], (around[7], 0, i * (depth // 2), 0))
+        ups, downs = after(weights[1], parts[1], pack), after(weights[2], parts[1], pack)
+        weights += both_ways(ups, downs)
+        weights += both_ways(*weights[3:])
+        ups, downs = halves(*weights[5:], 1)
+        weights += both_ways(after(ups, parts[3], columns), after(downs, parts[3], columns))
+        total = project(me, STEPS[:5], parts, weights[:5], None, depth, False, False)
+        total = project(me, STEPS[5:7], parts, weights[5:7], total, depth, False, False)
+        kv, kind, ids, ids_row = project(me, STEPS[7:], parts, weights[7:], total, depth, True, True)
+        weight = gather_blocks(me, weights[:6] + [after(weights[6], kv)] + weights[7:])
     else:
         kv, kind, ids, ids_row = project_plain(quarters, parts, weight, depth)
     weight_c = swap(weight, 1)
 
-    where_near = jnp.stack([me_s, me_s, me_s ^ 1])
-    where_far = jnp.stack([me_s ^ 2, me_s, me_s ^ 1])
     kv_far = swap(kv, 2)
-    attended, grad_queries, other_near, near = attend(where_near, 0, queries, cotangent, pack, kv, ids, ids_row)
+    attended, grad_queries, other_near, near = attend(me, 0, queries, cotangent, pack, kv, ids, ids_row)
     attended, grad_queries, other_far, far = attend(
-        where_far, 1, queries, cotangent, pack, kv_far, ids, ids_row, (attended, grad_queries)
-    )
-    grad_kv = (near + swap(far, 2)).astype(BF16)
-    attended, grad_queries = place_heads(
-        me_s ^ jnp.array([1, 3], jnp.int32), swap(other_near, 1), swap(other_far, 1), attended, grad_queries
-    )
-
-    mine, away = hidden_grad(
-        jnp.stack([me_s, me_s ^ 2]), kind, grad_kv, swap(grad_kv, 1), weight, weight_c, rows
-    )
+        me, 1, queries, cotangent, pack, kv_far, ids, ids_row, (attended, grad_queries)
+    )
+    grad_kv = (after(near, columns_across) + swap(far, 2)).astype(BF16)
+    attended, grad_queries = place_heads(me, swap(other_near, 1), swap(other_far, 1), attended, grad_queries)
+
+    mine, away = hidden_grad(me, kind, grad_kv, swap(grad_kv, 1), weight, weight_c, rows)
+    columns = [columns, swap(columns, 1), columns_across, swap(columns_across, 1)]
     if near_link:
-        grads = round_cycle(grad_kv, 0, away)
-        total = weight_grad(quarters, owners[0], columns, grads[:5], None, depth, False, False)
-        total = weight_grad(quarters, owners[1], columns, grads[5:7], total, depth, False, False)
-        grad_weight = weight_grad(quarters, owners[2], columns, grads[7:], total, depth, True, True)
+        first = after(grad_kv, away)
+        grads = [first, *both_ways(first, first)]
+        grads += both_ways(*grads[1:])
+        grads += both_ways(*grads[3:])
+        grads += both_ways(*halves(*grads[5:], 0))
+        total = weight_grad(me, STEPS[:5], columns, grads[:5], None, depth, False, False)
+        total = weight_grad(me, STEPS[5:7], columns, grads[5:7], total, depth, False, False)
+        grad_weight = weight_grad(me, STEPS[7:], columns, grads[7:], total, depth, True, True)
     else:
         grad_weight = weight_plain(quarters, columns, lax.all_gather(grad_kv, "fsdp", axis=0), depth)
     grad_tokens = (mine + swap(away, 2).astype(F32)).astype(BF16)

time: 193 us -> 302 us (1.56)
  Pallas kernels: 43.6 us -> 170 us
  between operations: 21.2 us -> 0.83 us
  local copies, waits for them, and re-layouts: 35 us -> 16.2 us
  waiting for transfers between devices: 57.1 us -> 71.5 us
  starting transfers between devices: 30.9 us -> 39 us
    pallas_call x12 -> x13, Pallas kernels: 43.6 us -> 170 us  [call(): pl.pallas_call(body, grid_spec=pltpu.PrefetchScalarGridSpec(num_scalar_pr...]
    ppermute x16, waiting for transfers between devices: 32.8 us -> 46.5 us  [turn(): lax.ppermute(x, 'fsdp', [(CYCLE[i], CYCLE[(i + by) % fsdp]) for i in rang...]
    all_to_all x1 -> x2, waiting for transfers between devices: 0.87 us -> 9.73 us  [exchange_columns(): return lax.all_to_all(x, 'fsdp', split_axis=0, concat_axis=0, tiled=True)]
    ppermute x14 -> x13, waiting for transfers between devices: 23.4 us -> 15.3 us  [swap(): return lax.ppermute(x, 'seq', [(i, i ^ bit) for i in range(seq)])]
    dynamic_update_slice x9 -> x0, local copies, waits for them, and re-layouts: 7.16 us -> none  [the longest x7 5.68 us: per_device(): weight = lax.dynamic_update_index_in_dim(weight, block, owner, 0)]
    unnamed x68 -> x56, local copies, waits for them, and re-layouts: 18 us -> 11.9 us
    all_to_all x1 -> x2, starting transfers between devices: 4.92 us -> 9.87 us  [exchange_columns(): return lax.all_to_all(x, 'fsdp', split_axis=0, concat_axis=0, tiled=True)]
    another operation x1 -> x0, local copies, waits for them, and re-layouts: 3.19 us -> none  [per_device(): owners = [jnp.stack(around[a:b]) for a, b in groups]]
  transfers between devices with their start and end apart: 31 -> 31, of which waited for: 9 -> 13; matrix products, arithmetic and copies ran while one was open for 10% -> 2% of each run, Pallas kernels for 23% -> 16%
where the time goes in v2:
time: 302 us; the launch traced here: 301 us
  Pallas kernels  170 us (56%)
  waiting for transfers between devices  71.5 us (24%)
  starting transfers between devices  39 us (13%)
  local copies, waits for them, and re-layouts  16.2 us (5%)
  other arithmetic  4.01 us (1%)
    pallas_call x13, Pallas kernels, call(): pl.pallas_call(body, grid_spec=pltpu.PrefetchScalarGridSpec(num_scalar_pr...  170 us
    ppermute x16, waiting for transfers between devices, turn(): lax.ppermute(x, 'fsdp', [(CYCLE[i], CYCLE[(i + by) % fsdp]) for i in rang...  46.5 us
    ppermute x16, starting transfers between devices, turn(): lax.ppermute(x, 'fsdp', [(CYCLE[i], CYCLE[(i + by) % fsdp]) for i in rang...  22.2 us
    ppermute x13, waiting for transfers between devices, swap(): return lax.ppermute(x, 'seq', [(i, i ^ bit) for i in range(seq)])  15.3 us
    unnamed x56, local copies, waits for them, and re-layouts  11.9 us
    all_to_all x2, starting transfers between devices, exchange_columns(): return lax.all_to_all(x, 'fsdp', split_axis=0, concat_axis=0, tiled=True)  9.87 us
    all_to_all x2, waiting for transfers between devices, exchange_columns(): return lax.all_to_all(x, 'fsdp', split_axis=0, concat_axis=0, tiled=True)  9.73 us
    ppermute x13, starting transfers between devices, swap(): return lax.ppermute(x, 'seq', [(i, i ^ bit) for i in range(seq)])  6.98 us
  transfers between devices with their start and end apart: 31, of which 13 were waited for; matrix products, arithmetic and copies ran while one was open for 2% of the time, Pallas kernels for 16%

profile of v2, /device:TPU:0, one launch (start us, length us, event | category | flops | bytes accessed | tf_op | source)
XLA Modules:
  0.0 301.2 jit_solution(11284867100066895163)
XLA Ops:
  0.6 1.4 copy.23.kind_ref
  2.0 1.4 copy.24.ids_ref
  3.4 2.6 shard_map.94.refs_0_.refs_4_.refs_8_.refs_12_.refs_16_
  6.0 3.0 collective-permute-start.2
  9.6 2.8 shard_map.93
  12.9 5.8 %all-to-all-start = ((bf16[8,128,512]{2,1,0:T(8,128)(2,1)}), bf16[8,128,512]{2,1,0:T(8,128)(2,1)S(1)}, u32[]{:S(2)}, u32[]{:S(2)}) async-start(bf16[8,128,512]{2,1,0:T(8,128)(2,1)} %shard_map.94.refs_0_.refs_4_.refs_8_.refs_12_.refs_16_), calls=%async_computation | async-start | bytes 2097152 | tf_op jit(solution)/shard_map/all_to_all | solution.py:462
  18.7 2.0 collective-permute-start.4
  20.8 11.7 %collective-permute-done.2.refs_2_.refs_6_.refs_10_.refs_14_.refs_18_ = bf16[8,128,512]{2,1,0:T(8,128)(2,1)} collective-permute-done((bf16[8,128,512]{2,1,0:T(8,128)(2,1)}, bf16[8,128,512]{2,1,0:T(8,128)(2,1)}, u32[]{:S(2)}, u32[]{:S(2)}) %collective-permute-start.2) | collective-permute-done | bytes 1048608 | tf_op jit(solution)/shard_map/ppermute | solution.py:449
  32.4 13.8 %collective-permute-done.4.refs_21_.refs_1_ = bf16[2,448,256]{2,1,0:T(8,128)(2,1)S(1)} collective-permute-done((bf16[2,448,256]{2,1,0:T(8,128)(2,1)}, bf16[2,448,256]{2,1,0:T(8,128)(2,1)S(1)}, u32[]{:S(2)}, u32[]{:S(2)}) %collective-permute-start.4) | collective-permute-done | bytes 458784 | tf_op jit(solution)/shard_map/ppermute | solution.py:452
  46.3 0.8 copy.25.refs_0_
  47.1 0.9 collective-permute-done.8.refs_22_.refs_2_
  48.0 0.8 copy.27.refs_0_
  48.9 1.0 copy-done.4
  49.9 7.1 %collective-permute-start.5 = (bf16[2,448,256]{2,1,0:T(8,128)(2,1)}, bf16[2,448,256]{2,1,0:T(8,128)(2,1)}, u32[]{:S(2)}, u32[]{:S(2)}) collective-permute-start(bf16[2,448,256]{2,1,0:T(8,128)(2,1)} %shard_map.95), channel_id=1, source_target_pairs={{0,8},{8,16},{16,24},{24,28},{28,20},{20,12},{12,4},{4,0},{1,9},{9... | collective-permute-start | bytes 1376264 | tf_op jit(solution)/shard_map/ppermute | solution.py:452
  57.0 9.3 %collective-permute-done.5.refs_23_.refs_3_ = bf16[2,448,256]{2,1,0:T(8,128)(2,1)} collective-permute-done((bf16[2,448,256]{2,1,0:T(8,128)(2,1)}, bf16[2,448,256]{2,1,0:T(8,128)(2,1)}, u32[]{:S(2)}, u32[]{:S(2)}) %collective-permute-start.5) | collective-permute-done | bytes 458784 | tf_op jit(solution)/shard_map/ppermute | solution.py:452
  66.3 2.5 collective-permute-start.6
  69.3 9.3 %collective-permute-done.6.refs_8_.refs_5_ = bf16[2,448,256]{2,1,0:T(8,128)(2,1)S(1)} collective-permute-done((bf16[2,448,256]{2,1,0:T(8,128)(2,1)}, bf16[2,448,256]{2,1,0:T(8,128)(2,1)S(1)}, u32[]{:S(2)}, u32[]{:S(2)}) %collective-permute-start.6) | collective-permute-done | bytes 458784 | tf_op jit(solution)/shard_map/ppermute | solution.py:452
  79.4 1.4 collective-permute-done.10.refs_9_.refs_0_
  81.5 1.0 copy-done
  82.5 1.0 copy-done.3
  83.5 1.7 collective-permute-start.7
  85.5 5.6 %shard_map.99.refs_10_ = f32[512,512]{1,0:T(8,128)} custom-call(s32[2]{0:T(128)} %pad_add_fusion.me_ref, bf16[8,128,512]{2,1,0:T(8,128)(2,1)} %shard_map.94.refs_0_.refs_4_.refs_8_.refs_12_.refs_16_, bf16[8,128,512]{2,1,0:T(8,128)(2,1)} %copy-done.4, bf16[8,128,512]{2,1,0:T(8,128)(2,1)} %collective-permute-done.2.refs_2_.refs_6_.refs_10_.refs_14_.refs_18_, ...), custom_call_target="tpu_custom_call" | custom-call | flops 1174405120 | bytes 23265280 | tf_op jit(solution)/shard_map/pallas_call | solution.py:39
  91.2 4.3 %shard_map.100.refs_6_ = f32[512,512]{1,0:T(8,128)} custom-call(s32[2]{0:T(128)} %pad_add_fusion.me_ref, bf16[8,128,512]{2,1,0:T(8,128)(2,1)} %shard_map.94.refs_0_.refs_4_.refs_8_.refs_12_.refs_16_, bf16[8,128,512]{2,1,0:T(8,128)(2,1)} %copy-done.4, ...), custom_call_target="tpu_custom_call", output_to_operand_aliasing={{}: (11, {})} | custom-call | flops 469762048 | bytes 10354688 | tf_op jit(solution)/shard_map/pallas_call | solution.py:39
  96.8 3.5 %shard_map.101 = (bf16[512,256]{1,0:T(8,128)(2,1)}, f32[512,1]{1,0:T(8,128)}, f32[512,1]{1,0:T(8,128)}, f32[1,512]{1,0:T(1,128)}) custom-call(s32[2]{0:T(128)} %pad_add_fusion.me_ref, bf16[8,128,512]{2,1,0:T(8,128)(2,1)} %shard_map.94.refs_0_.refs_4_.refs_8_.refs_12_.refs_16_, bf16[8,128,512]{2,1,0:T(8,128)(2,1)} %copy-done.4, ...), custom_call_target="tpu_custom_call" | custom-call | flops 234881024 | bytes 5701632 | tf_op jit(solution)/shard_map/pallas_call | solution.py:39
  100.3 113.0 %shard_map.107.w_ref = bf16[8,2,448,256]{3,2,1,0:T(8,128)(2,1)} custom-call(s32[2]{0:T(128)} %pad_add_fusion.me_ref, bf16[2,448,256]{2,1,0:T(8,128)(2,1)} %refs_0_.1, bf16[2,448,256]{2,1,0:T(8,128)(2,1)} %copy-done.9, bf16[2,448,256]{2,1,0:T(8,128)(2,1)} %copy-done.10, bf16[2,448,256]{2,1,0:T(8,128)(2,1)} %collective-permute-done.5.refs_23_.refs_3_, ...), custom_call_target="tpu_custom_call" | custom-call | bytes 3670016 | tf_op jit(solution)/shard_map/pallas_call | solution.py:39
  213.4 4.1 %all-to-all-start.1 = ((bf16[8,128,512]{2,1,0:T(8,128)(2,1)}), bf16[8,128,512]{2,1,0:T(8,128)(2,1)S(1)}, u32[]{:S(2)}, u32[]{:S(2)}) async-start(bf16[8,128,512]{2,1,0:T(8,128)(2,1)} %collective-permute-done.2.refs_2_.refs_6_.refs_10_.refs_14_.refs_18_), calls=%async_computation.1 | async-start | bytes 2097152 | tf_op jit(solution)/shard_map/all_to_all | solution.py:462
  218.0 6.9 %shard_map.102 = (bf16[128,3584]{1,0:T(8,128)(2,1)}, bf16[128,3584]{1,0:T(8,128)(2,1)}, bf16[2,128,896]{2,1,0:T(8,128)(2,1)}, f32[512,256]{1,0:T(8,128)}) custom-call(s32[2]{0:T(128)} %pad_add_fusion.me_ref, bf16[128,3584]{1,0:T(8,128)(2,1)} %bitcast.13, bf16[128,3584]{1,0:T(8,128)(2,1)} %bitcast.16, ...), custom_call_target="tpu_custom_call" | custom-call | flops 1879048192 | bytes 3018752 | tf_op jit(solution)/shard_map/pallas_call | solution.py:39
  225.0 1.0 collective-permute-done.13.kv_ref
  226.7 6.9 %shard_map.103 = (bf16[128,3584]{1,0:T(8,128)(2,1)}, bf16[128,3584]{1,0:T(8,128)(2,1)}, bf16[2,128,896]{2,1,0:T(8,128)(2,1)}, f32[512,256]{1,0:T(8,128)}) custom-call(s32[2]{0:T(128)} %pad_add_fusion.me_ref, bf16[128,3584]{1,0:T(8,128)(2,1)} %bitcast.14, bf16[128,3584]{1,0:T(8,128)(2,1)} %bitcast.17, ...), custom_call_target="tpu_custom_call", output_to_operand_aliasing={{0}: (7, {}), {1}: (8, {})} | custom-call | flops 1879048192 | bytes 4853760 | tf_op jit(solution)/shard_map/pallas_call | solution.py:39
  234.2 9.7 %all-to-all-done.1.refs_1_.refs_2_.refs_6_.refs_10_.refs_14_.refs_18_ = bf16[8,128,512]{2,1,0:T(8,128)(2,1)S(1)} async-done(((bf16[8,128,512]{2,1,0:T(8,128)(2,1)}), bf16[8,128,512]{2,1,0:T(8,128)(2,1)S(1)}, u32[]{:S(2)}, u32[]{:S(2)}) %all-to-all-start.1) | async-done | bytes 1048608 | tf_op jit(solution)/shard_map/all_to_all | solution.py:462
  243.9 1.0 copy-done.2
  244.9 2.2 collective-permute-done.15
  247.0 1.1 add_convert_fusion.1.g_ref.refs_0_
  250.4 7.5 %shard_map.108 = (f32[128,3584]{1,0:T(8,128)}, bf16[128,3584]{1,0:T(8,128)(2,1)}) custom-call(s32[2]{0:T(128)} %pad_add_fusion.me_ref, f32[512,1]{1,0:T(8,128)} %get-tuple-element.31.kind_ref, bf16[512,256]{1,0:T(8,128)(2,1)} %copy-done.8, bf16[512,256]{1,0:T(8,128)(2,1)} %copy-done.22, bf16[8,2,448,256]{3,2,1,0:T(8,128)(2,1)} %shard_map.107.w_ref, ...), custom_call_target="tpu_custom_call" | custom-call | flops 1879048192 | bytes 7866368 | tf_op jit(solution)/shard_map/pallas_call | solution.py:39
  258.0 1.1 collective-permute-start.18
  259.1 1.7 collective-permute-start.21
  261.1 6.2 %collective-permute-done.21.refs_21_ = bf16[512,256]{1,0:T(8,128)(2,1)S(1)} collective-permute-done((bf16[512,256]{1,0:T(8,128)(2,1)}, bf16[512,256]{1,0:T(8,128)(2,1)S(1)}, u32[]{:S(2)}, u32[]{:S(2)}) %collective-permute-start.21) | collective-permute-done | bytes 262176 | tf_op jit(solution)/shard_map/ppermute | solution.py:452
  267.3 1.7 collective-permute-start.22
  269.4 5.3 %collective-permute-done.22.refs_23_ = bf16[512,256]{1,0:T(8,128)(2,1)S(1)} collective-permute-done((bf16[512,256]{1,0:T(8,128)(2,1)S(1)}, bf16[512,256]{1,0:T(8,128)(2,1)S(1)}, u32[]{:S(2)}, u32[]{:S(2)}) %collective-permute-start.22) | collective-permute-done | bytes 262176 | tf_op jit(solution)/shard_map/ppermute | solution.py:452
  274.7 1.7 collective-permute-start.23
  276.7 2.8 shard_map.104
  279.6 1.0 copy-done.5
  280.5 1.0 copy-done.6
  281.5 5.7 %shard_map.110.refs_10_ = f32[512,512]{1,0:T(8,128)} custom-call(s32[2]{0:T(128)} %pad_add_fusion.me_ref, bf16[8,128,512]{2,1,0:T(8,128)(2,1)} %copy-done, bf16[8,128,512]{2,1,0:T(8,128)(2,1)} %copy-done.5, bf16[8,128,512]{2,1,0:T(8,128)(2,1)} %copy-done.2, bf16[8,128,512]{2,1,0:T(8,128)(2,1)} %copy-done.6, bf16[8,128,512]{2,1,0:T(8,128)(2,1)} %copy-done, ...), custom_call_target="tpu_custom_call" | custom-call | flops 1342177280 | bytes 22282240 | tf_op jit(solution)/shard_map/pallas_call | solution.py:39
  287.3 1.7 collective-permute-start.24
  289.7 4.4 %shard_map.111.refs_6_ = f32[512,512]{1,0:T(8,128)} custom-call(s32[2]{0:T(128)} %pad_add_fusion.me_ref, bf16[8,128,512]{2,1,0:T(8,128)(2,1)} %copy-done, bf16[8,128,512]{2,1,0:T(8,128)(2,1)} %copy-done.5, bf16[8,128,512]{2,1,0:T(8,128)(2,1)} %copy-done.2, bf16[8,128,512]{2,1,0:T(8,128)(2,1)} %copy-done.6, ...), custom_call_target="tpu_custom_call", output_to_operand_aliasing={{}: (11, {})} | custom-call | flops 536870912 | bytes 9961472 | tf_op jit(solution)/shard_map/pallas_call | solution.py:39
  294.1 2.3 fusion
  297.6 3.6 %shard_map.112 = f32[2,448,256]{2,1,0:T(8,128)} custom-call(s32[2]{0:T(128)} %pad_add_fusion.me_ref, bf16[8,128,512]{2,1,0:T(8,128)(2,1)} %copy-done, bf16[8,128,512]{2,1,0:T(8,128)(2,1)} %copy-done.5, bf16[8,128,512]{2,1,0:T(8,128)(2,1)} %copy-done.2, bf16[8,128,512]{2,1,0:T(8,128)(2,1)} %copy-done.6, bf16[256,256]{1,0:T(8,128)(2,1)} %copy-done.24, ...), custom_call_target="tpu_custom_call" | custom-call | flops 268435456 | bytes 5505024 | tf_op jit(solution)/shard_map/pallas_call | solution.py:39
  (99 shorter events, 12.4 us)
Async XLA Ops:
  6.0 26.4 %collective-permute-start.2 = (bf16[8,128,512]{2,1,0:T(8,128)(2,1)}, bf16[8,128,512]{2,1,0:T(8,128)(2,1)}, u32[]{:S(2)}, u32[]{:S(2)}) collective-permute-start(bf16[8,128,512]{2,1,0:T(8,128)(2,1)} %shard_map.94.refs_0_.refs_4_.refs_8_.refs_12_.refs_16_), channel_id=1, source_target_pairs={{0,2},{1,3},{2,0},{3,1},{4,6},{5,7},{6,4},{7,5},{8,10},{9,11},{10,... | collective-permute-start | bytes 3145736 | tf_op jit(solution)/shard_map/ppermute | solution.py:449
  8.9 40.0 %collective-permute-start.1 = (bf16[8,128,512]{2,1,0:T(8,128)(2,1)}, bf16[8,128,512]{2,1,0:T(8,128)(2,1)S(1)}, u32[]{:S(2)}, u32[]{:S(2)}) collective-permute-start(bf16[8,128,512]{2,1,0:T(8,128)(2,1)} %shard_map.94.refs_0_.refs_4_.refs_8_.refs_12_.refs_16_), channel_id=1, source_target_pairs={{0,1},{1,0},{2,3},{3,2},{4,5},{5,4},{6,7},{7,6},{8,9},{9,8},{10,11... | collective-permute-start | bytes 3145736 | tf_op jit(solution)/shard_map/ppermute | solution.py:449
  12.4 36.4 %collective-permute-start = (bf16[2,2,128,896]{3,2,1,0:T(8,128)(2,1)}, bf16[2,2,128,896]{3,2,1,0:T(8,128)(2,1)}, u32[]{:S(2)}, u32[]{:S(2)}) collective-permute-start(bf16[2,2,128,896]{3,2,1,0:T(8,128)(2,1)} %shard_map.93), channel_id=1, source_target_pairs={{0,1},{1,0},{2,3},{3,2},{4,5},{5,4},{6,7},{7,6},{8,9},{9,8},{10,11... | collective-permute-start | bytes 2752520 | tf_op jit(solution)/shard_map/ppermute | solution.py:449
  12.9 68.6 %all-to-all-start = ((bf16[8,128,512]{2,1,0:T(8,128)(2,1)}), bf16[8,128,512]{2,1,0:T(8,128)(2,1)S(1)}, u32[]{:S(2)}, u32[]{:S(2)}) async-start(bf16[8,128,512]{2,1,0:T(8,128)(2,1)} %shard_map.94.refs_0_.refs_4_.refs_8_.refs_12_.refs_16_), calls=%async_computation | async-start | bytes 2097152 | tf_op jit(solution)/shard_map/all_to_all | solution.py:462
  18.7 27.6 %collective-permute-start.4 = (bf16[2,448,256]{2,1,0:T(8,128)(2,1)}, bf16[2,448,256]{2,1,0:T(8,128)(2,1)S(1)}, u32[]{:S(2)}, u32[]{:S(2)}) collective-permute-start(bf16[2,448,256]{2,1,0:T(8,128)(2,1)} %refs_0_.1), channel_id=1, source_target_pairs={{0,8},{8,16},{16,24},{24,28},{28,20},{20,12},{12,4},{4,0},{1,9},{9... | collective-permute-start | bytes 1376264 | tf_op jit(solution)/shard_map/ppermute | solution.py:452
  20.7 27.2 %collective-permute-start.8 = (bf16[2,448,256]{2,1,0:T(8,128)(2,1)}, bf16[2,448,256]{2,1,0:T(8,128)(2,1)S(1)}, u32[]{:S(2)}, u32[]{:S(2)}) collective-permute-start(bf16[2,448,256]{2,1,0:T(8,128)(2,1)} %refs_0_.1), channel_id=1, source_target_pairs={{0,4},{8,0},{16,8},{24,16},{28,24},{20,28},{12,20},{4,12},{1,5},{9... | collective-permute-start | bytes 1376264 | tf_op jit(solution)/shard_map/ppermute | solution.py:452
  32.4 49.1 %collective-permute-start.3 = (bf16[8,128,512]{2,1,0:T(8,128)(2,1)}, bf16[8,128,512]{2,1,0:T(8,128)(2,1)S(1)}, u32[]{:S(2)}, u32[]{:S(2)}) collective-permute-start(bf16[8,128,512]{2,1,0:T(8,128)(2,1)} %collective-permute-done.2.refs_2_.refs_6_.refs_10_.refs_14_.refs_18_), channel_id=1, source_target_pairs={{0,1},{1,0},{2,3},{3,2},{4,5},{5,4},{6,7},{7,6},{8,9},{9,8},{10,11... | collective-permute-start | bytes 3145736 | tf_op jit(solution)/shard_map/ppermute | solution.py:449
  46.3 2.5 copy-start.9
  48.9 1.0 copy-start.4
  49.9 16.4 %collective-permute-start.5 = (bf16[2,448,256]{2,1,0:T(8,128)(2,1)}, bf16[2,448,256]{2,1,0:T(8,128)(2,1)}, u32[]{:S(2)}, u32[]{:S(2)}) collective-permute-start(bf16[2,448,256]{2,1,0:T(8,128)(2,1)} %shard_map.95), channel_id=1, source_target_pairs={{0,8},{8,16},{16,24},{24,28},{28,20},{20,12},{12,4},{4,0},{1,9},{9... | collective-permute-start | bytes 1376264 | tf_op jit(solution)/shard_map/ppermute | solution.py:452
  57.0 12.0 %collective-permute-start.9 = (bf16[2,448,256]{2,1,0:T(8,128)(2,1)}, bf16[2,448,256]{2,1,0:T(8,128)(2,1)S(1)}, u32[]{:S(2)}, u32[]{:S(2)}) collective-permute-start(bf16[2,448,256]{2,1,0:T(8,128)(2,1)} %shard_map.97), channel_id=1, source_target_pairs={{0,4},{8,0},{16,8},{24,16},{28,24},{20,28},{12,20},{4,12},{1,5},{9... | collective-permute-start | bytes 1376264 | tf_op jit(solution)/shard_map/ppermute | solution.py:452
  66.3 12.3 %collective-permute-start.6 = (bf16[2,448,256]{2,1,0:T(8,128)(2,1)}, bf16[2,448,256]{2,1,0:T(8,128)(2,1)S(1)}, u32[]{:S(2)}, u32[]{:S(2)}) collective-permute-start(bf16[2,448,256]{2,1,0:T(8,128)(2,1)} %collective-permute-done.5.refs_23_.refs_3_), channel_id=1, source_target_pairs={{0,8},{8,16},{16,24},{24,28},{28,20},{20,12},{12,4},{4,0},{1,9},{9... | collective-permute-start | bytes 1376264 | tf_op jit(solution)/shard_map/ppermute | solution.py:452
  69.0 11.7 %copy-start.13 = (bf16[2,448,256]{2,1,0:T(8,128)(2,1)}, bf16[2,448,256]{2,1,0:T(8,128)(2,1)S(1)}, u32[]{:S(2)}) copy-start(bf16[2,448,256]{2,1,0:T(8,128)(2,1)S(1)} %collective-permute-done.9.refs_24_.refs_4_) | copy-start | bytes 1376260
  69.0 11.7 %collective-permute-start.10 = (bf16[2,448,256]{2,1,0:T(8,128)(2,1)S(1)}, bf16[2,448,256]{2,1,0:T(8,128)(2,1)S(1)}, u32[]{:S(2)}, u32[]{:S(2)}) collective-permute-start(bf16[2,448,256]{2,1,0:T(8,128)(2,1)S(1)} %collective-permute-done.9.refs_24_.refs_4_), channel_id=1, source_target_pairs={{0,4},{8,0},{16,8},{24,16},{28,24},{20,28},{12,20},{4,12},{1,5},{9... | collective-permute-start | bytes 1376264 | tf_op jit(solution)/shard_map/ppermute | solution.py:452
  78.6 6.7 %copy-start.11 = (bf16[2,448,256]{2,1,0:T(8,128)(2,1)}, bf16[2,448,256]{2,1,0:T(8,128)(2,1)S(1)}, u32[]{:S(2)}) copy-start(bf16[2,448,256]{2,1,0:T(8,128)(2,1)S(1)} %collective-permute-done.6.refs_8_.refs_5_) | copy-start | bytes 1376260
  80.7 4.5 %copy-start.7 = (bf16[2,448,256]{2,1,0:T(8,128)(2,1)}, bf16[2,448,256]{2,1,0:T(8,128)(2,1)S(1)}, u32[]{:S(2)}) copy-start(bf16[2,448,256]{2,1,0:T(8,128)(2,1)S(1)} %collective-permute-done.10.refs_9_.refs_0_) | copy-start | bytes 1376260
  82.5 1.0 copy-start.3
  83.5 11.9 %collective-permute-start.7 = (bf16[2,224,256]{2,1,0:T(8,128)(2,1)}, bf16[2,224,256]{2,1,0:T(8,128)(2,1)S(1)}, u32[]{:S(2)}, u32[]{:S(2)}) collective-permute-start(bf16[2,224,256]{2,1,0:T(8,128)(2,1)} %shard_map.96), channel_id=1, source_target_pairs={{0,8},{8,16},{16,24},{24,28},{28,20},{20,12},{12,4},{4,0},{1,9},{9... | collective-permute-start | bytes 688136 | tf_op jit(solution)/shard_map/ppermute | solution.py:452
  85.2 10.2 %collective-permute-start.11 = (bf16[2,224,256]{2,1,0:T(8,128)(2,1)}, bf16[2,224,256]{2,1,0:T(8,128)(2,1)S(1)}, u32[]{:S(2)}, u32[]{:S(2)}) collective-permute-start(bf16[2,224,256]{2,1,0:T(8,128)(2,1)} %shard_map.98), channel_id=1, source_target_pairs={{0,4},{8,0},{16,8},{24,16},{28,24},{20,28},{12,20},{4,12},{1,5},{9... | collective-permute-start | bytes 688136 | tf_op jit(solution)/shard_map/ppermute | solution.py:452
  213.3 4.2 %copy-start.23 = (bf16[512,256]{1,0:T(8,128)(2,1)S(1)}, bf16[512,256]{1,0:T(8,128)(2,1)}, u32[]{:S(2)}) copy-start(bf16[512,256]{1,0:T(8,128)(2,1)} %get-tuple-element.20.kv_ref.refs_1_) | copy-start | bytes 786436
  213.3 36.6 %collective-permute-start.17 = (bf16[8,2,448,256]{3,2,1,0:T(8,128)(2,1)}, bf16[8,2,448,256]{3,2,1,0:T(8,128)(2,1)}, u32[]{:S(2)}, u32[]{:S(2)}) collective-permute-start(bf16[8,2,448,256]{3,2,1,0:T(8,128)(2,1)} %shard_map.107.w_ref), channel_id=1, source_target_pairs={{0,1},{1,0},{2,3},{3,2},{4,5},{5,4},{6,7},{7,6},{8,9},{9,8},{10,11... | collective-permute-start | bytes 11010056 | tf_op jit(solution)/shard_map/ppermute | solution.py:449
  213.4 30.5 %all-to-all-start.1 = ((bf16[8,128,512]{2,1,0:T(8,128)(2,1)}), bf16[8,128,512]{2,1,0:T(8,128)(2,1)S(1)}, u32[]{:S(2)}, u32[]{:S(2)}) async-start(bf16[8,128,512]{2,1,0:T(8,128)(2,1)} %collective-permute-done.2.refs_2_.refs_6_.refs_10_.refs_14_.refs_18_), calls=%async_computation.1 | async-start | bytes 2097152 | tf_op jit(solution)/shard_map/all_to_all | solution.py:462
  217.5 8.5 %collective-permute-start.13 = (bf16[512,256]{1,0:T(8,128)(2,1)S(1)}, bf16[512,256]{1,0:T(8,128)(2,1)S(1)}, u32[]{:S(2)}, u32[]{:S(2)}) collective-permute-start(bf16[512,256]{1,0:T(8,128)(2,1)S(1)} %copy-done.23), channel_id=1, source_target_pairs={{0,2},{1,3},{2,0},{3,1},{4,6},{5,7},{6,4},{7,5},{8,10},{9,11},{10,... | collective-permute-start | bytes 786440 | tf_op jit(solution)/shard_map/ppermute | solution.py:449
  233.6 15.2 %copy-start.1 = (bf16[8,128,512]{2,1,0:T(8,128)(2,1)S(1)}, bf16[8,128,512]{2,1,0:T(8,128)(2,1)}, u32[]{:S(2)}) copy-start(bf16[8,128,512]{2,1,0:T(8,128)(2,1)} %copy-done) | copy-start | bytes 3145732
  233.6 13.4 %collective-permute-start.15 = (f32[512,256]{1,0:T(8,128)}, f32[512,256]{1,0:T(8,128)S(1)}, u32[]{:S(2)}, u32[]{:S(2)}) collective-permute-start(f32[512,256]{1,0:T(8,128)} %get-tuple-element.33), channel_id=1, source_target_pairs={{0,2},{1,3},{2,0},{3,1},{4,6},{5,7},{6,4},{7,5},{8,10},{9,11},{10,... | collective-permute-start | bytes 1572872 | tf_op jit(solution)/shard_map/ppermute | solution.py:449
  248.1 1.8 copy-start.8
  248.1 1.6 collective-permute-start.16
  248.2 10.9 %collective-permute-start.12 = (bf16[2,128,896]{2,1,0:T(8,128)(2,1)}, bf16[2,128,896]{2,1,0:T(8,128)(2,1)}, u32[]{:S(2)}, u32[]{:S(2)}) collective-permute-start(bf16[2,128,896]{2,1,0:T(8,128)(2,1)} %get-tuple-element.23), channel_id=1, source_target_pairs={{0,1},{1,0},{2,3},{3,2},{4,5},{5,4},{6,7},{7,6},{8,9},{9,8},{10,11... | collective-permute-start | bytes 1376264 | tf_op jit(solution)/shard_map/ppermute | solution.py:449
  248.7 12.1 %collective-permute-start.14 = (bf16[2,128,896]{2,1,0:T(8,128)(2,1)}, bf16[2,128,896]{2,1,0:T(8,128)(2,1)}, u32[]{:S(2)}, u32[]{:S(2)}) collective-permute-start(bf16[2,128,896]{2,1,0:T(8,128)(2,1)} %get-tuple-element.26), channel_id=1, source_target_pairs={{0,1},{1,0},{2,3},{3,2},{4,5},{5,4},{6,7},{7,6},{8,9},{9,8},{10,11... | collective-permute-start | bytes 1376264 | tf_op jit(solution)/shard_map/ppermute | solution.py:449
  248.8 30.7 %collective-permute-start.19 = (bf16[8,128,512]{2,1,0:T(8,128)(2,1)S(1)}, bf16[8,128,512]{2,1,0:T(8,128)(2,1)S(1)}, u32[]{:S(2)}, u32[]{:S(2)}) collective-permute-start(bf16[8,128,512]{2,1,0:T(8,128)(2,1)S(1)} %copy-done.1), channel_id=1, source_target_pairs={{0,1},{1,0},{2,3},{3,2},{4,5},{5,4},{6,7},{7,6},{8,9},{9,8},{10,11... | collective-permute-start | bytes 3145736 | tf_op jit(solution)/shard_map/ppermute | solution.py:449
  249.7 29.8 %collective-permute-start.20 = (bf16[8,128,512]{2,1,0:T(8,128)(2,1)}, bf16[8,128,512]{2,1,0:T(8,128)(2,1)S(1)}, u32[]{:S(2)}, u32[]{:S(2)}) collective-permute-start(bf16[8,128,512]{2,1,0:T(8,128)(2,1)} %copy-done.2), channel_id=1, source_target_pairs={{0,1},{1,0},{2,3},{3,2},{4,5},{5,4},{6,7},{7,6},{8,9},{9,8},{10,11... | collective-permute-start | bytes 3145736 | tf_op jit(solution)/shard_map/ppermute | solution.py:449
  258.0 36.1 %collective-permute-start.18 = (bf16[128,3584]{1,0:T(8,128)(2,1)}, bf16[128,3584]{1,0:T(8,128)(2,1)}, u32[]{:S(2)}, u32[]{:S(2)}) collective-permute-start(bf16[128,3584]{1,0:T(8,128)(2,1)} %get-tuple-element.35.refs_1_), channel_id=1, source_target_pairs={{0,2},{1,3},{2,0},{3,1},{4,6},{5,7},{6,4},{7,5},{8,10},{9,11},{10,... | collective-permute-start | bytes 2752520 | tf_op jit(solution)/shard_map/ppermute | solution.py:449
  259.1 8.3 %collective-permute-start.21 = (bf16[512,256]{1,0:T(8,128)(2,1)}, bf16[512,256]{1,0:T(8,128)(2,1)S(1)}, u32[]{:S(2)}, u32[]{:S(2)}) collective-permute-start(bf16[512,256]{1,0:T(8,128)(2,1)} %shard_map.109.refs_20_), channel_id=1, source_target_pairs={{0,8},{8,16},{16,24},{24,28},{28,20},{20,12},{12,4},{4,0},{1,9},{9... | collective-permute-start | bytes 786440 | tf_op jit(solution)/shard_map/ppermute | solution.py:452
  260.8 8.3 %collective-permute-start.25 = (bf16[512,256]{1,0:T(8,128)(2,1)}, bf16[512,256]{1,0:T(8,128)(2,1)S(1)}, u32[]{:S(2)}, u32[]{:S(2)}) collective-permute-start(bf16[512,256]{1,0:T(8,128)(2,1)} %shard_map.109.refs_20_), channel_id=1, source_target_pairs={{0,4},{8,0},{16,8},{24,16},{28,24},{20,28},{12,20},{4,12},{1,5},{9... | collective-permute-start | bytes 786440 | tf_op jit(solution)/shard_map/ppermute | solution.py:452
  267.3 12.2 %copy-start.18 = (bf16[512,256]{1,0:T(8,128)(2,1)}, bf16[512,256]{1,0:T(8,128)(2,1)S(1)}, u32[]{:S(2)}) copy-start(bf16[512,256]{1,0:T(8,128)(2,1)S(1)} %collective-permute-done.21.refs_21_) | copy-start | bytes 786436
  267.3 7.3 %collective-permute-start.22 = (bf16[512,256]{1,0:T(8,128)(2,1)S(1)}, bf16[512,256]{1,0:T(8,128)(2,1)S(1)}, u32[]{:S(2)}, u32[]{:S(2)}) collective-permute-start(bf16[512,256]{1,0:T(8,128)(2,1)S(1)} %collective-permute-done.21.refs_21_), channel_id=1, source_target_pairs={{0,8},{8,16},{16,24},{24,28},{28,20},{20,12},{12,4},{4,0},{1,9},{9... | collective-permute-start | bytes 786440 | tf_op jit(solution)/shard_map/ppermute | solution.py:452
  269.0 10.5 %copy-start.19 = (bf16[512,256]{1,0:T(8,128)(2,1)}, bf16[512,256]{1,0:T(8,128)(2,1)S(1)}, u32[]{:S(2)}) copy-start(bf16[512,256]{1,0:T(8,128)(2,1)S(1)} %collective-permute-done.25.refs_22_) | copy-start | bytes 786436
  269.0 7.3 %collective-permute-start.26 = (bf16[512,256]{1,0:T(8,128)(2,1)S(1)}, bf16[512,256]{1,0:T(8,128)(2,1)S(1)}, u32[]{:S(2)}, u32[]{:S(2)}) collective-permute-start(bf16[512,256]{1,0:T(8,128)(2,1)S(1)} %collective-permute-done.25.refs_22_), channel_id=1, source_target_pairs={{0,4},{8,0},{16,8},{24,16},{28,24},{20,28},{12,20},{4,12},{1,5},{9... | collective-permute-start | bytes 786440 | tf_op jit(solution)/shard_map/ppermute | solution.py:452
  274.7 4.9 %copy-start.21 = (bf16[512,256]{1,0:T(8,128)(2,1)}, bf16[512,256]{1,0:T(8,128)(2,1)S(1)}, u32[]{:S(2)}) copy-start(bf16[512,256]{1,0:T(8,128)(2,1)S(1)} %collective-permute-done.22.refs_23_) | copy-start | bytes 786436
  274.7 12.6 %collective-permute-start.23 = (bf16[512,256]{1,0:T(8,128)(2,1)S(1)}, bf16[512,256]{1,0:T(8,128)(2,1)S(1)}, u32[]{:S(2)}, u32[]{:S(2)}) collective-permute-start(bf16[512,256]{1,0:T(8,128)(2,1)S(1)} %collective-permute-done.22.refs_23_), channel_id=1, source_target_pairs={{0,8},{8,16},{16,24},{24,28},{28,20},{20,12},{12,4},{4,0},{1,9},{9... | collective-permute-start | bytes 786440 | tf_op jit(solution)/shard_map/ppermute | solution.py:452
  276.3 3.2 %copy-start.20 = (bf16[512,256]{1,0:T(8,128)(2,1)}, bf16[512,256]{1,0:T(8,128)(2,1)S(1)}, u32[]{:S(2)}) copy-start(bf16[512,256]{1,0:T(8,128)(2,1)S(1)} %collective-permute-done.26.refs_24_) | copy-start | bytes 786436
  276.3 12.7 %collective-permute-start.27 = (bf16[512,256]{1,0:T(8,128)(2,1)S(1)}, bf16[512,256]{1,0:T(8,128)(2,1)S(1)}, u32[]{:S(2)}, u32[]{:S(2)}) collective-permute-start(bf16[512,256]{1,0:T(8,128)(2,1)S(1)} %collective-permute-done.26.refs_24_), channel_id=1, source_target_pairs={{0,4},{8,0},{16,8},{24,16},{28,24},{20,28},{12,20},{4,12},{1,5},{9... | collective-permute-start | bytes 786440 | tf_op jit(solution)/shard_map/ppermute | solution.py:452
  279.5 1.0 copy-start.5
  280.5 1.0 copy-start.6
  287.2 2.2 copy-start.16
  287.3 9.0 %collective-permute-start.24 = (bf16[256,256]{1,0:T(8,128)(2,1)S(1)}, bf16[256,256]{1,0:T(8,128)(2,1)S(1)}, u32[]{:S(2)}, u32[]{:S(2)}) collective-permute-start(bf16[256,256]{1,0:T(8,128)(2,1)S(1)} %slice.18), channel_id=1, source_target_pairs={{0,8},{8,16},{16,24},{24,28},{28,20},{20,12},{12,4},{4,0},{1,9},{9... | collective-permute-start | bytes 393224 | tf_op jit(solution)/shard_map/ppermute | solution.py:452
  289.0 5.0 %copy-start.12 = (f32[128,3584]{1,0:T(8,128)S(1)}, f32[128,3584]{1,0:T(8,128)}, u32[]{:S(2)}) copy-start(f32[128,3584]{1,0:T(8,128)} %get-tuple-element.34) | copy-start | bytes 5505028
  289.0 7.3 %collective-permute-start.28 = (bf16[256,256]{1,0:T(8,128)(2,1)S(1)}, bf16[256,256]{1,0:T(8,128)(2,1)S(1)}, u32[]{:S(2)}, u32[]{:S(2)}) collective-permute-start(bf16[256,256]{1,0:T(8,128)(2,1)S(1)} %slice.19), channel_id=1, source_target_pairs={{0,4},{8,0},{16,8},{24,16},{28,24},{20,28},{12,20},{4,12},{1,5},{9... | collective-permute-start | bytes 393224 | tf_op jit(solution)/shard_map/ppermute | solution.py:452
  (10 other events, 7.7 us)

commit v3 on v2

v3 whole, which is shorter than its diff:
```python
import functools

import jax
import jax.numpy as jnp
from jax import lax
from jax.experimental import pallas as pl
from jax.experimental.pallas import tpu as pltpu
from jax.sharding import PartitionSpec as P

HEAD_DIM = 128
GROUP = 7
SPAN = GROUP * HEAD_DIM
PAIR = 2 * HEAD_DIM
SCALE = HEAD_DIM ** (-0.5)
LOG2E = 1.4426950408889634
HIDDEN = -1e30
DIGIT = 16
F32 = jnp.float32
BF16 = jnp.bfloat16
ANYWHERE = pl.BlockSpec(memory_space=pl.ANY)
CYCLE = (0, 2, 4, 6, 7, 5, 3, 1)
STEPS = (0, -1, 1, -2, 2, -3, 3, 4)


def contract(a, b, da, db):
    return lax.dot_general(a, b, (((da,), (db,)), ((), ())), preferred_element_type=F32)


def shaped(shape, dtype):
    return jax.ShapeDtypeStruct(shape, dtype)


def call(body, me, operands, out_shape, flops, scratch=(), aliases=None, anywhere=0):
    moved = sum(x.size * x.dtype.itemsize for x in operands)
    near = pl.BlockSpec(memory_space=pltpu.VMEM)
    return pl.pallas_call(
        body,
        in_specs=[pl.BlockSpec(memory_space=pltpu.SMEM)]
        + [near] * (len(operands) - anywhere)
        + [ANYWHERE] * anywhere,
        out_specs=[near] * len(out_shape) if isinstance(out_shape, list) else near,
        out_shape=out_shape,
        scratch_shapes=scratch,
        input_output_aliases=aliases or {},
        compiler_params=pltpu.CompilerParams(vmem_limit_bytes=24 * 1024 * 1024),
        cost_estimate=pl.CostEstimate(flops=flops, bytes_accessed=moved, transcendentals=0),
    )(me, *operands)


def owner_at(me_f, by):
    size = len(CYCLE)
    half = size // 2
    line, side = lax.div(me_f, 2), lax.rem(me_f, 2)
    spot = jnp.where(side == 1, size - 1 - line, line)
    spot = lax.rem(spot + (size + by), size)
    return jnp.where(spot < half, 2 * spot, 2 * (size - 1 - spot) + 1)


def after(x, *others):
    return pl.pallas_call(
        lambda *refs: None,
        in_specs=[ANYWHERE] * (1 + len(others)),
        out_specs=ANYWHERE,
        out_shape=shaped(x.shape, x.dtype),
        input_output_aliases={0: 0},
        cost_estimate=pl.CostEstimate(flops=0, bytes_accessed=0, transcendentals=0),
    )(x, *others)


def as_column(row):
    return jnp.broadcast_to(row, (128, row.shape[1])).T[:, :1]


def blocks_kernel(depth, me_ref, tok_ref, kind_ref, ids_ref, out_ref):
    count, rows, lanes = out_ref.shape
    base = lanes - 128
    lane = lax.broadcasted_iota(jnp.int32, (rows, 128), 1) - (depth - base)
    ids = ids_ref[...]
    marks = [as_column(x.astype(F32)) for x in (kind_ref[...], lax.div(ids, DIGIT), lax.rem(ids, DIGIT))]
    for j in range(count):
        out_ref[j, :, :depth] = tok_ref[:, j * depth : (j + 1) * depth]
        last = out_ref[j, :, base:].astype(F32)
        last = jnp.where(lane >= 0, 0.0, last)
        for i, mark in enumerate(marks):
            last = jnp.where(lane == i, mark, last)
        out_ref[j, :, base:] = last.astype(BF16)


def token_blocks(me, tokens, kinds, ids, count):
    rows, width = tokens.shape
    depth = width // count
    lanes = -(-(depth + 3) // 128) * 128
    out = shaped((count, rows, lanes), BF16)
    return call(functools.partial(blocks_kernel, depth), me, (tokens, kinds, ids), out, 0)


def read_marks(block, depth):
    mark = [block[:, depth + i : depth + i + 1].astype(F32) for i in range(3)]
    return mark[0], mark[1] * DIGIT + mark[2]


def pack_kernel(me_ref, q_ref, up_ref, own_ref, other_ref):
    for i in range(4):
        here = pl.ds(pl.multiple_of((me_ref[0] ^ i) * SPAN, SPAN), SPAN)
        out_ref = other_ref if i % 2 else own_ref
        out_ref[i // 2, 0] = q_ref[:, here]
        out_ref[i // 2, 1] = up_ref[:, here]


def pack_heads(me, queries, upstream):
    out = shaped((2, 2, queries.shape[0], SPAN), BF16)
    return call(pack_kernel, me, (queries, upstream), [out, out], 0)


def place_kernel(me_ref, *refs):
    att_ref, gq_ref = refs[4:]
    for i, ref in enumerate(refs[:4]):
        here = pl.ds(pl.multiple_of((me_ref[0] ^ i) * SPAN, SPAN), SPAN)
        att_ref[:, here] = ref[0]
        gq_ref[:, here] = ref[1]


def place_heads(me, found):
    out = shaped((found[0].shape[1], 4 * SPAN), BF16)
    return call(place_kernel, me, found, [out, out], 0)


def project_kernel(steps, depth, halves, first, last, me_ref, *refs):
    parts, refs = refs[:4], refs[4:]
    weights, refs = refs[: len(steps) + halves], refs[len(steps) + halves :]
    rows, lanes = parts[0].shape[1:]
    sums = [0.0, 0.0]
    for b, by in enumerate(steps):
        owner = owner_at(me_ref[1], by)
        left = jnp.concatenate([ref[owner][:, :depth] for ref in parts], axis=0)
        for e in range(2):
            right = jnp.concatenate([ref[e] for ref in weights], axis=0) if halves else weights[b][e]
            sums[e] = sums[e] + contract(left, right, 1, 0)
    if not first:
        sums = [s + refs[0][:, e * PAIR : (e + 1) * PAIR] for e, s in enumerate(sums)]
        refs = refs[1:]
    if not last:
        for e in range(2):
            refs[-1][:, e * PAIR : (e + 1) * PAIR] = sums[e]
        return
    kv_ref, kind_ref, ids_ref, ids_row_ref = refs[-4:]
    for r in range(4):
        here = pl.ds(pl.multiple_of((me_ref[0] ^ r) * rows, rows), rows)
        kind, ids = read_marks(parts[r][0], depth)
        mine = slice(r * rows, (r + 1) * rows)
        kv_ref[here, :] = jnp.where(kind == 1.0, sums[1][mine], sums[0][mine]).astype(BF16)
        kind_ref[here, :] = kind
        ids_ref[here, :] = ids
    ids_row_ref[...] = jnp.broadcast_to(ids_ref[...], (4 * rows, 128)).T[:1]


def project(me, steps, parts, weights, total, depth, last=False, halves=False, wait=()):
    rows, lanes = parts[0].shape[1:]
    length = 4 * rows
    before = () if total is None else (total,)
    out = shaped((length, 2 * PAIR), F32)
    if last:
        out = [shaped((length, PAIR), BF16)] + [shaped(x, F32) for x in ((length, 1), (length, 1), (1, length))]
    operands = (*parts, *weights, *before, *wait)
    return call(
        functools.partial(project_kernel, steps, depth, int(halves), total is None, last),
        me,
        operands,
        out,
        4 * length * depth * PAIR * len(steps),
        anywhere=len(wait),
    )


def attend_kernel(me_ref, own_ref, pack_ref, kv_ref, ids_ref, ids_row_ref, *refs):
    mine_ref, other_ref, gkv_ref, bias, scores_all, dp_all, pbs, his, los = refs[-9:]
    rows = own_ref.shape[2]
    heads = [slice(h * HEAD_DIM, (h + 1) * HEAD_DIM) for h in range(GROUP)]
    for i in range(2):
        here = pl.ds(pl.multiple_of((me_ref[0] ^ i) * rows, rows), rows)
        bias[i * rows : (i + 1) * rows, :] = jnp.where(ids_row_ref[...] <= ids_ref[here, :], 0.0, HIDDEN)
    keys = kv_ref[:, :HEAD_DIM]
    values = kv_ref[:, HEAD_DIM:]
    spot = me_ref[2]
    q, up = [
        jnp.concatenate([ref[spot, i, :, cols] for ref in (own_ref, pack_ref) for cols in heads], axis=0)
        for i in range(2)
    ]
    scores_all[...] = contract(q, keys, 1, 1)
    dp_all[...] = contract(up, values, 1, 1).astype(BF16)
    for h in range(2 * GROUP):
        here = slice(h * rows, (h + 1) * rows)
        side = h // GROUP
        scores = scores_all[here, :] * (SCALE * LOG2E) + bias[side * rows : (side + 1) * rows, :]
        expo = jnp.exp2(scores - jnp.max(scores, axis=-1, keepdims=True))
        probs = expo * (1.0 / jnp.sum(expo, axis=-1, keepdims=True))
        pbs[here, :] = probs.astype(BF16)
        dp = dp_all[here, :].astype(F32)
        ds = probs * (dp - jnp.sum(probs * dp, axis=-1, keepdims=True))
        hi = ds.astype(BF16)
        his[here, :] = hi
        los[here, :] = (ds - hi.astype(F32)).astype(BF16)
    att = contract(pbs[...], values, 1, 0).astype(BF16)
    gq = ((contract(his[...], keys, 1, 0) + contract(los[...], keys, 1, 0)) * SCALE).astype(BF16)
    for i, ref in enumerate((mine_ref, other_ref)):
        for h, cols in enumerate(heads):
            here = slice((i * GROUP + h) * rows, (i * GROUP + h + 1) * rows)
            ref[0, :, cols] = att[here]
            ref[1, :, cols] = gq[here]
    dk = (contract(q, his[...], 0, 0) + contract(q, los[...], 0, 0)) * SCALE
    dv = contract(up, pbs[...], 0, 0)
    gkv_ref[:, :HEAD_DIM] = dk.T
    gkv_ref[:, HEAD_DIM:] = dv.T


def attend(me, own, pack, kv, ids, ids_row, wait=()):
    rows = own.shape[2]
    length = kv.shape[0]
    stacked = (2 * GROUP * rows, length)
    side = shaped((2, rows, SPAN), BF16)
    return call(
        attend_kernel,
        me,
        (own, pack, kv, ids, ids_row, *wait),
        [side, side, shaped((length, PAIR), F32)],
        16 * 2 * GROUP * rows * length * HEAD_DIM,
        scratch=[pltpu.VMEM((2 * rows, length), F32), pltpu.VMEM(stacked, F32)] + [pltpu.VMEM(stacked, BF16)] * 4,
        anywhere=len(wait),
    )


def by_expert(kind, x):
    return [jnp.where(kind == float(e), x, 0.0).astype(BF16) for e in range(2)]


def hidden_kernel(me_ref, kind_ref, g_ref, gc_ref, w_ref, wc_ref, mine_ref, away_ref):
    rows = mine_ref.shape[0]
    count, _, depth, _ = w_ref.shape
    masked = []
    for ref in (g_ref, gc_ref):
        sides = []
        for i in range(2):
            here = pl.ds(pl.multiple_of((me_ref[0] ^ (2 * i)) * rows, rows), rows)
            sides.append(by_expert(kind_ref[here, :], ref[here, :].astype(F32)))
        masked += [jnp.concatenate([sides[0][e], sides[1][e]], axis=0) for e in range(2)]
    group = count // 4
    for j in range(4):
        total = 0.0
        for k, ref in enumerate((w_ref, wc_ref)):
            for e in range(2):
                w = ref[j * group : (j + 1) * group, e].reshape(group * depth, PAIR)
                total = total + contract(w, masked[2 * k + e], 1, 1)
        total = total.T
        cols = slice(j * group * depth, (j + 1) * group * depth)
        mine_ref[:, cols] = total[:rows]
        away_ref[:, cols] = total[rows:].astype(BF16)


def hidden_grad(me, kind, grad, grad_c, weight, weight_c, rows):
    count, _, depth, _ = weight.shape
    width = count * depth
    return call(
        hidden_kernel,
        me,
        (kind, grad, grad_c, weight, weight_c),
        [shaped((rows, width), F32), shaped((rows, width), BF16)],
        16 * rows * width * PAIR,
    )


def weight_kernel(steps, depth, halves, first, last, me_ref, *refs):
    parts, refs = refs[:4], refs[4:]
    grads, refs = refs[: len(steps) + halves], refs[len(steps) + halves :]
    rows, lanes = parts[0].shape[1:]
    size = grads[0].shape[0]
    total = 0.0
    for b, by in enumerate(steps):
        owner = owner_at(me_ref[1], by)
        left = jnp.concatenate([ref[owner] for ref in parts], axis=0)
        quarter = []
        for r in range(4):
            start = (me_ref[0] ^ r) * rows
            if halves:
                inner = pl.ds(pl.multiple_of(lax.rem(start, size), rows), rows)
                quarter.append(jnp.where(start < size, grads[0][inner, :].astype(F32), grads[1][inner, :].astype(F32)))
            else:
                quarter.append(grads[b][pl.ds(pl.multiple_of(start, rows), rows), :].astype(F32))
        kind = left[:, depth : depth + 1].astype(F32)
        right = jnp.concatenate(by_expert(kind, jnp.concatenate(quarter, axis=0)), axis=-1)
        total = total + contract(left, right, 0, 0)
    if not first:
        total = total + refs[0][...]
    if not last:
        refs[-1][...] = total
        return
    for e in range(2):
        refs[-1][e] = total[:depth, e * PAIR : (e + 1) * PAIR]


def weight_grad(me, steps, parts, grads, total, depth, last=False, halves=False):
    rows, lanes = parts[0].shape[1:]
    before = () if total is None else (total,)
    return call(
        functools.partial(weight_kernel, steps, depth, int(halves), total is None, last),
        me,
        (*parts, *grads, *before),
        shaped((2, depth, PAIR) if last else (lanes, 2 * PAIR), F32),
        16 * rows * lanes * PAIR * len(steps),
    )


def gather_kernel(me_ref, *refs):
    blocks, whole_ref = refs[: len(STEPS) + 1], refs[-1]
    size = blocks[-1].shape[1]
    for i, block in enumerate(blocks):
        owner = owner_at(me_ref[1], STEPS[min(i, len(STEPS) - 1)])
        if i < len(STEPS) - 1:
            whole_ref[owner] = block[...]
        else:
            whole_ref[owner, :, (i - len(STEPS) + 1) * size : (i - len(STEPS) + 2) * size, :] = block[...]


def gather_blocks(me, blocks, wait=()):
    out = shaped((len(CYCLE), *blocks[0].shape), blocks[0].dtype)
    return call(gather_kernel, me, (*blocks, *wait), out, 0, anywhere=len(wait))


def in_order(parts, quarters):
    count, rows, lanes = parts[0].shape
    whole = jnp.stack(parts, axis=1)
    return jnp.take(whole, quarters, axis=1).reshape(count, 4 * rows, lanes)


def project_plain(quarters, parts, weights, depth):
    tokens = in_order(parts, quarters)
    kind, ids = read_marks(tokens[0], depth)
    sums = jnp.einsum("jmk,jekn->emn", tokens[:, :, :depth], weights, preferred_element_type=F32)
    return jnp.where(kind == 1.0, sums[1], sums[0]).astype(BF16), kind, ids, ids.reshape(1, -1)


def weight_plain(quarters, parts, grads, depth):
    tokens = in_order(parts, quarters)
    kind = tokens[:, :, depth : depth + 1].astype(F32)
    sums = [
        jnp.einsum("jmk,jmn->kn", tokens[:, :, :depth], g, preferred_element_type=F32)
        for g in by_expert(kind, grads.astype(F32))
    ]
    return jnp.stack(sums)


def per_device(fsdp, seq, tokens, queries, cotangent, modality, block_ids, kv_weight):
    tokens, queries, cotangent = tokens[0], queries[0], cotangent[0]
    me_f = lax.axis_index("fsdp")
    me_s = lax.axis_index("seq")
    rows, width = tokens.shape
    depth = kv_weight.shape[1]
    near_link = fsdp == len(CYCLE)

    def swap(x, bit):
        return lax.ppermute(x, "seq", [(i, i ^ bit) for i in range(seq)])

    def turn(x, by):
        return lax.ppermute(x, "fsdp", [(CYCLE[i], CYCLE[(i + by) % fsdp]) for i in range(fsdp)])

    def both_ways(ups, downs):
        return turn(ups, 1), turn(downs, -1)

    def halves(ups, downs, axis):
        size = ups.shape[axis] // 2
        return lax.slice_in_dim(ups, 0, size, axis=axis), lax.slice_in_dim(downs, size, 2 * size, axis=axis)

    def exchange_columns(x):
        return lax.all_to_all(x, "fsdp", split_axis=0, concat_axis=0, tiled=True)

    me = jnp.stack([me_s, me_f, jnp.int32(0)])
    me_far = jnp.stack([me_s, me_f, jnp.int32(1)])
    quarters = me_s ^ jnp.arange(seq, dtype=jnp.int32)
    if near_link:
        weights = [kv_weight, *both_ways(kv_weight, kv_weight)]
        weights += both_ways(*weights[1:])
        weights += both_ways(*weights[3:])
    else:
        weight = lax.all_gather(kv_weight, "fsdp", axis=0)

    blocks = token_blocks(me, tokens, modality, block_ids, fsdp)
    across = swap(blocks, 2)
    parts = [blocks, swap(blocks, 1), across, swap(across, 1)]
    own, pack = pack_heads(me, queries, cotangent)
    pack = swap(pack, 1)
    columns = exchange_columns(blocks)
    columns_across = exchange_columns(across)

    if near_link:
        ups, downs = halves(*weights[5:], 1)
        weights += both_ways(after(ups, parts[1], pack), after(downs, parts[1], pack))
        total = project(me, STEPS[:5], parts, weights[:5], None, depth)
        total = project(me, STEPS[5:7], parts, weights[5:7], total, depth)
        kv, kind, ids, ids_row = project(me, STEPS[7:], parts, weights[7:], total, depth, True, True, (columns,))
        weight = gather_blocks(me, weights, (kv,))
    else:
        kv, kind, ids, ids_row = project_plain(quarters, parts, weight, depth)
    weight_c = swap(weight, 1)

    kv_far = swap(kv, 2)
    near_own, near_other, near = attend(me, own, pack, kv, ids, ids_row)
    far_own, far_other, far = attend(me_far, own, pack, kv_far, ids, ids_row, (near,))
    grad_kv = (after(near, columns_across) + swap(far, 2)).astype(BF16)
    attended, grad_queries = place_heads(me, (near_own, swap(near_other, 1), far_own, swap(far_other, 1)))

    mine, away = hidden_grad(me, kind, grad_kv, swap(grad_kv, 1), weight, weight_c, rows)
    columns = [columns, swap(columns, 1), columns_across, swap(columns_across, 1)]
    if near_link:
        first = after(grad_kv, away)
        grads = [first, *both_ways(first, first)]
        grads += both_ways(*grads[1:])
        grads += both_ways(*grads[3:])
        grads += both_ways(*halves(*grads[5:], 0))
        total = weight_grad(me, STEPS[:5], columns, grads[:5], None, depth)
        total = weight_grad(me, STEPS[5:7], columns, grads[5:7], total, depth)
        grad_weight = weight_grad(me, STEPS[7:], columns, grads[7:], total, depth, True, True)
    else:
        grad_weight = weight_plain(quarters, columns, lax.all_gather(grad_kv, "fsdp", axis=0), depth)
    grad_tokens = (mine + swap(away, 2).astype(F32)).astype(BF16)
    return attended[None], grad_queries[None], grad_tokens[None], grad_weight


def solution(mesh):
    split = P("fsdp", "seq", None)
    weights = P(None, "fsdp", "seq")
    return jax.shard_map(
        functools.partial(per_device, mesh.shape["fsdp"], mesh.shape["seq"]),
        mesh=mesh,
        in_specs=(split, split, split, P("fsdp", "seq"), P("fsdp", "seq"), weights),
        out_specs=(split, split, split, weights),
        check_vma=False,
    )
```

time: 302 us -> 185 us (0.61)
  Pallas kernels: 170 us -> 43 us
  local copies, waits for them, and re-layouts: 16.2 us -> 28.1 us
  waiting for transfers between devices: 71.5 us -> 67.3 us
    pallas_call x13, Pallas kernels: 170 us -> 43 us  [call(): pl.pallas_call(body, in_specs=[pl.BlockSpec(memory_space=pltpu.SMEM)] + [...]
    unnamed x56 -> x90, local copies, waits for them, and re-layouts: 11.9 us -> 25.7 us
    ppermute x16, waiting for transfers between devices: 46.5 us -> 39.8 us  [turn(): lax.ppermute(x, 'fsdp', [(CYCLE[i], CYCLE[(i + by) % fsdp]) for i in rang...]
    ppermute x13, waiting for transfers between devices: 15.3 us -> 18.8 us  [swap(): return lax.ppermute(x, 'seq', [(i, i ^ bit) for i in range(seq)])]
  transfers between devices with their start and end apart: 31 -> 31, of which waited for: 13 -> 11; matrix products, arithmetic and copies ran while one was open for 2% -> 3% of each run, Pallas kernels for 16% -> 18%
where the time goes in v3:
time: 185 us; the launch traced here: 184 us
  waiting for transfers between devices  67.3 us (36%)
  Pallas kernels  43 us (23%)
  starting transfers between devices  40.8 us (22%)
  local copies, waits for them, and re-layouts  28.1 us (15%)
  other arithmetic  3.55 us (2%)
    pallas_call x13, Pallas kernels, call(): pl.pallas_call(body, in_specs=[pl.BlockSpec(memory_space=pltpu.SMEM)] + [...  43 us
    ppermute x16, waiting for transfers between devices, turn(): lax.ppermute(x, 'fsdp', [(CYCLE[i], CYCLE[(i + by) % fsdp]) for i in rang...  39.8 us
    unnamed x90, local copies, waits for them, and re-layouts  25.7 us
    ppermute x16, starting transfers between devices, turn(): lax.ppermute(x, 'fsdp', [(CYCLE[i], CYCLE[(i + by) % fsdp]) for i in rang...  21.9 us
    ppermute x13, waiting for transfers between devices, swap(): return lax.ppermute(x, 'seq', [(i, i ^ bit) for i in range(seq)])  18.8 us
    all_to_all x2, starting transfers between devices, exchange_columns(): return lax.all_to_all(x, 'fsdp', split_axis=0, concat_axis=0, tiled=True)  11 us
    all_to_all x2, waiting for transfers between devices, exchange_columns(): return lax.all_to_all(x, 'fsdp', split_axis=0, concat_axis=0, tiled=True)  8.7 us
    ppermute x13, starting transfers between devices, swap(): return lax.ppermute(x, 'seq', [(i, i ^ bit) for i in range(seq)])  7.82 us
  transfers between devices with their start and end apart: 31, of which 11 were waited for; matrix products, arithmetic and copies ran while one was open for 3% of the time, Pallas kernels for 18%

profile of v3, /device:TPU:0, one launch (start us, length us, event | category | flops | bytes accessed | tf_op | source)
XLA Modules:
  0.0 183.6 jit_solution(6108299278227103117)
XLA Ops:
  0.7 1.2 copy-done.23
  3.2 1.9 %shard_map.94.refs_0_ = bf16[8,128,512]{2,1,0:T(8,128)(2,1)} custom-call(s32[3]{0:T(128)S(1)} %pad_add_fusion.me_ref, bf16[128,3584]{1,0:T(8,128)(2,1)S(1)} %bitcast.9, s32[1,128]{1,0:T(1,128)S(1)} %copy-done.37, s32[1,128]{1,0:T(1,128)S(1)} %copy-done.38), custom_call_target="tpu_custom_call" | custom-call | bytes 918528 | tf_op jit(solution)/shard_map/pallas_call | solution.py:36
  5.1 3.0 %collective-permute-start.2 = (bf16[8,128,512]{2,1,0:T(8,128)(2,1)}, bf16[8,128,512]{2,1,0:T(8,128)(2,1)}, u32[]{:S(2)}, u32[]{:S(2)}) collective-permute-start(bf16[8,128,512]{2,1,0:T(8,128)(2,1)} %shard_map.94.refs_0_), channel_id=1, source_target_pairs={{0,2},{1,3},{2,0},{3,1},{4,6},{5,7},{6,4},{7,5},{8,10},{9,11},{10,... | collective-permute-start | bytes 3145736 | tf_op jit(solution)/shard_map/ppermute | solution.py:360
  8.1 5.8 %all-to-all-start = ((bf16[8,128,512]{2,1,0:T(8,128)(2,1)}), bf16[8,128,512]{2,1,0:T(8,128)(2,1)S(1)}, u32[]{:S(2)}, u32[]{:S(2)}) async-start(bf16[8,128,512]{2,1,0:T(8,128)(2,1)} %shard_map.94.refs_0_), calls=%async_computation | async-start | bytes 2097152 | tf_op jit(solution)/shard_map/all_to_all | solution.py:373
  13.9 2.0 %collective-permute-start.4 = (bf16[2,448,256]{2,1,0:T(8,128)(2,1)}, bf16[2,448,256]{2,1,0:T(8,128)(2,1)S(1)}, u32[]{:S(2)}, u32[]{:S(2)}) collective-permute-start(bf16[2,448,256]{2,1,0:T(8,128)(2,1)} %refs_0_.1), channel_id=1, source_target_pairs={{0,8},{8,16},{16,24},{24,28},{28,20},{20,12},{12,4},{4,0},{1,9},{9... | collective-permute-start | bytes 1376264 | tf_op jit(solution)/shard_map/ppermute | solution.py:363
  15.9 15.6 %collective-permute-done.2.refs_2_ = bf16[8,128,512]{2,1,0:T(8,128)(2,1)} collective-permute-done((bf16[8,128,512]{2,1,0:T(8,128)(2,1)}, bf16[8,128,512]{2,1,0:T(8,128)(2,1)}, u32[]{:S(2)}, u32[]{:S(2)}) %collective-permute-start.2) | collective-permute-done | bytes 1048608 | tf_op jit(solution)/shard_map/ppermute | solution.py:360
  31.5 9.0 %collective-permute-done.4.refs_5_.refs_1_ = bf16[2,448,256]{2,1,0:T(8,128)(2,1)S(1)} collective-permute-done((bf16[2,448,256]{2,1,0:T(8,128)(2,1)}, bf16[2,448,256]{2,1,0:T(8,128)(2,1)S(1)}, u32[]{:S(2)}, u32[]{:S(2)}) %collective-permute-start.4) | collective-permute-done | bytes 458784 | tf_op jit(solution)/shard_map/ppermute | solution.py:363
  40.5 7.1 %collective-permute-start.5 = (bf16[2,448,256]{2,1,0:T(8,128)(2,1)S(1)}, bf16[2,448,256]{2,1,0:T(8,128)(2,1)S(1)}, u32[]{:S(2)}, u32[]{:S(2)}) collective-permute-start(bf16[2,448,256]{2,1,0:T(8,128)(2,1)S(1)} %collective-permute-done.4.refs_5_.refs_1_), channel_id=1, source_target_pairs={{0,8},{8,16},{16,24},{24,28},{28,20},{20,12},{12,4},{4,0},{1,9},{9... | collective-permute-start | bytes 1376264 | tf_op jit(solution)/shard_map/ppermute | solution.py:363
  47.7 1.2 copy-done.24
  48.8 1.2 copy-done.25
  52.4 5.0 %collective-permute-done.5.refs_7_.refs_3_ = bf16[2,448,256]{2,1,0:T(8,128)(2,1)S(1)} collective-permute-done((bf16[2,448,256]{2,1,0:T(8,128)(2,1)S(1)}, bf16[2,448,256]{2,1,0:T(8,128)(2,1)S(1)}, u32[]{:S(2)}, u32[]{:S(2)}) %collective-permute-start.5) | collective-permute-done | bytes 458784 | tf_op jit(solution)/shard_map/ppermute | solution.py:363
  57.4 2.5 %collective-permute-start.6 = (bf16[2,448,256]{2,1,0:T(8,128)(2,1)S(1)}, bf16[2,448,256]{2,1,0:T(8,128)(2,1)S(1)}, u32[]{:S(2)}, u32[]{:S(2)}) collective-permute-start(bf16[2,448,256]{2,1,0:T(8,128)(2,1)S(1)} %collective-permute-done.5.refs_7_.refs_3_), channel_id=1, source_target_pairs={{0,8},{8,16},{16,24},{24,28},{28,20},{20,12},{12,4},{4,0},{1,9},{9... | collective-permute-start | bytes 1376264 | tf_op jit(solution)/shard_map/ppermute | solution.py:363
  60.7 4.7 %collective-permute-done.9.refs_8_.refs_4_ = bf16[2,448,256]{2,1,0:T(8,128)(2,1)} collective-permute-done((bf16[2,448,256]{2,1,0:T(8,128)(2,1)S(1)}, bf16[2,448,256]{2,1,0:T(8,128)(2,1)}, u32[]{:S(2)}, u32[]{:S(2)}) %collective-permute-start.9) | collective-permute-done | bytes 458784 | tf_op jit(solution)/shard_map/ppermute | solution.py:363
  65.8 4.3 %collective-permute-done.6.refs_4_.refs_5_ = bf16[2,448,256]{2,1,0:T(8,128)(2,1)S(1)} collective-permute-done((bf16[2,448,256]{2,1,0:T(8,128)(2,1)S(1)}, bf16[2,448,256]{2,1,0:T(8,128)(2,1)S(1)}, u32[]{:S(2)}, u32[]{:S(2)}) %collective-permute-start.6) | collective-permute-done | bytes 458784 | tf_op jit(solution)/shard_map/ppermute | solution.py:363
  71.9 1.2 collective-permute-start.7
  73.2 4.8 %collective-permute-done.10.refs_5_.refs_6_ = bf16[2,448,256]{2,1,0:T(8,128)(2,1)} collective-permute-done((bf16[2,448,256]{2,1,0:T(8,128)(2,1)}, bf16[2,448,256]{2,1,0:T(8,128)(2,1)}, u32[]{:S(2)}, u32[]{:S(2)}) %collective-permute-start.10) | collective-permute-done | bytes 458784 | tf_op jit(solution)/shard_map/ppermute | solution.py:363
  78.0 1.6 slice.17.refs_0_
  80.0 1.0 copy-done.15
  81.0 1.0 copy-done.18
  82.0 1.0 copy-done.21
  83.0 3.3 %shard_map.97.refs_6_ = f32[512,512]{1,0:T(8,128)S(1)} custom-call(s32[3]{0:T(128)S(1)} %pad_add_fusion.me_ref, bf16[8,128,512]{2,1,0:T(8,128)(2,1)} %shard_map.94.refs_0_, bf16[8,128,512]{2,1,0:T(8,128)(2,1)S(1)} %copy-done.3, bf16[8,128,512]{2,1,0:T(8,128)(2,1)} %collective-permute-done.2.refs_2_, bf16[8,128,512]{2,1,0:T(8,128)(2,1)S(1)} %collective-permute-done.3.refs_3_, ...), custom_call_target="tpu_custom_call" | custom-call | flops 1174405120 | bytes 6488064 | tf_op jit(solution)/shard_map/pallas_call | solution.py:36
  86.4 2.4 %shard_map.98.refs_6_ = f32[512,512]{1,0:T(8,128)S(1)} custom-call(s32[3]{0:T(128)S(1)} %pad_add_fusion.me_ref, bf16[8,128,512]{2,1,0:T(8,128)(2,1)} %shard_map.94.refs_0_, bf16[8,128,512]{2,1,0:T(8,128)(2,1)S(1)} %copy-done.3, bf16[8,128,512]{2,1,0:T(8,128)(2,1)} %collective-permute-done.2.refs_2_, bf16[8,128,512]{2,1,0:T(8,128)(2,1)S(1)} %collective-permute-done.3.refs_3_, ...), custom_call_target="tpu_custom_call" | custom-call | flops 469762048 | bytes 6160384 | tf_op jit(solution)/shard_map/pallas_call | solution.py:36
  90.4 1.2 copy-done.5
  92.6 2.3 %shard_map.99 = (bf16[512,256]{1,0:T(8,128)(2,1)S(1)}, f32[512,1]{1,0:T(8,128)S(1)}, f32[512,1]{1,0:T(8,128)S(1)}, f32[1,512]{1,0:T(1,128)S(1)}) custom-call(s32[3]{0:T(128)S(1)} %pad_add_fusion.me_ref, bf16[8,128,512]{2,1,0:T(8,128)(2,1)} %shard_map.94.refs_0_, bf16[8,128,512]{2,1,0:T(8,128)(2,1)S(1)} %copy-done.3, ...), custom_call_target="tpu_custom_call" | custom-call | flops 234881024 | bytes 6750208 | tf_op jit(solution)/shard_map/pallas_call | solution.py:36
  96.4 3.4 %shard_map.104.w_ref = bf16[8,2,448,256]{3,2,1,0:T(8,128)(2,1)} custom-call(s32[3]{0:T(128)S(1)} %pad_add_fusion.me_ref, bf16[2,448,256]{2,1,0:T(8,128)(2,1)} %refs_0_.1, bf16[2,448,256]{2,1,0:T(8,128)(2,1)S(1)} %copy-done.16, bf16[2,448,256]{2,1,0:T(8,128)(2,1)S(1)} %copy-done.19, bf16[2,448,256]{2,1,0:T(8,128)(2,1)S(1)} %copy-done.22, ...), custom_call_target="tpu_custom_call" | custom-call | bytes 3932160 | tf_op jit(solution)/shard_map/pallas_call | solution.py:36
  99.8 5.2 %all-to-all-start.1 = ((bf16[8,128,512]{2,1,0:T(8,128)(2,1)}), bf16[8,128,512]{2,1,0:T(8,128)(2,1)S(1)}, u32[]{:S(2)}, u32[]{:S(2)}) async-start(bf16[8,128,512]{2,1,0:T(8,128)(2,1)} %collective-permute-done.2.refs_2_), calls=%async_computation.1 | async-start | bytes 2097152 | tf_op jit(solution)/shard_map/all_to_all | solution.py:373
  105.7 1.2 copy-done.40
  107.8 5.4 %shard_map.100 = (bf16[2,128,896]{2,1,0:T(8,128)(2,1)S(1)}, bf16[2,128,896]{2,1,0:T(8,128)(2,1)S(1)}, f32[512,256]{1,0:T(8,128)S(1)}) custom-call(s32[3]{0:T(128)S(1)} %pad_add_fusion.me_ref, bf16[2,2,128,896]{3,2,1,0:T(8,128)(2,1)S(1)} %copy-done.40, bf16[2,2,128,896]{3,2,1,0:T(8,128)(2,1)} %collective-permute-done.refs_2_.pack_ref, ...), custom_call_target="tpu_custom_call" | custom-call | flops 1879048192 | bytes 2101248 | tf_op jit(solution)/shard_map/pallas_call | solution.py:36
  114.0 6.5 %shard_map.101 = (bf16[2,128,896]{2,1,0:T(8,128)(2,1)S(1)}, bf16[2,128,896]{2,1,0:T(8,128)(2,1)}, f32[512,256]{1,0:T(8,128)}) custom-call(s32[3]{0:T(128)S(1)} %pad_add_fusion.2.me_ref, bf16[2,2,128,896]{3,2,1,0:T(8,128)(2,1)S(1)} %copy-done.40, bf16[2,2,128,896]{3,2,1,0:T(8,128)(2,1)} %collective-permute-done.refs_2_.pack_ref, ...), custom_call_target="tpu_custom_call" | custom-call | flops 1879048192 | bytes 2625536 | tf_op jit(solution)/shard_map/pallas_call | solution.py:36
  121.2 1.5 collective-permute-start.15
  122.7 8.7 %all-to-all-done.1.refs_1_.refs_2_ = bf16[8,128,512]{2,1,0:T(8,128)(2,1)S(1)} async-done(((bf16[8,128,512]{2,1,0:T(8,128)(2,1)}), bf16[8,128,512]{2,1,0:T(8,128)(2,1)S(1)}, u32[]{:S(2)}, u32[]{:S(2)}) %all-to-all-start.1) | async-done | bytes 1048608 | tf_op jit(solution)/shard_map/all_to_all | solution.py:373
  131.4 1.1 copy-done
  132.5 2.7 %collective-permute-done.15 = f32[512,256]{1,0:T(8,128)S(1)} collective-permute-done((f32[512,256]{1,0:T(8,128)}, f32[512,256]{1,0:T(8,128)S(1)}, u32[]{:S(2)}, u32[]{:S(2)}) %collective-permute-start.15) | collective-permute-done | bytes 524320 | tf_op jit(solution)/shard_map/ppermute | solution.py:360
  135.2 1.1 add_convert_fusion.1.g_ref.refs_0_
  139.0 6.4 %shard_map.105 = (f32[128,3584]{1,0:T(8,128)S(1)}, bf16[128,3584]{1,0:T(8,128)(2,1)}) custom-call(s32[3]{0:T(128)S(1)} %pad_add_fusion.me_ref, f32[512,1]{1,0:T(8,128)S(1)} %copy-done.34, bf16[512,256]{1,0:T(8,128)(2,1)S(1)} %add_convert_fusion.1.g_ref.refs_0_, bf16[512,256]{1,0:T(8,128)(2,1)S(1)} %collective-permute-done.16.gc_ref, ...), custom_call_target="tpu_custom_call" | custom-call | flops 1879048192 | bytes 7866368 | tf_op jit(solution)/shard_map/pallas_call | solution.py:36
  145.4 1.2 copy-done.12
  146.7 1.5 collective-permute-start.18
  148.2 1.7 collective-permute-start.21
  150.2 6.5 %collective-permute-done.21.refs_5_ = bf16[512,256]{1,0:T(8,128)(2,1)S(1)} collective-permute-done((bf16[512,256]{1,0:T(8,128)(2,1)}, bf16[512,256]{1,0:T(8,128)(2,1)S(1)}, u32[]{:S(2)}, u32[]{:S(2)}) %collective-permute-start.21) | collective-permute-done | bytes 262176 | tf_op jit(solution)/shard_map/ppermute | solution.py:363
  156.7 1.7 collective-permute-start.22
  158.8 5.5 %collective-permute-done.22.refs_7_ = bf16[512,256]{1,0:T(8,128)(2,1)S(1)} collective-permute-done((bf16[512,256]{1,0:T(8,128)(2,1)S(1)}, bf16[512,256]{1,0:T(8,128)(2,1)S(1)}, u32[]{:S(2)}, u32[]{:S(2)}) %collective-permute-start.22) | collective-permute-done | bytes 262176 | tf_op jit(solution)/shard_map/ppermute | solution.py:363
  164.3 1.7 collective-permute-start.23
  168.3 2.5 %shard_map.102 = (bf16[128,3584]{1,0:T(8,128)(2,1)}, bf16[128,3584]{1,0:T(8,128)(2,1)}) custom-call(s32[3]{0:T(128)S(1)} %pad_add_fusion.me_ref, bf16[2,128,896]{2,1,0:T(8,128)(2,1)S(1)} %copy-done.30, bf16[2,128,896]{2,1,0:T(8,128)(2,1)} %collective-permute-done.12.refs_1_, bf16[2,128,896]{2,1,0:T(8,128)(2,1)S(1)} %copy-done.32, ...), custom_call_target="tpu_custom_call" | custom-call | bytes 1835008 | tf_op jit(solution)/shard_map/pallas_call | solution.py:36
  170.9 3.2 %shard_map.107.refs_6_ = f32[512,512]{1,0:T(8,128)S(1)} custom-call(s32[3]{0:T(128)S(1)} %pad_add_fusion.me_ref, bf16[8,128,512]{2,1,0:T(8,128)(2,1)S(1)} %all-to-all-done.refs_7_.refs_0_, bf16[8,128,512]{2,1,0:T(8,128)(2,1)S(1)} %collective-permute-done.19.refs_1_, bf16[8,128,512]{2,1,0:T(8,128)(2,1)S(1)} %copy-done.1, ...), custom_call_target="tpu_custom_call" | custom-call | flops 1342177280 | bytes 5505024 | tf_op jit(solution)/shard_map/pallas_call | solution.py:36
  174.1 1.7 collective-permute-start.24
  176.2 2.3 %shard_map.108.refs_6_ = f32[512,512]{1,0:T(8,128)S(1)} custom-call(s32[3]{0:T(128)S(1)} %pad_add_fusion.me_ref, bf16[8,128,512]{2,1,0:T(8,128)(2,1)S(1)} %all-to-all-done.refs_7_.refs_0_, bf16[8,128,512]{2,1,0:T(8,128)(2,1)S(1)} %collective-permute-done.19.refs_1_, bf16[8,128,512]{2,1,0:T(8,128)(2,1)S(1)} %copy-done.1, ...), custom_call_target="tpu_custom_call" | custom-call | flops 536870912 | bytes 5767168 | tf_op jit(solution)/shard_map/pallas_call | solution.py:36
  178.6 2.3 %fusion = bf16[1,128,3584]{2,1,0:T(8,128)(2,1)} fusion(f32[128,3584]{1,0:T(8,128)S(1)} %copy-done.13, bf16[128,3584]{1,0:T(8,128)(2,1)} %collective-permute-done.18), kind=kLoop, calls=%fused_computation.1 | loop fusion | flops 1376256 | bytes 3670016 | tf_op jit(solution)/shard_map/broadcast_in_dim | solution.py:424
  180.9 2.7 %shard_map.109 = f32[2,448,256]{2,1,0:T(8,128)} custom-call(s32[3]{0:T(128)S(1)} %pad_add_fusion.me_ref, bf16[8,128,512]{2,1,0:T(8,128)(2,1)S(1)} %all-to-all-done.refs_7_.refs_0_, bf16[8,128,512]{2,1,0:T(8,128)(2,1)S(1)} %collective-permute-done.19.refs_1_, bf16[8,128,512]{2,1,0:T(8,128)(2,1)S(1)} %copy-done.1, ...), custom_call_target="tpu_custom_call" | custom-call | flops 268435456 | bytes 5505024 | tf_op jit(solution)/shard_map/pallas_call | solution.py:36
  (129 shorter events, 20.7 us)
Async XLA Ops:
  5.1 26.4 %collective-permute-start.2 = (bf16[8,128,512]{2,1,0:T(8,128)(2,1)}, bf16[8,128,512]{2,1,0:T(8,128)(2,1)}, u32[]{:S(2)}, u32[]{:S(2)}) collective-permute-start(bf16[8,128,512]{2,1,0:T(8,128)(2,1)} %shard_map.94.refs_0_), channel_id=1, source_target_pairs={{0,2},{1,3},{2,0},{3,1},{4,6},{5,7},{6,4},{7,5},{8,10},{9,11},{10,... | collective-permute-start | bytes 3145736 | tf_op jit(solution)/shard_map/ppermute | solution.py:360
  8.1 82.3 %all-to-all-start = ((bf16[8,128,512]{2,1,0:T(8,128)(2,1)}), bf16[8,128,512]{2,1,0:T(8,128)(2,1)S(1)}, u32[]{:S(2)}, u32[]{:S(2)}) async-start(bf16[8,128,512]{2,1,0:T(8,128)(2,1)} %shard_map.94.refs_0_), calls=%async_computation | async-start | bytes 2097152 | tf_op jit(solution)/shard_map/all_to_all | solution.py:373
  13.9 26.7 %collective-permute-start.4 = (bf16[2,448,256]{2,1,0:T(8,128)(2,1)}, bf16[2,448,256]{2,1,0:T(8,128)(2,1)S(1)}, u32[]{:S(2)}, u32[]{:S(2)}) collective-permute-start(bf16[2,448,256]{2,1,0:T(8,128)(2,1)} %refs_0_.1), channel_id=1, source_target_pairs={{0,8},{8,16},{16,24},{24,28},{28,20},{20,12},{12,4},{4,0},{1,9},{9... | collective-permute-start | bytes 1376264 | tf_op jit(solution)/shard_map/ppermute | solution.py:363
  15.9 35.8 %collective-permute-start.8 = (bf16[2,448,256]{2,1,0:T(8,128)(2,1)}, bf16[2,448,256]{2,1,0:T(8,128)(2,1)S(1)}, u32[]{:S(2)}, u32[]{:S(2)}) collective-permute-start(bf16[2,448,256]{2,1,0:T(8,128)(2,1)} %refs_0_.1), channel_id=1, source_target_pairs={{0,4},{8,0},{16,8},{24,16},{28,24},{20,28},{12,20},{4,12},{1,5},{9... | collective-permute-start | bytes 1376264 | tf_op jit(solution)/shard_map/ppermute | solution.py:363
  15.9 55.0 %collective-permute-start.1 = (bf16[8,128,512]{2,1,0:T(8,128)(2,1)}, bf16[8,128,512]{2,1,0:T(8,128)(2,1)S(1)}, u32[]{:S(2)}, u32[]{:S(2)}) collective-permute-start(bf16[8,128,512]{2,1,0:T(8,128)(2,1)} %shard_map.94.refs_0_), channel_id=1, source_target_pairs={{0,1},{1,0},{2,3},{3,2},{4,5},{5,4},{6,7},{7,6},{8,9},{9,8},{10,11... | collective-permute-start | bytes 3145736 | tf_op jit(solution)/shard_map/ppermute | solution.py:360
  31.5 48.4 %collective-permute-start.3 = (bf16[8,128,512]{2,1,0:T(8,128)(2,1)}, bf16[8,128,512]{2,1,0:T(8,128)(2,1)S(1)}, u32[]{:S(2)}, u32[]{:S(2)}) collective-permute-start(bf16[8,128,512]{2,1,0:T(8,128)(2,1)} %collective-permute-done.2.refs_2_), channel_id=1, source_target_pairs={{0,1},{1,0},{2,3},{3,2},{4,5},{5,4},{6,7},{7,6},{8,9},{9,8},{10,11... | collective-permute-start | bytes 3145736 | tf_op jit(solution)/shard_map/ppermute | solution.py:360
  40.5 30.4 %copy-start.14 = (bf16[2,448,256]{2,1,0:T(8,128)(2,1)}, bf16[2,448,256]{2,1,0:T(8,128)(2,1)S(1)}, u32[]{:S(2)}) copy-start(bf16[2,448,256]{2,1,0:T(8,128)(2,1)S(1)} %collective-permute-done.4.refs_5_.refs_1_) | copy-start | bytes 1376260
  40.5 16.9 %collective-permute-start.5 = (bf16[2,448,256]{2,1,0:T(8,128)(2,1)S(1)}, bf16[2,448,256]{2,1,0:T(8,128)(2,1)S(1)}, u32[]{:S(2)}, u32[]{:S(2)}) collective-permute-start(bf16[2,448,256]{2,1,0:T(8,128)(2,1)S(1)} %collective-permute-done.4.refs_5_.refs_1_), channel_id=1, source_target_pairs={{0,8},{8,16},{16,24},{24,28},{28,20},{20,12},{12,4},{4,0},{1,9},{9... | collective-permute-start | bytes 1376264 | tf_op jit(solution)/shard_map/ppermute | solution.py:363
  51.6 19.3 %collective-permute-start = (bf16[2,2,128,896]{3,2,1,0:T(8,128)(2,1)S(1)}, bf16[2,2,128,896]{3,2,1,0:T(8,128)(2,1)}, u32[]{:S(2)}, u32[]{:S(2)}) collective-permute-start(bf16[2,2,128,896]{3,2,1,0:T(8,128)(2,1)S(1)} %get-tuple-element.21), channel_id=1, source_target_pairs={{0,1},{1,0},{2,3},{3,2},{4,5},{5,4},{6,7},{7,6},{8,9},{9,8},{10,11... | collective-permute-start | bytes 2752520 | tf_op jit(solution)/shard_map/ppermute | solution.py:360
  51.6 13.7 %collective-permute-start.9 = (bf16[2,448,256]{2,1,0:T(8,128)(2,1)S(1)}, bf16[2,448,256]{2,1,0:T(8,128)(2,1)}, u32[]{:S(2)}, u32[]{:S(2)}) collective-permute-start(bf16[2,448,256]{2,1,0:T(8,128)(2,1)S(1)} %collective-permute-done.8.refs_6_.refs_2_), channel_id=1, source_target_pairs={{0,4},{8,0},{16,8},{24,16},{28,24},{20,28},{12,20},{4,12},{1,5},{9... | collective-permute-start | bytes 1376264 | tf_op jit(solution)/shard_map/ppermute | solution.py:363
  57.4 12.7 %collective-permute-start.6 = (bf16[2,448,256]{2,1,0:T(8,128)(2,1)S(1)}, bf16[2,448,256]{2,1,0:T(8,128)(2,1)S(1)}, u32[]{:S(2)}, u32[]{:S(2)}) collective-permute-start(bf16[2,448,256]{2,1,0:T(8,128)(2,1)S(1)} %collective-permute-done.5.refs_7_.refs_3_), channel_id=1, source_target_pairs={{0,8},{8,16},{16,24},{24,28},{28,20},{20,12},{12,4},{4,0},{1,9},{9... | collective-permute-start | bytes 1376264 | tf_op jit(solution)/shard_map/ppermute | solution.py:363
  65.3 12.7 %collective-permute-start.10 = (bf16[2,448,256]{2,1,0:T(8,128)(2,1)}, bf16[2,448,256]{2,1,0:T(8,128)(2,1)}, u32[]{:S(2)}, u32[]{:S(2)}) collective-permute-start(bf16[2,448,256]{2,1,0:T(8,128)(2,1)} %collective-permute-done.9.refs_8_.refs_4_), channel_id=1, source_target_pairs={{0,4},{8,0},{16,8},{24,16},{28,24},{20,28},{12,20},{4,12},{1,5},{9... | collective-permute-start | bytes 1376264 | tf_op jit(solution)/shard_map/ppermute | solution.py:363
  71.9 8.1 %copy-start.3 = (bf16[8,128,512]{2,1,0:T(8,128)(2,1)S(1)}, bf16[8,128,512]{2,1,0:T(8,128)(2,1)}, u32[]{:S(2)}) copy-start(bf16[8,128,512]{2,1,0:T(8,128)(2,1)} %copy-done.2) | copy-start | bytes 3145732
  71.9 17.8 %collective-permute-start.7 = (bf16[2,224,256]{2,1,0:T(8,128)(2,1)}, bf16[2,224,256]{2,1,0:T(8,128)(2,1)S(1)}, u32[]{:S(2)}, u32[]{:S(2)}) collective-permute-start(bf16[2,224,256]{2,1,0:T(8,128)(2,1)} %shard_map.95), channel_id=1, source_target_pairs={{0,8},{8,16},{16,24},{24,28},{28,20},{20,12},{12,4},{4,0},{1,9},{9... | collective-permute-start | bytes 688136 | tf_op jit(solution)/shard_map/ppermute | solution.py:363
  79.6 6.7 %copy-start.9 = (bf16[2,448,256]{2,1,0:T(8,128)(2,1)S(1)}, bf16[2,448,256]{2,1,0:T(8,128)(2,1)}, u32[]{:S(2)}) copy-start(bf16[2,448,256]{2,1,0:T(8,128)(2,1)} %copy-done.8) | copy-start | bytes 1376260
  79.6 10.1 %collective-permute-start.11 = (bf16[2,224,256]{2,1,0:T(8,128)(2,1)}, bf16[2,224,256]{2,1,0:T(8,128)(2,1)S(1)}, u32[]{:S(2)}, u32[]{:S(2)}) collective-permute-start(bf16[2,224,256]{2,1,0:T(8,128)(2,1)} %shard_map.96), channel_id=1, source_target_pairs={{0,4},{8,0},{16,8},{24,16},{28,24},{20,28},{12,20},{4,12},{1,5},{9... | collective-permute-start | bytes 688136 | tf_op jit(solution)/shard_map/ppermute | solution.py:363
  92.6 3.8 %copy-start.10 = (bf16[2,448,256]{2,1,0:T(8,128)(2,1)S(1)}, bf16[2,448,256]{2,1,0:T(8,128)(2,1)}, u32[]{:S(2)}) copy-start(bf16[2,448,256]{2,1,0:T(8,128)(2,1)} %copy-done.8) | copy-start | bytes 1376260
  92.6 3.8 %copy-start.16 = (bf16[2,448,256]{2,1,0:T(8,128)(2,1)S(1)}, bf16[2,448,256]{2,1,0:T(8,128)(2,1)}, u32[]{:S(2)}) copy-start(bf16[2,448,256]{2,1,0:T(8,128)(2,1)} %copy-done.14) | copy-start | bytes 1376260
  92.6 3.8 %copy-start.19 = (bf16[2,448,256]{2,1,0:T(8,128)(2,1)S(1)}, bf16[2,448,256]{2,1,0:T(8,128)(2,1)}, u32[]{:S(2)}) copy-start(bf16[2,448,256]{2,1,0:T(8,128)(2,1)} %copy-done.17) | copy-start | bytes 1376260
  92.6 3.8 %copy-start.22 = (bf16[2,448,256]{2,1,0:T(8,128)(2,1)S(1)}, bf16[2,448,256]{2,1,0:T(8,128)(2,1)}, u32[]{:S(2)}) copy-start(bf16[2,448,256]{2,1,0:T(8,128)(2,1)} %copy-done.20) | copy-start | bytes 1376260
  92.6 3.8 %copy-start.28 = (bf16[2,224,256]{2,1,0:T(8,128)(2,1)S(1)}, bf16[2,224,256]{2,1,0:T(8,128)(2,1)}, u32[]{:S(2)}) copy-start(bf16[2,224,256]{2,1,0:T(8,128)(2,1)} %copy-done.26) | copy-start | bytes 688132
  96.3 3.5 %copy-start.35 = (bf16[512,256]{1,0:T(8,128)(2,1)}, bf16[512,256]{1,0:T(8,128)(2,1)S(1)}, u32[]{:S(2)}) copy-start(bf16[512,256]{1,0:T(8,128)(2,1)S(1)} %get-tuple-element.22.kv_ref.refs_9_) | copy-start | bytes 786436
  99.8 38.2 %collective-permute-start.17 = (bf16[8,2,448,256]{3,2,1,0:T(8,128)(2,1)}, bf16[8,2,448,256]{3,2,1,0:T(8,128)(2,1)}, u32[]{:S(2)}, u32[]{:S(2)}) collective-permute-start(bf16[8,2,448,256]{3,2,1,0:T(8,128)(2,1)} %shard_map.104.w_ref), channel_id=1, source_target_pairs={{0,1},{1,0},{2,3},{3,2},{4,5},{5,4},{6,7},{7,6},{8,9},{9,8},{10,11... | collective-permute-start | bytes 11010056 | tf_op jit(solution)/shard_map/ppermute | solution.py:360
  99.8 5.2 %copy-start.36 = (bf16[512,256]{1,0:T(8,128)(2,1)S(1)}, bf16[512,256]{1,0:T(8,128)(2,1)}, u32[]{:S(2)}) copy-start(bf16[512,256]{1,0:T(8,128)(2,1)} %copy-done.35) | copy-start | bytes 786436
  99.8 31.6 %all-to-all-start.1 = ((bf16[8,128,512]{2,1,0:T(8,128)(2,1)}), bf16[8,128,512]{2,1,0:T(8,128)(2,1)S(1)}, u32[]{:S(2)}, u32[]{:S(2)}) async-start(bf16[8,128,512]{2,1,0:T(8,128)(2,1)} %collective-permute-done.2.refs_2_), calls=%async_computation.1 | async-start | bytes 2097152 | tf_op jit(solution)/shard_map/all_to_all | solution.py:373
  105.0 8.9 %collective-permute-start.13 = (bf16[512,256]{1,0:T(8,128)(2,1)S(1)}, bf16[512,256]{1,0:T(8,128)(2,1)S(1)}, u32[]{:S(2)}, u32[]{:S(2)}) collective-permute-start(bf16[512,256]{1,0:T(8,128)(2,1)S(1)} %copy-done.36), channel_id=1, source_target_pairs={{0,2},{1,3},{2,0},{3,1},{4,6},{5,7},{6,4},{7,5},{8,10},{9,11},{10,... | collective-permute-start | bytes 786440 | tf_op jit(solution)/shard_map/ppermute | solution.py:360
  107.8 6.2 %copy-start.44 = (f32[512,1]{1,0:T(8,128)S(1)}, f32[512,1]{1,0:T(8,128)}, u32[]{:S(2)}) copy-start(f32[512,1]{1,0:T(8,128)} %copy-done.42) | copy-start | bytes 6148
  114.0 6.5 %copy-start.11 = (f32[512,256]{1,0:T(8,128)}, f32[512,256]{1,0:T(8,128)S(1)}, u32[]{:S(2)}) copy-start(f32[512,256]{1,0:T(8,128)S(1)} %get-tuple-element.27.refs_0_) | copy-start | bytes 1572868
  114.0 18.5 %copy-start.41 = (bf16[2,128,896]{2,1,0:T(8,128)(2,1)}, bf16[2,128,896]{2,1,0:T(8,128)(2,1)S(1)}, u32[]{:S(2)}) copy-start(bf16[2,128,896]{2,1,0:T(8,128)(2,1)S(1)} %get-tuple-element.26) | copy-start | bytes 1376260
  121.2 14.0 %collective-permute-start.15 = (f32[512,256]{1,0:T(8,128)}, f32[512,256]{1,0:T(8,128)S(1)}, u32[]{:S(2)}, u32[]{:S(2)}) collective-permute-start(f32[512,256]{1,0:T(8,128)} %get-tuple-element.33), channel_id=1, source_target_pairs={{0,2},{1,3},{2,0},{3,1},{4,6},{5,7},{6,4},{7,5},{8,10},{9,11},{10,... | collective-permute-start | bytes 1572872 | tf_op jit(solution)/shard_map/ppermute | solution.py:360
  136.3 9.1 %copy-start.6 = (bf16[512,256]{1,0:T(8,128)(2,1)}, bf16[512,256]{1,0:T(8,128)(2,1)S(1)}, u32[]{:S(2)}) copy-start(bf16[512,256]{1,0:T(8,128)(2,1)S(1)} %add_convert_fusion.1.g_ref.refs_0_) | copy-start | bytes 786436
  136.3 1.6 collective-permute-start.16
  136.4 11.8 %collective-permute-start.12 = (bf16[2,128,896]{2,1,0:T(8,128)(2,1)}, bf16[2,128,896]{2,1,0:T(8,128)(2,1)}, u32[]{:S(2)}, u32[]{:S(2)}) collective-permute-start(bf16[2,128,896]{2,1,0:T(8,128)(2,1)} %copy-done.41), channel_id=1, source_target_pairs={{0,1},{1,0},{2,3},{3,2},{4,5},{5,4},{6,7},{7,6},{8,9},{9,8},{10,11... | collective-permute-start | bytes 1376264 | tf_op jit(solution)/shard_map/ppermute | solution.py:360
  136.9 13.0 %collective-permute-start.14 = (bf16[2,128,896]{2,1,0:T(8,128)(2,1)}, bf16[2,128,896]{2,1,0:T(8,128)(2,1)}, u32[]{:S(2)}, u32[]{:S(2)}) collective-permute-start(bf16[2,128,896]{2,1,0:T(8,128)(2,1)} %get-tuple-element.29), channel_id=1, source_target_pairs={{0,1},{1,0},{2,3},{3,2},{4,5},{5,4},{6,7},{7,6},{8,9},{9,8},{10,11... | collective-permute-start | bytes 1376264 | tf_op jit(solution)/shard_map/ppermute | solution.py:360
  137.0 33.9 %collective-permute-start.19 = (bf16[8,128,512]{2,1,0:T(8,128)(2,1)S(1)}, bf16[8,128,512]{2,1,0:T(8,128)(2,1)S(1)}, u32[]{:S(2)}, u32[]{:S(2)}) collective-permute-start(bf16[8,128,512]{2,1,0:T(8,128)(2,1)S(1)} %all-to-all-done.refs_7_.refs_0_), channel_id=1, source_target_pairs={{0,1},{1,0},{2,3},{3,2},{4,5},{5,4},{6,7},{7,6},{8,9},{9,8},{10,11... | collective-permute-start | bytes 3145736 | tf_op jit(solution)/shard_map/ppermute | solution.py:360
  137.9 33.0 %collective-permute-start.20 = (bf16[8,128,512]{2,1,0:T(8,128)(2,1)}, bf16[8,128,512]{2,1,0:T(8,128)(2,1)}, u32[]{:S(2)}, u32[]{:S(2)}) collective-permute-start(bf16[8,128,512]{2,1,0:T(8,128)(2,1)} %copy-done), channel_id=1, source_target_pairs={{0,1},{1,0},{2,3},{3,2},{4,5},{5,4},{6,7},{7,6},{8,9},{9,8},{10,11... | collective-permute-start | bytes 3145736 | tf_op jit(solution)/shard_map/ppermute | solution.py:360
  146.7 24.2 %copy-start.1 = (bf16[8,128,512]{2,1,0:T(8,128)(2,1)S(1)}, bf16[8,128,512]{2,1,0:T(8,128)(2,1)}, u32[]{:S(2)}) copy-start(bf16[8,128,512]{2,1,0:T(8,128)(2,1)} %copy-done) | copy-start | bytes 3145732
  146.7 31.9 %collective-permute-start.18 = (bf16[128,3584]{1,0:T(8,128)(2,1)}, bf16[128,3584]{1,0:T(8,128)(2,1)}, u32[]{:S(2)}, u32[]{:S(2)}) collective-permute-start(bf16[128,3584]{1,0:T(8,128)(2,1)} %get-tuple-element.35.refs_1_), channel_id=1, source_target_pairs={{0,2},{1,3},{2,0},{3,1},{4,6},{5,7},{6,4},{7,5},{8,10},{9,11},{10,... | collective-permute-start | bytes 2752520 | tf_op jit(solution)/shard_map/ppermute | solution.py:360
  148.2 22.7 %copy-start.7 = (bf16[512,256]{1,0:T(8,128)(2,1)S(1)}, bf16[512,256]{1,0:T(8,128)(2,1)}, u32[]{:S(2)}) copy-start(bf16[512,256]{1,0:T(8,128)(2,1)} %shard_map.106.refs_4_) | copy-start | bytes 786436
  148.2 8.5 %collective-permute-start.21 = (bf16[512,256]{1,0:T(8,128)(2,1)}, bf16[512,256]{1,0:T(8,128)(2,1)S(1)}, u32[]{:S(2)}, u32[]{:S(2)}) collective-permute-start(bf16[512,256]{1,0:T(8,128)(2,1)} %shard_map.106.refs_4_), channel_id=1, source_target_pairs={{0,8},{8,16},{16,24},{24,28},{28,20},{20,12},{12,4},{4,0},{1,9},{9... | collective-permute-start | bytes 786440 | tf_op jit(solution)/shard_map/ppermute | solution.py:363
  149.9 8.5 %collective-permute-start.25 = (bf16[512,256]{1,0:T(8,128)(2,1)}, bf16[512,256]{1,0:T(8,128)(2,1)S(1)}, u32[]{:S(2)}, u32[]{:S(2)}) collective-permute-start(bf16[512,256]{1,0:T(8,128)(2,1)} %shard_map.106.refs_4_), channel_id=1, source_target_pairs={{0,4},{8,0},{16,8},{24,16},{28,24},{20,28},{12,20},{4,12},{1,5},{9... | collective-permute-start | bytes 786440 | tf_op jit(solution)/shard_map/ppermute | solution.py:363
  156.7 7.6 %collective-permute-start.22 = (bf16[512,256]{1,0:T(8,128)(2,1)S(1)}, bf16[512,256]{1,0:T(8,128)(2,1)S(1)}, u32[]{:S(2)}, u32[]{:S(2)}) collective-permute-start(bf16[512,256]{1,0:T(8,128)(2,1)S(1)} %collective-permute-done.21.refs_5_), channel_id=1, source_target_pairs={{0,8},{8,16},{16,24},{24,28},{28,20},{20,12},{12,4},{4,0},{1,9},{9... | collective-permute-start | bytes 786440 | tf_op jit(solution)/shard_map/ppermute | solution.py:363
  158.4 7.6 %collective-permute-start.26 = (bf16[512,256]{1,0:T(8,128)(2,1)S(1)}, bf16[512,256]{1,0:T(8,128)(2,1)S(1)}, u32[]{:S(2)}, u32[]{:S(2)}) collective-permute-start(bf16[512,256]{1,0:T(8,128)(2,1)S(1)} %collective-permute-done.25.refs_6_), channel_id=1, source_target_pairs={{0,4},{8,0},{16,8},{24,16},{28,24},{20,28},{12,20},{4,12},{1,5},{9... | collective-permute-start | bytes 786440 | tf_op jit(solution)/shard_map/ppermute | solution.py:363
  164.3 9.8 %collective-permute-start.23 = (bf16[512,256]{1,0:T(8,128)(2,1)S(1)}, bf16[512,256]{1,0:T(8,128)(2,1)S(1)}, u32[]{:S(2)}, u32[]{:S(2)}) collective-permute-start(bf16[512,256]{1,0:T(8,128)(2,1)S(1)} %collective-permute-done.22.refs_7_), channel_id=1, source_target_pairs={{0,8},{8,16},{16,24},{24,28},{28,20},{20,12},{12,4},{4,0},{1,9},{9... | collective-permute-start | bytes 786440 | tf_op jit(solution)/shard_map/ppermute | solution.py:363
  165.9 9.9 %collective-permute-start.27 = (bf16[512,256]{1,0:T(8,128)(2,1)S(1)}, bf16[512,256]{1,0:T(8,128)(2,1)S(1)}, u32[]{:S(2)}, u32[]{:S(2)}) collective-permute-start(bf16[512,256]{1,0:T(8,128)(2,1)S(1)} %collective-permute-done.26.refs_8_), channel_id=1, source_target_pairs={{0,4},{8,0},{16,8},{24,16},{28,24},{20,28},{12,20},{4,12},{1,5},{9... | collective-permute-start | bytes 786440 | tf_op jit(solution)/shard_map/ppermute | solution.py:363
  174.1 6.8 %collective-permute-start.24 = (bf16[256,256]{1,0:T(8,128)(2,1)S(1)}, bf16[256,256]{1,0:T(8,128)(2,1)S(1)}, u32[]{:S(2)}, u32[]{:S(2)}) collective-permute-start(bf16[256,256]{1,0:T(8,128)(2,1)S(1)} %slice.18), channel_id=1, source_target_pairs={{0,8},{8,16},{16,24},{24,28},{28,20},{20,12},{12,4},{4,0},{1,9},{9... | collective-permute-start | bytes 393224 | tf_op jit(solution)/shard_map/ppermute | solution.py:363
  175.8 2.7 %copy-start.13 = (f32[128,3584]{1,0:T(8,128)S(1)}, f32[128,3584]{1,0:T(8,128)}, u32[]{:S(2)}) copy-start(f32[128,3584]{1,0:T(8,128)} %copy-done.12) | copy-start | bytes 5505028
  175.8 5.0 %collective-permute-start.28 = (bf16[256,256]{1,0:T(8,128)(2,1)S(1)}, bf16[256,256]{1,0:T(8,128)(2,1)S(1)}, u32[]{:S(2)}, u32[]{:S(2)}) collective-permute-start(bf16[256,256]{1,0:T(8,128)(2,1)S(1)} %slice.19), channel_id=1, source_target_pairs={{0,4},{8,0},{16,8},{24,16},{28,24},{20,28},{12,20},{4,12},{1,5},{9... | collective-permute-start | bytes 393224 | tf_op jit(solution)/shard_map/ppermute | solution.py:363
  (28 other events, 26.4 us)

commit v4 on v3

--- a/solution.py
+++ b/solution.py
@@ -30,8 +30,7 @@
     return jax.ShapeDtypeStruct(shape, dtype)
 
 
-def call(body, me, operands, out_shape, flops, scratch=(), aliases=None, anywhere=0):
-    moved = sum(x.size * x.dtype.itemsize for x in operands)
+def call(body, me, operands, out_shape, scratch=(), anywhere=0):
     near = pl.BlockSpec(memory_space=pltpu.VMEM)
     return pl.pallas_call(
         body,
@@ -41,9 +40,8 @@
         out_specs=[near] * len(out_shape) if isinstance(out_shape, list) else near,
         out_shape=out_shape,
         scratch_shapes=scratch,
-        input_output_aliases=aliases or {},
         compiler_params=pltpu.CompilerParams(vmem_limit_bytes=24 * 1024 * 1024),
-        cost_estimate=pl.CostEstimate(flops=flops, bytes_accessed=moved, transcendentals=0),
+        cost_estimate=pl.CostEstimate(flops=0, bytes_accessed=0, transcendentals=0),
     )(me, *operands)
 
 
@@ -91,7 +89,7 @@
     depth = width // count
     lanes = -(-(depth + 3) // 128) * 128
     out = shaped((count, rows, lanes), BF16)
-    return call(functools.partial(blocks_kernel, depth), me, (tokens, kinds, ids), out, 0)
+    return call(functools.partial(blocks_kernel, depth), me, (tokens, kinds, ids), out)
 
 
 def read_marks(block, depth):
@@ -109,7 +107,7 @@
 
 def pack_heads(me, queries, upstream):
     out = shaped((2, 2, queries.shape[0], SPAN), BF16)
-    return call(pack_kernel, me, (queries, upstream), [out, out], 0)
+    return call(pack_kernel, me, (queries, upstream), [out, out])
 
 
 def place_kernel(me_ref, *refs):
@@ -122,7 +120,7 @@
 
 def place_heads(me, found):
     out = shaped((found[0].shape[1], 4 * SPAN), BF16)
-    return call(place_kernel, me, found, [out, out], 0)
+    return call(place_kernel, me, found, [out, out])
 
 
 def project_kernel(steps, depth, halves, first, last, me_ref, *refs):
@@ -167,7 +165,6 @@
         me,
         operands,
         out,
-        4 * length * depth * PAIR * len(steps),
         anywhere=len(wait),
     )
 
@@ -223,7 +220,6 @@
         me,
         (own, pack, kv, ids, ids_row, *wait),
         [side, side, shaped((length, PAIR), F32)],
-        16 * 2 * GROUP * rows * length * HEAD_DIM,
         scratch=[pltpu.VMEM((2 * rows, length), F32), pltpu.VMEM(stacked, F32)] + [pltpu.VMEM(stacked, BF16)] * 4,
         anywhere=len(wait),
     )
@@ -264,7 +260,6 @@
         me,
         (kind, grad, grad_c, weight, weight_c),
         [shaped((rows, width), F32), shaped((rows, width), BF16)],
-        16 * rows * width * PAIR,
     )
 
 
@@ -305,7 +300,6 @@
         me,
         (*parts, *grads, *before),
         shaped((2, depth, PAIR) if last else (lanes, 2 * PAIR), F32),
-        16 * rows * lanes * PAIR * len(steps),
     )
 
 
@@ -322,7 +316,7 @@
 
 def gather_blocks(me, blocks, wait=()):
     out = shaped((len(CYCLE), *blocks[0].shape), blocks[0].dtype)
-    return call(gather_kernel, me, (*blocks, *wait), out, 0, anywhere=len(wait))
+    return call(gather_kernel, me, (*blocks, *wait), out, anywhere=len(wait))
 
 
 def in_order(parts, quarters):
@@ -358,6 +352,10 @@
 
     def swap(x, bit):
         return lax.ppermute(x, "seq", [(i, i ^ bit) for i in range(seq)])
+
+    def over_seq(x):
+        across = swap(x, 2)
+        return [x, swap(x, 1), across, swap(across, 1)]
 
     def turn(x, by):
         return lax.ppermute(x, "fsdp", [(CYCLE[i], CYCLE[(i + by) % fsdp]) for i in range(fsdp)])
@@ -384,31 +382,32 @@
 
     blocks = token_blocks(me, tokens, modality, block_ids, fsdp)
     across = swap(blocks, 2)
-    parts = [blocks, swap(blocks, 1), across, swap(across, 1)]
+    held = (weights[3], weights[4]) if near_link else ()
+    parts = [blocks, swap(blocks, 1), across, swap(after(across, *held), 1)]
     own, pack = pack_heads(me, queries, cotangent)
     pack = swap(pack, 1)
-    columns = exchange_columns(blocks)
-    columns_across = exchange_columns(across)
 
     if near_link:
         ups, downs = halves(*weights[5:], 1)
         weights += both_ways(after(ups, parts[1], pack), after(downs, parts[1], pack))
         total = project(me, STEPS[:5], parts, weights[:5], None, depth)
         total = project(me, STEPS[5:7], parts, weights[5:7], total, depth)
-        kv, kind, ids, ids_row = project(me, STEPS[7:], parts, weights[7:], total, depth, True, True, (columns,))
+        kv, kind, ids, ids_row = project(me, STEPS[7:], parts, weights[7:], total, depth, True, True)
         weight = gather_blocks(me, weights, (kv,))
     else:
         kv, kind, ids, ids_row = project_plain(quarters, parts, weight, depth)
     weight_c = swap(weight, 1)
 
     kv_far = swap(kv, 2)
-    near_own, near_other, near = attend(me, own, pack, kv, ids, ids_row)
-    far_own, far_other, far = attend(me_far, own, pack, kv_far, ids, ids_row, (near,))
-    grad_kv = (after(near, columns_across) + swap(far, 2)).astype(BF16)
+    columns = exchange_columns(after(blocks, kv))
+    far_own, far_other, far = attend(me_far, own, pack, kv_far, ids, ids_row)
+    near_own, near_other, near = attend(me, own, pack, kv, ids, ids_row, (far,))
+    columns = after(columns, near)
+    grad_kv = (after(near, columns) + swap(far, 2)).astype(BF16)
     attended, grad_queries = place_heads(me, (near_own, swap(near_other, 1), far_own, swap(far_other, 1)))
 
     mine, away = hidden_grad(me, kind, grad_kv, swap(grad_kv, 1), weight, weight_c, rows)
-    columns = [columns, swap(columns, 1), columns_across, swap(columns_across, 1)]
+    columns = over_seq(columns)
     if near_link:
         first = after(grad_kv, away)
         grads = [first, *both_ways(first, first)]

time: 185 us -> 185 us (level)
  waiting for transfers between devices: 67.3 us -> 82.7 us
  starting transfers between devices: 40.8 us -> 32.2 us
  local copies, waits for them, and re-layouts: 28.1 us -> 23.1 us
    ppermute x13 -> x14, waiting for transfers between devices: 18.8 us -> 45.7 us  [swap(): return lax.ppermute(x, 'seq', [(i, i ^ bit) for i in range(seq)])]
    ppermute x16, waiting for transfers between devices: 39.8 us -> 32.9 us  [turn(): lax.ppermute(x, 'fsdp', [(CYCLE[i], CYCLE[(i + by) % fsdp]) for i in rang...]
    ppermute x16, starting transfers between devices: 21.9 us -> 16.3 us  [turn(): lax.ppermute(x, 'fsdp', [(CYCLE[i], CYCLE[(i + by) % fsdp]) for i in rang...]
    all_to_all x2 -> x1, starting transfers between devices: 11 us -> 5.95 us  [exchange_columns(): return lax.all_to_all(x, 'fsdp', split_axis=0, concat_axis=0, tiled=True)]
    unnamed x90 -> x81, local copies, waits for them, and re-layouts: 25.7 us -> 20.7 us
    all_to_all x2 -> x1, waiting for transfers between devices: 8.7 us -> 4.03 us  [exchange_columns(): return lax.all_to_all(x, 'fsdp', split_axis=0, concat_axis=0, tiled=True)]
    ppermute x13 -> x14, starting transfers between devices: 7.82 us -> 9.9 us  [swap(): return lax.ppermute(x, 'seq', [(i, i ^ bit) for i in range(seq)])]
  transfers between devices with their start and end apart: 31 -> 31, of which waited for: 11 -> 10; matrix products, arithmetic and copies ran while one was open for 3% -> 4% of each run, Pallas kernels for 18% -> 18%
where the time goes in v4:
time: 185 us; the launch traced here: 184 us
  waiting for transfers between devices  82.7 us (45%)
  Pallas kernels  41.5 us (22%)
  starting transfers between devices  32.2 us (17%)
  local copies, waits for them, and re-layouts  23.1 us (12%)
  other arithmetic  3.58 us (2%)
    ppermute x14, waiting for transfers between devices, swap(): return lax.ppermute(x, 'seq', [(i, i ^ bit) for i in range(seq)])  45.7 us
    pallas_call x13, Pallas kernels, call(): pl.pallas_call(body, in_specs=[pl.BlockSpec(memory_space=pltpu.SMEM)] + [...  41.5 us
    ppermute x16, waiting for transfers between devices, turn(): lax.ppermute(x, 'fsdp', [(CYCLE[i], CYCLE[(i + by) % fsdp]) for i in rang...  32.9 us
    unnamed x81, local copies, waits for them, and re-layouts  20.7 us
    ppermute x16, starting transfers between devices, turn(): lax.ppermute(x, 'fsdp', [(CYCLE[i], CYCLE[(i + by) % fsdp]) for i in rang...  16.3 us
    ppermute x14, starting transfers between devices, swap(): return lax.ppermute(x, 'seq', [(i, i ^ bit) for i in range(seq)])  9.9 us
    all_to_all x1, starting transfers between devices, exchange_columns(): return lax.all_to_all(x, 'fsdp', split_axis=0, concat_axis=0, tiled=True)  5.95 us
    all_to_all x1, waiting for transfers between devices, exchange_columns(): return lax.all_to_all(x, 'fsdp', split_axis=0, concat_axis=0, tiled=True)  4.03 us
  transfers between devices with their start and end apart: 31, of which 10 were waited for; matrix products, arithmetic and copies ran while one was open for 4% of the time, Pallas kernels for 18%

profile of v4, /device:TPU:0, one launch (start us, length us, event | category | flops | bytes accessed | tf_op | source)
XLA Modules:
  0.0 183.9 jit_solution(4842263106087688633)
XLA Ops:
  0.7 1.2 copy-done.27
  4.2 3.0 %collective-permute-start.2 = (bf16[8,128,512]{2,1,0:T(8,128)(2,1)S(1)}, bf16[8,128,512]{2,1,0:T(8,128)(2,1)S(1)}, u32[]{:S(2)}, u32[]{:S(2)}) collective-permute-start(bf16[8,128,512]{2,1,0:T(8,128)(2,1)S(1)} %shard_map.94.refs_0_), channel_id=1, source_target_pairs={{0,2},{1,3},{2,0},{3,1},{4,6},{5,7},{6,4},{7,5},{8,10},{9,11},{10,... | collective-permute-start | bytes 3145736 | tf_op jit(solution)/shard_map/ppermute | solution.py:354
  7.2 1.6 collective-permute-start.3
  9.2 10.0 %collective-permute-done.3.refs_5_.refs_1_ = bf16[2,448,256]{2,1,0:T(8,128)(2,1)S(1)} collective-permute-done((bf16[2,448,256]{2,1,0:T(8,128)(2,1)S(1)}, bf16[2,448,256]{2,1,0:T(8,128)(2,1)S(1)}, u32[]{:S(2)}, u32[]{:S(2)}) %collective-permute-start.3) | collective-permute-done | bytes 458784 | tf_op jit(solution)/shard_map/ppermute | solution.py:361
  19.2 1.6 collective-permute-start.4
  22.0 1.2 copy-done.29
  23.2 1.6 shard_map.93
  26.2 4.1 %collective-permute-done.2.refs_2_ = bf16[8,128,512]{2,1,0:T(8,128)(2,1)S(1)} collective-permute-done((bf16[8,128,512]{2,1,0:T(8,128)(2,1)S(1)}, bf16[8,128,512]{2,1,0:T(8,128)(2,1)S(1)}, u32[]{:S(2)}, u32[]{:S(2)}) %collective-permute-start.2) | collective-permute-done | bytes 1048608 | tf_op jit(solution)/shard_map/ppermute | solution.py:354
  30.4 1.0 copy.17.refs_0_
  31.7 1.6 collective-permute-start.8
  33.7 11.1 %collective-permute-done.8.refs_4_.refs_5_ = bf16[2,448,256]{2,1,0:T(8,128)(2,1)S(1)} collective-permute-done((bf16[2,448,256]{2,1,0:T(8,128)(2,1)}, bf16[2,448,256]{2,1,0:T(8,128)(2,1)S(1)}, u32[]{:S(2)}, u32[]{:S(2)}) %collective-permute-start.8) | collective-permute-done | bytes 458784 | tf_op jit(solution)/shard_map/ppermute | solution.py:361
  45.7 1.0 copy-done.3
  46.6 1.6 collective-permute-start.9
  48.2 1.6 slice.17.refs_0_
  50.3 1.0 copy-done.17
  51.3 1.0 copy-done.20
  52.4 1.0 copy-done.23
  53.4 3.0 %shard_map.98.refs_6_ = f32[512,512]{1,0:T(8,128)S(1)} custom-call(s32[3]{0:T(128)S(1)} %pad_add_fusion.me_ref, bf16[8,128,512]{2,1,0:T(8,128)(2,1)S(1)} %shard_map.94.refs_0_, bf16[8,128,512]{2,1,0:T(8,128)(2,1)S(1)} %copy-done.4, bf16[8,128,512]{2,1,0:T(8,128)(2,1)S(1)} %collective-permute-done.2.refs_2_, ...), custom_call_target="tpu_custom_call" | custom-call | tf_op jit(solution)/shard_map/pallas_call | solution.py:35
  56.4 2.0 %shard_map.99.refs_6_ = f32[512,512]{1,0:T(8,128)S(1)} custom-call(s32[3]{0:T(128)S(1)} %pad_add_fusion.me_ref, bf16[8,128,512]{2,1,0:T(8,128)(2,1)S(1)} %shard_map.94.refs_0_, bf16[8,128,512]{2,1,0:T(8,128)(2,1)S(1)} %copy-done.4, bf16[8,128,512]{2,1,0:T(8,128)(2,1)S(1)} %collective-permute-done.2.refs_2_, ...), custom_call_target="tpu_custom_call" | custom-call | tf_op jit(solution)/shard_map/pallas_call | solution.py:35
  60.1 1.8 shard_map.100
  62.7 3.5 %shard_map.107.w_ref = bf16[8,2,448,256]{3,2,1,0:T(8,128)(2,1)} custom-call(s32[3]{0:T(128)S(1)} %pad_add_fusion.me_ref, bf16[2,448,256]{2,1,0:T(8,128)(2,1)S(1)} %copy-done.18, bf16[2,448,256]{2,1,0:T(8,128)(2,1)S(1)} %copy-done.21, bf16[2,448,256]{2,1,0:T(8,128)(2,1)S(1)} %copy-done.24, ...), custom_call_target="tpu_custom_call" | custom-call | tf_op jit(solution)/shard_map/pallas_call | solution.py:35
  66.4 6.0 %all-to-all-start = ((bf16[8,128,512]{2,1,0:T(8,128)(2,1)}), bf16[8,128,512]{2,1,0:T(8,128)(2,1)S(1)}, u32[]{:S(2)}, u32[]{:S(2)}) async-start(bf16[8,128,512]{2,1,0:T(8,128)(2,1)} %shard_map.104), calls=%async_computation | async-start | bytes 2097152 | tf_op jit(solution)/shard_map/all_to_all | solution.py:371
  72.3 1.6 collective-permute-start.12
  74.0 6.8 %collective-permute-done.12.kv_ref = bf16[512,256]{1,0:T(8,128)(2,1)S(1)} collective-permute-done((bf16[512,256]{1,0:T(8,128)(2,1)S(1)}, bf16[512,256]{1,0:T(8,128)(2,1)S(1)}, u32[]{:S(2)}, u32[]{:S(2)}) %collective-permute-start.12) | collective-permute-done | bytes 262176 | tf_op jit(solution)/shard_map/ppermute | solution.py:354
  80.8 5.8 %shard_map.101 = (bf16[2,128,896]{2,1,0:T(8,128)(2,1)S(1)}, bf16[2,128,896]{2,1,0:T(8,128)(2,1)}, f32[512,256]{1,0:T(8,128)S(1)}) custom-call(s32[3]{0:T(128)S(1)} %pad_add_fusion.2.me_ref, bf16[2,2,128,896]{3,2,1,0:T(8,128)(2,1)S(1)} %copy-done.9, bf16[2,2,128,896]{3,2,1,0:T(8,128)(2,1)} %collective-permute-done.refs_2_.pack_ref, ...), custom_call_target="tpu_custom_call" | custom-call | tf_op jit(solution)/shard_map/pallas_call | solution.py:35
  87.3 5.8 %shard_map.102 = (bf16[2,128,896]{2,1,0:T(8,128)(2,1)S(1)}, bf16[2,128,896]{2,1,0:T(8,128)(2,1)}, f32[512,256]{1,0:T(8,128)S(1)}) custom-call(s32[3]{0:T(128)S(1)} %pad_add_fusion.me_ref, bf16[2,2,128,896]{3,2,1,0:T(8,128)(2,1)S(1)} %copy-done.9, bf16[2,2,128,896]{3,2,1,0:T(8,128)(2,1)} %collective-permute-done.refs_2_.pack_ref, ...), custom_call_target="tpu_custom_call" | custom-call | tf_op jit(solution)/shard_map/pallas_call | solution.py:35
  94.7 4.0 %all-to-all-done.refs_0_ = bf16[8,128,512]{2,1,0:T(8,128)(2,1)S(1)} async-done(((bf16[8,128,512]{2,1,0:T(8,128)(2,1)}), bf16[8,128,512]{2,1,0:T(8,128)(2,1)S(1)}, u32[]{:S(2)}, u32[]{:S(2)}) %all-to-all-start) | async-done | bytes 1048608 | tf_op jit(solution)/shard_map/all_to_all | solution.py:371
  98.7 1.1 copy-done.1
  99.8 1.5 collective-permute-start.20
  101.8 33.8 %collective-permute-done.15 = f32[512,256]{1,0:T(8,128)S(1)} collective-permute-done((f32[512,256]{1,0:T(8,128)S(1)}, f32[512,256]{1,0:T(8,128)S(1)}, u32[]{:S(2)}, u32[]{:S(2)}) %collective-permute-start.15) | collective-permute-done | bytes 524320 | tf_op jit(solution)/shard_map/ppermute | solution.py:354
  135.7 1.1 add_convert_fusion.1.g_ref.refs_0_
  138.9 0.9 copy-done.37
  139.9 6.4 %shard_map.108 = (f32[128,3584]{1,0:T(8,128)S(1)}, bf16[128,3584]{1,0:T(8,128)(2,1)}) custom-call(s32[3]{0:T(128)S(1)} %pad_add_fusion.me_ref, f32[512,1]{1,0:T(8,128)S(1)} %copy-done.37, bf16[512,256]{1,0:T(8,128)(2,1)S(1)} %add_convert_fusion.1.g_ref.refs_0_, bf16[512,256]{1,0:T(8,128)(2,1)S(1)} %collective-permute-done.16.gc_ref, ...), custom_call_target="tpu_custom_call" | custom-call | tf_op jit(solution)/shard_map/pallas_call | solution.py:35
  146.3 1.3 copy-done.14
  147.6 1.5 collective-permute-start.18
  149.3 1.9 %collective-permute-start.26 = (bf16[512,256]{1,0:T(8,128)(2,1)}, bf16[512,256]{1,0:T(8,128)(2,1)S(1)}, u32[]{:S(2)}, u32[]{:S(2)}) collective-permute-start(bf16[512,256]{1,0:T(8,128)(2,1)} %shard_map.109.refs_4_), channel_id=1, source_target_pairs={{0,4},{8,0},{16,8},{24,16},{28,24},{20,28},{12,20},{4,12},{1,5},{9... | collective-permute-start | bytes 786440 | tf_op jit(solution)/shard_map/ppermute | solution.py:361
  151.1 6.2 %collective-permute-done.22.refs_5_ = bf16[512,256]{1,0:T(8,128)(2,1)S(1)} collective-permute-done((bf16[512,256]{1,0:T(8,128)(2,1)}, bf16[512,256]{1,0:T(8,128)(2,1)S(1)}, u32[]{:S(2)}, u32[]{:S(2)}) %collective-permute-start.22) | collective-permute-done | bytes 262176 | tf_op jit(solution)/shard_map/ppermute | solution.py:361
  157.7 1.7 collective-permute-start.27
  159.4 5.3 %collective-permute-done.23.refs_7_ = bf16[512,256]{1,0:T(8,128)(2,1)S(1)} collective-permute-done((bf16[512,256]{1,0:T(8,128)(2,1)S(1)}, bf16[512,256]{1,0:T(8,128)(2,1)S(1)}, u32[]{:S(2)}, u32[]{:S(2)}) %collective-permute-start.23) | collective-permute-done | bytes 262176 | tf_op jit(solution)/shard_map/ppermute | solution.py:361
  165.3 1.4 collective-permute-start.28
  166.7 1.0 copy-done.33
  167.7 1.0 copy-done.35
  168.7 2.5 %shard_map.103 = (bf16[128,3584]{1,0:T(8,128)(2,1)}, bf16[128,3584]{1,0:T(8,128)(2,1)}) custom-call(s32[3]{0:T(128)S(1)} %pad_add_fusion.me_ref, bf16[2,128,896]{2,1,0:T(8,128)(2,1)S(1)} %copy-done.35, bf16[2,128,896]{2,1,0:T(8,128)(2,1)} %collective-permute-done.13.refs_1_, bf16[2,128,896]{2,1,0:T(8,128)(2,1)S(1)} %copy-done.33, ...), custom_call_target="tpu_custom_call" | custom-call | tf_op jit(solution)/shard_map/pallas_call | solution.py:35
  171.3 3.2 %shard_map.110.refs_6_ = f32[512,512]{1,0:T(8,128)S(1)} custom-call(s32[3]{0:T(128)S(1)} %pad_add_fusion.me_ref, bf16[8,128,512]{2,1,0:T(8,128)(2,1)S(1)} %copy-done.2, bf16[8,128,512]{2,1,0:T(8,128)(2,1)S(1)} %collective-permute-done.19.refs_1_, bf16[8,128,512]{2,1,0:T(8,128)(2,1)S(1)} %collective-permute-done.20.refs_2_, ...), custom_call_target="tpu_custom_call" | custom-call | tf_op jit(solution)/shard_map/pallas_call | solution.py:35
  175.1 1.5 collective-permute-start.29
  176.6 2.2 %shard_map.111.refs_6_ = f32[512,512]{1,0:T(8,128)S(1)} custom-call(s32[3]{0:T(128)S(1)} %pad_add_fusion.me_ref, bf16[8,128,512]{2,1,0:T(8,128)(2,1)S(1)} %copy-done.2, bf16[8,128,512]{2,1,0:T(8,128)(2,1)S(1)} %collective-permute-done.19.refs_1_, bf16[8,128,512]{2,1,0:T(8,128)(2,1)S(1)} %collective-permute-done.20.refs_2_, ...), custom_call_target="tpu_custom_call" | custom-call | tf_op jit(solution)/shard_map/pallas_call | solution.py:35
  178.8 2.3 %fusion = bf16[1,128,3584]{2,1,0:T(8,128)(2,1)} fusion(f32[128,3584]{1,0:T(8,128)S(1)} %copy-done.15, bf16[128,3584]{1,0:T(8,128)(2,1)} %collective-permute-done.18), kind=kLoop, calls=%fused_computation.1 | loop fusion | flops 1376256 | bytes 3670016 | tf_op jit(solution)/shard_map/broadcast_in_dim | solution.py:423
  181.1 2.7 %shard_map.112 = f32[2,448,256]{2,1,0:T(8,128)} custom-call(s32[3]{0:T(128)S(1)} %pad_add_fusion.me_ref, bf16[8,128,512]{2,1,0:T(8,128)(2,1)S(1)} %copy-done.2, bf16[8,128,512]{2,1,0:T(8,128)(2,1)S(1)} %collective-permute-done.19.refs_1_, bf16[8,128,512]{2,1,0:T(8,128)(2,1)S(1)} %collective-permute-done.20.refs_2_, ...), custom_call_target="tpu_custom_call" | custom-call | tf_op jit(solution)/shard_map/pallas_call | solution.py:35
  (123 shorter events, 16.7 us)
Async XLA Ops:
  0.6 6.6 %copy-start.16 = (bf16[2,448,256]{2,1,0:T(8,128)(2,1)S(1)}, bf16[2,448,256]{2,1,0:T(8,128)(2,1)}, u32[]{:S(2)}) copy-start(bf16[2,448,256]{2,1,0:T(8,128)(2,1)} %refs_0_.1) | copy-start | bytes 1376260
  3.3 18.7 %copy-start.28 = (bf16[1,128,3584]{2,1,0:T(8,128)(2,1)S(1)}, bf16[1,128,3584]{2,1,0:T(8,128)(2,1)}, u32[]{:S(2)}) copy-start(bf16[1,128,3584]{2,1,0:T(8,128)(2,1)} %param.7) | copy-start | bytes 2752516
  4.2 55.0 %copy-start = (bf16[8,128,512]{2,1,0:T(8,128)(2,1)}, bf16[8,128,512]{2,1,0:T(8,128)(2,1)S(1)}, u32[]{:S(2)}) copy-start(bf16[8,128,512]{2,1,0:T(8,128)(2,1)S(1)} %shard_map.94.refs_0_) | copy-start | bytes 3145732
  4.2 26.2 %collective-permute-start.2 = (bf16[8,128,512]{2,1,0:T(8,128)(2,1)S(1)}, bf16[8,128,512]{2,1,0:T(8,128)(2,1)S(1)}, u32[]{:S(2)}, u32[]{:S(2)}) collective-permute-start(bf16[8,128,512]{2,1,0:T(8,128)(2,1)S(1)} %shard_map.94.refs_0_), channel_id=1, source_target_pairs={{0,2},{1,3},{2,0},{3,1},{4,6},{5,7},{6,4},{7,5},{8,10},{9,11},{10,... | collective-permute-start | bytes 3145736 | tf_op jit(solution)/shard_map/ppermute | solution.py:354
  7.2 12.0 %collective-permute-start.3 = (bf16[2,448,256]{2,1,0:T(8,128)(2,1)S(1)}, bf16[2,448,256]{2,1,0:T(8,128)(2,1)S(1)}, u32[]{:S(2)}, u32[]{:S(2)}) collective-permute-start(bf16[2,448,256]{2,1,0:T(8,128)(2,1)S(1)} %copy-done.16), channel_id=1, source_target_pairs={{0,8},{8,16},{16,24},{24,28},{28,20},{20,12},{12,4},{4,0},{1,9},{9... | collective-permute-start | bytes 1376264 | tf_op jit(solution)/shard_map/ppermute | solution.py:361
  8.8 12.0 %collective-permute-start.5 = (bf16[2,448,256]{2,1,0:T(8,128)(2,1)S(1)}, bf16[2,448,256]{2,1,0:T(8,128)(2,1)S(1)}, u32[]{:S(2)}, u32[]{:S(2)}) collective-permute-start(bf16[2,448,256]{2,1,0:T(8,128)(2,1)S(1)} %copy-done.16), channel_id=1, source_target_pairs={{0,4},{8,0},{16,8},{24,16},{28,24},{20,28},{12,20},{4,12},{1,5},{9... | collective-permute-start | bytes 1376264 | tf_op jit(solution)/shard_map/ppermute | solution.py:361
  19.2 12.2 %copy-start.19 = (bf16[2,448,256]{2,1,0:T(8,128)(2,1)}, bf16[2,448,256]{2,1,0:T(8,128)(2,1)S(1)}, u32[]{:S(2)}) copy-start(bf16[2,448,256]{2,1,0:T(8,128)(2,1)S(1)} %collective-permute-done.3.refs_5_.refs_1_) | copy-start | bytes 1376260
  19.2 12.2 %collective-permute-start.4 = (bf16[2,448,256]{2,1,0:T(8,128)(2,1)S(1)}, bf16[2,448,256]{2,1,0:T(8,128)(2,1)}, u32[]{:S(2)}, u32[]{:S(2)}) collective-permute-start(bf16[2,448,256]{2,1,0:T(8,128)(2,1)S(1)} %collective-permute-done.3.refs_5_.refs_1_), channel_id=1, source_target_pairs={{0,8},{8,16},{16,24},{24,28},{28,20},{20,12},{12,4},{4,0},{1,9},{9... | collective-permute-start | bytes 1376264 | tf_op jit(solution)/shard_map/ppermute | solution.py:361
  20.8 10.9 %collective-permute-start.6 = (bf16[2,448,256]{2,1,0:T(8,128)(2,1)S(1)}, bf16[2,448,256]{2,1,0:T(8,128)(2,1)}, u32[]{:S(2)}, u32[]{:S(2)}) collective-permute-start(bf16[2,448,256]{2,1,0:T(8,128)(2,1)S(1)} %collective-permute-done.5.refs_6_.refs_2_), channel_id=1, source_target_pairs={{0,4},{8,0},{16,8},{24,16},{28,24},{20,28},{12,20},{4,12},{1,5},{9... | collective-permute-start | bytes 1376264 | tf_op jit(solution)/shard_map/ppermute | solution.py:361
  22.0 23.7 %collective-permute-start.1 = (bf16[8,128,512]{2,1,0:T(8,128)(2,1)S(1)}, bf16[8,128,512]{2,1,0:T(8,128)(2,1)S(1)}, u32[]{:S(2)}, u32[]{:S(2)}) collective-permute-start(bf16[8,128,512]{2,1,0:T(8,128)(2,1)S(1)} %shard_map.94.refs_0_), channel_id=1, source_target_pairs={{0,1},{1,0},{2,3},{3,2},{4,5},{5,4},{6,7},{7,6},{8,9},{9,8},{10,11... | collective-permute-start | bytes 3145736 | tf_op jit(solution)/shard_map/ppermute | solution.py:354
  25.7 19.9 %collective-permute-start = (bf16[2,2,128,896]{3,2,1,0:T(8,128)(2,1)}, bf16[2,2,128,896]{3,2,1,0:T(8,128)(2,1)}, u32[]{:S(2)}, u32[]{:S(2)}) collective-permute-start(bf16[2,2,128,896]{3,2,1,0:T(8,128)(2,1)} %get-tuple-element.21), channel_id=1, source_target_pairs={{0,1},{1,0},{2,3},{3,2},{4,5},{5,4},{6,7},{7,6},{8,9},{9,8},{10,11... | collective-permute-start | bytes 2752520 | tf_op jit(solution)/shard_map/ppermute | solution.py:354
  31.7 18.6 %collective-permute-start.7 = (bf16[8,128,512]{2,1,0:T(8,128)(2,1)}, bf16[8,128,512]{2,1,0:T(8,128)(2,1)}, u32[]{:S(2)}, u32[]{:S(2)}) collective-permute-start(bf16[8,128,512]{2,1,0:T(8,128)(2,1)} %shard_map.95), channel_id=1, source_target_pairs={{0,1},{1,0},{2,3},{3,2},{4,5},{5,4},{6,7},{7,6},{8,9},{9,8},{10,11... | collective-permute-start | bytes 3145736 | tf_op jit(solution)/shard_map/ppermute | solution.py:354
  31.7 13.1 %collective-permute-start.8 = (bf16[2,448,256]{2,1,0:T(8,128)(2,1)}, bf16[2,448,256]{2,1,0:T(8,128)(2,1)S(1)}, u32[]{:S(2)}, u32[]{:S(2)}) collective-permute-start(bf16[2,448,256]{2,1,0:T(8,128)(2,1)} %collective-permute-done.4.refs_1_.refs_7_.refs_3_), channel_id=1, source_target_pairs={{0,8},{8,16},{16,24},{24,28},{28,20},{20,12},{12,4},{4,0},{1,9},{9... | collective-permute-start | bytes 1376264 | tf_op jit(solution)/shard_map/ppermute | solution.py:361
  33.3 14.9 %collective-permute-start.10 = (bf16[2,448,256]{2,1,0:T(8,128)(2,1)}, bf16[2,448,256]{2,1,0:T(8,128)(2,1)}, u32[]{:S(2)}, u32[]{:S(2)}) collective-permute-start(bf16[2,448,256]{2,1,0:T(8,128)(2,1)} %collective-permute-done.6.refs_2_.refs_8_.refs_4_), channel_id=1, source_target_pairs={{0,4},{8,0},{16,8},{24,16},{28,24},{20,28},{12,20},{4,12},{1,5},{9... | collective-permute-start | bytes 1376264 | tf_op jit(solution)/shard_map/ppermute | solution.py:361
  46.6 3.7 %copy-start.4 = (bf16[8,128,512]{2,1,0:T(8,128)(2,1)S(1)}, bf16[8,128,512]{2,1,0:T(8,128)(2,1)}, u32[]{:S(2)}) copy-start(bf16[8,128,512]{2,1,0:T(8,128)(2,1)} %copy-done.3) | copy-start | bytes 3145732
  46.6 11.8 %collective-permute-start.9 = (bf16[2,224,256]{2,1,0:T(8,128)(2,1)}, bf16[2,224,256]{2,1,0:T(8,128)(2,1)S(1)}, u32[]{:S(2)}, u32[]{:S(2)}) collective-permute-start(bf16[2,224,256]{2,1,0:T(8,128)(2,1)} %shard_map.96), channel_id=1, source_target_pairs={{0,8},{8,16},{16,24},{24,28},{28,20},{20,12},{12,4},{4,0},{1,9},{9... | collective-permute-start | bytes 688136 | tf_op jit(solution)/shard_map/ppermute | solution.py:361
  49.9 6.5 %copy-start.11 = (bf16[2,448,256]{2,1,0:T(8,128)(2,1)S(1)}, bf16[2,448,256]{2,1,0:T(8,128)(2,1)}, u32[]{:S(2)}) copy-start(bf16[2,448,256]{2,1,0:T(8,128)(2,1)} %copy-done.10) | copy-start | bytes 1376260
  49.9 9.3 %collective-permute-start.11 = (bf16[2,224,256]{2,1,0:T(8,128)(2,1)}, bf16[2,224,256]{2,1,0:T(8,128)(2,1)S(1)}, u32[]{:S(2)}, u32[]{:S(2)}) collective-permute-start(bf16[2,224,256]{2,1,0:T(8,128)(2,1)} %shard_map.97), channel_id=1, source_target_pairs={{0,4},{8,0},{16,8},{24,16},{28,24},{20,28},{12,20},{4,12},{1,5},{9... | collective-permute-start | bytes 688136 | tf_op jit(solution)/shard_map/ppermute | solution.py:361
  58.4 4.3 %copy-start.18 = (bf16[2,448,256]{2,1,0:T(8,128)(2,1)S(1)}, bf16[2,448,256]{2,1,0:T(8,128)(2,1)}, u32[]{:S(2)}) copy-start(bf16[2,448,256]{2,1,0:T(8,128)(2,1)} %refs_0_.1) | copy-start | bytes 1376260
  58.4 4.2 %copy-start.21 = (bf16[2,448,256]{2,1,0:T(8,128)(2,1)S(1)}, bf16[2,448,256]{2,1,0:T(8,128)(2,1)}, u32[]{:S(2)}) copy-start(bf16[2,448,256]{2,1,0:T(8,128)(2,1)} %copy-done.19) | copy-start | bytes 1376260
  58.5 4.2 %copy-start.24 = (bf16[2,448,256]{2,1,0:T(8,128)(2,1)S(1)}, bf16[2,448,256]{2,1,0:T(8,128)(2,1)}, u32[]{:S(2)}) copy-start(bf16[2,448,256]{2,1,0:T(8,128)(2,1)} %copy-done.22) | copy-start | bytes 1376260
  62.7 3.6 %copy-start.25 = (f32[512,1]{1,0:T(8,128)}, f32[512,1]{1,0:T(8,128)S(1)}, u32[]{:S(2)}) copy-start(f32[512,1]{1,0:T(8,128)S(1)} %get-tuple-element.23.ids_ref) | copy-start | bytes 6148
  66.3 14.5 %copy-start.9 = (bf16[2,2,128,896]{3,2,1,0:T(8,128)(2,1)S(1)}, bf16[2,2,128,896]{3,2,1,0:T(8,128)(2,1)}, u32[]{:S(2)}) copy-start(bf16[2,2,128,896]{3,2,1,0:T(8,128)(2,1)} %copy-done.8) | copy-start | bytes 2752516
  66.3 72.7 %collective-permute-start.17 = (bf16[8,2,448,256]{3,2,1,0:T(8,128)(2,1)}, bf16[8,2,448,256]{3,2,1,0:T(8,128)(2,1)}, u32[]{:S(2)}, u32[]{:S(2)}) collective-permute-start(bf16[8,2,448,256]{3,2,1,0:T(8,128)(2,1)} %shard_map.107.w_ref), channel_id=1, source_target_pairs={{0,1},{1,0},{2,3},{3,2},{4,5},{5,4},{6,7},{7,6},{8,9},{9,8},{10,11... | collective-permute-start | bytes 11010056 | tf_op jit(solution)/shard_map/ppermute | solution.py:354
  66.3 6.0 %copy-start.13 = (bf16[512,256]{1,0:T(8,128)(2,1)S(1)}, bf16[512,256]{1,0:T(8,128)(2,1)}, u32[]{:S(2)}) copy-start(bf16[512,256]{1,0:T(8,128)(2,1)} %copy-done.12) | copy-start | bytes 786436
  66.4 14.4 %copy-start.26 = (f32[512,1]{1,0:T(8,128)S(1)}, f32[512,1]{1,0:T(8,128)}, u32[]{:S(2)}) copy-start(f32[512,1]{1,0:T(8,128)} %copy-done.25) | copy-start | bytes 6148
  66.4 32.3 %all-to-all-start = ((bf16[8,128,512]{2,1,0:T(8,128)(2,1)}), bf16[8,128,512]{2,1,0:T(8,128)(2,1)S(1)}, u32[]{:S(2)}, u32[]{:S(2)}) async-start(bf16[8,128,512]{2,1,0:T(8,128)(2,1)} %shard_map.104), calls=%async_computation | async-start | bytes 2097152 | tf_op jit(solution)/shard_map/all_to_all | solution.py:371
  72.3 8.5 %collective-permute-start.12 = (bf16[512,256]{1,0:T(8,128)(2,1)S(1)}, bf16[512,256]{1,0:T(8,128)(2,1)S(1)}, u32[]{:S(2)}, u32[]{:S(2)}) collective-permute-start(bf16[512,256]{1,0:T(8,128)(2,1)S(1)} %copy-done.13), channel_id=1, source_target_pairs={{0,2},{1,3},{2,0},{3,1},{4,6},{5,7},{6,4},{7,5},{8,10},{9,11},{10,... | collective-permute-start | bytes 786440 | tf_op jit(solution)/shard_map/ppermute | solution.py:354
  99.8 38.6 %copy-start.2 = (bf16[8,128,512]{2,1,0:T(8,128)(2,1)S(1)}, bf16[8,128,512]{2,1,0:T(8,128)(2,1)}, u32[]{:S(2)}) copy-start(bf16[8,128,512]{2,1,0:T(8,128)(2,1)} %shard_map.105.refs_1_.refs_0_) | copy-start | bytes 3145732
  99.8 38.7 %collective-permute-start.20 = (bf16[8,128,512]{2,1,0:T(8,128)(2,1)}, bf16[8,128,512]{2,1,0:T(8,128)(2,1)S(1)}, u32[]{:S(2)}, u32[]{:S(2)}) collective-permute-start(bf16[8,128,512]{2,1,0:T(8,128)(2,1)} %shard_map.105.refs_1_.refs_0_), channel_id=1, source_target_pairs={{0,2},{1,3},{2,0},{3,1},{4,6},{5,7},{6,4},{7,5},{8,10},{9,11},{10,... | collective-permute-start | bytes 3145736 | tf_op jit(solution)/shard_map/ppermute | solution.py:354
  101.3 34.3 %collective-permute-start.15 = (f32[512,256]{1,0:T(8,128)S(1)}, f32[512,256]{1,0:T(8,128)S(1)}, u32[]{:S(2)}, u32[]{:S(2)}) collective-permute-start(f32[512,256]{1,0:T(8,128)S(1)} %get-tuple-element.25.refs_0_), channel_id=1, source_target_pairs={{0,2},{1,3},{2,0},{3,1},{4,6},{5,7},{6,4},{7,5},{8,10},{9,11},{10,... | collective-permute-start | bytes 1572872 | tf_op jit(solution)/shard_map/ppermute | solution.py:354
  136.8 9.5 %copy-start.6 = (bf16[512,256]{1,0:T(8,128)(2,1)}, bf16[512,256]{1,0:T(8,128)(2,1)S(1)}, u32[]{:S(2)}) copy-start(bf16[512,256]{1,0:T(8,128)(2,1)S(1)} %add_convert_fusion.1.g_ref.refs_0_) | copy-start | bytes 786436
  136.8 1.6 collective-permute-start.16
  136.9 12.2 %collective-permute-start.13 = (bf16[2,128,896]{2,1,0:T(8,128)(2,1)}, bf16[2,128,896]{2,1,0:T(8,128)(2,1)}, u32[]{:S(2)}, u32[]{:S(2)}) collective-permute-start(bf16[2,128,896]{2,1,0:T(8,128)(2,1)} %get-tuple-element.27), channel_id=1, source_target_pairs={{0,1},{1,0},{2,3},{3,2},{4,5},{5,4},{6,7},{7,6},{8,9},{9,8},{10,11... | collective-permute-start | bytes 1376264 | tf_op jit(solution)/shard_map/ppermute | solution.py:354
  137.4 11.9 %collective-permute-start.14 = (bf16[2,128,896]{2,1,0:T(8,128)(2,1)}, bf16[2,128,896]{2,1,0:T(8,128)(2,1)}, u32[]{:S(2)}, u32[]{:S(2)}) collective-permute-start(bf16[2,128,896]{2,1,0:T(8,128)(2,1)} %get-tuple-element.29), channel_id=1, source_target_pairs={{0,1},{1,0},{2,3},{3,2},{4,5},{5,4},{6,7},{7,6},{8,9},{9,8},{10,11... | collective-permute-start | bytes 1376264 | tf_op jit(solution)/shard_map/ppermute | solution.py:354
  138.4 32.9 %collective-permute-start.19 = (bf16[8,128,512]{2,1,0:T(8,128)(2,1)S(1)}, bf16[8,128,512]{2,1,0:T(8,128)(2,1)S(1)}, u32[]{:S(2)}, u32[]{:S(2)}) collective-permute-start(bf16[8,128,512]{2,1,0:T(8,128)(2,1)S(1)} %copy-done.2), channel_id=1, source_target_pairs={{0,1},{1,0},{2,3},{3,2},{4,5},{5,4},{6,7},{7,6},{8,9},{9,8},{10,11... | collective-permute-start | bytes 3145736 | tf_op jit(solution)/shard_map/ppermute | solution.py:354
  138.5 32.7 %collective-permute-start.21 = (bf16[8,128,512]{2,1,0:T(8,128)(2,1)S(1)}, bf16[8,128,512]{2,1,0:T(8,128)(2,1)}, u32[]{:S(2)}, u32[]{:S(2)}) collective-permute-start(bf16[8,128,512]{2,1,0:T(8,128)(2,1)S(1)} %collective-permute-done.20.refs_2_), channel_id=1, source_target_pairs={{0,1},{1,0},{2,3},{3,2},{4,5},{5,4},{6,7},{7,6},{8,9},{9,8},{10,11... | collective-permute-start | bytes 3145736 | tf_op jit(solution)/shard_map/ppermute | solution.py:354
  147.6 31.2 %collective-permute-start.18 = (bf16[128,3584]{1,0:T(8,128)(2,1)}, bf16[128,3584]{1,0:T(8,128)(2,1)}, u32[]{:S(2)}, u32[]{:S(2)}) collective-permute-start(bf16[128,3584]{1,0:T(8,128)(2,1)} %get-tuple-element.35.refs_1_), channel_id=1, source_target_pairs={{0,2},{1,3},{2,0},{3,1},{4,6},{5,7},{6,4},{7,5},{8,10},{9,11},{10,... | collective-permute-start | bytes 2752520 | tf_op jit(solution)/shard_map/ppermute | solution.py:354
  149.1 22.2 %copy-start.7 = (bf16[512,256]{1,0:T(8,128)(2,1)S(1)}, bf16[512,256]{1,0:T(8,128)(2,1)}, u32[]{:S(2)}) copy-start(bf16[512,256]{1,0:T(8,128)(2,1)} %shard_map.109.refs_4_) | copy-start | bytes 786436
  149.1 8.3 %collective-permute-start.22 = (bf16[512,256]{1,0:T(8,128)(2,1)}, bf16[512,256]{1,0:T(8,128)(2,1)S(1)}, u32[]{:S(2)}, u32[]{:S(2)}) collective-permute-start(bf16[512,256]{1,0:T(8,128)(2,1)} %shard_map.109.refs_4_), channel_id=1, source_target_pairs={{0,8},{8,16},{16,24},{24,28},{28,20},{20,12},{12,4},{4,0},{1,9},{9... | collective-permute-start | bytes 786440 | tf_op jit(solution)/shard_map/ppermute | solution.py:361
  149.3 8.5 %collective-permute-start.26 = (bf16[512,256]{1,0:T(8,128)(2,1)}, bf16[512,256]{1,0:T(8,128)(2,1)S(1)}, u32[]{:S(2)}, u32[]{:S(2)}) collective-permute-start(bf16[512,256]{1,0:T(8,128)(2,1)} %shard_map.109.refs_4_), channel_id=1, source_target_pairs={{0,4},{8,0},{16,8},{24,16},{28,24},{20,28},{12,20},{4,12},{1,5},{9... | collective-permute-start | bytes 786440 | tf_op jit(solution)/shard_map/ppermute | solution.py:361
  157.4 7.3 %collective-permute-start.23 = (bf16[512,256]{1,0:T(8,128)(2,1)S(1)}, bf16[512,256]{1,0:T(8,128)(2,1)S(1)}, u32[]{:S(2)}, u32[]{:S(2)}) collective-permute-start(bf16[512,256]{1,0:T(8,128)(2,1)S(1)} %collective-permute-done.22.refs_5_), channel_id=1, source_target_pairs={{0,8},{8,16},{16,24},{24,28},{28,20},{20,12},{12,4},{4,0},{1,9},{9... | collective-permute-start | bytes 786440 | tf_op jit(solution)/shard_map/ppermute | solution.py:361
  157.7 7.5 %collective-permute-start.27 = (bf16[512,256]{1,0:T(8,128)(2,1)S(1)}, bf16[512,256]{1,0:T(8,128)(2,1)S(1)}, u32[]{:S(2)}, u32[]{:S(2)}) collective-permute-start(bf16[512,256]{1,0:T(8,128)(2,1)S(1)} %collective-permute-done.26.refs_6_), channel_id=1, source_target_pairs={{0,4},{8,0},{16,8},{24,16},{28,24},{20,28},{12,20},{4,12},{1,5},{9... | collective-permute-start | bytes 786440 | tf_op jit(solution)/shard_map/ppermute | solution.py:361
  164.7 9.8 %collective-permute-start.24 = (bf16[512,256]{1,0:T(8,128)(2,1)S(1)}, bf16[512,256]{1,0:T(8,128)(2,1)S(1)}, u32[]{:S(2)}, u32[]{:S(2)}) collective-permute-start(bf16[512,256]{1,0:T(8,128)(2,1)S(1)} %collective-permute-done.23.refs_7_), channel_id=1, source_target_pairs={{0,8},{8,16},{16,24},{24,28},{28,20},{20,12},{12,4},{4,0},{1,9},{9... | collective-permute-start | bytes 786440 | tf_op jit(solution)/shard_map/ppermute | solution.py:361
  165.3 9.9 %collective-permute-start.28 = (bf16[512,256]{1,0:T(8,128)(2,1)S(1)}, bf16[512,256]{1,0:T(8,128)(2,1)S(1)}, u32[]{:S(2)}, u32[]{:S(2)}) collective-permute-start(bf16[512,256]{1,0:T(8,128)(2,1)S(1)} %collective-permute-done.27.refs_8_), channel_id=1, source_target_pairs={{0,4},{8,0},{16,8},{24,16},{28,24},{20,28},{12,20},{4,12},{1,5},{9... | collective-permute-start | bytes 786440 | tf_op jit(solution)/shard_map/ppermute | solution.py:361
  174.5 6.6 %collective-permute-start.25 = (bf16[256,256]{1,0:T(8,128)(2,1)S(1)}, bf16[256,256]{1,0:T(8,128)(2,1)S(1)}, u32[]{:S(2)}, u32[]{:S(2)}) collective-permute-start(bf16[256,256]{1,0:T(8,128)(2,1)S(1)} %slice.18), channel_id=1, source_target_pairs={{0,8},{8,16},{16,24},{24,28},{28,20},{20,12},{12,4},{4,0},{1,9},{9... | collective-permute-start | bytes 393224 | tf_op jit(solution)/shard_map/ppermute | solution.py:361
  175.1 3.7 %copy-start.15 = (f32[128,3584]{1,0:T(8,128)S(1)}, f32[128,3584]{1,0:T(8,128)}, u32[]{:S(2)}) copy-start(f32[128,3584]{1,0:T(8,128)} %copy-done.14) | copy-start | bytes 5505028
  175.1 6.0 %collective-permute-start.29 = (bf16[256,256]{1,0:T(8,128)(2,1)S(1)}, bf16[256,256]{1,0:T(8,128)(2,1)S(1)}, u32[]{:S(2)}, u32[]{:S(2)}) collective-permute-start(bf16[256,256]{1,0:T(8,128)(2,1)S(1)} %slice.19), channel_id=1, source_target_pairs={{0,4},{8,0},{16,8},{24,16},{28,24},{20,28},{12,20},{4,12},{1,5},{9... | collective-permute-start | bytes 393224 | tf_op jit(solution)/shard_map/ppermute | solution.py:361
  (23 other events, 23.9 us)

commit v5 on v4

--- a/solution.py
+++ b/solution.py
@@ -30,7 +30,7 @@
     return jax.ShapeDtypeStruct(shape, dtype)
 
 
-def call(body, me, operands, out_shape, scratch=(), anywhere=0):
+def call(body, me, operands, out_shape, micros, scratch=(), anywhere=0):
     near = pl.BlockSpec(memory_space=pltpu.VMEM)
     return pl.pallas_call(
         body,
@@ -41,7 +41,7 @@
         out_shape=out_shape,
         scratch_shapes=scratch,
         compiler_params=pltpu.CompilerParams(vmem_limit_bytes=24 * 1024 * 1024),
-        cost_estimate=pl.CostEstimate(flops=0, bytes_accessed=0, transcendentals=0),
+        cost_estimate=pl.CostEstimate(flops=0, bytes_accessed=micros * 3000000, transcendentals=0),
     )(me, *operands)
 
 
@@ -89,7 +89,7 @@
     depth = width // count
     lanes = -(-(depth + 3) // 128) * 128
     out = shaped((count, rows, lanes), BF16)
-    return call(functools.partial(blocks_kernel, depth), me, (tokens, kinds, ids), out)
+    return call(functools.partial(blocks_kernel, depth), me, (tokens, kinds, ids), out, 1)
 
 
 def read_marks(block, depth):
@@ -107,7 +107,7 @@
 
 def pack_heads(me, queries, upstream):
     out = shaped((2, 2, queries.shape[0], SPAN), BF16)
-    return call(pack_kernel, me, (queries, upstream), [out, out])
+    return call(pack_kernel, me, (queries, upstream), [out, out], 2)
 
 
 def place_kernel(me_ref, *refs):
@@ -120,7 +120,7 @@
 
 def place_heads(me, found):
     out = shaped((found[0].shape[1], 4 * SPAN), BF16)
-    return call(place_kernel, me, found, [out, out])
+    return call(place_kernel, me, found, [out, out], 3)
 
 
 def project_kernel(steps, depth, halves, first, last, me_ref, *refs):
@@ -132,7 +132,7 @@
         owner = owner_at(me_ref[1], by)
         left = jnp.concatenate([ref[owner][:, :depth] for ref in parts], axis=0)
         for e in range(2):
-            right = jnp.concatenate([ref[e] for ref in weights], axis=0) if halves else weights[b][e]
+            right = weights[e][0] if halves else weights[b][e]
             sums[e] = sums[e] + contract(left, right, 1, 0)
     if not first:
         sums = [s + refs[0][:, e * PAIR : (e + 1) * PAIR] for e, s in enumerate(sums)]
@@ -165,6 +165,7 @@
         me,
         operands,
         out,
+        3,
         anywhere=len(wait),
     )
 
@@ -220,6 +221,7 @@
         me,
         (own, pack, kv, ids, ids_row, *wait),
         [side, side, shaped((length, PAIR), F32)],
+        6,
         scratch=[pltpu.VMEM((2 * rows, length), F32), pltpu.VMEM(stacked, F32)] + [pltpu.VMEM(stacked, BF16)] * 4,
         anywhere=len(wait),
     )
@@ -229,7 +231,8 @@
     return [jnp.where(kind == float(e), x, 0.0).astype(BF16) for e in range(2)]
 
 
-def hidden_kernel(me_ref, kind_ref, g_ref, gc_ref, w_ref, wc_ref, mine_ref, away_ref):
+def hidden_kernel(me_ref, kind_ref, g_ref, gc_ref, w_ref, wc_ref, *refs):
+    mine_ref, away_ref = refs[-2:]
     rows = mine_ref.shape[0]
     count, _, depth, _ = w_ref.shape
     masked = []
@@ -252,14 +255,16 @@
         away_ref[:, cols] = total[rows:].astype(BF16)
 
 
-def hidden_grad(me, kind, grad, grad_c, weight, weight_c, rows):
+def hidden_grad(me, kind, grad, grad_c, weight, weight_c, rows, wait=()):
     count, _, depth, _ = weight.shape
     width = count * depth
     return call(
         hidden_kernel,
         me,
-        (kind, grad, grad_c, weight, weight_c),
+        (kind, grad, grad_c, weight, weight_c, *wait),
         [shaped((rows, width), F32), shaped((rows, width), BF16)],
+        7,
+        anywhere=len(wait),
     )
 
 
@@ -300,23 +305,23 @@
         me,
         (*parts, *grads, *before),
         shaped((2, depth, PAIR) if last else (lanes, 2 * PAIR), F32),
+        3,
     )
 
 
 def gather_kernel(me_ref, *refs):
     blocks, whole_ref = refs[: len(STEPS) + 1], refs[-1]
-    size = blocks[-1].shape[1]
     for i, block in enumerate(blocks):
         owner = owner_at(me_ref[1], STEPS[min(i, len(STEPS) - 1)])
         if i < len(STEPS) - 1:
             whole_ref[owner] = block[...]
         else:
-            whole_ref[owner, :, (i - len(STEPS) + 1) * size : (i - len(STEPS) + 2) * size, :] = block[...]
+            whole_ref[owner, i - len(STEPS) + 1] = block[0]
 
 
 def gather_blocks(me, blocks, wait=()):
     out = shaped((len(CYCLE), *blocks[0].shape), blocks[0].dtype)
-    return call(gather_kernel, me, (*blocks, *wait), out, anywhere=len(wait))
+    return call(gather_kernel, me, (*blocks, *wait), out, 4, anywhere=len(wait))
 
 
 def in_order(parts, quarters):
@@ -388,26 +393,26 @@
     pack = swap(pack, 1)
 
     if near_link:
-        ups, downs = halves(*weights[5:], 1)
-        weights += both_ways(after(ups, parts[1], pack), after(downs, parts[1], pack))
         total = project(me, STEPS[:5], parts, weights[:5], None, depth)
+        ups, downs = halves(*weights[5:], 0)
+        weights += both_ways(after(ups, pack, total), after(downs, pack, total))
         total = project(me, STEPS[5:7], parts, weights[5:7], total, depth)
         kv, kind, ids, ids_row = project(me, STEPS[7:], parts, weights[7:], total, depth, True, True)
-        weight = gather_blocks(me, weights, (kv,))
     else:
         kv, kind, ids, ids_row = project_plain(quarters, parts, weight, depth)
-    weight_c = swap(weight, 1)
-
     kv_far = swap(kv, 2)
     columns = exchange_columns(after(blocks, kv))
     far_own, far_other, far = attend(me_far, own, pack, kv_far, ids, ids_row)
     near_own, near_other, near = attend(me, own, pack, kv, ids, ids_row, (far,))
-    columns = after(columns, near)
-    grad_kv = (after(near, columns) + swap(far, 2)).astype(BF16)
+    grad_kv = (near + swap(far, 2)).astype(BF16)
+    if near_link:
+        weight = gather_blocks(me, weights, (far,))
     attended, grad_queries = place_heads(me, (near_own, swap(near_other, 1), far_own, swap(far_other, 1)))
 
-    mine, away = hidden_grad(me, kind, grad_kv, swap(grad_kv, 1), weight, weight_c, rows)
-    columns = over_seq(columns)
+    mine, away = hidden_grad(
+        me, kind, grad_kv, swap(grad_kv, 1), weight, swap(weight, 1), rows, (columns,)
+    )
+    columns = over_seq(after(columns, away))
     if near_link:
         first = after(grad_kv, away)
         grads = [first, *both_ways(first, first)]

time: 185 us -> 177 us (0.957)
  Pallas kernels: 41.5 us -> 35.2 us
  waiting for transfers between devices: 82.7 us -> 86.9 us
  local copies, waits for them, and re-layouts: 23.1 us -> 20.5 us
  starting transfers between devices: 32.2 us -> 30.3 us
    all_to_all x1, waiting for transfers between devices: 4.03 us -> 10.6 us  [exchange_columns(): return lax.all_to_all(x, 'fsdp', split_axis=0, concat_axis=0, tiled=True)]
    pallas_call x13, Pallas kernels: 41.5 us -> 35.2 us  [call(): pl.pallas_call(body, in_specs=[pl.BlockSpec(memory_space=pltpu.SMEM)] + [...]
    ppermute x14, waiting for transfers between devices: 45.7 us -> 43.8 us  [swap(): return lax.ppermute(x, 'seq', [(i, i ^ bit) for i in range(seq)])]
    unnamed x81 -> x105, local copies, waits for them, and re-layouts: 20.7 us -> 19.1 us
  transfers between devices with their start and end apart: 31 -> 31, of which waited for: 10 -> 12; matrix products, arithmetic and copies ran while one was open for 4% -> 3% of each run, Pallas kernels for 18% -> 9%
where the time goes in v5:
time: 177 us
  waiting for transfers between devices  86.9 us (49%)
  Pallas kernels  35.2 us (20%)
  starting transfers between devices  30.3 us (17%)
  local copies, waits for them, and re-layouts  20.5 us (12%)
  other arithmetic  2.62 us (1%)
    ppermute x14, waiting for transfers between devices, swap(): return lax.ppermute(x, 'seq', [(i, i ^ bit) for i in range(seq)])  43.8 us
    pallas_call x13, Pallas kernels, call(): pl.pallas_call(body, in_specs=[pl.BlockSpec(memory_space=pltpu.SMEM)] + [...  35.2 us
    ppermute x16, waiting for transfers between devices, turn(): lax.ppermute(x, 'fsdp', [(CYCLE[i], CYCLE[(i + by) % fsdp]) for i in rang...  32.5 us
    unnamed x105, local copies, waits for them, and re-layouts  19.1 us
    ppermute x16, starting transfers between devices, turn(): lax.ppermute(x, 'fsdp', [(CYCLE[i], CYCLE[(i + by) % fsdp]) for i in rang...  16.3 us
    all_to_all x1, waiting for transfers between devices, exchange_columns(): return lax.all_to_all(x, 'fsdp', split_axis=0, concat_axis=0, tiled=True)  10.6 us
    ppermute x14, starting transfers between devices, swap(): return lax.ppermute(x, 'seq', [(i, i ^ bit) for i in range(seq)])  8.78 us
    all_to_all x1, starting transfers between devices, exchange_columns(): return lax.all_to_all(x, 'fsdp', split_axis=0, concat_axis=0, tiled=True)  5.22 us
  transfers between devices with their start and end apart: 31, of which 12 were waited for; matrix products, arithmetic and copies ran while one was open for 3% of the time, Pallas kernels for 9%

profile of v5, /device:TPU:0, one launch (start us, length us, event | category | flops | bytes accessed | tf_op | source)
XLA Modules:
  0.0 176.6 jit_solution(15099261341758388725)
XLA Ops:
  0.7 1.2 copy-done.36
  4.2 3.0 %collective-permute-start.2 = (bf16[8,128,512]{2,1,0:T(8,128)(2,1)S(1)}, bf16[8,128,512]{2,1,0:T(8,128)(2,1)S(1)}, u32[]{:S(2)}, u32[]{:S(2)}) collective-permute-start(bf16[8,128,512]{2,1,0:T(8,128)(2,1)S(1)} %shard_map.94.refs_0_), channel_id=1, source_target_pairs={{0,2},{1,3},{2,0},{3,1},{4,6},{5,7},{6,4},{7,5},{8,10},{9,11},{10,... | collective-permute-start | bytes 3145736 | tf_op jit(solution)/shard_map/ppermute | solution.py:359
  7.2 1.5 collective-permute-start.5
  9.2 10.0 %collective-permute-done.5.refs_6_.refs_2_ = bf16[2,448,256]{2,1,0:T(8,128)(2,1)S(1)} collective-permute-done((bf16[2,448,256]{2,1,0:T(8,128)(2,1)S(1)}, bf16[2,448,256]{2,1,0:T(8,128)(2,1)S(1)}, u32[]{:S(2)}, u32[]{:S(2)}) %collective-permute-start.5) | collective-permute-done | bytes 458784 | tf_op jit(solution)/shard_map/ppermute | solution.py:366
  19.2 1.5 collective-permute-start.6
  22.0 8.4 %collective-permute-done.2.refs_2_ = bf16[8,128,512]{2,1,0:T(8,128)(2,1)S(1)} collective-permute-done((bf16[8,128,512]{2,1,0:T(8,128)(2,1)S(1)}, bf16[8,128,512]{2,1,0:T(8,128)(2,1)S(1)}, u32[]{:S(2)}, u32[]{:S(2)}) %collective-permute-start.2) | collective-permute-done | bytes 1048608 | tf_op jit(solution)/shard_map/ppermute | solution.py:359
  30.4 1.0 copy.16.refs_0_
  31.4 1.0 collective-permute-done.4.refs_1_.refs_7_.refs_3_
  32.4 1.3 copy-done.37
  33.7 1.2 copy-done.38
  36.0 1.6 collective-permute-start.10
  38.1 10.7 %collective-permute-done.10.refs_5_.refs_6_ = bf16[2,448,256]{2,1,0:T(8,128)(2,1)S(1)} collective-permute-done((bf16[2,448,256]{2,1,0:T(8,128)(2,1)}, bf16[2,448,256]{2,1,0:T(8,128)(2,1)S(1)}, u32[]{:S(2)}, u32[]{:S(2)}) %collective-permute-start.10) | collective-permute-done | bytes 458784 | tf_op jit(solution)/shard_map/ppermute | solution.py:366
  51.8 3.4 %shard_map.96.refs_2_.refs_6_ = f32[512,512]{1,0:T(8,128)S(1)} custom-call(s32[3]{0:T(128)S(1)} %pad_add_fusion.me_ref, bf16[8,128,512]{2,1,0:T(8,128)(2,1)S(1)} %shard_map.94.refs_0_, bf16[8,128,512]{2,1,0:T(8,128)(2,1)S(1)} %collective-permute-done.1.refs_1_, bf16[8,128,512]{2,1,0:T(8,128)(2,1)S(1)} %collective-permute-done.2.refs_2_, ...), custom_call_target="tpu_custom_call" | custom-call | bytes 9000000 | tf_op jit(solution)/shard_map/pallas_call | solution.py:35
  55.2 1.0 copy-done.3
  57.0 1.2 collective-permute-start.11
  58.2 1.2 copy-done.6
  59.5 1.2 copy-done.9
  60.7 1.0 copy-done.18
  61.7 1.0 copy-done.21
  62.7 1.2 shard_map.99.refs_6_
  64.7 0.9 copy-done.40
  65.6 1.1 shard_map.100
  68.4 6.0 %collective-permute-done.12.kv_ref = bf16[512,256]{1,0:T(8,128)(2,1)S(1)} collective-permute-done((bf16[512,256]{1,0:T(8,128)(2,1)S(1)}, bf16[512,256]{1,0:T(8,128)(2,1)S(1)}, u32[]{:S(2)}, u32[]{:S(2)}) %collective-permute-start.12) | collective-permute-done | bytes 262176 | tf_op jit(solution)/shard_map/ppermute | solution.py:359
  74.5 5.3 %shard_map.101 = (bf16[2,128,896]{2,1,0:T(8,128)(2,1)S(1)}, bf16[2,128,896]{2,1,0:T(8,128)(2,1)S(1)}, f32[512,256]{1,0:T(8,128)S(1)}) custom-call(s32[3]{0:T(128)S(1)} %pad_add_fusion.2.me_ref, bf16[2,2,128,896]{3,2,1,0:T(8,128)(2,1)S(1)} %copy-done.16, bf16[2,2,128,896]{3,2,1,0:T(8,128)(2,1)} %collective-permute-done.refs_1_.pack_ref, ...), custom_call_target="tpu_custom_call" | custom-call | bytes 18000000 | tf_op jit(solution)/shard_map/pallas_call | solution.py:35
  80.6 3.4 %shard_map.104.w_ref = bf16[8,2,448,256]{3,2,1,0:T(8,128)(2,1)} custom-call(s32[3]{0:T(128)S(1)} %pad_add_fusion.me_ref, bf16[2,448,256]{2,1,0:T(8,128)(2,1)S(1)} %copy-done.27, bf16[2,448,256]{2,1,0:T(8,128)(2,1)S(1)} %copy-done.33, bf16[2,448,256]{2,1,0:T(8,128)(2,1)S(1)} %copy-done.30, ...), custom_call_target="tpu_custom_call" | custom-call | bytes 12000000 | tf_op jit(solution)/shard_map/pallas_call | solution.py:35
  84.1 5.2 %all-to-all-start = ((bf16[8,128,512]{2,1,0:T(8,128)(2,1)}), bf16[8,128,512]{2,1,0:T(8,128)(2,1)S(1)}, u32[]{:S(2)}, u32[]{:S(2)}) async-start(bf16[8,128,512]{2,1,0:T(8,128)(2,1)} %shard_map.105), calls=%async_computation | async-start | bytes 2097152 | tf_op jit(solution)/shard_map/all_to_all | solution.py:376
  89.3 1.6 collective-permute-start.15
  90.9 5.3 %shard_map.102 = (bf16[2,128,896]{2,1,0:T(8,128)(2,1)S(1)}, bf16[2,128,896]{2,1,0:T(8,128)(2,1)S(1)}, f32[512,256]{1,0:T(8,128)S(1)}) custom-call(s32[3]{0:T(128)S(1)} %pad_add_fusion.me_ref, bf16[2,2,128,896]{3,2,1,0:T(8,128)(2,1)S(1)} %copy-done.16, bf16[2,2,128,896]{3,2,1,0:T(8,128)(2,1)} %collective-permute-done.refs_1_.pack_ref, ...), custom_call_target="tpu_custom_call" | custom-call | bytes 18000000 | tf_op jit(solution)/shard_map/pallas_call | solution.py:35
  96.2 7.1 %collective-permute-done.15 = f32[512,256]{1,0:T(8,128)S(1)} collective-permute-done((f32[512,256]{1,0:T(8,128)S(1)}, f32[512,256]{1,0:T(8,128)S(1)}, u32[]{:S(2)}, u32[]{:S(2)}) %collective-permute-start.15) | collective-permute-done | bytes 524320 | tf_op jit(solution)/shard_map/ppermute | solution.py:359
  103.6 1.5 collective-permute-done.16.gc_ref
  105.1 10.6 %all-to-all-done.refs_0_ = bf16[8,128,512]{2,1,0:T(8,128)(2,1)S(1)} async-done(((bf16[8,128,512]{2,1,0:T(8,128)(2,1)}), bf16[8,128,512]{2,1,0:T(8,128)(2,1)S(1)}, u32[]{:S(2)}, u32[]{:S(2)}) %all-to-all-start) | async-done | bytes 1048608 | tf_op jit(solution)/shard_map/all_to_all | solution.py:376
  115.7 5.9 %shard_map.106 = (f32[128,3584]{1,0:T(8,128)S(1)}, bf16[128,3584]{1,0:T(8,128)(2,1)S(1)}) custom-call(s32[3]{0:T(128)S(1)} %pad_add_fusion.me_ref, f32[512,1]{1,0:T(8,128)S(1)} %copy-done.47, bf16[512,256]{1,0:T(8,128)(2,1)S(1)} %add_convert_fusion.1.g_ref.refs_0_, bf16[512,256]{1,0:T(8,128)(2,1)S(1)} %collective-permute-done.16.gc_ref, ...), custom_call_target="tpu_custom_call" | custom-call | bytes 21000000 | tf_op jit(solution)/shard_map/pallas_call | solution.py:35
  122.5 1.2 copy-done.23
  123.8 1.5 collective-permute-start.20
  125.3 1.2 collective-permute-start.18
  126.5 1.4 collective-permute-start.26
  128.5 6.0 %collective-permute-done.26.refs_6_ = bf16[512,256]{1,0:T(8,128)(2,1)S(1)} collective-permute-done((bf16[512,256]{1,0:T(8,128)(2,1)}, bf16[512,256]{1,0:T(8,128)(2,1)S(1)}, u32[]{:S(2)}, u32[]{:S(2)}) %collective-permute-start.26) | collective-permute-done | bytes 262176 | tf_op jit(solution)/shard_map/ppermute | solution.py:366
  134.5 1.4 collective-permute-start.27
  136.5 4.8 %collective-permute-done.27.refs_8_ = bf16[512,256]{1,0:T(8,128)(2,1)S(1)} collective-permute-done((bf16[512,256]{1,0:T(8,128)(2,1)S(1)}, bf16[512,256]{1,0:T(8,128)(2,1)S(1)}, u32[]{:S(2)}, u32[]{:S(2)}) %collective-permute-start.27) | collective-permute-done | bytes 262176 | tf_op jit(solution)/shard_map/ppermute | solution.py:366
  141.3 1.4 collective-permute-start.28
  143.4 6.7 %collective-permute-done.20.refs_2_ = bf16[8,128,512]{2,1,0:T(8,128)(2,1)S(1)} collective-permute-done((bf16[8,128,512]{2,1,0:T(8,128)(2,1)}, bf16[8,128,512]{2,1,0:T(8,128)(2,1)S(1)}, u32[]{:S(2)}, u32[]{:S(2)}) %collective-permute-start.20) | collective-permute-done | bytes 1048608 | tf_op jit(solution)/shard_map/ppermute | solution.py:359
  150.1 1.9 %shard_map.103 = (bf16[128,3584]{1,0:T(8,128)(2,1)}, bf16[128,3584]{1,0:T(8,128)(2,1)}) custom-call(s32[3]{0:T(128)S(1)} %pad_add_fusion.me_ref, bf16[2,128,896]{2,1,0:T(8,128)(2,1)S(1)} %copy-done.45, bf16[2,128,896]{2,1,0:T(8,128)(2,1)S(1)} %collective-permute-done.13.refs_1_, bf16[2,128,896]{2,1,0:T(8,128)(2,1)S(1)} %copy-done.43, ...), custom_call_target="tpu_custom_call" | custom-call | bytes 9000000 | tf_op jit(solution)/shard_map/pallas_call | solution.py:35
  152.0 1.5 collective-permute-start.29
  154.2 14.0 %collective-permute-done.18 = bf16[128,3584]{1,0:T(8,128)(2,1)} collective-permute-done((bf16[128,3584]{1,0:T(8,128)(2,1)S(1)}, bf16[128,3584]{1,0:T(8,128)(2,1)}, u32[]{:S(2)}, u32[]{:S(2)}) %collective-permute-start.18) | collective-permute-done | bytes 917536 | tf_op jit(solution)/shard_map/ppermute | solution.py:359
  168.2 2.4 %fusion = bf16[1,128,3584]{2,1,0:T(8,128)(2,1)} fusion(f32[128,3584]{1,0:T(8,128)S(1)} %copy-done.24, bf16[128,3584]{1,0:T(8,128)(2,1)} %collective-permute-done.18), kind=kLoop, calls=%fused_computation.1 | loop fusion | flops 1376256 | bytes 3670016 | tf_op jit(solution)/shard_map/broadcast_in_dim | solution.py:428
  170.6 2.5 %shard_map.109.refs_6_ = f32[512,512]{1,0:T(8,128)S(1)} custom-call(s32[3]{0:T(128)S(1)} %pad_add_fusion.me_ref, bf16[8,128,512]{2,1,0:T(8,128)(2,1)S(1)} %copy-done.1, bf16[8,128,512]{2,1,0:T(8,128)(2,1)S(1)} %collective-permute-done.19.refs_1_, bf16[8,128,512]{2,1,0:T(8,128)(2,1)S(1)} %collective-permute-done.20.refs_2_, ...), custom_call_target="tpu_custom_call" | custom-call | bytes 9000000 | tf_op jit(solution)/shard_map/pallas_call | solution.py:35
  173.1 1.5 shard_map.110.refs_6_
  174.6 2.0 %shard_map.111 = f32[2,448,256]{2,1,0:T(8,128)} custom-call(s32[3]{0:T(128)S(1)} %pad_add_fusion.me_ref, bf16[8,128,512]{2,1,0:T(8,128)(2,1)S(1)} %copy-done.1, bf16[8,128,512]{2,1,0:T(8,128)(2,1)S(1)} %collective-permute-done.19.refs_1_, bf16[8,128,512]{2,1,0:T(8,128)(2,1)S(1)} %collective-permute-done.20.refs_2_, ...), custom_call_target="tpu_custom_call" | custom-call | bytes 9000000 | tf_op jit(solution)/shard_map/pallas_call | solution.py:35
  (146 shorter events, 16.5 us)
Async XLA Ops:
  4.2 60.5 %copy-start.2 = (bf16[8,128,512]{2,1,0:T(8,128)(2,1)}, bf16[8,128,512]{2,1,0:T(8,128)(2,1)S(1)}, u32[]{:S(2)}) copy-start(bf16[8,128,512]{2,1,0:T(8,128)(2,1)S(1)} %shard_map.94.refs_0_) | copy-start | bytes 3145732
  4.2 26.2 %collective-permute-start.2 = (bf16[8,128,512]{2,1,0:T(8,128)(2,1)S(1)}, bf16[8,128,512]{2,1,0:T(8,128)(2,1)S(1)}, u32[]{:S(2)}, u32[]{:S(2)}) collective-permute-start(bf16[8,128,512]{2,1,0:T(8,128)(2,1)S(1)} %shard_map.94.refs_0_), channel_id=1, source_target_pairs={{0,2},{1,3},{2,0},{3,1},{4,6},{5,7},{6,4},{7,5},{8,10},{9,11},{10,... | collective-permute-start | bytes 3145736 | tf_op jit(solution)/shard_map/ppermute | solution.py:359
  7.2 12.0 %collective-permute-start.5 = (bf16[2,448,256]{2,1,0:T(8,128)(2,1)S(1)}, bf16[2,448,256]{2,1,0:T(8,128)(2,1)S(1)}, u32[]{:S(2)}, u32[]{:S(2)}) collective-permute-start(bf16[2,448,256]{2,1,0:T(8,128)(2,1)S(1)} %copy-done.25), channel_id=1, source_target_pairs={{0,4},{8,0},{16,8},{24,16},{28,24},{20,28},{12,20},{4,12},{1,5},{9... | collective-permute-start | bytes 1376264 | tf_op jit(solution)/shard_map/ppermute | solution.py:366
  8.7 12.7 %collective-permute-start.3 = (bf16[2,448,256]{2,1,0:T(8,128)(2,1)S(1)}, bf16[2,448,256]{2,1,0:T(8,128)(2,1)S(1)}, u32[]{:S(2)}, u32[]{:S(2)}) collective-permute-start(bf16[2,448,256]{2,1,0:T(8,128)(2,1)S(1)} %copy-done.25), channel_id=1, source_target_pairs={{0,8},{8,16},{16,24},{24,28},{28,20},{20,12},{12,4},{4,0},{1,9},{9... | collective-permute-start | bytes 1376264 | tf_op jit(solution)/shard_map/ppermute | solution.py:366
  19.2 12.2 %collective-permute-start.6 = (bf16[2,448,256]{2,1,0:T(8,128)(2,1)S(1)}, bf16[2,448,256]{2,1,0:T(8,128)(2,1)}, u32[]{:S(2)}, u32[]{:S(2)}) collective-permute-start(bf16[2,448,256]{2,1,0:T(8,128)(2,1)S(1)} %collective-permute-done.5.refs_6_.refs_2_), channel_id=1, source_target_pairs={{0,4},{8,0},{16,8},{24,16},{28,24},{20,28},{12,20},{4,12},{1,5},{9... | collective-permute-start | bytes 1376264 | tf_op jit(solution)/shard_map/ppermute | solution.py:366
  21.4 10.9 %collective-permute-start.4 = (bf16[2,448,256]{2,1,0:T(8,128)(2,1)S(1)}, bf16[2,448,256]{2,1,0:T(8,128)(2,1)}, u32[]{:S(2)}, u32[]{:S(2)}) collective-permute-start(bf16[2,448,256]{2,1,0:T(8,128)(2,1)S(1)} %collective-permute-done.3.refs_5_.refs_1_), channel_id=1, source_target_pairs={{0,8},{8,16},{16,24},{24,28},{28,20},{20,12},{12,4},{4,0},{1,9},{9... | collective-permute-start | bytes 1376264 | tf_op jit(solution)/shard_map/ppermute | solution.py:366
  22.0 29.8 %collective-permute-start.1 = (bf16[8,128,512]{2,1,0:T(8,128)(2,1)S(1)}, bf16[8,128,512]{2,1,0:T(8,128)(2,1)S(1)}, u32[]{:S(2)}, u32[]{:S(2)}) collective-permute-start(bf16[8,128,512]{2,1,0:T(8,128)(2,1)S(1)} %shard_map.94.refs_0_), channel_id=1, source_target_pairs={{0,1},{1,0},{2,3},{3,2},{4,5},{5,4},{6,7},{7,6},{8,9},{9,8},{10,11... | collective-permute-start | bytes 3145736 | tf_op jit(solution)/shard_map/ppermute | solution.py:359
  32.3 19.4 %copy-start.26 = (bf16[2,448,256]{2,1,0:T(8,128)(2,1)S(1)}, bf16[2,448,256]{2,1,0:T(8,128)(2,1)}, u32[]{:S(2)}) copy-start(bf16[2,448,256]{2,1,0:T(8,128)(2,1)} %refs_0_.1) | copy-start | bytes 1376260
  32.3 19.4 %copy-start.29 = (bf16[2,448,256]{2,1,0:T(8,128)(2,1)S(1)}, bf16[2,448,256]{2,1,0:T(8,128)(2,1)}, u32[]{:S(2)}) copy-start(bf16[2,448,256]{2,1,0:T(8,128)(2,1)} %copy-done.28) | copy-start | bytes 1376260
  32.4 19.4 %copy-start.32 = (bf16[2,448,256]{2,1,0:T(8,128)(2,1)S(1)}, bf16[2,448,256]{2,1,0:T(8,128)(2,1)}, u32[]{:S(2)}) copy-start(bf16[2,448,256]{2,1,0:T(8,128)(2,1)} %copy-done.31) | copy-start | bytes 1376260
  32.4 19.4 %collective-permute-start.7 = (bf16[8,128,512]{2,1,0:T(8,128)(2,1)}, bf16[8,128,512]{2,1,0:T(8,128)(2,1)S(1)}, u32[]{:S(2)}, u32[]{:S(2)}) collective-permute-start(bf16[8,128,512]{2,1,0:T(8,128)(2,1)} %shard_map.95), channel_id=1, source_target_pairs={{0,1},{1,0},{2,3},{3,2},{4,5},{5,4},{6,7},{7,6},{8,9},{9,8},{10,11... | collective-permute-start | bytes 3145736 | tf_op jit(solution)/shard_map/ppermute | solution.py:359
  35.6 16.2 %copy-start.15 = (bf16[2,2,128,896]{3,2,1,0:T(8,128)(2,1)}, bf16[2,2,128,896]{3,2,1,0:T(8,128)(2,1)S(1)}, u32[]{:S(2)}) copy-start(bf16[2,2,128,896]{3,2,1,0:T(8,128)(2,1)S(1)} %get-tuple-element.20.own_ref) | copy-start | bytes 2752516
  35.6 20.6 %collective-permute-start = (bf16[2,2,128,896]{3,2,1,0:T(8,128)(2,1)S(1)}, bf16[2,2,128,896]{3,2,1,0:T(8,128)(2,1)}, u32[]{:S(2)}, u32[]{:S(2)}) collective-permute-start(bf16[2,2,128,896]{3,2,1,0:T(8,128)(2,1)S(1)} %get-tuple-element.21), channel_id=1, source_target_pairs={{0,1},{1,0},{2,3},{3,2},{4,5},{5,4},{6,7},{7,6},{8,9},{9,8},{10,11... | collective-permute-start | bytes 2752520 | tf_op jit(solution)/shard_map/ppermute | solution.py:359
  36.0 12.7 %collective-permute-start.10 = (bf16[2,448,256]{2,1,0:T(8,128)(2,1)}, bf16[2,448,256]{2,1,0:T(8,128)(2,1)S(1)}, u32[]{:S(2)}, u32[]{:S(2)}) collective-permute-start(bf16[2,448,256]{2,1,0:T(8,128)(2,1)} %collective-permute-done.6.refs_2_.refs_8_.refs_4_), channel_id=1, source_target_pairs={{0,4},{8,0},{16,8},{24,16},{28,24},{20,28},{12,20},{4,12},{1,5},{9... | collective-permute-start | bytes 1376264 | tf_op jit(solution)/shard_map/ppermute | solution.py:366
  37.6 12.7 %collective-permute-start.8 = (bf16[2,448,256]{2,1,0:T(8,128)(2,1)}, bf16[2,448,256]{2,1,0:T(8,128)(2,1)S(1)}, u32[]{:S(2)}, u32[]{:S(2)}) collective-permute-start(bf16[2,448,256]{2,1,0:T(8,128)(2,1)} %collective-permute-done.4.refs_1_.refs_7_.refs_3_), channel_id=1, source_target_pairs={{0,8},{8,16},{16,24},{24,28},{28,20},{20,12},{12,4},{4,0},{1,9},{9... | collective-permute-start | bytes 1376264 | tf_op jit(solution)/shard_map/ppermute | solution.py:366
  56.2 7.8 %collective-permute-start.9 = (bf16[1,448,256]{2,1,0:T(8,128)(2,1)}, bf16[1,448,256]{2,1,0:T(8,128)(2,1)S(1)}, u32[]{:S(2)}, u32[]{:S(2)}) collective-permute-start(bf16[1,448,256]{2,1,0:T(8,128)(2,1)} %shard_map.97), channel_id=1, source_target_pairs={{0,8},{8,16},{16,24},{24,28},{28,20},{20,12},{12,4},{4,0},{1,9},{9... | collective-permute-start | bytes 688136 | tf_op jit(solution)/shard_map/ppermute | solution.py:366
  57.0 7.6 %collective-permute-start.11 = (bf16[1,448,256]{2,1,0:T(8,128)(2,1)}, bf16[1,448,256]{2,1,0:T(8,128)(2,1)S(1)}, u32[]{:S(2)}, u32[]{:S(2)}) collective-permute-start(bf16[1,448,256]{2,1,0:T(8,128)(2,1)} %shard_map.98), channel_id=1, source_target_pairs={{0,4},{8,0},{16,8},{24,16},{28,24},{20,28},{12,20},{4,12},{1,5},{9... | collective-permute-start | bytes 688136 | tf_op jit(solution)/shard_map/ppermute | solution.py:366
  65.6 15.0 %copy-start.41 = (bf16[1,448,256]{2,1,0:T(8,128)(2,1)S(1)}, bf16[1,448,256]{2,1,0:T(8,128)(2,1)}, u32[]{:S(2)}) copy-start(bf16[1,448,256]{2,1,0:T(8,128)(2,1)} %copy-done.39) | copy-start | bytes 688132
  67.5 16.6 %copy-start.34 = (bf16[512,256]{1,0:T(8,128)(2,1)}, bf16[512,256]{1,0:T(8,128)(2,1)S(1)}, u32[]{:S(2)}) copy-start(bf16[512,256]{1,0:T(8,128)(2,1)S(1)} %get-tuple-element.22.kv_ref.refs_1_) | copy-start | bytes 786436
  67.5 13.1 %copy-start.19 = (bf16[2,448,256]{2,1,0:T(8,128)(2,1)S(1)}, bf16[2,448,256]{2,1,0:T(8,128)(2,1)}, u32[]{:S(2)}) copy-start(bf16[2,448,256]{2,1,0:T(8,128)(2,1)} %copy-done.17) | copy-start | bytes 1376260
  67.5 13.1 %copy-start.22 = (bf16[2,448,256]{2,1,0:T(8,128)(2,1)S(1)}, bf16[2,448,256]{2,1,0:T(8,128)(2,1)}, u32[]{:S(2)}) copy-start(bf16[2,448,256]{2,1,0:T(8,128)(2,1)} %copy-done.20) | copy-start | bytes 1376260
  67.5 13.1 %copy-start.27 = (bf16[2,448,256]{2,1,0:T(8,128)(2,1)S(1)}, bf16[2,448,256]{2,1,0:T(8,128)(2,1)}, u32[]{:S(2)}) copy-start(bf16[2,448,256]{2,1,0:T(8,128)(2,1)} %refs_0_.1) | copy-start | bytes 1376260
  67.5 13.1 %copy-start.30 = (bf16[2,448,256]{2,1,0:T(8,128)(2,1)S(1)}, bf16[2,448,256]{2,1,0:T(8,128)(2,1)}, u32[]{:S(2)}) copy-start(bf16[2,448,256]{2,1,0:T(8,128)(2,1)} %copy-done.28) | copy-start | bytes 1376260
  67.5 13.1 %copy-start.33 = (bf16[2,448,256]{2,1,0:T(8,128)(2,1)S(1)}, bf16[2,448,256]{2,1,0:T(8,128)(2,1)}, u32[]{:S(2)}) copy-start(bf16[2,448,256]{2,1,0:T(8,128)(2,1)} %copy-done.31) | copy-start | bytes 1376260
  67.5 7.0 %collective-permute-start.12 = (bf16[512,256]{1,0:T(8,128)(2,1)S(1)}, bf16[512,256]{1,0:T(8,128)(2,1)S(1)}, u32[]{:S(2)}, u32[]{:S(2)}) collective-permute-start(bf16[512,256]{1,0:T(8,128)(2,1)S(1)} %get-tuple-element.22.kv_ref.refs_1_), channel_id=1, source_target_pairs={{0,2},{1,3},{2,0},{3,1},{4,6},{5,7},{6,4},{7,5},{8,10},{9,11},{10,... | collective-permute-start | bytes 786440 | tf_op jit(solution)/shard_map/ppermute | solution.py:359
  84.0 31.7 %collective-permute-start.17 = (bf16[8,2,448,256]{3,2,1,0:T(8,128)(2,1)}, bf16[8,2,448,256]{3,2,1,0:T(8,128)(2,1)}, u32[]{:S(2)}, u32[]{:S(2)}) collective-permute-start(bf16[8,2,448,256]{3,2,1,0:T(8,128)(2,1)} %shard_map.104.w_ref), channel_id=1, source_target_pairs={{0,1},{1,0},{2,3},{3,2},{4,5},{5,4},{6,7},{7,6},{8,9},{9,8},{10,11... | collective-permute-start | bytes 11010056 | tf_op jit(solution)/shard_map/ppermute | solution.py:359
  84.1 31.6 %all-to-all-start = ((bf16[8,128,512]{2,1,0:T(8,128)(2,1)}), bf16[8,128,512]{2,1,0:T(8,128)(2,1)S(1)}, u32[]{:S(2)}, u32[]{:S(2)}) async-start(bf16[8,128,512]{2,1,0:T(8,128)(2,1)} %shard_map.105), calls=%async_computation | async-start | bytes 2097152 | tf_op jit(solution)/shard_map/all_to_all | solution.py:376
  89.3 26.4 %copy-start.47 = (f32[512,1]{1,0:T(8,128)S(1)}, f32[512,1]{1,0:T(8,128)}, u32[]{:S(2)}) copy-start(f32[512,1]{1,0:T(8,128)} %copy-done.46) | copy-start | bytes 6148
  89.3 14.1 %collective-permute-start.15 = (f32[512,256]{1,0:T(8,128)S(1)}, f32[512,256]{1,0:T(8,128)S(1)}, u32[]{:S(2)}, u32[]{:S(2)}) collective-permute-start(f32[512,256]{1,0:T(8,128)S(1)} %get-tuple-element.25.refs_0_.refs_9_), channel_id=1, source_target_pairs={{0,2},{1,3},{2,0},{3,1},{4,6},{5,7},{6,4},{7,5},{8,10},{9,11},{10,... | collective-permute-start | bytes 1572872 | tf_op jit(solution)/shard_map/ppermute | solution.py:359
  103.4 18.2 %copy-start.11 = (bf16[512,256]{1,0:T(8,128)(2,1)}, bf16[512,256]{1,0:T(8,128)(2,1)S(1)}, u32[]{:S(2)}) copy-start(bf16[512,256]{1,0:T(8,128)(2,1)S(1)} %add_convert_fusion.1.g_ref.refs_0_) | copy-start | bytes 786436
  103.5 1.6 collective-permute-start.16
  123.8 26.3 %copy-start.43 = (bf16[2,128,896]{2,1,0:T(8,128)(2,1)S(1)}, bf16[2,128,896]{2,1,0:T(8,128)(2,1)}, u32[]{:S(2)}) copy-start(bf16[2,128,896]{2,1,0:T(8,128)(2,1)} %copy-done.42) | copy-start | bytes 1376260
  123.8 26.3 %copy-start.45 = (bf16[2,128,896]{2,1,0:T(8,128)(2,1)S(1)}, bf16[2,128,896]{2,1,0:T(8,128)(2,1)}, u32[]{:S(2)}) copy-start(bf16[2,128,896]{2,1,0:T(8,128)(2,1)} %copy-done.44) | copy-start | bytes 1376260
  123.8 26.3 %collective-permute-start.20 = (bf16[8,128,512]{2,1,0:T(8,128)(2,1)}, bf16[8,128,512]{2,1,0:T(8,128)(2,1)S(1)}, u32[]{:S(2)}, u32[]{:S(2)}) collective-permute-start(bf16[8,128,512]{2,1,0:T(8,128)(2,1)} %shard_map.107.refs_0_), channel_id=1, source_target_pairs={{0,2},{1,3},{2,0},{3,1},{4,6},{5,7},{6,4},{7,5},{8,10},{9,11},{10,... | collective-permute-start | bytes 3145736 | tf_op jit(solution)/shard_map/ppermute | solution.py:359
  125.3 11.2 %collective-permute-start.14 = (bf16[2,128,896]{2,1,0:T(8,128)(2,1)}, bf16[2,128,896]{2,1,0:T(8,128)(2,1)S(1)}, u32[]{:S(2)}, u32[]{:S(2)}) collective-permute-start(bf16[2,128,896]{2,1,0:T(8,128)(2,1)} %copy-done.50), channel_id=1, source_target_pairs={{0,1},{1,0},{2,3},{3,2},{4,5},{5,4},{6,7},{7,6},{8,9},{9,8},{10,11... | collective-permute-start | bytes 1376264 | tf_op jit(solution)/shard_map/ppermute | solution.py:359
  125.3 42.9 %collective-permute-start.18 = (bf16[128,3584]{1,0:T(8,128)(2,1)S(1)}, bf16[128,3584]{1,0:T(8,128)(2,1)}, u32[]{:S(2)}, u32[]{:S(2)}) collective-permute-start(bf16[128,3584]{1,0:T(8,128)(2,1)S(1)} %copy-done.14), channel_id=1, source_target_pairs={{0,2},{1,3},{2,0},{3,1},{4,6},{5,7},{6,4},{7,5},{8,10},{9,11},{10,... | collective-permute-start | bytes 2752520 | tf_op jit(solution)/shard_map/ppermute | solution.py:359
  126.5 41.7 %copy-start.24 = (f32[128,3584]{1,0:T(8,128)S(1)}, f32[128,3584]{1,0:T(8,128)}, u32[]{:S(2)}) copy-start(f32[128,3584]{1,0:T(8,128)} %copy-done.23) | copy-start | bytes 5505028
  126.5 8.0 %collective-permute-start.26 = (bf16[512,256]{1,0:T(8,128)(2,1)}, bf16[512,256]{1,0:T(8,128)(2,1)S(1)}, u32[]{:S(2)}, u32[]{:S(2)}) collective-permute-start(bf16[512,256]{1,0:T(8,128)(2,1)} %shard_map.108.refs_4_), channel_id=1, source_target_pairs={{0,4},{8,0},{16,8},{24,16},{28,24},{20,28},{12,20},{4,12},{1,5},{9... | collective-permute-start | bytes 786440 | tf_op jit(solution)/shard_map/ppermute | solution.py:366
  127.9 8.0 %collective-permute-start.22 = (bf16[512,256]{1,0:T(8,128)(2,1)}, bf16[512,256]{1,0:T(8,128)(2,1)S(1)}, u32[]{:S(2)}, u32[]{:S(2)}) collective-permute-start(bf16[512,256]{1,0:T(8,128)(2,1)} %shard_map.108.refs_4_), channel_id=1, source_target_pairs={{0,8},{8,16},{16,24},{24,28},{28,20},{20,12},{12,4},{4,0},{1,9},{9... | collective-permute-start | bytes 786440 | tf_op jit(solution)/shard_map/ppermute | solution.py:366
  134.5 6.9 %collective-permute-start.27 = (bf16[512,256]{1,0:T(8,128)(2,1)S(1)}, bf16[512,256]{1,0:T(8,128)(2,1)S(1)}, u32[]{:S(2)}, u32[]{:S(2)}) collective-permute-start(bf16[512,256]{1,0:T(8,128)(2,1)S(1)} %collective-permute-done.26.refs_6_), channel_id=1, source_target_pairs={{0,4},{8,0},{16,8},{24,16},{28,24},{20,28},{12,20},{4,12},{1,5},{9... | collective-permute-start | bytes 786440 | tf_op jit(solution)/shard_map/ppermute | solution.py:366
  135.9 6.9 %collective-permute-start.23 = (bf16[512,256]{1,0:T(8,128)(2,1)S(1)}, bf16[512,256]{1,0:T(8,128)(2,1)S(1)}, u32[]{:S(2)}, u32[]{:S(2)}) collective-permute-start(bf16[512,256]{1,0:T(8,128)(2,1)S(1)} %collective-permute-done.22.refs_5_), channel_id=1, source_target_pairs={{0,8},{8,16},{16,24},{24,28},{28,20},{20,12},{12,4},{4,0},{1,9},{9... | collective-permute-start | bytes 786440 | tf_op jit(solution)/shard_map/ppermute | solution.py:366
  136.5 6.9 %collective-permute-start.13 = (bf16[2,128,896]{2,1,0:T(8,128)(2,1)}, bf16[2,128,896]{2,1,0:T(8,128)(2,1)S(1)}, u32[]{:S(2)}, u32[]{:S(2)}) collective-permute-start(bf16[2,128,896]{2,1,0:T(8,128)(2,1)} %copy-done.51), channel_id=1, source_target_pairs={{0,1},{1,0},{2,3},{3,2},{4,5},{5,4},{6,7},{7,6},{8,9},{9,8},{10,11... | collective-permute-start | bytes 1376264 | tf_op jit(solution)/shard_map/ppermute | solution.py:359
  141.3 10.7 %collective-permute-start.28 = (bf16[512,256]{1,0:T(8,128)(2,1)S(1)}, bf16[512,256]{1,0:T(8,128)(2,1)S(1)}, u32[]{:S(2)}, u32[]{:S(2)}) collective-permute-start(bf16[512,256]{1,0:T(8,128)(2,1)S(1)} %collective-permute-done.27.refs_8_), channel_id=1, source_target_pairs={{0,4},{8,0},{16,8},{24,16},{28,24},{20,28},{12,20},{4,12},{1,5},{9... | collective-permute-start | bytes 786440 | tf_op jit(solution)/shard_map/ppermute | solution.py:366
  142.8 10.7 %collective-permute-start.24 = (bf16[512,256]{1,0:T(8,128)(2,1)S(1)}, bf16[512,256]{1,0:T(8,128)(2,1)S(1)}, u32[]{:S(2)}, u32[]{:S(2)}) collective-permute-start(bf16[512,256]{1,0:T(8,128)(2,1)S(1)} %collective-permute-done.23.refs_7_), channel_id=1, source_target_pairs={{0,8},{8,16},{16,24},{24,28},{28,20},{20,12},{12,4},{4,0},{1,9},{9... | collective-permute-start | bytes 786440 | tf_op jit(solution)/shard_map/ppermute | solution.py:366
  143.4 27.2 %collective-permute-start.19 = (bf16[8,128,512]{2,1,0:T(8,128)(2,1)}, bf16[8,128,512]{2,1,0:T(8,128)(2,1)S(1)}, u32[]{:S(2)}, u32[]{:S(2)}) collective-permute-start(bf16[8,128,512]{2,1,0:T(8,128)(2,1)} %shard_map.107.refs_0_), channel_id=1, source_target_pairs={{0,1},{1,0},{2,3},{3,2},{4,5},{5,4},{6,7},{7,6},{8,9},{9,8},{10,11... | collective-permute-start | bytes 3145736 | tf_op jit(solution)/shard_map/ppermute | solution.py:359
  150.1 20.5 %collective-permute-start.21 = (bf16[8,128,512]{2,1,0:T(8,128)(2,1)S(1)}, bf16[8,128,512]{2,1,0:T(8,128)(2,1)S(1)}, u32[]{:S(2)}, u32[]{:S(2)}) collective-permute-start(bf16[8,128,512]{2,1,0:T(8,128)(2,1)S(1)} %collective-permute-done.20.refs_2_), channel_id=1, source_target_pairs={{0,1},{1,0},{2,3},{3,2},{4,5},{5,4},{6,7},{7,6},{8,9},{9,8},{10,11... | collective-permute-start | bytes 3145736 | tf_op jit(solution)/shard_map/ppermute | solution.py:359
  152.0 22.5 %collective-permute-start.29 = (bf16[256,256]{1,0:T(8,128)(2,1)S(1)}, bf16[256,256]{1,0:T(8,128)(2,1)S(1)}, u32[]{:S(2)}, u32[]{:S(2)}) collective-permute-start(bf16[256,256]{1,0:T(8,128)(2,1)S(1)} %slice.19), channel_id=1, source_target_pairs={{0,4},{8,0},{16,8},{24,16},{28,24},{20,28},{12,20},{4,12},{1,5},{9... | collective-permute-start | bytes 393224 | tf_op jit(solution)/shard_map/ppermute | solution.py:366
  153.5 21.1 %collective-permute-start.25 = (bf16[256,256]{1,0:T(8,128)(2,1)S(1)}, bf16[256,256]{1,0:T(8,128)(2,1)S(1)}, u32[]{:S(2)}, u32[]{:S(2)}) collective-permute-start(bf16[256,256]{1,0:T(8,128)(2,1)S(1)} %slice.18), channel_id=1, source_target_pairs={{0,8},{8,16},{16,24},{24,28},{28,20},{20,12},{12,4},{4,0},{1,9},{9... | collective-permute-start | bytes 393224 | tf_op jit(solution)/shard_map/ppermute | solution.py:366
  (35 other events, 95.0 us)

commit v6 on v5

--- a/solution.py
+++ b/solution.py
@@ -30,19 +30,27 @@
     return jax.ShapeDtypeStruct(shape, dtype)
 
 
-def call(body, me, operands, out_shape, micros, scratch=(), anywhere=0):
+def call(body, me, operands, out_shape, micros, scratch=(), far=(), far_out=(), aliases=None):
     near = pl.BlockSpec(memory_space=pltpu.VMEM)
+    outs = [ANYWHERE if i in far_out else near for i in range(len(out_shape))] if isinstance(out_shape, list) else near
     return pl.pallas_call(
         body,
         in_specs=[pl.BlockSpec(memory_space=pltpu.SMEM)]
-        + [near] * (len(operands) - anywhere)
-        + [ANYWHERE] * anywhere,
-        out_specs=[near] * len(out_shape) if isinstance(out_shape, list) else near,
+        + [ANYWHERE if i in far else near for i in range(len(operands))],
+        out_specs=outs,
         out_shape=out_shape,
         scratch_shapes=scratch,
+        input_output_aliases=aliases or {},
         compiler_params=pltpu.CompilerParams(vmem_limit_bytes=24 * 1024 * 1024),
         cost_estimate=pl.CostEstimate(flops=0, bytes_accessed=micros * 3000000, transcendentals=0),
     )(me, *operands)
+
+
+def run_copies(copies):
+    for copy in copies:
+        copy.start()
+    for copy in copies:
+        copy.wait()
 
 
 def owner_at(me_f, by):
@@ -69,7 +77,9 @@
     return jnp.broadcast_to(row, (128, row.shape[1])).T[:, :1]
 
 
-def blocks_kernel(depth, me_ref, tok_ref, kind_ref, ids_ref, out_ref):
+def blocks_kernel(depth, me_ref, tok_far, kind_far, ids_far, out_ref, tok_ref, kind_ref, ids_ref, sems):
+    pairs = ((tok_far, tok_ref), (kind_far, kind_ref), (ids_far, ids_ref))
+    run_copies([pltpu.make_async_copy(a, b, sems.at[i]) for i, (a, b) in enumerate(pairs)])
     count, rows, lanes = out_ref.shape
     base = lanes - 128
     lane = lax.broadcasted_iota(jnp.int32, (rows, 128), 1) - (depth - base)
@@ -89,7 +99,20 @@
     depth = width // count
     lanes = -(-(depth + 3) // 128) * 128
     out = shaped((count, rows, lanes), BF16)
-    return call(functools.partial(blocks_kernel, depth), me, (tokens, kinds, ids), out, 1)
+    return call(
+        functools.partial(blocks_kernel, depth),
+        me,
+        (tokens, kinds, ids),
+        out,
+        2,
+        scratch=[
+            pltpu.VMEM((rows, width), BF16),
+            pltpu.VMEM((1, rows), jnp.int32),
+            pltpu.VMEM((1, rows), jnp.int32),
+            pltpu.SemaphoreType.DMA((3,)),
+        ],
+        far=(0, 1, 2),
+    )
 
 
 def read_marks(block, depth):
@@ -97,17 +120,21 @@
     return mark[0], mark[1] * DIGIT + mark[2]
 
 
-def pack_kernel(me_ref, q_ref, up_ref, own_ref, other_ref):
+def pack_kernel(me_ref, q_far, up_far, own_ref, other_ref, sems):
+    copies = []
     for i in range(4):
         here = pl.ds(pl.multiple_of((me_ref[0] ^ i) * SPAN, SPAN), SPAN)
         out_ref = other_ref if i % 2 else own_ref
-        out_ref[i // 2, 0] = q_ref[:, here]
-        out_ref[i // 2, 1] = up_ref[:, here]
+        for k, far in enumerate((q_far, up_far)):
+            copies.append(pltpu.make_async_copy(far.at[:, here], out_ref.at[i // 2, k], sems.at[2 * i + k]))
+    run_copies(copies)
 
 
 def pack_heads(me, queries, upstream):
     out = shaped((2, 2, queries.shape[0], SPAN), BF16)
-    return call(pack_kernel, me, (queries, upstream), [out, out], 2)
+    return call(
+        pack_kernel, me, (queries, upstream), [out, out], 2, scratch=[pltpu.SemaphoreType.DMA((8,))], far=(0, 1)
+    )
 
 
 def place_kernel(me_ref, *refs):
@@ -126,47 +153,59 @@
 def project_kernel(steps, depth, halves, first, last, me_ref, *refs):
     parts, refs = refs[:4], refs[4:]
     weights, refs = refs[: len(steps) + halves], refs[len(steps) + halves :]
+    whole_ref, sems = refs[-2:]
     rows, lanes = parts[0].shape[1:]
+    owners = [owner_at(me_ref[1], by) for by in steps]
+    copies = []
+    for i, ref in enumerate(weights):
+        there = whole_ref.at[owners[0], pl.ds(i, 1)] if halves else whole_ref.at[owners[i]]
+        copies.append(pltpu.make_async_copy(ref, there, sems.at[i]))
+    for copy in copies:
+        copy.start()
     sums = [0.0, 0.0]
-    for b, by in enumerate(steps):
-        owner = owner_at(me_ref[1], by)
+    for b, owner in enumerate(owners):
         left = jnp.concatenate([ref[owner][:, :depth] for ref in parts], axis=0)
         for e in range(2):
             right = weights[e][0] if halves else weights[b][e]
             sums[e] = sums[e] + contract(left, right, 1, 0)
     if not first:
         sums = [s + refs[0][:, e * PAIR : (e + 1) * PAIR] for e, s in enumerate(sums)]
-        refs = refs[1:]
     if not last:
         for e in range(2):
-            refs[-1][:, e * PAIR : (e + 1) * PAIR] = sums[e]
-        return
-    kv_ref, kind_ref, ids_ref, ids_row_ref = refs[-4:]
-    for r in range(4):
-        here = pl.ds(pl.multiple_of((me_ref[0] ^ r) * rows, rows), rows)
-        kind, ids = read_marks(parts[r][0], depth)
-        mine = slice(r * rows, (r + 1) * rows)
-        kv_ref[here, :] = jnp.where(kind == 1.0, sums[1][mine], sums[0][mine]).astype(BF16)
-        kind_ref[here, :] = kind
-        ids_ref[here, :] = ids
-    ids_row_ref[...] = jnp.broadcast_to(ids_ref[...], (4 * rows, 128)).T[:1]
-
-
-def project(me, steps, parts, weights, total, depth, last=False, halves=False, wait=()):
+            refs[-3][:, e * PAIR : (e + 1) * PAIR] = sums[e]
+    else:
+        kv_ref, kind_ref, ids_ref, ids_row_ref = refs[-6:-2]
+        for r in range(4):
+            here = pl.ds(pl.multiple_of((me_ref[0] ^ r) * rows, rows), rows)
+            kind, ids = read_marks(parts[r][0], depth)
+            mine = slice(r * rows, (r + 1) * rows)
+            kv_ref[here, :] = jnp.where(kind == 1.0, sums[1][mine], sums[0][mine]).astype(BF16)
+            kind_ref[here, :] = kind
+            ids_ref[here, :] = ids
+        ids_row_ref[...] = jnp.broadcast_to(ids_ref[...], (4 * rows, 128)).T[:1]
+    for copy in copies:
+        copy.wait()
+
+
+def project(me, steps, parts, weights, before, depth, last=False, halves=False):
     rows, lanes = parts[0].shape[1:]
     length = 4 * rows
-    before = () if total is None else (total,)
-    out = shaped((length, 2 * PAIR), F32)
+    outs = [shaped((length, 2 * PAIR), F32)]
     if last:
-        out = [shaped((length, PAIR), BF16)] + [shaped(x, F32) for x in ((length, 1), (length, 1), (1, length))]
-    operands = (*parts, *weights, *before, *wait)
+        outs = [shaped((length, PAIR), BF16)] + [shaped(x, F32) for x in ((length, 1), (length, 1), (1, length))]
+    outs.append(shaped((len(CYCLE), 2, depth, PAIR), BF16))
+    operands = (*parts, *weights, *before)
+    count = len(operands)
     return call(
-        functools.partial(project_kernel, steps, depth, int(halves), total is None, last),
+        functools.partial(project_kernel, steps, depth, int(halves), not before, last),
         me,
         operands,
-        out,
+        outs,
         3,
-        anywhere=len(wait),
+        scratch=[pltpu.SemaphoreType.DMA((len(weights),))],
+        far=(count - 1,) if before else (),
+        far_out=(len(outs) - 1,),
+        aliases={count: len(outs) - 1} if before else None,
     )
 
 
@@ -223,7 +262,7 @@
         [side, side, shaped((length, PAIR), F32)],
         6,
         scratch=[pltpu.VMEM((2 * rows, length), F32), pltpu.VMEM(stacked, F32)] + [pltpu.VMEM(stacked, BF16)] * 4,
-        anywhere=len(wait),
+        far=tuple(range(5, 5 + len(wait))),
     )
 
 
@@ -255,73 +294,42 @@
         away_ref[:, cols] = total[rows:].astype(BF16)
 
 
-def hidden_grad(me, kind, grad, grad_c, weight, weight_c, rows, wait=()):
+def hidden_grad(me, kind, grad, grad_c, weight, weight_c, rows):
     count, _, depth, _ = weight.shape
     width = count * depth
     return call(
         hidden_kernel,
         me,
-        (kind, grad, grad_c, weight, weight_c, *wait),
+        (kind, grad, grad_c, weight, weight_c),
         [shaped((rows, width), F32), shaped((rows, width), BF16)],
         7,
-        anywhere=len(wait),
-    )
-
-
-def weight_kernel(steps, depth, halves, first, last, me_ref, *refs):
-    parts, refs = refs[:4], refs[4:]
-    grads, refs = refs[: len(steps) + halves], refs[len(steps) + halves :]
+    )
+
+
+def share_kernel(steps, depth, me_ref, *refs):
+    parts, g_ref, outs = refs[:4], refs[4], refs[5:]
     rows, lanes = parts[0].shape[1:]
-    size = grads[0].shape[0]
-    total = 0.0
-    for b, by in enumerate(steps):
+    quarter = [g_ref[pl.ds(pl.multiple_of((me_ref[0] ^ r) * rows, rows), rows), :].astype(F32) for r in range(4)]
+    kind = jnp.concatenate([read_marks(ref[0], depth)[0] for ref in parts], axis=0)
+    right = jnp.concatenate(by_expert(kind, jnp.concatenate(quarter, axis=0)), axis=-1)
+    for i, by in enumerate(steps):
         owner = owner_at(me_ref[1], by)
         left = jnp.concatenate([ref[owner] for ref in parts], axis=0)
-        quarter = []
-        for r in range(4):
-            start = (me_ref[0] ^ r) * rows
-            if halves:
-                inner = pl.ds(pl.multiple_of(lax.rem(start, size), rows), rows)
-                quarter.append(jnp.where(start < size, grads[0][inner, :].astype(F32), grads[1][inner, :].astype(F32)))
+        total = contract(left, right, 0, 0)
+        for e in range(2):
+            block = total[:depth, e * PAIR : (e + 1) * PAIR]
+            if outs[0].dtype == BF16:
+                outs[2 * i + e][0] = block.astype(BF16)
             else:
-                quarter.append(grads[b][pl.ds(pl.multiple_of(start, rows), rows), :].astype(F32))
-        kind = left[:, depth : depth + 1].astype(F32)
-        right = jnp.concatenate(by_expert(kind, jnp.concatenate(quarter, axis=0)), axis=-1)
-        total = total + contract(left, right, 0, 0)
-    if not first:
-        total = total + refs[0][...]
-    if not last:
-        refs[-1][...] = total
-        return
-    for e in range(2):
-        refs[-1][e] = total[:depth, e * PAIR : (e + 1) * PAIR]
-
-
-def weight_grad(me, steps, parts, grads, total, depth, last=False, halves=False):
-    rows, lanes = parts[0].shape[1:]
-    before = () if total is None else (total,)
-    return call(
-        functools.partial(weight_kernel, steps, depth, int(halves), total is None, last),
-        me,
-        (*parts, *grads, *before),
-        shaped((2, depth, PAIR) if last else (lanes, 2 * PAIR), F32),
-        3,
-    )
-
-
-def gather_kernel(me_ref, *refs):
-    blocks, whole_ref = refs[: len(STEPS) + 1], refs[-1]
-    for i, block in enumerate(blocks):
-        owner = owner_at(me_ref[1], STEPS[min(i, len(STEPS) - 1)])
-        if i < len(STEPS) - 1:
-            whole_ref[owner] = block[...]
-        else:
-            whole_ref[owner, i - len(STEPS) + 1] = block[0]
-
-
-def gather_blocks(me, blocks, wait=()):
-    out = shaped((len(CYCLE), *blocks[0].shape), blocks[0].dtype)
-    return call(gather_kernel, me, (*blocks, *wait), out, 4, anywhere=len(wait))
+                outs[i][e] = block
+
+
+def shares(me, steps, parts, grad, depth, split):
+    if split:
+        out = [shaped((1, depth, PAIR), BF16)] * (2 * len(steps))
+    else:
+        out = [shaped((2, depth, PAIR), F32)] * len(steps)
+    return call(functools.partial(share_kernel, steps, depth), me, (*parts, grad), out, 1 + len(steps))
 
 
 def in_order(parts, quarters):
@@ -337,14 +345,14 @@
     return jnp.where(kind == 1.0, sums[1], sums[0]).astype(BF16), kind, ids, ids.reshape(1, -1)
 
 
-def weight_plain(quarters, parts, grads, depth):
+def weight_plain(quarters, parts, grad, depth):
     tokens = in_order(parts, quarters)
-    kind = tokens[:, :, depth : depth + 1].astype(F32)
+    kind = tokens[0, :, depth : depth + 1].astype(F32)
     sums = [
-        jnp.einsum("jmk,jmn->kn", tokens[:, :, :depth], g, preferred_element_type=F32)
-        for g in by_expert(kind, grads.astype(F32))
+        jnp.einsum("jmk,mn->jkn", tokens[:, :, :depth], g, preferred_element_type=F32)
+        for g in by_expert(kind, grad.astype(F32))
     ]
-    return jnp.stack(sums)
+    return lax.psum_scatter(jnp.stack(sums), "fsdp", scatter_dimension=1)
 
 
 def per_device(fsdp, seq, tokens, queries, cotangent, modality, block_ids, kv_weight):
@@ -358,10 +366,6 @@
     def swap(x, bit):
         return lax.ppermute(x, "seq", [(i, i ^ bit) for i in range(seq)])
 
-    def over_seq(x):
-        across = swap(x, 2)
-        return [x, swap(x, 1), across, swap(across, 1)]
-
     def turn(x, by):
         return lax.ppermute(x, "fsdp", [(CYCLE[i], CYCLE[(i + by) % fsdp]) for i in range(fsdp)])
 
@@ -371,9 +375,6 @@
     def halves(ups, downs, axis):
         size = ups.shape[axis] // 2
         return lax.slice_in_dim(ups, 0, size, axis=axis), lax.slice_in_dim(downs, size, 2 * size, axis=axis)
-
-    def exchange_columns(x):
-        return lax.all_to_all(x, "fsdp", split_axis=0, concat_axis=0, tiled=True)
 
     me = jnp.stack([me_s, me_f, jnp.int32(0)])
     me_far = jnp.stack([me_s, me_f, jnp.int32(1)])
@@ -387,43 +388,39 @@
 
     blocks = token_blocks(me, tokens, modality, block_ids, fsdp)
     across = swap(blocks, 2)
-    held = (weights[3], weights[4]) if near_link else ()
-    parts = [blocks, swap(blocks, 1), across, swap(after(across, *held), 1)]
+    if near_link:
+        across = after(across, weights[3], weights[4])
+    parts = [blocks, swap(blocks, 1), across, swap(across, 1)]
     own, pack = pack_heads(me, queries, cotangent)
     pack = swap(pack, 1)
 
     if near_link:
-        total = project(me, STEPS[:5], parts, weights[:5], None, depth)
         ups, downs = halves(*weights[5:], 0)
-        weights += both_ways(after(ups, pack, total), after(downs, pack, total))
-        total = project(me, STEPS[5:7], parts, weights[5:7], total, depth)
-        kv, kind, ids, ids_row = project(me, STEPS[7:], parts, weights[7:], total, depth, True, True)
+        weights += both_ways(after(ups, pack), after(downs, pack))
+        before = project(me, STEPS[:5], parts, weights[:5], (), depth)
+        before = project(me, STEPS[5:7], parts, weights[5:7], before, depth)
+        kv, kind, ids, ids_row, weight = project(me, STEPS[7:], parts, weights[7:], before, depth, True, True)
     else:
         kv, kind, ids, ids_row = project_plain(quarters, parts, weight, depth)
     kv_far = swap(kv, 2)
-    columns = exchange_columns(after(blocks, kv))
     far_own, far_other, far = attend(me_far, own, pack, kv_far, ids, ids_row)
     near_own, near_other, near = attend(me, own, pack, kv, ids, ids_row, (far,))
     grad_kv = (near + swap(far, 2)).astype(BF16)
+    attended, grad_queries = place_heads(me, (near_own, swap(near_other, 1), far_own, swap(far_other, 1)))
+
     if near_link:
-        weight = gather_blocks(me, weights, (far,))
-    attended, grad_queries = place_heads(me, (near_own, swap(near_other, 1), far_own, swap(far_other, 1)))
-
-    mine, away = hidden_grad(
-        me, kind, grad_kv, swap(grad_kv, 1), weight, swap(weight, 1), rows, (columns,)
-    )
-    columns = over_seq(after(columns, away))
-    if near_link:
-        first = after(grad_kv, away)
-        grads = [first, *both_ways(first, first)]
-        grads += both_ways(*grads[1:])
-        grads += both_ways(*grads[3:])
-        grads += both_ways(*halves(*grads[5:], 0))
-        total = weight_grad(me, STEPS[:5], columns, grads[:5], None, depth)
-        total = weight_grad(me, STEPS[5:7], columns, grads[5:7], total, depth)
-        grad_weight = weight_grad(me, STEPS[7:], columns, grads[7:], total, depth, True, True)
+        ups, downs = both_ways(*shares(me, STEPS[7:], parts, grad_kv, depth, True))
+        terms = shares(me, STEPS[5:7], parts, grad_kv, depth, False)
+        terms += shares(me, STEPS[:5], parts, grad_kv, depth, False)
+        none = jnp.zeros_like(ups)
+        ups, downs = jnp.concatenate([ups, none]), jnp.concatenate([none, downs])
+        for i in (0, 5, 3):
+            down, up = terms[i : i + 2]
+            ups, downs = both_ways((up + ups.astype(F32)).astype(BF16), (down + downs.astype(F32)).astype(BF16))
+        grad_weight = terms[2] + ups.astype(F32) + downs.astype(F32)
     else:
-        grad_weight = weight_plain(quarters, columns, lax.all_gather(grad_kv, "fsdp", axis=0), depth)
+        grad_weight = weight_plain(quarters, parts, grad_kv, depth)
+    mine, away = hidden_grad(me, kind, grad_kv, swap(grad_kv, 1), weight, swap(weight, 1), rows)
     grad_tokens = (mine + swap(away, 2).astype(F32)).astype(BF16)
     return attended[None], grad_queries[None], grad_tokens[None], grad_weight
 

time: 177 us -> 153 us (0.86)
  waiting for transfers between devices: 86.9 us -> 74.6 us
  starting transfers between devices: 30.3 us -> 22.5 us
  local copies, waits for them, and re-layouts: 20.5 us -> 16.5 us
    ppermute x14 -> x11, waiting for transfers between devices: 43.8 us -> 25.6 us  [swap(): return lax.ppermute(x, 'seq', [(i, i ^ bit) for i in range(seq)])]
    ppermute x16, waiting for transfers between devices: 32.5 us -> 49 us  [turn(): lax.ppermute(x, 'fsdp', [(CYCLE[i], CYCLE[(i + by) % fsdp]) for i in rang...]
    all_to_all x1 -> x0, waiting for transfers between devices: 10.6 us -> none  [exchange_columns(): return lax.all_to_all(x, 'fsdp', split_axis=0, concat_axis=0, tiled=True)]
    all_to_all x1 -> x0, starting transfers between devices: 5.22 us -> none  [exchange_columns(): return lax.all_to_all(x, 'fsdp', split_axis=0, concat_axis=0, tiled=True)]
    unnamed x105 -> x40, local copies, waits for them, and re-layouts: 19.1 us -> 14.2 us
    ppermute x14 -> x11, starting transfers between devices: 8.78 us -> 5.82 us  [swap(): return lax.ppermute(x, 'seq', [(i, i ^ bit) for i in range(seq)])]
    pallas_call x13 -> x12, Pallas kernels: 35.2 us -> 35 us  [call(): pl.pallas_call(body, in_specs=[pl.BlockSpec(memory_space=pltpu.SMEM)] + [...]
  transfers between devices with their start and end apart: 31 -> 27, of which waited for: 12 -> 13; matrix products, arithmetic and copies ran while one was open for 3% -> 3% of each run, Pallas kernels for 9% -> 21%
where the time goes in v6:
time: 153 us; the launch traced here: 152 us
  waiting for transfers between devices  74.6 us (49%)
  Pallas kernels  35 us (23%)
  starting transfers between devices  22.5 us (15%)
  local copies, waits for them, and re-layouts  16.5 us (11%)
  other arithmetic  2.93 us (2%)
    ppermute x16, waiting for transfers between devices, turn(): lax.ppermute(x, 'fsdp', [(CYCLE[i], CYCLE[(i + by) % fsdp]) for i in rang...  49 us
    pallas_call x12, Pallas kernels, call(): pl.pallas_call(body, in_specs=[pl.BlockSpec(memory_space=pltpu.SMEM)] + [...  35 us
    ppermute x11, waiting for transfers between devices, swap(): return lax.ppermute(x, 'seq', [(i, i ^ bit) for i in range(seq)])  25.6 us
    ppermute x16, starting transfers between devices, turn(): lax.ppermute(x, 'fsdp', [(CYCLE[i], CYCLE[(i + by) % fsdp]) for i in rang...  16.7 us
    unnamed x40, local copies, waits for them, and re-layouts  14.2 us
    ppermute x11, starting transfers between devices, swap(): return lax.ppermute(x, 'seq', [(i, i ^ bit) for i in range(seq)])  5.82 us
  transfers between devices with their start and end apart: 27, of which 13 were waited for; matrix products, arithmetic and copies ran while one was open for 3% of the time, Pallas kernels for 21%

profile of v6, /device:TPU:0, one launch (start us, length us, event | category | flops | bytes accessed | tf_op | source)
XLA Modules:
  0.0 152.4 jit_solution(5932665155103409200)
XLA Ops:
  0.7 1.2 copy-done.10
  3.2 1.2 shard_map.94.refs_0_
  4.4 3.0 %collective-permute-start.2 = (bf16[8,128,512]{2,1,0:T(8,128)(2,1)S(1)}, bf16[8,128,512]{2,1,0:T(8,128)(2,1)S(1)}, u32[]{:S(2)}, u32[]{:S(2)}) collective-permute-start(bf16[8,128,512]{2,1,0:T(8,128)(2,1)S(1)} %shard_map.94.refs_0_), channel_id=1, source_target_pairs={{0,2},{1,3},{2,0},{3,1},{4,6},{5,7},{6,4},{7,5},{8,10},{9,11},{10,... | collective-permute-start | bytes 3145736 | tf_op jit(solution)/shard_map/ppermute | solution.py:367
  7.4 1.6 %collective-permute-start.3 = (bf16[2,448,256]{2,1,0:T(8,128)(2,1)}, bf16[2,448,256]{2,1,0:T(8,128)(2,1)S(1)}, u32[]{:S(2)}, u32[]{:S(2)}) collective-permute-start(bf16[2,448,256]{2,1,0:T(8,128)(2,1)} %refs_4_.1), channel_id=1, source_target_pairs={{0,8},{8,16},{16,24},{24,28},{28,20},{20,12},{12,4},{4,0},{1,9},{9... | collective-permute-start | bytes 1376264 | tf_op jit(solution)/shard_map/ppermute | solution.py:370
  9.4 10.2 %collective-permute-done.3.refs_5_ = bf16[2,448,256]{2,1,0:T(8,128)(2,1)S(1)} collective-permute-done((bf16[2,448,256]{2,1,0:T(8,128)(2,1)}, bf16[2,448,256]{2,1,0:T(8,128)(2,1)S(1)}, u32[]{:S(2)}, u32[]{:S(2)}) %collective-permute-start.3) | collective-permute-done | bytes 458784 | tf_op jit(solution)/shard_map/ppermute | solution.py:370
  19.6 1.6 %collective-permute-start.4 = (bf16[2,448,256]{2,1,0:T(8,128)(2,1)S(1)}, bf16[2,448,256]{2,1,0:T(8,128)(2,1)S(1)}, u32[]{:S(2)}, u32[]{:S(2)}) collective-permute-start(bf16[2,448,256]{2,1,0:T(8,128)(2,1)S(1)} %collective-permute-done.3.refs_5_), channel_id=1, source_target_pairs={{0,8},{8,16},{16,24},{24,28},{28,20},{20,12},{12,4},{4,0},{1,9},{9... | collective-permute-start | bytes 1376264 | tf_op jit(solution)/shard_map/ppermute | solution.py:370
  21.6 1.2 copy-done.11
  22.8 1.2 copy-done.12
  24.0 1.7 %shard_map.93 = (bf16[2,2,128,896]{3,2,1,0:T(8,128)(2,1)S(1)}, bf16[2,2,128,896]{3,2,1,0:T(8,128)(2,1)}) custom-call(s32[3]{0:T(128)S(1)} %pad_add_fusion.me_ref, bf16[128,3584]{1,0:T(8,128)(2,1)S(1)} %bitcast.10, bf16[128,3584]{1,0:T(8,128)(2,1)S(1)} %bitcast.11), custom_call_target="tpu_custom_call" | custom-call | bytes 6000000 | tf_op jit(solution)/shard_map/pallas_call | solution.py:36
  25.7 0.9 copy-done.2
  27.2 3.5 %collective-permute-done.4.refs_1_.refs_7_ = bf16[2,448,256]{2,1,0:T(8,128)(2,1)S(1)} collective-permute-done((bf16[2,448,256]{2,1,0:T(8,128)(2,1)S(1)}, bf16[2,448,256]{2,1,0:T(8,128)(2,1)S(1)}, u32[]{:S(2)}, u32[]{:S(2)}) %collective-permute-start.4) | collective-permute-done | bytes 458784 | tf_op jit(solution)/shard_map/ppermute | solution.py:370
  32.8 1.0 copy-done
  33.7 1.0 collective-permute-start.10
  34.7 1.1 collective-permute-start.8
  35.8 11.1 %collective-permute-done.10.refs_5_ = bf16[2,448,256]{2,1,0:T(8,128)(2,1)S(1)} collective-permute-done((bf16[2,448,256]{2,1,0:T(8,128)(2,1)}, bf16[2,448,256]{2,1,0:T(8,128)(2,1)S(1)}, u32[]{:S(2)}, u32[]{:S(2)}) %collective-permute-start.10) | collective-permute-done | bytes 458784 | tf_op jit(solution)/shard_map/ppermute | solution.py:370
  48.4 1.0 collective-permute-start.11
  49.4 1.6 %slice.8.refs_0_ = bf16[1,448,256]{2,1,0:T(8,128)(2,1)} slice(bf16[2,448,256]{2,1,0:T(8,128)(2,1)} %collective-permute-done.8.refs_4_), slice={[0:1], [0:448], [0:256]} | slice | bytes 458752 | tf_op jit(solution)/shard_map/slice | solution.py:377
  51.0 1.1 collective-permute-start.9
  52.1 1.0 copy-done.5
  53.1 1.0 copy-done.7
  54.1 1.0 copy-done.13
  55.1 1.0 copy-done.15
  56.1 1.0 copy-done.17
  57.2 4.2 %shard_map.98 = (f32[512,512]{1,0:T(8,128)S(1)}, bf16[8,2,448,256]{3,2,1,0:T(8,128)(2,1)S(1)}) custom-call(s32[3]{0:T(128)S(1)} %pad_add_fusion.me_ref, bf16[8,128,512]{2,1,0:T(8,128)(2,1)S(1)} %shard_map.94.refs_0_, bf16[8,128,512]{2,1,0:T(8,128)(2,1)S(1)} %collective-permute-done.1.refs_1_, bf16[8,128,512]{2,1,0:T(8,128)(2,1)S(1)} %copy-done.1, ...), custom_call_target="tpu_custom_call" | custom-call | bytes 9000000 | tf_op jit(solution)/shard_map/pallas_call | solution.py:36
  61.4 2.6 %shard_map.99 = (f32[512,512]{1,0:T(8,128)S(1)}, bf16[8,2,448,256]{3,2,1,0:T(8,128)(2,1)S(1)}) custom-call(s32[3]{0:T(128)S(1)} %pad_add_fusion.me_ref, bf16[8,128,512]{2,1,0:T(8,128)(2,1)S(1)} %shard_map.94.refs_0_, bf16[8,128,512]{2,1,0:T(8,128)(2,1)S(1)} %collective-permute-done.1.refs_1_, ...), custom_call_target="tpu_custom_call", output_to_operand_aliasing={{1}: (8, {})} | custom-call | bytes 9000000 | tf_op jit(solution)/shard_map/pallas_call | solution.py:36
  64.1 2.5 %shard_map.100 = (bf16[512,256]{1,0:T(8,128)(2,1)S(1)}, f32[512,1]{1,0:T(8,128)S(1)}, f32[512,1]{1,0:T(8,128)S(1)}, f32[1,512]{1,0:T(1,128)S(1)}, bf16[8,2,448,256]{3,2,1,0:T(8,128)(2,1)S(1)}) custom-call(s32[3]{0:T(128)S(1)} %pad_add_fusion.me_ref, bf16[8,128,512]{2,1,0:T(8,128)(2,1)S(1)} %shard_map.94.refs_0_, ...), custom_call_target="tpu_custom_call", output_to_operand_aliasing={{4}: (8, {})} | custom-call | bytes 9000000 | tf_op jit(solution)/shard_map/pallas_call | solution.py:36
  67.4 8.1 %collective-permute-done.12.kv_ref = bf16[512,256]{1,0:T(8,128)(2,1)S(1)} collective-permute-done((bf16[512,256]{1,0:T(8,128)(2,1)S(1)}, bf16[512,256]{1,0:T(8,128)(2,1)S(1)}, u32[]{:S(2)}, u32[]{:S(2)}) %collective-permute-start.12) | collective-permute-done | bytes 262176 | tf_op jit(solution)/shard_map/ppermute | solution.py:367
  75.5 5.3 %shard_map.101 = (bf16[2,128,896]{2,1,0:T(8,128)(2,1)S(1)}, bf16[2,128,896]{2,1,0:T(8,128)(2,1)S(1)}, f32[512,256]{1,0:T(8,128)S(1)}) custom-call(s32[3]{0:T(128)S(1)} %pad_add_fusion.2.me_ref, bf16[2,2,128,896]{3,2,1,0:T(8,128)(2,1)S(1)} %copy-done.3, bf16[2,2,128,896]{3,2,1,0:T(8,128)(2,1)} %collective-permute-done.refs_1_.pack_ref, ...), custom_call_target="tpu_custom_call" | custom-call | bytes 18000000 | tf_op jit(solution)/shard_map/pallas_call | solution.py:36
  81.3 5.3 %shard_map.102 = (bf16[2,128,896]{2,1,0:T(8,128)(2,1)S(1)}, bf16[2,128,896]{2,1,0:T(8,128)(2,1)S(1)}, f32[512,256]{1,0:T(8,128)S(1)}) custom-call(s32[3]{0:T(128)S(1)} %pad_add_fusion.me_ref, bf16[2,2,128,896]{3,2,1,0:T(8,128)(2,1)S(1)} %copy-done.3, bf16[2,2,128,896]{3,2,1,0:T(8,128)(2,1)} %collective-permute-done.refs_1_.pack_ref, ...), custom_call_target="tpu_custom_call" | custom-call | bytes 18000000 | tf_op jit(solution)/shard_map/pallas_call | solution.py:36
  86.7 7.7 %collective-permute-done.15 = f32[512,256]{1,0:T(8,128)S(1)} collective-permute-done((f32[512,256]{1,0:T(8,128)S(1)}, f32[512,256]{1,0:T(8,128)S(1)}, u32[]{:S(2)}, u32[]{:S(2)}) %collective-permute-start.15) | collective-permute-done | bytes 524320 | tf_op jit(solution)/shard_map/ppermute | solution.py:367
  94.4 1.9 %shard_map.107 = (bf16[1,448,256]{2,1,0:T(8,128)(2,1)S(1)}, bf16[1,448,256]{2,1,0:T(8,128)(2,1)S(1)}) custom-call(s32[3]{0:T(128)S(1)} %pad_add_fusion.me_ref, bf16[8,128,512]{2,1,0:T(8,128)(2,1)S(1)} %shard_map.94.refs_0_, bf16[8,128,512]{2,1,0:T(8,128)(2,1)S(1)} %collective-permute-done.1.refs_1_, bf16[8,128,512]{2,1,0:T(8,128)(2,1)S(1)} %copy-done.1, ...), custom_call_target="tpu_custom_call" | custom-call | bytes 6000000 | tf_op jit(solution)/shard_map/pallas_call | solution.py:36
  96.4 1.6 %collective-permute-start.19 = (bf16[1,448,256]{2,1,0:T(8,128)(2,1)S(1)}, bf16[1,448,256]{2,1,0:T(8,128)(2,1)S(1)}, u32[]{:S(2)}, u32[]{:S(2)}) collective-permute-start(bf16[1,448,256]{2,1,0:T(8,128)(2,1)S(1)} %get-tuple-element.59), channel_id=1, source_target_pairs={{0,8},{8,16},{16,24},{24,28},{28,20},{20,12},{12,4},{4,0},{1,9},{9... | collective-permute-start | bytes 688136 | tf_op jit(solution)/shard_map/ppermute | solution.py:370
  98.4 2.2 %shard_map.106 = (f32[2,448,256]{2,1,0:T(8,128)S(1)}, f32[2,448,256]{2,1,0:T(8,128)S(1)}) custom-call(s32[3]{0:T(128)S(1)} %pad_add_fusion.me_ref, bf16[8,128,512]{2,1,0:T(8,128)(2,1)S(1)} %shard_map.94.refs_0_, bf16[8,128,512]{2,1,0:T(8,128)(2,1)S(1)} %collective-permute-done.1.refs_1_, bf16[8,128,512]{2,1,0:T(8,128)(2,1)S(1)} %copy-done.1, ...), custom_call_target="tpu_custom_call" | custom-call | bytes 9000000 | tf_op jit(solution)/shard_map/pallas_call | solution.py:36
  100.7 2.0 %collective-permute-done.19 = bf16[1,448,256]{2,1,0:T(8,128)(2,1)S(1)} collective-permute-done((bf16[1,448,256]{2,1,0:T(8,128)(2,1)S(1)}, bf16[1,448,256]{2,1,0:T(8,128)(2,1)S(1)}, u32[]{:S(2)}, u32[]{:S(2)}) %collective-permute-start.19) | collective-permute-done | bytes 229408 | tf_op jit(solution)/shard_map/ppermute | solution.py:370
  102.8 1.8 %collective-permute-start.20 = (bf16[2,448,256]{2,1,0:T(8,128)(2,1)S(1)}, bf16[2,448,256]{2,1,0:T(8,128)(2,1)S(1)}, u32[]{:S(2)}, u32[]{:S(2)}) collective-permute-start(bf16[2,448,256]{2,1,0:T(8,128)(2,1)S(1)} %add_convert_fusion.6), channel_id=1, source_target_pairs={{0,8},{8,16},{16,24},{24,28},{28,20},{20,12},{12,4},{4,0},{1,9},{9... | collective-permute-start | bytes 1376264 | tf_op jit(solution)/shard_map/ppermute | solution.py:370
  105.1 3.0 %shard_map.105 = (f32[2,448,256]{2,1,0:T(8,128)S(1)}, f32[2,448,256]{2,1,0:T(8,128)S(1)}, f32[2,448,256]{2,1,0:T(8,128)S(1)}, f32[2,448,256]{2,1,0:T(8,128)S(1)}, f32[2,448,256]{2,1,0:T(8,128)S(1)}) custom-call(s32[3]{0:T(128)S(1)} %pad_add_fusion.me_ref, bf16[8,128,512]{2,1,0:T(8,128)(2,1)S(1)} %shard_map.94.refs_0_, ...), custom_call_target="tpu_custom_call" | custom-call | bytes 18000000 | tf_op jit(solution)/shard_map/pallas_call | solution.py:36
  108.2 5.3 %collective-permute-done.20 = bf16[2,448,256]{2,1,0:T(8,128)(2,1)S(1)} collective-permute-done((bf16[2,448,256]{2,1,0:T(8,128)(2,1)S(1)}, bf16[2,448,256]{2,1,0:T(8,128)(2,1)S(1)}, u32[]{:S(2)}, u32[]{:S(2)}) %collective-permute-start.20) | collective-permute-done | bytes 458784 | tf_op jit(solution)/shard_map/ppermute | solution.py:370
  113.6 1.6 %collective-permute-start.21 = (bf16[2,448,256]{2,1,0:T(8,128)(2,1)S(1)}, bf16[2,448,256]{2,1,0:T(8,128)(2,1)S(1)}, u32[]{:S(2)}, u32[]{:S(2)}) collective-permute-start(bf16[2,448,256]{2,1,0:T(8,128)(2,1)S(1)} %add_convert_fusion.5), channel_id=1, source_target_pairs={{0,8},{8,16},{16,24},{24,28},{28,20},{20,12},{12,4},{4,0},{1,9},{9... | collective-permute-start | bytes 1376264 | tf_op jit(solution)/shard_map/ppermute | solution.py:370
  116.4 6.7 %collective-permute-done.21 = bf16[2,448,256]{2,1,0:T(8,128)(2,1)S(1)} collective-permute-done((bf16[2,448,256]{2,1,0:T(8,128)(2,1)S(1)}, bf16[2,448,256]{2,1,0:T(8,128)(2,1)S(1)}, u32[]{:S(2)}, u32[]{:S(2)}) %collective-permute-start.21) | collective-permute-done | bytes 458784 | tf_op jit(solution)/shard_map/ppermute | solution.py:370
  123.2 1.4 collective-permute-done.16.gc_ref
  124.6 1.6 %collective-permute-start.22 = (bf16[2,448,256]{2,1,0:T(8,128)(2,1)S(1)}, bf16[2,448,256]{2,1,0:T(8,128)(2,1)S(1)}, u32[]{:S(2)}, u32[]{:S(2)}) collective-permute-start(bf16[2,448,256]{2,1,0:T(8,128)(2,1)S(1)} %add_convert_fusion.4), channel_id=1, source_target_pairs={{0,8},{8,16},{16,24},{24,28},{28,20},{20,12},{12,4},{4,0},{1,9},{9... | collective-permute-start | bytes 1376264 | tf_op jit(solution)/shard_map/ppermute | solution.py:370
  126.2 2.9 %shard_map.104 = (f32[128,3584]{1,0:T(8,128)S(1)}, bf16[128,3584]{1,0:T(8,128)(2,1)S(1)}) custom-call(s32[3]{0:T(128)S(1)} %pad_add_fusion.me_ref, f32[512,1]{1,0:T(8,128)S(1)} %get-tuple-element.50.kind_ref, bf16[512,256]{1,0:T(8,128)(2,1)S(1)} %add_convert_fusion.7.g_ref.refs_4_, bf16[512,256]{1,0:T(8,128)(2,1)S(1)} %collective-permute-done.16.gc_ref, ...), custom_call_target="tpu_custom_call" | custom-call | bytes 21000000 | tf_op jit(solution)/shard_map/pallas_call | solution.py:36
  130.3 1.9 %shard_map.103 = (bf16[128,3584]{1,0:T(8,128)(2,1)}, bf16[128,3584]{1,0:T(8,128)(2,1)}) custom-call(s32[3]{0:T(128)S(1)} %pad_add_fusion.me_ref, bf16[2,128,896]{2,1,0:T(8,128)(2,1)S(1)} %get-tuple-element.44.refs_0_, bf16[2,128,896]{2,1,0:T(8,128)(2,1)S(1)} %collective-permute-done.13.refs_1_, bf16[2,128,896]{2,1,0:T(8,128)(2,1)S(1)} %get-tuple-element.46.refs_2_, ...), custom_call_target="tpu_custom_call" | custom-call | bytes 9000000 | tf_op jit(solution)/shard_map/pallas_call | solution.py:36
  132.2 5.0 %collective-permute-done.22 = bf16[2,448,256]{2,1,0:T(8,128)(2,1)S(1)} collective-permute-done((bf16[2,448,256]{2,1,0:T(8,128)(2,1)S(1)}, bf16[2,448,256]{2,1,0:T(8,128)(2,1)S(1)}, u32[]{:S(2)}, u32[]{:S(2)}) %collective-permute-start.22) | collective-permute-done | bytes 458784 | tf_op jit(solution)/shard_map/ppermute | solution.py:370
  137.2 4.7 %collective-permute-done.26 = bf16[2,448,256]{2,1,0:T(8,128)(2,1)S(1)} collective-permute-done((bf16[2,448,256]{2,1,0:T(8,128)(2,1)S(1)}, bf16[2,448,256]{2,1,0:T(8,128)(2,1)S(1)}, u32[]{:S(2)}, u32[]{:S(2)}) %collective-permute-start.26) | collective-permute-done | bytes 458784 | tf_op jit(solution)/shard_map/ppermute | solution.py:370
  141.9 1.0 convert_add_fusion
  142.9 8.4 %collective-permute-done.18 = bf16[128,3584]{1,0:T(8,128)(2,1)S(1)} collective-permute-done((bf16[128,3584]{1,0:T(8,128)(2,1)S(1)}, bf16[128,3584]{1,0:T(8,128)(2,1)S(1)}, u32[]{:S(2)}, u32[]{:S(2)}) %collective-permute-start.18) | collective-permute-done | bytes 917536 | tf_op jit(solution)/shard_map/ppermute | solution.py:367
  151.3 1.1 fusion
  (74 shorter events, 11.4 us)
Async XLA Ops:
  0.7 1.2 copy-start.10
  1.9 0.7 copy-start.18
  2.5 0.7 copy-start.19
  4.4 28.4 %collective-permute-start.2 = (bf16[8,128,512]{2,1,0:T(8,128)(2,1)S(1)}, bf16[8,128,512]{2,1,0:T(8,128)(2,1)S(1)}, u32[]{:S(2)}, u32[]{:S(2)}) collective-permute-start(bf16[8,128,512]{2,1,0:T(8,128)(2,1)S(1)} %shard_map.94.refs_0_), channel_id=1, source_target_pairs={{0,2},{1,3},{2,0},{3,1},{4,6},{5,7},{6,4},{7,5},{8,10},{9,11},{10,... | collective-permute-start | bytes 3145736 | tf_op jit(solution)/shard_map/ppermute | solution.py:367
  7.4 12.2 %collective-permute-start.3 = (bf16[2,448,256]{2,1,0:T(8,128)(2,1)}, bf16[2,448,256]{2,1,0:T(8,128)(2,1)S(1)}, u32[]{:S(2)}, u32[]{:S(2)}) collective-permute-start(bf16[2,448,256]{2,1,0:T(8,128)(2,1)} %refs_4_.1), channel_id=1, source_target_pairs={{0,8},{8,16},{16,24},{24,28},{28,20},{20,12},{12,4},{4,0},{1,9},{9... | collective-permute-start | bytes 1376264 | tf_op jit(solution)/shard_map/ppermute | solution.py:370
  9.0 12.2 %collective-permute-start.5 = (bf16[2,448,256]{2,1,0:T(8,128)(2,1)}, bf16[2,448,256]{2,1,0:T(8,128)(2,1)S(1)}, u32[]{:S(2)}, u32[]{:S(2)}) collective-permute-start(bf16[2,448,256]{2,1,0:T(8,128)(2,1)} %refs_4_.1), channel_id=1, source_target_pairs={{0,4},{8,0},{16,8},{24,16},{28,24},{20,28},{12,20},{4,12},{1,5},{9... | collective-permute-start | bytes 1376264 | tf_op jit(solution)/shard_map/ppermute | solution.py:370
  19.6 12.4 %copy-start.14 = (bf16[2,448,256]{2,1,0:T(8,128)(2,1)}, bf16[2,448,256]{2,1,0:T(8,128)(2,1)S(1)}, u32[]{:S(2)}) copy-start(bf16[2,448,256]{2,1,0:T(8,128)(2,1)S(1)} %collective-permute-done.3.refs_5_) | copy-start | bytes 1376260
  19.6 11.1 %collective-permute-start.4 = (bf16[2,448,256]{2,1,0:T(8,128)(2,1)S(1)}, bf16[2,448,256]{2,1,0:T(8,128)(2,1)S(1)}, u32[]{:S(2)}, u32[]{:S(2)}) collective-permute-start(bf16[2,448,256]{2,1,0:T(8,128)(2,1)S(1)} %collective-permute-done.3.refs_5_), channel_id=1, source_target_pairs={{0,8},{8,16},{16,24},{24,28},{28,20},{20,12},{12,4},{4,0},{1,9},{9... | collective-permute-start | bytes 1376264 | tf_op jit(solution)/shard_map/ppermute | solution.py:370
  21.2 10.8 %copy-start.16 = (bf16[2,448,256]{2,1,0:T(8,128)(2,1)}, bf16[2,448,256]{2,1,0:T(8,128)(2,1)S(1)}, u32[]{:S(2)}) copy-start(bf16[2,448,256]{2,1,0:T(8,128)(2,1)S(1)} %collective-permute-done.5.refs_6_) | copy-start | bytes 1376260
  21.2 10.8 %collective-permute-start.6 = (bf16[2,448,256]{2,1,0:T(8,128)(2,1)S(1)}, bf16[2,448,256]{2,1,0:T(8,128)(2,1)S(1)}, u32[]{:S(2)}, u32[]{:S(2)}) collective-permute-start(bf16[2,448,256]{2,1,0:T(8,128)(2,1)S(1)} %collective-permute-done.5.refs_6_), channel_id=1, source_target_pairs={{0,4},{8,0},{16,8},{24,16},{28,24},{20,28},{12,20},{4,12},{1,5},{9... | collective-permute-start | bytes 1376264 | tf_op jit(solution)/shard_map/ppermute | solution.py:370
  21.6 1.2 copy-start.11
  22.8 1.2 copy-start.12
  25.7 0.9 copy-start.2
  26.7 21.7 %collective-permute-start = (bf16[2,2,128,896]{3,2,1,0:T(8,128)(2,1)}, bf16[2,2,128,896]{3,2,1,0:T(8,128)(2,1)}, u32[]{:S(2)}, u32[]{:S(2)}) collective-permute-start(bf16[2,2,128,896]{3,2,1,0:T(8,128)(2,1)} %get-tuple-element.35), channel_id=1, source_target_pairs={{0,1},{1,0},{2,3},{3,2},{4,5},{5,4},{6,7},{7,6},{8,9},{9,8},{10,11... | collective-permute-start | bytes 2752520 | tf_op jit(solution)/shard_map/ppermute | solution.py:367
  26.7 25.4 %collective-permute-start.1 = (bf16[8,128,512]{2,1,0:T(8,128)(2,1)S(1)}, bf16[8,128,512]{2,1,0:T(8,128)(2,1)S(1)}, u32[]{:S(2)}, u32[]{:S(2)}) collective-permute-start(bf16[8,128,512]{2,1,0:T(8,128)(2,1)S(1)} %shard_map.94.refs_0_), channel_id=1, source_target_pairs={{0,1},{1,0},{2,3},{3,2},{4,5},{5,4},{6,7},{7,6},{8,9},{9,8},{10,11... | collective-permute-start | bytes 3145736 | tf_op jit(solution)/shard_map/ppermute | solution.py:367
  30.7 0.8 copy-start.4
  32.0 0.8 copy-start.6
  32.7 1.0 copy-start
  33.7 18.3 %copy-start.1 = (bf16[8,128,512]{2,1,0:T(8,128)(2,1)S(1)}, bf16[8,128,512]{2,1,0:T(8,128)(2,1)}, u32[]{:S(2)}) copy-start(bf16[8,128,512]{2,1,0:T(8,128)(2,1)} %shard_map.95.refs_2_) | copy-start | bytes 3145732
  33.7 18.3 %collective-permute-start.7 = (bf16[8,128,512]{2,1,0:T(8,128)(2,1)}, bf16[8,128,512]{2,1,0:T(8,128)(2,1)}, u32[]{:S(2)}, u32[]{:S(2)}) collective-permute-start(bf16[8,128,512]{2,1,0:T(8,128)(2,1)} %shard_map.95.refs_2_), channel_id=1, source_target_pairs={{0,1},{1,0},{2,3},{3,2},{4,5},{5,4},{6,7},{7,6},{8,9},{9,8},{10,11... | collective-permute-start | bytes 3145736 | tf_op jit(solution)/shard_map/ppermute | solution.py:367
  33.7 13.1 %collective-permute-start.10 = (bf16[2,448,256]{2,1,0:T(8,128)(2,1)}, bf16[2,448,256]{2,1,0:T(8,128)(2,1)S(1)}, u32[]{:S(2)}, u32[]{:S(2)}) collective-permute-start(bf16[2,448,256]{2,1,0:T(8,128)(2,1)} %copy-done.6), channel_id=1, source_target_pairs={{0,4},{8,0},{16,8},{24,16},{28,24},{20,28},{12,20},{4,12},{1,5},{9... | collective-permute-start | bytes 1376264 | tf_op jit(solution)/shard_map/ppermute | solution.py:370
  34.7 14.7 %collective-permute-start.8 = (bf16[2,448,256]{2,1,0:T(8,128)(2,1)}, bf16[2,448,256]{2,1,0:T(8,128)(2,1)}, u32[]{:S(2)}, u32[]{:S(2)}) collective-permute-start(bf16[2,448,256]{2,1,0:T(8,128)(2,1)} %copy-done.4), channel_id=1, source_target_pairs={{0,8},{8,16},{16,24},{24,28},{28,20},{20,12},{12,4},{4,0},{1,9},{9... | collective-permute-start | bytes 1376264 | tf_op jit(solution)/shard_map/ppermute | solution.py:370
  47.6 0.8 copy-start.8
  48.4 15.7 %collective-permute-start.11 = (bf16[1,448,256]{2,1,0:T(8,128)(2,1)}, bf16[1,448,256]{2,1,0:T(8,128)(2,1)S(1)}, u32[]{:S(2)}, u32[]{:S(2)}) collective-permute-start(bf16[1,448,256]{2,1,0:T(8,128)(2,1)} %shard_map.97), channel_id=1, source_target_pairs={{0,4},{8,0},{16,8},{24,16},{28,24},{20,28},{12,20},{4,12},{1,5},{9... | collective-permute-start | bytes 688136 | tf_op jit(solution)/shard_map/ppermute | solution.py:370
  51.0 13.1 %collective-permute-start.9 = (bf16[1,448,256]{2,1,0:T(8,128)(2,1)}, bf16[1,448,256]{2,1,0:T(8,128)(2,1)S(1)}, u32[]{:S(2)}, u32[]{:S(2)}) collective-permute-start(bf16[1,448,256]{2,1,0:T(8,128)(2,1)} %shard_map.96), channel_id=1, source_target_pairs={{0,8},{8,16},{16,24},{24,28},{28,20},{20,12},{12,4},{4,0},{1,9},{9... | collective-permute-start | bytes 688136 | tf_op jit(solution)/shard_map/ppermute | solution.py:370
  52.1 1.0 copy-start.5
  53.1 1.0 copy-start.7
  54.1 1.0 copy-start.13
  55.1 1.0 copy-start.15
  56.1 1.0 copy-start.17
  57.2 4.2 %copy-start.9 = (bf16[2,448,256]{2,1,0:T(8,128)(2,1)S(1)}, bf16[2,448,256]{2,1,0:T(8,128)(2,1)}, u32[]{:S(2)}) copy-start(bf16[2,448,256]{2,1,0:T(8,128)(2,1)} %copy-done.8) | copy-start | bytes 1376260
  64.1 11.4 %copy-start.3 = (bf16[2,2,128,896]{3,2,1,0:T(8,128)(2,1)S(1)}, bf16[2,2,128,896]{3,2,1,0:T(8,128)(2,1)}, u32[]{:S(2)}) copy-start(bf16[2,2,128,896]{3,2,1,0:T(8,128)(2,1)} %copy-done.2) | copy-start | bytes 2752516
  66.7 59.5 %collective-permute-start.17 = (bf16[8,2,448,256]{3,2,1,0:T(8,128)(2,1)S(1)}, bf16[8,2,448,256]{3,2,1,0:T(8,128)(2,1)S(1)}, u32[]{:S(2)}, u32[]{:S(2)}) collective-permute-start(bf16[8,2,448,256]{3,2,1,0:T(8,128)(2,1)S(1)} %get-tuple-element.52.w_ref), channel_id=1, source_target_pairs={{0,1},{1,0},{2,3},{3,2},{4,5},{5,4},{6,7},{7,6},{8,9},{9,8},{10,11... | collective-permute-start | bytes 11010056 | tf_op jit(solution)/shard_map/ppermute | solution.py:367
  66.7 8.7 %collective-permute-start.12 = (bf16[512,256]{1,0:T(8,128)(2,1)S(1)}, bf16[512,256]{1,0:T(8,128)(2,1)S(1)}, u32[]{:S(2)}, u32[]{:S(2)}) collective-permute-start(bf16[512,256]{1,0:T(8,128)(2,1)S(1)} %get-tuple-element.40.kv_ref), channel_id=1, source_target_pairs={{0,2},{1,3},{2,0},{3,1},{4,6},{5,7},{6,4},{7,5},{8,10},{9,11},{10,... | collective-permute-start | bytes 786440 | tf_op jit(solution)/shard_map/ppermute | solution.py:367
  80.8 13.6 %collective-permute-start.15 = (f32[512,256]{1,0:T(8,128)S(1)}, f32[512,256]{1,0:T(8,128)S(1)}, u32[]{:S(2)}, u32[]{:S(2)}) collective-permute-start(f32[512,256]{1,0:T(8,128)S(1)} %get-tuple-element.43.refs_0_), channel_id=1, source_target_pairs={{0,2},{1,3},{2,0},{3,1},{4,6},{5,7},{6,4},{7,5},{8,10},{9,11},{10,... | collective-permute-start | bytes 1572872 | tf_op jit(solution)/shard_map/ppermute | solution.py:367
  96.4 6.3 %collective-permute-start.19 = (bf16[1,448,256]{2,1,0:T(8,128)(2,1)S(1)}, bf16[1,448,256]{2,1,0:T(8,128)(2,1)S(1)}, u32[]{:S(2)}, u32[]{:S(2)}) collective-permute-start(bf16[1,448,256]{2,1,0:T(8,128)(2,1)S(1)} %get-tuple-element.59), channel_id=1, source_target_pairs={{0,8},{8,16},{16,24},{24,28},{28,20},{20,12},{12,4},{4,0},{1,9},{9... | collective-permute-start | bytes 688136 | tf_op jit(solution)/shard_map/ppermute | solution.py:370
  98.0 6.6 %collective-permute-start.23 = (bf16[1,448,256]{2,1,0:T(8,128)(2,1)S(1)}, bf16[1,448,256]{2,1,0:T(8,128)(2,1)S(1)}, u32[]{:S(2)}, u32[]{:S(2)}) collective-permute-start(bf16[1,448,256]{2,1,0:T(8,128)(2,1)S(1)} %get-tuple-element.63), channel_id=1, source_target_pairs={{0,4},{8,0},{16,8},{24,16},{28,24},{20,28},{12,20},{4,12},{1,5},{9... | collective-permute-start | bytes 688136 | tf_op jit(solution)/shard_map/ppermute | solution.py:370
  102.8 10.7 %collective-permute-start.20 = (bf16[2,448,256]{2,1,0:T(8,128)(2,1)S(1)}, bf16[2,448,256]{2,1,0:T(8,128)(2,1)S(1)}, u32[]{:S(2)}, u32[]{:S(2)}) collective-permute-start(bf16[2,448,256]{2,1,0:T(8,128)(2,1)S(1)} %add_convert_fusion.6), channel_id=1, source_target_pairs={{0,8},{8,16},{16,24},{24,28},{28,20},{20,12},{12,4},{4,0},{1,9},{9... | collective-permute-start | bytes 1376264 | tf_op jit(solution)/shard_map/ppermute | solution.py:370
  104.6 10.6 %collective-permute-start.24 = (bf16[2,448,256]{2,1,0:T(8,128)(2,1)S(1)}, bf16[2,448,256]{2,1,0:T(8,128)(2,1)S(1)}, u32[]{:S(2)}, u32[]{:S(2)}) collective-permute-start(bf16[2,448,256]{2,1,0:T(8,128)(2,1)S(1)} %add_convert_fusion.3), channel_id=1, source_target_pairs={{0,4},{8,0},{16,8},{24,16},{28,24},{20,28},{12,20},{4,12},{1,5},{9... | collective-permute-start | bytes 1376264 | tf_op jit(solution)/shard_map/ppermute | solution.py:370
  113.6 9.5 %collective-permute-start.21 = (bf16[2,448,256]{2,1,0:T(8,128)(2,1)S(1)}, bf16[2,448,256]{2,1,0:T(8,128)(2,1)S(1)}, u32[]{:S(2)}, u32[]{:S(2)}) collective-permute-start(bf16[2,448,256]{2,1,0:T(8,128)(2,1)S(1)} %add_convert_fusion.5), channel_id=1, source_target_pairs={{0,8},{8,16},{16,24},{24,28},{28,20},{20,12},{12,4},{4,0},{1,9},{9... | collective-permute-start | bytes 1376264 | tf_op jit(solution)/shard_map/ppermute | solution.py:370
  115.4 14.3 %collective-permute-start.25 = (bf16[2,448,256]{2,1,0:T(8,128)(2,1)S(1)}, bf16[2,448,256]{2,1,0:T(8,128)(2,1)S(1)}, u32[]{:S(2)}, u32[]{:S(2)}) collective-permute-start(bf16[2,448,256]{2,1,0:T(8,128)(2,1)S(1)} %add_convert_fusion.2), channel_id=1, source_target_pairs={{0,4},{8,0},{16,8},{24,16},{28,24},{20,28},{12,20},{4,12},{1,5},{9... | collective-permute-start | bytes 1376264 | tf_op jit(solution)/shard_map/ppermute | solution.py:370
  115.9 14.4 %collective-permute-start.13 = (bf16[2,128,896]{2,1,0:T(8,128)(2,1)S(1)}, bf16[2,128,896]{2,1,0:T(8,128)(2,1)S(1)}, u32[]{:S(2)}, u32[]{:S(2)}) collective-permute-start(bf16[2,128,896]{2,1,0:T(8,128)(2,1)S(1)} %get-tuple-element.45), channel_id=1, source_target_pairs={{0,1},{1,0},{2,3},{3,2},{4,5},{5,4},{6,7},{7,6},{8,9},{9,8},{10,11... | collective-permute-start | bytes 1376264 | tf_op jit(solution)/shard_map/ppermute | solution.py:367
  115.9 14.4 %collective-permute-start.14 = (bf16[2,128,896]{2,1,0:T(8,128)(2,1)S(1)}, bf16[2,128,896]{2,1,0:T(8,128)(2,1)S(1)}, u32[]{:S(2)}, u32[]{:S(2)}) collective-permute-start(bf16[2,128,896]{2,1,0:T(8,128)(2,1)S(1)} %get-tuple-element.47), channel_id=1, source_target_pairs={{0,1},{1,0},{2,3},{3,2},{4,5},{5,4},{6,7},{7,6},{8,9},{9,8},{10,11... | collective-permute-start | bytes 1376264 | tf_op jit(solution)/shard_map/ppermute | solution.py:367
  123.1 1.5 %collective-permute-start.16 = (bf16[512,256]{1,0:T(8,128)(2,1)S(1)}, bf16[512,256]{1,0:T(8,128)(2,1)S(1)}, u32[]{:S(2)}, u32[]{:S(2)}) collective-permute-start(bf16[512,256]{1,0:T(8,128)(2,1)S(1)} %add_convert_fusion.7.g_ref.refs_4_), channel_id=1, source_target_pairs={{0,1},{1,0},{2,3},{3,2},{4,5},{5,4},{6,7},{7,6},{8,9},{9,8},{10,11... | collective-permute-start | bytes 786440 | tf_op jit(solution)/shard_map/ppermute | solution.py:367
  124.6 12.6 %collective-permute-start.22 = (bf16[2,448,256]{2,1,0:T(8,128)(2,1)S(1)}, bf16[2,448,256]{2,1,0:T(8,128)(2,1)S(1)}, u32[]{:S(2)}, u32[]{:S(2)}) collective-permute-start(bf16[2,448,256]{2,1,0:T(8,128)(2,1)S(1)} %add_convert_fusion.4), channel_id=1, source_target_pairs={{0,8},{8,16},{16,24},{24,28},{28,20},{20,12},{12,4},{4,0},{1,9},{9... | collective-permute-start | bytes 1376264 | tf_op jit(solution)/shard_map/ppermute | solution.py:370
  129.1 22.2 %collective-permute-start.18 = (bf16[128,3584]{1,0:T(8,128)(2,1)S(1)}, bf16[128,3584]{1,0:T(8,128)(2,1)S(1)}, u32[]{:S(2)}, u32[]{:S(2)}) collective-permute-start(bf16[128,3584]{1,0:T(8,128)(2,1)S(1)} %get-tuple-element.54), channel_id=1, source_target_pairs={{0,2},{1,3},{2,0},{3,1},{4,6},{5,7},{6,4},{7,5},{8,10},{9,11},{10,... | collective-permute-start | bytes 2752520 | tf_op jit(solution)/shard_map/ppermute | solution.py:367
  129.8 12.1 %collective-permute-start.26 = (bf16[2,448,256]{2,1,0:T(8,128)(2,1)S(1)}, bf16[2,448,256]{2,1,0:T(8,128)(2,1)S(1)}, u32[]{:S(2)}, u32[]{:S(2)}) collective-permute-start(bf16[2,448,256]{2,1,0:T(8,128)(2,1)S(1)} %add_convert_fusion.1), channel_id=1, source_target_pairs={{0,4},{8,0},{16,8},{24,16},{28,24},{20,28},{12,20},{4,12},{1,5},{9... | collective-permute-start | bytes 1376264 | tf_op jit(solution)/shard_map/ppermute | solution.py:370

commit v7 on v6

--- a/solution.py
+++ b/solution.py
@@ -18,6 +18,7 @@
 F32 = jnp.float32
 BF16 = jnp.bfloat16
 ANYWHERE = pl.BlockSpec(memory_space=pl.ANY)
+IN_HBM = pl.BlockSpec(memory_space=pltpu.HBM)
 CYCLE = (0, 2, 4, 6, 7, 5, 3, 1)
 STEPS = (0, -1, 1, -2, 2, -3, 3, 4)
 
@@ -30,13 +31,13 @@
     return jax.ShapeDtypeStruct(shape, dtype)
 
 
-def call(body, me, operands, out_shape, micros, scratch=(), far=(), far_out=(), aliases=None):
+def call(body, me, operands, out_shape, micros, scratch=(), far=(), far_out=(), aliases=None, hbm=()):
     near = pl.BlockSpec(memory_space=pltpu.VMEM)
     outs = [ANYWHERE if i in far_out else near for i in range(len(out_shape))] if isinstance(out_shape, list) else near
     return pl.pallas_call(
         body,
         in_specs=[pl.BlockSpec(memory_space=pltpu.SMEM)]
-        + [ANYWHERE if i in far else near for i in range(len(operands))],
+        + [ANYWHERE if i in far else IN_HBM if i in hbm else near for i in range(len(operands))],
         out_specs=outs,
         out_shape=out_shape,
         scratch_shapes=scratch,
@@ -111,7 +112,7 @@
             pltpu.VMEM((1, rows), jnp.int32),
             pltpu.SemaphoreType.DMA((3,)),
         ],
-        far=(0, 1, 2),
+        hbm=(0, 1, 2),
     )
 
 
@@ -133,7 +134,7 @@
 def pack_heads(me, queries, upstream):
     out = shaped((2, 2, queries.shape[0], SPAN), BF16)
     return call(
-        pack_kernel, me, (queries, upstream), [out, out], 2, scratch=[pltpu.SemaphoreType.DMA((8,))], far=(0, 1)
+        pack_kernel, me, (queries, upstream), [out, out], 2, scratch=[pltpu.SemaphoreType.DMA((8,))], hbm=(0, 1)
     )
 
 
@@ -207,6 +208,16 @@
         far_out=(len(outs) - 1,),
         aliases={count: len(outs) - 1} if before else None,
     )
+
+
+def halve_kernel(me_ref, ups_ref, downs_ref, *refs):
+    refs[-2][...] = ups_ref[:1]
+    refs[-1][...] = downs_ref[1:]
+
+
+def halve(me, ups, downs, wait):
+    out = [shaped((1, *ups.shape[1:]), ups.dtype)] * 2
+    return call(halve_kernel, me, (ups, downs, *wait), out, 1, far=tuple(range(2, 2 + len(wait))))
 
 
 def attend_kernel(me_ref, own_ref, pack_ref, kv_ref, ids_ref, ids_row_ref, *refs):
@@ -306,8 +317,8 @@
     )
 
 
-def share_kernel(steps, depth, me_ref, *refs):
-    parts, g_ref, outs = refs[:4], refs[4], refs[5:]
+def share_kernel(steps, depth, split, me_ref, *refs):
+    parts, g_ref, outs = refs[:4], refs[4], refs[-(2 if split else 1) * len(steps) :]
     rows, lanes = parts[0].shape[1:]
     quarter = [g_ref[pl.ds(pl.multiple_of((me_ref[0] ^ r) * rows, rows), rows), :].astype(F32) for r in range(4)]
     kind = jnp.concatenate([read_marks(ref[0], depth)[0] for ref in parts], axis=0)
@@ -318,18 +329,19 @@
         total = contract(left, right, 0, 0)
         for e in range(2):
             block = total[:depth, e * PAIR : (e + 1) * PAIR]
-            if outs[0].dtype == BF16:
+            if split:
                 outs[2 * i + e][0] = block.astype(BF16)
             else:
                 outs[i][e] = block
 
 
-def shares(me, steps, parts, grad, depth, split):
+def shares(me, steps, parts, grad, depth, split=False, wait=()):
     if split:
         out = [shaped((1, depth, PAIR), BF16)] * (2 * len(steps))
     else:
         out = [shaped((2, depth, PAIR), F32)] * len(steps)
-    return call(functools.partial(share_kernel, steps, depth), me, (*parts, grad), out, 1 + len(steps))
+    far = tuple(range(5, 5 + len(wait)))
+    return call(functools.partial(share_kernel, steps, depth, split), me, (*parts, grad, *wait), out, 1 + len(steps), far=far)
 
 
 def in_order(parts, quarters):
@@ -371,10 +383,6 @@
 
     def both_ways(ups, downs):
         return turn(ups, 1), turn(downs, -1)
-
-    def halves(ups, downs, axis):
-        size = ups.shape[axis] // 2
-        return lax.slice_in_dim(ups, 0, size, axis=axis), lax.slice_in_dim(downs, size, 2 * size, axis=axis)
 
     me = jnp.stack([me_s, me_f, jnp.int32(0)])
     me_far = jnp.stack([me_s, me_f, jnp.int32(1)])
@@ -395,9 +403,8 @@
     pack = swap(pack, 1)
 
     if near_link:
-        ups, downs = halves(*weights[5:], 0)
-        weights += both_ways(after(ups, pack), after(downs, pack))
         before = project(me, STEPS[:5], parts, weights[:5], (), depth)
+        weights += both_ways(*halve(me, *weights[5:], (pack, before[0])))
         before = project(me, STEPS[5:7], parts, weights[5:7], before, depth)
         kv, kind, ids, ids_row, weight = project(me, STEPS[7:], parts, weights[7:], before, depth, True, True)
     else:
@@ -408,10 +415,13 @@
     grad_kv = (near + swap(far, 2)).astype(BF16)
     attended, grad_queries = place_heads(me, (near_own, swap(near_other, 1), far_own, swap(far_other, 1)))
 
+    grad_c = swap(grad_kv, 1)
     if near_link:
         ups, downs = both_ways(*shares(me, STEPS[7:], parts, grad_kv, depth, True))
-        terms = shares(me, STEPS[5:7], parts, grad_kv, depth, False)
-        terms += shares(me, STEPS[:5], parts, grad_kv, depth, False)
+    mine, away = hidden_grad(me, kind, grad_kv, grad_c, weight, swap(weight, 1), rows)
+    if near_link:
+        terms = shares(me, STEPS[5:7], parts, grad_kv, depth, wait=(away,))
+        terms += shares(me, STEPS[:5], parts, grad_kv, depth)
         none = jnp.zeros_like(ups)
         ups, downs = jnp.concatenate([ups, none]), jnp.concatenate([none, downs])
         for i in (0, 5, 3):
@@ -420,7 +430,6 @@
         grad_weight = terms[2] + ups.astype(F32) + downs.astype(F32)
     else:
         grad_weight = weight_plain(quarters, parts, grad_kv, depth)
-    mine, away = hidden_grad(me, kind, grad_kv, swap(grad_kv, 1), weight, swap(weight, 1), rows)
     grad_tokens = (mine + swap(away, 2).astype(F32)).astype(BF16)
     return attended[None], grad_queries[None], grad_tokens[None], grad_weight
 

time: 153 us -> 135 us (0.88)
  waiting for transfers between devices: 74.6 us -> 64 us
  Pallas kernels: 35 us -> 28.8 us
    ppermute x11, waiting for transfers between devices: 25.6 us -> 17.9 us  [swap(): return lax.ppermute(x, 'seq', [(i, i ^ bit) for i in range(seq)])]
    pallas_call x12 -> x13, Pallas kernels: 35 us -> 28.8 us  [call(): pl.pallas_call(body, in_specs=[pl.BlockSpec(memory_space=pltpu.SMEM)] + [...]
    ppermute x16, waiting for transfers between devices: 49 us -> 46.1 us  [turn(): lax.ppermute(x, 'fsdp', [(CYCLE[i], CYCLE[(i + by) % fsdp]) for i in rang...]
    slice x2 -> x0, local copies, waits for them, and re-layouts: 2.35 us -> none  [the longest x1 1.64 us: halves(): lax.slice_in_dim(ups, 0, size, axis=axis)]
    unnamed x40 -> x34, local copies, waits for them, and re-layouts: 14.2 us -> 15.2 us
  transfers between devices with their start and end apart: 27 -> 27, of which waited for: 13 -> 15; matrix products, arithmetic and copies ran while one was open for 3% -> 1% of each run, Pallas kernels for 21% -> 19%
where the time goes in v7:
time: 135 us; the launch traced here: 134 us
  waiting for transfers between devices  64 us (47%)
  Pallas kernels  28.8 us (21%)
  starting transfers between devices  22.6 us (17%)
  local copies, waits for them, and re-layouts  15.2 us (11%)
  other arithmetic  2.97 us (2%)
    ppermute x16, waiting for transfers between devices, turn(): lax.ppermute(x, 'fsdp', [(CYCLE[i], CYCLE[(i + by) % fsdp]) for i in rang...  46.1 us
    pallas_call x13, Pallas kernels, call(): pl.pallas_call(body, in_specs=[pl.BlockSpec(memory_space=pltpu.SMEM)] + [...  28.8 us
    ppermute x11, waiting for transfers between devices, swap(): return lax.ppermute(x, 'seq', [(i, i ^ bit) for i in range(seq)])  17.9 us
    ppermute x16, starting transfers between devices, turn(): lax.ppermute(x, 'fsdp', [(CYCLE[i], CYCLE[(i + by) % fsdp]) for i in rang...  16.6 us
    unnamed x34, local copies, waits for them, and re-layouts  15.2 us
    ppermute x11, starting transfers between devices, swap(): return lax.ppermute(x, 'seq', [(i, i ^ bit) for i in range(seq)])  5.98 us
  transfers between devices with their start and end apart: 27, of which 15 were waited for; matrix products, arithmetic and copies ran while one was open for 1% of the time, Pallas kernels for 19%

profile of v7, /device:TPU:0, one launch (start us, length us, event | category | flops | bytes accessed | tf_op | source)
XLA Modules:
  0.0 134.4 jit_solution(82869199668439218)
XLA Ops:
  0.7 1.2 copy-done.7
  3.2 1.2 shard_map.94.refs_0_
  4.4 3.0 %collective-permute-start.2 = (bf16[8,128,512]{2,1,0:T(8,128)(2,1)S(1)}, bf16[8,128,512]{2,1,0:T(8,128)(2,1)S(1)}, u32[]{:S(2)}, u32[]{:S(2)}) collective-permute-start(bf16[8,128,512]{2,1,0:T(8,128)(2,1)S(1)} %shard_map.94.refs_0_), channel_id=1, source_target_pairs={{0,2},{1,3},{2,0},{3,1},{4,6},{5,7},{6,4},{7,5},{8,10},{9,11},{10,... | collective-permute-start | bytes 3145736 | tf_op jit(solution)/shard_map/ppermute | solution.py:379
  7.4 1.6 %collective-permute-start.3 = (bf16[2,448,256]{2,1,0:T(8,128)(2,1)}, bf16[2,448,256]{2,1,0:T(8,128)(2,1)S(1)}, u32[]{:S(2)}, u32[]{:S(2)}) collective-permute-start(bf16[2,448,256]{2,1,0:T(8,128)(2,1)} %refs_4_.1), channel_id=1, source_target_pairs={{0,8},{8,16},{16,24},{24,28},{28,20},{20,12},{12,4},{4,0},{1,9},{9... | collective-permute-start | bytes 1376264 | tf_op jit(solution)/shard_map/ppermute | solution.py:382
  9.4 10.2 %collective-permute-done.3.refs_5_ = bf16[2,448,256]{2,1,0:T(8,128)(2,1)S(1)} collective-permute-done((bf16[2,448,256]{2,1,0:T(8,128)(2,1)}, bf16[2,448,256]{2,1,0:T(8,128)(2,1)S(1)}, u32[]{:S(2)}, u32[]{:S(2)}) %collective-permute-start.3) | collective-permute-done | bytes 458784 | tf_op jit(solution)/shard_map/ppermute | solution.py:382
  19.6 1.6 %collective-permute-start.4 = (bf16[2,448,256]{2,1,0:T(8,128)(2,1)S(1)}, bf16[2,448,256]{2,1,0:T(8,128)(2,1)S(1)}, u32[]{:S(2)}, u32[]{:S(2)}) collective-permute-start(bf16[2,448,256]{2,1,0:T(8,128)(2,1)S(1)} %collective-permute-done.3.refs_5_), channel_id=1, source_target_pairs={{0,8},{8,16},{16,24},{24,28},{28,20},{20,12},{12,4},{4,0},{1,9},{9... | collective-permute-start | bytes 1376264 | tf_op jit(solution)/shard_map/ppermute | solution.py:382
  23.2 7.5 %collective-permute-done.4.refs_1_.refs_7_ = bf16[2,448,256]{2,1,0:T(8,128)(2,1)S(1)} collective-permute-done((bf16[2,448,256]{2,1,0:T(8,128)(2,1)S(1)}, bf16[2,448,256]{2,1,0:T(8,128)(2,1)S(1)}, u32[]{:S(2)}, u32[]{:S(2)}) %collective-permute-start.4) | collective-permute-done | bytes 458784 | tf_op jit(solution)/shard_map/ppermute | solution.py:382
  30.7 0.8 copy-done.3
  31.4 1.3 collective-permute-done.6.refs_2_.refs_8_
  33.5 1.0 copy-done
  34.5 1.2 copy-done.8
  35.7 1.2 copy-done.9
  36.9 0.8 shard_map.93
  38.3 1.6 %collective-permute-start.8 = (bf16[2,448,256]{2,1,0:T(8,128)(2,1)}, bf16[2,448,256]{2,1,0:T(8,128)(2,1)S(1)}, u32[]{:S(2)}, u32[]{:S(2)}) collective-permute-start(bf16[2,448,256]{2,1,0:T(8,128)(2,1)} %copy-done.3), channel_id=1, source_target_pairs={{0,8},{8,16},{16,24},{24,28},{28,20},{20,12},{12,4},{4,0},{1,9},{9... | collective-permute-start | bytes 1376264 | tf_op jit(solution)/shard_map/ppermute | solution.py:382
  40.3 1.2 copy-done.1
  41.5 1.0 copy-done.4
  42.5 1.0 copy-done.6
  43.6 1.0 copy-done.10
  44.6 1.0 copy-done.12
  45.6 1.0 copy-done.14
  46.6 3.5 %shard_map.96 = (f32[512,512]{1,0:T(8,128)S(1)}, bf16[8,2,448,256]{3,2,1,0:T(8,128)(2,1)S(1)}) custom-call(s32[3]{0:T(128)S(1)} %pad_add_fusion.me_ref, bf16[8,128,512]{2,1,0:T(8,128)(2,1)S(1)} %shard_map.94.refs_0_, bf16[8,128,512]{2,1,0:T(8,128)(2,1)S(1)} %collective-permute-done.1.refs_1_, bf16[8,128,512]{2,1,0:T(8,128)(2,1)S(1)} %copy-done.1, ...), custom_call_target="tpu_custom_call" | custom-call | bytes 9000000 | tf_op jit(solution)/shard_map/pallas_call | solution.py:37
  50.1 0.8 collective-permute-done.8.ups_ref.refs_4_
  51.0 1.3 collective-permute-done.9.downs_ref.refs_5_
  52.8 1.6 %collective-permute-start.10 = (bf16[1,448,256]{2,1,0:T(8,128)(2,1)S(1)}, bf16[1,448,256]{2,1,0:T(8,128)(2,1)S(1)}, u32[]{:S(2)}, u32[]{:S(2)}) collective-permute-start(bf16[1,448,256]{2,1,0:T(8,128)(2,1)S(1)} %get-tuple-element.39), channel_id=1, source_target_pairs={{0,8},{8,16},{16,24},{24,28},{28,20},{20,12},{12,4},{4,0},{1,9},{9... | collective-permute-start | bytes 688136 | tf_op jit(solution)/shard_map/ppermute | solution.py:382
  54.9 1.8 %shard_map.98 = (f32[512,512]{1,0:T(8,128)S(1)}, bf16[8,2,448,256]{3,2,1,0:T(8,128)(2,1)S(1)}) custom-call(s32[3]{0:T(128)S(1)} %pad_add_fusion.me_ref, bf16[8,128,512]{2,1,0:T(8,128)(2,1)S(1)} %shard_map.94.refs_0_, bf16[8,128,512]{2,1,0:T(8,128)(2,1)S(1)} %collective-permute-done.1.refs_1_, ...), custom_call_target="tpu_custom_call", output_to_operand_aliasing={{1}: (8, {})} | custom-call | bytes 9000000 | tf_op jit(solution)/shard_map/pallas_call | solution.py:37
  56.8 2.6 %collective-permute-done.10.refs_4_ = bf16[1,448,256]{2,1,0:T(8,128)(2,1)S(1)} collective-permute-done((bf16[1,448,256]{2,1,0:T(8,128)(2,1)S(1)}, bf16[1,448,256]{2,1,0:T(8,128)(2,1)S(1)}, u32[]{:S(2)}, u32[]{:S(2)}) %collective-permute-start.10) | collective-permute-done | bytes 229408 | tf_op jit(solution)/shard_map/ppermute | solution.py:382
  59.3 1.3 collective-permute-done.11.refs_5_
  60.6 1.8 %shard_map.99 = (bf16[512,256]{1,0:T(8,128)(2,1)S(1)}, f32[512,1]{1,0:T(8,128)S(1)}, f32[512,1]{1,0:T(8,128)S(1)}, f32[1,512]{1,0:T(1,128)S(1)}, bf16[8,2,448,256]{3,2,1,0:T(8,128)(2,1)S(1)}) custom-call(s32[3]{0:T(128)S(1)} %pad_add_fusion.me_ref, bf16[8,128,512]{2,1,0:T(8,128)(2,1)S(1)} %shard_map.94.refs_0_, ...), custom_call_target="tpu_custom_call", output_to_operand_aliasing={{4}: (8, {})} | custom-call | bytes 9000000 | tf_op jit(solution)/shard_map/pallas_call | solution.py:37
  63.1 8.1 %collective-permute-done.12.kv_ref = bf16[512,256]{1,0:T(8,128)(2,1)S(1)} collective-permute-done((bf16[512,256]{1,0:T(8,128)(2,1)S(1)}, bf16[512,256]{1,0:T(8,128)(2,1)S(1)}, u32[]{:S(2)}, u32[]{:S(2)}) %collective-permute-start.12) | collective-permute-done | bytes 262176 | tf_op jit(solution)/shard_map/ppermute | solution.py:379
  71.2 4.6 %shard_map.100 = (bf16[2,128,896]{2,1,0:T(8,128)(2,1)S(1)}, bf16[2,128,896]{2,1,0:T(8,128)(2,1)S(1)}, f32[512,256]{1,0:T(8,128)S(1)}) custom-call(s32[3]{0:T(128)S(1)} %pad_add_fusion.2.me_ref, bf16[2,2,128,896]{3,2,1,0:T(8,128)(2,1)S(1)} %get-tuple-element.36.own_ref, bf16[2,2,128,896]{3,2,1,0:T(8,128)(2,1)S(1)} %collective-permute-done.refs_0_.pack_ref, ...), custom_call_target="tpu_custom_call" | custom-call | bytes 18000000 | tf_op jit(solution)/shard_map/pallas_call | solution.py:37
  76.4 4.6 %shard_map.101 = (bf16[2,128,896]{2,1,0:T(8,128)(2,1)S(1)}, bf16[2,128,896]{2,1,0:T(8,128)(2,1)S(1)}, f32[512,256]{1,0:T(8,128)S(1)}) custom-call(s32[3]{0:T(128)S(1)} %pad_add_fusion.me_ref, bf16[2,2,128,896]{3,2,1,0:T(8,128)(2,1)S(1)} %get-tuple-element.36.own_ref, bf16[2,2,128,896]{3,2,1,0:T(8,128)(2,1)S(1)} %collective-permute-done.refs_0_.pack_ref, ...), custom_call_target="tpu_custom_call" | custom-call | bytes 18000000 | tf_op jit(solution)/shard_map/pallas_call | solution.py:37
  81.0 8.4 %collective-permute-done.15 = f32[512,256]{1,0:T(8,128)S(1)} collective-permute-done((f32[512,256]{1,0:T(8,128)S(1)}, f32[512,256]{1,0:T(8,128)S(1)}, u32[]{:S(2)}, u32[]{:S(2)}) %collective-permute-start.15) | collective-permute-done | bytes 524320 | tf_op jit(solution)/shard_map/ppermute | solution.py:379
  89.5 1.3 shard_map.106
  91.3 1.6 %collective-permute-start.19 = (bf16[1,448,256]{2,1,0:T(8,128)(2,1)S(1)}, bf16[1,448,256]{2,1,0:T(8,128)(2,1)S(1)}, u32[]{:S(2)}, u32[]{:S(2)}) collective-permute-start(bf16[1,448,256]{2,1,0:T(8,128)(2,1)S(1)} %get-tuple-element.63), channel_id=1, source_target_pairs={{0,8},{8,16},{16,24},{24,28},{28,20},{20,12},{12,4},{4,0},{1,9},{9... | collective-permute-start | bytes 688136 | tf_op jit(solution)/shard_map/ppermute | solution.py:382
  92.9 2.9 %shard_map.103 = (f32[128,3584]{1,0:T(8,128)S(1)}, bf16[128,3584]{1,0:T(8,128)(2,1)S(1)}) custom-call(s32[3]{0:T(128)S(1)} %pad_add_fusion.me_ref, f32[512,1]{1,0:T(8,128)S(1)} %get-tuple-element.54.kind_ref, bf16[512,256]{1,0:T(8,128)(2,1)S(1)} %add_convert_fusion.7.g_ref.refs_4_, bf16[512,256]{1,0:T(8,128)(2,1)S(1)} %collective-permute-done.16.gc_ref, ...), custom_call_target="tpu_custom_call" | custom-call | bytes 21000000 | tf_op jit(solution)/shard_map/pallas_call | solution.py:37
  95.8 1.5 %shard_map.105 = (f32[2,448,256]{2,1,0:T(8,128)S(1)}, f32[2,448,256]{2,1,0:T(8,128)S(1)}) custom-call(s32[3]{0:T(128)S(1)} %pad_add_fusion.me_ref, bf16[8,128,512]{2,1,0:T(8,128)(2,1)S(1)} %shard_map.94.refs_0_, bf16[8,128,512]{2,1,0:T(8,128)(2,1)S(1)} %collective-permute-done.1.refs_1_, bf16[8,128,512]{2,1,0:T(8,128)(2,1)S(1)} %copy-done.2, ...), custom_call_target="tpu_custom_call" | custom-call | bytes 9000000 | tf_op jit(solution)/shard_map/pallas_call | solution.py:37
  97.3 1.5 %collective-permute-done.23 = bf16[1,448,256]{2,1,0:T(8,128)(2,1)S(1)} collective-permute-done((bf16[1,448,256]{2,1,0:T(8,128)(2,1)S(1)}, bf16[1,448,256]{2,1,0:T(8,128)(2,1)S(1)}, u32[]{:S(2)}, u32[]{:S(2)}) %collective-permute-start.23) | collective-permute-done | bytes 229408 | tf_op jit(solution)/shard_map/ppermute | solution.py:382
  99.5 1.6 %collective-permute-start.20 = (bf16[2,448,256]{2,1,0:T(8,128)(2,1)S(1)}, bf16[2,448,256]{2,1,0:T(8,128)(2,1)S(1)}, u32[]{:S(2)}, u32[]{:S(2)}) collective-permute-start(bf16[2,448,256]{2,1,0:T(8,128)(2,1)S(1)} %add_convert_fusion.6), channel_id=1, source_target_pairs={{0,8},{8,16},{16,24},{24,28},{28,20},{20,12},{12,4},{4,0},{1,9},{9... | collective-permute-start | bytes 1376264 | tf_op jit(solution)/shard_map/ppermute | solution.py:382
  101.6 2.3 %shard_map.104 = (f32[2,448,256]{2,1,0:T(8,128)S(1)}, f32[2,448,256]{2,1,0:T(8,128)S(1)}, f32[2,448,256]{2,1,0:T(8,128)S(1)}, f32[2,448,256]{2,1,0:T(8,128)S(1)}, f32[2,448,256]{2,1,0:T(8,128)S(1)}) custom-call(s32[3]{0:T(128)S(1)} %pad_add_fusion.me_ref, bf16[8,128,512]{2,1,0:T(8,128)(2,1)S(1)} %shard_map.94.refs_0_, ...), custom_call_target="tpu_custom_call" | custom-call | bytes 18000000 | tf_op jit(solution)/shard_map/pallas_call | solution.py:37
  104.5 6.5 %collective-permute-done.24 = bf16[2,448,256]{2,1,0:T(8,128)(2,1)S(1)} collective-permute-done((bf16[2,448,256]{2,1,0:T(8,128)(2,1)S(1)}, bf16[2,448,256]{2,1,0:T(8,128)(2,1)S(1)}, u32[]{:S(2)}, u32[]{:S(2)}) %collective-permute-start.24) | collective-permute-done | bytes 458784 | tf_op jit(solution)/shard_map/ppermute | solution.py:382
  111.8 1.6 %collective-permute-start.21 = (bf16[2,448,256]{2,1,0:T(8,128)(2,1)S(1)}, bf16[2,448,256]{2,1,0:T(8,128)(2,1)S(1)}, u32[]{:S(2)}, u32[]{:S(2)}) collective-permute-start(bf16[2,448,256]{2,1,0:T(8,128)(2,1)S(1)} %add_convert_fusion.5), channel_id=1, source_target_pairs={{0,8},{8,16},{16,24},{24,28},{28,20},{20,12},{12,4},{4,0},{1,9},{9... | collective-permute-start | bytes 1376264 | tf_op jit(solution)/shard_map/ppermute | solution.py:382
  113.5 1.9 %shard_map.102 = (bf16[128,3584]{1,0:T(8,128)(2,1)}, bf16[128,3584]{1,0:T(8,128)(2,1)}) custom-call(s32[3]{0:T(128)S(1)} %pad_add_fusion.me_ref, bf16[2,128,896]{2,1,0:T(8,128)(2,1)S(1)} %get-tuple-element.48.refs_0_, bf16[2,128,896]{2,1,0:T(8,128)(2,1)S(1)} %collective-permute-done.13.refs_1_, bf16[2,128,896]{2,1,0:T(8,128)(2,1)S(1)} %get-tuple-element.50.refs_2_, ...), custom_call_target="tpu_custom_call" | custom-call | bytes 9000000 | tf_op jit(solution)/shard_map/pallas_call | solution.py:37
  115.4 7.1 %collective-permute-done.25 = bf16[2,448,256]{2,1,0:T(8,128)(2,1)S(1)} collective-permute-done((bf16[2,448,256]{2,1,0:T(8,128)(2,1)S(1)}, bf16[2,448,256]{2,1,0:T(8,128)(2,1)S(1)}, u32[]{:S(2)}, u32[]{:S(2)}) %collective-permute-start.25) | collective-permute-done | bytes 458784 | tf_op jit(solution)/shard_map/ppermute | solution.py:382
  123.3 1.6 %collective-permute-start.22 = (bf16[2,448,256]{2,1,0:T(8,128)(2,1)S(1)}, bf16[2,448,256]{2,1,0:T(8,128)(2,1)S(1)}, u32[]{:S(2)}, u32[]{:S(2)}) collective-permute-start(bf16[2,448,256]{2,1,0:T(8,128)(2,1)S(1)} %add_convert_fusion.4), channel_id=1, source_target_pairs={{0,8},{8,16},{16,24},{24,28},{28,20},{20,12},{12,4},{4,0},{1,9},{9... | collective-permute-start | bytes 1376264 | tf_op jit(solution)/shard_map/ppermute | solution.py:382
  124.9 1.4 %collective-permute-done.18 = bf16[128,3584]{1,0:T(8,128)(2,1)S(1)} collective-permute-done((bf16[128,3584]{1,0:T(8,128)(2,1)S(1)}, bf16[128,3584]{1,0:T(8,128)(2,1)S(1)}, u32[]{:S(2)}, u32[]{:S(2)}) %collective-permute-start.18) | collective-permute-done | bytes 917536 | tf_op jit(solution)/shard_map/ppermute | solution.py:379
  126.3 1.1 fusion
  127.4 5.6 %collective-permute-done.26 = bf16[2,448,256]{2,1,0:T(8,128)(2,1)S(1)} collective-permute-done((bf16[2,448,256]{2,1,0:T(8,128)(2,1)S(1)}, bf16[2,448,256]{2,1,0:T(8,128)(2,1)S(1)}, u32[]{:S(2)}, u32[]{:S(2)}) %collective-permute-start.26) | collective-permute-done | bytes 458784 | tf_op jit(solution)/shard_map/ppermute | solution.py:382
  133.4 1.1 convert_add_fusion
  (65 shorter events, 12.2 us)
Async XLA Ops:
  0.7 1.2 copy-start.7
  1.9 0.7 copy-start.15
  2.5 0.7 copy-start.16
  4.4 29.1 %collective-permute-start.2 = (bf16[8,128,512]{2,1,0:T(8,128)(2,1)S(1)}, bf16[8,128,512]{2,1,0:T(8,128)(2,1)S(1)}, u32[]{:S(2)}, u32[]{:S(2)}) collective-permute-start(bf16[8,128,512]{2,1,0:T(8,128)(2,1)S(1)} %shard_map.94.refs_0_), channel_id=1, source_target_pairs={{0,2},{1,3},{2,0},{3,1},{4,6},{5,7},{6,4},{7,5},{8,10},{9,11},{10,... | collective-permute-start | bytes 3145736 | tf_op jit(solution)/shard_map/ppermute | solution.py:379
  7.4 12.2 %collective-permute-start.3 = (bf16[2,448,256]{2,1,0:T(8,128)(2,1)}, bf16[2,448,256]{2,1,0:T(8,128)(2,1)S(1)}, u32[]{:S(2)}, u32[]{:S(2)}) collective-permute-start(bf16[2,448,256]{2,1,0:T(8,128)(2,1)} %refs_4_.1), channel_id=1, source_target_pairs={{0,8},{8,16},{16,24},{24,28},{28,20},{20,12},{12,4},{4,0},{1,9},{9... | collective-permute-start | bytes 1376264 | tf_op jit(solution)/shard_map/ppermute | solution.py:382
  9.0 13.0 %collective-permute-start.5 = (bf16[2,448,256]{2,1,0:T(8,128)(2,1)}, bf16[2,448,256]{2,1,0:T(8,128)(2,1)S(1)}, u32[]{:S(2)}, u32[]{:S(2)}) collective-permute-start(bf16[2,448,256]{2,1,0:T(8,128)(2,1)} %refs_4_.1), channel_id=1, source_target_pairs={{0,4},{8,0},{16,8},{24,16},{28,24},{20,28},{12,20},{4,12},{1,5},{9... | collective-permute-start | bytes 1376264 | tf_op jit(solution)/shard_map/ppermute | solution.py:382
  19.6 11.1 %collective-permute-start.4 = (bf16[2,448,256]{2,1,0:T(8,128)(2,1)S(1)}, bf16[2,448,256]{2,1,0:T(8,128)(2,1)S(1)}, u32[]{:S(2)}, u32[]{:S(2)}) collective-permute-start(bf16[2,448,256]{2,1,0:T(8,128)(2,1)S(1)} %collective-permute-done.3.refs_5_), channel_id=1, source_target_pairs={{0,8},{8,16},{16,24},{24,28},{28,20},{20,12},{12,4},{4,0},{1,9},{9... | collective-permute-start | bytes 1376264 | tf_op jit(solution)/shard_map/ppermute | solution.py:382
  21.2 0.8 copy-start.11
  21.9 10.8 %collective-permute-start.6 = (bf16[2,448,256]{2,1,0:T(8,128)(2,1)S(1)}, bf16[2,448,256]{2,1,0:T(8,128)(2,1)S(1)}, u32[]{:S(2)}, u32[]{:S(2)}) collective-permute-start(bf16[2,448,256]{2,1,0:T(8,128)(2,1)S(1)} %collective-permute-done.5.refs_6_), channel_id=1, source_target_pairs={{0,4},{8,0},{16,8},{24,16},{28,24},{20,28},{12,20},{4,12},{1,5},{9... | collective-permute-start | bytes 1376264 | tf_op jit(solution)/shard_map/ppermute | solution.py:382
  22.4 0.8 copy-start.13
  23.2 17.1 %collective-permute-start.1 = (bf16[8,128,512]{2,1,0:T(8,128)(2,1)S(1)}, bf16[8,128,512]{2,1,0:T(8,128)(2,1)S(1)}, u32[]{:S(2)}, u32[]{:S(2)}) collective-permute-start(bf16[8,128,512]{2,1,0:T(8,128)(2,1)S(1)} %shard_map.94.refs_0_), channel_id=1, source_target_pairs={{0,1},{1,0},{2,3},{3,2},{4,5},{5,4},{6,7},{7,6},{8,9},{9,8},{10,11... | collective-permute-start | bytes 3145736 | tf_op jit(solution)/shard_map/ppermute | solution.py:379
  30.7 0.8 copy-start.3
  32.7 0.8 copy-start.5
  33.5 1.0 copy-start
  34.5 5.8 %collective-permute-start.7 = (bf16[8,128,512]{2,1,0:T(8,128)(2,1)}, bf16[8,128,512]{2,1,0:T(8,128)(2,1)S(1)}, u32[]{:S(2)}, u32[]{:S(2)}) collective-permute-start(bf16[8,128,512]{2,1,0:T(8,128)(2,1)} %shard_map.95.refs_2_), channel_id=1, source_target_pairs={{0,1},{1,0},{2,3},{3,2},{4,5},{5,4},{6,7},{7,6},{8,9},{9,8},{10,11... | collective-permute-start | bytes 3145736 | tf_op jit(solution)/shard_map/ppermute | solution.py:379
  34.5 1.2 copy-start.8
  35.7 1.2 copy-start.9
  36.9 18.1 %copy-start.2 = (bf16[8,128,512]{2,1,0:T(8,128)(2,1)S(1)}, bf16[8,128,512]{2,1,0:T(8,128)(2,1)}, u32[]{:S(2)}) copy-start(bf16[8,128,512]{2,1,0:T(8,128)(2,1)} %shard_map.95.refs_2_) | copy-start | bytes 3145732
  37.7 12.4 %collective-permute-start = (bf16[2,2,128,896]{3,2,1,0:T(8,128)(2,1)S(1)}, bf16[2,2,128,896]{3,2,1,0:T(8,128)(2,1)S(1)}, u32[]{:S(2)}, u32[]{:S(2)}) collective-permute-start(bf16[2,2,128,896]{3,2,1,0:T(8,128)(2,1)S(1)} %get-tuple-element.37), channel_id=1, source_target_pairs={{0,1},{1,0},{2,3},{3,2},{4,5},{5,4},{6,7},{7,6},{8,9},{9,8},{10,11... | collective-permute-start | bytes 2752520 | tf_op jit(solution)/shard_map/ppermute | solution.py:379
  38.3 12.7 %collective-permute-start.8 = (bf16[2,448,256]{2,1,0:T(8,128)(2,1)}, bf16[2,448,256]{2,1,0:T(8,128)(2,1)S(1)}, u32[]{:S(2)}, u32[]{:S(2)}) collective-permute-start(bf16[2,448,256]{2,1,0:T(8,128)(2,1)} %copy-done.3), channel_id=1, source_target_pairs={{0,8},{8,16},{16,24},{24,28},{28,20},{20,12},{12,4},{4,0},{1,9},{9... | collective-permute-start | bytes 1376264 | tf_op jit(solution)/shard_map/ppermute | solution.py:382
  39.8 12.4 %collective-permute-start.9 = (bf16[2,448,256]{2,1,0:T(8,128)(2,1)}, bf16[2,448,256]{2,1,0:T(8,128)(2,1)S(1)}, u32[]{:S(2)}, u32[]{:S(2)}) collective-permute-start(bf16[2,448,256]{2,1,0:T(8,128)(2,1)} %copy-done.5), channel_id=1, source_target_pairs={{0,4},{8,0},{16,8},{24,16},{28,24},{20,28},{12,20},{4,12},{1,5},{9... | collective-permute-start | bytes 1376264 | tf_op jit(solution)/shard_map/ppermute | solution.py:382
  40.3 1.2 copy-start.1
  41.5 1.0 copy-start.4
  42.5 1.0 copy-start.6
  43.6 1.0 copy-start.10
  44.6 1.0 copy-start.12
  45.6 1.0 copy-start.14
  52.8 6.5 %collective-permute-start.10 = (bf16[1,448,256]{2,1,0:T(8,128)(2,1)S(1)}, bf16[1,448,256]{2,1,0:T(8,128)(2,1)S(1)}, u32[]{:S(2)}, u32[]{:S(2)}) collective-permute-start(bf16[1,448,256]{2,1,0:T(8,128)(2,1)S(1)} %get-tuple-element.39), channel_id=1, source_target_pairs={{0,8},{8,16},{16,24},{24,28},{28,20},{20,12},{12,4},{4,0},{1,9},{9... | collective-permute-start | bytes 688136 | tf_op jit(solution)/shard_map/ppermute | solution.py:382
  54.5 6.1 %collective-permute-start.11 = (bf16[1,448,256]{2,1,0:T(8,128)(2,1)S(1)}, bf16[1,448,256]{2,1,0:T(8,128)(2,1)S(1)}, u32[]{:S(2)}, u32[]{:S(2)}) collective-permute-start(bf16[1,448,256]{2,1,0:T(8,128)(2,1)S(1)} %get-tuple-element.40), channel_id=1, source_target_pairs={{0,4},{8,0},{16,8},{24,16},{28,24},{20,28},{12,20},{4,12},{1,5},{9... | collective-permute-start | bytes 688136 | tf_op jit(solution)/shard_map/ppermute | solution.py:382
  62.4 30.5 %collective-permute-start.17 = (bf16[8,2,448,256]{3,2,1,0:T(8,128)(2,1)S(1)}, bf16[8,2,448,256]{3,2,1,0:T(8,128)(2,1)S(1)}, u32[]{:S(2)}, u32[]{:S(2)}) collective-permute-start(bf16[8,2,448,256]{3,2,1,0:T(8,128)(2,1)S(1)} %get-tuple-element.56.w_ref), channel_id=1, source_target_pairs={{0,1},{1,0},{2,3},{3,2},{4,5},{5,4},{6,7},{7,6},{8,9},{9,8},{10,11... | collective-permute-start | bytes 11010056 | tf_op jit(solution)/shard_map/ppermute | solution.py:379
  62.5 8.7 %collective-permute-start.12 = (bf16[512,256]{1,0:T(8,128)(2,1)S(1)}, bf16[512,256]{1,0:T(8,128)(2,1)S(1)}, u32[]{:S(2)}, u32[]{:S(2)}) collective-permute-start(bf16[512,256]{1,0:T(8,128)(2,1)S(1)} %get-tuple-element.44.kv_ref), channel_id=1, source_target_pairs={{0,2},{1,3},{2,0},{3,1},{4,6},{5,7},{6,4},{7,5},{8,10},{9,11},{10,... | collective-permute-start | bytes 786440 | tf_op jit(solution)/shard_map/ppermute | solution.py:379
  75.8 13.6 %collective-permute-start.15 = (f32[512,256]{1,0:T(8,128)S(1)}, f32[512,256]{1,0:T(8,128)S(1)}, u32[]{:S(2)}, u32[]{:S(2)}) collective-permute-start(f32[512,256]{1,0:T(8,128)S(1)} %get-tuple-element.47.refs_0_), channel_id=1, source_target_pairs={{0,2},{1,3},{2,0},{3,1},{4,6},{5,7},{6,4},{7,5},{8,10},{9,11},{10,... | collective-permute-start | bytes 1572872 | tf_op jit(solution)/shard_map/ppermute | solution.py:379
  89.4 3.4 %collective-permute-start.16 = (bf16[512,256]{1,0:T(8,128)(2,1)S(1)}, bf16[512,256]{1,0:T(8,128)(2,1)S(1)}, u32[]{:S(2)}, u32[]{:S(2)}) collective-permute-start(bf16[512,256]{1,0:T(8,128)(2,1)S(1)} %add_convert_fusion.7.g_ref.refs_4_), channel_id=1, source_target_pairs={{0,1},{1,0},{2,3},{3,2},{4,5},{5,4},{6,7},{7,6},{8,9},{9,8},{10,11... | collective-permute-start | bytes 786440 | tf_op jit(solution)/shard_map/ppermute | solution.py:379
  90.8 8.1 %collective-permute-start.23 = (bf16[1,448,256]{2,1,0:T(8,128)(2,1)S(1)}, bf16[1,448,256]{2,1,0:T(8,128)(2,1)S(1)}, u32[]{:S(2)}, u32[]{:S(2)}) collective-permute-start(bf16[1,448,256]{2,1,0:T(8,128)(2,1)S(1)} %get-tuple-element.67), channel_id=1, source_target_pairs={{0,4},{8,0},{16,8},{24,16},{28,24},{20,28},{12,20},{4,12},{1,5},{9... | collective-permute-start | bytes 688136 | tf_op jit(solution)/shard_map/ppermute | solution.py:382
  91.3 8.1 %collective-permute-start.19 = (bf16[1,448,256]{2,1,0:T(8,128)(2,1)S(1)}, bf16[1,448,256]{2,1,0:T(8,128)(2,1)S(1)}, u32[]{:S(2)}, u32[]{:S(2)}) collective-permute-start(bf16[1,448,256]{2,1,0:T(8,128)(2,1)S(1)} %get-tuple-element.63), channel_id=1, source_target_pairs={{0,8},{8,16},{16,24},{24,28},{28,20},{20,12},{12,4},{4,0},{1,9},{9... | collective-permute-start | bytes 688136 | tf_op jit(solution)/shard_map/ppermute | solution.py:382
  98.9 12.2 %collective-permute-start.24 = (bf16[2,448,256]{2,1,0:T(8,128)(2,1)S(1)}, bf16[2,448,256]{2,1,0:T(8,128)(2,1)S(1)}, u32[]{:S(2)}, u32[]{:S(2)}) collective-permute-start(bf16[2,448,256]{2,1,0:T(8,128)(2,1)S(1)} %add_convert_fusion.3), channel_id=1, source_target_pairs={{0,4},{8,0},{16,8},{24,16},{28,24},{20,28},{12,20},{4,12},{1,5},{9... | collective-permute-start | bytes 1376264 | tf_op jit(solution)/shard_map/ppermute | solution.py:382
  99.5 12.2 %collective-permute-start.20 = (bf16[2,448,256]{2,1,0:T(8,128)(2,1)S(1)}, bf16[2,448,256]{2,1,0:T(8,128)(2,1)S(1)}, u32[]{:S(2)}, u32[]{:S(2)}) collective-permute-start(bf16[2,448,256]{2,1,0:T(8,128)(2,1)S(1)} %add_convert_fusion.6), channel_id=1, source_target_pairs={{0,8},{8,16},{16,24},{24,28},{28,20},{20,12},{12,4},{4,0},{1,9},{9... | collective-permute-start | bytes 1376264 | tf_op jit(solution)/shard_map/ppermute | solution.py:382
  101.1 12.4 %collective-permute-start.13 = (bf16[2,128,896]{2,1,0:T(8,128)(2,1)S(1)}, bf16[2,128,896]{2,1,0:T(8,128)(2,1)S(1)}, u32[]{:S(2)}, u32[]{:S(2)}) collective-permute-start(bf16[2,128,896]{2,1,0:T(8,128)(2,1)S(1)} %get-tuple-element.49), channel_id=1, source_target_pairs={{0,1},{1,0},{2,3},{3,2},{4,5},{5,4},{6,7},{7,6},{8,9},{9,8},{10,11... | collective-permute-start | bytes 1376264 | tf_op jit(solution)/shard_map/ppermute | solution.py:379
  101.1 12.4 %collective-permute-start.14 = (bf16[2,128,896]{2,1,0:T(8,128)(2,1)S(1)}, bf16[2,128,896]{2,1,0:T(8,128)(2,1)S(1)}, u32[]{:S(2)}, u32[]{:S(2)}) collective-permute-start(bf16[2,128,896]{2,1,0:T(8,128)(2,1)S(1)} %get-tuple-element.51), channel_id=1, source_target_pairs={{0,1},{1,0},{2,3},{3,2},{4,5},{5,4},{6,7},{7,6},{8,9},{9,8},{10,11... | collective-permute-start | bytes 1376264 | tf_op jit(solution)/shard_map/ppermute | solution.py:379
  104.0 22.3 %collective-permute-start.18 = (bf16[128,3584]{1,0:T(8,128)(2,1)S(1)}, bf16[128,3584]{1,0:T(8,128)(2,1)S(1)}, u32[]{:S(2)}, u32[]{:S(2)}) collective-permute-start(bf16[128,3584]{1,0:T(8,128)(2,1)S(1)} %get-tuple-element.58.refs_5_), channel_id=1, source_target_pairs={{0,2},{1,3},{2,0},{3,1},{4,6},{5,7},{6,4},{7,5},{8,10},{9,11},{10,... | collective-permute-start | bytes 2752520 | tf_op jit(solution)/shard_map/ppermute | solution.py:379
  111.2 11.3 %collective-permute-start.25 = (bf16[2,448,256]{2,1,0:T(8,128)(2,1)S(1)}, bf16[2,448,256]{2,1,0:T(8,128)(2,1)S(1)}, u32[]{:S(2)}, u32[]{:S(2)}) collective-permute-start(bf16[2,448,256]{2,1,0:T(8,128)(2,1)S(1)} %add_convert_fusion.2), channel_id=1, source_target_pairs={{0,4},{8,0},{16,8},{24,16},{28,24},{20,28},{12,20},{4,12},{1,5},{9... | collective-permute-start | bytes 1376264 | tf_op jit(solution)/shard_map/ppermute | solution.py:382
  111.8 11.3 %collective-permute-start.21 = (bf16[2,448,256]{2,1,0:T(8,128)(2,1)S(1)}, bf16[2,448,256]{2,1,0:T(8,128)(2,1)S(1)}, u32[]{:S(2)}, u32[]{:S(2)}) collective-permute-start(bf16[2,448,256]{2,1,0:T(8,128)(2,1)S(1)} %add_convert_fusion.5), channel_id=1, source_target_pairs={{0,8},{8,16},{16,24},{24,28},{28,20},{20,12},{12,4},{4,0},{1,9},{9... | collective-permute-start | bytes 1376264 | tf_op jit(solution)/shard_map/ppermute | solution.py:382
  122.6 10.4 %collective-permute-start.26 = (bf16[2,448,256]{2,1,0:T(8,128)(2,1)S(1)}, bf16[2,448,256]{2,1,0:T(8,128)(2,1)S(1)}, u32[]{:S(2)}, u32[]{:S(2)}) collective-permute-start(bf16[2,448,256]{2,1,0:T(8,128)(2,1)S(1)} %add_convert_fusion.1), channel_id=1, source_target_pairs={{0,4},{8,0},{16,8},{24,16},{28,24},{20,28},{12,20},{4,12},{1,5},{9... | collective-permute-start | bytes 1376264 | tf_op jit(solution)/shard_map/ppermute | solution.py:382
  123.3 10.1 %collective-permute-start.22 = (bf16[2,448,256]{2,1,0:T(8,128)(2,1)S(1)}, bf16[2,448,256]{2,1,0:T(8,128)(2,1)S(1)}, u32[]{:S(2)}, u32[]{:S(2)}) collective-permute-start(bf16[2,448,256]{2,1,0:T(8,128)(2,1)S(1)} %add_convert_fusion.4), channel_id=1, source_target_pairs={{0,8},{8,16},{16,24},{24,28},{28,20},{20,12},{12,4},{4,0},{1,9},{9... | collective-permute-start | bytes 1376264 | tf_op jit(solution)/shard_map/ppermute | solution.py:382

commit v8 on v7

--- a/solution.py
+++ b/solution.py
@@ -18,7 +18,6 @@
 F32 = jnp.float32
 BF16 = jnp.bfloat16
 ANYWHERE = pl.BlockSpec(memory_space=pl.ANY)
-IN_HBM = pl.BlockSpec(memory_space=pltpu.HBM)
 CYCLE = (0, 2, 4, 6, 7, 5, 3, 1)
 STEPS = (0, -1, 1, -2, 2, -3, 3, 4)
 
@@ -31,13 +30,13 @@
     return jax.ShapeDtypeStruct(shape, dtype)
 
 
-def call(body, me, operands, out_shape, micros, scratch=(), far=(), far_out=(), aliases=None, hbm=()):
+def call(body, me, operands, out_shape, micros, scratch=(), far=(), far_out=(), aliases=None):
     near = pl.BlockSpec(memory_space=pltpu.VMEM)
     outs = [ANYWHERE if i in far_out else near for i in range(len(out_shape))] if isinstance(out_shape, list) else near
     return pl.pallas_call(
         body,
         in_specs=[pl.BlockSpec(memory_space=pltpu.SMEM)]
-        + [ANYWHERE if i in far else IN_HBM if i in hbm else near for i in range(len(operands))],
+        + [ANYWHERE if i in far else near for i in range(len(operands))],
         out_specs=outs,
         out_shape=out_shape,
         scratch_shapes=scratch,
@@ -47,13 +46,6 @@
     )(me, *operands)
 
 
-def run_copies(copies):
-    for copy in copies:
-        copy.start()
-    for copy in copies:
-        copy.wait()
-
-
 def owner_at(me_f, by):
     size = len(CYCLE)
     half = size // 2
@@ -63,29 +55,32 @@
     return jnp.where(spot < half, 2 * spot, 2 * (size - 1 - spot) + 1)
 
 
-def after(x, *others):
+def after_kernel(x_ref, other_ref, out_ref):
+    out_ref[...] = x_ref[...]
+
+
+def after(x, other):
+    near = pl.BlockSpec(memory_space=pltpu.VMEM)
     return pl.pallas_call(
-        lambda *refs: None,
-        in_specs=[ANYWHERE] * (1 + len(others)),
-        out_specs=ANYWHERE,
+        after_kernel,
+        in_specs=[near, ANYWHERE],
+        out_specs=near,
         out_shape=shaped(x.shape, x.dtype),
-        input_output_aliases={0: 0},
-        cost_estimate=pl.CostEstimate(flops=0, bytes_accessed=0, transcendentals=0),
-    )(x, *others)
+        cost_estimate=pl.CostEstimate(flops=0, bytes_accessed=3000000, transcendentals=0),
+    )(x, other)
 
 
 def as_column(row):
     return jnp.broadcast_to(row, (128, row.shape[1])).T[:, :1]
 
 
-def blocks_kernel(depth, me_ref, tok_far, kind_far, ids_far, out_ref, tok_ref, kind_ref, ids_ref, sems):
-    pairs = ((tok_far, tok_ref), (kind_far, kind_ref), (ids_far, ids_ref))
-    run_copies([pltpu.make_async_copy(a, b, sems.at[i]) for i, (a, b) in enumerate(pairs)])
+def blocks_kernel(depth, me_ref, tok_ref, ids_ref, out_ref):
     count, rows, lanes = out_ref.shape
     base = lanes - 128
     lane = lax.broadcasted_iota(jnp.int32, (rows, 128), 1) - (depth - base)
-    ids = ids_ref[...]
-    marks = [as_column(x.astype(F32)) for x in (kind_ref[...], lax.div(ids, DIGIT), lax.rem(ids, DIGIT))]
+    ids = lax.div(ids_ref[...], 2)
+    marks = (lax.rem(ids_ref[...], 2), lax.div(ids, DIGIT), lax.rem(ids, DIGIT))
+    marks = [as_column(x.astype(F32)) for x in marks]
     for j in range(count):
         out_ref[j, :, :depth] = tok_ref[:, j * depth : (j + 1) * depth]
         last = out_ref[j, :, base:].astype(F32)
@@ -95,47 +90,17 @@
         out_ref[j, :, base:] = last.astype(BF16)
 
 
-def token_blocks(me, tokens, kinds, ids, count):
+def token_blocks(me, tokens, ids, count):
     rows, width = tokens.shape
     depth = width // count
     lanes = -(-(depth + 3) // 128) * 128
     out = shaped((count, rows, lanes), BF16)
-    return call(
-        functools.partial(blocks_kernel, depth),
-        me,
-        (tokens, kinds, ids),
-        out,
-        2,
-        scratch=[
-            pltpu.VMEM((rows, width), BF16),
-            pltpu.VMEM((1, rows), jnp.int32),
-            pltpu.VMEM((1, rows), jnp.int32),
-            pltpu.SemaphoreType.DMA((3,)),
-        ],
-        hbm=(0, 1, 2),
-    )
+    return call(functools.partial(blocks_kernel, depth), me, (tokens, ids), out, 2)
 
 
 def read_marks(block, depth):
     mark = [block[:, depth + i : depth + i + 1].astype(F32) for i in range(3)]
     return mark[0], mark[1] * DIGIT + mark[2]
-
-
-def pack_kernel(me_ref, q_far, up_far, own_ref, other_ref, sems):
-    copies = []
-    for i in range(4):
-        here = pl.ds(pl.multiple_of((me_ref[0] ^ i) * SPAN, SPAN), SPAN)
-        out_ref = other_ref if i % 2 else own_ref
-        for k, far in enumerate((q_far, up_far)):
-            copies.append(pltpu.make_async_copy(far.at[:, here], out_ref.at[i // 2, k], sems.at[2 * i + k]))
-    run_copies(copies)
-
-
-def pack_heads(me, queries, upstream):
-    out = shaped((2, 2, queries.shape[0], SPAN), BF16)
-    return call(
-        pack_kernel, me, (queries, upstream), [out, out], 2, scratch=[pltpu.SemaphoreType.DMA((8,))], hbm=(0, 1)
-    )
 
 
 def place_kernel(me_ref, *refs):
@@ -220,19 +185,20 @@
     return call(halve_kernel, me, (ups, downs, *wait), out, 1, far=tuple(range(2, 2 + len(wait))))
 
 
-def attend_kernel(me_ref, own_ref, pack_ref, kv_ref, ids_ref, ids_row_ref, *refs):
-    mine_ref, other_ref, gkv_ref, bias, scores_all, dp_all, pbs, his, los = refs[-9:]
-    rows = own_ref.shape[2]
+def attend_kernel(me_ref, q_ref, up_ref, q_other, up_other, kv_ref, ids_ref, ids_row_ref, *refs):
+    mine_ref, other_ref, early_ref, late_ref, bias, scores_all, dp_all, pbs, his, los = refs[-10:]
+    rows = q_ref.shape[0]
     heads = [slice(h * HEAD_DIM, (h + 1) * HEAD_DIM) for h in range(GROUP)]
     for i in range(2):
         here = pl.ds(pl.multiple_of((me_ref[0] ^ i) * rows, rows), rows)
         bias[i * rows : (i + 1) * rows, :] = jnp.where(ids_row_ref[...] <= ids_ref[here, :], 0.0, HIDDEN)
     keys = kv_ref[:, :HEAD_DIM]
     values = kv_ref[:, HEAD_DIM:]
-    spot = me_ref[2]
+    start = me_ref[2] * SPAN
+    places = [pl.ds(pl.multiple_of(start + h * HEAD_DIM, HEAD_DIM), HEAD_DIM) for h in range(GROUP)]
     q, up = [
-        jnp.concatenate([ref[spot, i, :, cols] for ref in (own_ref, pack_ref) for cols in heads], axis=0)
-        for i in range(2)
+        jnp.concatenate([ref[:, place] for ref in pair for place in places], axis=0)
+        for pair in ((q_ref, q_other), (up_ref, up_other))
     ]
     scores_all[...] = contract(q, keys, 1, 1)
     dp_all[...] = contract(up, values, 1, 1).astype(BF16)
@@ -257,23 +223,26 @@
             ref[1, :, cols] = gq[here]
     dk = (contract(q, his[...], 0, 0) + contract(q, los[...], 0, 0)) * SCALE
     dv = contract(up, pbs[...], 0, 0)
-    gkv_ref[:, :HEAD_DIM] = dk.T
-    gkv_ref[:, HEAD_DIM:] = dv.T
-
-
-def attend(me, own, pack, kv, ids, ids_row, wait=()):
-    rows = own.shape[2]
+    half = early_ref.shape[0]
+    for i, x in enumerate((dk.T, dv.T)):
+        cols = slice(i * HEAD_DIM, (i + 1) * HEAD_DIM)
+        early_ref[:, cols] = x[:half]
+        late_ref[:, cols] = x[half:].astype(late_ref.dtype)
+
+
+def attend(me, sides, kv, ids, ids_row, late, wait=()):
+    rows = sides[0].shape[0]
     length = kv.shape[0]
     stacked = (2 * GROUP * rows, length)
     side = shaped((2, rows, SPAN), BF16)
     return call(
         attend_kernel,
         me,
-        (own, pack, kv, ids, ids_row, *wait),
-        [side, side, shaped((length, PAIR), F32)],
+        (*sides, kv, ids, ids_row, *wait),
+        [side, side, shaped((length // 2, PAIR), F32), shaped((length // 2, PAIR), late)],
         6,
         scratch=[pltpu.VMEM((2 * rows, length), F32), pltpu.VMEM(stacked, F32)] + [pltpu.VMEM(stacked, BF16)] * 4,
-        far=tuple(range(5, 5 + len(wait))),
+        far=tuple(range(7, 7 + len(wait))),
     )
 
 
@@ -384,8 +353,8 @@
     def both_ways(ups, downs):
         return turn(ups, 1), turn(downs, -1)
 
-    me = jnp.stack([me_s, me_f, jnp.int32(0)])
-    me_far = jnp.stack([me_s, me_f, jnp.int32(1)])
+    me = jnp.stack([me_s, me_f, me_s])
+    me_far = jnp.stack([me_s, me_f, me_s ^ 2])
     quarters = me_s ^ jnp.arange(seq, dtype=jnp.int32)
     if near_link:
         weights = [kv_weight, *both_ways(kv_weight, kv_weight)]
@@ -394,25 +363,24 @@
     else:
         weight = lax.all_gather(kv_weight, "fsdp", axis=0)
 
-    blocks = token_blocks(me, tokens, modality, block_ids, fsdp)
+    blocks = token_blocks(me, tokens, block_ids * 2 + modality, fsdp)
     across = swap(blocks, 2)
     if near_link:
-        across = after(across, weights[3], weights[4])
+        across = after(across, weights[3][0, :16, :128])
     parts = [blocks, swap(blocks, 1), across, swap(across, 1)]
-    own, pack = pack_heads(me, queries, cotangent)
-    pack = swap(pack, 1)
+    sides = (queries, cotangent, swap(queries, 1), swap(cotangent, 1))
 
     if near_link:
         before = project(me, STEPS[:5], parts, weights[:5], (), depth)
-        weights += both_ways(*halve(me, *weights[5:], (pack, before[0])))
+        weights += both_ways(*halve(me, *weights[5:], (before[0], sides[2][:16, :128], sides[3][:16, :128])))
         before = project(me, STEPS[5:7], parts, weights[5:7], before, depth)
         kv, kind, ids, ids_row, weight = project(me, STEPS[7:], parts, weights[7:], before, depth, True, True)
     else:
         kv, kind, ids, ids_row = project_plain(quarters, parts, weight, depth)
     kv_far = swap(kv, 2)
-    far_own, far_other, far = attend(me_far, own, pack, kv_far, ids, ids_row)
-    near_own, near_other, near = attend(me, own, pack, kv, ids, ids_row, (far,))
-    grad_kv = (near + swap(far, 2)).astype(BF16)
+    far_own, far_other, early, late = attend(me_far, sides, kv_far, ids, ids_row, BF16)
+    near_own, near_other, *near = attend(me, sides, kv, ids, ids_row, F32, (early,))
+    grad_kv = jnp.concatenate([near[0] + swap(early, 2), near[1] + swap(late, 2).astype(F32)]).astype(BF16)
     attended, grad_queries = place_heads(me, (near_own, swap(near_other, 1), far_own, swap(far_other, 1)))
 
     grad_c = swap(grad_kv, 1)

time: 135 us -> 147 us (1.089)
  Pallas kernels: 28.8 us -> 35 us
  waiting for transfers between devices: 64 us -> 68.1 us
  starting transfers between devices: 22.6 us -> 26.1 us
  local copies, waits for them, and re-layouts: 15.2 us -> 13 us
    ppermute x16, waiting for transfers between devices: 46.1 us -> 52.5 us  [turn(): lax.ppermute(x, 'fsdp', [(CYCLE[i], CYCLE[(i + by) % fsdp]) for i in rang...]
    pallas_call x13 -> x12, Pallas kernels: 28.8 us -> 32.7 us  [call(): pl.pallas_call(body, in_specs=[pl.BlockSpec(memory_space=pltpu.SMEM)] + [...]
    unnamed x34, local copies, waits for them, and re-layouts: 15.2 us -> 11.7 us
    ppermute x11 -> x13, waiting for transfers between devices: 17.9 us -> 15.6 us  [swap(): return lax.ppermute(x, 'seq', [(i, i ^ bit) for i in range(seq)])]
    pallas_call x1, Pallas kernels: 0.01 us -> 2.3 us  [after(): pl.pallas_call(after_kernel, in_specs=[near, ANYWHERE], out_specs=near, o...]
    ppermute x11 -> x13, starting transfers between devices: 5.98 us -> 8.17 us  [swap(): return lax.ppermute(x, 'seq', [(i, i ^ bit) for i in range(seq)])]
  transfers between devices with their start and end apart: 27 -> 29, of which waited for: 15 -> 14; matrix products, arithmetic and copies ran while one was open for 1% -> 3% of each run, Pallas kernels for 19% -> 22%
where the time goes in v8:
time: 147 us
  waiting for transfers between devices  68.1 us (46%)
  Pallas kernels  35 us (24%)
  starting transfers between devices  26.1 us (18%)
  local copies, waits for them, and re-layouts  13 us (9%)
  other arithmetic  3.71 us (3%)
    ppermute x16, waiting for transfers between devices, turn(): lax.ppermute(x, 'fsdp', [(CYCLE[i], CYCLE[(i + by) % fsdp]) for i in rang...  52.5 us
    pallas_call x12, Pallas kernels, call(): pl.pallas_call(body, in_specs=[pl.BlockSpec(memory_space=pltpu.SMEM)] + [...  32.7 us
    ppermute x16, starting transfers between devices, turn(): lax.ppermute(x, 'fsdp', [(CYCLE[i], CYCLE[(i + by) % fsdp]) for i in rang...  18 us
    ppermute x13, waiting for transfers between devices, swap(): return lax.ppermute(x, 'seq', [(i, i ^ bit) for i in range(seq)])  15.6 us
    unnamed x34, local copies, waits for them, and re-layouts  11.7 us
    ppermute x13, starting transfers between devices, swap(): return lax.ppermute(x, 'seq', [(i, i ^ bit) for i in range(seq)])  8.17 us
  transfers between devices with their start and end apart: 29, of which 14 were waited for; matrix products, arithmetic and copies ran while one was open for 3% of the time, Pallas kernels for 22%

profile of v8, /device:TPU:0, one launch (start us, length us, event | category | flops | bytes accessed | tf_op | source)
XLA Modules:
  0.0 146.8 jit_solution(1276498484802992123)
XLA Ops:
  0.6 3.1 %collective-permute-start.4 = (bf16[2,448,256]{2,1,0:T(8,128)(2,1)}, bf16[2,448,256]{2,1,0:T(8,128)(2,1)S(1)}, u32[]{:S(2)}, u32[]{:S(2)}) collective-permute-start(bf16[2,448,256]{2,1,0:T(8,128)(2,1)} %refs_4_.1), channel_id=1, source_target_pairs={{0,8},{8,16},{16,24},{24,28},{28,20},{20,12},{12,4},{4,0},{1,9},{9... | collective-permute-start | bytes 1376264 | tf_op jit(solution)/shard_map/ppermute | solution.py:351
  4.5 1.2 copy-done.11
  6.5 1.6 %collective-permute-start.3 = (bf16[8,128,512]{2,1,0:T(8,128)(2,1)S(1)}, bf16[8,128,512]{2,1,0:T(8,128)(2,1)}, u32[]{:S(2)}, u32[]{:S(2)}) collective-permute-start(bf16[8,128,512]{2,1,0:T(8,128)(2,1)S(1)} %shard_map.93.refs_0_), channel_id=1, source_target_pairs={{0,2},{1,3},{2,0},{3,1},{4,6},{5,7},{6,4},{7,5},{8,10},{9,11},{10,... | collective-permute-start | bytes 3145736 | tf_op jit(solution)/shard_map/ppermute | solution.py:348
  8.1 6.2 %collective-permute-done.4.refs_5_ = bf16[2,448,256]{2,1,0:T(8,128)(2,1)S(1)} collective-permute-done((bf16[2,448,256]{2,1,0:T(8,128)(2,1)}, bf16[2,448,256]{2,1,0:T(8,128)(2,1)S(1)}, u32[]{:S(2)}, u32[]{:S(2)}) %collective-permute-start.4) | collective-permute-done | bytes 458784 | tf_op jit(solution)/shard_map/ppermute | solution.py:351
  14.4 1.8 %collective-permute-start.5 = (bf16[2,448,256]{2,1,0:T(8,128)(2,1)S(1)}, bf16[2,448,256]{2,1,0:T(8,128)(2,1)}, u32[]{:S(2)}, u32[]{:S(2)}) collective-permute-start(bf16[2,448,256]{2,1,0:T(8,128)(2,1)S(1)} %collective-permute-done.4.refs_5_), channel_id=1, source_target_pairs={{0,8},{8,16},{16,24},{24,28},{28,20},{20,12},{12,4},{4,0},{1,9},{9... | collective-permute-start | bytes 1376264 | tf_op jit(solution)/shard_map/ppermute | solution.py:351
  16.7 9.6 %collective-permute-done.5.refs_7_ = bf16[2,448,256]{2,1,0:T(8,128)(2,1)} collective-permute-done((bf16[2,448,256]{2,1,0:T(8,128)(2,1)S(1)}, bf16[2,448,256]{2,1,0:T(8,128)(2,1)}, u32[]{:S(2)}, u32[]{:S(2)}) %collective-permute-start.5) | collective-permute-done | bytes 458784 | tf_op jit(solution)/shard_map/ppermute | solution.py:351
  26.3 1.3 slice_bitcast_fusion.other_ref
  27.5 3.8 %collective-permute-done.3.x_ref = bf16[8,128,512]{2,1,0:T(8,128)(2,1)} collective-permute-done((bf16[8,128,512]{2,1,0:T(8,128)(2,1)S(1)}, bf16[8,128,512]{2,1,0:T(8,128)(2,1)}, u32[]{:S(2)}, u32[]{:S(2)}) %collective-permute-start.3) | collective-permute-done | bytes 1048608 | tf_op jit(solution)/shard_map/ppermute | solution.py:348
  31.3 2.3 %shard_map.94.refs_2_ = bf16[8,128,512]{2,1,0:T(8,128)(2,1)} custom-call(bf16[8,128,512]{2,1,0:T(8,128)(2,1)} %collective-permute-done.3.x_ref, bf16[16,128]{1,0:T(8,128)(2,1)} %slice_bitcast_fusion.other_ref), custom_call_target="tpu_custom_call" | custom-call | bytes 3000000 | tf_op jit(solution)/shard_map/pallas_call | solution.py:64
  34.4 1.8 %collective-permute-start.7 = (bf16[2,448,256]{2,1,0:T(8,128)(2,1)}, bf16[2,448,256]{2,1,0:T(8,128)(2,1)S(1)}, u32[]{:S(2)}, u32[]{:S(2)}) collective-permute-start(bf16[2,448,256]{2,1,0:T(8,128)(2,1)} %collective-permute-done.5.refs_7_), channel_id=1, source_target_pairs={{0,8},{8,16},{16,24},{24,28},{28,20},{20,12},{12,4},{4,0},{1,9},{9... | collective-permute-start | bytes 1376264 | tf_op jit(solution)/shard_map/ppermute | solution.py:351
  36.2 10.6 %collective-permute-done.9.refs_8_ = bf16[2,448,256]{2,1,0:T(8,128)(2,1)S(1)} collective-permute-done((bf16[2,448,256]{2,1,0:T(8,128)(2,1)}, bf16[2,448,256]{2,1,0:T(8,128)(2,1)S(1)}, u32[]{:S(2)}, u32[]{:S(2)}) %collective-permute-start.9) | collective-permute-done | bytes 458784 | tf_op jit(solution)/shard_map/ppermute | solution.py:351
  47.1 0.9 copy-done.4
  48.0 0.9 copy-done.6
  48.9 1.2 copy-done
  50.1 1.0 copy-done.12
  51.2 1.0 copy-done.14
  52.2 4.3 %shard_map.95 = (f32[512,512]{1,0:T(8,128)S(1)}, bf16[8,2,448,256]{3,2,1,0:T(8,128)(2,1)}) custom-call(s32[3]{0:T(128)S(1)} %pad_add_fusion.me_ref, bf16[8,128,512]{2,1,0:T(8,128)(2,1)S(1)} %shard_map.93.refs_0_, bf16[8,128,512]{2,1,0:T(8,128)(2,1)S(1)} %collective-permute-done.2.refs_1_, bf16[8,128,512]{2,1,0:T(8,128)(2,1)S(1)} %copy-done, ...), custom_call_target="tpu_custom_call" | custom-call | bytes 9000000 | tf_op jit(solution)/shard_map/pallas_call | solution.py:36
  56.5 1.9 %collective-permute-done.10.downs_ref.refs_5_ = bf16[2,448,256]{2,1,0:T(8,128)(2,1)S(1)} collective-permute-done((bf16[2,448,256]{2,1,0:T(8,128)(2,1)S(1)}, bf16[2,448,256]{2,1,0:T(8,128)(2,1)S(1)}, u32[]{:S(2)}, u32[]{:S(2)}) %collective-permute-start.10) | collective-permute-done | bytes 458784 | tf_op jit(solution)/shard_map/ppermute | solution.py:351
  58.9 1.6 %collective-permute-start.11 = (bf16[1,448,256]{2,1,0:T(8,128)(2,1)S(1)}, bf16[1,448,256]{2,1,0:T(8,128)(2,1)S(1)}, u32[]{:S(2)}, u32[]{:S(2)}) collective-permute-start(bf16[1,448,256]{2,1,0:T(8,128)(2,1)S(1)} %get-tuple-element.37), channel_id=1, source_target_pairs={{0,8},{8,16},{16,24},{24,28},{28,20},{20,12},{12,4},{4,0},{1,9},{9... | collective-permute-start | bytes 688136 | tf_op jit(solution)/shard_map/ppermute | solution.py:351
  61.0 1.7 %shard_map.97 = (f32[512,512]{1,0:T(8,128)S(1)}, bf16[8,2,448,256]{3,2,1,0:T(8,128)(2,1)}) custom-call(s32[3]{0:T(128)S(1)} %pad_add_fusion.me_ref, bf16[8,128,512]{2,1,0:T(8,128)(2,1)S(1)} %shard_map.93.refs_0_, bf16[8,128,512]{2,1,0:T(8,128)(2,1)S(1)} %collective-permute-done.2.refs_1_, ...), custom_call_target="tpu_custom_call", output_to_operand_aliasing={{1}: (8, {})} | custom-call | bytes 9000000 | tf_op jit(solution)/shard_map/pallas_call | solution.py:36
  62.7 2.3 %collective-permute-done.11.refs_4_ = bf16[1,448,256]{2,1,0:T(8,128)(2,1)S(1)} collective-permute-done((bf16[1,448,256]{2,1,0:T(8,128)(2,1)S(1)}, bf16[1,448,256]{2,1,0:T(8,128)(2,1)S(1)}, u32[]{:S(2)}, u32[]{:S(2)}) %collective-permute-start.11) | collective-permute-done | bytes 229408 | tf_op jit(solution)/shard_map/ppermute | solution.py:351
  65.0 1.6 %collective-permute-done.12.refs_5_ = bf16[1,448,256]{2,1,0:T(8,128)(2,1)S(1)} collective-permute-done((bf16[1,448,256]{2,1,0:T(8,128)(2,1)S(1)}, bf16[1,448,256]{2,1,0:T(8,128)(2,1)S(1)}, u32[]{:S(2)}, u32[]{:S(2)}) %collective-permute-start.12) | collective-permute-done | bytes 229408 | tf_op jit(solution)/shard_map/ppermute | solution.py:351
  66.6 2.5 %shard_map.98 = (bf16[512,256]{1,0:T(8,128)(2,1)}, f32[512,1]{1,0:T(8,128)S(1)}, f32[512,1]{1,0:T(8,128)S(1)}, f32[1,512]{1,0:T(1,128)S(1)}, bf16[8,2,448,256]{3,2,1,0:T(8,128)(2,1)}) custom-call(s32[3]{0:T(128)S(1)} %pad_add_fusion.me_ref, bf16[8,128,512]{2,1,0:T(8,128)(2,1)S(1)} %shard_map.93.refs_0_, ...), custom_call_target="tpu_custom_call", output_to_operand_aliasing={{4}: (8, {})} | custom-call | bytes 9000000 | tf_op jit(solution)/shard_map/pallas_call | solution.py:36
  69.8 1.5 %collective-permute-start.13 = (bf16[512,256]{1,0:T(8,128)(2,1)}, bf16[512,256]{1,0:T(8,128)(2,1)}, u32[]{:S(2)}, u32[]{:S(2)}) collective-permute-start(bf16[512,256]{1,0:T(8,128)(2,1)} %get-tuple-element.42.kv_ref), channel_id=1, source_target_pairs={{0,2},{1,3},{2,0},{3,1},{4,6},{5,7},{6,4},{7,5},{8,10},{9,11},{10,... | collective-permute-start | bytes 786440 | tf_op jit(solution)/shard_map/ppermute | solution.py:348
  71.4 7.4 %collective-permute-done.13.kv_ref = bf16[512,256]{1,0:T(8,128)(2,1)} collective-permute-done((bf16[512,256]{1,0:T(8,128)(2,1)}, bf16[512,256]{1,0:T(8,128)(2,1)}, u32[]{:S(2)}, u32[]{:S(2)}) %collective-permute-start.13) | collective-permute-done | bytes 262176 | tf_op jit(solution)/shard_map/ppermute | solution.py:348
  78.8 1.2 copy-done.5
  80.0 1.2 copy-done.7
  81.2 1.2 copy-done.8
  82.4 1.2 copy-done.9
  83.5 5.2 %shard_map.99 = (bf16[2,128,896]{2,1,0:T(8,128)(2,1)S(1)}, bf16[2,128,896]{2,1,0:T(8,128)(2,1)S(1)}, f32[256,256]{1,0:T(8,128)S(1)}, bf16[256,256]{1,0:T(8,128)(2,1)S(1)}) custom-call(s32[3]{0:T(128)S(1)} %pad_add_fusion.2.me_ref, bf16[128,3584]{1,0:T(8,128)(2,1)S(1)} %bitcast.13, bf16[128,3584]{1,0:T(8,128)(2,1)S(1)} %bitcast.16, ...), custom_call_target="tpu_custom_call" | custom-call | bytes 18000000 | tf_op jit(solution)/shard_map/pallas_call | solution.py:36
  88.7 1.6 %collective-permute-start.17 = (bf16[256,256]{1,0:T(8,128)(2,1)S(1)}, bf16[256,256]{1,0:T(8,128)(2,1)S(1)}, u32[]{:S(2)}, u32[]{:S(2)}) collective-permute-start(bf16[256,256]{1,0:T(8,128)(2,1)S(1)} %get-tuple-element.55), channel_id=1, source_target_pairs={{0,2},{1,3},{2,0},{3,1},{4,6},{5,7},{6,4},{7,5},{8,10},{9,11},{10,... | collective-permute-start | bytes 393224 | tf_op jit(solution)/shard_map/ppermute | solution.py:348
  90.8 5.1 %shard_map.100 = (bf16[2,128,896]{2,1,0:T(8,128)(2,1)S(1)}, bf16[2,128,896]{2,1,0:T(8,128)(2,1)S(1)}, f32[256,256]{1,0:T(8,128)S(1)}, f32[256,256]{1,0:T(8,128)S(1)}) custom-call(s32[3]{0:T(128)S(1)} %pad_add_fusion.me_ref, bf16[128,3584]{1,0:T(8,128)(2,1)S(1)} %bitcast.14, bf16[128,3584]{1,0:T(8,128)(2,1)S(1)} %bitcast.17, bf16[128,3584]{1,0:T(8,128)(2,1)S(1)} %copy-done.5, ...), custom_call_target="tpu_custom_call" | custom-call | bytes 18000000 | tf_op jit(solution)/shard_map/pallas_call | solution.py:36
  95.9 3.6 %collective-permute-done.16 = f32[256,256]{1,0:T(8,128)S(1)} collective-permute-done((f32[256,256]{1,0:T(8,128)S(1)}, f32[256,256]{1,0:T(8,128)S(1)}, u32[]{:S(2)}, u32[]{:S(2)}) %collective-permute-start.16) | collective-permute-done | bytes 262176 | tf_op jit(solution)/shard_map/ppermute | solution.py:348
  99.7 1.3 shard_map.105
  101.4 1.6 %collective-permute-start.21 = (bf16[1,448,256]{2,1,0:T(8,128)(2,1)S(1)}, bf16[1,448,256]{2,1,0:T(8,128)(2,1)S(1)}, u32[]{:S(2)}, u32[]{:S(2)}) collective-permute-start(bf16[1,448,256]{2,1,0:T(8,128)(2,1)S(1)} %get-tuple-element.63), channel_id=1, source_target_pairs={{0,8},{8,16},{16,24},{24,28},{28,20},{20,12},{12,4},{4,0},{1,9},{9... | collective-permute-start | bytes 688136 | tf_op jit(solution)/shard_map/ppermute | solution.py:351
  103.0 5.5 %shard_map.102 = (f32[128,3584]{1,0:T(8,128)S(1)}, bf16[128,3584]{1,0:T(8,128)(2,1)S(1)}) custom-call(s32[3]{0:T(128)S(1)} %pad_add_fusion.me_ref, f32[512,1]{1,0:T(8,128)S(1)} %copy-done.16, bf16[512,256]{1,0:T(8,128)(2,1)S(1)} %pad_maximum_fusion.g_ref.refs_4_, bf16[512,256]{1,0:T(8,128)(2,1)S(1)} %collective-permute-done.18.gc_ref, ...), custom_call_target="tpu_custom_call" | custom-call | bytes 21000000 | tf_op jit(solution)/shard_map/pallas_call | solution.py:36
  108.6 1.5 %shard_map.104 = (f32[2,448,256]{2,1,0:T(8,128)S(1)}, f32[2,448,256]{2,1,0:T(8,128)S(1)}) custom-call(s32[3]{0:T(128)S(1)} %pad_add_fusion.me_ref, bf16[8,128,512]{2,1,0:T(8,128)(2,1)S(1)} %shard_map.93.refs_0_, bf16[8,128,512]{2,1,0:T(8,128)(2,1)S(1)} %collective-permute-done.2.refs_1_, bf16[8,128,512]{2,1,0:T(8,128)(2,1)S(1)} %copy-done.1, ...), custom_call_target="tpu_custom_call" | custom-call | bytes 9000000 | tf_op jit(solution)/shard_map/pallas_call | solution.py:36
  110.8 1.6 %collective-permute-start.22 = (bf16[2,448,256]{2,1,0:T(8,128)(2,1)S(1)}, bf16[2,448,256]{2,1,0:T(8,128)(2,1)S(1)}, u32[]{:S(2)}, u32[]{:S(2)}) collective-permute-start(bf16[2,448,256]{2,1,0:T(8,128)(2,1)S(1)} %add_convert_fusion.6), channel_id=1, source_target_pairs={{0,8},{8,16},{16,24},{24,28},{28,20},{20,12},{12,4},{4,0},{1,9},{9... | collective-permute-start | bytes 1376264 | tf_op jit(solution)/shard_map/ppermute | solution.py:351
  112.9 2.3 %shard_map.103 = (f32[2,448,256]{2,1,0:T(8,128)S(1)}, f32[2,448,256]{2,1,0:T(8,128)S(1)}, f32[2,448,256]{2,1,0:T(8,128)S(1)}, f32[2,448,256]{2,1,0:T(8,128)S(1)}, f32[2,448,256]{2,1,0:T(8,128)S(1)}) custom-call(s32[3]{0:T(128)S(1)} %pad_add_fusion.me_ref, bf16[8,128,512]{2,1,0:T(8,128)(2,1)S(1)} %shard_map.93.refs_0_, ...), custom_call_target="tpu_custom_call" | custom-call | bytes 18000000 | tf_op jit(solution)/shard_map/pallas_call | solution.py:36
  115.3 1.6 %collective-permute-start.20 = (bf16[128,3584]{1,0:T(8,128)(2,1)S(1)}, bf16[128,3584]{1,0:T(8,128)(2,1)S(1)}, u32[]{:S(2)}, u32[]{:S(2)}) collective-permute-start(bf16[128,3584]{1,0:T(8,128)(2,1)S(1)} %get-tuple-element.58.refs_5_), channel_id=1, source_target_pairs={{0,2},{1,3},{2,0},{3,1},{4,6},{5,7},{6,4},{7,5},{8,10},{9,11},{10,... | collective-permute-start | bytes 2752520 | tf_op jit(solution)/shard_map/ppermute | solution.py:348
  116.9 5.9 %collective-permute-done.26 = bf16[2,448,256]{2,1,0:T(8,128)(2,1)S(1)} collective-permute-done((bf16[2,448,256]{2,1,0:T(8,128)(2,1)S(1)}, bf16[2,448,256]{2,1,0:T(8,128)(2,1)S(1)}, u32[]{:S(2)}, u32[]{:S(2)}) %collective-permute-start.26) | collective-permute-done | bytes 458784 | tf_op jit(solution)/shard_map/ppermute | solution.py:351
  123.4 1.6 %collective-permute-start.23 = (bf16[2,448,256]{2,1,0:T(8,128)(2,1)S(1)}, bf16[2,448,256]{2,1,0:T(8,128)(2,1)S(1)}, u32[]{:S(2)}, u32[]{:S(2)}) collective-permute-start(bf16[2,448,256]{2,1,0:T(8,128)(2,1)S(1)} %add_convert_fusion.5), channel_id=1, source_target_pairs={{0,8},{8,16},{16,24},{24,28},{28,20},{20,12},{12,4},{4,0},{1,9},{9... | collective-permute-start | bytes 1376264 | tf_op jit(solution)/shard_map/ppermute | solution.py:351
  125.1 1.9 %shard_map.101 = (bf16[128,3584]{1,0:T(8,128)(2,1)}, bf16[128,3584]{1,0:T(8,128)(2,1)}) custom-call(s32[3]{0:T(128)S(1)} %pad_add_fusion.me_ref, bf16[2,128,896]{2,1,0:T(8,128)(2,1)S(1)} %get-tuple-element.46.refs_0_, bf16[2,128,896]{2,1,0:T(8,128)(2,1)S(1)} %collective-permute-done.14.refs_1_, bf16[2,128,896]{2,1,0:T(8,128)(2,1)S(1)} %get-tuple-element.48.refs_2_, ...), custom_call_target="tpu_custom_call" | custom-call | bytes 9000000 | tf_op jit(solution)/shard_map/pallas_call | solution.py:36
  127.0 7.5 %collective-permute-done.27 = bf16[2,448,256]{2,1,0:T(8,128)(2,1)S(1)} collective-permute-done((bf16[2,448,256]{2,1,0:T(8,128)(2,1)S(1)}, bf16[2,448,256]{2,1,0:T(8,128)(2,1)S(1)}, u32[]{:S(2)}, u32[]{:S(2)}) %collective-permute-start.27) | collective-permute-done | bytes 458784 | tf_op jit(solution)/shard_map/ppermute | solution.py:351
  135.2 1.6 %collective-permute-start.24 = (bf16[2,448,256]{2,1,0:T(8,128)(2,1)S(1)}, bf16[2,448,256]{2,1,0:T(8,128)(2,1)S(1)}, u32[]{:S(2)}, u32[]{:S(2)}) collective-permute-start(bf16[2,448,256]{2,1,0:T(8,128)(2,1)S(1)} %add_convert_fusion.4), channel_id=1, source_target_pairs={{0,8},{8,16},{16,24},{24,28},{28,20},{20,12},{12,4},{4,0},{1,9},{9... | collective-permute-start | bytes 1376264 | tf_op jit(solution)/shard_map/ppermute | solution.py:351
  137.6 1.1 fusion
  138.8 6.6 %collective-permute-done.28 = bf16[2,448,256]{2,1,0:T(8,128)(2,1)S(1)} collective-permute-done((bf16[2,448,256]{2,1,0:T(8,128)(2,1)S(1)}, bf16[2,448,256]{2,1,0:T(8,128)(2,1)S(1)}, u32[]{:S(2)}, u32[]{:S(2)}) %collective-permute-start.28) | collective-permute-done | bytes 458784 | tf_op jit(solution)/shard_map/ppermute | solution.py:351
  145.7 1.1 convert_add_fusion
  (74 shorter events, 9.9 us)
Async XLA Ops:
  0.6 13.7 %collective-permute-start.4 = (bf16[2,448,256]{2,1,0:T(8,128)(2,1)}, bf16[2,448,256]{2,1,0:T(8,128)(2,1)S(1)}, u32[]{:S(2)}, u32[]{:S(2)}) collective-permute-start(bf16[2,448,256]{2,1,0:T(8,128)(2,1)} %refs_4_.1), channel_id=1, source_target_pairs={{0,8},{8,16},{16,24},{24,28},{28,20},{20,12},{12,4},{4,0},{1,9},{9... | collective-permute-start | bytes 1376264 | tf_op jit(solution)/shard_map/ppermute | solution.py:351
  4.5 1.2 copy-start.11
  6.5 24.8 %collective-permute-start.3 = (bf16[8,128,512]{2,1,0:T(8,128)(2,1)S(1)}, bf16[8,128,512]{2,1,0:T(8,128)(2,1)}, u32[]{:S(2)}, u32[]{:S(2)}) collective-permute-start(bf16[8,128,512]{2,1,0:T(8,128)(2,1)S(1)} %shard_map.93.refs_0_), channel_id=1, source_target_pairs={{0,2},{1,3},{2,0},{3,1},{4,6},{5,7},{6,4},{7,5},{8,10},{9,11},{10,... | collective-permute-start | bytes 3145736 | tf_op jit(solution)/shard_map/ppermute | solution.py:348
  14.4 34.6 %copy-start.13 = (bf16[2,448,256]{2,1,0:T(8,128)(2,1)}, bf16[2,448,256]{2,1,0:T(8,128)(2,1)S(1)}, u32[]{:S(2)}) copy-start(bf16[2,448,256]{2,1,0:T(8,128)(2,1)S(1)} %collective-permute-done.4.refs_5_) | copy-start | bytes 1376260
  14.4 11.9 %collective-permute-start.5 = (bf16[2,448,256]{2,1,0:T(8,128)(2,1)S(1)}, bf16[2,448,256]{2,1,0:T(8,128)(2,1)}, u32[]{:S(2)}, u32[]{:S(2)}) collective-permute-start(bf16[2,448,256]{2,1,0:T(8,128)(2,1)S(1)} %collective-permute-done.4.refs_5_), channel_id=1, source_target_pairs={{0,8},{8,16},{16,24},{24,28},{28,20},{20,12},{12,4},{4,0},{1,9},{9... | collective-permute-start | bytes 1376264 | tf_op jit(solution)/shard_map/ppermute | solution.py:351
  16.2 18.2 %collective-permute-start = (bf16[128,3584]{1,0:T(8,128)(2,1)}, bf16[128,3584]{1,0:T(8,128)(2,1)S(1)}, u32[]{:S(2)}, u32[]{:S(2)}) collective-permute-start(bf16[128,3584]{1,0:T(8,128)(2,1)} %bitcast.12), channel_id=1, source_target_pairs={{0,1},{1,0},{2,3},{3,2},{4,5},{5,4},{6,7},{7,6},{8,9},{9,8},{10,11... | collective-permute-start | bytes 2752520 | tf_op jit(solution)/shard_map/ppermute | solution.py:348
  16.2 17.9 %collective-permute-start.8 = (bf16[2,448,256]{2,1,0:T(8,128)(2,1)}, bf16[2,448,256]{2,1,0:T(8,128)(2,1)}, u32[]{:S(2)}, u32[]{:S(2)}) collective-permute-start(bf16[2,448,256]{2,1,0:T(8,128)(2,1)} %refs_4_.1), channel_id=1, source_target_pairs={{0,4},{8,0},{16,8},{24,16},{28,24},{20,28},{12,20},{4,12},{1,5},{9... | collective-permute-start | bytes 1376264 | tf_op jit(solution)/shard_map/ppermute | solution.py:351
  16.4 32.5 %collective-permute-start.2 = (bf16[8,128,512]{2,1,0:T(8,128)(2,1)S(1)}, bf16[8,128,512]{2,1,0:T(8,128)(2,1)S(1)}, u32[]{:S(2)}, u32[]{:S(2)}) collective-permute-start(bf16[8,128,512]{2,1,0:T(8,128)(2,1)S(1)} %shard_map.93.refs_0_), channel_id=1, source_target_pairs={{0,1},{1,0},{2,3},{3,2},{4,5},{5,4},{6,7},{7,6},{8,9},{9,8},{10,11... | collective-permute-start | bytes 3145736 | tf_op jit(solution)/shard_map/ppermute | solution.py:348
  33.6 15.3 %collective-permute-start.6 = (bf16[8,128,512]{2,1,0:T(8,128)(2,1)}, bf16[8,128,512]{2,1,0:T(8,128)(2,1)S(1)}, u32[]{:S(2)}, u32[]{:S(2)}) collective-permute-start(bf16[8,128,512]{2,1,0:T(8,128)(2,1)} %shard_map.94.refs_2_), channel_id=1, source_target_pairs={{0,1},{1,0},{2,3},{3,2},{4,5},{5,4},{6,7},{7,6},{8,9},{9,8},{10,11... | collective-permute-start | bytes 3145736 | tf_op jit(solution)/shard_map/ppermute | solution.py:348
  33.6 14.4 %collective-permute-start.1 = (bf16[128,3584]{1,0:T(8,128)(2,1)}, bf16[128,3584]{1,0:T(8,128)(2,1)S(1)}, u32[]{:S(2)}, u32[]{:S(2)}) collective-permute-start(bf16[128,3584]{1,0:T(8,128)(2,1)} %bitcast.15), channel_id=1, source_target_pairs={{0,1},{1,0},{2,3},{3,2},{4,5},{5,4},{6,7},{7,6},{8,9},{9,8},{10,11... | collective-permute-start | bytes 2752520 | tf_op jit(solution)/shard_map/ppermute | solution.py:348
  34.1 12.6 %collective-permute-start.9 = (bf16[2,448,256]{2,1,0:T(8,128)(2,1)}, bf16[2,448,256]{2,1,0:T(8,128)(2,1)S(1)}, u32[]{:S(2)}, u32[]{:S(2)}) collective-permute-start(bf16[2,448,256]{2,1,0:T(8,128)(2,1)} %collective-permute-done.8.refs_6_), channel_id=1, source_target_pairs={{0,4},{8,0},{16,8},{24,16},{28,24},{20,28},{12,20},{4,12},{1,5},{9... | collective-permute-start | bytes 1376264 | tf_op jit(solution)/shard_map/ppermute | solution.py:351
  34.4 22.1 %collective-permute-start.7 = (bf16[2,448,256]{2,1,0:T(8,128)(2,1)}, bf16[2,448,256]{2,1,0:T(8,128)(2,1)S(1)}, u32[]{:S(2)}, u32[]{:S(2)}) collective-permute-start(bf16[2,448,256]{2,1,0:T(8,128)(2,1)} %collective-permute-done.5.refs_7_), channel_id=1, source_target_pairs={{0,8},{8,16},{16,24},{24,28},{28,20},{20,12},{12,4},{4,0},{1,9},{9... | collective-permute-start | bytes 1376264 | tf_op jit(solution)/shard_map/ppermute | solution.py:351
  46.8 11.6 %collective-permute-start.10 = (bf16[2,448,256]{2,1,0:T(8,128)(2,1)S(1)}, bf16[2,448,256]{2,1,0:T(8,128)(2,1)S(1)}, u32[]{:S(2)}, u32[]{:S(2)}) collective-permute-start(bf16[2,448,256]{2,1,0:T(8,128)(2,1)S(1)} %collective-permute-done.9.refs_8_), channel_id=1, source_target_pairs={{0,4},{8,0},{16,8},{24,16},{28,24},{20,28},{12,20},{4,12},{1,5},{9... | collective-permute-start | bytes 1376264 | tf_op jit(solution)/shard_map/ppermute | solution.py:351
  47.1 0.9 copy-start.4
  48.0 0.9 copy-start.6
  48.9 1.2 copy-start
  50.1 1.0 copy-start.12
  51.2 1.0 copy-start.14
  52.2 14.4 %copy-start.2 = (bf16[8,128,512]{2,1,0:T(8,128)(2,1)}, bf16[8,128,512]{2,1,0:T(8,128)(2,1)S(1)}, u32[]{:S(2)}) copy-start(bf16[8,128,512]{2,1,0:T(8,128)(2,1)S(1)} %collective-permute-done.6.refs_3_) | copy-start | bytes 3145732
  52.2 8.8 %copy-start.1 = (bf16[8,128,512]{2,1,0:T(8,128)(2,1)S(1)}, bf16[8,128,512]{2,1,0:T(8,128)(2,1)}, u32[]{:S(2)}) copy-start(bf16[8,128,512]{2,1,0:T(8,128)(2,1)} %shard_map.94.refs_2_) | copy-start | bytes 3145732
  58.9 6.1 %collective-permute-start.11 = (bf16[1,448,256]{2,1,0:T(8,128)(2,1)S(1)}, bf16[1,448,256]{2,1,0:T(8,128)(2,1)S(1)}, u32[]{:S(2)}, u32[]{:S(2)}) collective-permute-start(bf16[1,448,256]{2,1,0:T(8,128)(2,1)S(1)} %get-tuple-element.37), channel_id=1, source_target_pairs={{0,8},{8,16},{16,24},{24,28},{28,20},{20,12},{12,4},{4,0},{1,9},{9... | collective-permute-start | bytes 688136 | tf_op jit(solution)/shard_map/ppermute | solution.py:351
  60.6 6.0 %collective-permute-start.12 = (bf16[1,448,256]{2,1,0:T(8,128)(2,1)S(1)}, bf16[1,448,256]{2,1,0:T(8,128)(2,1)S(1)}, u32[]{:S(2)}, u32[]{:S(2)}) collective-permute-start(bf16[1,448,256]{2,1,0:T(8,128)(2,1)S(1)} %get-tuple-element.38), channel_id=1, source_target_pairs={{0,4},{8,0},{16,8},{24,16},{28,24},{20,28},{12,20},{4,12},{1,5},{9... | collective-permute-start | bytes 688136 | tf_op jit(solution)/shard_map/ppermute | solution.py:351
  69.1 0.7 copy-start.15
  69.8 33.2 %collective-permute-start.19 = (bf16[8,2,448,256]{3,2,1,0:T(8,128)(2,1)}, bf16[8,2,448,256]{3,2,1,0:T(8,128)(2,1)}, u32[]{:S(2)}, u32[]{:S(2)}) collective-permute-start(bf16[8,2,448,256]{3,2,1,0:T(8,128)(2,1)} %get-tuple-element.56.w_ref), channel_id=1, source_target_pairs={{0,1},{1,0},{2,3},{3,2},{4,5},{5,4},{6,7},{7,6},{8,9},{9,8},{10,11... | collective-permute-start | bytes 11010056 | tf_op jit(solution)/shard_map/ppermute | solution.py:348
  69.8 9.0 %collective-permute-start.13 = (bf16[512,256]{1,0:T(8,128)(2,1)}, bf16[512,256]{1,0:T(8,128)(2,1)}, u32[]{:S(2)}, u32[]{:S(2)}) collective-permute-start(bf16[512,256]{1,0:T(8,128)(2,1)} %get-tuple-element.42.kv_ref), channel_id=1, source_target_pairs={{0,2},{1,3},{2,0},{3,1},{4,6},{5,7},{6,4},{7,5},{8,10},{9,11},{10,... | collective-permute-start | bytes 786440 | tf_op jit(solution)/shard_map/ppermute | solution.py:348
  78.8 1.2 copy-start.5
  80.0 1.2 copy-start.7
  81.2 1.2 copy-start.8
  82.4 1.2 copy-start.9
  83.5 7.3 %copy-start.10 = (bf16[1,128,3584]{2,1,0:T(8,128)(2,1)S(1)}, bf16[1,128,3584]{2,1,0:T(8,128)(2,1)}, u32[]{:S(2)}) copy-start(bf16[1,128,3584]{2,1,0:T(8,128)(2,1)} %param.8) | copy-start | bytes 2752516
  88.7 11.0 %copy-start.3 = (bf16[8,128,512]{2,1,0:T(8,128)(2,1)S(1)}, bf16[8,128,512]{2,1,0:T(8,128)(2,1)}, u32[]{:S(2)}) copy-start(bf16[8,128,512]{2,1,0:T(8,128)(2,1)} %copy-done.2) | copy-start | bytes 3145732
  88.7 7.2 %collective-permute-start.17 = (bf16[256,256]{1,0:T(8,128)(2,1)S(1)}, bf16[256,256]{1,0:T(8,128)(2,1)S(1)}, u32[]{:S(2)}, u32[]{:S(2)}) collective-permute-start(bf16[256,256]{1,0:T(8,128)(2,1)S(1)} %get-tuple-element.55), channel_id=1, source_target_pairs={{0,2},{1,3},{2,0},{3,1},{4,6},{5,7},{6,4},{7,5},{8,10},{9,11},{10,... | collective-permute-start | bytes 393224 | tf_op jit(solution)/shard_map/ppermute | solution.py:348
  90.3 9.2 %collective-permute-start.16 = (f32[256,256]{1,0:T(8,128)S(1)}, f32[256,256]{1,0:T(8,128)S(1)}, u32[]{:S(2)}, u32[]{:S(2)}) collective-permute-start(f32[256,256]{1,0:T(8,128)S(1)} %get-tuple-element.45.refs_0_), channel_id=1, source_target_pairs={{0,2},{1,3},{2,0},{3,1},{4,6},{5,7},{6,4},{7,5},{8,10},{9,11},{10,... | collective-permute-start | bytes 786440 | tf_op jit(solution)/shard_map/ppermute | solution.py:348
  95.9 7.1 %copy-start.16 = (f32[512,1]{1,0:T(8,128)S(1)}, f32[512,1]{1,0:T(8,128)}, u32[]{:S(2)}) copy-start(f32[512,1]{1,0:T(8,128)} %copy-done.15) | copy-start | bytes 6148
  99.6 3.4 %collective-permute-start.18 = (bf16[512,256]{1,0:T(8,128)(2,1)S(1)}, bf16[512,256]{1,0:T(8,128)(2,1)S(1)}, u32[]{:S(2)}, u32[]{:S(2)}) collective-permute-start(bf16[512,256]{1,0:T(8,128)(2,1)S(1)} %pad_maximum_fusion.g_ref.refs_4_), channel_id=1, source_target_pairs={{0,1},{1,0},{2,3},{3,2},{4,5},{5,4},{6,7},{7,6},{8,9},{9,8},{10,11... | collective-permute-start | bytes 786440 | tf_op jit(solution)/shard_map/ppermute | solution.py:348
  100.9 9.2 %collective-permute-start.25 = (bf16[1,448,256]{2,1,0:T(8,128)(2,1)S(1)}, bf16[1,448,256]{2,1,0:T(8,128)(2,1)S(1)}, u32[]{:S(2)}, u32[]{:S(2)}) collective-permute-start(bf16[1,448,256]{2,1,0:T(8,128)(2,1)S(1)} %get-tuple-element.67), channel_id=1, source_target_pairs={{0,4},{8,0},{16,8},{24,16},{28,24},{20,28},{12,20},{4,12},{1,5},{9... | collective-permute-start | bytes 688136 | tf_op jit(solution)/shard_map/ppermute | solution.py:351
  101.4 9.3 %collective-permute-start.21 = (bf16[1,448,256]{2,1,0:T(8,128)(2,1)S(1)}, bf16[1,448,256]{2,1,0:T(8,128)(2,1)S(1)}, u32[]{:S(2)}, u32[]{:S(2)}) collective-permute-start(bf16[1,448,256]{2,1,0:T(8,128)(2,1)S(1)} %get-tuple-element.63), channel_id=1, source_target_pairs={{0,8},{8,16},{16,24},{24,28},{28,20},{20,12},{12,4},{4,0},{1,9},{9... | collective-permute-start | bytes 688136 | tf_op jit(solution)/shard_map/ppermute | solution.py:351
  110.2 12.5 %collective-permute-start.26 = (bf16[2,448,256]{2,1,0:T(8,128)(2,1)S(1)}, bf16[2,448,256]{2,1,0:T(8,128)(2,1)S(1)}, u32[]{:S(2)}, u32[]{:S(2)}) collective-permute-start(bf16[2,448,256]{2,1,0:T(8,128)(2,1)S(1)} %add_convert_fusion.3), channel_id=1, source_target_pairs={{0,4},{8,0},{16,8},{24,16},{28,24},{20,28},{12,20},{4,12},{1,5},{9... | collective-permute-start | bytes 1376264 | tf_op jit(solution)/shard_map/ppermute | solution.py:351
  110.8 12.5 %collective-permute-start.22 = (bf16[2,448,256]{2,1,0:T(8,128)(2,1)S(1)}, bf16[2,448,256]{2,1,0:T(8,128)(2,1)S(1)}, u32[]{:S(2)}, u32[]{:S(2)}) collective-permute-start(bf16[2,448,256]{2,1,0:T(8,128)(2,1)S(1)} %add_convert_fusion.6), channel_id=1, source_target_pairs={{0,8},{8,16},{16,24},{24,28},{28,20},{20,12},{12,4},{4,0},{1,9},{9... | collective-permute-start | bytes 1376264 | tf_op jit(solution)/shard_map/ppermute | solution.py:351
  112.4 12.6 %collective-permute-start.14 = (bf16[2,128,896]{2,1,0:T(8,128)(2,1)S(1)}, bf16[2,128,896]{2,1,0:T(8,128)(2,1)S(1)}, u32[]{:S(2)}, u32[]{:S(2)}) collective-permute-start(bf16[2,128,896]{2,1,0:T(8,128)(2,1)S(1)} %get-tuple-element.47), channel_id=1, source_target_pairs={{0,1},{1,0},{2,3},{3,2},{4,5},{5,4},{6,7},{7,6},{8,9},{9,8},{10,11... | collective-permute-start | bytes 1376264 | tf_op jit(solution)/shard_map/ppermute | solution.py:348
  112.4 12.6 %collective-permute-start.15 = (bf16[2,128,896]{2,1,0:T(8,128)(2,1)S(1)}, bf16[2,128,896]{2,1,0:T(8,128)(2,1)S(1)}, u32[]{:S(2)}, u32[]{:S(2)}) collective-permute-start(bf16[2,128,896]{2,1,0:T(8,128)(2,1)S(1)} %get-tuple-element.49), channel_id=1, source_target_pairs={{0,1},{1,0},{2,3},{3,2},{4,5},{5,4},{6,7},{7,6},{8,9},{9,8},{10,11... | collective-permute-start | bytes 1376264 | tf_op jit(solution)/shard_map/ppermute | solution.py:348
  115.3 22.3 %collective-permute-start.20 = (bf16[128,3584]{1,0:T(8,128)(2,1)S(1)}, bf16[128,3584]{1,0:T(8,128)(2,1)S(1)}, u32[]{:S(2)}, u32[]{:S(2)}) collective-permute-start(bf16[128,3584]{1,0:T(8,128)(2,1)S(1)} %get-tuple-element.58.refs_5_), channel_id=1, source_target_pairs={{0,2},{1,3},{2,0},{3,1},{4,6},{5,7},{6,4},{7,5},{8,10},{9,11},{10,... | collective-permute-start | bytes 2752520 | tf_op jit(solution)/shard_map/ppermute | solution.py:348
  122.8 11.7 %collective-permute-start.27 = (bf16[2,448,256]{2,1,0:T(8,128)(2,1)S(1)}, bf16[2,448,256]{2,1,0:T(8,128)(2,1)S(1)}, u32[]{:S(2)}, u32[]{:S(2)}) collective-permute-start(bf16[2,448,256]{2,1,0:T(8,128)(2,1)S(1)} %add_convert_fusion.2), channel_id=1, source_target_pairs={{0,4},{8,0},{16,8},{24,16},{28,24},{20,28},{12,20},{4,12},{1,5},{9... | collective-permute-start | bytes 1376264 | tf_op jit(solution)/shard_map/ppermute | solution.py:351
  123.4 11.7 %collective-permute-start.23 = (bf16[2,448,256]{2,1,0:T(8,128)(2,1)S(1)}, bf16[2,448,256]{2,1,0:T(8,128)(2,1)S(1)}, u32[]{:S(2)}, u32[]{:S(2)}) collective-permute-start(bf16[2,448,256]{2,1,0:T(8,128)(2,1)S(1)} %add_convert_fusion.5), channel_id=1, source_target_pairs={{0,8},{8,16},{16,24},{24,28},{28,20},{20,12},{12,4},{4,0},{1,9},{9... | collective-permute-start | bytes 1376264 | tf_op jit(solution)/shard_map/ppermute | solution.py:351
  134.6 10.8 %collective-permute-start.28 = (bf16[2,448,256]{2,1,0:T(8,128)(2,1)S(1)}, bf16[2,448,256]{2,1,0:T(8,128)(2,1)S(1)}, u32[]{:S(2)}, u32[]{:S(2)}) collective-permute-start(bf16[2,448,256]{2,1,0:T(8,128)(2,1)S(1)} %add_convert_fusion.1), channel_id=1, source_target_pairs={{0,4},{8,0},{16,8},{24,16},{28,24},{20,28},{12,20},{4,12},{1,5},{9... | collective-permute-start | bytes 1376264 | tf_op jit(solution)/shard_map/ppermute | solution.py:351
  135.2 10.5 %collective-permute-start.24 = (bf16[2,448,256]{2,1,0:T(8,128)(2,1)S(1)}, bf16[2,448,256]{2,1,0:T(8,128)(2,1)S(1)}, u32[]{:S(2)}, u32[]{:S(2)}) collective-permute-start(bf16[2,448,256]{2,1,0:T(8,128)(2,1)S(1)} %add_convert_fusion.4), channel_id=1, source_target_pairs={{0,8},{8,16},{16,24},{24,28},{28,20},{20,12},{12,4},{4,0},{1,9},{9... | collective-permute-start | bytes 1376264 | tf_op jit(solution)/shard_map/ppermute | solution.py:351

commit v9 on v8

--- a/solution.py
+++ b/solution.py
@@ -55,19 +55,15 @@
     return jnp.where(spot < half, 2 * spot, 2 * (size - 1 - spot) + 1)
 
 
-def after_kernel(x_ref, other_ref, out_ref):
-    out_ref[...] = x_ref[...]
-
-
-def after(x, other):
-    near = pl.BlockSpec(memory_space=pltpu.VMEM)
+def after(x, *others):
     return pl.pallas_call(
-        after_kernel,
-        in_specs=[near, ANYWHERE],
-        out_specs=near,
+        lambda *refs: None,
+        in_specs=[ANYWHERE] + [pl.BlockSpec(memory_space=pltpu.VMEM)] * len(others),
+        out_specs=ANYWHERE,
         out_shape=shaped(x.shape, x.dtype),
-        cost_estimate=pl.CostEstimate(flops=0, bytes_accessed=3000000, transcendentals=0),
-    )(x, other)
+        input_output_aliases={0: 0},
+        cost_estimate=pl.CostEstimate(flops=0, bytes_accessed=0, transcendentals=0),
+    )(x, *others)
 
 
 def as_column(row):
@@ -101,6 +97,22 @@
 def read_marks(block, depth):
     mark = [block[:, depth + i : depth + i + 1].astype(F32) for i in range(3)]
     return mark[0], mark[1] * DIGIT + mark[2]
+
+
+def pack_kernel(me_ref, q_ref, up_ref, own_ref, *other_refs):
+    for i in range(4):
+        here = pl.ds(pl.multiple_of((me_ref[0] ^ i) * SPAN, SPAN), SPAN)
+        for k, ref in enumerate((q_ref, up_ref)):
+            if i % 2:
+                other_refs[i // 2 * 2 + k][...] = ref[:, here]
+            else:
+                own_ref[i // 2, k] = ref[:, here]
+
+
+def pack_heads(me, queries, upstream):
+    rows = queries.shape[0]
+    out = [shaped((2, 2, rows, SPAN), BF16)] + [shaped((rows, SPAN), BF16)] * 4
+    return call(pack_kernel, me, (queries, upstream), out, 2)
 
 
 def place_kernel(me_ref, *refs):
@@ -185,20 +197,18 @@
     return call(halve_kernel, me, (ups, downs, *wait), out, 1, far=tuple(range(2, 2 + len(wait))))
 
 
-def attend_kernel(me_ref, q_ref, up_ref, q_other, up_other, kv_ref, ids_ref, ids_row_ref, *refs):
+def attend_kernel(spot, me_ref, own_ref, q_other, up_other, kv_ref, ids_ref, ids_row_ref, *refs):
     mine_ref, other_ref, early_ref, late_ref, bias, scores_all, dp_all, pbs, his, los = refs[-10:]
-    rows = q_ref.shape[0]
+    rows = q_other.shape[0]
     heads = [slice(h * HEAD_DIM, (h + 1) * HEAD_DIM) for h in range(GROUP)]
     for i in range(2):
         here = pl.ds(pl.multiple_of((me_ref[0] ^ i) * rows, rows), rows)
         bias[i * rows : (i + 1) * rows, :] = jnp.where(ids_row_ref[...] <= ids_ref[here, :], 0.0, HIDDEN)
     keys = kv_ref[:, :HEAD_DIM]
     values = kv_ref[:, HEAD_DIM:]
-    start = me_ref[2] * SPAN
-    places = [pl.ds(pl.multiple_of(start + h * HEAD_DIM, HEAD_DIM), HEAD_DIM) for h in range(GROUP)]
     q, up = [
-        jnp.concatenate([ref[:, place] for ref in pair for place in places], axis=0)
-        for pair in ((q_ref, q_other), (up_ref, up_other))
+        jnp.concatenate([own_ref[spot, i, :, cols] for cols in heads] + [ref[:, cols] for cols in heads], axis=0)
+        for i, ref in enumerate((q_other, up_other))
     ]
     scores_all[...] = contract(q, keys, 1, 1)
     dp_all[...] = contract(up, values, 1, 1).astype(BF16)
@@ -230,19 +240,19 @@
         late_ref[:, cols] = x[half:].astype(late_ref.dtype)
 
 
-def attend(me, sides, kv, ids, ids_row, late, wait=()):
-    rows = sides[0].shape[0]
+def attend(spot, me, own, others, kv, ids, ids_row, late, wait=()):
+    rows = own.shape[2]
     length = kv.shape[0]
     stacked = (2 * GROUP * rows, length)
     side = shaped((2, rows, SPAN), BF16)
     return call(
-        attend_kernel,
+        functools.partial(attend_kernel, spot),
         me,
-        (*sides, kv, ids, ids_row, *wait),
+        (own, *others, kv, ids, ids_row, *wait),
         [side, side, shaped((length // 2, PAIR), F32), shaped((length // 2, PAIR), late)],
         6,
         scratch=[pltpu.VMEM((2 * rows, length), F32), pltpu.VMEM(stacked, F32)] + [pltpu.VMEM(stacked, BF16)] * 4,
-        far=tuple(range(7, 7 + len(wait))),
+        far=tuple(range(6, 6 + len(wait))),
     )
 
 
@@ -353,8 +363,7 @@
     def both_ways(ups, downs):
         return turn(ups, 1), turn(downs, -1)
 
-    me = jnp.stack([me_s, me_f, me_s])
-    me_far = jnp.stack([me_s, me_f, me_s ^ 2])
+    me = jnp.stack([me_s, me_f])
     quarters = me_s ^ jnp.arange(seq, dtype=jnp.int32)
     if near_link:
         weights = [kv_weight, *both_ways(kv_weight, kv_weight)]
@@ -365,21 +374,22 @@
 
     blocks = token_blocks(me, tokens, block_ids * 2 + modality, fsdp)
     across = swap(blocks, 2)
+    own, *others = pack_heads(me, queries, cotangent)
+    others = [swap(x, 1) for x in others]
     if near_link:
-        across = after(across, weights[3][0, :16, :128])
+        across = after(across, weights[3], weights[4], *others)
     parts = [blocks, swap(blocks, 1), across, swap(across, 1)]
-    sides = (queries, cotangent, swap(queries, 1), swap(cotangent, 1))
 
     if near_link:
         before = project(me, STEPS[:5], parts, weights[:5], (), depth)
-        weights += both_ways(*halve(me, *weights[5:], (before[0], sides[2][:16, :128], sides[3][:16, :128])))
+        weights += both_ways(*halve(me, *weights[5:], (before[0],)))
         before = project(me, STEPS[5:7], parts, weights[5:7], before, depth)
         kv, kind, ids, ids_row, weight = project(me, STEPS[7:], parts, weights[7:], before, depth, True, True)
     else:
         kv, kind, ids, ids_row = project_plain(quarters, parts, weight, depth)
     kv_far = swap(kv, 2)
-    far_own, far_other, early, late = attend(me_far, sides, kv_far, ids, ids_row, BF16)
-    near_own, near_other, *near = attend(me, sides, kv, ids, ids_row, F32, (early,))
+    far_own, far_other, early, late = attend(1, me, own, others[2:], kv_far, ids, ids_row, BF16)
+    near_own, near_other, *near = attend(0, me, own, others[:2], kv, ids, ids_row, F32, (early,))
     grad_kv = jnp.concatenate([near[0] + swap(early, 2), near[1] + swap(late, 2).astype(F32)]).astype(BF16)
     attended, grad_queries = place_heads(me, (near_own, swap(near_other, 1), far_own, swap(far_other, 1)))
 

time: 147 us -> 130 us (0.88)
  waiting for transfers between devices: 68.1 us -> 55.2 us
  Pallas kernels: 35 us -> 29.9 us
  local copies, waits for them, and re-layouts: 13 us -> 15.1 us
    ppermute x16, waiting for transfers between devices: 52.5 us -> 39.9 us  [turn(): lax.ppermute(x, 'fsdp', [(CYCLE[i], CYCLE[(i + by) % fsdp]) for i in rang...]
    pallas_call x12 -> x13, Pallas kernels: 32.7 us -> 28.5 us  [call(): pl.pallas_call(body, in_specs=[pl.BlockSpec(memory_space=pltpu.SMEM)] + [...]
    unnamed x34 -> x50, local copies, waits for them, and re-layouts: 11.7 us -> 15.1 us
    ppermute x13 -> x15, waiting for transfers between devices: 15.6 us -> 15.3 us  [swap(): return lax.ppermute(x, 'seq', [(i, i ^ bit) for i in range(seq)])]
    ppermute x13 -> x15, starting transfers between devices: 8.17 us -> 8.07 us  [swap(): return lax.ppermute(x, 'seq', [(i, i ^ bit) for i in range(seq)])]
  transfers between devices with their start and end apart: 29 -> 31, of which waited for: 14 -> 18; matrix products, arithmetic and copies ran while one was open for 3% -> 1% of each run, Pallas kernels for 22% -> 21%
where the time goes in v9:
time: 130 us; the launch traced here: 129 us
  waiting for transfers between devices  55.2 us (42%)
  Pallas kernels  29.9 us (23%)
  starting transfers between devices  24.7 us (19%)
  local copies, waits for them, and re-layouts  15.1 us (12%)
  other arithmetic  3.52 us (3%)
    ppermute x16, waiting for transfers between devices, turn(): lax.ppermute(x, 'fsdp', [(CYCLE[i], CYCLE[(i + by) % fsdp]) for i in rang...  39.9 us
    pallas_call x13, Pallas kernels, call(): pl.pallas_call(body, in_specs=[pl.BlockSpec(memory_space=pltpu.SMEM)] + [...  28.5 us
    ppermute x16, starting transfers between devices, turn(): lax.ppermute(x, 'fsdp', [(CYCLE[i], CYCLE[(i + by) % fsdp]) for i in rang...  16.6 us
    ppermute x15, waiting for transfers between devices, swap(): return lax.ppermute(x, 'seq', [(i, i ^ bit) for i in range(seq)])  15.3 us
    unnamed x50, local copies, waits for them, and re-layouts  15.1 us
    ppermute x15, starting transfers between devices, swap(): return lax.ppermute(x, 'seq', [(i, i ^ bit) for i in range(seq)])  8.07 us
  transfers between devices with their start and end apart: 31, of which 18 were waited for; matrix products, arithmetic and copies ran while one was open for 1% of the time, Pallas kernels for 21%

profile of v9, /device:TPU:0, one launch (start us, length us, event | category | flops | bytes accessed | tf_op | source)
XLA Modules:
  0.0 129.4 jit_solution(9117194193973862974)
XLA Ops:
  1.4 1.2 copy-done.9
  2.6 0.9 shard_map.94.refs_0_
  3.5 3.0 %collective-permute-start.3 = (bf16[8,128,512]{2,1,0:T(8,128)(2,1)S(1)}, bf16[8,128,512]{2,1,0:T(8,128)(2,1)S(1)}, u32[]{:S(2)}, u32[]{:S(2)}) collective-permute-start(bf16[8,128,512]{2,1,0:T(8,128)(2,1)S(1)} %shard_map.94.refs_0_), channel_id=1, source_target_pairs={{0,2},{1,3},{2,0},{3,1},{4,6},{5,7},{6,4},{7,5},{8,10},{9,11},{10,... | collective-permute-start | bytes 3145736 | tf_op jit(solution)/shard_map/ppermute | solution.py:358
  6.5 1.6 %collective-permute-start.4 = (bf16[2,448,256]{2,1,0:T(8,128)(2,1)}, bf16[2,448,256]{2,1,0:T(8,128)(2,1)S(1)}, u32[]{:S(2)}, u32[]{:S(2)}) collective-permute-start(bf16[2,448,256]{2,1,0:T(8,128)(2,1)} %refs_4_.1), channel_id=1, source_target_pairs={{0,8},{8,16},{16,24},{24,28},{28,20},{20,12},{12,4},{4,0},{1,9},{9... | collective-permute-start | bytes 1376264 | tf_op jit(solution)/shard_map/ppermute | solution.py:361
  8.5 1.2 copy-done.10
  9.7 1.2 copy-done.11
  11.6 0.9 copy-done.3
  13.0 5.7 %collective-permute-done.4.refs_5_ = bf16[2,448,256]{2,1,0:T(8,128)(2,1)S(1)} collective-permute-done((bf16[2,448,256]{2,1,0:T(8,128)(2,1)}, bf16[2,448,256]{2,1,0:T(8,128)(2,1)S(1)}, u32[]{:S(2)}, u32[]{:S(2)}) %collective-permute-start.4) | collective-permute-done | bytes 458784 | tf_op jit(solution)/shard_map/ppermute | solution.py:361
  18.7 1.6 %collective-permute-start.5 = (bf16[2,448,256]{2,1,0:T(8,128)(2,1)S(1)}, bf16[2,448,256]{2,1,0:T(8,128)(2,1)S(1)}, u32[]{:S(2)}, u32[]{:S(2)}) collective-permute-start(bf16[2,448,256]{2,1,0:T(8,128)(2,1)S(1)} %collective-permute-done.4.refs_5_), channel_id=1, source_target_pairs={{0,8},{8,16},{16,24},{24,28},{28,20},{20,12},{12,4},{4,0},{1,9},{9... | collective-permute-start | bytes 1376264 | tf_op jit(solution)/shard_map/ppermute | solution.py:361
  24.1 5.7 %collective-permute-done.5.refs_1_.refs_7_ = bf16[2,448,256]{2,1,0:T(8,128)(2,1)S(1)} collective-permute-done((bf16[2,448,256]{2,1,0:T(8,128)(2,1)S(1)}, bf16[2,448,256]{2,1,0:T(8,128)(2,1)S(1)}, u32[]{:S(2)}, u32[]{:S(2)}) %collective-permute-start.5) | collective-permute-done | bytes 458784 | tf_op jit(solution)/shard_map/ppermute | solution.py:361
  30.5 1.3 %collective-permute-done.7.refs_2_.refs_8_ = bf16[2,448,256]{2,1,0:T(8,128)(2,1)S(1)} collective-permute-done((bf16[2,448,256]{2,1,0:T(8,128)(2,1)S(1)}, bf16[2,448,256]{2,1,0:T(8,128)(2,1)S(1)}, u32[]{:S(2)}, u32[]{:S(2)}) %collective-permute-start.7) | collective-permute-done | bytes 458784 | tf_op jit(solution)/shard_map/ppermute | solution.py:361
  32.6 1.0 copy-done
  33.6 1.5 %shard_map.95.refs_2_ = bf16[8,128,512]{2,1,0:T(8,128)(2,1)} custom-call(bf16[8,128,512]{2,1,0:T(8,128)(2,1)} %copy-done, bf16[2,448,256]{2,1,0:T(8,128)(2,1)} %copy-done.5, bf16[2,448,256]{2,1,0:T(8,128)(2,1)} %copy-done.7, bf16[128,896]{1,0:T(8,128)(2,1)} %copy-done.16, bf16[128,896]{1,0:T(8,128)(2,1)} %copy-done.18, ...), custom_call_target="tpu_custom_call", output_to_operand_aliasing={{}: (0, {})} | custom-call | tf_op jit(solution)/shard_map/pallas_call | solution.py:59
  35.1 1.6 %collective-permute-start.11 = (bf16[2,448,256]{2,1,0:T(8,128)(2,1)}, bf16[2,448,256]{2,1,0:T(8,128)(2,1)S(1)}, u32[]{:S(2)}, u32[]{:S(2)}) collective-permute-start(bf16[2,448,256]{2,1,0:T(8,128)(2,1)} %copy-done.5), channel_id=1, source_target_pairs={{0,8},{8,16},{16,24},{24,28},{28,20},{20,12},{12,4},{4,0},{1,9},{9... | collective-permute-start | bytes 1376264 | tf_op jit(solution)/shard_map/ppermute | solution.py:361
  37.9 1.2 copy-done.1
  39.2 1.0 copy-done.6
  40.2 1.0 copy-done.8
  41.2 1.0 copy-done.20
  42.2 1.0 copy-done.22
  43.3 1.0 copy-done.24
  44.3 3.5 %shard_map.96 = (f32[512,512]{1,0:T(8,128)S(1)}, bf16[8,2,448,256]{3,2,1,0:T(8,128)(2,1)S(1)}) custom-call(s32[2]{0:T(128)S(1)} %pad_add_fusion.me_ref, bf16[8,128,512]{2,1,0:T(8,128)(2,1)S(1)} %shard_map.94.refs_0_, bf16[8,128,512]{2,1,0:T(8,128)(2,1)S(1)} %collective-permute-done.2.refs_1_, bf16[8,128,512]{2,1,0:T(8,128)(2,1)S(1)} %copy-done.1, ...), custom_call_target="tpu_custom_call" | custom-call | bytes 9000000 | tf_op jit(solution)/shard_map/pallas_call | solution.py:36
  48.2 1.3 %collective-permute-done.12.downs_ref.refs_5_ = bf16[2,448,256]{2,1,0:T(8,128)(2,1)S(1)} collective-permute-done((bf16[2,448,256]{2,1,0:T(8,128)(2,1)}, bf16[2,448,256]{2,1,0:T(8,128)(2,1)S(1)}, u32[]{:S(2)}, u32[]{:S(2)}) %collective-permute-start.12) | collective-permute-done | bytes 458784 | tf_op jit(solution)/shard_map/ppermute | solution.py:361
  50.1 1.6 %collective-permute-start.13 = (bf16[1,448,256]{2,1,0:T(8,128)(2,1)S(1)}, bf16[1,448,256]{2,1,0:T(8,128)(2,1)S(1)}, u32[]{:S(2)}, u32[]{:S(2)}) collective-permute-start(bf16[1,448,256]{2,1,0:T(8,128)(2,1)S(1)} %get-tuple-element.47), channel_id=1, source_target_pairs={{0,8},{8,16},{16,24},{24,28},{28,20},{20,12},{12,4},{4,0},{1,9},{9... | collective-permute-start | bytes 688136 | tf_op jit(solution)/shard_map/ppermute | solution.py:361
  52.2 1.8 %shard_map.98 = (f32[512,512]{1,0:T(8,128)S(1)}, bf16[8,2,448,256]{3,2,1,0:T(8,128)(2,1)S(1)}) custom-call(s32[2]{0:T(128)S(1)} %pad_add_fusion.me_ref, bf16[8,128,512]{2,1,0:T(8,128)(2,1)S(1)} %shard_map.94.refs_0_, bf16[8,128,512]{2,1,0:T(8,128)(2,1)S(1)} %collective-permute-done.2.refs_1_, ...), custom_call_target="tpu_custom_call", output_to_operand_aliasing={{1}: (8, {})} | custom-call | bytes 9000000 | tf_op jit(solution)/shard_map/pallas_call | solution.py:36
  54.0 3.1 %collective-permute-done.13.refs_4_ = bf16[1,448,256]{2,1,0:T(8,128)(2,1)S(1)} collective-permute-done((bf16[1,448,256]{2,1,0:T(8,128)(2,1)S(1)}, bf16[1,448,256]{2,1,0:T(8,128)(2,1)S(1)}, u32[]{:S(2)}, u32[]{:S(2)}) %collective-permute-start.13) | collective-permute-done | bytes 229408 | tf_op jit(solution)/shard_map/ppermute | solution.py:361
  57.1 1.3 %collective-permute-done.14.refs_5_ = bf16[1,448,256]{2,1,0:T(8,128)(2,1)S(1)} collective-permute-done((bf16[1,448,256]{2,1,0:T(8,128)(2,1)S(1)}, bf16[1,448,256]{2,1,0:T(8,128)(2,1)S(1)}, u32[]{:S(2)}, u32[]{:S(2)}) %collective-permute-start.14) | collective-permute-done | bytes 229408 | tf_op jit(solution)/shard_map/ppermute | solution.py:361
  58.4 1.8 %shard_map.99 = (bf16[512,256]{1,0:T(8,128)(2,1)S(1)}, f32[512,1]{1,0:T(8,128)S(1)}, f32[512,1]{1,0:T(8,128)S(1)}, f32[1,512]{1,0:T(1,128)S(1)}, bf16[8,2,448,256]{3,2,1,0:T(8,128)(2,1)S(1)}) custom-call(s32[2]{0:T(128)S(1)} %pad_add_fusion.me_ref, bf16[8,128,512]{2,1,0:T(8,128)(2,1)S(1)} %shard_map.94.refs_0_, ...), custom_call_target="tpu_custom_call", output_to_operand_aliasing={{4}: (8, {})} | custom-call | bytes 9000000 | tf_op jit(solution)/shard_map/pallas_call | solution.py:36
  60.8 8.1 %collective-permute-done.15.kv_ref = bf16[512,256]{1,0:T(8,128)(2,1)S(1)} collective-permute-done((bf16[512,256]{1,0:T(8,128)(2,1)S(1)}, bf16[512,256]{1,0:T(8,128)(2,1)S(1)}, u32[]{:S(2)}, u32[]{:S(2)}) %collective-permute-start.15) | collective-permute-done | bytes 262176 | tf_op jit(solution)/shard_map/ppermute | solution.py:358
  69.0 4.6 %shard_map.100 = (bf16[2,128,896]{2,1,0:T(8,128)(2,1)S(1)}, bf16[2,128,896]{2,1,0:T(8,128)(2,1)S(1)}, f32[256,256]{1,0:T(8,128)S(1)}, bf16[256,256]{1,0:T(8,128)(2,1)S(1)}) custom-call(s32[2]{0:T(128)S(1)} %pad_add_fusion.me_ref, bf16[2,2,128,896]{3,2,1,0:T(8,128)(2,1)S(1)} %copy-done.4, bf16[128,896]{1,0:T(8,128)(2,1)S(1)} %copy-done.13, ...), custom_call_target="tpu_custom_call" | custom-call | bytes 18000000 | tf_op jit(solution)/shard_map/pallas_call | solution.py:36
  74.2 1.5 %collective-permute-start.18 = (f32[256,256]{1,0:T(8,128)S(1)}, f32[256,256]{1,0:T(8,128)S(1)}, u32[]{:S(2)}, u32[]{:S(2)}) collective-permute-start(f32[256,256]{1,0:T(8,128)S(1)} %get-tuple-element.55.refs_0_), channel_id=1, source_target_pairs={{0,2},{1,3},{2,0},{3,1},{4,6},{5,7},{6,4},{7,5},{8,10},{9,11},{10,... | collective-permute-start | bytes 786440 | tf_op jit(solution)/shard_map/ppermute | solution.py:358
  75.7 4.7 %shard_map.101 = (bf16[2,128,896]{2,1,0:T(8,128)(2,1)S(1)}, bf16[2,128,896]{2,1,0:T(8,128)(2,1)S(1)}, f32[256,256]{1,0:T(8,128)S(1)}, f32[256,256]{1,0:T(8,128)S(1)}) custom-call(s32[2]{0:T(128)S(1)} %pad_add_fusion.me_ref, bf16[2,2,128,896]{3,2,1,0:T(8,128)(2,1)S(1)} %copy-done.4, bf16[128,896]{1,0:T(8,128)(2,1)S(1)} %copy-done.17, ...), custom_call_target="tpu_custom_call" | custom-call | bytes 18000000 | tf_op jit(solution)/shard_map/pallas_call | solution.py:36
  80.4 3.9 %collective-permute-done.18 = f32[256,256]{1,0:T(8,128)S(1)} collective-permute-done((f32[256,256]{1,0:T(8,128)S(1)}, f32[256,256]{1,0:T(8,128)S(1)}, u32[]{:S(2)}, u32[]{:S(2)}) %collective-permute-start.18) | collective-permute-done | bytes 262176 | tf_op jit(solution)/shard_map/ppermute | solution.py:358
  84.5 1.3 shard_map.106
  86.3 1.6 %collective-permute-start.23 = (bf16[1,448,256]{2,1,0:T(8,128)(2,1)S(1)}, bf16[1,448,256]{2,1,0:T(8,128)(2,1)S(1)}, u32[]{:S(2)}, u32[]{:S(2)}) collective-permute-start(bf16[1,448,256]{2,1,0:T(8,128)(2,1)S(1)} %get-tuple-element.73), channel_id=1, source_target_pairs={{0,8},{8,16},{16,24},{24,28},{28,20},{20,12},{12,4},{4,0},{1,9},{9... | collective-permute-start | bytes 688136 | tf_op jit(solution)/shard_map/ppermute | solution.py:361
  87.9 2.9 %shard_map.103 = (f32[128,3584]{1,0:T(8,128)S(1)}, bf16[128,3584]{1,0:T(8,128)(2,1)S(1)}) custom-call(s32[2]{0:T(128)S(1)} %pad_add_fusion.me_ref, f32[512,1]{1,0:T(8,128)S(1)} %get-tuple-element.62.kind_ref, bf16[512,256]{1,0:T(8,128)(2,1)S(1)} %pad_maximum_fusion.g_ref.refs_4_, bf16[512,256]{1,0:T(8,128)(2,1)S(1)} %collective-permute-done.20.gc_ref, ...), custom_call_target="tpu_custom_call" | custom-call | bytes 21000000 | tf_op jit(solution)/shard_map/pallas_call | solution.py:36
  90.8 1.5 %shard_map.105 = (f32[2,448,256]{2,1,0:T(8,128)S(1)}, f32[2,448,256]{2,1,0:T(8,128)S(1)}) custom-call(s32[2]{0:T(128)S(1)} %pad_add_fusion.me_ref, bf16[8,128,512]{2,1,0:T(8,128)(2,1)S(1)} %shard_map.94.refs_0_, bf16[8,128,512]{2,1,0:T(8,128)(2,1)S(1)} %collective-permute-done.2.refs_1_, bf16[8,128,512]{2,1,0:T(8,128)(2,1)S(1)} %copy-done.2, ...), custom_call_target="tpu_custom_call" | custom-call | bytes 9000000 | tf_op jit(solution)/shard_map/pallas_call | solution.py:36
  92.3 1.5 %collective-permute-done.27 = bf16[1,448,256]{2,1,0:T(8,128)(2,1)S(1)} collective-permute-done((bf16[1,448,256]{2,1,0:T(8,128)(2,1)S(1)}, bf16[1,448,256]{2,1,0:T(8,128)(2,1)S(1)}, u32[]{:S(2)}, u32[]{:S(2)}) %collective-permute-start.27) | collective-permute-done | bytes 229408 | tf_op jit(solution)/shard_map/ppermute | solution.py:361
  94.5 1.6 %collective-permute-start.24 = (bf16[2,448,256]{2,1,0:T(8,128)(2,1)S(1)}, bf16[2,448,256]{2,1,0:T(8,128)(2,1)S(1)}, u32[]{:S(2)}, u32[]{:S(2)}) collective-permute-start(bf16[2,448,256]{2,1,0:T(8,128)(2,1)S(1)} %add_convert_fusion.6), channel_id=1, source_target_pairs={{0,8},{8,16},{16,24},{24,28},{28,20},{20,12},{12,4},{4,0},{1,9},{9... | collective-permute-start | bytes 1376264 | tf_op jit(solution)/shard_map/ppermute | solution.py:361
  96.6 2.3 %shard_map.104 = (f32[2,448,256]{2,1,0:T(8,128)S(1)}, f32[2,448,256]{2,1,0:T(8,128)S(1)}, f32[2,448,256]{2,1,0:T(8,128)S(1)}, f32[2,448,256]{2,1,0:T(8,128)S(1)}, f32[2,448,256]{2,1,0:T(8,128)S(1)}) custom-call(s32[2]{0:T(128)S(1)} %pad_add_fusion.me_ref, bf16[8,128,512]{2,1,0:T(8,128)(2,1)S(1)} %shard_map.94.refs_0_, ...), custom_call_target="tpu_custom_call" | custom-call | bytes 18000000 | tf_op jit(solution)/shard_map/pallas_call | solution.py:36
  99.5 6.5 %collective-permute-done.28 = bf16[2,448,256]{2,1,0:T(8,128)(2,1)S(1)} collective-permute-done((bf16[2,448,256]{2,1,0:T(8,128)(2,1)S(1)}, bf16[2,448,256]{2,1,0:T(8,128)(2,1)S(1)}, u32[]{:S(2)}, u32[]{:S(2)}) %collective-permute-start.28) | collective-permute-done | bytes 458784 | tf_op jit(solution)/shard_map/ppermute | solution.py:361
  106.8 1.6 %collective-permute-start.25 = (bf16[2,448,256]{2,1,0:T(8,128)(2,1)S(1)}, bf16[2,448,256]{2,1,0:T(8,128)(2,1)S(1)}, u32[]{:S(2)}, u32[]{:S(2)}) collective-permute-start(bf16[2,448,256]{2,1,0:T(8,128)(2,1)S(1)} %add_convert_fusion.5), channel_id=1, source_target_pairs={{0,8},{8,16},{16,24},{24,28},{28,20},{20,12},{12,4},{4,0},{1,9},{9... | collective-permute-start | bytes 1376264 | tf_op jit(solution)/shard_map/ppermute | solution.py:361
  108.4 1.9 %shard_map.102 = (bf16[128,3584]{1,0:T(8,128)(2,1)}, bf16[128,3584]{1,0:T(8,128)(2,1)}) custom-call(s32[2]{0:T(128)S(1)} %pad_add_fusion.me_ref, bf16[2,128,896]{2,1,0:T(8,128)(2,1)S(1)} %get-tuple-element.56.refs_0_, bf16[2,128,896]{2,1,0:T(8,128)(2,1)S(1)} %collective-permute-done.16.refs_1_, bf16[2,128,896]{2,1,0:T(8,128)(2,1)S(1)} %get-tuple-element.58.refs_2_, ...), custom_call_target="tpu_custom_call" | custom-call | bytes 9000000 | tf_op jit(solution)/shard_map/pallas_call | solution.py:36
  110.3 7.1 %collective-permute-done.29 = bf16[2,448,256]{2,1,0:T(8,128)(2,1)S(1)} collective-permute-done((bf16[2,448,256]{2,1,0:T(8,128)(2,1)S(1)}, bf16[2,448,256]{2,1,0:T(8,128)(2,1)S(1)}, u32[]{:S(2)}, u32[]{:S(2)}) %collective-permute-start.29) | collective-permute-done | bytes 458784 | tf_op jit(solution)/shard_map/ppermute | solution.py:361
  118.2 1.6 %collective-permute-start.26 = (bf16[2,448,256]{2,1,0:T(8,128)(2,1)S(1)}, bf16[2,448,256]{2,1,0:T(8,128)(2,1)S(1)}, u32[]{:S(2)}, u32[]{:S(2)}) collective-permute-start(bf16[2,448,256]{2,1,0:T(8,128)(2,1)S(1)} %add_convert_fusion.4), channel_id=1, source_target_pairs={{0,8},{8,16},{16,24},{24,28},{28,20},{20,12},{12,4},{4,0},{1,9},{9... | collective-permute-start | bytes 1376264 | tf_op jit(solution)/shard_map/ppermute | solution.py:361
  119.8 1.5 %collective-permute-done.22 = bf16[128,3584]{1,0:T(8,128)(2,1)S(1)} collective-permute-done((bf16[128,3584]{1,0:T(8,128)(2,1)S(1)}, bf16[128,3584]{1,0:T(8,128)(2,1)S(1)}, u32[]{:S(2)}, u32[]{:S(2)}) %collective-permute-start.22) | collective-permute-done | bytes 917536 | tf_op jit(solution)/shard_map/ppermute | solution.py:358
  121.3 1.1 fusion
  122.4 5.5 %collective-permute-done.30 = bf16[2,448,256]{2,1,0:T(8,128)(2,1)S(1)} collective-permute-done((bf16[2,448,256]{2,1,0:T(8,128)(2,1)S(1)}, bf16[2,448,256]{2,1,0:T(8,128)(2,1)S(1)}, u32[]{:S(2)}, u32[]{:S(2)}) %collective-permute-start.30) | collective-permute-done | bytes 458784 | tf_op jit(solution)/shard_map/ppermute | solution.py:361
  128.3 1.1 convert_add_fusion
  (91 shorter events, 16.0 us)
Async XLA Ops:
  1.4 1.2 copy-start.9
  3.5 29.1 %collective-permute-start.3 = (bf16[8,128,512]{2,1,0:T(8,128)(2,1)S(1)}, bf16[8,128,512]{2,1,0:T(8,128)(2,1)S(1)}, u32[]{:S(2)}, u32[]{:S(2)}) collective-permute-start(bf16[8,128,512]{2,1,0:T(8,128)(2,1)S(1)} %shard_map.94.refs_0_), channel_id=1, source_target_pairs={{0,2},{1,3},{2,0},{3,1},{4,6},{5,7},{6,4},{7,5},{8,10},{9,11},{10,... | collective-permute-start | bytes 3145736 | tf_op jit(solution)/shard_map/ppermute | solution.py:358
  6.5 12.2 %collective-permute-start.4 = (bf16[2,448,256]{2,1,0:T(8,128)(2,1)}, bf16[2,448,256]{2,1,0:T(8,128)(2,1)S(1)}, u32[]{:S(2)}, u32[]{:S(2)}) collective-permute-start(bf16[2,448,256]{2,1,0:T(8,128)(2,1)} %refs_4_.1), channel_id=1, source_target_pairs={{0,8},{8,16},{16,24},{24,28},{28,20},{20,12},{12,4},{4,0},{1,9},{9... | collective-permute-start | bytes 1376264 | tf_op jit(solution)/shard_map/ppermute | solution.py:361
  8.1 13.0 %collective-permute-start.6 = (bf16[2,448,256]{2,1,0:T(8,128)(2,1)}, bf16[2,448,256]{2,1,0:T(8,128)(2,1)S(1)}, u32[]{:S(2)}, u32[]{:S(2)}) collective-permute-start(bf16[2,448,256]{2,1,0:T(8,128)(2,1)} %refs_4_.1), channel_id=1, source_target_pairs={{0,4},{8,0},{16,8},{24,16},{28,24},{20,28},{12,20},{4,12},{1,5},{9... | collective-permute-start | bytes 1376264 | tf_op jit(solution)/shard_map/ppermute | solution.py:361
  8.5 1.2 copy-start.10
  9.7 1.2 copy-start.11
  12.5 9.8 %collective-permute-start = (bf16[128,896]{1,0:T(8,128)(2,1)S(1)}, bf16[128,896]{1,0:T(8,128)(2,1)S(1)}, u32[]{:S(2)}, u32[]{:S(2)}) collective-permute-start(bf16[128,896]{1,0:T(8,128)(2,1)S(1)} %get-tuple-element.42), channel_id=1, source_target_pairs={{0,1},{1,0},{2,3},{3,2},{4,5},{5,4},{6,7},{7,6},{8,9},{9,8},{10,11... | collective-permute-start | bytes 688136 | tf_op jit(solution)/shard_map/ppermute | solution.py:358
  12.5 9.8 %collective-permute-start.1 = (bf16[128,896]{1,0:T(8,128)(2,1)S(1)}, bf16[128,896]{1,0:T(8,128)(2,1)S(1)}, u32[]{:S(2)}, u32[]{:S(2)}) collective-permute-start(bf16[128,896]{1,0:T(8,128)(2,1)S(1)} %get-tuple-element.43), channel_id=1, source_target_pairs={{0,1},{1,0},{2,3},{3,2},{4,5},{5,4},{6,7},{7,6},{8,9},{9,8},{10,11... | collective-permute-start | bytes 688136 | tf_op jit(solution)/shard_map/ppermute | solution.py:358
  18.7 11.1 %collective-permute-start.5 = (bf16[2,448,256]{2,1,0:T(8,128)(2,1)S(1)}, bf16[2,448,256]{2,1,0:T(8,128)(2,1)S(1)}, u32[]{:S(2)}, u32[]{:S(2)}) collective-permute-start(bf16[2,448,256]{2,1,0:T(8,128)(2,1)S(1)} %collective-permute-done.4.refs_5_), channel_id=1, source_target_pairs={{0,8},{8,16},{16,24},{24,28},{28,20},{20,12},{12,4},{4,0},{1,9},{9... | collective-permute-start | bytes 1376264 | tf_op jit(solution)/shard_map/ppermute | solution.py:361
  21.0 10.8 %collective-permute-start.7 = (bf16[2,448,256]{2,1,0:T(8,128)(2,1)S(1)}, bf16[2,448,256]{2,1,0:T(8,128)(2,1)S(1)}, u32[]{:S(2)}, u32[]{:S(2)}) collective-permute-start(bf16[2,448,256]{2,1,0:T(8,128)(2,1)S(1)} %collective-permute-done.6.refs_6_), channel_id=1, source_target_pairs={{0,4},{8,0},{16,8},{24,16},{28,24},{20,28},{12,20},{4,12},{1,5},{9... | collective-permute-start | bytes 1376264 | tf_op jit(solution)/shard_map/ppermute | solution.py:361
  22.2 1.5 %collective-permute-start.8 = (bf16[128,896]{1,0:T(8,128)(2,1)S(1)}, bf16[128,896]{1,0:T(8,128)(2,1)S(1)}, u32[]{:S(2)}, u32[]{:S(2)}) collective-permute-start(bf16[128,896]{1,0:T(8,128)(2,1)S(1)} %get-tuple-element.44), channel_id=1, source_target_pairs={{0,1},{1,0},{2,3},{3,2},{4,5},{5,4},{6,7},{7,6},{8,9},{9,8},{10,11... | collective-permute-start | bytes 688136 | tf_op jit(solution)/shard_map/ppermute | solution.py:358
  22.3 1.8 %collective-permute-start.9 = (bf16[128,896]{1,0:T(8,128)(2,1)S(1)}, bf16[128,896]{1,0:T(8,128)(2,1)S(1)}, u32[]{:S(2)}, u32[]{:S(2)}) collective-permute-start(bf16[128,896]{1,0:T(8,128)(2,1)S(1)} %get-tuple-element.45), channel_id=1, source_target_pairs={{0,1},{1,0},{2,3},{3,2},{4,5},{5,4},{6,7},{7,6},{8,9},{9,8},{10,11... | collective-permute-start | bytes 688136 | tf_op jit(solution)/shard_map/ppermute | solution.py:358
  23.7 8.9 %copy-start.12 = (bf16[128,896]{1,0:T(8,128)(2,1)}, bf16[128,896]{1,0:T(8,128)(2,1)S(1)}, u32[]{:S(2)}) copy-start(bf16[128,896]{1,0:T(8,128)(2,1)S(1)} %collective-permute-done.8.refs_5_.q_other) | copy-start | bytes 688132
  23.7 13.4 %collective-permute-start.2 = (bf16[8,128,512]{2,1,0:T(8,128)(2,1)S(1)}, bf16[8,128,512]{2,1,0:T(8,128)(2,1)S(1)}, u32[]{:S(2)}, u32[]{:S(2)}) collective-permute-start(bf16[8,128,512]{2,1,0:T(8,128)(2,1)S(1)} %shard_map.94.refs_0_), channel_id=1, source_target_pairs={{0,1},{1,0},{2,3},{3,2},{4,5},{5,4},{6,7},{7,6},{8,9},{9,8},{10,11... | collective-permute-start | bytes 3145736 | tf_op jit(solution)/shard_map/ppermute | solution.py:358
  24.1 7.8 %copy-start.14 = (bf16[128,896]{1,0:T(8,128)(2,1)}, bf16[128,896]{1,0:T(8,128)(2,1)S(1)}, u32[]{:S(2)}) copy-start(bf16[128,896]{1,0:T(8,128)(2,1)S(1)} %collective-permute-done.9.refs_6_.up_other) | copy-start | bytes 688132
  35.1 2.9 %collective-permute-start.10 = (bf16[8,128,512]{2,1,0:T(8,128)(2,1)}, bf16[8,128,512]{2,1,0:T(8,128)(2,1)S(1)}, u32[]{:S(2)}, u32[]{:S(2)}) collective-permute-start(bf16[8,128,512]{2,1,0:T(8,128)(2,1)} %shard_map.95.refs_2_), channel_id=1, source_target_pairs={{0,1},{1,0},{2,3},{3,2},{4,5},{5,4},{6,7},{7,6},{8,9},{9,8},{10,11... | collective-permute-start | bytes 3145736 | tf_op jit(solution)/shard_map/ppermute | solution.py:358
  35.1 13.1 %collective-permute-start.11 = (bf16[2,448,256]{2,1,0:T(8,128)(2,1)}, bf16[2,448,256]{2,1,0:T(8,128)(2,1)S(1)}, u32[]{:S(2)}, u32[]{:S(2)}) collective-permute-start(bf16[2,448,256]{2,1,0:T(8,128)(2,1)} %copy-done.5), channel_id=1, source_target_pairs={{0,8},{8,16},{16,24},{24,28},{28,20},{20,12},{12,4},{4,0},{1,9},{9... | collective-permute-start | bytes 1376264 | tf_op jit(solution)/shard_map/ppermute | solution.py:361
  36.7 12.9 %collective-permute-start.12 = (bf16[2,448,256]{2,1,0:T(8,128)(2,1)}, bf16[2,448,256]{2,1,0:T(8,128)(2,1)S(1)}, u32[]{:S(2)}, u32[]{:S(2)}) collective-permute-start(bf16[2,448,256]{2,1,0:T(8,128)(2,1)} %copy-done.7), channel_id=1, source_target_pairs={{0,4},{8,0},{16,8},{24,16},{28,24},{20,28},{12,20},{4,12},{1,5},{9... | collective-permute-start | bytes 1376264 | tf_op jit(solution)/shard_map/ppermute | solution.py:361
  37.9 1.2 copy-start.1
  39.2 1.0 copy-start.6
  40.2 1.0 copy-start.8
  41.2 1.0 copy-start.20
  42.2 1.0 copy-start.22
  43.2 1.0 copy-start.24
  44.3 7.9 %copy-start.2 = (bf16[8,128,512]{2,1,0:T(8,128)(2,1)S(1)}, bf16[8,128,512]{2,1,0:T(8,128)(2,1)}, u32[]{:S(2)}) copy-start(bf16[8,128,512]{2,1,0:T(8,128)(2,1)} %shard_map.95.refs_2_) | copy-start | bytes 3145732
  50.1 7.0 %collective-permute-start.13 = (bf16[1,448,256]{2,1,0:T(8,128)(2,1)S(1)}, bf16[1,448,256]{2,1,0:T(8,128)(2,1)S(1)}, u32[]{:S(2)}, u32[]{:S(2)}) collective-permute-start(bf16[1,448,256]{2,1,0:T(8,128)(2,1)S(1)} %get-tuple-element.47), channel_id=1, source_target_pairs={{0,8},{8,16},{16,24},{24,28},{28,20},{20,12},{12,4},{4,0},{1,9},{9... | collective-permute-start | bytes 688136 | tf_op jit(solution)/shard_map/ppermute | solution.py:361
  51.7 6.6 %collective-permute-start.14 = (bf16[1,448,256]{2,1,0:T(8,128)(2,1)S(1)}, bf16[1,448,256]{2,1,0:T(8,128)(2,1)S(1)}, u32[]{:S(2)}, u32[]{:S(2)}) collective-permute-start(bf16[1,448,256]{2,1,0:T(8,128)(2,1)S(1)} %get-tuple-element.48), channel_id=1, source_target_pairs={{0,4},{8,0},{16,8},{24,16},{28,24},{20,28},{12,20},{4,12},{1,5},{9... | collective-permute-start | bytes 688136 | tf_op jit(solution)/shard_map/ppermute | solution.py:361
  58.4 10.6 %copy-start.4 = (bf16[2,2,128,896]{3,2,1,0:T(8,128)(2,1)S(1)}, bf16[2,2,128,896]{3,2,1,0:T(8,128)(2,1)}, u32[]{:S(2)}) copy-start(bf16[2,2,128,896]{3,2,1,0:T(8,128)(2,1)} %copy-done.3) | copy-start | bytes 2752516
  58.4 10.6 %copy-start.13 = (bf16[128,896]{1,0:T(8,128)(2,1)S(1)}, bf16[128,896]{1,0:T(8,128)(2,1)}, u32[]{:S(2)}) copy-start(bf16[128,896]{1,0:T(8,128)(2,1)} %copy-done.12) | copy-start | bytes 688132
  58.4 10.6 %copy-start.15 = (bf16[128,896]{1,0:T(8,128)(2,1)S(1)}, bf16[128,896]{1,0:T(8,128)(2,1)}, u32[]{:S(2)}) copy-start(bf16[128,896]{1,0:T(8,128)(2,1)} %copy-done.14) | copy-start | bytes 688132
  58.4 17.4 %copy-start.17 = (bf16[128,896]{1,0:T(8,128)(2,1)S(1)}, bf16[128,896]{1,0:T(8,128)(2,1)}, u32[]{:S(2)}) copy-start(bf16[128,896]{1,0:T(8,128)(2,1)} %copy-done.16) | copy-start | bytes 688132
  58.4 17.3 %copy-start.19 = (bf16[128,896]{1,0:T(8,128)(2,1)S(1)}, bf16[128,896]{1,0:T(8,128)(2,1)}, u32[]{:S(2)}) copy-start(bf16[128,896]{1,0:T(8,128)(2,1)} %copy-done.18) | copy-start | bytes 688132
  60.2 27.7 %collective-permute-start.21 = (bf16[8,2,448,256]{3,2,1,0:T(8,128)(2,1)S(1)}, bf16[8,2,448,256]{3,2,1,0:T(8,128)(2,1)S(1)}, u32[]{:S(2)}, u32[]{:S(2)}) collective-permute-start(bf16[8,2,448,256]{3,2,1,0:T(8,128)(2,1)S(1)} %get-tuple-element.66.w_ref), channel_id=1, source_target_pairs={{0,1},{1,0},{2,3},{3,2},{4,5},{5,4},{6,7},{7,6},{8,9},{9,8},{10,11... | collective-permute-start | bytes 11010056 | tf_op jit(solution)/shard_map/ppermute | solution.py:358
  60.2 8.7 %collective-permute-start.15 = (bf16[512,256]{1,0:T(8,128)(2,1)S(1)}, bf16[512,256]{1,0:T(8,128)(2,1)S(1)}, u32[]{:S(2)}, u32[]{:S(2)}) collective-permute-start(bf16[512,256]{1,0:T(8,128)(2,1)S(1)} %get-tuple-element.52.kv_ref), channel_id=1, source_target_pairs={{0,2},{1,3},{2,0},{3,1},{4,6},{5,7},{6,4},{7,5},{8,10},{9,11},{10,... | collective-permute-start | bytes 786440 | tf_op jit(solution)/shard_map/ppermute | solution.py:358
  73.6 6.8 %collective-permute-start.19 = (bf16[256,256]{1,0:T(8,128)(2,1)S(1)}, bf16[256,256]{1,0:T(8,128)(2,1)S(1)}, u32[]{:S(2)}, u32[]{:S(2)}) collective-permute-start(bf16[256,256]{1,0:T(8,128)(2,1)S(1)} %get-tuple-element.65), channel_id=1, source_target_pairs={{0,2},{1,3},{2,0},{3,1},{4,6},{5,7},{6,4},{7,5},{8,10},{9,11},{10,... | collective-permute-start | bytes 393224 | tf_op jit(solution)/shard_map/ppermute | solution.py:358
  74.2 10.2 %collective-permute-start.18 = (f32[256,256]{1,0:T(8,128)S(1)}, f32[256,256]{1,0:T(8,128)S(1)}, u32[]{:S(2)}, u32[]{:S(2)}) collective-permute-start(f32[256,256]{1,0:T(8,128)S(1)} %get-tuple-element.55.refs_0_), channel_id=1, source_target_pairs={{0,2},{1,3},{2,0},{3,1},{4,6},{5,7},{6,4},{7,5},{8,10},{9,11},{10,... | collective-permute-start | bytes 786440 | tf_op jit(solution)/shard_map/ppermute | solution.py:358
  84.4 3.4 %collective-permute-start.20 = (bf16[512,256]{1,0:T(8,128)(2,1)S(1)}, bf16[512,256]{1,0:T(8,128)(2,1)S(1)}, u32[]{:S(2)}, u32[]{:S(2)}) collective-permute-start(bf16[512,256]{1,0:T(8,128)(2,1)S(1)} %pad_maximum_fusion.g_ref.refs_4_), channel_id=1, source_target_pairs={{0,1},{1,0},{2,3},{3,2},{4,5},{5,4},{6,7},{7,6},{8,9},{9,8},{10,11... | collective-permute-start | bytes 786440 | tf_op jit(solution)/shard_map/ppermute | solution.py:358
  85.8 8.0 %collective-permute-start.27 = (bf16[1,448,256]{2,1,0:T(8,128)(2,1)S(1)}, bf16[1,448,256]{2,1,0:T(8,128)(2,1)S(1)}, u32[]{:S(2)}, u32[]{:S(2)}) collective-permute-start(bf16[1,448,256]{2,1,0:T(8,128)(2,1)S(1)} %get-tuple-element.77), channel_id=1, source_target_pairs={{0,4},{8,0},{16,8},{24,16},{28,24},{20,28},{12,20},{4,12},{1,5},{9... | collective-permute-start | bytes 688136 | tf_op jit(solution)/shard_map/ppermute | solution.py:361
  86.3 8.1 %collective-permute-start.23 = (bf16[1,448,256]{2,1,0:T(8,128)(2,1)S(1)}, bf16[1,448,256]{2,1,0:T(8,128)(2,1)S(1)}, u32[]{:S(2)}, u32[]{:S(2)}) collective-permute-start(bf16[1,448,256]{2,1,0:T(8,128)(2,1)S(1)} %get-tuple-element.73), channel_id=1, source_target_pairs={{0,8},{8,16},{16,24},{24,28},{28,20},{20,12},{12,4},{4,0},{1,9},{9... | collective-permute-start | bytes 688136 | tf_op jit(solution)/shard_map/ppermute | solution.py:361
  93.9 12.2 %collective-permute-start.28 = (bf16[2,448,256]{2,1,0:T(8,128)(2,1)S(1)}, bf16[2,448,256]{2,1,0:T(8,128)(2,1)S(1)}, u32[]{:S(2)}, u32[]{:S(2)}) collective-permute-start(bf16[2,448,256]{2,1,0:T(8,128)(2,1)S(1)} %add_convert_fusion.3), channel_id=1, source_target_pairs={{0,4},{8,0},{16,8},{24,16},{28,24},{20,28},{12,20},{4,12},{1,5},{9... | collective-permute-start | bytes 1376264 | tf_op jit(solution)/shard_map/ppermute | solution.py:361
  94.5 12.2 %collective-permute-start.24 = (bf16[2,448,256]{2,1,0:T(8,128)(2,1)S(1)}, bf16[2,448,256]{2,1,0:T(8,128)(2,1)S(1)}, u32[]{:S(2)}, u32[]{:S(2)}) collective-permute-start(bf16[2,448,256]{2,1,0:T(8,128)(2,1)S(1)} %add_convert_fusion.6), channel_id=1, source_target_pairs={{0,8},{8,16},{16,24},{24,28},{28,20},{20,12},{12,4},{4,0},{1,9},{9... | collective-permute-start | bytes 1376264 | tf_op jit(solution)/shard_map/ppermute | solution.py:361
  96.1 12.3 %collective-permute-start.16 = (bf16[2,128,896]{2,1,0:T(8,128)(2,1)S(1)}, bf16[2,128,896]{2,1,0:T(8,128)(2,1)S(1)}, u32[]{:S(2)}, u32[]{:S(2)}) collective-permute-start(bf16[2,128,896]{2,1,0:T(8,128)(2,1)S(1)} %get-tuple-element.57), channel_id=1, source_target_pairs={{0,1},{1,0},{2,3},{3,2},{4,5},{5,4},{6,7},{7,6},{8,9},{9,8},{10,11... | collective-permute-start | bytes 1376264 | tf_op jit(solution)/shard_map/ppermute | solution.py:358
  96.1 12.3 %collective-permute-start.17 = (bf16[2,128,896]{2,1,0:T(8,128)(2,1)S(1)}, bf16[2,128,896]{2,1,0:T(8,128)(2,1)S(1)}, u32[]{:S(2)}, u32[]{:S(2)}) collective-permute-start(bf16[2,128,896]{2,1,0:T(8,128)(2,1)S(1)} %get-tuple-element.59), channel_id=1, source_target_pairs={{0,1},{1,0},{2,3},{3,2},{4,5},{5,4},{6,7},{7,6},{8,9},{9,8},{10,11... | collective-permute-start | bytes 1376264 | tf_op jit(solution)/shard_map/ppermute | solution.py:358
  99.0 22.3 %collective-permute-start.22 = (bf16[128,3584]{1,0:T(8,128)(2,1)S(1)}, bf16[128,3584]{1,0:T(8,128)(2,1)S(1)}, u32[]{:S(2)}, u32[]{:S(2)}) collective-permute-start(bf16[128,3584]{1,0:T(8,128)(2,1)S(1)} %get-tuple-element.68.refs_5_), channel_id=1, source_target_pairs={{0,2},{1,3},{2,0},{3,1},{4,6},{5,7},{6,4},{7,5},{8,10},{9,11},{10,... | collective-permute-start | bytes 2752520 | tf_op jit(solution)/shard_map/ppermute | solution.py:358
  106.2 11.3 %collective-permute-start.29 = (bf16[2,448,256]{2,1,0:T(8,128)(2,1)S(1)}, bf16[2,448,256]{2,1,0:T(8,128)(2,1)S(1)}, u32[]{:S(2)}, u32[]{:S(2)}) collective-permute-start(bf16[2,448,256]{2,1,0:T(8,128)(2,1)S(1)} %add_convert_fusion.2), channel_id=1, source_target_pairs={{0,4},{8,0},{16,8},{24,16},{28,24},{20,28},{12,20},{4,12},{1,5},{9... | collective-permute-start | bytes 1376264 | tf_op jit(solution)/shard_map/ppermute | solution.py:361
  106.8 11.3 %collective-permute-start.25 = (bf16[2,448,256]{2,1,0:T(8,128)(2,1)S(1)}, bf16[2,448,256]{2,1,0:T(8,128)(2,1)S(1)}, u32[]{:S(2)}, u32[]{:S(2)}) collective-permute-start(bf16[2,448,256]{2,1,0:T(8,128)(2,1)S(1)} %add_convert_fusion.5), channel_id=1, source_target_pairs={{0,8},{8,16},{16,24},{24,28},{28,20},{20,12},{12,4},{4,0},{1,9},{9... | collective-permute-start | bytes 1376264 | tf_op jit(solution)/shard_map/ppermute | solution.py:361
  117.6 10.4 %collective-permute-start.30 = (bf16[2,448,256]{2,1,0:T(8,128)(2,1)S(1)}, bf16[2,448,256]{2,1,0:T(8,128)(2,1)S(1)}, u32[]{:S(2)}, u32[]{:S(2)}) collective-permute-start(bf16[2,448,256]{2,1,0:T(8,128)(2,1)S(1)} %add_convert_fusion.1), channel_id=1, source_target_pairs={{0,4},{8,0},{16,8},{24,16},{28,24},{20,28},{12,20},{4,12},{1,5},{9... | collective-permute-start | bytes 1376264 | tf_op jit(solution)/shard_map/ppermute | solution.py:361
  118.2 10.1 %collective-permute-start.26 = (bf16[2,448,256]{2,1,0:T(8,128)(2,1)S(1)}, bf16[2,448,256]{2,1,0:T(8,128)(2,1)S(1)}, u32[]{:S(2)}, u32[]{:S(2)}) collective-permute-start(bf16[2,448,256]{2,1,0:T(8,128)(2,1)S(1)} %add_convert_fusion.4), channel_id=1, source_target_pairs={{0,8},{8,16},{16,24},{24,28},{28,20},{20,12},{12,4},{4,0},{1,9},{9... | collective-permute-start | bytes 1376264 | tf_op jit(solution)/shard_map/ppermute | solution.py:361
  (8 other events, 6.5 us)

commit v10 on v9

--- a/solution.py
+++ b/solution.py
@@ -99,7 +99,8 @@
     return mark[0], mark[1] * DIGIT + mark[2]
 
 
-def pack_kernel(me_ref, q_ref, up_ref, own_ref, *other_refs):
+def pack_kernel(me_ref, q_ref, up_ref, *refs):
+    own_ref, other_refs = refs[-5], refs[-4:]
     for i in range(4):
         here = pl.ds(pl.multiple_of((me_ref[0] ^ i) * SPAN, SPAN), SPAN)
         for k, ref in enumerate((q_ref, up_ref)):
@@ -109,10 +110,10 @@
                 own_ref[i // 2, k] = ref[:, here]
 
 
-def pack_heads(me, queries, upstream):
+def pack_heads(me, queries, upstream, wait):
     rows = queries.shape[0]
     out = [shaped((2, 2, rows, SPAN), BF16)] + [shaped((rows, SPAN), BF16)] * 4
-    return call(pack_kernel, me, (queries, upstream), out, 2)
+    return call(pack_kernel, me, (queries, upstream, *wait), out, 2)
 
 
 def place_kernel(me_ref, *refs):
@@ -128,24 +129,22 @@
     return call(place_kernel, me, found, [out, out], 3)
 
 
-def project_kernel(steps, depth, halves, first, last, me_ref, *refs):
+def project_kernel(steps, depth, first, last, me_ref, *refs):
     parts, refs = refs[:4], refs[4:]
-    weights, refs = refs[: len(steps) + halves], refs[len(steps) + halves :]
+    weights, refs = refs[: 2 * len(steps)], refs[2 * len(steps) :]
     whole_ref, sems = refs[-2:]
     rows, lanes = parts[0].shape[1:]
     owners = [owner_at(me_ref[1], by) for by in steps]
-    copies = []
-    for i, ref in enumerate(weights):
-        there = whole_ref.at[owners[0], pl.ds(i, 1)] if halves else whole_ref.at[owners[i]]
-        copies.append(pltpu.make_async_copy(ref, there, sems.at[i]))
+    copies = [
+        pltpu.make_async_copy(ref, whole_ref.at[owners[i // 2], i % 2], sems.at[i]) for i, ref in enumerate(weights)
+    ]
     for copy in copies:
         copy.start()
     sums = [0.0, 0.0]
     for b, owner in enumerate(owners):
         left = jnp.concatenate([ref[owner][:, :depth] for ref in parts], axis=0)
         for e in range(2):
-            right = weights[e][0] if halves else weights[b][e]
-            sums[e] = sums[e] + contract(left, right, 1, 0)
+            sums[e] = sums[e] + contract(left, weights[2 * b + e][...], 1, 0)
     if not first:
         sums = [s + refs[0][:, e * PAIR : (e + 1) * PAIR] for e, s in enumerate(sums)]
     if not last:
@@ -165,7 +164,7 @@
         copy.wait()
 
 
-def project(me, steps, parts, weights, before, depth, last=False, halves=False):
+def project(me, steps, parts, weights, before, depth, last=False):
     rows, lanes = parts[0].shape[1:]
     length = 4 * rows
     outs = [shaped((length, 2 * PAIR), F32)]
@@ -175,7 +174,7 @@
     operands = (*parts, *weights, *before)
     count = len(operands)
     return call(
-        functools.partial(project_kernel, steps, depth, int(halves), not before, last),
+        functools.partial(project_kernel, steps, depth, not before, last),
         me,
         operands,
         outs,
@@ -187,14 +186,25 @@
     )
 
 
-def halve_kernel(me_ref, ups_ref, downs_ref, *refs):
-    refs[-2][...] = ups_ref[:1]
-    refs[-1][...] = downs_ref[1:]
-
-
-def halve(me, ups, downs, wait):
-    out = [shaped((1, *ups.shape[1:]), ups.dtype)] * 2
-    return call(halve_kernel, me, (ups, downs, *wait), out, 1, far=tuple(range(2, 2 + len(wait))))
+def hold_kernel(count, me_ref, *refs):
+    for i in range(count):
+        refs[i - count][...] = refs[i][...]
+
+
+def hold(me, arrays, wait):
+    out = [shaped(x.shape, x.dtype) for x in arrays]
+    far = tuple(range(len(arrays), len(arrays) + len(wait)))
+    return call(functools.partial(hold_kernel, len(arrays)), me, (*arrays, *wait), out, 1, far=far)
+
+
+def finish_kernel(me_ref, *refs):
+    for e in range(2):
+        own, ups, downs = refs[3 * e : 3 * e + 3]
+        refs[-1][e] = own[...] + ups[...].astype(F32) + downs[...].astype(F32)
+
+
+def finish(me, terms):
+    return call(finish_kernel, me, terms, shaped((2, *terms[0].shape), F32), 1)
 
 
 def attend_kernel(spot, me_ref, own_ref, q_other, up_other, kv_ref, ids_ref, ids_row_ref, *refs):
@@ -296,8 +306,8 @@
     )
 
 
-def share_kernel(steps, depth, split, me_ref, *refs):
-    parts, g_ref, outs = refs[:4], refs[4], refs[-(2 if split else 1) * len(steps) :]
+def share_kernel(steps, depth, me_ref, *refs):
+    parts, g_ref, outs = refs[:4], refs[4], refs[-2 * len(steps) :]
     rows, lanes = parts[0].shape[1:]
     quarter = [g_ref[pl.ds(pl.multiple_of((me_ref[0] ^ r) * rows, rows), rows), :].astype(F32) for r in range(4)]
     kind = jnp.concatenate([read_marks(ref[0], depth)[0] for ref in parts], axis=0)
@@ -307,20 +317,14 @@
         left = jnp.concatenate([ref[owner] for ref in parts], axis=0)
         total = contract(left, right, 0, 0)
         for e in range(2):
-            block = total[:depth, e * PAIR : (e + 1) * PAIR]
-            if split:
-                outs[2 * i + e][0] = block.astype(BF16)
-            else:
-                outs[i][e] = block
-
-
-def shares(me, steps, parts, grad, depth, split=False, wait=()):
-    if split:
-        out = [shaped((1, depth, PAIR), BF16)] * (2 * len(steps))
-    else:
-        out = [shaped((2, depth, PAIR), F32)] * len(steps)
+            ref = outs[2 * i + e]
+            ref[...] = total[:depth, e * PAIR : (e + 1) * PAIR].astype(ref.dtype)
+
+
+def shares(me, steps, parts, grad, depth, dtype=F32, wait=()):
+    out = [shaped((depth, PAIR), dtype)] * (2 * len(steps))
     far = tuple(range(5, 5 + len(wait)))
-    return call(functools.partial(share_kernel, steps, depth, split), me, (*parts, grad, *wait), out, 1 + len(steps), far=far)
+    return call(functools.partial(share_kernel, steps, depth), me, (*parts, grad, *wait), out, 1 + len(steps), far=far)
 
 
 def in_order(parts, quarters):
@@ -360,31 +364,31 @@
     def turn(x, by):
         return lax.ppermute(x, "fsdp", [(CYCLE[i], CYCLE[(i + by) % fsdp]) for i in range(fsdp)])
 
-    def both_ways(ups, downs):
-        return turn(ups, 1), turn(downs, -1)
-
     me = jnp.stack([me_s, me_f])
     quarters = me_s ^ jnp.arange(seq, dtype=jnp.int32)
     if near_link:
-        weights = [kv_weight, *both_ways(kv_weight, kv_weight)]
-        weights += both_ways(*weights[1:])
-        weights += both_ways(*weights[3:])
+        pair = [kv_weight[0], kv_weight[1]]
+        ups, downs = [pair], [pair]
+        for _ in range(3):
+            ups.append([turn(x, 1) for x in ups[-1]])
+            downs.append([turn(x, -1) for x in downs[-1]])
     else:
         weight = lax.all_gather(kv_weight, "fsdp", axis=0)
 
     blocks = token_blocks(me, tokens, block_ids * 2 + modality, fsdp)
     across = swap(blocks, 2)
-    own, *others = pack_heads(me, queries, cotangent)
+    own, *others = pack_heads(me, queries, cotangent, ups[1][:1] if near_link else ())
     others = [swap(x, 1) for x in others]
     if near_link:
-        across = after(across, weights[3], weights[4], *others)
+        across = after(across, *ups[2], *downs[2], *others)
     parts = [blocks, swap(blocks, 1), across, swap(across, 1)]
 
     if near_link:
-        before = project(me, STEPS[:5], parts, weights[:5], (), depth)
-        weights += both_ways(*halve(me, *weights[5:], (before[0],)))
-        before = project(me, STEPS[5:7], parts, weights[5:7], before, depth)
-        kv, kind, ids, ids_row, weight = project(me, STEPS[7:], parts, weights[7:], before, depth, True, True)
+        before = project(me, STEPS[:5], parts, pair + ups[1] + downs[1] + ups[2] + downs[2], (), depth)
+        last = hold(me, (ups[3][0], downs[3][1]), before[:1])
+        last = [turn(last[0], 1), turn(last[1], -1)]
+        before = project(me, STEPS[5:7], parts, ups[3] + downs[3], before, depth)
+        kv, kind, ids, ids_row, weight = project(me, STEPS[7:], parts, last, before, depth, True)
     else:
         kv, kind, ids, ids_row = project_plain(quarters, parts, weight, depth)
     kv_far = swap(kv, 2)
@@ -395,17 +399,21 @@
 
     grad_c = swap(grad_kv, 1)
     if near_link:
-        ups, downs = both_ways(*shares(me, STEPS[7:], parts, grad_kv, depth, True))
+        first = shares(me, STEPS[7:], parts, grad_kv, depth, BF16)
+        ups, downs = [turn(first[0], 1), None], [None, turn(first[1], -1)]
     mine, away = hidden_grad(me, kind, grad_kv, grad_c, weight, swap(weight, 1), rows)
     if near_link:
         terms = shares(me, STEPS[5:7], parts, grad_kv, depth, wait=(away,))
         terms += shares(me, STEPS[:5], parts, grad_kv, depth)
-        none = jnp.zeros_like(ups)
-        ups, downs = jnp.concatenate([ups, none]), jnp.concatenate([none, downs])
-        for i in (0, 5, 3):
-            down, up = terms[i : i + 2]
-            ups, downs = both_ways((up + ups.astype(F32)).astype(BF16), (down + downs.astype(F32)).astype(BF16))
-        grad_weight = terms[2] + ups.astype(F32) + downs.astype(F32)
+
+        def added(term, x):
+            return (term if x is None else term + x.astype(F32)).astype(BF16)
+
+        for i in (0, 10, 6):
+            down, up = terms[i : i + 2], terms[i + 2 : i + 4]
+            ups = [turn(added(up[e], ups[e]), 1) for e in range(2)]
+            downs = [turn(added(down[e], downs[e]), -1) for e in range(2)]
+        grad_weight = finish(me, (terms[4], ups[0], downs[0], terms[5], ups[1], downs[1]))
     else:
         grad_weight = weight_plain(quarters, parts, grad_kv, depth)
     grad_tokens = (mine + swap(away, 2).astype(F32)).astype(BF16)

time: 130 us -> 148 us (1.14)
  starting transfers between devices: 24.7 us -> 38.1 us
  local copies, waits for them, and re-layouts: 15.1 us -> 20.4 us
  Pallas kernels: 29.9 us -> 33.9 us
  waiting for transfers between devices: 55.2 us -> 51.4 us
    ppermute x16 -> x28, starting transfers between devices: 16.6 us -> 30.1 us  [turn(): lax.ppermute(x, 'fsdp', [(CYCLE[i], CYCLE[(i + by) % fsdp]) for i in rang...]
    unnamed x50 -> x68, local copies, waits for them, and re-layouts: 15.1 us -> 19.3 us
    pallas_call x13 -> x14, Pallas kernels: 28.5 us -> 32.4 us  [call(): pl.pallas_call(body, in_specs=[pl.BlockSpec(memory_space=pltpu.SMEM)] + [...]
    ppermute x15, waiting for transfers between devices: 15.3 us -> 12.2 us  [swap(): return lax.ppermute(x, 'seq', [(i, i ^ bit) for i in range(seq)])]
    ppermute x16 -> x28, waiting for transfers between devices: 39.9 us -> 39.3 us  [turn(): lax.ppermute(x, 'fsdp', [(CYCLE[i], CYCLE[(i + by) % fsdp]) for i in rang...]
  transfers between devices with their start and end apart: 31 -> 43, of which waited for: 18 -> 19; matrix products, arithmetic and copies ran while one was open for 1% -> 1% of each run, Pallas kernels for 21% -> 21%
where the time goes in v10:
time: 148 us; the launch traced here: 147 us
  waiting for transfers between devices  51.4 us (35%)
  starting transfers between devices  38.1 us (26%)
  Pallas kernels  33.9 us (23%)
  local copies, waits for them, and re-layouts  20.4 us (14%)
  other arithmetic  2.52 us (2%)
    ppermute x28, waiting for transfers between devices, turn(): lax.ppermute(x, 'fsdp', [(CYCLE[i], CYCLE[(i + by) % fsdp]) for i in rang...  39.3 us
    pallas_call x14, Pallas kernels, call(): pl.pallas_call(body, in_specs=[pl.BlockSpec(memory_space=pltpu.SMEM)] + [...  32.4 us
    ppermute x28, starting transfers between devices, turn(): lax.ppermute(x, 'fsdp', [(CYCLE[i], CYCLE[(i + by) % fsdp]) for i in rang...  30.1 us
    unnamed x68, local copies, waits for them, and re-layouts  19.3 us
    ppermute x15, waiting for transfers between devices, swap(): return lax.ppermute(x, 'seq', [(i, i ^ bit) for i in range(seq)])  12.2 us
    ppermute x15, starting transfers between devices, swap(): return lax.ppermute(x, 'seq', [(i, i ^ bit) for i in range(seq)])  8.01 us
  transfers between devices with their start and end apart: 43, of which 19 were waited for; matrix products, arithmetic and copies ran while one was open for 1% of the time, Pallas kernels for 21%

profile of v10, /device:TPU:0, one launch (start us, length us, event | category | flops | bytes accessed | tf_op | source)
XLA Modules:
  0.0 147.4 jit_solution(4043650258140761883)
XLA Ops:
  1.4 1.2 copy-done.5
  3.5 3.0 %collective-permute-start.4 = (bf16[8,128,512]{2,1,0:T(8,128)(2,1)S(1)}, bf16[8,128,512]{2,1,0:T(8,128)(2,1)S(1)}, u32[]{:S(2)}, u32[]{:S(2)}) collective-permute-start(bf16[8,128,512]{2,1,0:T(8,128)(2,1)S(1)} %shard_map.94.refs_0_), channel_id=1, source_target_pairs={{0,2},{1,3},{2,0},{3,1},{4,6},{5,7},{6,4},{7,5},{8,10},{9,11},{10,... | collective-permute-start | bytes 3145736 | tf_op jit(solution)/shard_map/ppermute | solution.py:362
  6.5 1.1 slice_bitcast_fusion
  7.6 1.6 %collective-permute-start = (bf16[448,256]{1,0:T(8,128)(2,1)S(1)}, bf16[448,256]{1,0:T(8,128)(2,1)S(1)}, u32[]{:S(2)}, u32[]{:S(2)}) collective-permute-start(bf16[448,256]{1,0:T(8,128)(2,1)S(1)} %get-tuple-element.93.refs_4_), channel_id=1, source_target_pairs={{0,8},{8,16},{16,24},{24,28},{28,20},{20,12},{12,4},{4,0},{1,9},{9... | collective-permute-start | bytes 688136 | tf_op jit(solution)/shard_map/ppermute | solution.py:365
  9.2 1.6 %collective-permute-start.6 = (bf16[448,256]{1,0:T(8,128)(2,1)S(1)}, bf16[448,256]{1,0:T(8,128)(2,1)S(1)}, u32[]{:S(2)}, u32[]{:S(2)}) collective-permute-start(bf16[448,256]{1,0:T(8,128)(2,1)S(1)} %get-tuple-element.92.refs_5_), channel_id=1, source_target_pairs={{0,8},{8,16},{16,24},{24,28},{28,20},{20,12},{12,4},{4,0},{1,9},{9... | collective-permute-start | bytes 688136 | tf_op jit(solution)/shard_map/ppermute | solution.py:365
  11.7 4.5 %collective-permute-done.refs_0_.refs_6_ = bf16[448,256]{1,0:T(8,128)(2,1)S(1)} collective-permute-done((bf16[448,256]{1,0:T(8,128)(2,1)S(1)}, bf16[448,256]{1,0:T(8,128)(2,1)S(1)}, u32[]{:S(2)}, u32[]{:S(2)}) %collective-permute-start) | collective-permute-done | bytes 229408 | tf_op jit(solution)/shard_map/ppermute | solution.py:365
  16.2 1.2 copy-done.6
  17.4 1.2 copy-done.7
  20.7 1.6 %collective-permute-start.5 = (bf16[448,256]{1,0:T(8,128)(2,1)S(1)}, bf16[448,256]{1,0:T(8,128)(2,1)S(1)}, u32[]{:S(2)}, u32[]{:S(2)}) collective-permute-start(bf16[448,256]{1,0:T(8,128)(2,1)S(1)} %collective-permute-done.refs_0_.refs_6_), channel_id=1, source_target_pairs={{0,8},{8,16},{16,24},{24,28},{28,20},{20,12},{12,4},{4,0},{1,9},{9... | collective-permute-start | bytes 688136 | tf_op jit(solution)/shard_map/ppermute | solution.py:365
  22.2 1.6 %collective-permute-start.7 = (bf16[448,256]{1,0:T(8,128)(2,1)S(1)}, bf16[448,256]{1,0:T(8,128)(2,1)S(1)}, u32[]{:S(2)}, u32[]{:S(2)}) collective-permute-start(bf16[448,256]{1,0:T(8,128)(2,1)S(1)} %collective-permute-done.6.refs_7_), channel_id=1, source_target_pairs={{0,8},{8,16},{16,24},{24,28},{28,20},{20,12},{12,4},{4,0},{1,9},{9... | collective-permute-start | bytes 688136 | tf_op jit(solution)/shard_map/ppermute | solution.py:365
  25.7 3.4 %collective-permute-done.5.refs_1_.refs_10_ = bf16[448,256]{1,0:T(8,128)(2,1)S(1)} collective-permute-done((bf16[448,256]{1,0:T(8,128)(2,1)S(1)}, bf16[448,256]{1,0:T(8,128)(2,1)S(1)}, u32[]{:S(2)}, u32[]{:S(2)}) %collective-permute-start.5) | collective-permute-done | bytes 229408 | tf_op jit(solution)/shard_map/ppermute | solution.py:365
  29.1 1.5 %collective-permute-start.11 = (bf16[448,256]{1,0:T(8,128)(2,1)S(1)}, bf16[448,256]{1,0:T(8,128)(2,1)S(1)}, u32[]{:S(2)}, u32[]{:S(2)}) collective-permute-start(bf16[448,256]{1,0:T(8,128)(2,1)S(1)} %collective-permute-done.10.refs_9_), channel_id=1, source_target_pairs={{0,4},{8,0},{16,8},{24,16},{28,24},{20,28},{12,20},{4,12},{1,5},{9... | collective-permute-start | bytes 688136 | tf_op jit(solution)/shard_map/ppermute | solution.py:365
  31.3 1.9 %collective-permute-done.7.refs_2_.refs_11_ = bf16[448,256]{1,0:T(8,128)(2,1)S(1)} collective-permute-done((bf16[448,256]{1,0:T(8,128)(2,1)S(1)}, bf16[448,256]{1,0:T(8,128)(2,1)S(1)}, u32[]{:S(2)}, u32[]{:S(2)}) %collective-permute-start.7) | collective-permute-done | bytes 229408 | tf_op jit(solution)/shard_map/ppermute | solution.py:365
  34.4 3.0 %collective-permute-done.11.refs_4_.refs_13_ = bf16[448,256]{1,0:T(8,128)(2,1)S(1)} collective-permute-done((bf16[448,256]{1,0:T(8,128)(2,1)S(1)}, bf16[448,256]{1,0:T(8,128)(2,1)S(1)}, u32[]{:S(2)}, u32[]{:S(2)}) %collective-permute-start.11) | collective-permute-done | bytes 229408 | tf_op jit(solution)/shard_map/ppermute | solution.py:365
  39.9 1.6 %shard_map.95.refs_2_ = bf16[8,128,512]{2,1,0:T(8,128)(2,1)} custom-call(bf16[8,128,512]{2,1,0:T(8,128)(2,1)} %copy-done, bf16[448,256]{1,0:T(8,128)(2,1)} %copy-done.24, bf16[448,256]{1,0:T(8,128)(2,1)} %copy-done.20, bf16[448,256]{1,0:T(8,128)(2,1)} %copy-done.22, bf16[448,256]{1,0:T(8,128)(2,1)} %copy-done.26, ...), custom_call_target="tpu_custom_call", output_to_operand_aliasing={{}: (0, {})} | custom-call | tf_op jit(solution)/shard_map/pallas_call | solution.py:59
  41.5 1.6 %collective-permute-start.15 = (bf16[448,256]{1,0:T(8,128)(2,1)}, bf16[448,256]{1,0:T(8,128)(2,1)S(1)}, u32[]{:S(2)}, u32[]{:S(2)}) collective-permute-start(bf16[448,256]{1,0:T(8,128)(2,1)} %copy-done.24), channel_id=1, source_target_pairs={{0,8},{8,16},{16,24},{24,28},{28,20},{20,12},{12,4},{4,0},{1,9},{9... | collective-permute-start | bytes 688136 | tf_op jit(solution)/shard_map/ppermute | solution.py:365
  43.5 1.6 %collective-permute-start.19 = (bf16[448,256]{1,0:T(8,128)(2,1)}, bf16[448,256]{1,0:T(8,128)(2,1)S(1)}, u32[]{:S(2)}, u32[]{:S(2)}) collective-permute-start(bf16[448,256]{1,0:T(8,128)(2,1)} %copy-done.20), channel_id=1, source_target_pairs={{0,8},{8,16},{16,24},{24,28},{28,20},{20,12},{12,4},{4,0},{1,9},{9... | collective-permute-start | bytes 688136 | tf_op jit(solution)/shard_map/ppermute | solution.py:365
  45.6 1.2 copy-done.1
  55.2 5.2 %shard_map.96 = (f32[512,512]{1,0:T(8,128)S(1)}, bf16[8,2,448,256]{3,2,1,0:T(8,128)(2,1)S(1)}) custom-call(s32[2]{0:T(128)S(1)} %pad_add_fusion.me_ref, bf16[8,128,512]{2,1,0:T(8,128)(2,1)S(1)} %shard_map.94.refs_0_, bf16[8,128,512]{2,1,0:T(8,128)(2,1)S(1)} %collective-permute-done.3.refs_1_, bf16[8,128,512]{2,1,0:T(8,128)(2,1)S(1)} %copy-done.1, ...), custom_call_target="tpu_custom_call" | custom-call | bytes 9000000 | tf_op jit(solution)/shard_map/pallas_call | solution.py:36
  61.0 1.6 %collective-permute-start.17 = (bf16[448,256]{1,0:T(8,128)(2,1)S(1)}, bf16[448,256]{1,0:T(8,128)(2,1)S(1)}, u32[]{:S(2)}, u32[]{:S(2)}) collective-permute-start(bf16[448,256]{1,0:T(8,128)(2,1)S(1)} %get-tuple-element.54), channel_id=1, source_target_pairs={{0,8},{8,16},{16,24},{24,28},{28,20},{20,12},{12,4},{4,0},{1,9},{9... | collective-permute-start | bytes 688136 | tf_op jit(solution)/shard_map/ppermute | solution.py:365
  63.1 2.5 %shard_map.98 = (f32[512,512]{1,0:T(8,128)S(1)}, bf16[8,2,448,256]{3,2,1,0:T(8,128)(2,1)S(1)}) custom-call(s32[2]{0:T(128)S(1)} %pad_add_fusion.me_ref, bf16[8,128,512]{2,1,0:T(8,128)(2,1)S(1)} %shard_map.94.refs_0_, bf16[8,128,512]{2,1,0:T(8,128)(2,1)S(1)} %collective-permute-done.3.refs_1_, ...), custom_call_target="tpu_custom_call", output_to_operand_aliasing={{1}: (10, {})} | custom-call | bytes 9000000 | tf_op jit(solution)/shard_map/pallas_call | solution.py:36
  65.6 2.4 %collective-permute-done.17.refs_4_ = bf16[448,256]{1,0:T(8,128)(2,1)S(1)} collective-permute-done((bf16[448,256]{1,0:T(8,128)(2,1)S(1)}, bf16[448,256]{1,0:T(8,128)(2,1)S(1)}, u32[]{:S(2)}, u32[]{:S(2)}) %collective-permute-start.17) | collective-permute-done | bytes 229408 | tf_op jit(solution)/shard_map/ppermute | solution.py:365
  68.0 1.3 collective-permute-done.18.refs_5_
  69.3 1.8 %shard_map.99 = (bf16[512,256]{1,0:T(8,128)(2,1)S(1)}, f32[512,1]{1,0:T(8,128)S(1)}, f32[512,1]{1,0:T(8,128)S(1)}, f32[1,512]{1,0:T(1,128)S(1)}, bf16[8,2,448,256]{3,2,1,0:T(8,128)(2,1)S(1)}) custom-call(s32[2]{0:T(128)S(1)} %pad_add_fusion.me_ref, bf16[8,128,512]{2,1,0:T(8,128)(2,1)S(1)} %shard_map.94.refs_0_, ...), custom_call_target="tpu_custom_call", output_to_operand_aliasing={{4}: (8, {})} | custom-call | bytes 9000000 | tf_op jit(solution)/shard_map/pallas_call | solution.py:36
  71.7 8.1 %collective-permute-done.21.kv_ref = bf16[512,256]{1,0:T(8,128)(2,1)S(1)} collective-permute-done((bf16[512,256]{1,0:T(8,128)(2,1)S(1)}, bf16[512,256]{1,0:T(8,128)(2,1)S(1)}, u32[]{:S(2)}, u32[]{:S(2)}) %collective-permute-start.21) | collective-permute-done | bytes 262176 | tf_op jit(solution)/shard_map/ppermute | solution.py:362
  79.9 4.6 %shard_map.100 = (bf16[2,128,896]{2,1,0:T(8,128)(2,1)S(1)}, bf16[2,128,896]{2,1,0:T(8,128)(2,1)S(1)}, f32[256,256]{1,0:T(8,128)S(1)}, bf16[256,256]{1,0:T(8,128)(2,1)S(1)}) custom-call(s32[2]{0:T(128)S(1)} %pad_add_fusion.me_ref, bf16[2,2,128,896]{3,2,1,0:T(8,128)(2,1)S(1)} %copy-done.4, bf16[128,896]{1,0:T(8,128)(2,1)S(1)} %copy-done.13, ...), custom_call_target="tpu_custom_call" | custom-call | bytes 18000000 | tf_op jit(solution)/shard_map/pallas_call | solution.py:36
  85.1 1.5 %collective-permute-start.24 = (f32[256,256]{1,0:T(8,128)S(1)}, f32[256,256]{1,0:T(8,128)S(1)}, u32[]{:S(2)}, u32[]{:S(2)}) collective-permute-start(f32[256,256]{1,0:T(8,128)S(1)} %get-tuple-element.62.refs_0_), channel_id=1, source_target_pairs={{0,2},{1,3},{2,0},{3,1},{4,6},{5,7},{6,4},{7,5},{8,10},{9,11},{10,... | collective-permute-start | bytes 786440 | tf_op jit(solution)/shard_map/ppermute | solution.py:362
  86.6 4.6 %shard_map.101 = (bf16[2,128,896]{2,1,0:T(8,128)(2,1)S(1)}, bf16[2,128,896]{2,1,0:T(8,128)(2,1)S(1)}, f32[256,256]{1,0:T(8,128)S(1)}, f32[256,256]{1,0:T(8,128)S(1)}) custom-call(s32[2]{0:T(128)S(1)} %pad_add_fusion.me_ref, bf16[2,2,128,896]{3,2,1,0:T(8,128)(2,1)S(1)} %copy-done.4, bf16[128,896]{1,0:T(8,128)(2,1)S(1)} %copy-done.17, ...), custom_call_target="tpu_custom_call" | custom-call | bytes 18000000 | tf_op jit(solution)/shard_map/pallas_call | solution.py:36
  91.3 4.0 %collective-permute-done.24 = f32[256,256]{1,0:T(8,128)S(1)} collective-permute-done((f32[256,256]{1,0:T(8,128)S(1)}, f32[256,256]{1,0:T(8,128)S(1)}, u32[]{:S(2)}, u32[]{:S(2)}) %collective-permute-start.24) | collective-permute-done | bytes 262176 | tf_op jit(solution)/shard_map/ppermute | solution.py:362
  95.4 1.3 shard_map.106
  96.6 1.6 %collective-permute-start.29 = (bf16[448,256]{1,0:T(8,128)(2,1)S(1)}, bf16[448,256]{1,0:T(8,128)(2,1)S(1)}, u32[]{:S(2)}, u32[]{:S(2)}) collective-permute-start(bf16[448,256]{1,0:T(8,128)(2,1)S(1)} %get-tuple-element.80), channel_id=1, source_target_pairs={{0,8},{8,16},{16,24},{24,28},{28,20},{20,12},{12,4},{4,0},{1,9},{9... | collective-permute-start | bytes 688136 | tf_op jit(solution)/shard_map/ppermute | solution.py:365
  98.7 2.3 %shard_map.104 = (f32[448,256]{1,0:T(8,128)S(1)}, f32[448,256]{1,0:T(8,128)S(1)}, f32[448,256]{1,0:T(8,128)S(1)}, f32[448,256]{1,0:T(8,128)S(1)}, f32[448,256]{1...) custom-call(s32[2]{0:T(128)S(1)} %pad_add_fusion.me_ref, ...), custom_call_target="tpu_custom_call" | custom-call | bytes 18000000 | tf_op jit(solution)/shard_map/pallas_call | solution.py:36
  101.9 2.9 %shard_map.103 = (f32[128,3584]{1,0:T(8,128)S(1)}, bf16[128,3584]{1,0:T(8,128)(2,1)S(1)}) custom-call(s32[2]{0:T(128)S(1)} %pad_add_fusion.me_ref, f32[512,1]{1,0:T(8,128)S(1)} %get-tuple-element.69.kind_ref, bf16[512,256]{1,0:T(8,128)(2,1)S(1)} %pad_maximum_fusion.g_ref.refs_4_, bf16[512,256]{1,0:T(8,128)(2,1)S(1)} %collective-permute-done.26.gc_ref, ...), custom_call_target="tpu_custom_call" | custom-call | bytes 21000000 | tf_op jit(solution)/shard_map/pallas_call | solution.py:36
  105.4 1.5 %shard_map.105 = (f32[448,256]{1,0:T(8,128)S(1)}, f32[448,256]{1,0:T(8,128)S(1)}, f32[448,256]{1,0:T(8,128)S(1)}, f32[448,256]{1,0:T(8,128)S(1)}) custom-call(s32[2]{0:T(128)S(1)} %pad_add_fusion.me_ref, bf16[8,128,512]{2,1,0:T(8,128)(2,1)S(1)} %shard_map.94.refs_0_, bf16[8,128,512]{2,1,0:T(8,128)(2,1)S(1)} %collective-permute-done.3.refs_1_, ...), custom_call_target="tpu_custom_call" | custom-call | bytes 9000000 | tf_op jit(solution)/shard_map/pallas_call | solution.py:36
  107.0 1.5 %collective-permute-start.30 = (bf16[448,256]{1,0:T(8,128)(2,1)S(1)}, bf16[448,256]{1,0:T(8,128)(2,1)S(1)}, u32[]{:S(2)}, u32[]{:S(2)}) collective-permute-start(bf16[448,256]{1,0:T(8,128)(2,1)S(1)} %add_convert_fusion.10), channel_id=1, source_target_pairs={{0,8},{8,16},{16,24},{24,28},{28,20},{20,12},{12,4},{4,0},{1,9},{9... | collective-permute-start | bytes 688136 | tf_op jit(solution)/shard_map/ppermute | solution.py:365
  109.6 4.5 %collective-permute-done.30 = bf16[448,256]{1,0:T(8,128)(2,1)S(1)} collective-permute-done((bf16[448,256]{1,0:T(8,128)(2,1)S(1)}, bf16[448,256]{1,0:T(8,128)(2,1)S(1)}, u32[]{:S(2)}, u32[]{:S(2)}) %collective-permute-start.30) | collective-permute-done | bytes 229408 | tf_op jit(solution)/shard_map/ppermute | solution.py:365
  114.2 1.5 %collective-permute-start.36 = (bf16[448,256]{1,0:T(8,128)(2,1)S(1)}, bf16[448,256]{1,0:T(8,128)(2,1)S(1)}, u32[]{:S(2)}, u32[]{:S(2)}) collective-permute-start(bf16[448,256]{1,0:T(8,128)(2,1)S(1)} %convert_element_type.90), channel_id=1, source_target_pairs={{0,8},{8,16},{16,24},{24,28},{28,20},{20,12},{12,4},{4,0},{1,9},{9... | collective-permute-start | bytes 688136 | tf_op jit(solution)/shard_map/ppermute | solution.py:365
  116.5 3.9 %collective-permute-done.36 = bf16[448,256]{1,0:T(8,128)(2,1)S(1)} collective-permute-done((bf16[448,256]{1,0:T(8,128)(2,1)S(1)}, bf16[448,256]{1,0:T(8,128)(2,1)S(1)}, u32[]{:S(2)}, u32[]{:S(2)}) %collective-permute-start.36) | collective-permute-done | bytes 229408 | tf_op jit(solution)/shard_map/ppermute | solution.py:365
  120.4 1.5 %collective-permute-start.31 = (bf16[448,256]{1,0:T(8,128)(2,1)S(1)}, bf16[448,256]{1,0:T(8,128)(2,1)S(1)}, u32[]{:S(2)}, u32[]{:S(2)}) collective-permute-start(bf16[448,256]{1,0:T(8,128)(2,1)S(1)} %add_convert_fusion.9), channel_id=1, source_target_pairs={{0,8},{8,16},{16,24},{24,28},{28,20},{20,12},{12,4},{4,0},{1,9},{9... | collective-permute-start | bytes 688136 | tf_op jit(solution)/shard_map/ppermute | solution.py:365
  122.6 4.2 %collective-permute-done.31 = bf16[448,256]{1,0:T(8,128)(2,1)S(1)} collective-permute-done((bf16[448,256]{1,0:T(8,128)(2,1)S(1)}, bf16[448,256]{1,0:T(8,128)(2,1)S(1)}, u32[]{:S(2)}, u32[]{:S(2)}) %collective-permute-start.31) | collective-permute-done | bytes 229408 | tf_op jit(solution)/shard_map/ppermute | solution.py:365
  126.8 1.5 %collective-permute-start.37 = (bf16[448,256]{1,0:T(8,128)(2,1)S(1)}, bf16[448,256]{1,0:T(8,128)(2,1)S(1)}, u32[]{:S(2)}, u32[]{:S(2)}) collective-permute-start(bf16[448,256]{1,0:T(8,128)(2,1)S(1)} %add_convert_fusion.5), channel_id=1, source_target_pairs={{0,8},{8,16},{16,24},{24,28},{28,20},{20,12},{12,4},{4,0},{1,9},{9... | collective-permute-start | bytes 688136 | tf_op jit(solution)/shard_map/ppermute | solution.py:365
  129.3 5.0 %collective-permute-done.37 = bf16[448,256]{1,0:T(8,128)(2,1)S(1)} collective-permute-done((bf16[448,256]{1,0:T(8,128)(2,1)S(1)}, bf16[448,256]{1,0:T(8,128)(2,1)S(1)}, u32[]{:S(2)}, u32[]{:S(2)}) %collective-permute-start.37) | collective-permute-done | bytes 229408 | tf_op jit(solution)/shard_map/ppermute | solution.py:365
  134.3 1.6 %collective-permute-start.32 = (bf16[448,256]{1,0:T(8,128)(2,1)S(1)}, bf16[448,256]{1,0:T(8,128)(2,1)S(1)}, u32[]{:S(2)}, u32[]{:S(2)}) collective-permute-start(bf16[448,256]{1,0:T(8,128)(2,1)S(1)} %add_convert_fusion.8), channel_id=1, source_target_pairs={{0,8},{8,16},{16,24},{24,28},{28,20},{20,12},{12,4},{4,0},{1,9},{9... | collective-permute-start | bytes 688136 | tf_op jit(solution)/shard_map/ppermute | solution.py:365
  136.8 1.5 %collective-permute-start.38 = (bf16[448,256]{1,0:T(8,128)(2,1)S(1)}, bf16[448,256]{1,0:T(8,128)(2,1)S(1)}, u32[]{:S(2)}, u32[]{:S(2)}) collective-permute-start(bf16[448,256]{1,0:T(8,128)(2,1)S(1)} %add_convert_fusion.4), channel_id=1, source_target_pairs={{0,8},{8,16},{16,24},{24,28},{28,20},{20,12},{12,4},{4,0},{1,9},{9... | collective-permute-start | bytes 688136 | tf_op jit(solution)/shard_map/ppermute | solution.py:365
  138.9 1.9 %shard_map.102 = (bf16[128,3584]{1,0:T(8,128)(2,1)}, bf16[128,3584]{1,0:T(8,128)(2,1)}) custom-call(s32[2]{0:T(128)S(1)} %pad_add_fusion.me_ref, bf16[2,128,896]{2,1,0:T(8,128)(2,1)S(1)} %get-tuple-element.63.refs_0_, bf16[2,128,896]{2,1,0:T(8,128)(2,1)S(1)} %collective-permute-done.22.refs_1_, bf16[2,128,896]{2,1,0:T(8,128)(2,1)S(1)} %get-tuple-element.65.refs_2_, ...), custom_call_target="tpu_custom_call" | custom-call | bytes 9000000 | tf_op jit(solution)/shard_map/pallas_call | solution.py:36
  140.8 1.4 collective-permute-done.35.refs_2_
  142.9 1.8 %collective-permute-done.42.refs_5_ = bf16[448,256]{1,0:T(8,128)(2,1)S(1)} collective-permute-done((bf16[448,256]{1,0:T(8,128)(2,1)S(1)}, bf16[448,256]{1,0:T(8,128)(2,1)S(1)}, u32[]{:S(2)}, u32[]{:S(2)}) %collective-permute-start.42) | collective-permute-done | bytes 229408 | tf_op jit(solution)/shard_map/ppermute | solution.py:365
  144.7 1.6 %shard_map.107 = f32[2,448,256]{2,1,0:T(8,128)} custom-call(s32[2]{0:T(128)S(1)} %pad_add_fusion.me_ref, f32[448,256]{1,0:T(8,128)S(1)} %get-tuple-element.76.refs_0_, bf16[448,256]{1,0:T(8,128)(2,1)S(1)} %collective-permute-done.32.refs_1_, bf16[448,256]{1,0:T(8,128)(2,1)S(1)} %collective-permute-done.35.refs_2_, f32[448,256]{1,0:T(8,128)S(1)} %get-tuple-element.84.refs_3_, ...), custom_call_target="tpu_custom_call" | custom-call | bytes 3000000 | tf_op jit(solution)/shard_map/pallas_call | solution.py:36
  (140 shorter events, 31.6 us)
Async XLA Ops:
  3.5 35.5 %collective-permute-start.4 = (bf16[8,128,512]{2,1,0:T(8,128)(2,1)S(1)}, bf16[8,128,512]{2,1,0:T(8,128)(2,1)S(1)}, u32[]{:S(2)}, u32[]{:S(2)}) collective-permute-start(bf16[8,128,512]{2,1,0:T(8,128)(2,1)S(1)} %shard_map.94.refs_0_), channel_id=1, source_target_pairs={{0,2},{1,3},{2,0},{3,1},{4,6},{5,7},{6,4},{7,5},{8,10},{9,11},{10,... | collective-permute-start | bytes 3145736 | tf_op jit(solution)/shard_map/ppermute | solution.py:362
  7.6 26.3 %copy-start.10 = (bf16[448,256]{1,0:T(8,128)(2,1)}, bf16[448,256]{1,0:T(8,128)(2,1)S(1)}, u32[]{:S(2)}) copy-start(bf16[448,256]{1,0:T(8,128)(2,1)S(1)} %get-tuple-element.93.refs_4_) | copy-start | bytes 688132
  7.6 29.9 %copy-start.8 = (bf16[448,256]{1,0:T(8,128)(2,1)}, bf16[448,256]{1,0:T(8,128)(2,1)S(1)}, u32[]{:S(2)}) copy-start(bf16[448,256]{1,0:T(8,128)(2,1)S(1)} %get-tuple-element.92.refs_5_) | copy-start | bytes 688132
  7.6 8.6 %collective-permute-start = (bf16[448,256]{1,0:T(8,128)(2,1)S(1)}, bf16[448,256]{1,0:T(8,128)(2,1)S(1)}, u32[]{:S(2)}, u32[]{:S(2)}) collective-permute-start(bf16[448,256]{1,0:T(8,128)(2,1)S(1)} %get-tuple-element.93.refs_4_), channel_id=1, source_target_pairs={{0,8},{8,16},{16,24},{24,28},{28,20},{20,12},{12,4},{4,0},{1,9},{9... | collective-permute-start | bytes 688136 | tf_op jit(solution)/shard_map/ppermute | solution.py:365
  9.2 10.9 %collective-permute-start.6 = (bf16[448,256]{1,0:T(8,128)(2,1)S(1)}, bf16[448,256]{1,0:T(8,128)(2,1)S(1)}, u32[]{:S(2)}, u32[]{:S(2)}) collective-permute-start(bf16[448,256]{1,0:T(8,128)(2,1)S(1)} %get-tuple-element.92.refs_5_), channel_id=1, source_target_pairs={{0,8},{8,16},{16,24},{24,28},{28,20},{20,12},{12,4},{4,0},{1,9},{9... | collective-permute-start | bytes 688136 | tf_op jit(solution)/shard_map/ppermute | solution.py:365
  10.8 9.9 %collective-permute-start.8 = (bf16[448,256]{1,0:T(8,128)(2,1)S(1)}, bf16[448,256]{1,0:T(8,128)(2,1)S(1)}, u32[]{:S(2)}, u32[]{:S(2)}) collective-permute-start(bf16[448,256]{1,0:T(8,128)(2,1)S(1)} %get-tuple-element.93.refs_4_), channel_id=1, source_target_pairs={{0,4},{8,0},{16,8},{24,16},{28,24},{20,28},{12,20},{4,12},{1,5},{9... | collective-permute-start | bytes 688136 | tf_op jit(solution)/shard_map/ppermute | solution.py:365
  11.2 11.0 %collective-permute-start.10 = (bf16[448,256]{1,0:T(8,128)(2,1)S(1)}, bf16[448,256]{1,0:T(8,128)(2,1)S(1)}, u32[]{:S(2)}, u32[]{:S(2)}) collective-permute-start(bf16[448,256]{1,0:T(8,128)(2,1)S(1)} %get-tuple-element.92.refs_5_), channel_id=1, source_target_pairs={{0,4},{8,0},{16,8},{24,16},{28,24},{20,28},{12,20},{4,12},{1,5},{9... | collective-permute-start | bytes 688136 | tf_op jit(solution)/shard_map/ppermute | solution.py:365
  20.1 4.4 %collective-permute-start.1 = (bf16[128,896]{1,0:T(8,128)(2,1)S(1)}, bf16[128,896]{1,0:T(8,128)(2,1)S(1)}, u32[]{:S(2)}, u32[]{:S(2)}) collective-permute-start(bf16[128,896]{1,0:T(8,128)(2,1)S(1)} %get-tuple-element.49), channel_id=1, source_target_pairs={{0,1},{1,0},{2,3},{3,2},{4,5},{5,4},{6,7},{7,6},{8,9},{9,8},{10,11... | collective-permute-start | bytes 688136 | tf_op jit(solution)/shard_map/ppermute | solution.py:362
  20.2 4.4 %collective-permute-start.2 = (bf16[128,896]{1,0:T(8,128)(2,1)S(1)}, bf16[128,896]{1,0:T(8,128)(2,1)S(1)}, u32[]{:S(2)}, u32[]{:S(2)}) collective-permute-start(bf16[128,896]{1,0:T(8,128)(2,1)S(1)} %get-tuple-element.50), channel_id=1, source_target_pairs={{0,1},{1,0},{2,3},{3,2},{4,5},{5,4},{6,7},{7,6},{8,9},{9,8},{10,11... | collective-permute-start | bytes 688136 | tf_op jit(solution)/shard_map/ppermute | solution.py:362
  20.7 8.5 %collective-permute-start.5 = (bf16[448,256]{1,0:T(8,128)(2,1)S(1)}, bf16[448,256]{1,0:T(8,128)(2,1)S(1)}, u32[]{:S(2)}, u32[]{:S(2)}) collective-permute-start(bf16[448,256]{1,0:T(8,128)(2,1)S(1)} %collective-permute-done.refs_0_.refs_6_), channel_id=1, source_target_pairs={{0,8},{8,16},{16,24},{24,28},{28,20},{20,12},{12,4},{4,0},{1,9},{9... | collective-permute-start | bytes 688136 | tf_op jit(solution)/shard_map/ppermute | solution.py:365
  22.2 10.9 %collective-permute-start.7 = (bf16[448,256]{1,0:T(8,128)(2,1)S(1)}, bf16[448,256]{1,0:T(8,128)(2,1)S(1)}, u32[]{:S(2)}, u32[]{:S(2)}) collective-permute-start(bf16[448,256]{1,0:T(8,128)(2,1)S(1)} %collective-permute-done.6.refs_7_), channel_id=1, source_target_pairs={{0,8},{8,16},{16,24},{24,28},{28,20},{20,12},{12,4},{4,0},{1,9},{9... | collective-permute-start | bytes 688136 | tf_op jit(solution)/shard_map/ppermute | solution.py:365
  24.5 12.9 %collective-permute-start.12 = (bf16[128,896]{1,0:T(8,128)(2,1)S(1)}, bf16[128,896]{1,0:T(8,128)(2,1)S(1)}, u32[]{:S(2)}, u32[]{:S(2)}) collective-permute-start(bf16[128,896]{1,0:T(8,128)(2,1)S(1)} %get-tuple-element.51), channel_id=1, source_target_pairs={{0,1},{1,0},{2,3},{3,2},{4,5},{5,4},{6,7},{7,6},{8,9},{9,8},{10,11... | collective-permute-start | bytes 688136 | tf_op jit(solution)/shard_map/ppermute | solution.py:362
  24.5 9.3 %collective-permute-start.9 = (bf16[448,256]{1,0:T(8,128)(2,1)S(1)}, bf16[448,256]{1,0:T(8,128)(2,1)S(1)}, u32[]{:S(2)}, u32[]{:S(2)}) collective-permute-start(bf16[448,256]{1,0:T(8,128)(2,1)S(1)} %collective-permute-done.8.refs_8_), channel_id=1, source_target_pairs={{0,4},{8,0},{16,8},{24,16},{28,24},{20,28},{12,20},{4,12},{1,5},{9... | collective-permute-start | bytes 688136 | tf_op jit(solution)/shard_map/ppermute | solution.py:365
  29.1 8.3 %collective-permute-start.11 = (bf16[448,256]{1,0:T(8,128)(2,1)S(1)}, bf16[448,256]{1,0:T(8,128)(2,1)S(1)}, u32[]{:S(2)}, u32[]{:S(2)}) collective-permute-start(bf16[448,256]{1,0:T(8,128)(2,1)S(1)} %collective-permute-done.10.refs_9_), channel_id=1, source_target_pairs={{0,4},{8,0},{16,8},{24,16},{28,24},{20,28},{12,20},{4,12},{1,5},{9... | collective-permute-start | bytes 688136 | tf_op jit(solution)/shard_map/ppermute | solution.py:365
  33.8 3.6 %collective-permute-start.13 = (bf16[128,896]{1,0:T(8,128)(2,1)S(1)}, bf16[128,896]{1,0:T(8,128)(2,1)S(1)}, u32[]{:S(2)}, u32[]{:S(2)}) collective-permute-start(bf16[128,896]{1,0:T(8,128)(2,1)S(1)} %get-tuple-element.52), channel_id=1, source_target_pairs={{0,1},{1,0},{2,3},{3,2},{4,5},{5,4},{6,7},{7,6},{8,9},{9,8},{10,11... | collective-permute-start | bytes 688136 | tf_op jit(solution)/shard_map/ppermute | solution.py:362
  33.9 11.2 %collective-permute-start.3 = (bf16[8,128,512]{2,1,0:T(8,128)(2,1)S(1)}, bf16[8,128,512]{2,1,0:T(8,128)(2,1)S(1)}, u32[]{:S(2)}, u32[]{:S(2)}) collective-permute-start(bf16[8,128,512]{2,1,0:T(8,128)(2,1)S(1)} %shard_map.94.refs_0_), channel_id=1, source_target_pairs={{0,1},{1,0},{2,3},{3,2},{4,5},{5,4},{6,7},{7,6},{8,9},{9,8},{10,11... | collective-permute-start | bytes 3145736 | tf_op jit(solution)/shard_map/ppermute | solution.py:362
  41.5 4.1 %collective-permute-start.14 = (bf16[8,128,512]{2,1,0:T(8,128)(2,1)}, bf16[8,128,512]{2,1,0:T(8,128)(2,1)S(1)}, u32[]{:S(2)}, u32[]{:S(2)}) collective-permute-start(bf16[8,128,512]{2,1,0:T(8,128)(2,1)} %shard_map.95.refs_2_), channel_id=1, source_target_pairs={{0,1},{1,0},{2,3},{3,2},{4,5},{5,4},{6,7},{7,6},{8,9},{9,8},{10,11... | collective-permute-start | bytes 3145736 | tf_op jit(solution)/shard_map/ppermute | solution.py:362
  41.5 18.9 %collective-permute-start.15 = (bf16[448,256]{1,0:T(8,128)(2,1)}, bf16[448,256]{1,0:T(8,128)(2,1)S(1)}, u32[]{:S(2)}, u32[]{:S(2)}) collective-permute-start(bf16[448,256]{1,0:T(8,128)(2,1)} %copy-done.24), channel_id=1, source_target_pairs={{0,8},{8,16},{16,24},{24,28},{28,20},{20,12},{12,4},{4,0},{1,9},{9... | collective-permute-start | bytes 688136 | tf_op jit(solution)/shard_map/ppermute | solution.py:365
  43.1 17.4 %collective-permute-start.16 = (bf16[448,256]{1,0:T(8,128)(2,1)}, bf16[448,256]{1,0:T(8,128)(2,1)S(1)}, u32[]{:S(2)}, u32[]{:S(2)}) collective-permute-start(bf16[448,256]{1,0:T(8,128)(2,1)} %copy-done.26), channel_id=1, source_target_pairs={{0,4},{8,0},{16,8},{24,16},{28,24},{20,28},{12,20},{4,12},{1,5},{9... | collective-permute-start | bytes 688136 | tf_op jit(solution)/shard_map/ppermute | solution.py:365
  43.5 19.6 %collective-permute-start.19 = (bf16[448,256]{1,0:T(8,128)(2,1)}, bf16[448,256]{1,0:T(8,128)(2,1)S(1)}, u32[]{:S(2)}, u32[]{:S(2)}) collective-permute-start(bf16[448,256]{1,0:T(8,128)(2,1)} %copy-done.20), channel_id=1, source_target_pairs={{0,8},{8,16},{16,24},{24,28},{28,20},{20,12},{12,4},{4,0},{1,9},{9... | collective-permute-start | bytes 688136 | tf_op jit(solution)/shard_map/ppermute | solution.py:365
  45.1 18.0 %collective-permute-start.20 = (bf16[448,256]{1,0:T(8,128)(2,1)}, bf16[448,256]{1,0:T(8,128)(2,1)S(1)}, u32[]{:S(2)}, u32[]{:S(2)}) collective-permute-start(bf16[448,256]{1,0:T(8,128)(2,1)} %copy-done.22), channel_id=1, source_target_pairs={{0,4},{8,0},{16,8},{24,16},{28,24},{20,28},{12,20},{4,12},{1,5},{9... | collective-permute-start | bytes 688136 | tf_op jit(solution)/shard_map/ppermute | solution.py:365
  61.0 7.0 %collective-permute-start.17 = (bf16[448,256]{1,0:T(8,128)(2,1)S(1)}, bf16[448,256]{1,0:T(8,128)(2,1)S(1)}, u32[]{:S(2)}, u32[]{:S(2)}) collective-permute-start(bf16[448,256]{1,0:T(8,128)(2,1)S(1)} %get-tuple-element.54), channel_id=1, source_target_pairs={{0,8},{8,16},{16,24},{24,28},{28,20},{20,12},{12,4},{4,0},{1,9},{9... | collective-permute-start | bytes 688136 | tf_op jit(solution)/shard_map/ppermute | solution.py:365
  62.7 6.6 %collective-permute-start.18 = (bf16[448,256]{1,0:T(8,128)(2,1)S(1)}, bf16[448,256]{1,0:T(8,128)(2,1)S(1)}, u32[]{:S(2)}, u32[]{:S(2)}) collective-permute-start(bf16[448,256]{1,0:T(8,128)(2,1)S(1)} %get-tuple-element.55), channel_id=1, source_target_pairs={{0,4},{8,0},{16,8},{24,16},{28,24},{20,28},{12,20},{4,12},{1,5},{9... | collective-permute-start | bytes 688136 | tf_op jit(solution)/shard_map/ppermute | solution.py:365
  69.3 10.6 %copy-start.15 = (bf16[128,896]{1,0:T(8,128)(2,1)S(1)}, bf16[128,896]{1,0:T(8,128)(2,1)}, u32[]{:S(2)}) copy-start(bf16[128,896]{1,0:T(8,128)(2,1)} %copy-done.14) | copy-start | bytes 688132
  69.3 17.3 %copy-start.17 = (bf16[128,896]{1,0:T(8,128)(2,1)S(1)}, bf16[128,896]{1,0:T(8,128)(2,1)}, u32[]{:S(2)}) copy-start(bf16[128,896]{1,0:T(8,128)(2,1)} %copy-done.16) | copy-start | bytes 688132
  69.3 17.3 %copy-start.19 = (bf16[128,896]{1,0:T(8,128)(2,1)S(1)}, bf16[128,896]{1,0:T(8,128)(2,1)}, u32[]{:S(2)}) copy-start(bf16[128,896]{1,0:T(8,128)(2,1)} %copy-done.18) | copy-start | bytes 688132
  71.1 30.8 %collective-permute-start.27 = (bf16[8,2,448,256]{3,2,1,0:T(8,128)(2,1)S(1)}, bf16[8,2,448,256]{3,2,1,0:T(8,128)(2,1)S(1)}, u32[]{:S(2)}, u32[]{:S(2)}) collective-permute-start(bf16[8,2,448,256]{3,2,1,0:T(8,128)(2,1)S(1)} %get-tuple-element.73.w_ref), channel_id=1, source_target_pairs={{0,1},{1,0},{2,3},{3,2},{4,5},{5,4},{6,7},{7,6},{8,9},{9,8},{10,11... | collective-permute-start | bytes 11010056 | tf_op jit(solution)/shard_map/ppermute | solution.py:362
  71.2 8.7 %collective-permute-start.21 = (bf16[512,256]{1,0:T(8,128)(2,1)S(1)}, bf16[512,256]{1,0:T(8,128)(2,1)S(1)}, u32[]{:S(2)}, u32[]{:S(2)}) collective-permute-start(bf16[512,256]{1,0:T(8,128)(2,1)S(1)} %get-tuple-element.59.kv_ref), channel_id=1, source_target_pairs={{0,2},{1,3},{2,0},{3,1},{4,6},{5,7},{6,4},{7,5},{8,10},{9,11},{10,... | collective-permute-start | bytes 786440 | tf_op jit(solution)/shard_map/ppermute | solution.py:362
  84.5 6.7 %collective-permute-start.25 = (bf16[256,256]{1,0:T(8,128)(2,1)S(1)}, bf16[256,256]{1,0:T(8,128)(2,1)S(1)}, u32[]{:S(2)}, u32[]{:S(2)}) collective-permute-start(bf16[256,256]{1,0:T(8,128)(2,1)S(1)} %get-tuple-element.72), channel_id=1, source_target_pairs={{0,2},{1,3},{2,0},{3,1},{4,6},{5,7},{6,4},{7,5},{8,10},{9,11},{10,... | collective-permute-start | bytes 393224 | tf_op jit(solution)/shard_map/ppermute | solution.py:362
  85.1 10.2 %collective-permute-start.24 = (f32[256,256]{1,0:T(8,128)S(1)}, f32[256,256]{1,0:T(8,128)S(1)}, u32[]{:S(2)}, u32[]{:S(2)}) collective-permute-start(f32[256,256]{1,0:T(8,128)S(1)} %get-tuple-element.62.refs_0_), channel_id=1, source_target_pairs={{0,2},{1,3},{2,0},{3,1},{4,6},{5,7},{6,4},{7,5},{8,10},{9,11},{10,... | collective-permute-start | bytes 786440 | tf_op jit(solution)/shard_map/ppermute | solution.py:362
  95.3 5.8 %collective-permute-start.26 = (bf16[512,256]{1,0:T(8,128)(2,1)S(1)}, bf16[512,256]{1,0:T(8,128)(2,1)S(1)}, u32[]{:S(2)}, u32[]{:S(2)}) collective-permute-start(bf16[512,256]{1,0:T(8,128)(2,1)S(1)} %pad_maximum_fusion.g_ref.refs_4_), channel_id=1, source_target_pairs={{0,1},{1,0},{2,3},{3,2},{4,5},{5,4},{6,7},{7,6},{8,9},{9,8},{10,11... | collective-permute-start | bytes 786440 | tf_op jit(solution)/shard_map/ppermute | solution.py:362
  96.6 10.3 %collective-permute-start.29 = (bf16[448,256]{1,0:T(8,128)(2,1)S(1)}, bf16[448,256]{1,0:T(8,128)(2,1)S(1)}, u32[]{:S(2)}, u32[]{:S(2)}) collective-permute-start(bf16[448,256]{1,0:T(8,128)(2,1)S(1)} %get-tuple-element.80), channel_id=1, source_target_pairs={{0,8},{8,16},{16,24},{24,28},{28,20},{20,12},{12,4},{4,0},{1,9},{9... | collective-permute-start | bytes 688136 | tf_op jit(solution)/shard_map/ppermute | solution.py:365
  98.2 38.6 %collective-permute-start.22 = (bf16[2,128,896]{2,1,0:T(8,128)(2,1)S(1)}, bf16[2,128,896]{2,1,0:T(8,128)(2,1)S(1)}, u32[]{:S(2)}, u32[]{:S(2)}) collective-permute-start(bf16[2,128,896]{2,1,0:T(8,128)(2,1)S(1)} %get-tuple-element.64), channel_id=1, source_target_pairs={{0,1},{1,0},{2,3},{3,2},{4,5},{5,4},{6,7},{7,6},{8,9},{9,8},{10,11... | collective-permute-start | bytes 1376264 | tf_op jit(solution)/shard_map/ppermute | solution.py:362
  98.4 40.0 %collective-permute-start.23 = (bf16[2,128,896]{2,1,0:T(8,128)(2,1)S(1)}, bf16[2,128,896]{2,1,0:T(8,128)(2,1)S(1)}, u32[]{:S(2)}, u32[]{:S(2)}) collective-permute-start(bf16[2,128,896]{2,1,0:T(8,128)(2,1)S(1)} %get-tuple-element.66), channel_id=1, source_target_pairs={{0,1},{1,0},{2,3},{3,2},{4,5},{5,4},{6,7},{7,6},{8,9},{9,8},{10,11... | collective-permute-start | bytes 1376264 | tf_op jit(solution)/shard_map/ppermute | solution.py:362
  101.1 8.0 %collective-permute-start.39 = (bf16[448,256]{1,0:T(8,128)(2,1)S(1)}, bf16[448,256]{1,0:T(8,128)(2,1)S(1)}, u32[]{:S(2)}, u32[]{:S(2)}) collective-permute-start(bf16[448,256]{1,0:T(8,128)(2,1)S(1)} %get-tuple-element.91), channel_id=1, source_target_pairs={{0,4},{8,0},{16,8},{24,16},{28,24},{20,28},{12,20},{4,12},{1,5},{9... | collective-permute-start | bytes 688136 | tf_op jit(solution)/shard_map/ppermute | solution.py:365
  104.8 41.5 %collective-permute-start.28 = (bf16[128,3584]{1,0:T(8,128)(2,1)S(1)}, bf16[128,3584]{1,0:T(8,128)(2,1)S(1)}, u32[]{:S(2)}, u32[]{:S(2)}) collective-permute-start(bf16[128,3584]{1,0:T(8,128)(2,1)S(1)} %get-tuple-element.75.refs_5_), channel_id=1, source_target_pairs={{0,2},{1,3},{2,0},{3,1},{4,6},{5,7},{6,4},{7,5},{8,10},{9,11},{10,... | collective-permute-start | bytes 2752520 | tf_op jit(solution)/shard_map/ppermute | solution.py:362
  107.0 7.2 %collective-permute-start.30 = (bf16[448,256]{1,0:T(8,128)(2,1)S(1)}, bf16[448,256]{1,0:T(8,128)(2,1)S(1)}, u32[]{:S(2)}, u32[]{:S(2)}) collective-permute-start(bf16[448,256]{1,0:T(8,128)(2,1)S(1)} %add_convert_fusion.10), channel_id=1, source_target_pairs={{0,8},{8,16},{16,24},{24,28},{28,20},{20,12},{12,4},{4,0},{1,9},{9... | collective-permute-start | bytes 688136 | tf_op jit(solution)/shard_map/ppermute | solution.py:365
  109.1 6.9 %collective-permute-start.33 = (bf16[448,256]{1,0:T(8,128)(2,1)S(1)}, bf16[448,256]{1,0:T(8,128)(2,1)S(1)}, u32[]{:S(2)}, u32[]{:S(2)}) collective-permute-start(bf16[448,256]{1,0:T(8,128)(2,1)S(1)} %convert_element_type.85), channel_id=1, source_target_pairs={{0,4},{8,0},{16,8},{24,16},{28,24},{20,28},{12,20},{4,12},{1,5},{9... | collective-permute-start | bytes 688136 | tf_op jit(solution)/shard_map/ppermute | solution.py:365
  114.2 6.3 %collective-permute-start.36 = (bf16[448,256]{1,0:T(8,128)(2,1)S(1)}, bf16[448,256]{1,0:T(8,128)(2,1)S(1)}, u32[]{:S(2)}, u32[]{:S(2)}) collective-permute-start(bf16[448,256]{1,0:T(8,128)(2,1)S(1)} %convert_element_type.90), channel_id=1, source_target_pairs={{0,8},{8,16},{16,24},{24,28},{28,20},{20,12},{12,4},{4,0},{1,9},{9... | collective-permute-start | bytes 688136 | tf_op jit(solution)/shard_map/ppermute | solution.py:365
  116.0 6.0 %collective-permute-start.40 = (bf16[448,256]{1,0:T(8,128)(2,1)S(1)}, bf16[448,256]{1,0:T(8,128)(2,1)S(1)}, u32[]{:S(2)}, u32[]{:S(2)}) collective-permute-start(bf16[448,256]{1,0:T(8,128)(2,1)S(1)} %add_convert_fusion.3), channel_id=1, source_target_pairs={{0,4},{8,0},{16,8},{24,16},{28,24},{20,28},{12,20},{4,12},{1,5},{9... | collective-permute-start | bytes 688136 | tf_op jit(solution)/shard_map/ppermute | solution.py:365
  120.4 6.4 %collective-permute-start.31 = (bf16[448,256]{1,0:T(8,128)(2,1)S(1)}, bf16[448,256]{1,0:T(8,128)(2,1)S(1)}, u32[]{:S(2)}, u32[]{:S(2)}) collective-permute-start(bf16[448,256]{1,0:T(8,128)(2,1)S(1)} %add_convert_fusion.9), channel_id=1, source_target_pairs={{0,8},{8,16},{16,24},{24,28},{28,20},{20,12},{12,4},{4,0},{1,9},{9... | collective-permute-start | bytes 688136 | tf_op jit(solution)/shard_map/ppermute | solution.py:365
  122.0 6.7 %collective-permute-start.34 = (bf16[448,256]{1,0:T(8,128)(2,1)S(1)}, bf16[448,256]{1,0:T(8,128)(2,1)S(1)}, u32[]{:S(2)}, u32[]{:S(2)}) collective-permute-start(bf16[448,256]{1,0:T(8,128)(2,1)S(1)} %add_convert_fusion.7), channel_id=1, source_target_pairs={{0,4},{8,0},{16,8},{24,16},{28,24},{20,28},{12,20},{4,12},{1,5},{9... | collective-permute-start | bytes 688136 | tf_op jit(solution)/shard_map/ppermute | solution.py:365
  126.8 7.4 %collective-permute-start.37 = (bf16[448,256]{1,0:T(8,128)(2,1)S(1)}, bf16[448,256]{1,0:T(8,128)(2,1)S(1)}, u32[]{:S(2)}, u32[]{:S(2)}) collective-permute-start(bf16[448,256]{1,0:T(8,128)(2,1)S(1)} %add_convert_fusion.5), channel_id=1, source_target_pairs={{0,8},{8,16},{16,24},{24,28},{28,20},{20,12},{12,4},{4,0},{1,9},{9... | collective-permute-start | bytes 688136 | tf_op jit(solution)/shard_map/ppermute | solution.py:365
  128.7 7.5 %collective-permute-start.41 = (bf16[448,256]{1,0:T(8,128)(2,1)S(1)}, bf16[448,256]{1,0:T(8,128)(2,1)S(1)}, u32[]{:S(2)}, u32[]{:S(2)}) collective-permute-start(bf16[448,256]{1,0:T(8,128)(2,1)S(1)} %add_convert_fusion.2), channel_id=1, source_target_pairs={{0,4},{8,0},{16,8},{24,16},{28,24},{20,28},{12,20},{4,12},{1,5},{9... | collective-permute-start | bytes 688136 | tf_op jit(solution)/shard_map/ppermute | solution.py:365
  134.3 6.6 %collective-permute-start.32 = (bf16[448,256]{1,0:T(8,128)(2,1)S(1)}, bf16[448,256]{1,0:T(8,128)(2,1)S(1)}, u32[]{:S(2)}, u32[]{:S(2)}) collective-permute-start(bf16[448,256]{1,0:T(8,128)(2,1)S(1)} %add_convert_fusion.8), channel_id=1, source_target_pairs={{0,8},{8,16},{16,24},{24,28},{28,20},{20,12},{12,4},{4,0},{1,9},{9... | collective-permute-start | bytes 688136 | tf_op jit(solution)/shard_map/ppermute | solution.py:365
  136.2 6.0 %collective-permute-start.35 = (bf16[448,256]{1,0:T(8,128)(2,1)S(1)}, bf16[448,256]{1,0:T(8,128)(2,1)S(1)}, u32[]{:S(2)}, u32[]{:S(2)}) collective-permute-start(bf16[448,256]{1,0:T(8,128)(2,1)S(1)} %add_convert_fusion.6), channel_id=1, source_target_pairs={{0,4},{8,0},{16,8},{24,16},{28,24},{20,28},{12,20},{4,12},{1,5},{9... | collective-permute-start | bytes 688136 | tf_op jit(solution)/shard_map/ppermute | solution.py:365
  136.8 6.1 %collective-permute-start.38 = (bf16[448,256]{1,0:T(8,128)(2,1)S(1)}, bf16[448,256]{1,0:T(8,128)(2,1)S(1)}, u32[]{:S(2)}, u32[]{:S(2)}) collective-permute-start(bf16[448,256]{1,0:T(8,128)(2,1)S(1)} %add_convert_fusion.4), channel_id=1, source_target_pairs={{0,8},{8,16},{16,24},{24,28},{28,20},{20,12},{12,4},{4,0},{1,9},{9... | collective-permute-start | bytes 688136 | tf_op jit(solution)/shard_map/ppermute | solution.py:365
  138.4 6.3 %collective-permute-start.42 = (bf16[448,256]{1,0:T(8,128)(2,1)S(1)}, bf16[448,256]{1,0:T(8,128)(2,1)S(1)}, u32[]{:S(2)}, u32[]{:S(2)}) collective-permute-start(bf16[448,256]{1,0:T(8,128)(2,1)S(1)} %add_convert_fusion.1), channel_id=1, source_target_pairs={{0,4},{8,0},{16,8},{24,16},{28,24},{20,28},{12,20},{4,12},{1,5},{9... | collective-permute-start | bytes 688136 | tf_op jit(solution)/shard_map/ppermute | solution.py:365
  (29 other events, 79.8 us)

commit v11 on v9

--- a/solution.py
+++ b/solution.py
@@ -55,43 +55,38 @@
     return jnp.where(spot < half, 2 * spot, 2 * (size - 1 - spot) + 1)
 
 
-def after(x, *others):
-    return pl.pallas_call(
-        lambda *refs: None,
-        in_specs=[ANYWHERE] + [pl.BlockSpec(memory_space=pltpu.VMEM)] * len(others),
-        out_specs=ANYWHERE,
-        out_shape=shaped(x.shape, x.dtype),
-        input_output_aliases={0: 0},
-        cost_estimate=pl.CostEstimate(flops=0, bytes_accessed=0, transcendentals=0),
-    )(x, *others)
-
-
 def as_column(row):
     return jnp.broadcast_to(row, (128, row.shape[1])).T[:, :1]
 
 
-def blocks_kernel(depth, me_ref, tok_ref, ids_ref, out_ref):
-    count, rows, lanes = out_ref.shape
+def blocks_kernel(depth, me_ref, tok_ref, ids_ref, *out_refs):
+    count, rows, lanes = out_refs[0].shape
     base = lanes - 128
     lane = lax.broadcasted_iota(jnp.int32, (rows, 128), 1) - (depth - base)
     ids = lax.div(ids_ref[...], 2)
     marks = (lax.rem(ids_ref[...], 2), lax.div(ids, DIGIT), lax.rem(ids, DIGIT))
     marks = [as_column(x.astype(F32)) for x in marks]
-    for j in range(count):
-        out_ref[j, :, :depth] = tok_ref[:, j * depth : (j + 1) * depth]
-        last = out_ref[j, :, base:].astype(F32)
-        last = jnp.where(lane >= 0, 0.0, last)
-        for i, mark in enumerate(marks):
-            last = jnp.where(lane == i, mark, last)
-        out_ref[j, :, base:] = last.astype(BF16)
+    for h, out_ref in enumerate(out_refs):
+        here = slice(h * rows, (h + 1) * rows)
+        for j in range(count):
+            out_ref[j, :, :depth] = tok_ref[here, j * depth : (j + 1) * depth]
+            last = out_ref[j, :, base:].astype(F32)
+            last = jnp.where(lane >= 0, 0.0, last)
+            for i, mark in enumerate(marks):
+                last = jnp.where(lane == i, mark[here], last)
+            out_ref[j, :, base:] = last.astype(BF16)
 
 
 def token_blocks(me, tokens, ids, count):
     rows, width = tokens.shape
     depth = width // count
     lanes = -(-(depth + 3) // 128) * 128
-    out = shaped((count, rows, lanes), BF16)
-    return call(functools.partial(blocks_kernel, depth), me, (tokens, ids), out, 2)
+    out = [shaped((count, rows // 2, lanes), BF16)] * 2
+    return call(functools.partial(blocks_kernel, depth), me, (tokens, ids), out, 1)
+
+
+def piece_start(me, i, rows):
+    return pl.multiple_of((me ^ (i // 2)) * (2 * rows) + i % 2 * rows, rows)
 
 
 def read_marks(block, depth):
@@ -99,7 +94,8 @@
     return mark[0], mark[1] * DIGIT + mark[2]
 
 
-def pack_kernel(me_ref, q_ref, up_ref, own_ref, *other_refs):
+def pack_kernel(me_ref, q_ref, up_ref, *refs):
+    own_ref, other_refs = refs[-5], refs[-4:]
     for i in range(4):
         here = pl.ds(pl.multiple_of((me_ref[0] ^ i) * SPAN, SPAN), SPAN)
         for k, ref in enumerate((q_ref, up_ref)):
@@ -109,10 +105,10 @@
                 own_ref[i // 2, k] = ref[:, here]
 
 
-def pack_heads(me, queries, upstream):
+def pack_heads(me, queries, upstream, wait):
     rows = queries.shape[0]
     out = [shaped((2, 2, rows, SPAN), BF16)] + [shaped((rows, SPAN), BF16)] * 4
-    return call(pack_kernel, me, (queries, upstream), out, 2)
+    return call(pack_kernel, me, (queries, upstream, *wait), out, 2)
 
 
 def place_kernel(me_ref, *refs):
@@ -129,7 +125,7 @@
 
 
 def project_kernel(steps, depth, halves, first, last, me_ref, *refs):
-    parts, refs = refs[:4], refs[4:]
+    parts, refs = refs[:8], refs[8:]
     weights, refs = refs[: len(steps) + halves], refs[len(steps) + halves :]
     whole_ref, sems = refs[-2:]
     rows, lanes = parts[0].shape[1:]
@@ -153,21 +149,20 @@
             refs[-3][:, e * PAIR : (e + 1) * PAIR] = sums[e]
     else:
         kv_ref, kind_ref, ids_ref, ids_row_ref = refs[-6:-2]
-        for r in range(4):
-            here = pl.ds(pl.multiple_of((me_ref[0] ^ r) * rows, rows), rows)
-            kind, ids = read_marks(parts[r][0], depth)
-            mine = slice(r * rows, (r + 1) * rows)
+        for i, ref in enumerate(parts):
+            here = pl.ds(piece_start(me_ref[0], i, rows), rows)
+            kind, ids = read_marks(ref[0], depth)
+            mine = slice(i * rows, (i + 1) * rows)
             kv_ref[here, :] = jnp.where(kind == 1.0, sums[1][mine], sums[0][mine]).astype(BF16)
             kind_ref[here, :] = kind
             ids_ref[here, :] = ids
-        ids_row_ref[...] = jnp.broadcast_to(ids_ref[...], (4 * rows, 128)).T[:1]
+        ids_row_ref[...] = jnp.broadcast_to(ids_ref[...], (8 * rows, 128)).T[:1]
     for copy in copies:
         copy.wait()
 
 
 def project(me, steps, parts, weights, before, depth, last=False, halves=False):
-    rows, lanes = parts[0].shape[1:]
-    length = 4 * rows
+    length = 8 * parts[0].shape[1]
     outs = [shaped((length, 2 * PAIR), F32)]
     if last:
         outs = [shaped((length, PAIR), BF16)] + [shaped(x, F32) for x in ((length, 1), (length, 1), (1, length))]
@@ -192,9 +187,10 @@
     refs[-1][...] = downs_ref[1:]
 
 
-def halve(me, ups, downs, wait):
+def halve(me, ups, downs, near, wait):
     out = [shaped((1, *ups.shape[1:]), ups.dtype)] * 2
-    return call(halve_kernel, me, (ups, downs, *wait), out, 1, far=tuple(range(2, 2 + len(wait))))
+    first = 2 + len(near)
+    return call(halve_kernel, me, (ups, downs, *near, *wait), out, 1, far=tuple(range(first, first + len(wait))))
 
 
 def attend_kernel(spot, me_ref, own_ref, q_other, up_other, kv_ref, ids_ref, ids_row_ref, *refs):
@@ -297,11 +293,11 @@
 
 
 def share_kernel(steps, depth, split, me_ref, *refs):
-    parts, g_ref, outs = refs[:4], refs[4], refs[-(2 if split else 1) * len(steps) :]
+    parts, g_ref, outs = refs[:8], refs[8], refs[-(2 if split else 1) * len(steps) :]
     rows, lanes = parts[0].shape[1:]
-    quarter = [g_ref[pl.ds(pl.multiple_of((me_ref[0] ^ r) * rows, rows), rows), :].astype(F32) for r in range(4)]
+    pieces = [g_ref[pl.ds(piece_start(me_ref[0], i, rows), rows), :].astype(F32) for i in range(8)]
     kind = jnp.concatenate([read_marks(ref[0], depth)[0] for ref in parts], axis=0)
-    right = jnp.concatenate(by_expert(kind, jnp.concatenate(quarter, axis=0)), axis=-1)
+    right = jnp.concatenate(by_expert(kind, jnp.concatenate(pieces, axis=0)), axis=-1)
     for i, by in enumerate(steps):
         owner = owner_at(me_ref[1], by)
         left = jnp.concatenate([ref[owner] for ref in parts], axis=0)
@@ -319,14 +315,14 @@
         out = [shaped((1, depth, PAIR), BF16)] * (2 * len(steps))
     else:
         out = [shaped((2, depth, PAIR), F32)] * len(steps)
-    far = tuple(range(5, 5 + len(wait)))
+    far = tuple(range(9, 9 + len(wait)))
     return call(functools.partial(share_kernel, steps, depth, split), me, (*parts, grad, *wait), out, 1 + len(steps), far=far)
 
 
 def in_order(parts, quarters):
     count, rows, lanes = parts[0].shape
-    whole = jnp.stack(parts, axis=1)
-    return jnp.take(whole, quarters, axis=1).reshape(count, 4 * rows, lanes)
+    whole = jnp.stack(parts, axis=1).reshape(count, 4, 2 * rows, lanes)
+    return jnp.take(whole, quarters, axis=1).reshape(count, 8 * rows, lanes)
 
 
 def project_plain(quarters, parts, weights, depth):
@@ -373,16 +369,14 @@
         weight = lax.all_gather(kv_weight, "fsdp", axis=0)
 
     blocks = token_blocks(me, tokens, block_ids * 2 + modality, fsdp)
-    across = swap(blocks, 2)
-    own, *others = pack_heads(me, queries, cotangent)
+    across = [swap(x, 2) for x in blocks]
+    parts = [*blocks, *[swap(x, 1) for x in blocks], *across, *[swap(x, 1) for x in across]]
+    own, *others = pack_heads(me, queries, cotangent, weights[1:3] if near_link else ())
     others = [swap(x, 1) for x in others]
-    if near_link:
-        across = after(across, weights[3], weights[4], *others)
-    parts = [blocks, swap(blocks, 1), across, swap(across, 1)]
 
     if near_link:
         before = project(me, STEPS[:5], parts, weights[:5], (), depth)
-        weights += both_ways(*halve(me, *weights[5:], (before[0],)))
+        weights += both_ways(*halve(me, *weights[5:], others, (before[0],)))
         before = project(me, STEPS[5:7], parts, weights[5:7], before, depth)
         kv, kind, ids, ids_row, weight = project(me, STEPS[7:], parts, weights[7:], before, depth, True, True)
     else:

time: 130 us -> 130 us (level)
  local copies, waits for them, and re-layouts: 15.1 us -> 3.54 us
  waiting for transfers between devices: 55.2 us -> 65.6 us
  starting transfers between devices: 24.7 us -> 27 us
    unnamed x50 -> x8, local copies, waits for them, and re-layouts: 15.1 us -> 3.54 us
    ppermute x15 -> x18, waiting for transfers between devices: 15.3 us -> 22.9 us  [swap(): return lax.ppermute(x, 'seq', [(i, i ^ bit) for i in range(seq)])]
    ppermute x16, waiting for transfers between devices: 39.9 us -> 42.7 us  [turn(): lax.ppermute(x, 'fsdp', [(CYCLE[i], CYCLE[(i + by) % fsdp]) for i in rang...]
    pallas_call x1 -> x0, Pallas kernels: 1.46 us -> none  [after(): pl.pallas_call(lambda *refs: None, in_specs=[ANYWHERE] + [pl.BlockSpec(me...]
    ppermute x15 -> x18, starting transfers between devices: 8.07 us -> 9.26 us  [swap(): return lax.ppermute(x, 'seq', [(i, i ^ bit) for i in range(seq)])]
  transfers between devices with their start and end apart: 31 -> 34, of which waited for: 18 -> 15; matrix products, arithmetic and copies ran while one was open for 1% -> 2% of each run, Pallas kernels for 21% -> 20%
where the time goes in v11:
time: 130 us; the launch traced here: 129 us
  waiting for transfers between devices  65.6 us (50%)
  Pallas kernels  28.8 us (22%)
  starting transfers between devices  27 us (21%)
  other arithmetic  3.56 us (3%)
  local copies, waits for them, and re-layouts  3.54 us (3%)
    ppermute x16, waiting for transfers between devices, turn(): lax.ppermute(x, 'fsdp', [(CYCLE[i], CYCLE[(i + by) % fsdp]) for i in rang...  42.7 us
    pallas_call x13, Pallas kernels, call(): pl.pallas_call(body, in_specs=[pl.BlockSpec(memory_space=pltpu.SMEM)] + [...  28.8 us
    ppermute x18, waiting for transfers between devices, swap(): return lax.ppermute(x, 'seq', [(i, i ^ bit) for i in range(seq)])  22.9 us
    ppermute x16, starting transfers between devices, turn(): lax.ppermute(x, 'fsdp', [(CYCLE[i], CYCLE[(i + by) % fsdp]) for i in rang...  17.7 us
    ppermute x18, starting transfers between devices, swap(): return lax.ppermute(x, 'seq', [(i, i ^ bit) for i in range(seq)])  9.26 us
    unnamed x8, local copies, waits for them, and re-layouts  3.54 us
  transfers between devices with their start and end apart: 34, of which 15 were waited for; matrix products, arithmetic and copies ran while one was open for 2% of the time, Pallas kernels for 20%

profile of v11, /device:TPU:0, one launch (start us, length us, event | category | flops | bytes accessed | tf_op | source)
XLA Modules:
  0.0 129.4 jit_solution(8966544305163113732)
XLA Ops:
  0.6 3.1 %collective-permute-start = (bf16[2,448,256]{2,1,0:T(8,128)(2,1)}, bf16[2,448,256]{2,1,0:T(8,128)(2,1)S(1)}, u32[]{:S(2)}, u32[]{:S(2)}) collective-permute-start(bf16[2,448,256]{2,1,0:T(8,128)(2,1)} %refs_8_.1), channel_id=1, source_target_pairs={{0,8},{8,16},{16,24},{24,28},{28,20},{20,12},{12,4},{4,0},{1,9},{9... | collective-permute-start | bytes 1376264 | tf_op jit(solution)/shard_map/ppermute | solution.py:357
  3.7 0.7 multiply_add_fusion.ids_ref
  4.5 1.2 copy-done
  5.6 0.9 shard_map.94
  6.7 2.0 %collective-permute-start.6 = (bf16[8,64,512]{2,1,0:T(8,128)(2,1)S(1)}, bf16[8,64,512]{2,1,0:T(8,128)(2,1)S(1)}, u32[]{:S(2)}, u32[]{:S(2)}) collective-permute-start(bf16[8,64,512]{2,1,0:T(8,128)(2,1)S(1)} %get-tuple-element.46.refs_0_), channel_id=1, source_target_pairs={{0,2},{1,3},{2,0},{3,1},{4,6},{5,7},{6,4},{7,5},{8,10},{9,11},{10,... | collective-permute-start | bytes 1572872 | tf_op jit(solution)/shard_map/ppermute | solution.py:354
  8.8 5.6 %collective-permute-done.refs_0_.refs_9_ = bf16[2,448,256]{2,1,0:T(8,128)(2,1)S(1)} collective-permute-done((bf16[2,448,256]{2,1,0:T(8,128)(2,1)}, bf16[2,448,256]{2,1,0:T(8,128)(2,1)S(1)}, u32[]{:S(2)}, u32[]{:S(2)}) %collective-permute-start) | collective-permute-done | bytes 458784 | tf_op jit(solution)/shard_map/ppermute | solution.py:357
  14.4 5.4 %collective-permute-done.1.refs_1_.refs_10_ = bf16[2,448,256]{2,1,0:T(8,128)(2,1)S(1)} collective-permute-done((bf16[2,448,256]{2,1,0:T(8,128)(2,1)}, bf16[2,448,256]{2,1,0:T(8,128)(2,1)S(1)}, u32[]{:S(2)}, u32[]{:S(2)}) %collective-permute-start.1) | collective-permute-done | bytes 458784 | tf_op jit(solution)/shard_map/ppermute | solution.py:357
  19.7 1.6 %collective-permute-start.10 = (bf16[2,448,256]{2,1,0:T(8,128)(2,1)S(1)}, bf16[2,448,256]{2,1,0:T(8,128)(2,1)S(1)}, u32[]{:S(2)}, u32[]{:S(2)}) collective-permute-start(bf16[2,448,256]{2,1,0:T(8,128)(2,1)S(1)} %collective-permute-done.refs_0_.refs_9_), channel_id=1, source_target_pairs={{0,8},{8,16},{16,24},{24,28},{28,20},{20,12},{12,4},{4,0},{1,9},{9... | collective-permute-start | bytes 1376264 | tf_op jit(solution)/shard_map/ppermute | solution.py:357
  21.8 10.4 %collective-permute-done.7.refs_5_ = bf16[8,64,512]{2,1,0:T(8,128)(2,1)S(1)} collective-permute-done((bf16[8,64,512]{2,1,0:T(8,128)(2,1)S(1)}, bf16[8,64,512]{2,1,0:T(8,128)(2,1)S(1)}, u32[]{:S(2)}, u32[]{:S(2)}) %collective-permute-start.7) | collective-permute-done | bytes 524320 | tf_op jit(solution)/shard_map/ppermute | solution.py:354
  32.2 1.2 copy-done.1
  33.4 1.2 copy-done.2
  34.5 0.7 shard_map.93
  35.2 0.6 collective-permute-start.2
  35.8 1.7 %collective-permute-start.11 = (bf16[2,448,256]{2,1,0:T(8,128)(2,1)S(1)}, bf16[2,448,256]{2,1,0:T(8,128)(2,1)S(1)}, u32[]{:S(2)}, u32[]{:S(2)}) collective-permute-start(bf16[2,448,256]{2,1,0:T(8,128)(2,1)S(1)} %collective-permute-done.10.refs_11_), channel_id=1, source_target_pairs={{0,8},{8,16},{16,24},{24,28},{28,20},{20,12},{12,4},{4,0},{1,9},{9... | collective-permute-start | bytes 1376264 | tf_op jit(solution)/shard_map/ppermute | solution.py:357
  37.9 0.5 collective-permute-start.14
  38.4 3.5 %shard_map.95 = (f32[512,512]{1,0:T(8,128)S(1)}, bf16[8,2,448,256]{3,2,1,0:T(8,128)(2,1)S(1)}) custom-call(s32[2]{0:T(128)S(1)} %pad_add_fusion.me_ref, bf16[8,64,512]{2,1,0:T(8,128)(2,1)S(1)} %get-tuple-element.46.refs_0_, bf16[8,64,512]{2,1,0:T(8,128)(2,1)S(1)} %get-tuple-element.47.refs_1_, bf16[8,64,512]{2,1,0:T(8,128)(2,1)S(1)} %collective-permute-done.4.refs_2_, ...), custom_call_target="tpu_custom_call" | custom-call | bytes 9000000 | tf_op jit(solution)/shard_map/pallas_call | solution.py:36
  42.0 6.3 %collective-permute-done.11.ups_ref.refs_8_ = bf16[2,448,256]{2,1,0:T(8,128)(2,1)S(1)} collective-permute-done((bf16[2,448,256]{2,1,0:T(8,128)(2,1)S(1)}, bf16[2,448,256]{2,1,0:T(8,128)(2,1)S(1)}, u32[]{:S(2)}, u32[]{:S(2)}) %collective-permute-start.11) | collective-permute-done | bytes 458784 | tf_op jit(solution)/shard_map/ppermute | solution.py:357
  48.3 1.5 %collective-permute-done.13.downs_ref.refs_9_ = bf16[2,448,256]{2,1,0:T(8,128)(2,1)S(1)} collective-permute-done((bf16[2,448,256]{2,1,0:T(8,128)(2,1)S(1)}, bf16[2,448,256]{2,1,0:T(8,128)(2,1)S(1)}, u32[]{:S(2)}, u32[]{:S(2)}) %collective-permute-start.13) | collective-permute-done | bytes 458784 | tf_op jit(solution)/shard_map/ppermute | solution.py:357
  49.8 0.6 shard_map.96
  50.4 1.6 %collective-permute-start.16 = (bf16[1,448,256]{2,1,0:T(8,128)(2,1)S(1)}, bf16[1,448,256]{2,1,0:T(8,128)(2,1)S(1)}, u32[]{:S(2)}, u32[]{:S(2)}) collective-permute-start(bf16[1,448,256]{2,1,0:T(8,128)(2,1)S(1)} %get-tuple-element.51), channel_id=1, source_target_pairs={{0,8},{8,16},{16,24},{24,28},{28,20},{20,12},{12,4},{4,0},{1,9},{9... | collective-permute-start | bytes 688136 | tf_op jit(solution)/shard_map/ppermute | solution.py:357
  52.4 1.8 %shard_map.97 = (f32[512,512]{1,0:T(8,128)S(1)}, bf16[8,2,448,256]{3,2,1,0:T(8,128)(2,1)S(1)}) custom-call(s32[2]{0:T(128)S(1)} %pad_add_fusion.me_ref, bf16[8,64,512]{2,1,0:T(8,128)(2,1)S(1)} %get-tuple-element.46.refs_0_, bf16[8,64,512]{2,1,0:T(8,128)(2,1)S(1)} %get-tuple-element.47.refs_1_, ...), custom_call_target="tpu_custom_call", output_to_operand_aliasing={{1}: (12, {})} | custom-call | bytes 9000000 | tf_op jit(solution)/shard_map/pallas_call | solution.py:36
  54.3 2.6 %collective-permute-done.16.refs_8_ = bf16[1,448,256]{2,1,0:T(8,128)(2,1)S(1)} collective-permute-done((bf16[1,448,256]{2,1,0:T(8,128)(2,1)S(1)}, bf16[1,448,256]{2,1,0:T(8,128)(2,1)S(1)}, u32[]{:S(2)}, u32[]{:S(2)}) %collective-permute-start.16) | collective-permute-done | bytes 229408 | tf_op jit(solution)/shard_map/ppermute | solution.py:357
  56.8 1.3 %collective-permute-done.17.refs_9_ = bf16[1,448,256]{2,1,0:T(8,128)(2,1)S(1)} collective-permute-done((bf16[1,448,256]{2,1,0:T(8,128)(2,1)S(1)}, bf16[1,448,256]{2,1,0:T(8,128)(2,1)S(1)}, u32[]{:S(2)}, u32[]{:S(2)}) %collective-permute-start.17) | collective-permute-done | bytes 229408 | tf_op jit(solution)/shard_map/ppermute | solution.py:357
  58.1 2.0 %shard_map.98 = (bf16[512,256]{1,0:T(8,128)(2,1)S(1)}, f32[512,1]{1,0:T(8,128)S(1)}, f32[512,1]{1,0:T(8,128)S(1)}, f32[1,512]{1,0:T(1,128)S(1)}, bf16[8,2,448,256]{3,2,1,0:T(8,128)(2,1)S(1)}) custom-call(s32[2]{0:T(128)S(1)} %pad_add_fusion.me_ref, bf16[8,64,512]{2,1,0:T(8,128)(2,1)S(1)} %get-tuple-element.46.refs_0_, ...), custom_call_target="tpu_custom_call", output_to_operand_aliasing={{4}: (12, {})} | custom-call | bytes 9000000 | tf_op jit(solution)/shard_map/pallas_call | solution.py:36
  60.2 1.6 %collective-permute-start.18 = (bf16[512,256]{1,0:T(8,128)(2,1)S(1)}, bf16[512,256]{1,0:T(8,128)(2,1)S(1)}, u32[]{:S(2)}, u32[]{:S(2)}) collective-permute-start(bf16[512,256]{1,0:T(8,128)(2,1)S(1)} %get-tuple-element.56.kv_ref), channel_id=1, source_target_pairs={{0,2},{1,3},{2,0},{3,1},{4,6},{5,7},{6,4},{7,5},{8,10},{9,11},{10,... | collective-permute-start | bytes 786440 | tf_op jit(solution)/shard_map/ppermute | solution.py:354
  61.8 7.1 %collective-permute-done.18.kv_ref = bf16[512,256]{1,0:T(8,128)(2,1)S(1)} collective-permute-done((bf16[512,256]{1,0:T(8,128)(2,1)S(1)}, bf16[512,256]{1,0:T(8,128)(2,1)S(1)}, u32[]{:S(2)}, u32[]{:S(2)}) %collective-permute-start.18) | collective-permute-done | bytes 262176 | tf_op jit(solution)/shard_map/ppermute | solution.py:354
  69.0 4.7 %shard_map.99 = (bf16[2,128,896]{2,1,0:T(8,128)(2,1)S(1)}, bf16[2,128,896]{2,1,0:T(8,128)(2,1)S(1)}, f32[256,256]{1,0:T(8,128)S(1)}, bf16[256,256]{1,0:T(8,128)(2,1)S(1)}) custom-call(s32[2]{0:T(128)S(1)} %pad_add_fusion.me_ref, bf16[2,2,128,896]{3,2,1,0:T(8,128)(2,1)S(1)} %get-tuple-element.43.own_ref, ...), custom_call_target="tpu_custom_call" | custom-call | bytes 18000000 | tf_op jit(solution)/shard_map/pallas_call | solution.py:36
  73.7 1.6 %collective-permute-start.22 = (bf16[256,256]{1,0:T(8,128)(2,1)S(1)}, bf16[256,256]{1,0:T(8,128)(2,1)S(1)}, u32[]{:S(2)}, u32[]{:S(2)}) collective-permute-start(bf16[256,256]{1,0:T(8,128)(2,1)S(1)} %get-tuple-element.69), channel_id=1, source_target_pairs={{0,2},{1,3},{2,0},{3,1},{4,6},{5,7},{6,4},{7,5},{8,10},{9,11},{10,... | collective-permute-start | bytes 393224 | tf_op jit(solution)/shard_map/ppermute | solution.py:354
  75.7 4.7 %shard_map.100 = (bf16[2,128,896]{2,1,0:T(8,128)(2,1)S(1)}, bf16[2,128,896]{2,1,0:T(8,128)(2,1)S(1)}, f32[256,256]{1,0:T(8,128)S(1)}, f32[256,256]{1,0:T(8,128)S(1)}) custom-call(s32[2]{0:T(128)S(1)} %pad_add_fusion.me_ref, bf16[2,2,128,896]{3,2,1,0:T(8,128)(2,1)S(1)} %get-tuple-element.43.own_ref, ...), custom_call_target="tpu_custom_call" | custom-call | bytes 18000000 | tf_op jit(solution)/shard_map/pallas_call | solution.py:36
  80.5 3.9 %collective-permute-done.21 = f32[256,256]{1,0:T(8,128)S(1)} collective-permute-done((f32[256,256]{1,0:T(8,128)S(1)}, f32[256,256]{1,0:T(8,128)S(1)}, u32[]{:S(2)}, u32[]{:S(2)}) %collective-permute-start.21) | collective-permute-done | bytes 262176 | tf_op jit(solution)/shard_map/ppermute | solution.py:354
  84.5 1.3 shard_map.105
  86.3 1.6 %collective-permute-start.26 = (bf16[1,448,256]{2,1,0:T(8,128)(2,1)S(1)}, bf16[1,448,256]{2,1,0:T(8,128)(2,1)S(1)}, u32[]{:S(2)}, u32[]{:S(2)}) collective-permute-start(bf16[1,448,256]{2,1,0:T(8,128)(2,1)S(1)} %get-tuple-element.77), channel_id=1, source_target_pairs={{0,8},{8,16},{16,24},{24,28},{28,20},{20,12},{12,4},{4,0},{1,9},{9... | collective-permute-start | bytes 688136 | tf_op jit(solution)/shard_map/ppermute | solution.py:357
  87.9 2.9 %shard_map.102 = (f32[128,3584]{1,0:T(8,128)S(1)}, bf16[128,3584]{1,0:T(8,128)(2,1)S(1)}) custom-call(s32[2]{0:T(128)S(1)} %pad_add_fusion.me_ref, f32[512,1]{1,0:T(8,128)S(1)} %get-tuple-element.66.kind_ref, bf16[512,256]{1,0:T(8,128)(2,1)S(1)} %pad_maximum_fusion.g_ref.refs_8_, bf16[512,256]{1,0:T(8,128)(2,1)S(1)} %collective-permute-done.23.gc_ref, ...), custom_call_target="tpu_custom_call" | custom-call | bytes 21000000 | tf_op jit(solution)/shard_map/pallas_call | solution.py:36
  90.8 1.5 %shard_map.104 = (f32[2,448,256]{2,1,0:T(8,128)S(1)}, f32[2,448,256]{2,1,0:T(8,128)S(1)}) custom-call(s32[2]{0:T(128)S(1)} %pad_add_fusion.me_ref, bf16[8,64,512]{2,1,0:T(8,128)(2,1)S(1)} %get-tuple-element.46.refs_0_, bf16[8,64,512]{2,1,0:T(8,128)(2,1)S(1)} %get-tuple-element.47.refs_1_, bf16[8,64,512]{2,1,0:T(8,128)(2,1)S(1)} %collective-permute-done.4.refs_2_, ...), custom_call_target="tpu_custom_call" | custom-call | bytes 9000000 | tf_op jit(solution)/shard_map/pallas_call | solution.py:36
  92.4 1.5 %collective-permute-done.30 = bf16[1,448,256]{2,1,0:T(8,128)(2,1)S(1)} collective-permute-done((bf16[1,448,256]{2,1,0:T(8,128)(2,1)S(1)}, bf16[1,448,256]{2,1,0:T(8,128)(2,1)S(1)}, u32[]{:S(2)}, u32[]{:S(2)}) %collective-permute-start.30) | collective-permute-done | bytes 229408 | tf_op jit(solution)/shard_map/ppermute | solution.py:357
  94.5 1.6 %collective-permute-start.27 = (bf16[2,448,256]{2,1,0:T(8,128)(2,1)S(1)}, bf16[2,448,256]{2,1,0:T(8,128)(2,1)S(1)}, u32[]{:S(2)}, u32[]{:S(2)}) collective-permute-start(bf16[2,448,256]{2,1,0:T(8,128)(2,1)S(1)} %add_convert_fusion.6), channel_id=1, source_target_pairs={{0,8},{8,16},{16,24},{24,28},{28,20},{20,12},{12,4},{4,0},{1,9},{9... | collective-permute-start | bytes 1376264 | tf_op jit(solution)/shard_map/ppermute | solution.py:357
  96.1 0.5 collective-permute-start.20
  96.7 2.3 %shard_map.103 = (f32[2,448,256]{2,1,0:T(8,128)S(1)}, f32[2,448,256]{2,1,0:T(8,128)S(1)}, f32[2,448,256]{2,1,0:T(8,128)S(1)}, f32[2,448,256]{2,1,0:T(8,128)S(1)}, f32[2,448,256]{2,1,0:T(8,128)S(1)}) custom-call(s32[2]{0:T(128)S(1)} %pad_add_fusion.me_ref, bf16[8,64,512]{2,1,0:T(8,128)(2,1)S(1)} %get-tuple-element.46.refs_0_, ...), custom_call_target="tpu_custom_call" | custom-call | bytes 18000000 | tf_op jit(solution)/shard_map/pallas_call | solution.py:36
  99.0 1.6 %collective-permute-start.25 = (bf16[128,3584]{1,0:T(8,128)(2,1)S(1)}, bf16[128,3584]{1,0:T(8,128)(2,1)S(1)}, u32[]{:S(2)}, u32[]{:S(2)}) collective-permute-start(bf16[128,3584]{1,0:T(8,128)(2,1)S(1)} %get-tuple-element.72.refs_9_), channel_id=1, source_target_pairs={{0,2},{1,3},{2,0},{3,1},{4,6},{5,7},{6,4},{7,5},{8,10},{9,11},{10,... | collective-permute-start | bytes 2752520 | tf_op jit(solution)/shard_map/ppermute | solution.py:354
  100.6 5.5 %collective-permute-done.31 = bf16[2,448,256]{2,1,0:T(8,128)(2,1)S(1)} collective-permute-done((bf16[2,448,256]{2,1,0:T(8,128)(2,1)S(1)}, bf16[2,448,256]{2,1,0:T(8,128)(2,1)S(1)}, u32[]{:S(2)}, u32[]{:S(2)}) %collective-permute-start.31) | collective-permute-done | bytes 458784 | tf_op jit(solution)/shard_map/ppermute | solution.py:357
  106.8 1.6 %collective-permute-start.28 = (bf16[2,448,256]{2,1,0:T(8,128)(2,1)S(1)}, bf16[2,448,256]{2,1,0:T(8,128)(2,1)S(1)}, u32[]{:S(2)}, u32[]{:S(2)}) collective-permute-start(bf16[2,448,256]{2,1,0:T(8,128)(2,1)S(1)} %add_convert_fusion.5), channel_id=1, source_target_pairs={{0,8},{8,16},{16,24},{24,28},{28,20},{20,12},{12,4},{4,0},{1,9},{9... | collective-permute-start | bytes 1376264 | tf_op jit(solution)/shard_map/ppermute | solution.py:357
  108.5 1.9 %shard_map.101 = (bf16[128,3584]{1,0:T(8,128)(2,1)}, bf16[128,3584]{1,0:T(8,128)(2,1)}) custom-call(s32[2]{0:T(128)S(1)} %pad_add_fusion.me_ref, bf16[2,128,896]{2,1,0:T(8,128)(2,1)S(1)} %get-tuple-element.60.refs_0_, bf16[2,128,896]{2,1,0:T(8,128)(2,1)S(1)} %collective-permute-done.19.refs_1_, bf16[2,128,896]{2,1,0:T(8,128)(2,1)S(1)} %get-tuple-element.62.refs_2_, ...), custom_call_target="tpu_custom_call" | custom-call | bytes 9000000 | tf_op jit(solution)/shard_map/pallas_call | solution.py:36
  110.4 7.1 %collective-permute-done.32 = bf16[2,448,256]{2,1,0:T(8,128)(2,1)S(1)} collective-permute-done((bf16[2,448,256]{2,1,0:T(8,128)(2,1)S(1)}, bf16[2,448,256]{2,1,0:T(8,128)(2,1)S(1)}, u32[]{:S(2)}, u32[]{:S(2)}) %collective-permute-start.32) | collective-permute-done | bytes 458784 | tf_op jit(solution)/shard_map/ppermute | solution.py:357
  118.3 1.6 %collective-permute-start.29 = (bf16[2,448,256]{2,1,0:T(8,128)(2,1)S(1)}, bf16[2,448,256]{2,1,0:T(8,128)(2,1)S(1)}, u32[]{:S(2)}, u32[]{:S(2)}) collective-permute-start(bf16[2,448,256]{2,1,0:T(8,128)(2,1)S(1)} %add_convert_fusion.4), channel_id=1, source_target_pairs={{0,8},{8,16},{16,24},{24,28},{28,20},{20,12},{12,4},{4,0},{1,9},{9... | collective-permute-start | bytes 1376264 | tf_op jit(solution)/shard_map/ppermute | solution.py:357
  119.9 1.4 %collective-permute-done.25 = bf16[128,3584]{1,0:T(8,128)(2,1)S(1)} collective-permute-done((bf16[128,3584]{1,0:T(8,128)(2,1)S(1)}, bf16[128,3584]{1,0:T(8,128)(2,1)S(1)}, u32[]{:S(2)}, u32[]{:S(2)}) %collective-permute-start.25) | collective-permute-done | bytes 917536 | tf_op jit(solution)/shard_map/ppermute | solution.py:354
  121.3 1.1 fusion
  122.4 5.6 %collective-permute-done.33 = bf16[2,448,256]{2,1,0:T(8,128)(2,1)S(1)} collective-permute-done((bf16[2,448,256]{2,1,0:T(8,128)(2,1)S(1)}, bf16[2,448,256]{2,1,0:T(8,128)(2,1)S(1)}, u32[]{:S(2)}, u32[]{:S(2)}) %collective-permute-start.33) | collective-permute-done | bytes 458784 | tf_op jit(solution)/shard_map/ppermute | solution.py:357
  128.3 1.0 convert_add_fusion
  (54 shorter events, 5.3 us)
Async XLA Ops:
  0.6 13.7 %collective-permute-start = (bf16[2,448,256]{2,1,0:T(8,128)(2,1)}, bf16[2,448,256]{2,1,0:T(8,128)(2,1)S(1)}, u32[]{:S(2)}, u32[]{:S(2)}) collective-permute-start(bf16[2,448,256]{2,1,0:T(8,128)(2,1)} %refs_8_.1), channel_id=1, source_target_pairs={{0,8},{8,16},{16,24},{24,28},{28,20},{20,12},{12,4},{4,0},{1,9},{9... | collective-permute-start | bytes 1376264 | tf_op jit(solution)/shard_map/ppermute | solution.py:357
  4.5 1.2 copy-start
  5.6 32.8 %copy-start.3 = (bf16[2,448,256]{2,1,0:T(8,128)(2,1)S(1)}, bf16[2,448,256]{2,1,0:T(8,128)(2,1)}, u32[]{:S(2)}) copy-start(bf16[2,448,256]{2,1,0:T(8,128)(2,1)} %refs_8_.1) | copy-start | bytes 1376260
  6.5 14.8 %collective-permute-start.4 = (bf16[8,64,512]{2,1,0:T(8,128)(2,1)S(1)}, bf16[8,64,512]{2,1,0:T(8,128)(2,1)S(1)}, u32[]{:S(2)}, u32[]{:S(2)}) collective-permute-start(bf16[8,64,512]{2,1,0:T(8,128)(2,1)S(1)} %get-tuple-element.46.refs_0_), channel_id=1, source_target_pairs={{0,1},{1,0},{2,3},{3,2},{4,5},{5,4},{6,7},{7,6},{8,9},{9,8},{10,11... | collective-permute-start | bytes 1572872 | tf_op jit(solution)/shard_map/ppermute | solution.py:354
  6.6 13.1 %collective-permute-start.1 = (bf16[2,448,256]{2,1,0:T(8,128)(2,1)}, bf16[2,448,256]{2,1,0:T(8,128)(2,1)S(1)}, u32[]{:S(2)}, u32[]{:S(2)}) collective-permute-start(bf16[2,448,256]{2,1,0:T(8,128)(2,1)} %refs_8_.1), channel_id=1, source_target_pairs={{0,4},{8,0},{16,8},{24,16},{28,24},{20,28},{12,20},{4,12},{1,5},{9... | collective-permute-start | bytes 1376264 | tf_op jit(solution)/shard_map/ppermute | solution.py:357
  6.7 15.1 %collective-permute-start.6 = (bf16[8,64,512]{2,1,0:T(8,128)(2,1)S(1)}, bf16[8,64,512]{2,1,0:T(8,128)(2,1)S(1)}, u32[]{:S(2)}, u32[]{:S(2)}) collective-permute-start(bf16[8,64,512]{2,1,0:T(8,128)(2,1)S(1)} %get-tuple-element.46.refs_0_), channel_id=1, source_target_pairs={{0,2},{1,3},{2,0},{3,1},{4,6},{5,7},{6,4},{7,5},{8,10},{9,11},{10,... | collective-permute-start | bytes 1572872 | tf_op jit(solution)/shard_map/ppermute | solution.py:354
  8.6 23.5 %collective-permute-start.7 = (bf16[8,64,512]{2,1,0:T(8,128)(2,1)S(1)}, bf16[8,64,512]{2,1,0:T(8,128)(2,1)S(1)}, u32[]{:S(2)}, u32[]{:S(2)}) collective-permute-start(bf16[8,64,512]{2,1,0:T(8,128)(2,1)S(1)} %get-tuple-element.47.refs_1_), channel_id=1, source_target_pairs={{0,2},{1,3},{2,0},{3,1},{4,6},{5,7},{6,4},{7,5},{8,10},{9,11},{10,... | collective-permute-start | bytes 1572872 | tf_op jit(solution)/shard_map/ppermute | solution.py:354
  14.4 20.9 %collective-permute-start.5 = (bf16[8,64,512]{2,1,0:T(8,128)(2,1)S(1)}, bf16[8,64,512]{2,1,0:T(8,128)(2,1)S(1)}, u32[]{:S(2)}, u32[]{:S(2)}) collective-permute-start(bf16[8,64,512]{2,1,0:T(8,128)(2,1)S(1)} %get-tuple-element.47.refs_1_), channel_id=1, source_target_pairs={{0,1},{1,0},{2,3},{3,2},{4,5},{5,4},{6,7},{7,6},{8,9},{9,8},{10,11... | collective-permute-start | bytes 1572872 | tf_op jit(solution)/shard_map/ppermute | solution.py:354
  19.7 16.1 %collective-permute-start.10 = (bf16[2,448,256]{2,1,0:T(8,128)(2,1)S(1)}, bf16[2,448,256]{2,1,0:T(8,128)(2,1)S(1)}, u32[]{:S(2)}, u32[]{:S(2)}) collective-permute-start(bf16[2,448,256]{2,1,0:T(8,128)(2,1)S(1)} %collective-permute-done.refs_0_.refs_9_), channel_id=1, source_target_pairs={{0,8},{8,16},{16,24},{24,28},{28,20},{20,12},{12,4},{4,0},{1,9},{9... | collective-permute-start | bytes 1376264 | tf_op jit(solution)/shard_map/ppermute | solution.py:357
  21.3 16.2 %collective-permute-start.12 = (bf16[2,448,256]{2,1,0:T(8,128)(2,1)S(1)}, bf16[2,448,256]{2,1,0:T(8,128)(2,1)S(1)}, u32[]{:S(2)}, u32[]{:S(2)}) collective-permute-start(bf16[2,448,256]{2,1,0:T(8,128)(2,1)S(1)} %collective-permute-done.1.refs_1_.refs_10_), channel_id=1, source_target_pairs={{0,4},{8,0},{16,8},{24,16},{28,24},{20,28},{12,20},{4,12},{1,5},{9... | collective-permute-start | bytes 1376264 | tf_op jit(solution)/shard_map/ppermute | solution.py:357
  21.8 16.1 %collective-permute-start.8 = (bf16[8,64,512]{2,1,0:T(8,128)(2,1)S(1)}, bf16[8,64,512]{2,1,0:T(8,128)(2,1)S(1)}, u32[]{:S(2)}, u32[]{:S(2)}) collective-permute-start(bf16[8,64,512]{2,1,0:T(8,128)(2,1)S(1)} %collective-permute-done.6.refs_4_), channel_id=1, source_target_pairs={{0,1},{1,0},{2,3},{3,2},{4,5},{5,4},{6,7},{7,6},{8,9},{9,8},{10,11... | collective-permute-start | bytes 1572872 | tf_op jit(solution)/shard_map/ppermute | solution.py:354
  32.2 6.2 %collective-permute-start.9 = (bf16[8,64,512]{2,1,0:T(8,128)(2,1)S(1)}, bf16[8,64,512]{2,1,0:T(8,128)(2,1)S(1)}, u32[]{:S(2)}, u32[]{:S(2)}) collective-permute-start(bf16[8,64,512]{2,1,0:T(8,128)(2,1)S(1)} %collective-permute-done.7.refs_5_), channel_id=1, source_target_pairs={{0,1},{1,0},{2,3},{3,2},{4,5},{5,4},{6,7},{7,6},{8,9},{9,8},{10,11... | collective-permute-start | bytes 1572872 | tf_op jit(solution)/shard_map/ppermute | solution.py:354
  32.2 1.2 copy-start.1
  33.4 1.2 copy-start.2
  35.2 2.6 %collective-permute-start.2 = (bf16[128,896]{1,0:T(8,128)(2,1)S(1)}, bf16[128,896]{1,0:T(8,128)(2,1)S(1)}, u32[]{:S(2)}, u32[]{:S(2)}) collective-permute-start(bf16[128,896]{1,0:T(8,128)(2,1)S(1)} %get-tuple-element.44), channel_id=1, source_target_pairs={{0,1},{1,0},{2,3},{3,2},{4,5},{5,4},{6,7},{7,6},{8,9},{9,8},{10,11... | collective-permute-start | bytes 688136 | tf_op jit(solution)/shard_map/ppermute | solution.py:354
  35.8 12.5 %collective-permute-start.11 = (bf16[2,448,256]{2,1,0:T(8,128)(2,1)S(1)}, bf16[2,448,256]{2,1,0:T(8,128)(2,1)S(1)}, u32[]{:S(2)}, u32[]{:S(2)}) collective-permute-start(bf16[2,448,256]{2,1,0:T(8,128)(2,1)S(1)} %collective-permute-done.10.refs_11_), channel_id=1, source_target_pairs={{0,8},{8,16},{16,24},{24,28},{28,20},{20,12},{12,4},{4,0},{1,9},{9... | collective-permute-start | bytes 1376264 | tf_op jit(solution)/shard_map/ppermute | solution.py:357
  37.6 12.2 %collective-permute-start.13 = (bf16[2,448,256]{2,1,0:T(8,128)(2,1)S(1)}, bf16[2,448,256]{2,1,0:T(8,128)(2,1)S(1)}, u32[]{:S(2)}, u32[]{:S(2)}) collective-permute-start(bf16[2,448,256]{2,1,0:T(8,128)(2,1)S(1)} %collective-permute-done.12.refs_12_), channel_id=1, source_target_pairs={{0,4},{8,0},{16,8},{24,16},{28,24},{20,28},{12,20},{4,12},{1,5},{9... | collective-permute-start | bytes 1376264 | tf_op jit(solution)/shard_map/ppermute | solution.py:357
  37.8 4.1 %collective-permute-start.3 = (bf16[128,896]{1,0:T(8,128)(2,1)S(1)}, bf16[128,896]{1,0:T(8,128)(2,1)S(1)}, u32[]{:S(2)}, u32[]{:S(2)}) collective-permute-start(bf16[128,896]{1,0:T(8,128)(2,1)S(1)} %get-tuple-element.45), channel_id=1, source_target_pairs={{0,1},{1,0},{2,3},{3,2},{4,5},{5,4},{6,7},{7,6},{8,9},{9,8},{10,11... | collective-permute-start | bytes 688136 | tf_op jit(solution)/shard_map/ppermute | solution.py:354
  37.9 4.1 %collective-permute-start.14 = (bf16[128,896]{1,0:T(8,128)(2,1)S(1)}, bf16[128,896]{1,0:T(8,128)(2,1)S(1)}, u32[]{:S(2)}, u32[]{:S(2)}) collective-permute-start(bf16[128,896]{1,0:T(8,128)(2,1)S(1)} %get-tuple-element.48), channel_id=1, source_target_pairs={{0,1},{1,0},{2,3},{3,2},{4,5},{5,4},{6,7},{7,6},{8,9},{9,8},{10,11... | collective-permute-start | bytes 688136 | tf_op jit(solution)/shard_map/ppermute | solution.py:354
  38.4 3.6 %collective-permute-start.15 = (bf16[128,896]{1,0:T(8,128)(2,1)S(1)}, bf16[128,896]{1,0:T(8,128)(2,1)S(1)}, u32[]{:S(2)}, u32[]{:S(2)}) collective-permute-start(bf16[128,896]{1,0:T(8,128)(2,1)S(1)} %get-tuple-element.49), channel_id=1, source_target_pairs={{0,1},{1,0},{2,3},{3,2},{4,5},{5,4},{6,7},{7,6},{8,9},{9,8},{10,11... | collective-permute-start | bytes 688136 | tf_op jit(solution)/shard_map/ppermute | solution.py:354
  50.4 6.5 %collective-permute-start.16 = (bf16[1,448,256]{2,1,0:T(8,128)(2,1)S(1)}, bf16[1,448,256]{2,1,0:T(8,128)(2,1)S(1)}, u32[]{:S(2)}, u32[]{:S(2)}) collective-permute-start(bf16[1,448,256]{2,1,0:T(8,128)(2,1)S(1)} %get-tuple-element.51), channel_id=1, source_target_pairs={{0,8},{8,16},{16,24},{24,28},{28,20},{20,12},{12,4},{4,0},{1,9},{9... | collective-permute-start | bytes 688136 | tf_op jit(solution)/shard_map/ppermute | solution.py:357
  52.0 6.1 %collective-permute-start.17 = (bf16[1,448,256]{2,1,0:T(8,128)(2,1)S(1)}, bf16[1,448,256]{2,1,0:T(8,128)(2,1)S(1)}, u32[]{:S(2)}, u32[]{:S(2)}) collective-permute-start(bf16[1,448,256]{2,1,0:T(8,128)(2,1)S(1)} %get-tuple-element.52), channel_id=1, source_target_pairs={{0,4},{8,0},{16,8},{24,16},{28,24},{20,28},{12,20},{4,12},{1,5},{9... | collective-permute-start | bytes 688136 | tf_op jit(solution)/shard_map/ppermute | solution.py:357
  60.2 27.7 %collective-permute-start.24 = (bf16[8,2,448,256]{3,2,1,0:T(8,128)(2,1)S(1)}, bf16[8,2,448,256]{3,2,1,0:T(8,128)(2,1)S(1)}, u32[]{:S(2)}, u32[]{:S(2)}) collective-permute-start(bf16[8,2,448,256]{3,2,1,0:T(8,128)(2,1)S(1)} %get-tuple-element.70.w_ref), channel_id=1, source_target_pairs={{0,1},{1,0},{2,3},{3,2},{4,5},{5,4},{6,7},{7,6},{8,9},{9,8},{10,11... | collective-permute-start | bytes 11010056 | tf_op jit(solution)/shard_map/ppermute | solution.py:354
  60.2 8.7 %collective-permute-start.18 = (bf16[512,256]{1,0:T(8,128)(2,1)S(1)}, bf16[512,256]{1,0:T(8,128)(2,1)S(1)}, u32[]{:S(2)}, u32[]{:S(2)}) collective-permute-start(bf16[512,256]{1,0:T(8,128)(2,1)S(1)} %get-tuple-element.56.kv_ref), channel_id=1, source_target_pairs={{0,2},{1,3},{2,0},{3,1},{4,6},{5,7},{6,4},{7,5},{8,10},{9,11},{10,... | collective-permute-start | bytes 786440 | tf_op jit(solution)/shard_map/ppermute | solution.py:354
  73.7 6.8 %collective-permute-start.22 = (bf16[256,256]{1,0:T(8,128)(2,1)S(1)}, bf16[256,256]{1,0:T(8,128)(2,1)S(1)}, u32[]{:S(2)}, u32[]{:S(2)}) collective-permute-start(bf16[256,256]{1,0:T(8,128)(2,1)S(1)} %get-tuple-element.69), channel_id=1, source_target_pairs={{0,2},{1,3},{2,0},{3,1},{4,6},{5,7},{6,4},{7,5},{8,10},{9,11},{10,... | collective-permute-start | bytes 393224 | tf_op jit(solution)/shard_map/ppermute | solution.py:354
  75.2 9.2 %collective-permute-start.21 = (f32[256,256]{1,0:T(8,128)S(1)}, f32[256,256]{1,0:T(8,128)S(1)}, u32[]{:S(2)}, u32[]{:S(2)}) collective-permute-start(f32[256,256]{1,0:T(8,128)S(1)} %get-tuple-element.59.refs_0_), channel_id=1, source_target_pairs={{0,2},{1,3},{2,0},{3,1},{4,6},{5,7},{6,4},{7,5},{8,10},{9,11},{10,... | collective-permute-start | bytes 786440 | tf_op jit(solution)/shard_map/ppermute | solution.py:354
  84.5 3.4 %collective-permute-start.23 = (bf16[512,256]{1,0:T(8,128)(2,1)S(1)}, bf16[512,256]{1,0:T(8,128)(2,1)S(1)}, u32[]{:S(2)}, u32[]{:S(2)}) collective-permute-start(bf16[512,256]{1,0:T(8,128)(2,1)S(1)} %pad_maximum_fusion.g_ref.refs_8_), channel_id=1, source_target_pairs={{0,1},{1,0},{2,3},{3,2},{4,5},{5,4},{6,7},{7,6},{8,9},{9,8},{10,11... | collective-permute-start | bytes 786440 | tf_op jit(solution)/shard_map/ppermute | solution.py:354
  85.8 8.0 %collective-permute-start.30 = (bf16[1,448,256]{2,1,0:T(8,128)(2,1)S(1)}, bf16[1,448,256]{2,1,0:T(8,128)(2,1)S(1)}, u32[]{:S(2)}, u32[]{:S(2)}) collective-permute-start(bf16[1,448,256]{2,1,0:T(8,128)(2,1)S(1)} %get-tuple-element.81), channel_id=1, source_target_pairs={{0,4},{8,0},{16,8},{24,16},{28,24},{20,28},{12,20},{4,12},{1,5},{9... | collective-permute-start | bytes 688136 | tf_op jit(solution)/shard_map/ppermute | solution.py:357
  86.3 8.1 %collective-permute-start.26 = (bf16[1,448,256]{2,1,0:T(8,128)(2,1)S(1)}, bf16[1,448,256]{2,1,0:T(8,128)(2,1)S(1)}, u32[]{:S(2)}, u32[]{:S(2)}) collective-permute-start(bf16[1,448,256]{2,1,0:T(8,128)(2,1)S(1)} %get-tuple-element.77), channel_id=1, source_target_pairs={{0,8},{8,16},{16,24},{24,28},{28,20},{20,12},{12,4},{4,0},{1,9},{9... | collective-permute-start | bytes 688136 | tf_op jit(solution)/shard_map/ppermute | solution.py:357
  93.9 12.2 %collective-permute-start.31 = (bf16[2,448,256]{2,1,0:T(8,128)(2,1)S(1)}, bf16[2,448,256]{2,1,0:T(8,128)(2,1)S(1)}, u32[]{:S(2)}, u32[]{:S(2)}) collective-permute-start(bf16[2,448,256]{2,1,0:T(8,128)(2,1)S(1)} %add_convert_fusion.3), channel_id=1, source_target_pairs={{0,4},{8,0},{16,8},{24,16},{28,24},{20,28},{12,20},{4,12},{1,5},{9... | collective-permute-start | bytes 1376264 | tf_op jit(solution)/shard_map/ppermute | solution.py:357
  94.5 12.2 %collective-permute-start.27 = (bf16[2,448,256]{2,1,0:T(8,128)(2,1)S(1)}, bf16[2,448,256]{2,1,0:T(8,128)(2,1)S(1)}, u32[]{:S(2)}, u32[]{:S(2)}) collective-permute-start(bf16[2,448,256]{2,1,0:T(8,128)(2,1)S(1)} %add_convert_fusion.6), channel_id=1, source_target_pairs={{0,8},{8,16},{16,24},{24,28},{28,20},{20,12},{12,4},{4,0},{1,9},{9... | collective-permute-start | bytes 1376264 | tf_op jit(solution)/shard_map/ppermute | solution.py:357
  96.1 12.3 %collective-permute-start.19 = (bf16[2,128,896]{2,1,0:T(8,128)(2,1)S(1)}, bf16[2,128,896]{2,1,0:T(8,128)(2,1)S(1)}, u32[]{:S(2)}, u32[]{:S(2)}) collective-permute-start(bf16[2,128,896]{2,1,0:T(8,128)(2,1)S(1)} %get-tuple-element.61), channel_id=1, source_target_pairs={{0,1},{1,0},{2,3},{3,2},{4,5},{5,4},{6,7},{7,6},{8,9},{9,8},{10,11... | collective-permute-start | bytes 1376264 | tf_op jit(solution)/shard_map/ppermute | solution.py:354
  96.1 12.3 %collective-permute-start.20 = (bf16[2,128,896]{2,1,0:T(8,128)(2,1)S(1)}, bf16[2,128,896]{2,1,0:T(8,128)(2,1)S(1)}, u32[]{:S(2)}, u32[]{:S(2)}) collective-permute-start(bf16[2,128,896]{2,1,0:T(8,128)(2,1)S(1)} %get-tuple-element.63), channel_id=1, source_target_pairs={{0,1},{1,0},{2,3},{3,2},{4,5},{5,4},{6,7},{7,6},{8,9},{9,8},{10,11... | collective-permute-start | bytes 1376264 | tf_op jit(solution)/shard_map/ppermute | solution.py:354
  99.0 22.3 %collective-permute-start.25 = (bf16[128,3584]{1,0:T(8,128)(2,1)S(1)}, bf16[128,3584]{1,0:T(8,128)(2,1)S(1)}, u32[]{:S(2)}, u32[]{:S(2)}) collective-permute-start(bf16[128,3584]{1,0:T(8,128)(2,1)S(1)} %get-tuple-element.72.refs_9_), channel_id=1, source_target_pairs={{0,2},{1,3},{2,0},{3,1},{4,6},{5,7},{6,4},{7,5},{8,10},{9,11},{10,... | collective-permute-start | bytes 2752520 | tf_op jit(solution)/shard_map/ppermute | solution.py:354
  106.2 11.3 %collective-permute-start.32 = (bf16[2,448,256]{2,1,0:T(8,128)(2,1)S(1)}, bf16[2,448,256]{2,1,0:T(8,128)(2,1)S(1)}, u32[]{:S(2)}, u32[]{:S(2)}) collective-permute-start(bf16[2,448,256]{2,1,0:T(8,128)(2,1)S(1)} %add_convert_fusion.2), channel_id=1, source_target_pairs={{0,4},{8,0},{16,8},{24,16},{28,24},{20,28},{12,20},{4,12},{1,5},{9... | collective-permute-start | bytes 1376264 | tf_op jit(solution)/shard_map/ppermute | solution.py:357
  106.8 11.3 %collective-permute-start.28 = (bf16[2,448,256]{2,1,0:T(8,128)(2,1)S(1)}, bf16[2,448,256]{2,1,0:T(8,128)(2,1)S(1)}, u32[]{:S(2)}, u32[]{:S(2)}) collective-permute-start(bf16[2,448,256]{2,1,0:T(8,128)(2,1)S(1)} %add_convert_fusion.5), channel_id=1, source_target_pairs={{0,8},{8,16},{16,24},{24,28},{28,20},{20,12},{12,4},{4,0},{1,9},{9... | collective-permute-start | bytes 1376264 | tf_op jit(solution)/shard_map/ppermute | solution.py:357
  117.6 10.4 %collective-permute-start.33 = (bf16[2,448,256]{2,1,0:T(8,128)(2,1)S(1)}, bf16[2,448,256]{2,1,0:T(8,128)(2,1)S(1)}, u32[]{:S(2)}, u32[]{:S(2)}) collective-permute-start(bf16[2,448,256]{2,1,0:T(8,128)(2,1)S(1)} %add_convert_fusion.1), channel_id=1, source_target_pairs={{0,4},{8,0},{16,8},{24,16},{28,24},{20,28},{12,20},{4,12},{1,5},{9... | collective-permute-start | bytes 1376264 | tf_op jit(solution)/shard_map/ppermute | solution.py:357
  118.3 10.1 %collective-permute-start.29 = (bf16[2,448,256]{2,1,0:T(8,128)(2,1)S(1)}, bf16[2,448,256]{2,1,0:T(8,128)(2,1)S(1)}, u32[]{:S(2)}, u32[]{:S(2)}) collective-permute-start(bf16[2,448,256]{2,1,0:T(8,128)(2,1)S(1)} %add_convert_fusion.4), channel_id=1, source_target_pairs={{0,8},{8,16},{16,24},{24,28},{28,20},{20,12},{12,4},{4,0},{1,9},{9... | collective-permute-start | bytes 1376264 | tf_op jit(solution)/shard_map/ppermute | solution.py:357

commit v12 on v11

--- a/solution.py
+++ b/solution.py
@@ -95,20 +95,20 @@
 
 
 def pack_kernel(me_ref, q_ref, up_ref, *refs):
-    own_ref, other_refs = refs[-5], refs[-4:]
+    own_ref, other_refs = refs[-3], refs[-2:]
     for i in range(4):
         here = pl.ds(pl.multiple_of((me_ref[0] ^ i) * SPAN, SPAN), SPAN)
         for k, ref in enumerate((q_ref, up_ref)):
             if i % 2:
-                other_refs[i // 2 * 2 + k][...] = ref[:, here]
+                other_refs[i // 2][k] = ref[:, here]
             else:
                 own_ref[i // 2, k] = ref[:, here]
 
 
-def pack_heads(me, queries, upstream, wait):
+def pack_heads(me, queries, upstream):
     rows = queries.shape[0]
-    out = [shaped((2, 2, rows, SPAN), BF16)] + [shaped((rows, SPAN), BF16)] * 4
-    return call(pack_kernel, me, (queries, upstream, *wait), out, 2)
+    out = [shaped((2, 2, rows, SPAN), BF16)] + [shaped((2, rows, SPAN), BF16)] * 2
+    return call(pack_kernel, me, (queries, upstream), out, 2)
 
 
 def place_kernel(me_ref, *refs):
@@ -174,7 +174,7 @@
         me,
         operands,
         outs,
-        3,
+        1,
         scratch=[pltpu.SemaphoreType.DMA((len(weights),))],
         far=(count - 1,) if before else (),
         far_out=(len(outs) - 1,),
@@ -182,20 +182,29 @@
     )
 
 
+def hold_kernel(count, me_ref, *refs):
+    for i in range(count):
+        refs[i - count][...] = refs[i][...]
+
+
+def hold(me, arrays, others):
+    out = [shaped(x.shape, x.dtype) for x in arrays]
+    return call(functools.partial(hold_kernel, len(arrays)), me, (*arrays, *others), out, 1)
+
+
 def halve_kernel(me_ref, ups_ref, downs_ref, *refs):
     refs[-2][...] = ups_ref[:1]
     refs[-1][...] = downs_ref[1:]
 
 
-def halve(me, ups, downs, near, wait):
+def halve(me, ups, downs, wait):
     out = [shaped((1, *ups.shape[1:]), ups.dtype)] * 2
-    first = 2 + len(near)
-    return call(halve_kernel, me, (ups, downs, *near, *wait), out, 1, far=tuple(range(first, first + len(wait))))
-
-
-def attend_kernel(spot, me_ref, own_ref, q_other, up_other, kv_ref, ids_ref, ids_row_ref, *refs):
+    return call(halve_kernel, me, (ups, downs, *wait), out, 1, far=tuple(range(2, 2 + len(wait))))
+
+
+def attend_kernel(spot, me_ref, own_ref, sibling_ref, kv_ref, ids_ref, ids_row_ref, *refs):
     mine_ref, other_ref, early_ref, late_ref, bias, scores_all, dp_all, pbs, his, los = refs[-10:]
-    rows = q_other.shape[0]
+    rows = own_ref.shape[2]
     heads = [slice(h * HEAD_DIM, (h + 1) * HEAD_DIM) for h in range(GROUP)]
     for i in range(2):
         here = pl.ds(pl.multiple_of((me_ref[0] ^ i) * rows, rows), rows)
@@ -203,8 +212,8 @@
     keys = kv_ref[:, :HEAD_DIM]
     values = kv_ref[:, HEAD_DIM:]
     q, up = [
-        jnp.concatenate([own_ref[spot, i, :, cols] for cols in heads] + [ref[:, cols] for cols in heads], axis=0)
-        for i, ref in enumerate((q_other, up_other))
+        jnp.concatenate([own_ref[spot, i, :, c] for c in heads] + [sibling_ref[i, :, c] for c in heads], axis=0)
+        for i in range(2)
     ]
     scores_all[...] = contract(q, keys, 1, 1)
     dp_all[...] = contract(up, values, 1, 1).astype(BF16)
@@ -236,7 +245,7 @@
         late_ref[:, cols] = x[half:].astype(late_ref.dtype)
 
 
-def attend(spot, me, own, others, kv, ids, ids_row, late, wait=()):
+def attend(spot, me, own, other, kv, ids, ids_row, late, wait=()):
     rows = own.shape[2]
     length = kv.shape[0]
     stacked = (2 * GROUP * rows, length)
@@ -244,11 +253,11 @@
     return call(
         functools.partial(attend_kernel, spot),
         me,
-        (own, *others, kv, ids, ids_row, *wait),
+        (own, other, kv, ids, ids_row, *wait),
         [side, side, shaped((length // 2, PAIR), F32), shaped((length // 2, PAIR), late)],
         6,
         scratch=[pltpu.VMEM((2 * rows, length), F32), pltpu.VMEM(stacked, F32)] + [pltpu.VMEM(stacked, BF16)] * 4,
-        far=tuple(range(6, 6 + len(wait))),
+        far=tuple(range(5, 5 + len(wait))),
     )
 
 
@@ -370,20 +379,21 @@
 
     blocks = token_blocks(me, tokens, block_ids * 2 + modality, fsdp)
     across = [swap(x, 2) for x in blocks]
-    parts = [*blocks, *[swap(x, 1) for x in blocks], *across, *[swap(x, 1) for x in across]]
-    own, *others = pack_heads(me, queries, cotangent, weights[1:3] if near_link else ())
+    own, *others = pack_heads(me, queries, cotangent)
     others = [swap(x, 1) for x in others]
+    here = hold(me, blocks, (*weights[1:3], *others)) if near_link else blocks
+    parts = [*here, *[swap(x, 1) for x in here], *across, *[swap(x, 1) for x in across]]
 
     if near_link:
         before = project(me, STEPS[:5], parts, weights[:5], (), depth)
-        weights += both_ways(*halve(me, *weights[5:], others, (before[0],)))
+        weights += both_ways(*halve(me, *weights[5:], (before[0],)))
         before = project(me, STEPS[5:7], parts, weights[5:7], before, depth)
         kv, kind, ids, ids_row, weight = project(me, STEPS[7:], parts, weights[7:], before, depth, True, True)
     else:
         kv, kind, ids, ids_row = project_plain(quarters, parts, weight, depth)
     kv_far = swap(kv, 2)
-    far_own, far_other, early, late = attend(1, me, own, others[2:], kv_far, ids, ids_row, BF16)
-    near_own, near_other, *near = attend(0, me, own, others[:2], kv, ids, ids_row, F32, (early,))
+    far_own, far_other, early, late = attend(1, me, own, others[1], kv_far, ids, ids_row, BF16)
+    near_own, near_other, *near = attend(0, me, own, others[0], kv, ids, ids_row, F32, (early,))
     grad_kv = jnp.concatenate([near[0] + swap(early, 2), near[1] + swap(late, 2).astype(F32)]).astype(BF16)
     attended, grad_queries = place_heads(me, (near_own, swap(near_other, 1), far_own, swap(far_other, 1)))
 

time: 130 us -> 130 us (level)
    ppermute x18 -> x16, waiting for transfers between devices: 22.9 us -> 27.2 us  [swap(): return lax.ppermute(x, 'seq', [(i, i ^ bit) for i in range(seq)])]
    ppermute x16, waiting for transfers between devices: 42.7 us -> 38.6 us  [turn(): lax.ppermute(x, 'fsdp', [(CYCLE[i], CYCLE[(i + by) % fsdp]) for i in rang...]
    pallas_call x13 -> x14, Pallas kernels: 28.8 us -> 29.4 us  [call(): pl.pallas_call(body, in_specs=[pl.BlockSpec(memory_space=pltpu.SMEM)] + [...]
    ppermute x18 -> x16, starting transfers between devices: 9.26 us -> 9.28 us  [swap(): return lax.ppermute(x, 'seq', [(i, i ^ bit) for i in range(seq)])]
  transfers between devices with their start and end apart: 34 -> 32, of which waited for: 15 -> 16; matrix products, arithmetic and copies ran while one was open for 2% -> 2% of each run, Pallas kernels for 20% -> 20%
where the time goes in v12:
time: 130 us
  waiting for transfers between devices  65.8 us (51%)
  Pallas kernels  29.4 us (23%)
  starting transfers between devices  26.6 us (20%)
  other arithmetic  3.55 us (3%)
  local copies, waits for them, and re-layouts  3.54 us (3%)
    ppermute x16, waiting for transfers between devices, turn(): lax.ppermute(x, 'fsdp', [(CYCLE[i], CYCLE[(i + by) % fsdp]) for i in rang...  38.6 us
    pallas_call x14, Pallas kernels, call(): pl.pallas_call(body, in_specs=[pl.BlockSpec(memory_space=pltpu.SMEM)] + [...  29.4 us
    ppermute x16, waiting for transfers between devices, swap(): return lax.ppermute(x, 'seq', [(i, i ^ bit) for i in range(seq)])  27.2 us
    ppermute x16, starting transfers between devices, turn(): lax.ppermute(x, 'fsdp', [(CYCLE[i], CYCLE[(i + by) % fsdp]) for i in rang...  17.3 us
    ppermute x16, starting transfers between devices, swap(): return lax.ppermute(x, 'seq', [(i, i ^ bit) for i in range(seq)])  9.28 us
    unnamed x8, local copies, waits for them, and re-layouts  3.54 us
  transfers between devices with their start and end apart: 32, of which 16 were waited for; matrix products, arithmetic and copies ran while one was open for 2% of the time, Pallas kernels for 20%

profile of v12, /device:TPU:0, one launch (start us, length us, event | category | flops | bytes accessed | tf_op | source)
XLA Modules:
  0.0 129.7 jit_solution(11223398019641935541)
XLA Ops:
  0.7 1.2 copy-done
  1.9 1.2 copy-done.1
  3.1 0.7 shard_map.93
  3.8 0.5 collective-permute-start
  4.3 2.6 %collective-permute-start.1 = (bf16[2,448,256]{2,1,0:T(8,128)(2,1)}, bf16[2,448,256]{2,1,0:T(8,128)(2,1)S(1)}, u32[]{:S(2)}, u32[]{:S(2)}) collective-permute-start(bf16[2,448,256]{2,1,0:T(8,128)(2,1)} %refs_8_.1), channel_id=1, source_target_pairs={{0,8},{8,16},{16,24},{24,28},{28,20},{20,12},{12,4},{4,0},{1,9},{9... | collective-permute-start | bytes 1376264 | tf_op jit(solution)/shard_map/ppermute | solution.py:366
  7.1 0.7 multiply_add_fusion.ids_ref
  7.8 1.2 copy-done.2
  8.9 0.9 shard_map.94
  9.8 1.9 %collective-permute-start.6 = (bf16[8,64,512]{2,1,0:T(8,128)(2,1)S(1)}, bf16[8,64,512]{2,1,0:T(8,128)(2,1)S(1)}, u32[]{:S(2)}, u32[]{:S(2)}) collective-permute-start(bf16[8,64,512]{2,1,0:T(8,128)(2,1)S(1)} %get-tuple-element.45.refs_0_), channel_id=1, source_target_pairs={{0,2},{1,3},{2,0},{3,1},{4,6},{5,7},{6,4},{7,5},{8,10},{9,11},{10,... | collective-permute-start | bytes 1572872 | tf_op jit(solution)/shard_map/ppermute | solution.py:363
  11.9 6.2 %collective-permute-done.1.refs_2_.refs_9_ = bf16[2,448,256]{2,1,0:T(8,128)(2,1)S(1)} collective-permute-done((bf16[2,448,256]{2,1,0:T(8,128)(2,1)}, bf16[2,448,256]{2,1,0:T(8,128)(2,1)S(1)}, u32[]{:S(2)}, u32[]{:S(2)}) %collective-permute-start.1) | collective-permute-done | bytes 458784 | tf_op jit(solution)/shard_map/ppermute | solution.py:366
  18.2 1.8 %collective-permute-start.10 = (bf16[2,448,256]{2,1,0:T(8,128)(2,1)S(1)}, bf16[2,448,256]{2,1,0:T(8,128)(2,1)S(1)}, u32[]{:S(2)}, u32[]{:S(2)}) collective-permute-start(bf16[2,448,256]{2,1,0:T(8,128)(2,1)S(1)} %collective-permute-done.1.refs_2_.refs_9_), channel_id=1, source_target_pairs={{0,8},{8,16},{16,24},{24,28},{28,20},{20,12},{12,4},{4,0},{1,9},{9... | collective-permute-start | bytes 1376264 | tf_op jit(solution)/shard_map/ppermute | solution.py:366
  20.0 0.6 shard_map.95
  20.9 3.7 %collective-permute-done.6.refs_4_ = bf16[8,64,512]{2,1,0:T(8,128)(2,1)S(1)} collective-permute-done((bf16[8,64,512]{2,1,0:T(8,128)(2,1)S(1)}, bf16[8,64,512]{2,1,0:T(8,128)(2,1)S(1)}, u32[]{:S(2)}, u32[]{:S(2)}) %collective-permute-start.6) | collective-permute-done | bytes 524320 | tf_op jit(solution)/shard_map/ppermute | solution.py:363
  24.6 10.9 %collective-permute-done.7.refs_5_ = bf16[8,64,512]{2,1,0:T(8,128)(2,1)S(1)} collective-permute-done((bf16[8,64,512]{2,1,0:T(8,128)(2,1)S(1)}, bf16[8,64,512]{2,1,0:T(8,128)(2,1)S(1)}, u32[]{:S(2)}, u32[]{:S(2)}) %collective-permute-start.7) | collective-permute-done | bytes 524320 | tf_op jit(solution)/shard_map/ppermute | solution.py:363
  36.0 1.8 %collective-permute-start.11 = (bf16[2,448,256]{2,1,0:T(8,128)(2,1)S(1)}, bf16[2,448,256]{2,1,0:T(8,128)(2,1)S(1)}, u32[]{:S(2)}, u32[]{:S(2)}) collective-permute-start(bf16[2,448,256]{2,1,0:T(8,128)(2,1)S(1)} %collective-permute-done.10.refs_11_), channel_id=1, source_target_pairs={{0,8},{8,16},{16,24},{24,28},{28,20},{20,12},{12,4},{4,0},{1,9},{9... | collective-permute-start | bytes 1376264 | tf_op jit(solution)/shard_map/ppermute | solution.py:366
  38.2 3.5 %shard_map.96 = (f32[512,512]{1,0:T(8,128)S(1)}, bf16[8,2,448,256]{3,2,1,0:T(8,128)(2,1)S(1)}) custom-call(s32[2]{0:T(128)S(1)} %pad_add_fusion.me_ref, bf16[8,64,512]{2,1,0:T(8,128)(2,1)S(1)} %get-tuple-element.48.refs_0_, bf16[8,64,512]{2,1,0:T(8,128)(2,1)S(1)} %get-tuple-element.49.refs_1_, bf16[8,64,512]{2,1,0:T(8,128)(2,1)S(1)} %collective-permute-done.4.refs_2_, ...), custom_call_target="tpu_custom_call" | custom-call | bytes 3000000 | tf_op jit(solution)/shard_map/pallas_call | solution.py:36
  41.7 6.8 %collective-permute-done.11.ups_ref.refs_8_ = bf16[2,448,256]{2,1,0:T(8,128)(2,1)S(1)} collective-permute-done((bf16[2,448,256]{2,1,0:T(8,128)(2,1)S(1)}, bf16[2,448,256]{2,1,0:T(8,128)(2,1)S(1)}, u32[]{:S(2)}, u32[]{:S(2)}) %collective-permute-start.11) | collective-permute-done | bytes 458784 | tf_op jit(solution)/shard_map/ppermute | solution.py:366
  48.5 1.5 %collective-permute-done.13.downs_ref.refs_9_ = bf16[2,448,256]{2,1,0:T(8,128)(2,1)S(1)} collective-permute-done((bf16[2,448,256]{2,1,0:T(8,128)(2,1)S(1)}, bf16[2,448,256]{2,1,0:T(8,128)(2,1)S(1)}, u32[]{:S(2)}, u32[]{:S(2)}) %collective-permute-start.13) | collective-permute-done | bytes 458784 | tf_op jit(solution)/shard_map/ppermute | solution.py:366
  50.1 0.6 shard_map.97
  50.6 1.6 %collective-permute-start.14 = (bf16[1,448,256]{2,1,0:T(8,128)(2,1)S(1)}, bf16[1,448,256]{2,1,0:T(8,128)(2,1)S(1)}, u32[]{:S(2)}, u32[]{:S(2)}) collective-permute-start(bf16[1,448,256]{2,1,0:T(8,128)(2,1)S(1)} %get-tuple-element.51), channel_id=1, source_target_pairs={{0,8},{8,16},{16,24},{24,28},{28,20},{20,12},{12,4},{4,0},{1,9},{9... | collective-permute-start | bytes 688136 | tf_op jit(solution)/shard_map/ppermute | solution.py:366
  52.7 1.8 %shard_map.98 = (f32[512,512]{1,0:T(8,128)S(1)}, bf16[8,2,448,256]{3,2,1,0:T(8,128)(2,1)S(1)}) custom-call(s32[2]{0:T(128)S(1)} %pad_add_fusion.me_ref, bf16[8,64,512]{2,1,0:T(8,128)(2,1)S(1)} %get-tuple-element.48.refs_0_, bf16[8,64,512]{2,1,0:T(8,128)(2,1)S(1)} %get-tuple-element.49.refs_1_, ...), custom_call_target="tpu_custom_call", output_to_operand_aliasing={{1}: (12, {})} | custom-call | bytes 3000000 | tf_op jit(solution)/shard_map/pallas_call | solution.py:36
  54.5 2.5 %collective-permute-done.14.refs_8_ = bf16[1,448,256]{2,1,0:T(8,128)(2,1)S(1)} collective-permute-done((bf16[1,448,256]{2,1,0:T(8,128)(2,1)S(1)}, bf16[1,448,256]{2,1,0:T(8,128)(2,1)S(1)}, u32[]{:S(2)}, u32[]{:S(2)}) %collective-permute-start.14) | collective-permute-done | bytes 229408 | tf_op jit(solution)/shard_map/ppermute | solution.py:366
  57.1 1.3 %collective-permute-done.15.refs_9_ = bf16[1,448,256]{2,1,0:T(8,128)(2,1)S(1)} collective-permute-done((bf16[1,448,256]{2,1,0:T(8,128)(2,1)S(1)}, bf16[1,448,256]{2,1,0:T(8,128)(2,1)S(1)}, u32[]{:S(2)}, u32[]{:S(2)}) %collective-permute-start.15) | collective-permute-done | bytes 229408 | tf_op jit(solution)/shard_map/ppermute | solution.py:366
  58.4 2.0 %shard_map.99 = (bf16[512,256]{1,0:T(8,128)(2,1)S(1)}, f32[512,1]{1,0:T(8,128)S(1)}, f32[512,1]{1,0:T(8,128)S(1)}, f32[1,512]{1,0:T(1,128)S(1)}, bf16[8,2,448,256]{3,2,1,0:T(8,128)(2,1)S(1)}) custom-call(s32[2]{0:T(128)S(1)} %pad_add_fusion.me_ref, bf16[8,64,512]{2,1,0:T(8,128)(2,1)S(1)} %get-tuple-element.48.refs_0_, ...), custom_call_target="tpu_custom_call", output_to_operand_aliasing={{4}: (12, {})} | custom-call | bytes 3000000 | tf_op jit(solution)/shard_map/pallas_call | solution.py:36
  60.5 1.6 %collective-permute-start.16 = (bf16[512,256]{1,0:T(8,128)(2,1)S(1)}, bf16[512,256]{1,0:T(8,128)(2,1)S(1)}, u32[]{:S(2)}, u32[]{:S(2)}) collective-permute-start(bf16[512,256]{1,0:T(8,128)(2,1)S(1)} %get-tuple-element.56.kv_ref), channel_id=1, source_target_pairs={{0,2},{1,3},{2,0},{3,1},{4,6},{5,7},{6,4},{7,5},{8,10},{9,11},{10,... | collective-permute-start | bytes 786440 | tf_op jit(solution)/shard_map/ppermute | solution.py:363
  62.1 7.1 %collective-permute-done.16.kv_ref = bf16[512,256]{1,0:T(8,128)(2,1)S(1)} collective-permute-done((bf16[512,256]{1,0:T(8,128)(2,1)S(1)}, bf16[512,256]{1,0:T(8,128)(2,1)S(1)}, u32[]{:S(2)}, u32[]{:S(2)}) %collective-permute-start.16) | collective-permute-done | bytes 262176 | tf_op jit(solution)/shard_map/ppermute | solution.py:363
  69.2 4.7 %shard_map.100 = (bf16[2,128,896]{2,1,0:T(8,128)(2,1)S(1)}, bf16[2,128,896]{2,1,0:T(8,128)(2,1)S(1)}, f32[256,256]{1,0:T(8,128)S(1)}, bf16[256,256]{1,0:T(8,128)(2,1)S(1)}) custom-call(s32[2]{0:T(128)S(1)} %pad_add_fusion.me_ref, bf16[2,2,128,896]{3,2,1,0:T(8,128)(2,1)S(1)} %get-tuple-element.43.own_ref, ...), custom_call_target="tpu_custom_call" | custom-call | bytes 18000000 | tf_op jit(solution)/shard_map/pallas_call | solution.py:36
  73.9 1.6 %collective-permute-start.20 = (bf16[256,256]{1,0:T(8,128)(2,1)S(1)}, bf16[256,256]{1,0:T(8,128)(2,1)S(1)}, u32[]{:S(2)}, u32[]{:S(2)}) collective-permute-start(bf16[256,256]{1,0:T(8,128)(2,1)S(1)} %get-tuple-element.69), channel_id=1, source_target_pairs={{0,2},{1,3},{2,0},{3,1},{4,6},{5,7},{6,4},{7,5},{8,10},{9,11},{10,... | collective-permute-start | bytes 393224 | tf_op jit(solution)/shard_map/ppermute | solution.py:363
  76.0 4.7 %shard_map.101 = (bf16[2,128,896]{2,1,0:T(8,128)(2,1)S(1)}, bf16[2,128,896]{2,1,0:T(8,128)(2,1)S(1)}, f32[256,256]{1,0:T(8,128)S(1)}, f32[256,256]{1,0:T(8,128)S(1)}) custom-call(s32[2]{0:T(128)S(1)} %pad_add_fusion.me_ref, bf16[2,2,128,896]{3,2,1,0:T(8,128)(2,1)S(1)} %get-tuple-element.43.own_ref, ...), custom_call_target="tpu_custom_call" | custom-call | bytes 18000000 | tf_op jit(solution)/shard_map/pallas_call | solution.py:36
  80.7 3.9 %collective-permute-done.19 = f32[256,256]{1,0:T(8,128)S(1)} collective-permute-done((f32[256,256]{1,0:T(8,128)S(1)}, f32[256,256]{1,0:T(8,128)S(1)}, u32[]{:S(2)}, u32[]{:S(2)}) %collective-permute-start.19) | collective-permute-done | bytes 262176 | tf_op jit(solution)/shard_map/ppermute | solution.py:363
  84.8 1.3 shard_map.106
  86.0 0.5 collective-permute-start.28
  86.6 1.6 %collective-permute-start.24 = (bf16[1,448,256]{2,1,0:T(8,128)(2,1)S(1)}, bf16[1,448,256]{2,1,0:T(8,128)(2,1)S(1)}, u32[]{:S(2)}, u32[]{:S(2)}) collective-permute-start(bf16[1,448,256]{2,1,0:T(8,128)(2,1)S(1)} %get-tuple-element.77), channel_id=1, source_target_pairs={{0,8},{8,16},{16,24},{24,28},{28,20},{20,12},{12,4},{4,0},{1,9},{9... | collective-permute-start | bytes 688136 | tf_op jit(solution)/shard_map/ppermute | solution.py:366
  88.1 2.9 %shard_map.103 = (f32[128,3584]{1,0:T(8,128)S(1)}, bf16[128,3584]{1,0:T(8,128)(2,1)S(1)}) custom-call(s32[2]{0:T(128)S(1)} %pad_add_fusion.me_ref, f32[512,1]{1,0:T(8,128)S(1)} %get-tuple-element.66.kind_ref, bf16[512,256]{1,0:T(8,128)(2,1)S(1)} %pad_maximum_fusion.g_ref.refs_8_, bf16[512,256]{1,0:T(8,128)(2,1)S(1)} %collective-permute-done.21.gc_ref, ...), custom_call_target="tpu_custom_call" | custom-call | bytes 21000000 | tf_op jit(solution)/shard_map/pallas_call | solution.py:36
  91.1 1.5 %shard_map.105 = (f32[2,448,256]{2,1,0:T(8,128)S(1)}, f32[2,448,256]{2,1,0:T(8,128)S(1)}) custom-call(s32[2]{0:T(128)S(1)} %pad_add_fusion.me_ref, bf16[8,64,512]{2,1,0:T(8,128)(2,1)S(1)} %get-tuple-element.48.refs_0_, bf16[8,64,512]{2,1,0:T(8,128)(2,1)S(1)} %get-tuple-element.49.refs_1_, bf16[8,64,512]{2,1,0:T(8,128)(2,1)S(1)} %collective-permute-done.4.refs_2_, ...), custom_call_target="tpu_custom_call" | custom-call | bytes 9000000 | tf_op jit(solution)/shard_map/pallas_call | solution.py:36
  92.6 1.5 %collective-permute-done.28 = bf16[1,448,256]{2,1,0:T(8,128)(2,1)S(1)} collective-permute-done((bf16[1,448,256]{2,1,0:T(8,128)(2,1)S(1)}, bf16[1,448,256]{2,1,0:T(8,128)(2,1)S(1)}, u32[]{:S(2)}, u32[]{:S(2)}) %collective-permute-start.28) | collective-permute-done | bytes 229408 | tf_op jit(solution)/shard_map/ppermute | solution.py:366
  94.8 1.6 %collective-permute-start.25 = (bf16[2,448,256]{2,1,0:T(8,128)(2,1)S(1)}, bf16[2,448,256]{2,1,0:T(8,128)(2,1)S(1)}, u32[]{:S(2)}, u32[]{:S(2)}) collective-permute-start(bf16[2,448,256]{2,1,0:T(8,128)(2,1)S(1)} %add_convert_fusion.6), channel_id=1, source_target_pairs={{0,8},{8,16},{16,24},{24,28},{28,20},{20,12},{12,4},{4,0},{1,9},{9... | collective-permute-start | bytes 1376264 | tf_op jit(solution)/shard_map/ppermute | solution.py:366
  96.9 2.3 %shard_map.104 = (f32[2,448,256]{2,1,0:T(8,128)S(1)}, f32[2,448,256]{2,1,0:T(8,128)S(1)}, f32[2,448,256]{2,1,0:T(8,128)S(1)}, f32[2,448,256]{2,1,0:T(8,128)S(1)}, f32[2,448,256]{2,1,0:T(8,128)S(1)}) custom-call(s32[2]{0:T(128)S(1)} %pad_add_fusion.me_ref, bf16[8,64,512]{2,1,0:T(8,128)(2,1)S(1)} %get-tuple-element.48.refs_0_, ...), custom_call_target="tpu_custom_call" | custom-call | bytes 18000000 | tf_op jit(solution)/shard_map/pallas_call | solution.py:36
  99.2 1.6 %collective-permute-start.23 = (bf16[128,3584]{1,0:T(8,128)(2,1)S(1)}, bf16[128,3584]{1,0:T(8,128)(2,1)S(1)}, u32[]{:S(2)}, u32[]{:S(2)}) collective-permute-start(bf16[128,3584]{1,0:T(8,128)(2,1)S(1)} %get-tuple-element.72.refs_9_), channel_id=1, source_target_pairs={{0,2},{1,3},{2,0},{3,1},{4,6},{5,7},{6,4},{7,5},{8,10},{9,11},{10,... | collective-permute-start | bytes 2752520 | tf_op jit(solution)/shard_map/ppermute | solution.py:363
  100.8 5.5 %collective-permute-done.29 = bf16[2,448,256]{2,1,0:T(8,128)(2,1)S(1)} collective-permute-done((bf16[2,448,256]{2,1,0:T(8,128)(2,1)S(1)}, bf16[2,448,256]{2,1,0:T(8,128)(2,1)S(1)}, u32[]{:S(2)}, u32[]{:S(2)}) %collective-permute-start.29) | collective-permute-done | bytes 458784 | tf_op jit(solution)/shard_map/ppermute | solution.py:366
  107.1 1.6 %collective-permute-start.26 = (bf16[2,448,256]{2,1,0:T(8,128)(2,1)S(1)}, bf16[2,448,256]{2,1,0:T(8,128)(2,1)S(1)}, u32[]{:S(2)}, u32[]{:S(2)}) collective-permute-start(bf16[2,448,256]{2,1,0:T(8,128)(2,1)S(1)} %add_convert_fusion.5), channel_id=1, source_target_pairs={{0,8},{8,16},{16,24},{24,28},{28,20},{20,12},{12,4},{4,0},{1,9},{9... | collective-permute-start | bytes 1376264 | tf_op jit(solution)/shard_map/ppermute | solution.py:366
  108.7 1.9 %shard_map.102 = (bf16[128,3584]{1,0:T(8,128)(2,1)}, bf16[128,3584]{1,0:T(8,128)(2,1)}) custom-call(s32[2]{0:T(128)S(1)} %pad_add_fusion.me_ref, bf16[2,128,896]{2,1,0:T(8,128)(2,1)S(1)} %get-tuple-element.60.refs_0_, bf16[2,128,896]{2,1,0:T(8,128)(2,1)S(1)} %collective-permute-done.17.refs_1_, bf16[2,128,896]{2,1,0:T(8,128)(2,1)S(1)} %get-tuple-element.62.refs_2_, ...), custom_call_target="tpu_custom_call" | custom-call | bytes 9000000 | tf_op jit(solution)/shard_map/pallas_call | solution.py:36
  110.6 7.1 %collective-permute-done.30 = bf16[2,448,256]{2,1,0:T(8,128)(2,1)S(1)} collective-permute-done((bf16[2,448,256]{2,1,0:T(8,128)(2,1)S(1)}, bf16[2,448,256]{2,1,0:T(8,128)(2,1)S(1)}, u32[]{:S(2)}, u32[]{:S(2)}) %collective-permute-start.30) | collective-permute-done | bytes 458784 | tf_op jit(solution)/shard_map/ppermute | solution.py:366
  118.5 1.6 %collective-permute-start.27 = (bf16[2,448,256]{2,1,0:T(8,128)(2,1)S(1)}, bf16[2,448,256]{2,1,0:T(8,128)(2,1)S(1)}, u32[]{:S(2)}, u32[]{:S(2)}) collective-permute-start(bf16[2,448,256]{2,1,0:T(8,128)(2,1)S(1)} %add_convert_fusion.4), channel_id=1, source_target_pairs={{0,8},{8,16},{16,24},{24,28},{28,20},{20,12},{12,4},{4,0},{1,9},{9... | collective-permute-start | bytes 1376264 | tf_op jit(solution)/shard_map/ppermute | solution.py:366
  120.1 1.4 %collective-permute-done.23 = bf16[128,3584]{1,0:T(8,128)(2,1)S(1)} collective-permute-done((bf16[128,3584]{1,0:T(8,128)(2,1)S(1)}, bf16[128,3584]{1,0:T(8,128)(2,1)S(1)}, u32[]{:S(2)}, u32[]{:S(2)}) %collective-permute-start.23) | collective-permute-done | bytes 917536 | tf_op jit(solution)/shard_map/ppermute | solution.py:363
  121.6 1.1 fusion
  122.6 5.6 %collective-permute-done.31 = bf16[2,448,256]{2,1,0:T(8,128)(2,1)S(1)} collective-permute-done((bf16[2,448,256]{2,1,0:T(8,128)(2,1)S(1)}, bf16[2,448,256]{2,1,0:T(8,128)(2,1)S(1)}, u32[]{:S(2)}, u32[]{:S(2)}) %collective-permute-start.31) | collective-permute-done | bytes 458784 | tf_op jit(solution)/shard_map/ppermute | solution.py:366
  128.6 1.0 convert_add_fusion
  (51 shorter events, 5.9 us)
Async XLA Ops:
  0.7 1.2 copy-start
  1.9 1.2 copy-start.1
  3.1 35.1 %copy-start.3 = (bf16[2,448,256]{2,1,0:T(8,128)(2,1)S(1)}, bf16[2,448,256]{2,1,0:T(8,128)(2,1)}, u32[]{:S(2)}) copy-start(bf16[2,448,256]{2,1,0:T(8,128)(2,1)} %refs_8_.1) | copy-start | bytes 1376260
  3.8 7.9 %collective-permute-start = (bf16[2,128,896]{2,1,0:T(8,128)(2,1)S(1)}, bf16[2,128,896]{2,1,0:T(8,128)(2,1)S(1)}, u32[]{:S(2)}, u32[]{:S(2)}) collective-permute-start(bf16[2,128,896]{2,1,0:T(8,128)(2,1)S(1)} %get-tuple-element.44), channel_id=1, source_target_pairs={{0,1},{1,0},{2,3},{3,2},{4,5},{5,4},{6,7},{7,6},{8,9},{9,8},{10,11... | collective-permute-start | bytes 1376264 | tf_op jit(solution)/shard_map/ppermute | solution.py:363
  4.3 13.9 %collective-permute-start.1 = (bf16[2,448,256]{2,1,0:T(8,128)(2,1)}, bf16[2,448,256]{2,1,0:T(8,128)(2,1)S(1)}, u32[]{:S(2)}, u32[]{:S(2)}) collective-permute-start(bf16[2,448,256]{2,1,0:T(8,128)(2,1)} %refs_8_.1), channel_id=1, source_target_pairs={{0,8},{8,16},{16,24},{24,28},{28,20},{20,12},{12,4},{4,0},{1,9},{9... | collective-permute-start | bytes 1376264 | tf_op jit(solution)/shard_map/ppermute | solution.py:366
  6.9 13.1 %collective-permute-start.2 = (bf16[2,448,256]{2,1,0:T(8,128)(2,1)}, bf16[2,448,256]{2,1,0:T(8,128)(2,1)S(1)}, u32[]{:S(2)}, u32[]{:S(2)}) collective-permute-start(bf16[2,448,256]{2,1,0:T(8,128)(2,1)} %refs_8_.1), channel_id=1, source_target_pairs={{0,4},{8,0},{16,8},{24,16},{28,24},{20,28},{12,20},{4,12},{1,5},{9... | collective-permute-start | bytes 1376264 | tf_op jit(solution)/shard_map/ppermute | solution.py:366
  6.9 13.1 %collective-permute-start.3 = (bf16[2,128,896]{2,1,0:T(8,128)(2,1)S(1)}, bf16[2,128,896]{2,1,0:T(8,128)(2,1)S(1)}, u32[]{:S(2)}, u32[]{:S(2)}) collective-permute-start(bf16[2,128,896]{2,1,0:T(8,128)(2,1)S(1)} %get-tuple-element.47), channel_id=1, source_target_pairs={{0,1},{1,0},{2,3},{3,2},{4,5},{5,4},{6,7},{7,6},{8,9},{9,8},{10,11... | collective-permute-start | bytes 1376264 | tf_op jit(solution)/shard_map/ppermute | solution.py:363
  7.8 1.2 copy-start.2
  9.8 14.8 %collective-permute-start.6 = (bf16[8,64,512]{2,1,0:T(8,128)(2,1)S(1)}, bf16[8,64,512]{2,1,0:T(8,128)(2,1)S(1)}, u32[]{:S(2)}, u32[]{:S(2)}) collective-permute-start(bf16[8,64,512]{2,1,0:T(8,128)(2,1)S(1)} %get-tuple-element.45.refs_0_), channel_id=1, source_target_pairs={{0,2},{1,3},{2,0},{3,1},{4,6},{5,7},{6,4},{7,5},{8,10},{9,11},{10,... | collective-permute-start | bytes 1572872 | tf_op jit(solution)/shard_map/ppermute | solution.py:363
  11.7 23.8 %collective-permute-start.7 = (bf16[8,64,512]{2,1,0:T(8,128)(2,1)S(1)}, bf16[8,64,512]{2,1,0:T(8,128)(2,1)S(1)}, u32[]{:S(2)}, u32[]{:S(2)}) collective-permute-start(bf16[8,64,512]{2,1,0:T(8,128)(2,1)S(1)} %get-tuple-element.46.refs_1_), channel_id=1, source_target_pairs={{0,2},{1,3},{2,0},{3,1},{4,6},{5,7},{6,4},{7,5},{8,10},{9,11},{10,... | collective-permute-start | bytes 1572872 | tf_op jit(solution)/shard_map/ppermute | solution.py:363
  18.2 17.4 %collective-permute-start.10 = (bf16[2,448,256]{2,1,0:T(8,128)(2,1)S(1)}, bf16[2,448,256]{2,1,0:T(8,128)(2,1)S(1)}, u32[]{:S(2)}, u32[]{:S(2)}) collective-permute-start(bf16[2,448,256]{2,1,0:T(8,128)(2,1)S(1)} %collective-permute-done.1.refs_2_.refs_9_), channel_id=1, source_target_pairs={{0,8},{8,16},{16,24},{24,28},{28,20},{20,12},{12,4},{4,0},{1,9},{9... | collective-permute-start | bytes 1376264 | tf_op jit(solution)/shard_map/ppermute | solution.py:366
  20.6 17.2 %collective-permute-start.4 = (bf16[8,64,512]{2,1,0:T(8,128)(2,1)S(1)}, bf16[8,64,512]{2,1,0:T(8,128)(2,1)S(1)}, u32[]{:S(2)}, u32[]{:S(2)}) collective-permute-start(bf16[8,64,512]{2,1,0:T(8,128)(2,1)S(1)} %get-tuple-element.48.refs_0_), channel_id=1, source_target_pairs={{0,1},{1,0},{2,3},{3,2},{4,5},{5,4},{6,7},{7,6},{8,9},{9,8},{10,11... | collective-permute-start | bytes 1572872 | tf_op jit(solution)/shard_map/ppermute | solution.py:363
  20.7 15.4 %collective-permute-start.12 = (bf16[2,448,256]{2,1,0:T(8,128)(2,1)S(1)}, bf16[2,448,256]{2,1,0:T(8,128)(2,1)S(1)}, u32[]{:S(2)}, u32[]{:S(2)}) collective-permute-start(bf16[2,448,256]{2,1,0:T(8,128)(2,1)S(1)} %collective-permute-done.2.refs_3_.refs_10_), channel_id=1, source_target_pairs={{0,4},{8,0},{16,8},{24,16},{28,24},{20,28},{12,20},{4,12},{1,5},{9... | collective-permute-start | bytes 1376264 | tf_op jit(solution)/shard_map/ppermute | solution.py:366
  24.6 13.5 %collective-permute-start.5 = (bf16[8,64,512]{2,1,0:T(8,128)(2,1)S(1)}, bf16[8,64,512]{2,1,0:T(8,128)(2,1)S(1)}, u32[]{:S(2)}, u32[]{:S(2)}) collective-permute-start(bf16[8,64,512]{2,1,0:T(8,128)(2,1)S(1)} %get-tuple-element.49.refs_1_), channel_id=1, source_target_pairs={{0,1},{1,0},{2,3},{3,2},{4,5},{5,4},{6,7},{7,6},{8,9},{9,8},{10,11... | collective-permute-start | bytes 1572872 | tf_op jit(solution)/shard_map/ppermute | solution.py:363
  35.5 2.6 %collective-permute-start.8 = (bf16[8,64,512]{2,1,0:T(8,128)(2,1)S(1)}, bf16[8,64,512]{2,1,0:T(8,128)(2,1)S(1)}, u32[]{:S(2)}, u32[]{:S(2)}) collective-permute-start(bf16[8,64,512]{2,1,0:T(8,128)(2,1)S(1)} %collective-permute-done.6.refs_4_), channel_id=1, source_target_pairs={{0,1},{1,0},{2,3},{3,2},{4,5},{5,4},{6,7},{7,6},{8,9},{9,8},{10,11... | collective-permute-start | bytes 1572872 | tf_op jit(solution)/shard_map/ppermute | solution.py:363
  35.5 2.7 %collective-permute-start.9 = (bf16[8,64,512]{2,1,0:T(8,128)(2,1)S(1)}, bf16[8,64,512]{2,1,0:T(8,128)(2,1)S(1)}, u32[]{:S(2)}, u32[]{:S(2)}) collective-permute-start(bf16[8,64,512]{2,1,0:T(8,128)(2,1)S(1)} %collective-permute-done.7.refs_5_), channel_id=1, source_target_pairs={{0,1},{1,0},{2,3},{3,2},{4,5},{5,4},{6,7},{7,6},{8,9},{9,8},{10,11... | collective-permute-start | bytes 1572872 | tf_op jit(solution)/shard_map/ppermute | solution.py:363
  36.0 12.5 %collective-permute-start.11 = (bf16[2,448,256]{2,1,0:T(8,128)(2,1)S(1)}, bf16[2,448,256]{2,1,0:T(8,128)(2,1)S(1)}, u32[]{:S(2)}, u32[]{:S(2)}) collective-permute-start(bf16[2,448,256]{2,1,0:T(8,128)(2,1)S(1)} %collective-permute-done.10.refs_11_), channel_id=1, source_target_pairs={{0,8},{8,16},{16,24},{24,28},{28,20},{20,12},{12,4},{4,0},{1,9},{9... | collective-permute-start | bytes 1376264 | tf_op jit(solution)/shard_map/ppermute | solution.py:366
  37.9 12.2 %collective-permute-start.13 = (bf16[2,448,256]{2,1,0:T(8,128)(2,1)S(1)}, bf16[2,448,256]{2,1,0:T(8,128)(2,1)S(1)}, u32[]{:S(2)}, u32[]{:S(2)}) collective-permute-start(bf16[2,448,256]{2,1,0:T(8,128)(2,1)S(1)} %collective-permute-done.12.refs_12_), channel_id=1, source_target_pairs={{0,4},{8,0},{16,8},{24,16},{28,24},{20,28},{12,20},{4,12},{1,5},{9... | collective-permute-start | bytes 1376264 | tf_op jit(solution)/shard_map/ppermute | solution.py:366
  50.6 6.5 %collective-permute-start.14 = (bf16[1,448,256]{2,1,0:T(8,128)(2,1)S(1)}, bf16[1,448,256]{2,1,0:T(8,128)(2,1)S(1)}, u32[]{:S(2)}, u32[]{:S(2)}) collective-permute-start(bf16[1,448,256]{2,1,0:T(8,128)(2,1)S(1)} %get-tuple-element.51), channel_id=1, source_target_pairs={{0,8},{8,16},{16,24},{24,28},{28,20},{20,12},{12,4},{4,0},{1,9},{9... | collective-permute-start | bytes 688136 | tf_op jit(solution)/shard_map/ppermute | solution.py:366
  52.3 6.1 %collective-permute-start.15 = (bf16[1,448,256]{2,1,0:T(8,128)(2,1)S(1)}, bf16[1,448,256]{2,1,0:T(8,128)(2,1)S(1)}, u32[]{:S(2)}, u32[]{:S(2)}) collective-permute-start(bf16[1,448,256]{2,1,0:T(8,128)(2,1)S(1)} %get-tuple-element.52), channel_id=1, source_target_pairs={{0,4},{8,0},{16,8},{24,16},{28,24},{20,28},{12,20},{4,12},{1,5},{9... | collective-permute-start | bytes 688136 | tf_op jit(solution)/shard_map/ppermute | solution.py:366
  60.4 27.7 %collective-permute-start.22 = (bf16[8,2,448,256]{3,2,1,0:T(8,128)(2,1)S(1)}, bf16[8,2,448,256]{3,2,1,0:T(8,128)(2,1)S(1)}, u32[]{:S(2)}, u32[]{:S(2)}) collective-permute-start(bf16[8,2,448,256]{3,2,1,0:T(8,128)(2,1)S(1)} %get-tuple-element.70.w_ref), channel_id=1, source_target_pairs={{0,1},{1,0},{2,3},{3,2},{4,5},{5,4},{6,7},{7,6},{8,9},{9,8},{10,11... | collective-permute-start | bytes 11010056 | tf_op jit(solution)/shard_map/ppermute | solution.py:363
  60.5 8.7 %collective-permute-start.16 = (bf16[512,256]{1,0:T(8,128)(2,1)S(1)}, bf16[512,256]{1,0:T(8,128)(2,1)S(1)}, u32[]{:S(2)}, u32[]{:S(2)}) collective-permute-start(bf16[512,256]{1,0:T(8,128)(2,1)S(1)} %get-tuple-element.56.kv_ref), channel_id=1, source_target_pairs={{0,2},{1,3},{2,0},{3,1},{4,6},{5,7},{6,4},{7,5},{8,10},{9,11},{10,... | collective-permute-start | bytes 786440 | tf_op jit(solution)/shard_map/ppermute | solution.py:363
  73.9 6.8 %collective-permute-start.20 = (bf16[256,256]{1,0:T(8,128)(2,1)S(1)}, bf16[256,256]{1,0:T(8,128)(2,1)S(1)}, u32[]{:S(2)}, u32[]{:S(2)}) collective-permute-start(bf16[256,256]{1,0:T(8,128)(2,1)S(1)} %get-tuple-element.69), channel_id=1, source_target_pairs={{0,2},{1,3},{2,0},{3,1},{4,6},{5,7},{6,4},{7,5},{8,10},{9,11},{10,... | collective-permute-start | bytes 393224 | tf_op jit(solution)/shard_map/ppermute | solution.py:363
  75.5 9.2 %collective-permute-start.19 = (f32[256,256]{1,0:T(8,128)S(1)}, f32[256,256]{1,0:T(8,128)S(1)}, u32[]{:S(2)}, u32[]{:S(2)}) collective-permute-start(f32[256,256]{1,0:T(8,128)S(1)} %get-tuple-element.59.refs_0_), channel_id=1, source_target_pairs={{0,2},{1,3},{2,0},{3,1},{4,6},{5,7},{6,4},{7,5},{8,10},{9,11},{10,... | collective-permute-start | bytes 786440 | tf_op jit(solution)/shard_map/ppermute | solution.py:363
  84.7 3.4 %collective-permute-start.21 = (bf16[512,256]{1,0:T(8,128)(2,1)S(1)}, bf16[512,256]{1,0:T(8,128)(2,1)S(1)}, u32[]{:S(2)}, u32[]{:S(2)}) collective-permute-start(bf16[512,256]{1,0:T(8,128)(2,1)S(1)} %pad_maximum_fusion.g_ref.refs_8_), channel_id=1, source_target_pairs={{0,1},{1,0},{2,3},{3,2},{4,5},{5,4},{6,7},{7,6},{8,9},{9,8},{10,11... | collective-permute-start | bytes 786440 | tf_op jit(solution)/shard_map/ppermute | solution.py:363
  86.0 8.1 %collective-permute-start.28 = (bf16[1,448,256]{2,1,0:T(8,128)(2,1)S(1)}, bf16[1,448,256]{2,1,0:T(8,128)(2,1)S(1)}, u32[]{:S(2)}, u32[]{:S(2)}) collective-permute-start(bf16[1,448,256]{2,1,0:T(8,128)(2,1)S(1)} %get-tuple-element.81), channel_id=1, source_target_pairs={{0,4},{8,0},{16,8},{24,16},{28,24},{20,28},{12,20},{4,12},{1,5},{9... | collective-permute-start | bytes 688136 | tf_op jit(solution)/shard_map/ppermute | solution.py:366
  86.6 8.1 %collective-permute-start.24 = (bf16[1,448,256]{2,1,0:T(8,128)(2,1)S(1)}, bf16[1,448,256]{2,1,0:T(8,128)(2,1)S(1)}, u32[]{:S(2)}, u32[]{:S(2)}) collective-permute-start(bf16[1,448,256]{2,1,0:T(8,128)(2,1)S(1)} %get-tuple-element.77), channel_id=1, source_target_pairs={{0,8},{8,16},{16,24},{24,28},{28,20},{20,12},{12,4},{4,0},{1,9},{9... | collective-permute-start | bytes 688136 | tf_op jit(solution)/shard_map/ppermute | solution.py:366
  94.2 12.2 %collective-permute-start.29 = (bf16[2,448,256]{2,1,0:T(8,128)(2,1)S(1)}, bf16[2,448,256]{2,1,0:T(8,128)(2,1)S(1)}, u32[]{:S(2)}, u32[]{:S(2)}) collective-permute-start(bf16[2,448,256]{2,1,0:T(8,128)(2,1)S(1)} %add_convert_fusion.3), channel_id=1, source_target_pairs={{0,4},{8,0},{16,8},{24,16},{28,24},{20,28},{12,20},{4,12},{1,5},{9... | collective-permute-start | bytes 1376264 | tf_op jit(solution)/shard_map/ppermute | solution.py:366
  94.8 12.2 %collective-permute-start.25 = (bf16[2,448,256]{2,1,0:T(8,128)(2,1)S(1)}, bf16[2,448,256]{2,1,0:T(8,128)(2,1)S(1)}, u32[]{:S(2)}, u32[]{:S(2)}) collective-permute-start(bf16[2,448,256]{2,1,0:T(8,128)(2,1)S(1)} %add_convert_fusion.6), channel_id=1, source_target_pairs={{0,8},{8,16},{16,24},{24,28},{28,20},{20,12},{12,4},{4,0},{1,9},{9... | collective-permute-start | bytes 1376264 | tf_op jit(solution)/shard_map/ppermute | solution.py:366
  96.4 12.4 %collective-permute-start.17 = (bf16[2,128,896]{2,1,0:T(8,128)(2,1)S(1)}, bf16[2,128,896]{2,1,0:T(8,128)(2,1)S(1)}, u32[]{:S(2)}, u32[]{:S(2)}) collective-permute-start(bf16[2,128,896]{2,1,0:T(8,128)(2,1)S(1)} %get-tuple-element.61), channel_id=1, source_target_pairs={{0,1},{1,0},{2,3},{3,2},{4,5},{5,4},{6,7},{7,6},{8,9},{9,8},{10,11... | collective-permute-start | bytes 1376264 | tf_op jit(solution)/shard_map/ppermute | solution.py:363
  96.4 12.4 %collective-permute-start.18 = (bf16[2,128,896]{2,1,0:T(8,128)(2,1)S(1)}, bf16[2,128,896]{2,1,0:T(8,128)(2,1)S(1)}, u32[]{:S(2)}, u32[]{:S(2)}) collective-permute-start(bf16[2,128,896]{2,1,0:T(8,128)(2,1)S(1)} %get-tuple-element.63), channel_id=1, source_target_pairs={{0,1},{1,0},{2,3},{3,2},{4,5},{5,4},{6,7},{7,6},{8,9},{9,8},{10,11... | collective-permute-start | bytes 1376264 | tf_op jit(solution)/shard_map/ppermute | solution.py:363
  99.2 22.3 %collective-permute-start.23 = (bf16[128,3584]{1,0:T(8,128)(2,1)S(1)}, bf16[128,3584]{1,0:T(8,128)(2,1)S(1)}, u32[]{:S(2)}, u32[]{:S(2)}) collective-permute-start(bf16[128,3584]{1,0:T(8,128)(2,1)S(1)} %get-tuple-element.72.refs_9_), channel_id=1, source_target_pairs={{0,2},{1,3},{2,0},{3,1},{4,6},{5,7},{6,4},{7,5},{8,10},{9,11},{10,... | collective-permute-start | bytes 2752520 | tf_op jit(solution)/shard_map/ppermute | solution.py:363
  106.5 11.3 %collective-permute-start.30 = (bf16[2,448,256]{2,1,0:T(8,128)(2,1)S(1)}, bf16[2,448,256]{2,1,0:T(8,128)(2,1)S(1)}, u32[]{:S(2)}, u32[]{:S(2)}) collective-permute-start(bf16[2,448,256]{2,1,0:T(8,128)(2,1)S(1)} %add_convert_fusion.2), channel_id=1, source_target_pairs={{0,4},{8,0},{16,8},{24,16},{28,24},{20,28},{12,20},{4,12},{1,5},{9... | collective-permute-start | bytes 1376264 | tf_op jit(solution)/shard_map/ppermute | solution.py:366
  107.1 11.3 %collective-permute-start.26 = (bf16[2,448,256]{2,1,0:T(8,128)(2,1)S(1)}, bf16[2,448,256]{2,1,0:T(8,128)(2,1)S(1)}, u32[]{:S(2)}, u32[]{:S(2)}) collective-permute-start(bf16[2,448,256]{2,1,0:T(8,128)(2,1)S(1)} %add_convert_fusion.5), channel_id=1, source_target_pairs={{0,8},{8,16},{16,24},{24,28},{28,20},{20,12},{12,4},{4,0},{1,9},{9... | collective-permute-start | bytes 1376264 | tf_op jit(solution)/shard_map/ppermute | solution.py:366
  117.9 10.4 %collective-permute-start.31 = (bf16[2,448,256]{2,1,0:T(8,128)(2,1)S(1)}, bf16[2,448,256]{2,1,0:T(8,128)(2,1)S(1)}, u32[]{:S(2)}, u32[]{:S(2)}) collective-permute-start(bf16[2,448,256]{2,1,0:T(8,128)(2,1)S(1)} %add_convert_fusion.1), channel_id=1, source_target_pairs={{0,4},{8,0},{16,8},{24,16},{28,24},{20,28},{12,20},{4,12},{1,5},{9... | collective-permute-start | bytes 1376264 | tf_op jit(solution)/shard_map/ppermute | solution.py:366
  118.5 10.1 %collective-permute-start.27 = (bf16[2,448,256]{2,1,0:T(8,128)(2,1)S(1)}, bf16[2,448,256]{2,1,0:T(8,128)(2,1)S(1)}, u32[]{:S(2)}, u32[]{:S(2)}) collective-permute-start(bf16[2,448,256]{2,1,0:T(8,128)(2,1)S(1)} %add_convert_fusion.4), channel_id=1, source_target_pairs={{0,8},{8,16},{16,24},{24,28},{28,20},{20,12},{12,4},{4,0},{1,9},{9... | collective-permute-start | bytes 1376264 | tf_op jit(solution)/shard_map/ppermute | solution.py:366

commit v13 on v12

--- a/solution.py
+++ b/solution.py
@@ -59,7 +59,7 @@
     return jnp.broadcast_to(row, (128, row.shape[1])).T[:, :1]
 
 
-def blocks_kernel(depth, me_ref, tok_ref, ids_ref, *out_refs):
+def blocks_kernel(depth, me_ref, tok_ref, ids_ref, whole_ref, *out_refs):
     count, rows, lanes = out_refs[0].shape
     base = lanes - 128
     lane = lax.broadcasted_iota(jnp.int32, (rows, 128), 1) - (depth - base)
@@ -75,13 +75,14 @@
             for i, mark in enumerate(marks):
                 last = jnp.where(lane == i, mark[here], last)
             out_ref[j, :, base:] = last.astype(BF16)
+        whole_ref[h] = out_ref[...]
 
 
 def token_blocks(me, tokens, ids, count):
     rows, width = tokens.shape
     depth = width // count
     lanes = -(-(depth + 3) // 128) * 128
-    out = [shaped((count, rows // 2, lanes), BF16)] * 2
+    out = [shaped((2, count, rows // 2, lanes), BF16)] + [shaped((count, rows // 2, lanes), BF16)] * 2
     return call(functools.partial(blocks_kernel, depth), me, (tokens, ids), out, 1)
 
 
@@ -108,7 +109,7 @@
 def pack_heads(me, queries, upstream):
     rows = queries.shape[0]
     out = [shaped((2, 2, rows, SPAN), BF16)] + [shaped((2, rows, SPAN), BF16)] * 2
-    return call(pack_kernel, me, (queries, upstream), out, 2)
+    return call(pack_kernel, me, (queries, upstream), out, 1)
 
 
 def place_kernel(me_ref, *refs):
@@ -190,6 +191,15 @@
 def hold(me, arrays, others):
     out = [shaped(x.shape, x.dtype) for x in arrays]
     return call(functools.partial(hold_kernel, len(arrays)), me, (*arrays, *others), out, 1)
+
+
+def split_kernel(me_ref, x_ref, *out_refs):
+    for h, ref in enumerate(out_refs):
+        ref[...] = x_ref[h]
+
+
+def split(me, x):
+    return call(split_kernel, me, (x,), [shaped(x.shape[1:], x.dtype)] * 2, 1)
 
 
 def halve_kernel(me_ref, ups_ref, downs_ref, *refs):
@@ -377,8 +387,8 @@
     else:
         weight = lax.all_gather(kv_weight, "fsdp", axis=0)
 
-    blocks = token_blocks(me, tokens, block_ids * 2 + modality, fsdp)
-    across = [swap(x, 2) for x in blocks]
+    whole, *blocks = token_blocks(me, tokens, block_ids * 2 + modality, fsdp)
+    across = split(me, swap(whole, 2))
     own, *others = pack_heads(me, queries, cotangent)
     others = [swap(x, 1) for x in others]
     here = hold(me, blocks, (*weights[1:3], *others)) if near_link else blocks

time: 130 us -> 127 us (0.977)
  waiting for transfers between devices: 65.8 us -> 63.9 us
  starting transfers between devices: 26.6 us -> 25 us
    ppermute x16 -> x15, waiting for transfers between devices: 27.2 us -> 21.5 us  [swap(): return lax.ppermute(x, 'seq', [(i, i ^ bit) for i in range(seq)])]
    ppermute x16, waiting for transfers between devices: 38.6 us -> 42.3 us  [turn(): lax.ppermute(x, 'fsdp', [(CYCLE[i], CYCLE[(i + by) % fsdp]) for i in rang...]
    ppermute x16 -> x15, starting transfers between devices: 9.28 us -> 8.29 us  [swap(): return lax.ppermute(x, 'seq', [(i, i ^ bit) for i in range(seq)])]
    pallas_call x14 -> x15, Pallas kernels: 29.4 us -> 30.1 us  [call(): pl.pallas_call(body, in_specs=[pl.BlockSpec(memory_space=pltpu.SMEM)] + [...]
  transfers between devices with their start and end apart: 32 -> 31, of which waited for: 16 -> 15; matrix products, arithmetic and copies ran while one was open for 2% -> 1% of each run, Pallas kernels for 20% -> 21%
where the time goes in v13:
time: 127 us
  waiting for transfers between devices  63.9 us (50%)
  Pallas kernels  30.1 us (24%)
  starting transfers between devices  25 us (20%)
  other arithmetic  3.56 us (3%)
  local copies, waits for them, and re-layouts  3.54 us (3%)
    ppermute x16, waiting for transfers between devices, turn(): lax.ppermute(x, 'fsdp', [(CYCLE[i], CYCLE[(i + by) % fsdp]) for i in rang...  42.3 us
    pallas_call x15, Pallas kernels, call(): pl.pallas_call(body, in_specs=[pl.BlockSpec(memory_space=pltpu.SMEM)] + [...  30.1 us
    ppermute x15, waiting for transfers between devices, swap(): return lax.ppermute(x, 'seq', [(i, i ^ bit) for i in range(seq)])  21.5 us
    ppermute x16, starting transfers between devices, turn(): lax.ppermute(x, 'fsdp', [(CYCLE[i], CYCLE[(i + by) % fsdp]) for i in rang...  16.7 us
    ppermute x15, starting transfers between devices, swap(): return lax.ppermute(x, 'seq', [(i, i ^ bit) for i in range(seq)])  8.29 us
    unnamed x8, local copies, waits for them, and re-layouts  3.54 us
  transfers between devices with their start and end apart: 31, of which 15 were waited for; matrix products, arithmetic and copies ran while one was open for 1% of the time, Pallas kernels for 21%

profile of v13, /device:TPU:0, one launch (start us, length us, event | category | flops | bytes accessed | tf_op | source)
XLA Modules:
  0.0 126.9 jit_solution(1275431827394707606)
XLA Ops:
  0.7 0.7 multiply_add_fusion.ids_ref
  1.4 1.2 copy-done
  2.6 1.0 shard_map.94
  3.5 3.0 %collective-permute-start.6 = (bf16[2,8,64,512]{3,2,1,0:T(8,128)(2,1)S(1)}, bf16[2,8,64,512]{3,2,1,0:T(8,128)(2,1)S(1)}, u32[]{:S(2)}, u32[]{:S(2)}) collective-permute-start(bf16[2,8,64,512]{3,2,1,0:T(8,128)(2,1)S(1)} %get-tuple-element.53), channel_id=1, source_target_pairs={{0,2},{1,3},{2,0},{3,1},{4,6},{5,7},{6,4},{7,5},{8,10},{9,11},{10,... | collective-permute-start | bytes 3145736 | tf_op jit(solution)/shard_map/ppermute | solution.py:373
  6.6 1.6 %collective-permute-start.1 = (bf16[2,448,256]{2,1,0:T(8,128)(2,1)}, bf16[2,448,256]{2,1,0:T(8,128)(2,1)S(1)}, u32[]{:S(2)}, u32[]{:S(2)}) collective-permute-start(bf16[2,448,256]{2,1,0:T(8,128)(2,1)} %refs_8_.1), channel_id=1, source_target_pairs={{0,8},{8,16},{16,24},{24,28},{28,20},{20,12},{12,4},{4,0},{1,9},{9... | collective-permute-start | bytes 1376264 | tf_op jit(solution)/shard_map/ppermute | solution.py:376
  8.6 1.2 copy-done.1
  9.8 1.2 copy-done.2
  10.9 0.7 shard_map.93
  12.2 6.5 %collective-permute-done.1.refs_2_.refs_9_ = bf16[2,448,256]{2,1,0:T(8,128)(2,1)S(1)} collective-permute-done((bf16[2,448,256]{2,1,0:T(8,128)(2,1)}, bf16[2,448,256]{2,1,0:T(8,128)(2,1)S(1)}, u32[]{:S(2)}, u32[]{:S(2)}) %collective-permute-start.1) | collective-permute-done | bytes 458784 | tf_op jit(solution)/shard_map/ppermute | solution.py:376
  18.7 1.6 %collective-permute-start.9 = (bf16[2,448,256]{2,1,0:T(8,128)(2,1)S(1)}, bf16[2,448,256]{2,1,0:T(8,128)(2,1)S(1)}, u32[]{:S(2)}, u32[]{:S(2)}) collective-permute-start(bf16[2,448,256]{2,1,0:T(8,128)(2,1)S(1)} %collective-permute-done.1.refs_2_.refs_9_), channel_id=1, source_target_pairs={{0,8},{8,16},{16,24},{24,28},{28,20},{20,12},{12,4},{4,0},{1,9},{9... | collective-permute-start | bytes 1376264 | tf_op jit(solution)/shard_map/ppermute | solution.py:376
  20.3 0.6 shard_map.95
  21.7 8.0 %collective-permute-done.6.x_ref = bf16[2,8,64,512]{3,2,1,0:T(8,128)(2,1)S(1)} collective-permute-done((bf16[2,8,64,512]{3,2,1,0:T(8,128)(2,1)S(1)}, bf16[2,8,64,512]{3,2,1,0:T(8,128)(2,1)S(1)}, u32[]{:S(2)}, u32[]{:S(2)}) %collective-permute-start.6) | collective-permute-done | bytes 1048608 | tf_op jit(solution)/shard_map/ppermute | solution.py:373
  29.7 0.6 shard_map.96
  30.9 3.0 %collective-permute-done.11.refs_12_ = bf16[2,448,256]{2,1,0:T(8,128)(2,1)S(1)} collective-permute-done((bf16[2,448,256]{2,1,0:T(8,128)(2,1)S(1)}, bf16[2,448,256]{2,1,0:T(8,128)(2,1)S(1)}, u32[]{:S(2)}, u32[]{:S(2)}) %collective-permute-start.11) | collective-permute-done | bytes 458784 | tf_op jit(solution)/shard_map/ppermute | solution.py:376
  34.0 1.6 %collective-permute-start.10 = (bf16[2,448,256]{2,1,0:T(8,128)(2,1)S(1)}, bf16[2,448,256]{2,1,0:T(8,128)(2,1)S(1)}, u32[]{:S(2)}, u32[]{:S(2)}) collective-permute-start(bf16[2,448,256]{2,1,0:T(8,128)(2,1)S(1)} %collective-permute-done.9.refs_11_), channel_id=1, source_target_pairs={{0,8},{8,16},{16,24},{24,28},{28,20},{20,12},{12,4},{4,0},{1,9},{9... | collective-permute-start | bytes 1376264 | tf_op jit(solution)/shard_map/ppermute | solution.py:376
  36.0 3.5 %shard_map.97 = (f32[512,512]{1,0:T(8,128)S(1)}, bf16[8,2,448,256]{3,2,1,0:T(8,128)(2,1)S(1)}) custom-call(s32[2]{0:T(128)S(1)} %pad_add_fusion.me_ref, bf16[8,64,512]{2,1,0:T(8,128)(2,1)S(1)} %get-tuple-element.51.refs_0_, bf16[8,64,512]{2,1,0:T(8,128)(2,1)S(1)} %get-tuple-element.52.refs_1_, bf16[8,64,512]{2,1,0:T(8,128)(2,1)S(1)} %collective-permute-done.4.refs_2_, ...), custom_call_target="tpu_custom_call" | custom-call | bytes 3000000 | tf_op jit(solution)/shard_map/pallas_call | solution.py:36
  39.5 6.5 %collective-permute-done.10.ups_ref.refs_8_ = bf16[2,448,256]{2,1,0:T(8,128)(2,1)S(1)} collective-permute-done((bf16[2,448,256]{2,1,0:T(8,128)(2,1)S(1)}, bf16[2,448,256]{2,1,0:T(8,128)(2,1)S(1)}, u32[]{:S(2)}, u32[]{:S(2)}) %collective-permute-start.10) | collective-permute-done | bytes 458784 | tf_op jit(solution)/shard_map/ppermute | solution.py:376
  46.0 1.3 %collective-permute-done.12.downs_ref.refs_9_ = bf16[2,448,256]{2,1,0:T(8,128)(2,1)S(1)} collective-permute-done((bf16[2,448,256]{2,1,0:T(8,128)(2,1)S(1)}, bf16[2,448,256]{2,1,0:T(8,128)(2,1)S(1)}, u32[]{:S(2)}, u32[]{:S(2)}) %collective-permute-start.12) | collective-permute-done | bytes 458784 | tf_op jit(solution)/shard_map/ppermute | solution.py:376
  47.3 0.6 shard_map.98
  47.9 1.6 %collective-permute-start.13 = (bf16[1,448,256]{2,1,0:T(8,128)(2,1)S(1)}, bf16[1,448,256]{2,1,0:T(8,128)(2,1)S(1)}, u32[]{:S(2)}, u32[]{:S(2)}) collective-permute-start(bf16[1,448,256]{2,1,0:T(8,128)(2,1)S(1)} %get-tuple-element.57), channel_id=1, source_target_pairs={{0,8},{8,16},{16,24},{24,28},{28,20},{20,12},{12,4},{4,0},{1,9},{9... | collective-permute-start | bytes 688136 | tf_op jit(solution)/shard_map/ppermute | solution.py:376
  50.0 1.8 %shard_map.99 = (f32[512,512]{1,0:T(8,128)S(1)}, bf16[8,2,448,256]{3,2,1,0:T(8,128)(2,1)S(1)}) custom-call(s32[2]{0:T(128)S(1)} %pad_add_fusion.me_ref, bf16[8,64,512]{2,1,0:T(8,128)(2,1)S(1)} %get-tuple-element.51.refs_0_, bf16[8,64,512]{2,1,0:T(8,128)(2,1)S(1)} %get-tuple-element.52.refs_1_, ...), custom_call_target="tpu_custom_call", output_to_operand_aliasing={{1}: (12, {})} | custom-call | bytes 3000000 | tf_op jit(solution)/shard_map/pallas_call | solution.py:36
  51.8 2.2 %collective-permute-done.13.refs_8_ = bf16[1,448,256]{2,1,0:T(8,128)(2,1)S(1)} collective-permute-done((bf16[1,448,256]{2,1,0:T(8,128)(2,1)S(1)}, bf16[1,448,256]{2,1,0:T(8,128)(2,1)S(1)}, u32[]{:S(2)}, u32[]{:S(2)}) %collective-permute-start.13) | collective-permute-done | bytes 229408 | tf_op jit(solution)/shard_map/ppermute | solution.py:376
  54.0 1.6 %collective-permute-done.14.refs_9_ = bf16[1,448,256]{2,1,0:T(8,128)(2,1)S(1)} collective-permute-done((bf16[1,448,256]{2,1,0:T(8,128)(2,1)S(1)}, bf16[1,448,256]{2,1,0:T(8,128)(2,1)S(1)}, u32[]{:S(2)}, u32[]{:S(2)}) %collective-permute-start.14) | collective-permute-done | bytes 229408 | tf_op jit(solution)/shard_map/ppermute | solution.py:376
  55.6 2.0 %shard_map.100 = (bf16[512,256]{1,0:T(8,128)(2,1)S(1)}, f32[512,1]{1,0:T(8,128)S(1)}, f32[512,1]{1,0:T(8,128)S(1)}, f32[1,512]{1,0:T(1,128)S(1)}, bf16[8,2,448,256]{3,2,1,0:T(8,128)(2,1)S(1)}) custom-call(s32[2]{0:T(128)S(1)} %pad_add_fusion.me_ref, bf16[8,64,512]{2,1,0:T(8,128)(2,1)S(1)} %get-tuple-element.51.refs_0_, ...), custom_call_target="tpu_custom_call", output_to_operand_aliasing={{4}: (12, {})} | custom-call | bytes 3000000 | tf_op jit(solution)/shard_map/pallas_call | solution.py:36
  57.7 0.6 collective-permute-start.15
  58.3 8.1 %collective-permute-done.15.kv_ref = bf16[512,256]{1,0:T(8,128)(2,1)S(1)} collective-permute-done((bf16[512,256]{1,0:T(8,128)(2,1)S(1)}, bf16[512,256]{1,0:T(8,128)(2,1)S(1)}, u32[]{:S(2)}, u32[]{:S(2)}) %collective-permute-start.15) | collective-permute-done | bytes 262176 | tf_op jit(solution)/shard_map/ppermute | solution.py:373
  66.4 4.7 %shard_map.101 = (bf16[2,128,896]{2,1,0:T(8,128)(2,1)S(1)}, bf16[2,128,896]{2,1,0:T(8,128)(2,1)S(1)}, f32[256,256]{1,0:T(8,128)S(1)}, bf16[256,256]{1,0:T(8,128)(2,1)S(1)}) custom-call(s32[2]{0:T(128)S(1)} %pad_add_fusion.me_ref, bf16[2,2,128,896]{3,2,1,0:T(8,128)(2,1)S(1)} %get-tuple-element.46.own_ref, ...), custom_call_target="tpu_custom_call" | custom-call | bytes 18000000 | tf_op jit(solution)/shard_map/pallas_call | solution.py:36
  71.1 0.6 collective-permute-start.19
  71.6 1.5 %collective-permute-start.18 = (f32[256,256]{1,0:T(8,128)S(1)}, f32[256,256]{1,0:T(8,128)S(1)}, u32[]{:S(2)}, u32[]{:S(2)}) collective-permute-start(f32[256,256]{1,0:T(8,128)S(1)} %get-tuple-element.65.refs_0_), channel_id=1, source_target_pairs={{0,2},{1,3},{2,0},{3,1},{4,6},{5,7},{6,4},{7,5},{8,10},{9,11},{10,... | collective-permute-start | bytes 786440 | tf_op jit(solution)/shard_map/ppermute | solution.py:373
  73.2 4.7 %shard_map.102 = (bf16[2,128,896]{2,1,0:T(8,128)(2,1)S(1)}, bf16[2,128,896]{2,1,0:T(8,128)(2,1)S(1)}, f32[256,256]{1,0:T(8,128)S(1)}, f32[256,256]{1,0:T(8,128)S(1)}) custom-call(s32[2]{0:T(128)S(1)} %pad_add_fusion.me_ref, bf16[2,2,128,896]{3,2,1,0:T(8,128)(2,1)S(1)} %get-tuple-element.46.own_ref, ...), custom_call_target="tpu_custom_call" | custom-call | bytes 18000000 | tf_op jit(solution)/shard_map/pallas_call | solution.py:36
  77.9 3.9 %collective-permute-done.18 = f32[256,256]{1,0:T(8,128)S(1)} collective-permute-done((f32[256,256]{1,0:T(8,128)S(1)}, f32[256,256]{1,0:T(8,128)S(1)}, u32[]{:S(2)}, u32[]{:S(2)}) %collective-permute-start.18) | collective-permute-done | bytes 262176 | tf_op jit(solution)/shard_map/ppermute | solution.py:373
  82.0 1.3 shard_map.107
  83.7 1.6 %collective-permute-start.23 = (bf16[1,448,256]{2,1,0:T(8,128)(2,1)S(1)}, bf16[1,448,256]{2,1,0:T(8,128)(2,1)S(1)}, u32[]{:S(2)}, u32[]{:S(2)}) collective-permute-start(bf16[1,448,256]{2,1,0:T(8,128)(2,1)S(1)} %get-tuple-element.83), channel_id=1, source_target_pairs={{0,8},{8,16},{16,24},{24,28},{28,20},{20,12},{12,4},{4,0},{1,9},{9... | collective-permute-start | bytes 688136 | tf_op jit(solution)/shard_map/ppermute | solution.py:376
  85.3 2.9 %shard_map.104 = (f32[128,3584]{1,0:T(8,128)S(1)}, bf16[128,3584]{1,0:T(8,128)(2,1)S(1)}) custom-call(s32[2]{0:T(128)S(1)} %pad_add_fusion.me_ref, f32[512,1]{1,0:T(8,128)S(1)} %get-tuple-element.72.kind_ref, bf16[512,256]{1,0:T(8,128)(2,1)S(1)} %pad_maximum_fusion.g_ref.refs_8_, bf16[512,256]{1,0:T(8,128)(2,1)S(1)} %collective-permute-done.20.gc_ref, ...), custom_call_target="tpu_custom_call" | custom-call | bytes 21000000 | tf_op jit(solution)/shard_map/pallas_call | solution.py:36
  88.2 1.5 %shard_map.106 = (f32[2,448,256]{2,1,0:T(8,128)S(1)}, f32[2,448,256]{2,1,0:T(8,128)S(1)}) custom-call(s32[2]{0:T(128)S(1)} %pad_add_fusion.me_ref, bf16[8,64,512]{2,1,0:T(8,128)(2,1)S(1)} %get-tuple-element.51.refs_0_, bf16[8,64,512]{2,1,0:T(8,128)(2,1)S(1)} %get-tuple-element.52.refs_1_, bf16[8,64,512]{2,1,0:T(8,128)(2,1)S(1)} %collective-permute-done.4.refs_2_, ...), custom_call_target="tpu_custom_call" | custom-call | bytes 9000000 | tf_op jit(solution)/shard_map/pallas_call | solution.py:36
  89.8 1.5 %collective-permute-done.27 = bf16[1,448,256]{2,1,0:T(8,128)(2,1)S(1)} collective-permute-done((bf16[1,448,256]{2,1,0:T(8,128)(2,1)S(1)}, bf16[1,448,256]{2,1,0:T(8,128)(2,1)S(1)}, u32[]{:S(2)}, u32[]{:S(2)}) %collective-permute-start.27) | collective-permute-done | bytes 229408 | tf_op jit(solution)/shard_map/ppermute | solution.py:376
  91.9 1.6 %collective-permute-start.24 = (bf16[2,448,256]{2,1,0:T(8,128)(2,1)S(1)}, bf16[2,448,256]{2,1,0:T(8,128)(2,1)S(1)}, u32[]{:S(2)}, u32[]{:S(2)}) collective-permute-start(bf16[2,448,256]{2,1,0:T(8,128)(2,1)S(1)} %add_convert_fusion.6), channel_id=1, source_target_pairs={{0,8},{8,16},{16,24},{24,28},{28,20},{20,12},{12,4},{4,0},{1,9},{9... | collective-permute-start | bytes 1376264 | tf_op jit(solution)/shard_map/ppermute | solution.py:376
  94.1 2.3 %shard_map.105 = (f32[2,448,256]{2,1,0:T(8,128)S(1)}, f32[2,448,256]{2,1,0:T(8,128)S(1)}, f32[2,448,256]{2,1,0:T(8,128)S(1)}, f32[2,448,256]{2,1,0:T(8,128)S(1)}, f32[2,448,256]{2,1,0:T(8,128)S(1)}) custom-call(s32[2]{0:T(128)S(1)} %pad_add_fusion.me_ref, bf16[8,64,512]{2,1,0:T(8,128)(2,1)S(1)} %get-tuple-element.51.refs_0_, ...), custom_call_target="tpu_custom_call" | custom-call | bytes 18000000 | tf_op jit(solution)/shard_map/pallas_call | solution.py:36
  96.4 0.6 collective-permute-start.22
  97.0 6.5 %collective-permute-done.28 = bf16[2,448,256]{2,1,0:T(8,128)(2,1)S(1)} collective-permute-done((bf16[2,448,256]{2,1,0:T(8,128)(2,1)S(1)}, bf16[2,448,256]{2,1,0:T(8,128)(2,1)S(1)}, u32[]{:S(2)}, u32[]{:S(2)}) %collective-permute-start.28) | collective-permute-done | bytes 458784 | tf_op jit(solution)/shard_map/ppermute | solution.py:376
  104.3 1.6 %collective-permute-start.25 = (bf16[2,448,256]{2,1,0:T(8,128)(2,1)S(1)}, bf16[2,448,256]{2,1,0:T(8,128)(2,1)S(1)}, u32[]{:S(2)}, u32[]{:S(2)}) collective-permute-start(bf16[2,448,256]{2,1,0:T(8,128)(2,1)S(1)} %add_convert_fusion.5), channel_id=1, source_target_pairs={{0,8},{8,16},{16,24},{24,28},{28,20},{20,12},{12,4},{4,0},{1,9},{9... | collective-permute-start | bytes 1376264 | tf_op jit(solution)/shard_map/ppermute | solution.py:376
  105.9 1.9 %shard_map.103 = (bf16[128,3584]{1,0:T(8,128)(2,1)}, bf16[128,3584]{1,0:T(8,128)(2,1)}) custom-call(s32[2]{0:T(128)S(1)} %pad_add_fusion.me_ref, bf16[2,128,896]{2,1,0:T(8,128)(2,1)S(1)} %get-tuple-element.66.refs_0_, bf16[2,128,896]{2,1,0:T(8,128)(2,1)S(1)} %collective-permute-done.16.refs_1_, bf16[2,128,896]{2,1,0:T(8,128)(2,1)S(1)} %get-tuple-element.68.refs_2_, ...), custom_call_target="tpu_custom_call" | custom-call | bytes 9000000 | tf_op jit(solution)/shard_map/pallas_call | solution.py:36
  107.8 7.1 %collective-permute-done.29 = bf16[2,448,256]{2,1,0:T(8,128)(2,1)S(1)} collective-permute-done((bf16[2,448,256]{2,1,0:T(8,128)(2,1)S(1)}, bf16[2,448,256]{2,1,0:T(8,128)(2,1)S(1)}, u32[]{:S(2)}, u32[]{:S(2)}) %collective-permute-start.29) | collective-permute-done | bytes 458784 | tf_op jit(solution)/shard_map/ppermute | solution.py:376
  115.7 1.6 %collective-permute-start.26 = (bf16[2,448,256]{2,1,0:T(8,128)(2,1)S(1)}, bf16[2,448,256]{2,1,0:T(8,128)(2,1)S(1)}, u32[]{:S(2)}, u32[]{:S(2)}) collective-permute-start(bf16[2,448,256]{2,1,0:T(8,128)(2,1)S(1)} %add_convert_fusion.4), channel_id=1, source_target_pairs={{0,8},{8,16},{16,24},{24,28},{28,20},{20,12},{12,4},{4,0},{1,9},{9... | collective-permute-start | bytes 1376264 | tf_op jit(solution)/shard_map/ppermute | solution.py:376
  117.3 1.4 %collective-permute-done.22 = bf16[128,3584]{1,0:T(8,128)(2,1)S(1)} collective-permute-done((bf16[128,3584]{1,0:T(8,128)(2,1)S(1)}, bf16[128,3584]{1,0:T(8,128)(2,1)S(1)}, u32[]{:S(2)}, u32[]{:S(2)}) %collective-permute-start.22) | collective-permute-done | bytes 917536 | tf_op jit(solution)/shard_map/ppermute | solution.py:373
  118.7 1.1 fusion
  119.8 5.6 %collective-permute-done.30 = bf16[2,448,256]{2,1,0:T(8,128)(2,1)S(1)} collective-permute-done((bf16[2,448,256]{2,1,0:T(8,128)(2,1)S(1)}, bf16[2,448,256]{2,1,0:T(8,128)(2,1)S(1)}, u32[]{:S(2)}, u32[]{:S(2)}) %collective-permute-start.30) | collective-permute-done | bytes 458784 | tf_op jit(solution)/shard_map/ppermute | solution.py:376
  125.8 1.0 convert_add_fusion
  (50 shorter events, 7.1 us)
Async XLA Ops:
  1.4 1.2 copy-start
  2.6 33.4 %copy-start.3 = (bf16[2,448,256]{2,1,0:T(8,128)(2,1)S(1)}, bf16[2,448,256]{2,1,0:T(8,128)(2,1)}, u32[]{:S(2)}) copy-start(bf16[2,448,256]{2,1,0:T(8,128)(2,1)} %refs_8_.1) | copy-start | bytes 1376260
  3.5 26.2 %collective-permute-start.6 = (bf16[2,8,64,512]{3,2,1,0:T(8,128)(2,1)S(1)}, bf16[2,8,64,512]{3,2,1,0:T(8,128)(2,1)S(1)}, u32[]{:S(2)}, u32[]{:S(2)}) collective-permute-start(bf16[2,8,64,512]{3,2,1,0:T(8,128)(2,1)S(1)} %get-tuple-element.53), channel_id=1, source_target_pairs={{0,2},{1,3},{2,0},{3,1},{4,6},{5,7},{6,4},{7,5},{8,10},{9,11},{10,... | collective-permute-start | bytes 3145736 | tf_op jit(solution)/shard_map/ppermute | solution.py:373
  6.6 12.2 %collective-permute-start.1 = (bf16[2,448,256]{2,1,0:T(8,128)(2,1)}, bf16[2,448,256]{2,1,0:T(8,128)(2,1)S(1)}, u32[]{:S(2)}, u32[]{:S(2)}) collective-permute-start(bf16[2,448,256]{2,1,0:T(8,128)(2,1)} %refs_8_.1), channel_id=1, source_target_pairs={{0,8},{8,16},{16,24},{24,28},{28,20},{20,12},{12,4},{4,0},{1,9},{9... | collective-permute-start | bytes 1376264 | tf_op jit(solution)/shard_map/ppermute | solution.py:376
  8.1 12.2 %collective-permute-start.2 = (bf16[2,448,256]{2,1,0:T(8,128)(2,1)}, bf16[2,448,256]{2,1,0:T(8,128)(2,1)S(1)}, u32[]{:S(2)}, u32[]{:S(2)}) collective-permute-start(bf16[2,448,256]{2,1,0:T(8,128)(2,1)} %refs_8_.1), channel_id=1, source_target_pairs={{0,4},{8,0},{16,8},{24,16},{28,24},{20,28},{12,20},{4,12},{1,5},{9... | collective-permute-start | bytes 1376264 | tf_op jit(solution)/shard_map/ppermute | solution.py:376
  8.6 1.2 copy-start.1
  9.8 1.2 copy-start.2
  11.6 8.7 %collective-permute-start = (bf16[2,128,896]{2,1,0:T(8,128)(2,1)S(1)}, bf16[2,128,896]{2,1,0:T(8,128)(2,1)S(1)}, u32[]{:S(2)}, u32[]{:S(2)}) collective-permute-start(bf16[2,128,896]{2,1,0:T(8,128)(2,1)S(1)} %get-tuple-element.47), channel_id=1, source_target_pairs={{0,1},{1,0},{2,3},{3,2},{4,5},{5,4},{6,7},{7,6},{8,9},{9,8},{10,11... | collective-permute-start | bytes 1376264 | tf_op jit(solution)/shard_map/ppermute | solution.py:373
  11.7 8.6 %collective-permute-start.3 = (bf16[2,128,896]{2,1,0:T(8,128)(2,1)S(1)}, bf16[2,128,896]{2,1,0:T(8,128)(2,1)S(1)}, u32[]{:S(2)}, u32[]{:S(2)}) collective-permute-start(bf16[2,128,896]{2,1,0:T(8,128)(2,1)S(1)} %get-tuple-element.50), channel_id=1, source_target_pairs={{0,1},{1,0},{2,3},{3,2},{4,5},{5,4},{6,7},{7,6},{8,9},{9,8},{10,11... | collective-permute-start | bytes 1376264 | tf_op jit(solution)/shard_map/ppermute | solution.py:373
  18.7 11.7 %collective-permute-start.9 = (bf16[2,448,256]{2,1,0:T(8,128)(2,1)S(1)}, bf16[2,448,256]{2,1,0:T(8,128)(2,1)S(1)}, u32[]{:S(2)}, u32[]{:S(2)}) collective-permute-start(bf16[2,448,256]{2,1,0:T(8,128)(2,1)S(1)} %collective-permute-done.1.refs_2_.refs_9_), channel_id=1, source_target_pairs={{0,8},{8,16},{16,24},{24,28},{28,20},{20,12},{12,4},{4,0},{1,9},{9... | collective-permute-start | bytes 1376264 | tf_op jit(solution)/shard_map/ppermute | solution.py:376
  21.0 14.6 %collective-permute-start.4 = (bf16[8,64,512]{2,1,0:T(8,128)(2,1)S(1)}, bf16[8,64,512]{2,1,0:T(8,128)(2,1)S(1)}, u32[]{:S(2)}, u32[]{:S(2)}) collective-permute-start(bf16[8,64,512]{2,1,0:T(8,128)(2,1)S(1)} %get-tuple-element.51.refs_0_), channel_id=1, source_target_pairs={{0,1},{1,0},{2,3},{3,2},{4,5},{5,4},{6,7},{7,6},{8,9},{9,8},{10,11... | collective-permute-start | bytes 1572872 | tf_op jit(solution)/shard_map/ppermute | solution.py:373
  21.0 12.9 %collective-permute-start.11 = (bf16[2,448,256]{2,1,0:T(8,128)(2,1)S(1)}, bf16[2,448,256]{2,1,0:T(8,128)(2,1)S(1)}, u32[]{:S(2)}, u32[]{:S(2)}) collective-permute-start(bf16[2,448,256]{2,1,0:T(8,128)(2,1)S(1)} %collective-permute-done.2.refs_3_.refs_10_), channel_id=1, source_target_pairs={{0,4},{8,0},{16,8},{24,16},{28,24},{20,28},{12,20},{4,12},{1,5},{9... | collective-permute-start | bytes 1376264 | tf_op jit(solution)/shard_map/ppermute | solution.py:376
  21.5 14.5 %collective-permute-start.5 = (bf16[8,64,512]{2,1,0:T(8,128)(2,1)S(1)}, bf16[8,64,512]{2,1,0:T(8,128)(2,1)S(1)}, u32[]{:S(2)}, u32[]{:S(2)}) collective-permute-start(bf16[8,64,512]{2,1,0:T(8,128)(2,1)S(1)} %get-tuple-element.52.refs_1_), channel_id=1, source_target_pairs={{0,1},{1,0},{2,3},{3,2},{4,5},{5,4},{6,7},{7,6},{8,9},{9,8},{10,11... | collective-permute-start | bytes 1572872 | tf_op jit(solution)/shard_map/ppermute | solution.py:373
  30.3 5.7 %collective-permute-start.7 = (bf16[8,64,512]{2,1,0:T(8,128)(2,1)S(1)}, bf16[8,64,512]{2,1,0:T(8,128)(2,1)S(1)}, u32[]{:S(2)}, u32[]{:S(2)}) collective-permute-start(bf16[8,64,512]{2,1,0:T(8,128)(2,1)S(1)} %get-tuple-element.54.refs_4_), channel_id=1, source_target_pairs={{0,1},{1,0},{2,3},{3,2},{4,5},{5,4},{6,7},{7,6},{8,9},{9,8},{10,11... | collective-permute-start | bytes 1572872 | tf_op jit(solution)/shard_map/ppermute | solution.py:373
  30.4 5.6 %collective-permute-start.8 = (bf16[8,64,512]{2,1,0:T(8,128)(2,1)S(1)}, bf16[8,64,512]{2,1,0:T(8,128)(2,1)S(1)}, u32[]{:S(2)}, u32[]{:S(2)}) collective-permute-start(bf16[8,64,512]{2,1,0:T(8,128)(2,1)S(1)} %get-tuple-element.55.refs_5_), channel_id=1, source_target_pairs={{0,1},{1,0},{2,3},{3,2},{4,5},{5,4},{6,7},{7,6},{8,9},{9,8},{10,11... | collective-permute-start | bytes 1572872 | tf_op jit(solution)/shard_map/ppermute | solution.py:373
  34.0 12.1 %collective-permute-start.10 = (bf16[2,448,256]{2,1,0:T(8,128)(2,1)S(1)}, bf16[2,448,256]{2,1,0:T(8,128)(2,1)S(1)}, u32[]{:S(2)}, u32[]{:S(2)}) collective-permute-start(bf16[2,448,256]{2,1,0:T(8,128)(2,1)S(1)} %collective-permute-done.9.refs_11_), channel_id=1, source_target_pairs={{0,8},{8,16},{16,24},{24,28},{28,20},{20,12},{12,4},{4,0},{1,9},{9... | collective-permute-start | bytes 1376264 | tf_op jit(solution)/shard_map/ppermute | solution.py:376
  35.5 11.8 %collective-permute-start.12 = (bf16[2,448,256]{2,1,0:T(8,128)(2,1)S(1)}, bf16[2,448,256]{2,1,0:T(8,128)(2,1)S(1)}, u32[]{:S(2)}, u32[]{:S(2)}) collective-permute-start(bf16[2,448,256]{2,1,0:T(8,128)(2,1)S(1)} %collective-permute-done.11.refs_12_), channel_id=1, source_target_pairs={{0,4},{8,0},{16,8},{24,16},{28,24},{20,28},{12,20},{4,12},{1,5},{9... | collective-permute-start | bytes 1376264 | tf_op jit(solution)/shard_map/ppermute | solution.py:376
  47.9 6.1 %collective-permute-start.13 = (bf16[1,448,256]{2,1,0:T(8,128)(2,1)S(1)}, bf16[1,448,256]{2,1,0:T(8,128)(2,1)S(1)}, u32[]{:S(2)}, u32[]{:S(2)}) collective-permute-start(bf16[1,448,256]{2,1,0:T(8,128)(2,1)S(1)} %get-tuple-element.57), channel_id=1, source_target_pairs={{0,8},{8,16},{16,24},{24,28},{28,20},{20,12},{12,4},{4,0},{1,9},{9... | collective-permute-start | bytes 688136 | tf_op jit(solution)/shard_map/ppermute | solution.py:376
  49.5 6.0 %collective-permute-start.14 = (bf16[1,448,256]{2,1,0:T(8,128)(2,1)S(1)}, bf16[1,448,256]{2,1,0:T(8,128)(2,1)S(1)}, u32[]{:S(2)}, u32[]{:S(2)}) collective-permute-start(bf16[1,448,256]{2,1,0:T(8,128)(2,1)S(1)} %get-tuple-element.58), channel_id=1, source_target_pairs={{0,4},{8,0},{16,8},{24,16},{28,24},{20,28},{12,20},{4,12},{1,5},{9... | collective-permute-start | bytes 688136 | tf_op jit(solution)/shard_map/ppermute | solution.py:376
  57.6 27.7 %collective-permute-start.21 = (bf16[8,2,448,256]{3,2,1,0:T(8,128)(2,1)S(1)}, bf16[8,2,448,256]{3,2,1,0:T(8,128)(2,1)S(1)}, u32[]{:S(2)}, u32[]{:S(2)}) collective-permute-start(bf16[8,2,448,256]{3,2,1,0:T(8,128)(2,1)S(1)} %get-tuple-element.76.w_ref), channel_id=1, source_target_pairs={{0,1},{1,0},{2,3},{3,2},{4,5},{5,4},{6,7},{7,6},{8,9},{9,8},{10,11... | collective-permute-start | bytes 11010056 | tf_op jit(solution)/shard_map/ppermute | solution.py:373
  57.7 8.7 %collective-permute-start.15 = (bf16[512,256]{1,0:T(8,128)(2,1)S(1)}, bf16[512,256]{1,0:T(8,128)(2,1)S(1)}, u32[]{:S(2)}, u32[]{:S(2)}) collective-permute-start(bf16[512,256]{1,0:T(8,128)(2,1)S(1)} %get-tuple-element.62.kv_ref), channel_id=1, source_target_pairs={{0,2},{1,3},{2,0},{3,1},{4,6},{5,7},{6,4},{7,5},{8,10},{9,11},{10,... | collective-permute-start | bytes 786440 | tf_op jit(solution)/shard_map/ppermute | solution.py:373
  71.1 6.8 %collective-permute-start.19 = (bf16[256,256]{1,0:T(8,128)(2,1)S(1)}, bf16[256,256]{1,0:T(8,128)(2,1)S(1)}, u32[]{:S(2)}, u32[]{:S(2)}) collective-permute-start(bf16[256,256]{1,0:T(8,128)(2,1)S(1)} %get-tuple-element.75), channel_id=1, source_target_pairs={{0,2},{1,3},{2,0},{3,1},{4,6},{5,7},{6,4},{7,5},{8,10},{9,11},{10,... | collective-permute-start | bytes 393224 | tf_op jit(solution)/shard_map/ppermute | solution.py:373
  71.6 10.2 %collective-permute-start.18 = (f32[256,256]{1,0:T(8,128)S(1)}, f32[256,256]{1,0:T(8,128)S(1)}, u32[]{:S(2)}, u32[]{:S(2)}) collective-permute-start(f32[256,256]{1,0:T(8,128)S(1)} %get-tuple-element.65.refs_0_), channel_id=1, source_target_pairs={{0,2},{1,3},{2,0},{3,1},{4,6},{5,7},{6,4},{7,5},{8,10},{9,11},{10,... | collective-permute-start | bytes 786440 | tf_op jit(solution)/shard_map/ppermute | solution.py:373
  81.9 3.4 %collective-permute-start.20 = (bf16[512,256]{1,0:T(8,128)(2,1)S(1)}, bf16[512,256]{1,0:T(8,128)(2,1)S(1)}, u32[]{:S(2)}, u32[]{:S(2)}) collective-permute-start(bf16[512,256]{1,0:T(8,128)(2,1)S(1)} %pad_maximum_fusion.g_ref.refs_8_), channel_id=1, source_target_pairs={{0,1},{1,0},{2,3},{3,2},{4,5},{5,4},{6,7},{7,6},{8,9},{9,8},{10,11... | collective-permute-start | bytes 786440 | tf_op jit(solution)/shard_map/ppermute | solution.py:373
  83.2 8.1 %collective-permute-start.27 = (bf16[1,448,256]{2,1,0:T(8,128)(2,1)S(1)}, bf16[1,448,256]{2,1,0:T(8,128)(2,1)S(1)}, u32[]{:S(2)}, u32[]{:S(2)}) collective-permute-start(bf16[1,448,256]{2,1,0:T(8,128)(2,1)S(1)} %get-tuple-element.87), channel_id=1, source_target_pairs={{0,4},{8,0},{16,8},{24,16},{28,24},{20,28},{12,20},{4,12},{1,5},{9... | collective-permute-start | bytes 688136 | tf_op jit(solution)/shard_map/ppermute | solution.py:376
  83.7 8.1 %collective-permute-start.23 = (bf16[1,448,256]{2,1,0:T(8,128)(2,1)S(1)}, bf16[1,448,256]{2,1,0:T(8,128)(2,1)S(1)}, u32[]{:S(2)}, u32[]{:S(2)}) collective-permute-start(bf16[1,448,256]{2,1,0:T(8,128)(2,1)S(1)} %get-tuple-element.83), channel_id=1, source_target_pairs={{0,8},{8,16},{16,24},{24,28},{28,20},{20,12},{12,4},{4,0},{1,9},{9... | collective-permute-start | bytes 688136 | tf_op jit(solution)/shard_map/ppermute | solution.py:376
  91.3 12.2 %collective-permute-start.28 = (bf16[2,448,256]{2,1,0:T(8,128)(2,1)S(1)}, bf16[2,448,256]{2,1,0:T(8,128)(2,1)S(1)}, u32[]{:S(2)}, u32[]{:S(2)}) collective-permute-start(bf16[2,448,256]{2,1,0:T(8,128)(2,1)S(1)} %add_convert_fusion.3), channel_id=1, source_target_pairs={{0,4},{8,0},{16,8},{24,16},{28,24},{20,28},{12,20},{4,12},{1,5},{9... | collective-permute-start | bytes 1376264 | tf_op jit(solution)/shard_map/ppermute | solution.py:376
  91.9 12.2 %collective-permute-start.24 = (bf16[2,448,256]{2,1,0:T(8,128)(2,1)S(1)}, bf16[2,448,256]{2,1,0:T(8,128)(2,1)S(1)}, u32[]{:S(2)}, u32[]{:S(2)}) collective-permute-start(bf16[2,448,256]{2,1,0:T(8,128)(2,1)S(1)} %add_convert_fusion.6), channel_id=1, source_target_pairs={{0,8},{8,16},{16,24},{24,28},{28,20},{20,12},{12,4},{4,0},{1,9},{9... | collective-permute-start | bytes 1376264 | tf_op jit(solution)/shard_map/ppermute | solution.py:376
  93.5 12.4 %collective-permute-start.16 = (bf16[2,128,896]{2,1,0:T(8,128)(2,1)S(1)}, bf16[2,128,896]{2,1,0:T(8,128)(2,1)S(1)}, u32[]{:S(2)}, u32[]{:S(2)}) collective-permute-start(bf16[2,128,896]{2,1,0:T(8,128)(2,1)S(1)} %get-tuple-element.67), channel_id=1, source_target_pairs={{0,1},{1,0},{2,3},{3,2},{4,5},{5,4},{6,7},{7,6},{8,9},{9,8},{10,11... | collective-permute-start | bytes 1376264 | tf_op jit(solution)/shard_map/ppermute | solution.py:373
  93.6 12.4 %collective-permute-start.17 = (bf16[2,128,896]{2,1,0:T(8,128)(2,1)S(1)}, bf16[2,128,896]{2,1,0:T(8,128)(2,1)S(1)}, u32[]{:S(2)}, u32[]{:S(2)}) collective-permute-start(bf16[2,128,896]{2,1,0:T(8,128)(2,1)S(1)} %get-tuple-element.69), channel_id=1, source_target_pairs={{0,1},{1,0},{2,3},{3,2},{4,5},{5,4},{6,7},{7,6},{8,9},{9,8},{10,11... | collective-permute-start | bytes 1376264 | tf_op jit(solution)/shard_map/ppermute | solution.py:373
  96.4 22.3 %collective-permute-start.22 = (bf16[128,3584]{1,0:T(8,128)(2,1)S(1)}, bf16[128,3584]{1,0:T(8,128)(2,1)S(1)}, u32[]{:S(2)}, u32[]{:S(2)}) collective-permute-start(bf16[128,3584]{1,0:T(8,128)(2,1)S(1)} %get-tuple-element.78.refs_9_), channel_id=1, source_target_pairs={{0,2},{1,3},{2,0},{3,1},{4,6},{5,7},{6,4},{7,5},{8,10},{9,11},{10,... | collective-permute-start | bytes 2752520 | tf_op jit(solution)/shard_map/ppermute | solution.py:373
  103.7 11.3 %collective-permute-start.29 = (bf16[2,448,256]{2,1,0:T(8,128)(2,1)S(1)}, bf16[2,448,256]{2,1,0:T(8,128)(2,1)S(1)}, u32[]{:S(2)}, u32[]{:S(2)}) collective-permute-start(bf16[2,448,256]{2,1,0:T(8,128)(2,1)S(1)} %add_convert_fusion.2), channel_id=1, source_target_pairs={{0,4},{8,0},{16,8},{24,16},{28,24},{20,28},{12,20},{4,12},{1,5},{9... | collective-permute-start | bytes 1376264 | tf_op jit(solution)/shard_map/ppermute | solution.py:376
  104.3 11.3 %collective-permute-start.25 = (bf16[2,448,256]{2,1,0:T(8,128)(2,1)S(1)}, bf16[2,448,256]{2,1,0:T(8,128)(2,1)S(1)}, u32[]{:S(2)}, u32[]{:S(2)}) collective-permute-start(bf16[2,448,256]{2,1,0:T(8,128)(2,1)S(1)} %add_convert_fusion.5), channel_id=1, source_target_pairs={{0,8},{8,16},{16,24},{24,28},{28,20},{20,12},{12,4},{4,0},{1,9},{9... | collective-permute-start | bytes 1376264 | tf_op jit(solution)/shard_map/ppermute | solution.py:376
  115.1 10.4 %collective-permute-start.30 = (bf16[2,448,256]{2,1,0:T(8,128)(2,1)S(1)}, bf16[2,448,256]{2,1,0:T(8,128)(2,1)S(1)}, u32[]{:S(2)}, u32[]{:S(2)}) collective-permute-start(bf16[2,448,256]{2,1,0:T(8,128)(2,1)S(1)} %add_convert_fusion.1), channel_id=1, source_target_pairs={{0,4},{8,0},{16,8},{24,16},{28,24},{20,28},{12,20},{4,12},{1,5},{9... | collective-permute-start | bytes 1376264 | tf_op jit(solution)/shard_map/ppermute | solution.py:376
  115.7 10.1 %collective-permute-start.26 = (bf16[2,448,256]{2,1,0:T(8,128)(2,1)S(1)}, bf16[2,448,256]{2,1,0:T(8,128)(2,1)S(1)}, u32[]{:S(2)}, u32[]{:S(2)}) collective-permute-start(bf16[2,448,256]{2,1,0:T(8,128)(2,1)S(1)} %add_convert_fusion.4), channel_id=1, source_target_pairs={{0,8},{8,16},{16,24},{24,28},{28,20},{20,12},{12,4},{4,0},{1,9},{9... | collective-permute-start | bytes 1376264 | tf_op jit(solution)/shard_map/ppermute | solution.py:376

commit v14 on v12

--- a/solution.py
+++ b/solution.py
@@ -108,7 +108,7 @@
 def pack_heads(me, queries, upstream):
     rows = queries.shape[0]
     out = [shaped((2, 2, rows, SPAN), BF16)] + [shaped((2, rows, SPAN), BF16)] * 2
-    return call(pack_kernel, me, (queries, upstream), out, 2)
+    return call(pack_kernel, me, (queries, upstream), out, 1)
 
 
 def place_kernel(me_ref, *refs):
@@ -377,8 +377,9 @@
     else:
         weight = lax.all_gather(kv_weight, "fsdp", axis=0)
 
-    blocks = token_blocks(me, tokens, block_ids * 2 + modality, fsdp)
-    across = [swap(x, 2) for x in blocks]
+    marks = block_ids * 2 + modality
+    blocks = token_blocks(me, tokens, marks, fsdp)
+    across = token_blocks(me, swap(tokens, 2), swap(marks, 2), fsdp)
     own, *others = pack_heads(me, queries, cotangent)
     others = [swap(x, 1) for x in others]
     here = hold(me, blocks, (*weights[1:3], *others)) if near_link else blocks

time: 130 us -> 123 us (0.946)
  waiting for transfers between devices: 65.8 us -> 55.8 us
  starting transfers between devices: 26.6 us -> 28.6 us
    ppermute x16, waiting for transfers between devices: 27.2 us -> 19.4 us  [swap(): return lax.ppermute(x, 'seq', [(i, i ^ bit) for i in range(seq)])]
    ppermute x16, waiting for transfers between devices: 38.6 us -> 36.4 us  [turn(): lax.ppermute(x, 'fsdp', [(CYCLE[i], CYCLE[(i + by) % fsdp]) for i in rang...]
    ppermute x16, starting transfers between devices: 9.28 us -> 10.9 us  [swap(): return lax.ppermute(x, 'seq', [(i, i ^ bit) for i in range(seq)])]
    pallas_call x14 -> x15, Pallas kernels: 29.4 us -> 30.3 us  [call(): pl.pallas_call(body, in_specs=[pl.BlockSpec(memory_space=pltpu.SMEM)] + [...]
  transfers between devices with their start and end apart: 32 -> 32, of which waited for: 16 -> 15; matrix products, arithmetic and copies ran while one was open for 2% -> 2% of each run, Pallas kernels for 20% -> 23%
where the time goes in v14:
time: 123 us
  waiting for transfers between devices  55.8 us (45%)
  Pallas kernels  30.3 us (25%)
  starting transfers between devices  28.6 us (23%)
  other arithmetic  3.56 us (3%)
  local copies, waits for them, and re-layouts  3.54 us (3%)
    ppermute x16, waiting for transfers between devices, turn(): lax.ppermute(x, 'fsdp', [(CYCLE[i], CYCLE[(i + by) % fsdp]) for i in rang...  36.4 us
    pallas_call x15, Pallas kernels, call(): pl.pallas_call(body, in_specs=[pl.BlockSpec(memory_space=pltpu.SMEM)] + [...  30.3 us
    ppermute x16, waiting for transfers between devices, swap(): return lax.ppermute(x, 'seq', [(i, i ^ bit) for i in range(seq)])  19.4 us
    ppermute x16, starting transfers between devices, turn(): lax.ppermute(x, 'fsdp', [(CYCLE[i], CYCLE[(i + by) % fsdp]) for i in rang...  17.7 us
    ppermute x16, starting transfers between devices, swap(): return lax.ppermute(x, 'seq', [(i, i ^ bit) for i in range(seq)])  10.9 us
    unnamed x8, local copies, waits for them, and re-layouts  3.54 us
  transfers between devices with their start and end apart: 32, of which 15 were waited for; matrix products, arithmetic and copies ran while one was open for 2% of the time, Pallas kernels for 23%

profile of v14, /device:TPU:0, one launch (start us, length us, event | category | flops | bytes accessed | tf_op | source)
XLA Modules:
  0.0 122.7 jit_solution(8518845512605336088)
XLA Ops:
  0.6 3.1 %collective-permute-start.1 = (bf16[2,448,256]{2,1,0:T(8,128)(2,1)}, bf16[2,448,256]{2,1,0:T(8,128)(2,1)S(1)}, u32[]{:S(2)}, u32[]{:S(2)}) collective-permute-start(bf16[2,448,256]{2,1,0:T(8,128)(2,1)} %refs_8_.1), channel_id=1, source_target_pairs={{0,8},{8,16},{16,24},{24,28},{28,20},{20,12},{12,4},{4,0},{1,9},{9... | collective-permute-start | bytes 1376264 | tf_op jit(solution)/shard_map/ppermute | solution.py:366
  3.7 2.0 %collective-permute-start.6 = (bf16[128,3584]{1,0:T(8,128)(2,1)}, bf16[128,3584]{1,0:T(8,128)(2,1)S(1)}, u32[]{:S(2)}, u32[]{:S(2)}) collective-permute-start(bf16[128,3584]{1,0:T(8,128)(2,1)} %bitcast.11), channel_id=1, source_target_pairs={{0,2},{1,3},{2,0},{3,1},{4,6},{5,7},{6,4},{7,5},{8,10},{9,11},{10,... | collective-permute-start | bytes 2752520 | tf_op jit(solution)/shard_map/ppermute | solution.py:363
  5.8 1.2 copy-done
  6.9 1.2 copy-done.1
  8.1 0.7 shard_map.93
  9.4 0.7 multiply_add_fusion.ids_ref
  10.1 1.2 copy-done.2
  11.2 0.9 shard_map.94
  12.1 2.2 %collective-permute-done.1.refs_2_.refs_9_ = bf16[2,448,256]{2,1,0:T(8,128)(2,1)S(1)} collective-permute-done((bf16[2,448,256]{2,1,0:T(8,128)(2,1)}, bf16[2,448,256]{2,1,0:T(8,128)(2,1)S(1)}, u32[]{:S(2)}, u32[]{:S(2)}) %collective-permute-start.1) | collective-permute-done | bytes 458784 | tf_op jit(solution)/shard_map/ppermute | solution.py:366
  14.4 1.8 %collective-permute-start.10 = (bf16[2,448,256]{2,1,0:T(8,128)(2,1)S(1)}, bf16[2,448,256]{2,1,0:T(8,128)(2,1)S(1)}, u32[]{:S(2)}, u32[]{:S(2)}) collective-permute-start(bf16[2,448,256]{2,1,0:T(8,128)(2,1)S(1)} %collective-permute-done.1.refs_2_.refs_9_), channel_id=1, source_target_pairs={{0,8},{8,16},{16,24},{24,28},{28,20},{20,12},{12,4},{4,0},{1,9},{9... | collective-permute-start | bytes 1376264 | tf_op jit(solution)/shard_map/ppermute | solution.py:366
  16.2 0.6 shard_map.95
  17.1 1.8 %collective-permute-start.7 = (s32[1,128]{1,0:T(1,128)S(1)}, s32[1,128]{1,0:T(1,128)S(1)}, u32[]{:S(2)}, u32[]{:S(2)}) collective-permute-start(s32[1,128]{1,0:T(1,128)S(1)} %multiply_add_fusion.ids_ref), channel_id=1, source_target_pairs={{0,2},{1,3},{2,0},{3,1},{4,6},{5,7},{6,4},{7,5},{8,10},{9,11},{10,... | collective-permute-start | bytes 1544 | tf_op jit(solution)/shard_map/ppermute | solution.py:363
  18.9 6.9 %collective-permute-done.7.ids_ref = s32[1,128]{1,0:T(1,128)S(1)} collective-permute-done((s32[1,128]{1,0:T(1,128)S(1)}, s32[1,128]{1,0:T(1,128)S(1)}, u32[]{:S(2)}, u32[]{:S(2)}) %collective-permute-start.7) | collective-permute-done | bytes 544 | tf_op jit(solution)/shard_map/ppermute | solution.py:363
  25.8 0.9 shard_map.96
  26.7 0.6 collective-permute-start.8
  27.4 2.4 %collective-permute-done.12.refs_12_ = bf16[2,448,256]{2,1,0:T(8,128)(2,1)S(1)} collective-permute-done((bf16[2,448,256]{2,1,0:T(8,128)(2,1)S(1)}, bf16[2,448,256]{2,1,0:T(8,128)(2,1)S(1)}, u32[]{:S(2)}, u32[]{:S(2)}) %collective-permute-start.12) | collective-permute-done | bytes 458784 | tf_op jit(solution)/shard_map/ppermute | solution.py:366
  29.8 1.6 %collective-permute-start.11 = (bf16[2,448,256]{2,1,0:T(8,128)(2,1)S(1)}, bf16[2,448,256]{2,1,0:T(8,128)(2,1)S(1)}, u32[]{:S(2)}, u32[]{:S(2)}) collective-permute-start(bf16[2,448,256]{2,1,0:T(8,128)(2,1)S(1)} %collective-permute-done.10.refs_11_), channel_id=1, source_target_pairs={{0,8},{8,16},{16,24},{24,28},{28,20},{20,12},{12,4},{4,0},{1,9},{9... | collective-permute-start | bytes 1376264 | tf_op jit(solution)/shard_map/ppermute | solution.py:366
  31.9 3.5 %shard_map.97 = (f32[512,512]{1,0:T(8,128)S(1)}, bf16[8,2,448,256]{3,2,1,0:T(8,128)(2,1)S(1)}) custom-call(s32[2]{0:T(128)S(1)} %pad_add_fusion.me_ref, bf16[8,64,512]{2,1,0:T(8,128)(2,1)S(1)} %get-tuple-element.50.refs_0_, bf16[8,64,512]{2,1,0:T(8,128)(2,1)S(1)} %get-tuple-element.51.refs_1_, bf16[8,64,512]{2,1,0:T(8,128)(2,1)S(1)} %collective-permute-done.4.refs_2_, ...), custom_call_target="tpu_custom_call" | custom-call | bytes 3000000 | tf_op jit(solution)/shard_map/pallas_call | solution.py:36
  35.4 6.5 %collective-permute-done.11.ups_ref.refs_8_ = bf16[2,448,256]{2,1,0:T(8,128)(2,1)S(1)} collective-permute-done((bf16[2,448,256]{2,1,0:T(8,128)(2,1)S(1)}, bf16[2,448,256]{2,1,0:T(8,128)(2,1)S(1)}, u32[]{:S(2)}, u32[]{:S(2)}) %collective-permute-start.11) | collective-permute-done | bytes 458784 | tf_op jit(solution)/shard_map/ppermute | solution.py:366
  41.9 1.3 %collective-permute-done.13.downs_ref.refs_9_ = bf16[2,448,256]{2,1,0:T(8,128)(2,1)S(1)} collective-permute-done((bf16[2,448,256]{2,1,0:T(8,128)(2,1)S(1)}, bf16[2,448,256]{2,1,0:T(8,128)(2,1)S(1)}, u32[]{:S(2)}, u32[]{:S(2)}) %collective-permute-start.13) | collective-permute-done | bytes 458784 | tf_op jit(solution)/shard_map/ppermute | solution.py:366
  43.8 1.6 %collective-permute-start.14 = (bf16[1,448,256]{2,1,0:T(8,128)(2,1)S(1)}, bf16[1,448,256]{2,1,0:T(8,128)(2,1)S(1)}, u32[]{:S(2)}, u32[]{:S(2)}) collective-permute-start(bf16[1,448,256]{2,1,0:T(8,128)(2,1)S(1)} %get-tuple-element.55), channel_id=1, source_target_pairs={{0,8},{8,16},{16,24},{24,28},{28,20},{20,12},{12,4},{4,0},{1,9},{9... | collective-permute-start | bytes 688136 | tf_op jit(solution)/shard_map/ppermute | solution.py:366
  45.9 1.8 %shard_map.99 = (f32[512,512]{1,0:T(8,128)S(1)}, bf16[8,2,448,256]{3,2,1,0:T(8,128)(2,1)S(1)}) custom-call(s32[2]{0:T(128)S(1)} %pad_add_fusion.me_ref, bf16[8,64,512]{2,1,0:T(8,128)(2,1)S(1)} %get-tuple-element.50.refs_0_, bf16[8,64,512]{2,1,0:T(8,128)(2,1)S(1)} %get-tuple-element.51.refs_1_, ...), custom_call_target="tpu_custom_call", output_to_operand_aliasing={{1}: (12, {})} | custom-call | bytes 3000000 | tf_op jit(solution)/shard_map/pallas_call | solution.py:36
  47.7 2.2 %collective-permute-done.14.refs_8_ = bf16[1,448,256]{2,1,0:T(8,128)(2,1)S(1)} collective-permute-done((bf16[1,448,256]{2,1,0:T(8,128)(2,1)S(1)}, bf16[1,448,256]{2,1,0:T(8,128)(2,1)S(1)}, u32[]{:S(2)}, u32[]{:S(2)}) %collective-permute-start.14) | collective-permute-done | bytes 229408 | tf_op jit(solution)/shard_map/ppermute | solution.py:366
  49.8 1.6 %collective-permute-done.15.refs_9_ = bf16[1,448,256]{2,1,0:T(8,128)(2,1)S(1)} collective-permute-done((bf16[1,448,256]{2,1,0:T(8,128)(2,1)S(1)}, bf16[1,448,256]{2,1,0:T(8,128)(2,1)S(1)}, u32[]{:S(2)}, u32[]{:S(2)}) %collective-permute-start.15) | collective-permute-done | bytes 229408 | tf_op jit(solution)/shard_map/ppermute | solution.py:366
  51.4 2.0 %shard_map.100 = (bf16[512,256]{1,0:T(8,128)(2,1)S(1)}, f32[512,1]{1,0:T(8,128)S(1)}, f32[512,1]{1,0:T(8,128)S(1)}, f32[1,512]{1,0:T(1,128)S(1)}, bf16[8,2,448,256]{3,2,1,0:T(8,128)(2,1)S(1)}) custom-call(s32[2]{0:T(128)S(1)} %pad_add_fusion.me_ref, bf16[8,64,512]{2,1,0:T(8,128)(2,1)S(1)} %get-tuple-element.50.refs_0_, ...), custom_call_target="tpu_custom_call", output_to_operand_aliasing={{4}: (12, {})} | custom-call | bytes 3000000 | tf_op jit(solution)/shard_map/pallas_call | solution.py:36
  53.6 1.6 %collective-permute-start.16 = (bf16[512,256]{1,0:T(8,128)(2,1)S(1)}, bf16[512,256]{1,0:T(8,128)(2,1)S(1)}, u32[]{:S(2)}, u32[]{:S(2)}) collective-permute-start(bf16[512,256]{1,0:T(8,128)(2,1)S(1)} %get-tuple-element.60.kv_ref), channel_id=1, source_target_pairs={{0,2},{1,3},{2,0},{3,1},{4,6},{5,7},{6,4},{7,5},{8,10},{9,11},{10,... | collective-permute-start | bytes 786440 | tf_op jit(solution)/shard_map/ppermute | solution.py:363
  55.1 7.2 %collective-permute-done.16.kv_ref = bf16[512,256]{1,0:T(8,128)(2,1)S(1)} collective-permute-done((bf16[512,256]{1,0:T(8,128)(2,1)S(1)}, bf16[512,256]{1,0:T(8,128)(2,1)S(1)}, u32[]{:S(2)}, u32[]{:S(2)}) %collective-permute-start.16) | collective-permute-done | bytes 262176 | tf_op jit(solution)/shard_map/ppermute | solution.py:363
  62.3 4.7 %shard_map.101 = (bf16[2,128,896]{2,1,0:T(8,128)(2,1)S(1)}, bf16[2,128,896]{2,1,0:T(8,128)(2,1)S(1)}, f32[256,256]{1,0:T(8,128)S(1)}, bf16[256,256]{1,0:T(8,128)(2,1)S(1)}) custom-call(s32[2]{0:T(128)S(1)} %pad_add_fusion.me_ref, bf16[2,2,128,896]{3,2,1,0:T(8,128)(2,1)S(1)} %get-tuple-element.45.own_ref, ...), custom_call_target="tpu_custom_call" | custom-call | bytes 18000000 | tf_op jit(solution)/shard_map/pallas_call | solution.py:36
  67.0 1.6 %collective-permute-start.20 = (bf16[256,256]{1,0:T(8,128)(2,1)S(1)}, bf16[256,256]{1,0:T(8,128)(2,1)S(1)}, u32[]{:S(2)}, u32[]{:S(2)}) collective-permute-start(bf16[256,256]{1,0:T(8,128)(2,1)S(1)} %get-tuple-element.73), channel_id=1, source_target_pairs={{0,2},{1,3},{2,0},{3,1},{4,6},{5,7},{6,4},{7,5},{8,10},{9,11},{10,... | collective-permute-start | bytes 393224 | tf_op jit(solution)/shard_map/ppermute | solution.py:363
  69.0 4.7 %shard_map.102 = (bf16[2,128,896]{2,1,0:T(8,128)(2,1)S(1)}, bf16[2,128,896]{2,1,0:T(8,128)(2,1)S(1)}, f32[256,256]{1,0:T(8,128)S(1)}, f32[256,256]{1,0:T(8,128)S(1)}) custom-call(s32[2]{0:T(128)S(1)} %pad_add_fusion.me_ref, bf16[2,2,128,896]{3,2,1,0:T(8,128)(2,1)S(1)} %get-tuple-element.45.own_ref, ...), custom_call_target="tpu_custom_call" | custom-call | bytes 18000000 | tf_op jit(solution)/shard_map/pallas_call | solution.py:36
  73.8 3.9 %collective-permute-done.19 = f32[256,256]{1,0:T(8,128)S(1)} collective-permute-done((f32[256,256]{1,0:T(8,128)S(1)}, f32[256,256]{1,0:T(8,128)S(1)}, u32[]{:S(2)}, u32[]{:S(2)}) %collective-permute-start.19) | collective-permute-done | bytes 262176 | tf_op jit(solution)/shard_map/ppermute | solution.py:363
  77.8 1.3 %shard_map.107 = (bf16[1,448,256]{2,1,0:T(8,128)(2,1)S(1)}, bf16[1,448,256]{2,1,0:T(8,128)(2,1)S(1)}) custom-call(s32[2]{0:T(128)S(1)} %pad_add_fusion.me_ref, bf16[8,64,512]{2,1,0:T(8,128)(2,1)S(1)} %get-tuple-element.50.refs_0_, bf16[8,64,512]{2,1,0:T(8,128)(2,1)S(1)} %get-tuple-element.51.refs_1_, bf16[8,64,512]{2,1,0:T(8,128)(2,1)S(1)} %collective-permute-done.4.refs_2_, ...), custom_call_target="tpu_custom_call" | custom-call | bytes 6000000 | tf_op jit(solution)/shard_map/pallas_call | solution.py:36
  79.6 1.6 %collective-permute-start.24 = (bf16[1,448,256]{2,1,0:T(8,128)(2,1)S(1)}, bf16[1,448,256]{2,1,0:T(8,128)(2,1)S(1)}, u32[]{:S(2)}, u32[]{:S(2)}) collective-permute-start(bf16[1,448,256]{2,1,0:T(8,128)(2,1)S(1)} %get-tuple-element.81), channel_id=1, source_target_pairs={{0,8},{8,16},{16,24},{24,28},{28,20},{20,12},{12,4},{4,0},{1,9},{9... | collective-permute-start | bytes 688136 | tf_op jit(solution)/shard_map/ppermute | solution.py:366
  81.2 2.9 %shard_map.104 = (f32[128,3584]{1,0:T(8,128)S(1)}, bf16[128,3584]{1,0:T(8,128)(2,1)S(1)}) custom-call(s32[2]{0:T(128)S(1)} %pad_add_fusion.me_ref, f32[512,1]{1,0:T(8,128)S(1)} %get-tuple-element.70.kind_ref, bf16[512,256]{1,0:T(8,128)(2,1)S(1)} %pad_maximum_fusion.g_ref.refs_8_, bf16[512,256]{1,0:T(8,128)(2,1)S(1)} %collective-permute-done.21.gc_ref, ...), custom_call_target="tpu_custom_call" | custom-call | bytes 21000000 | tf_op jit(solution)/shard_map/pallas_call | solution.py:36
  84.1 1.5 %shard_map.106 = (f32[2,448,256]{2,1,0:T(8,128)S(1)}, f32[2,448,256]{2,1,0:T(8,128)S(1)}) custom-call(s32[2]{0:T(128)S(1)} %pad_add_fusion.me_ref, bf16[8,64,512]{2,1,0:T(8,128)(2,1)S(1)} %get-tuple-element.50.refs_0_, bf16[8,64,512]{2,1,0:T(8,128)(2,1)S(1)} %get-tuple-element.51.refs_1_, bf16[8,64,512]{2,1,0:T(8,128)(2,1)S(1)} %collective-permute-done.4.refs_2_, ...), custom_call_target="tpu_custom_call" | custom-call | bytes 9000000 | tf_op jit(solution)/shard_map/pallas_call | solution.py:36
  85.7 1.5 %collective-permute-done.28 = bf16[1,448,256]{2,1,0:T(8,128)(2,1)S(1)} collective-permute-done((bf16[1,448,256]{2,1,0:T(8,128)(2,1)S(1)}, bf16[1,448,256]{2,1,0:T(8,128)(2,1)S(1)}, u32[]{:S(2)}, u32[]{:S(2)}) %collective-permute-start.28) | collective-permute-done | bytes 229408 | tf_op jit(solution)/shard_map/ppermute | solution.py:366
  87.8 1.6 %collective-permute-start.25 = (bf16[2,448,256]{2,1,0:T(8,128)(2,1)S(1)}, bf16[2,448,256]{2,1,0:T(8,128)(2,1)S(1)}, u32[]{:S(2)}, u32[]{:S(2)}) collective-permute-start(bf16[2,448,256]{2,1,0:T(8,128)(2,1)S(1)} %add_convert_fusion.6), channel_id=1, source_target_pairs={{0,8},{8,16},{16,24},{24,28},{28,20},{20,12},{12,4},{4,0},{1,9},{9... | collective-permute-start | bytes 1376264 | tf_op jit(solution)/shard_map/ppermute | solution.py:366
  89.9 2.3 %shard_map.105 = (f32[2,448,256]{2,1,0:T(8,128)S(1)}, f32[2,448,256]{2,1,0:T(8,128)S(1)}, f32[2,448,256]{2,1,0:T(8,128)S(1)}, f32[2,448,256]{2,1,0:T(8,128)S(1)}, f32[2,448,256]{2,1,0:T(8,128)S(1)}) custom-call(s32[2]{0:T(128)S(1)} %pad_add_fusion.me_ref, bf16[8,64,512]{2,1,0:T(8,128)(2,1)S(1)} %get-tuple-element.50.refs_0_, ...), custom_call_target="tpu_custom_call" | custom-call | bytes 18000000 | tf_op jit(solution)/shard_map/pallas_call | solution.py:36
  92.3 1.6 %collective-permute-start.23 = (bf16[128,3584]{1,0:T(8,128)(2,1)S(1)}, bf16[128,3584]{1,0:T(8,128)(2,1)S(1)}, u32[]{:S(2)}, u32[]{:S(2)}) collective-permute-start(bf16[128,3584]{1,0:T(8,128)(2,1)S(1)} %get-tuple-element.76.refs_9_), channel_id=1, source_target_pairs={{0,2},{1,3},{2,0},{3,1},{4,6},{5,7},{6,4},{7,5},{8,10},{9,11},{10,... | collective-permute-start | bytes 2752520 | tf_op jit(solution)/shard_map/ppermute | solution.py:363
  93.9 5.6 %collective-permute-done.29 = bf16[2,448,256]{2,1,0:T(8,128)(2,1)S(1)} collective-permute-done((bf16[2,448,256]{2,1,0:T(8,128)(2,1)S(1)}, bf16[2,448,256]{2,1,0:T(8,128)(2,1)S(1)}, u32[]{:S(2)}, u32[]{:S(2)}) %collective-permute-start.29) | collective-permute-done | bytes 458784 | tf_op jit(solution)/shard_map/ppermute | solution.py:366
  100.1 1.6 %collective-permute-start.26 = (bf16[2,448,256]{2,1,0:T(8,128)(2,1)S(1)}, bf16[2,448,256]{2,1,0:T(8,128)(2,1)S(1)}, u32[]{:S(2)}, u32[]{:S(2)}) collective-permute-start(bf16[2,448,256]{2,1,0:T(8,128)(2,1)S(1)} %add_convert_fusion.5), channel_id=1, source_target_pairs={{0,8},{8,16},{16,24},{24,28},{28,20},{20,12},{12,4},{4,0},{1,9},{9... | collective-permute-start | bytes 1376264 | tf_op jit(solution)/shard_map/ppermute | solution.py:366
  101.8 1.9 %shard_map.103 = (bf16[128,3584]{1,0:T(8,128)(2,1)}, bf16[128,3584]{1,0:T(8,128)(2,1)}) custom-call(s32[2]{0:T(128)S(1)} %pad_add_fusion.me_ref, bf16[2,128,896]{2,1,0:T(8,128)(2,1)S(1)} %get-tuple-element.64.refs_0_, bf16[2,128,896]{2,1,0:T(8,128)(2,1)S(1)} %collective-permute-done.17.refs_1_, bf16[2,128,896]{2,1,0:T(8,128)(2,1)S(1)} %get-tuple-element.66.refs_2_, ...), custom_call_target="tpu_custom_call" | custom-call | bytes 9000000 | tf_op jit(solution)/shard_map/pallas_call | solution.py:36
  103.7 7.1 %collective-permute-done.30 = bf16[2,448,256]{2,1,0:T(8,128)(2,1)S(1)} collective-permute-done((bf16[2,448,256]{2,1,0:T(8,128)(2,1)S(1)}, bf16[2,448,256]{2,1,0:T(8,128)(2,1)S(1)}, u32[]{:S(2)}, u32[]{:S(2)}) %collective-permute-start.30) | collective-permute-done | bytes 458784 | tf_op jit(solution)/shard_map/ppermute | solution.py:366
  111.6 1.7 %collective-permute-start.27 = (bf16[2,448,256]{2,1,0:T(8,128)(2,1)S(1)}, bf16[2,448,256]{2,1,0:T(8,128)(2,1)S(1)}, u32[]{:S(2)}, u32[]{:S(2)}) collective-permute-start(bf16[2,448,256]{2,1,0:T(8,128)(2,1)S(1)} %add_convert_fusion.4), channel_id=1, source_target_pairs={{0,8},{8,16},{16,24},{24,28},{28,20},{20,12},{12,4},{4,0},{1,9},{9... | collective-permute-start | bytes 1376264 | tf_op jit(solution)/shard_map/ppermute | solution.py:366
  113.2 1.4 %collective-permute-done.23 = bf16[128,3584]{1,0:T(8,128)(2,1)S(1)} collective-permute-done((bf16[128,3584]{1,0:T(8,128)(2,1)S(1)}, bf16[128,3584]{1,0:T(8,128)(2,1)S(1)}, u32[]{:S(2)}, u32[]{:S(2)}) %collective-permute-start.23) | collective-permute-done | bytes 917536 | tf_op jit(solution)/shard_map/ppermute | solution.py:363
  114.6 1.1 fusion
  115.7 5.6 %collective-permute-done.31 = bf16[2,448,256]{2,1,0:T(8,128)(2,1)S(1)} collective-permute-done((bf16[2,448,256]{2,1,0:T(8,128)(2,1)S(1)}, bf16[2,448,256]{2,1,0:T(8,128)(2,1)S(1)}, u32[]{:S(2)}, u32[]{:S(2)}) %collective-permute-start.31) | collective-permute-done | bytes 458784 | tf_op jit(solution)/shard_map/ppermute | solution.py:366
  121.7 1.0 convert_add_fusion
  (52 shorter events, 6.7 us)
Async XLA Ops:
  0.6 13.7 %collective-permute-start.1 = (bf16[2,448,256]{2,1,0:T(8,128)(2,1)}, bf16[2,448,256]{2,1,0:T(8,128)(2,1)S(1)}, u32[]{:S(2)}, u32[]{:S(2)}) collective-permute-start(bf16[2,448,256]{2,1,0:T(8,128)(2,1)} %refs_8_.1), channel_id=1, source_target_pairs={{0,8},{8,16},{16,24},{24,28},{28,20},{20,12},{12,4},{4,0},{1,9},{9... | collective-permute-start | bytes 1376264 | tf_op jit(solution)/shard_map/ppermute | solution.py:366
  3.7 12.5 %collective-permute-start.2 = (bf16[2,448,256]{2,1,0:T(8,128)(2,1)}, bf16[2,448,256]{2,1,0:T(8,128)(2,1)S(1)}, u32[]{:S(2)}, u32[]{:S(2)}) collective-permute-start(bf16[2,448,256]{2,1,0:T(8,128)(2,1)} %refs_8_.1), channel_id=1, source_target_pairs={{0,4},{8,0},{16,8},{24,16},{28,24},{20,28},{12,20},{4,12},{1,5},{9... | collective-permute-start | bytes 1376264 | tf_op jit(solution)/shard_map/ppermute | solution.py:366
  3.7 22.1 %collective-permute-start.6 = (bf16[128,3584]{1,0:T(8,128)(2,1)}, bf16[128,3584]{1,0:T(8,128)(2,1)S(1)}, u32[]{:S(2)}, u32[]{:S(2)}) collective-permute-start(bf16[128,3584]{1,0:T(8,128)(2,1)} %bitcast.11), channel_id=1, source_target_pairs={{0,2},{1,3},{2,0},{3,1},{4,6},{5,7},{6,4},{7,5},{8,10},{9,11},{10,... | collective-permute-start | bytes 2752520 | tf_op jit(solution)/shard_map/ppermute | solution.py:363
  5.8 1.2 copy-start
  6.9 1.2 copy-start.1
  8.1 23.7 %copy-start.3 = (bf16[2,448,256]{2,1,0:T(8,128)(2,1)S(1)}, bf16[2,448,256]{2,1,0:T(8,128)(2,1)}, u32[]{:S(2)}) copy-start(bf16[2,448,256]{2,1,0:T(8,128)(2,1)} %refs_8_.1) | copy-start | bytes 1376260
  8.8 7.4 %collective-permute-start = (bf16[2,128,896]{2,1,0:T(8,128)(2,1)S(1)}, bf16[2,128,896]{2,1,0:T(8,128)(2,1)S(1)}, u32[]{:S(2)}, u32[]{:S(2)}) collective-permute-start(bf16[2,128,896]{2,1,0:T(8,128)(2,1)S(1)} %get-tuple-element.46), channel_id=1, source_target_pairs={{0,1},{1,0},{2,3},{3,2},{4,5},{5,4},{6,7},{7,6},{8,9},{9,8},{10,11... | collective-permute-start | bytes 1376264 | tf_op jit(solution)/shard_map/ppermute | solution.py:363
  8.9 7.3 %collective-permute-start.3 = (bf16[2,128,896]{2,1,0:T(8,128)(2,1)S(1)}, bf16[2,128,896]{2,1,0:T(8,128)(2,1)S(1)}, u32[]{:S(2)}, u32[]{:S(2)}) collective-permute-start(bf16[2,128,896]{2,1,0:T(8,128)(2,1)S(1)} %get-tuple-element.49), channel_id=1, source_target_pairs={{0,1},{1,0},{2,3},{3,2},{4,5},{5,4},{6,7},{7,6},{8,9},{9,8},{10,11... | collective-permute-start | bytes 1376264 | tf_op jit(solution)/shard_map/ppermute | solution.py:363
  10.1 1.2 copy-start.2
  14.4 12.9 %collective-permute-start.10 = (bf16[2,448,256]{2,1,0:T(8,128)(2,1)S(1)}, bf16[2,448,256]{2,1,0:T(8,128)(2,1)S(1)}, u32[]{:S(2)}, u32[]{:S(2)}) collective-permute-start(bf16[2,448,256]{2,1,0:T(8,128)(2,1)S(1)} %collective-permute-done.1.refs_2_.refs_9_), channel_id=1, source_target_pairs={{0,8},{8,16},{16,24},{24,28},{28,20},{20,12},{12,4},{4,0},{1,9},{9... | collective-permute-start | bytes 1376264 | tf_op jit(solution)/shard_map/ppermute | solution.py:366
  16.8 14.6 %collective-permute-start.4 = (bf16[8,64,512]{2,1,0:T(8,128)(2,1)S(1)}, bf16[8,64,512]{2,1,0:T(8,128)(2,1)S(1)}, u32[]{:S(2)}, u32[]{:S(2)}) collective-permute-start(bf16[8,64,512]{2,1,0:T(8,128)(2,1)S(1)} %get-tuple-element.50.refs_0_), channel_id=1, source_target_pairs={{0,1},{1,0},{2,3},{3,2},{4,5},{5,4},{6,7},{7,6},{8,9},{9,8},{10,11... | collective-permute-start | bytes 1572872 | tf_op jit(solution)/shard_map/ppermute | solution.py:363
  16.9 12.9 %collective-permute-start.12 = (bf16[2,448,256]{2,1,0:T(8,128)(2,1)S(1)}, bf16[2,448,256]{2,1,0:T(8,128)(2,1)S(1)}, u32[]{:S(2)}, u32[]{:S(2)}) collective-permute-start(bf16[2,448,256]{2,1,0:T(8,128)(2,1)S(1)} %collective-permute-done.2.refs_3_.refs_10_), channel_id=1, source_target_pairs={{0,4},{8,0},{16,8},{24,16},{28,24},{20,28},{12,20},{4,12},{1,5},{9... | collective-permute-start | bytes 1376264 | tf_op jit(solution)/shard_map/ppermute | solution.py:366
  17.1 8.7 %collective-permute-start.7 = (s32[1,128]{1,0:T(1,128)S(1)}, s32[1,128]{1,0:T(1,128)S(1)}, u32[]{:S(2)}, u32[]{:S(2)}) collective-permute-start(s32[1,128]{1,0:T(1,128)S(1)} %multiply_add_fusion.ids_ref), channel_id=1, source_target_pairs={{0,2},{1,3},{2,0},{3,1},{4,6},{5,7},{6,4},{7,5},{8,10},{9,11},{10,... | collective-permute-start | bytes 1544 | tf_op jit(solution)/shard_map/ppermute | solution.py:363
  25.8 6.0 %collective-permute-start.5 = (bf16[8,64,512]{2,1,0:T(8,128)(2,1)S(1)}, bf16[8,64,512]{2,1,0:T(8,128)(2,1)S(1)}, u32[]{:S(2)}, u32[]{:S(2)}) collective-permute-start(bf16[8,64,512]{2,1,0:T(8,128)(2,1)S(1)} %get-tuple-element.51.refs_1_), channel_id=1, source_target_pairs={{0,1},{1,0},{2,3},{3,2},{4,5},{5,4},{6,7},{7,6},{8,9},{9,8},{10,11... | collective-permute-start | bytes 1572872 | tf_op jit(solution)/shard_map/ppermute | solution.py:363
  26.7 5.1 %collective-permute-start.8 = (bf16[8,64,512]{2,1,0:T(8,128)(2,1)S(1)}, bf16[8,64,512]{2,1,0:T(8,128)(2,1)S(1)}, u32[]{:S(2)}, u32[]{:S(2)}) collective-permute-start(bf16[8,64,512]{2,1,0:T(8,128)(2,1)S(1)} %get-tuple-element.52.refs_4_), channel_id=1, source_target_pairs={{0,1},{1,0},{2,3},{3,2},{4,5},{5,4},{6,7},{7,6},{8,9},{9,8},{10,11... | collective-permute-start | bytes 1572872 | tf_op jit(solution)/shard_map/ppermute | solution.py:363
  27.3 4.6 %collective-permute-start.9 = (bf16[8,64,512]{2,1,0:T(8,128)(2,1)S(1)}, bf16[8,64,512]{2,1,0:T(8,128)(2,1)S(1)}, u32[]{:S(2)}, u32[]{:S(2)}) collective-permute-start(bf16[8,64,512]{2,1,0:T(8,128)(2,1)S(1)} %get-tuple-element.53.refs_5_), channel_id=1, source_target_pairs={{0,1},{1,0},{2,3},{3,2},{4,5},{5,4},{6,7},{7,6},{8,9},{9,8},{10,11... | collective-permute-start | bytes 1572872 | tf_op jit(solution)/shard_map/ppermute | solution.py:363
  29.8 12.1 %collective-permute-start.11 = (bf16[2,448,256]{2,1,0:T(8,128)(2,1)S(1)}, bf16[2,448,256]{2,1,0:T(8,128)(2,1)S(1)}, u32[]{:S(2)}, u32[]{:S(2)}) collective-permute-start(bf16[2,448,256]{2,1,0:T(8,128)(2,1)S(1)} %collective-permute-done.10.refs_11_), channel_id=1, source_target_pairs={{0,8},{8,16},{16,24},{24,28},{28,20},{20,12},{12,4},{4,0},{1,9},{9... | collective-permute-start | bytes 1376264 | tf_op jit(solution)/shard_map/ppermute | solution.py:366
  31.4 11.8 %collective-permute-start.13 = (bf16[2,448,256]{2,1,0:T(8,128)(2,1)S(1)}, bf16[2,448,256]{2,1,0:T(8,128)(2,1)S(1)}, u32[]{:S(2)}, u32[]{:S(2)}) collective-permute-start(bf16[2,448,256]{2,1,0:T(8,128)(2,1)S(1)} %collective-permute-done.12.refs_12_), channel_id=1, source_target_pairs={{0,4},{8,0},{16,8},{24,16},{28,24},{20,28},{12,20},{4,12},{1,5},{9... | collective-permute-start | bytes 1376264 | tf_op jit(solution)/shard_map/ppermute | solution.py:366
  43.8 6.1 %collective-permute-start.14 = (bf16[1,448,256]{2,1,0:T(8,128)(2,1)S(1)}, bf16[1,448,256]{2,1,0:T(8,128)(2,1)S(1)}, u32[]{:S(2)}, u32[]{:S(2)}) collective-permute-start(bf16[1,448,256]{2,1,0:T(8,128)(2,1)S(1)} %get-tuple-element.55), channel_id=1, source_target_pairs={{0,8},{8,16},{16,24},{24,28},{28,20},{20,12},{12,4},{4,0},{1,9},{9... | collective-permute-start | bytes 688136 | tf_op jit(solution)/shard_map/ppermute | solution.py:366
  45.4 6.0 %collective-permute-start.15 = (bf16[1,448,256]{2,1,0:T(8,128)(2,1)S(1)}, bf16[1,448,256]{2,1,0:T(8,128)(2,1)S(1)}, u32[]{:S(2)}, u32[]{:S(2)}) collective-permute-start(bf16[1,448,256]{2,1,0:T(8,128)(2,1)S(1)} %get-tuple-element.56), channel_id=1, source_target_pairs={{0,4},{8,0},{16,8},{24,16},{28,24},{20,28},{12,20},{4,12},{1,5},{9... | collective-permute-start | bytes 688136 | tf_op jit(solution)/shard_map/ppermute | solution.py:366
  53.5 27.7 %collective-permute-start.22 = (bf16[8,2,448,256]{3,2,1,0:T(8,128)(2,1)S(1)}, bf16[8,2,448,256]{3,2,1,0:T(8,128)(2,1)S(1)}, u32[]{:S(2)}, u32[]{:S(2)}) collective-permute-start(bf16[8,2,448,256]{3,2,1,0:T(8,128)(2,1)S(1)} %get-tuple-element.74.w_ref), channel_id=1, source_target_pairs={{0,1},{1,0},{2,3},{3,2},{4,5},{5,4},{6,7},{7,6},{8,9},{9,8},{10,11... | collective-permute-start | bytes 11010056 | tf_op jit(solution)/shard_map/ppermute | solution.py:363
  53.6 8.7 %collective-permute-start.16 = (bf16[512,256]{1,0:T(8,128)(2,1)S(1)}, bf16[512,256]{1,0:T(8,128)(2,1)S(1)}, u32[]{:S(2)}, u32[]{:S(2)}) collective-permute-start(bf16[512,256]{1,0:T(8,128)(2,1)S(1)} %get-tuple-element.60.kv_ref), channel_id=1, source_target_pairs={{0,2},{1,3},{2,0},{3,1},{4,6},{5,7},{6,4},{7,5},{8,10},{9,11},{10,... | collective-permute-start | bytes 786440 | tf_op jit(solution)/shard_map/ppermute | solution.py:363
  67.0 6.8 %collective-permute-start.20 = (bf16[256,256]{1,0:T(8,128)(2,1)S(1)}, bf16[256,256]{1,0:T(8,128)(2,1)S(1)}, u32[]{:S(2)}, u32[]{:S(2)}) collective-permute-start(bf16[256,256]{1,0:T(8,128)(2,1)S(1)} %get-tuple-element.73), channel_id=1, source_target_pairs={{0,2},{1,3},{2,0},{3,1},{4,6},{5,7},{6,4},{7,5},{8,10},{9,11},{10,... | collective-permute-start | bytes 393224 | tf_op jit(solution)/shard_map/ppermute | solution.py:363
  68.5 9.2 %collective-permute-start.19 = (f32[256,256]{1,0:T(8,128)S(1)}, f32[256,256]{1,0:T(8,128)S(1)}, u32[]{:S(2)}, u32[]{:S(2)}) collective-permute-start(f32[256,256]{1,0:T(8,128)S(1)} %get-tuple-element.63.refs_0_), channel_id=1, source_target_pairs={{0,2},{1,3},{2,0},{3,1},{4,6},{5,7},{6,4},{7,5},{8,10},{9,11},{10,... | collective-permute-start | bytes 786440 | tf_op jit(solution)/shard_map/ppermute | solution.py:363
  77.8 3.4 %collective-permute-start.21 = (bf16[512,256]{1,0:T(8,128)(2,1)S(1)}, bf16[512,256]{1,0:T(8,128)(2,1)S(1)}, u32[]{:S(2)}, u32[]{:S(2)}) collective-permute-start(bf16[512,256]{1,0:T(8,128)(2,1)S(1)} %pad_maximum_fusion.g_ref.refs_8_), channel_id=1, source_target_pairs={{0,1},{1,0},{2,3},{3,2},{4,5},{5,4},{6,7},{7,6},{8,9},{9,8},{10,11... | collective-permute-start | bytes 786440 | tf_op jit(solution)/shard_map/ppermute | solution.py:363
  79.1 8.1 %collective-permute-start.28 = (bf16[1,448,256]{2,1,0:T(8,128)(2,1)S(1)}, bf16[1,448,256]{2,1,0:T(8,128)(2,1)S(1)}, u32[]{:S(2)}, u32[]{:S(2)}) collective-permute-start(bf16[1,448,256]{2,1,0:T(8,128)(2,1)S(1)} %get-tuple-element.85), channel_id=1, source_target_pairs={{0,4},{8,0},{16,8},{24,16},{28,24},{20,28},{12,20},{4,12},{1,5},{9... | collective-permute-start | bytes 688136 | tf_op jit(solution)/shard_map/ppermute | solution.py:366
  79.6 8.1 %collective-permute-start.24 = (bf16[1,448,256]{2,1,0:T(8,128)(2,1)S(1)}, bf16[1,448,256]{2,1,0:T(8,128)(2,1)S(1)}, u32[]{:S(2)}, u32[]{:S(2)}) collective-permute-start(bf16[1,448,256]{2,1,0:T(8,128)(2,1)S(1)} %get-tuple-element.81), channel_id=1, source_target_pairs={{0,8},{8,16},{16,24},{24,28},{28,20},{20,12},{12,4},{4,0},{1,9},{9... | collective-permute-start | bytes 688136 | tf_op jit(solution)/shard_map/ppermute | solution.py:366
  87.2 12.2 %collective-permute-start.29 = (bf16[2,448,256]{2,1,0:T(8,128)(2,1)S(1)}, bf16[2,448,256]{2,1,0:T(8,128)(2,1)S(1)}, u32[]{:S(2)}, u32[]{:S(2)}) collective-permute-start(bf16[2,448,256]{2,1,0:T(8,128)(2,1)S(1)} %add_convert_fusion.3), channel_id=1, source_target_pairs={{0,4},{8,0},{16,8},{24,16},{28,24},{20,28},{12,20},{4,12},{1,5},{9... | collective-permute-start | bytes 1376264 | tf_op jit(solution)/shard_map/ppermute | solution.py:366
  87.8 12.2 %collective-permute-start.25 = (bf16[2,448,256]{2,1,0:T(8,128)(2,1)S(1)}, bf16[2,448,256]{2,1,0:T(8,128)(2,1)S(1)}, u32[]{:S(2)}, u32[]{:S(2)}) collective-permute-start(bf16[2,448,256]{2,1,0:T(8,128)(2,1)S(1)} %add_convert_fusion.6), channel_id=1, source_target_pairs={{0,8},{8,16},{16,24},{24,28},{28,20},{20,12},{12,4},{4,0},{1,9},{9... | collective-permute-start | bytes 1376264 | tf_op jit(solution)/shard_map/ppermute | solution.py:366
  89.4 12.4 %collective-permute-start.17 = (bf16[2,128,896]{2,1,0:T(8,128)(2,1)S(1)}, bf16[2,128,896]{2,1,0:T(8,128)(2,1)S(1)}, u32[]{:S(2)}, u32[]{:S(2)}) collective-permute-start(bf16[2,128,896]{2,1,0:T(8,128)(2,1)S(1)} %get-tuple-element.65), channel_id=1, source_target_pairs={{0,1},{1,0},{2,3},{3,2},{4,5},{5,4},{6,7},{7,6},{8,9},{9,8},{10,11... | collective-permute-start | bytes 1376264 | tf_op jit(solution)/shard_map/ppermute | solution.py:363
  89.4 12.4 %collective-permute-start.18 = (bf16[2,128,896]{2,1,0:T(8,128)(2,1)S(1)}, bf16[2,128,896]{2,1,0:T(8,128)(2,1)S(1)}, u32[]{:S(2)}, u32[]{:S(2)}) collective-permute-start(bf16[2,128,896]{2,1,0:T(8,128)(2,1)S(1)} %get-tuple-element.67), channel_id=1, source_target_pairs={{0,1},{1,0},{2,3},{3,2},{4,5},{5,4},{6,7},{7,6},{8,9},{9,8},{10,11... | collective-permute-start | bytes 1376264 | tf_op jit(solution)/shard_map/ppermute | solution.py:363
  92.3 22.3 %collective-permute-start.23 = (bf16[128,3584]{1,0:T(8,128)(2,1)S(1)}, bf16[128,3584]{1,0:T(8,128)(2,1)S(1)}, u32[]{:S(2)}, u32[]{:S(2)}) collective-permute-start(bf16[128,3584]{1,0:T(8,128)(2,1)S(1)} %get-tuple-element.76.refs_9_), channel_id=1, source_target_pairs={{0,2},{1,3},{2,0},{3,1},{4,6},{5,7},{6,4},{7,5},{8,10},{9,11},{10,... | collective-permute-start | bytes 2752520 | tf_op jit(solution)/shard_map/ppermute | solution.py:363
  99.5 11.3 %collective-permute-start.30 = (bf16[2,448,256]{2,1,0:T(8,128)(2,1)S(1)}, bf16[2,448,256]{2,1,0:T(8,128)(2,1)S(1)}, u32[]{:S(2)}, u32[]{:S(2)}) collective-permute-start(bf16[2,448,256]{2,1,0:T(8,128)(2,1)S(1)} %add_convert_fusion.2), channel_id=1, source_target_pairs={{0,4},{8,0},{16,8},{24,16},{28,24},{20,28},{12,20},{4,12},{1,5},{9... | collective-permute-start | bytes 1376264 | tf_op jit(solution)/shard_map/ppermute | solution.py:366
  100.1 11.3 %collective-permute-start.26 = (bf16[2,448,256]{2,1,0:T(8,128)(2,1)S(1)}, bf16[2,448,256]{2,1,0:T(8,128)(2,1)S(1)}, u32[]{:S(2)}, u32[]{:S(2)}) collective-permute-start(bf16[2,448,256]{2,1,0:T(8,128)(2,1)S(1)} %add_convert_fusion.5), channel_id=1, source_target_pairs={{0,8},{8,16},{16,24},{24,28},{28,20},{20,12},{12,4},{4,0},{1,9},{9... | collective-permute-start | bytes 1376264 | tf_op jit(solution)/shard_map/ppermute | solution.py:366
  111.0 10.4 %collective-permute-start.31 = (bf16[2,448,256]{2,1,0:T(8,128)(2,1)S(1)}, bf16[2,448,256]{2,1,0:T(8,128)(2,1)S(1)}, u32[]{:S(2)}, u32[]{:S(2)}) collective-permute-start(bf16[2,448,256]{2,1,0:T(8,128)(2,1)S(1)} %add_convert_fusion.1), channel_id=1, source_target_pairs={{0,4},{8,0},{16,8},{24,16},{28,24},{20,28},{12,20},{4,12},{1,5},{9... | collective-permute-start | bytes 1376264 | tf_op jit(solution)/shard_map/ppermute | solution.py:366
  111.6 10.1 %collective-permute-start.27 = (bf16[2,448,256]{2,1,0:T(8,128)(2,1)S(1)}, bf16[2,448,256]{2,1,0:T(8,128)(2,1)S(1)}, u32[]{:S(2)}, u32[]{:S(2)}) collective-permute-start(bf16[2,448,256]{2,1,0:T(8,128)(2,1)S(1)} %add_convert_fusion.4), channel_id=1, source_target_pairs={{0,8},{8,16},{16,24},{24,28},{28,20},{20,12},{12,4},{4,0},{1,9},{9... | collective-permute-start | bytes 1376264 | tf_op jit(solution)/shard_map/ppermute | solution.py:366

commit v15 on v14

--- a/solution.py
+++ b/solution.py
@@ -147,25 +147,26 @@
     if not last:
         for e in range(2):
             refs[-3][:, e * PAIR : (e + 1) * PAIR] = sums[e]
-    else:
-        kv_ref, kind_ref, ids_ref, ids_row_ref = refs[-6:-2]
-        for i, ref in enumerate(parts):
-            here = pl.ds(piece_start(me_ref[0], i, rows), rows)
-            kind, ids = read_marks(ref[0], depth)
-            mine = slice(i * rows, (i + 1) * rows)
-            kv_ref[here, :] = jnp.where(kind == 1.0, sums[1][mine], sums[0][mine]).astype(BF16)
-            kind_ref[here, :] = kind
-            ids_ref[here, :] = ids
-        ids_row_ref[...] = jnp.broadcast_to(ids_ref[...], (8 * rows, 128)).T[:1]
+    for i, ref in enumerate(parts):
+        here = pl.ds(piece_start(me_ref[0], i, rows), rows)
+        kind, ids = read_marks(ref[0], depth)
+        mine = slice(i * rows, (i + 1) * rows)
+        if last:
+            refs[-3][here, :] = jnp.where(kind == 1.0, sums[1][mine], sums[0][mine]).astype(BF16)
+        if first:
+            refs[-6][here, :] = kind
+            refs[-5][here, :] = ids
+    if first:
+        refs[-4][...] = jnp.broadcast_to(refs[-5][...], (8 * rows, 128)).T[:1]
     for copy in copies:
         copy.wait()
 
 
 def project(me, steps, parts, weights, before, depth, last=False, halves=False):
     length = 8 * parts[0].shape[1]
-    outs = [shaped((length, 2 * PAIR), F32)]
-    if last:
-        outs = [shaped((length, PAIR), BF16)] + [shaped(x, F32) for x in ((length, 1), (length, 1), (1, length))]
+    outs = [shaped((length, PAIR), BF16) if last else shaped((length, 2 * PAIR), F32)]
+    if not before:
+        outs = [shaped(x, F32) for x in ((length, 1), (length, 1), (1, length))] + outs
     outs.append(shaped((len(CYCLE), 2, depth, PAIR), BF16))
     operands = (*parts, *weights, *before)
     count = len(operands)
@@ -203,7 +204,7 @@
 
 
 def attend_kernel(spot, me_ref, own_ref, sibling_ref, kv_ref, ids_ref, ids_row_ref, *refs):
-    mine_ref, other_ref, early_ref, late_ref, bias, scores_all, dp_all, pbs, his, los = refs[-10:]
+    mine_ref, other_ref, gkv_ref, bias, scores_all, dp_all, pbs, his, los = refs[-9:]
     rows = own_ref.shape[2]
     heads = [slice(h * HEAD_DIM, (h + 1) * HEAD_DIM) for h in range(GROUP)]
     for i in range(2):
@@ -238,14 +239,11 @@
             ref[1, :, cols] = gq[here]
     dk = (contract(q, his[...], 0, 0) + contract(q, los[...], 0, 0)) * SCALE
     dv = contract(up, pbs[...], 0, 0)
-    half = early_ref.shape[0]
     for i, x in enumerate((dk.T, dv.T)):
-        cols = slice(i * HEAD_DIM, (i + 1) * HEAD_DIM)
-        early_ref[:, cols] = x[:half]
-        late_ref[:, cols] = x[half:].astype(late_ref.dtype)
-
-
-def attend(spot, me, own, other, kv, ids, ids_row, late, wait=()):
+        gkv_ref[:, i * HEAD_DIM : (i + 1) * HEAD_DIM] = x.astype(gkv_ref.dtype)
+
+
+def attend(spot, me, own, other, kv, ids, ids_row, dtype, wait=()):
     rows = own.shape[2]
     length = kv.shape[0]
     stacked = (2 * GROUP * rows, length)
@@ -254,7 +252,7 @@
         functools.partial(attend_kernel, spot),
         me,
         (own, other, kv, ids, ids_row, *wait),
-        [side, side, shaped((length // 2, PAIR), F32), shaped((length // 2, PAIR), late)],
+        [side, side, shaped((length, PAIR), dtype)],
         6,
         scratch=[pltpu.VMEM((2 * rows, length), F32), pltpu.VMEM(stacked, F32)] + [pltpu.VMEM(stacked, BF16)] * 4,
         far=tuple(range(5, 5 + len(wait))),
@@ -386,16 +384,16 @@
     parts = [*here, *[swap(x, 1) for x in here], *across, *[swap(x, 1) for x in across]]
 
     if near_link:
-        before = project(me, STEPS[:5], parts, weights[:5], (), depth)
+        kind, ids, ids_row, *before = project(me, STEPS[:5], parts, weights[:5], (), depth)
         weights += both_ways(*halve(me, *weights[5:], (before[0],)))
         before = project(me, STEPS[5:7], parts, weights[5:7], before, depth)
-        kv, kind, ids, ids_row, weight = project(me, STEPS[7:], parts, weights[7:], before, depth, True, True)
+        kv, weight = project(me, STEPS[7:], parts, weights[7:], before, depth, True, True)
     else:
         kv, kind, ids, ids_row = project_plain(quarters, parts, weight, depth)
     kv_far = swap(kv, 2)
-    far_own, far_other, early, late = attend(1, me, own, others[1], kv_far, ids, ids_row, BF16)
-    near_own, near_other, *near = attend(0, me, own, others[0], kv, ids, ids_row, F32, (early,))
-    grad_kv = jnp.concatenate([near[0] + swap(early, 2), near[1] + swap(late, 2).astype(F32)]).astype(BF16)
+    far_own, far_other, far = attend(1, me, own, others[1], kv_far, ids, ids_row, BF16)
+    near_own, near_other, near = attend(0, me, own, others[0], kv, ids, ids_row, F32, (far,))
+    grad_kv = (near + swap(far, 2).astype(F32)).astype(BF16)
     attended, grad_queries = place_heads(me, (near_own, swap(near_other, 1), far_own, swap(far_other, 1)))
 
     grad_c = swap(grad_kv, 1)

time: 123 us -> 126 us (1.024)
  waiting for transfers between devices: 55.8 us -> 64.7 us
  starting transfers between devices: 28.6 us -> 23.5 us
    ppermute x16, waiting for transfers between devices: 36.4 us -> 45.9 us  [turn(): lax.ppermute(x, 'fsdp', [(CYCLE[i], CYCLE[(i + by) % fsdp]) for i in rang...]
    ppermute x16 -> x15, starting transfers between devices: 10.9 us -> 5.47 us  [swap(): return lax.ppermute(x, 'seq', [(i, i ^ bit) for i in range(seq)])]
    ppermute x16 -> x15, waiting for transfers between devices: 19.4 us -> 18.8 us  [swap(): return lax.ppermute(x, 'seq', [(i, i ^ bit) for i in range(seq)])]
  transfers between devices with their start and end apart: 32 -> 31, of which waited for: 15 -> 16; matrix products, arithmetic and copies ran while one was open for 2% -> 2% of each run, Pallas kernels for 23% -> 21%
where the time goes in v15:
time: 126 us
  waiting for transfers between devices  64.7 us (51%)
  Pallas kernels  29.8 us (24%)
  starting transfers between devices  23.5 us (19%)
  local copies, waits for them, and re-layouts  3.54 us (3%)
  other arithmetic  3.53 us (3%)
    ppermute x16, waiting for transfers between devices, turn(): lax.ppermute(x, 'fsdp', [(CYCLE[i], CYCLE[(i + by) % fsdp]) for i in rang...  45.9 us
    pallas_call x15, Pallas kernels, call(): pl.pallas_call(body, in_specs=[pl.BlockSpec(memory_space=pltpu.SMEM)] + [...  29.8 us
    ppermute x15, waiting for transfers between devices, swap(): return lax.ppermute(x, 'seq', [(i, i ^ bit) for i in range(seq)])  18.8 us
    ppermute x16, starting transfers between devices, turn(): lax.ppermute(x, 'fsdp', [(CYCLE[i], CYCLE[(i + by) % fsdp]) for i in rang...  18 us
    ppermute x15, starting transfers between devices, swap(): return lax.ppermute(x, 'seq', [(i, i ^ bit) for i in range(seq)])  5.47 us
    unnamed x8, local copies, waits for them, and re-layouts  3.54 us
  transfers between devices with their start and end apart: 31, of which 16 were waited for; matrix products, arithmetic and copies ran while one was open for 2% of the time, Pallas kernels for 21%

profile of v15, /device:TPU:0, one launch (start us, length us, event | category | flops | bytes accessed | tf_op | source)
XLA Modules:
  0.0 125.9 jit_solution(12885198568296299935)
XLA Ops:
  0.7 1.2 copy-done
  1.9 1.2 copy-done.1
  3.1 0.7 shard_map.93
  4.3 2.6 %collective-permute-start.1 = (bf16[2,448,256]{2,1,0:T(8,128)(2,1)}, bf16[2,448,256]{2,1,0:T(8,128)(2,1)S(1)}, u32[]{:S(2)}, u32[]{:S(2)}) collective-permute-start(bf16[2,448,256]{2,1,0:T(8,128)(2,1)} %refs_8_.1), channel_id=1, source_target_pairs={{0,8},{8,16},{16,24},{24,28},{28,20},{20,12},{12,4},{4,0},{1,9},{9... | collective-permute-start | bytes 1376264 | tf_op jit(solution)/shard_map/ppermute | solution.py:364
  6.9 1.5 %collective-permute-start.6 = (bf16[128,3584]{1,0:T(8,128)(2,1)}, bf16[128,3584]{1,0:T(8,128)(2,1)S(1)}, u32[]{:S(2)}, u32[]{:S(2)}) collective-permute-start(bf16[128,3584]{1,0:T(8,128)(2,1)} %bitcast.11), channel_id=1, source_target_pairs={{0,2},{1,3},{2,0},{3,1},{4,6},{5,7},{6,4},{7,5},{8,10},{9,11},{10,... | collective-permute-start | bytes 2752520 | tf_op jit(solution)/shard_map/ppermute | solution.py:361
  8.9 0.7 multiply_add_fusion.ids_ref
  9.6 1.2 copy-done.2
  10.7 0.9 shard_map.94
  11.6 6.5 %collective-permute-done.1.refs_2_.refs_9_ = bf16[2,448,256]{2,1,0:T(8,128)(2,1)S(1)} collective-permute-done((bf16[2,448,256]{2,1,0:T(8,128)(2,1)}, bf16[2,448,256]{2,1,0:T(8,128)(2,1)S(1)}, u32[]{:S(2)}, u32[]{:S(2)}) %collective-permute-start.1) | collective-permute-done | bytes 458784 | tf_op jit(solution)/shard_map/ppermute | solution.py:364
  18.2 1.8 %collective-permute-start.10 = (bf16[2,448,256]{2,1,0:T(8,128)(2,1)S(1)}, bf16[2,448,256]{2,1,0:T(8,128)(2,1)S(1)}, u32[]{:S(2)}, u32[]{:S(2)}) collective-permute-start(bf16[2,448,256]{2,1,0:T(8,128)(2,1)S(1)} %collective-permute-done.1.refs_2_.refs_9_), channel_id=1, source_target_pairs={{0,8},{8,16},{16,24},{24,28},{28,20},{20,12},{12,4},{4,0},{1,9},{9... | collective-permute-start | bytes 1376264 | tf_op jit(solution)/shard_map/ppermute | solution.py:364
  20.0 1.6 %collective-permute-done.2.refs_3_.refs_10_ = bf16[2,448,256]{2,1,0:T(8,128)(2,1)S(1)} collective-permute-done((bf16[2,448,256]{2,1,0:T(8,128)(2,1)}, bf16[2,448,256]{2,1,0:T(8,128)(2,1)S(1)}, u32[]{:S(2)}, u32[]{:S(2)}) %collective-permute-start.2) | collective-permute-done | bytes 458784 | tf_op jit(solution)/shard_map/ppermute | solution.py:364
  21.6 0.6 shard_map.95
  23.1 6.5 %collective-permute-done.7.ids_ref = s32[1,128]{1,0:T(1,128)S(1)} collective-permute-done((s32[1,128]{1,0:T(1,128)S(1)}, s32[1,128]{1,0:T(1,128)S(1)}, u32[]{:S(2)}, u32[]{:S(2)}) %collective-permute-start.7) | collective-permute-done | bytes 544 | tf_op jit(solution)/shard_map/ppermute | solution.py:361
  29.6 0.9 shard_map.96
  31.2 4.0 %collective-permute-done.12.refs_12_ = bf16[2,448,256]{2,1,0:T(8,128)(2,1)S(1)} collective-permute-done((bf16[2,448,256]{2,1,0:T(8,128)(2,1)S(1)}, bf16[2,448,256]{2,1,0:T(8,128)(2,1)S(1)}, u32[]{:S(2)}, u32[]{:S(2)}) %collective-permute-start.12) | collective-permute-done | bytes 458784 | tf_op jit(solution)/shard_map/ppermute | solution.py:364
  35.2 1.6 %collective-permute-start.11 = (bf16[2,448,256]{2,1,0:T(8,128)(2,1)S(1)}, bf16[2,448,256]{2,1,0:T(8,128)(2,1)S(1)}, u32[]{:S(2)}, u32[]{:S(2)}) collective-permute-start(bf16[2,448,256]{2,1,0:T(8,128)(2,1)S(1)} %collective-permute-done.10.refs_11_), channel_id=1, source_target_pairs={{0,8},{8,16},{16,24},{24,28},{28,20},{20,12},{12,4},{4,0},{1,9},{9... | collective-permute-start | bytes 1376264 | tf_op jit(solution)/shard_map/ppermute | solution.py:364
  37.2 3.5 %shard_map.97 = (f32[512,1]{1,0:T(8,128)S(1)}, f32[512,1]{1,0:T(8,128)S(1)}, f32[1,512]{1,0:T(1,128)S(1)}, f32[512,512]{1,0:T(8,128)S(1)}, bf16[8,2,448,256]{3,2,1,0:T(8,128)(2,1)S(1)}) custom-call(s32[2]{0:T(128)S(1)} %pad_add_fusion.me_ref, bf16[8,64,512]{2,1,0:T(8,128)(2,1)S(1)} %get-tuple-element.48.refs_0_, ...), custom_call_target="tpu_custom_call" | custom-call | bytes 3000000 | tf_op jit(solution)/shard_map/pallas_call | solution.py:36
  40.8 6.5 %collective-permute-done.11.ups_ref.refs_8_ = bf16[2,448,256]{2,1,0:T(8,128)(2,1)S(1)} collective-permute-done((bf16[2,448,256]{2,1,0:T(8,128)(2,1)S(1)}, bf16[2,448,256]{2,1,0:T(8,128)(2,1)S(1)}, u32[]{:S(2)}, u32[]{:S(2)}) %collective-permute-start.11) | collective-permute-done | bytes 458784 | tf_op jit(solution)/shard_map/ppermute | solution.py:364
  47.3 1.3 %collective-permute-done.13.downs_ref.refs_9_ = bf16[2,448,256]{2,1,0:T(8,128)(2,1)S(1)} collective-permute-done((bf16[2,448,256]{2,1,0:T(8,128)(2,1)S(1)}, bf16[2,448,256]{2,1,0:T(8,128)(2,1)S(1)}, u32[]{:S(2)}, u32[]{:S(2)}) %collective-permute-start.13) | collective-permute-done | bytes 458784 | tf_op jit(solution)/shard_map/ppermute | solution.py:364
  49.2 1.6 %collective-permute-start.14 = (bf16[1,448,256]{2,1,0:T(8,128)(2,1)S(1)}, bf16[1,448,256]{2,1,0:T(8,128)(2,1)S(1)}, u32[]{:S(2)}, u32[]{:S(2)}) collective-permute-start(bf16[1,448,256]{2,1,0:T(8,128)(2,1)S(1)} %get-tuple-element.53), channel_id=1, source_target_pairs={{0,8},{8,16},{16,24},{24,28},{28,20},{20,12},{12,4},{4,0},{1,9},{9... | collective-permute-start | bytes 688136 | tf_op jit(solution)/shard_map/ppermute | solution.py:364
  51.2 1.8 %shard_map.99 = (f32[512,512]{1,0:T(8,128)S(1)}, bf16[8,2,448,256]{3,2,1,0:T(8,128)(2,1)S(1)}) custom-call(s32[2]{0:T(128)S(1)} %pad_add_fusion.me_ref, bf16[8,64,512]{2,1,0:T(8,128)(2,1)S(1)} %get-tuple-element.48.refs_0_, bf16[8,64,512]{2,1,0:T(8,128)(2,1)S(1)} %get-tuple-element.49.refs_1_, ...), custom_call_target="tpu_custom_call", output_to_operand_aliasing={{1}: (12, {})} | custom-call | bytes 3000000 | tf_op jit(solution)/shard_map/pallas_call | solution.py:36
  53.1 2.2 %collective-permute-done.14.refs_8_ = bf16[1,448,256]{2,1,0:T(8,128)(2,1)S(1)} collective-permute-done((bf16[1,448,256]{2,1,0:T(8,128)(2,1)S(1)}, bf16[1,448,256]{2,1,0:T(8,128)(2,1)S(1)}, u32[]{:S(2)}, u32[]{:S(2)}) %collective-permute-start.14) | collective-permute-done | bytes 229408 | tf_op jit(solution)/shard_map/ppermute | solution.py:364
  55.2 1.6 %collective-permute-done.15.refs_9_ = bf16[1,448,256]{2,1,0:T(8,128)(2,1)S(1)} collective-permute-done((bf16[1,448,256]{2,1,0:T(8,128)(2,1)S(1)}, bf16[1,448,256]{2,1,0:T(8,128)(2,1)S(1)}, u32[]{:S(2)}, u32[]{:S(2)}) %collective-permute-start.15) | collective-permute-done | bytes 229408 | tf_op jit(solution)/shard_map/ppermute | solution.py:364
  56.8 1.6 %shard_map.100 = (bf16[512,256]{1,0:T(8,128)(2,1)S(1)}, bf16[8,2,448,256]{3,2,1,0:T(8,128)(2,1)S(1)}) custom-call(s32[2]{0:T(128)S(1)} %pad_add_fusion.me_ref, bf16[8,64,512]{2,1,0:T(8,128)(2,1)S(1)} %get-tuple-element.48.refs_0_, bf16[8,64,512]{2,1,0:T(8,128)(2,1)S(1)} %get-tuple-element.49.refs_1_, ...), custom_call_target="tpu_custom_call", output_to_operand_aliasing={{1}: (12, {})} | custom-call | bytes 3000000 | tf_op jit(solution)/shard_map/pallas_call | solution.py:36
  59.1 8.2 %collective-permute-done.16.kv_ref = bf16[512,256]{1,0:T(8,128)(2,1)S(1)} collective-permute-done((bf16[512,256]{1,0:T(8,128)(2,1)S(1)}, bf16[512,256]{1,0:T(8,128)(2,1)S(1)}, u32[]{:S(2)}, u32[]{:S(2)}) %collective-permute-start.16) | collective-permute-done | bytes 262176 | tf_op jit(solution)/shard_map/ppermute | solution.py:361
  67.2 4.6 %shard_map.101 = (bf16[2,128,896]{2,1,0:T(8,128)(2,1)S(1)}, bf16[2,128,896]{2,1,0:T(8,128)(2,1)S(1)}, bf16[512,256]{1,0:T(8,128)(2,1)S(1)}) custom-call(s32[2]{0:T(128)S(1)} %pad_add_fusion.me_ref, bf16[2,2,128,896]{3,2,1,0:T(8,128)(2,1)S(1)} %get-tuple-element.43.own_ref, bf16[2,128,896]{2,1,0:T(8,128)(2,1)S(1)} %collective-permute-done.3.refs_5_.sibling_ref, ...), custom_call_target="tpu_custom_call" | custom-call | bytes 18000000 | tf_op jit(solution)/shard_map/pallas_call | solution.py:36
  72.4 4.7 %shard_map.102 = (bf16[2,128,896]{2,1,0:T(8,128)(2,1)S(1)}, bf16[2,128,896]{2,1,0:T(8,128)(2,1)S(1)}, f32[512,256]{1,0:T(8,128)S(1)}) custom-call(s32[2]{0:T(128)S(1)} %pad_add_fusion.me_ref, bf16[2,2,128,896]{3,2,1,0:T(8,128)(2,1)S(1)} %get-tuple-element.43.own_ref, bf16[2,128,896]{2,1,0:T(8,128)(2,1)S(1)} %collective-permute-done.refs_4_.sibling_ref, ...), custom_call_target="tpu_custom_call" | custom-call | bytes 18000000 | tf_op jit(solution)/shard_map/pallas_call | solution.py:36
  77.1 2.7 %collective-permute-done.19 = bf16[512,256]{1,0:T(8,128)(2,1)S(1)} collective-permute-done((bf16[512,256]{1,0:T(8,128)(2,1)S(1)}, bf16[512,256]{1,0:T(8,128)(2,1)S(1)}, u32[]{:S(2)}, u32[]{:S(2)}) %collective-permute-start.19) | collective-permute-done | bytes 262176 | tf_op jit(solution)/shard_map/ppermute | solution.py:361
  80.0 1.3 shard_map.107
  81.2 1.5 %collective-permute-start.23 = (bf16[1,448,256]{2,1,0:T(8,128)(2,1)S(1)}, bf16[1,448,256]{2,1,0:T(8,128)(2,1)S(1)}, u32[]{:S(2)}, u32[]{:S(2)}) collective-permute-start(bf16[1,448,256]{2,1,0:T(8,128)(2,1)S(1)} %get-tuple-element.77), channel_id=1, source_target_pairs={{0,8},{8,16},{16,24},{24,28},{28,20},{20,12},{12,4},{4,0},{1,9},{9... | collective-permute-start | bytes 688136 | tf_op jit(solution)/shard_map/ppermute | solution.py:364
  83.3 2.9 %shard_map.104 = (f32[128,3584]{1,0:T(8,128)S(1)}, bf16[128,3584]{1,0:T(8,128)(2,1)S(1)}) custom-call(s32[2]{0:T(128)S(1)} %pad_add_fusion.me_ref, f32[512,1]{1,0:T(8,128)S(1)} %get-tuple-element.68.kind_ref, bf16[512,256]{1,0:T(8,128)(2,1)S(1)} %add_convert_fusion.7.g_ref.refs_8_, bf16[512,256]{1,0:T(8,128)(2,1)S(1)} %collective-permute-done.20.gc_ref, ...), custom_call_target="tpu_custom_call" | custom-call | bytes 21000000 | tf_op jit(solution)/shard_map/pallas_call | solution.py:36
  86.2 1.5 %shard_map.106 = (f32[2,448,256]{2,1,0:T(8,128)S(1)}, f32[2,448,256]{2,1,0:T(8,128)S(1)}) custom-call(s32[2]{0:T(128)S(1)} %pad_add_fusion.me_ref, bf16[8,64,512]{2,1,0:T(8,128)(2,1)S(1)} %get-tuple-element.48.refs_0_, bf16[8,64,512]{2,1,0:T(8,128)(2,1)S(1)} %get-tuple-element.49.refs_1_, bf16[8,64,512]{2,1,0:T(8,128)(2,1)S(1)} %collective-permute-done.4.refs_2_, ...), custom_call_target="tpu_custom_call" | custom-call | bytes 9000000 | tf_op jit(solution)/shard_map/pallas_call | solution.py:36
  87.8 1.5 %collective-permute-done.23 = bf16[1,448,256]{2,1,0:T(8,128)(2,1)S(1)} collective-permute-done((bf16[1,448,256]{2,1,0:T(8,128)(2,1)S(1)}, bf16[1,448,256]{2,1,0:T(8,128)(2,1)S(1)}, u32[]{:S(2)}, u32[]{:S(2)}) %collective-permute-start.23) | collective-permute-done | bytes 229408 | tf_op jit(solution)/shard_map/ppermute | solution.py:364
  89.3 1.5 %collective-permute-start.24 = (bf16[2,448,256]{2,1,0:T(8,128)(2,1)S(1)}, bf16[2,448,256]{2,1,0:T(8,128)(2,1)S(1)}, u32[]{:S(2)}, u32[]{:S(2)}) collective-permute-start(bf16[2,448,256]{2,1,0:T(8,128)(2,1)S(1)} %add_convert_fusion.6), channel_id=1, source_target_pairs={{0,8},{8,16},{16,24},{24,28},{28,20},{20,12},{12,4},{4,0},{1,9},{9... | collective-permute-start | bytes 1376264 | tf_op jit(solution)/shard_map/ppermute | solution.py:364
  91.0 0.6 collective-permute-start.28
  92.1 2.3 %shard_map.105 = (f32[2,448,256]{2,1,0:T(8,128)S(1)}, f32[2,448,256]{2,1,0:T(8,128)S(1)}, f32[2,448,256]{2,1,0:T(8,128)S(1)}, f32[2,448,256]{2,1,0:T(8,128)S(1)}, f32[2,448,256]{2,1,0:T(8,128)S(1)}) custom-call(s32[2]{0:T(128)S(1)} %pad_add_fusion.me_ref, bf16[8,64,512]{2,1,0:T(8,128)(2,1)S(1)} %get-tuple-element.48.refs_0_, ...), custom_call_target="tpu_custom_call" | custom-call | bytes 18000000 | tf_op jit(solution)/shard_map/pallas_call | solution.py:36
  95.0 6.5 %collective-permute-done.24 = bf16[2,448,256]{2,1,0:T(8,128)(2,1)S(1)} collective-permute-done((bf16[2,448,256]{2,1,0:T(8,128)(2,1)S(1)}, bf16[2,448,256]{2,1,0:T(8,128)(2,1)S(1)}, u32[]{:S(2)}, u32[]{:S(2)}) %collective-permute-start.24) | collective-permute-done | bytes 458784 | tf_op jit(solution)/shard_map/ppermute | solution.py:364
  101.7 1.5 %collective-permute-start.25 = (bf16[2,448,256]{2,1,0:T(8,128)(2,1)S(1)}, bf16[2,448,256]{2,1,0:T(8,128)(2,1)S(1)}, u32[]{:S(2)}, u32[]{:S(2)}) collective-permute-start(bf16[2,448,256]{2,1,0:T(8,128)(2,1)S(1)} %add_convert_fusion.5), channel_id=1, source_target_pairs={{0,8},{8,16},{16,24},{24,28},{28,20},{20,12},{12,4},{4,0},{1,9},{9... | collective-permute-start | bytes 1376264 | tf_op jit(solution)/shard_map/ppermute | solution.py:364
  103.3 0.6 collective-permute-start.29
  103.9 1.9 %shard_map.103 = (bf16[128,3584]{1,0:T(8,128)(2,1)}, bf16[128,3584]{1,0:T(8,128)(2,1)}) custom-call(s32[2]{0:T(128)S(1)} %pad_add_fusion.me_ref, bf16[2,128,896]{2,1,0:T(8,128)(2,1)S(1)} %get-tuple-element.62.refs_0_, bf16[2,128,896]{2,1,0:T(8,128)(2,1)S(1)} %collective-permute-done.17.refs_1_, bf16[2,128,896]{2,1,0:T(8,128)(2,1)S(1)} %get-tuple-element.64.refs_2_, ...), custom_call_target="tpu_custom_call" | custom-call | bytes 9000000 | tf_op jit(solution)/shard_map/pallas_call | solution.py:36
  105.8 7.1 %collective-permute-done.25 = bf16[2,448,256]{2,1,0:T(8,128)(2,1)S(1)} collective-permute-done((bf16[2,448,256]{2,1,0:T(8,128)(2,1)S(1)}, bf16[2,448,256]{2,1,0:T(8,128)(2,1)S(1)}, u32[]{:S(2)}, u32[]{:S(2)}) %collective-permute-start.25) | collective-permute-done | bytes 458784 | tf_op jit(solution)/shard_map/ppermute | solution.py:364
  113.1 1.5 %collective-permute-start.26 = (bf16[2,448,256]{2,1,0:T(8,128)(2,1)S(1)}, bf16[2,448,256]{2,1,0:T(8,128)(2,1)S(1)}, u32[]{:S(2)}, u32[]{:S(2)}) collective-permute-start(bf16[2,448,256]{2,1,0:T(8,128)(2,1)S(1)} %add_convert_fusion.4), channel_id=1, source_target_pairs={{0,8},{8,16},{16,24},{24,28},{28,20},{20,12},{12,4},{4,0},{1,9},{9... | collective-permute-start | bytes 1376264 | tf_op jit(solution)/shard_map/ppermute | solution.py:364
  114.7 0.6 collective-permute-start.30
  115.3 1.4 %collective-permute-done.22 = bf16[128,3584]{1,0:T(8,128)(2,1)S(1)} collective-permute-done((bf16[128,3584]{1,0:T(8,128)(2,1)S(1)}, bf16[128,3584]{1,0:T(8,128)(2,1)S(1)}, u32[]{:S(2)}, u32[]{:S(2)}) %collective-permute-start.22) | collective-permute-done | bytes 917536 | tf_op jit(solution)/shard_map/ppermute | solution.py:361
  116.7 1.1 fusion
  117.8 5.6 %collective-permute-done.26 = bf16[2,448,256]{2,1,0:T(8,128)(2,1)S(1)} collective-permute-done((bf16[2,448,256]{2,1,0:T(8,128)(2,1)S(1)}, bf16[2,448,256]{2,1,0:T(8,128)(2,1)S(1)}, u32[]{:S(2)}, u32[]{:S(2)}) %collective-permute-start.26) | collective-permute-done | bytes 458784 | tf_op jit(solution)/shard_map/ppermute | solution.py:364
  123.5 1.4 %collective-permute-done.30 = bf16[2,448,256]{2,1,0:T(8,128)(2,1)S(1)} collective-permute-done((bf16[2,448,256]{2,1,0:T(8,128)(2,1)S(1)}, bf16[2,448,256]{2,1,0:T(8,128)(2,1)S(1)}, u32[]{:S(2)}, u32[]{:S(2)}) %collective-permute-start.30) | collective-permute-done | bytes 458784 | tf_op jit(solution)/shard_map/ppermute | solution.py:364
  124.8 1.0 convert_add_fusion
  (48 shorter events, 7.7 us)
Async XLA Ops:
  0.7 1.2 copy-start
  1.9 1.2 copy-start.1
  3.1 34.2 %copy-start.3 = (bf16[2,448,256]{2,1,0:T(8,128)(2,1)S(1)}, bf16[2,448,256]{2,1,0:T(8,128)(2,1)}, u32[]{:S(2)}) copy-start(bf16[2,448,256]{2,1,0:T(8,128)(2,1)} %refs_8_.1) | copy-start | bytes 1376260
  3.8 16.2 %collective-permute-start = (bf16[2,128,896]{2,1,0:T(8,128)(2,1)S(1)}, bf16[2,128,896]{2,1,0:T(8,128)(2,1)S(1)}, u32[]{:S(2)}, u32[]{:S(2)}) collective-permute-start(bf16[2,128,896]{2,1,0:T(8,128)(2,1)S(1)} %get-tuple-element.44), channel_id=1, source_target_pairs={{0,1},{1,0},{2,3},{3,2},{4,5},{5,4},{6,7},{7,6},{8,9},{9,8},{10,11... | collective-permute-start | bytes 1376264 | tf_op jit(solution)/shard_map/ppermute | solution.py:361
  4.3 13.9 %collective-permute-start.1 = (bf16[2,448,256]{2,1,0:T(8,128)(2,1)}, bf16[2,448,256]{2,1,0:T(8,128)(2,1)S(1)}, u32[]{:S(2)}, u32[]{:S(2)}) collective-permute-start(bf16[2,448,256]{2,1,0:T(8,128)(2,1)} %refs_8_.1), channel_id=1, source_target_pairs={{0,8},{8,16},{16,24},{24,28},{28,20},{20,12},{12,4},{4,0},{1,9},{9... | collective-permute-start | bytes 1376264 | tf_op jit(solution)/shard_map/ppermute | solution.py:364
  6.9 22.7 %collective-permute-start.6 = (bf16[128,3584]{1,0:T(8,128)(2,1)}, bf16[128,3584]{1,0:T(8,128)(2,1)S(1)}, u32[]{:S(2)}, u32[]{:S(2)}) collective-permute-start(bf16[128,3584]{1,0:T(8,128)(2,1)} %bitcast.11), channel_id=1, source_target_pairs={{0,2},{1,3},{2,0},{3,1},{4,6},{5,7},{6,4},{7,5},{8,10},{9,11},{10,... | collective-permute-start | bytes 2752520 | tf_op jit(solution)/shard_map/ppermute | solution.py:361
  8.4 11.6 %collective-permute-start.3 = (bf16[2,128,896]{2,1,0:T(8,128)(2,1)S(1)}, bf16[2,128,896]{2,1,0:T(8,128)(2,1)S(1)}, u32[]{:S(2)}, u32[]{:S(2)}) collective-permute-start(bf16[2,128,896]{2,1,0:T(8,128)(2,1)S(1)} %get-tuple-element.47), channel_id=1, source_target_pairs={{0,1},{1,0},{2,3},{3,2},{4,5},{5,4},{6,7},{7,6},{8,9},{9,8},{10,11... | collective-permute-start | bytes 1376264 | tf_op jit(solution)/shard_map/ppermute | solution.py:361
  8.4 13.1 %collective-permute-start.2 = (bf16[2,448,256]{2,1,0:T(8,128)(2,1)}, bf16[2,448,256]{2,1,0:T(8,128)(2,1)S(1)}, u32[]{:S(2)}, u32[]{:S(2)}) collective-permute-start(bf16[2,448,256]{2,1,0:T(8,128)(2,1)} %refs_8_.1), channel_id=1, source_target_pairs={{0,4},{8,0},{16,8},{24,16},{28,24},{20,28},{12,20},{4,12},{1,5},{9... | collective-permute-start | bytes 1376264 | tf_op jit(solution)/shard_map/ppermute | solution.py:364
  9.6 1.2 copy-start.2
  18.2 12.9 %collective-permute-start.10 = (bf16[2,448,256]{2,1,0:T(8,128)(2,1)S(1)}, bf16[2,448,256]{2,1,0:T(8,128)(2,1)S(1)}, u32[]{:S(2)}, u32[]{:S(2)}) collective-permute-start(bf16[2,448,256]{2,1,0:T(8,128)(2,1)S(1)} %collective-permute-done.1.refs_2_.refs_9_), channel_id=1, source_target_pairs={{0,8},{8,16},{16,24},{24,28},{28,20},{20,12},{12,4},{4,0},{1,9},{9... | collective-permute-start | bytes 1376264 | tf_op jit(solution)/shard_map/ppermute | solution.py:364
  22.2 14.6 %collective-permute-start.4 = (bf16[8,64,512]{2,1,0:T(8,128)(2,1)S(1)}, bf16[8,64,512]{2,1,0:T(8,128)(2,1)S(1)}, u32[]{:S(2)}, u32[]{:S(2)}) collective-permute-start(bf16[8,64,512]{2,1,0:T(8,128)(2,1)S(1)} %get-tuple-element.48.refs_0_), channel_id=1, source_target_pairs={{0,1},{1,0},{2,3},{3,2},{4,5},{5,4},{6,7},{7,6},{8,9},{9,8},{10,11... | collective-permute-start | bytes 1572872 | tf_op jit(solution)/shard_map/ppermute | solution.py:361
  22.3 12.9 %collective-permute-start.12 = (bf16[2,448,256]{2,1,0:T(8,128)(2,1)S(1)}, bf16[2,448,256]{2,1,0:T(8,128)(2,1)S(1)}, u32[]{:S(2)}, u32[]{:S(2)}) collective-permute-start(bf16[2,448,256]{2,1,0:T(8,128)(2,1)S(1)} %collective-permute-done.2.refs_3_.refs_10_), channel_id=1, source_target_pairs={{0,4},{8,0},{16,8},{24,16},{28,24},{20,28},{12,20},{4,12},{1,5},{9... | collective-permute-start | bytes 1376264 | tf_op jit(solution)/shard_map/ppermute | solution.py:364
  22.8 6.8 %collective-permute-start.7 = (s32[1,128]{1,0:T(1,128)S(1)}, s32[1,128]{1,0:T(1,128)S(1)}, u32[]{:S(2)}, u32[]{:S(2)}) collective-permute-start(s32[1,128]{1,0:T(1,128)S(1)} %multiply_add_fusion.ids_ref), channel_id=1, source_target_pairs={{0,2},{1,3},{2,0},{3,1},{4,6},{5,7},{6,4},{7,5},{8,10},{9,11},{10,... | collective-permute-start | bytes 1544 | tf_op jit(solution)/shard_map/ppermute | solution.py:361
  29.6 7.6 %collective-permute-start.5 = (bf16[8,64,512]{2,1,0:T(8,128)(2,1)S(1)}, bf16[8,64,512]{2,1,0:T(8,128)(2,1)S(1)}, u32[]{:S(2)}, u32[]{:S(2)}) collective-permute-start(bf16[8,64,512]{2,1,0:T(8,128)(2,1)S(1)} %get-tuple-element.49.refs_1_), channel_id=1, source_target_pairs={{0,1},{1,0},{2,3},{3,2},{4,5},{5,4},{6,7},{7,6},{8,9},{9,8},{10,11... | collective-permute-start | bytes 1572872 | tf_op jit(solution)/shard_map/ppermute | solution.py:361
  30.5 6.7 %collective-permute-start.8 = (bf16[8,64,512]{2,1,0:T(8,128)(2,1)S(1)}, bf16[8,64,512]{2,1,0:T(8,128)(2,1)S(1)}, u32[]{:S(2)}, u32[]{:S(2)}) collective-permute-start(bf16[8,64,512]{2,1,0:T(8,128)(2,1)S(1)} %get-tuple-element.50.refs_4_), channel_id=1, source_target_pairs={{0,1},{1,0},{2,3},{3,2},{4,5},{5,4},{6,7},{7,6},{8,9},{9,8},{10,11... | collective-permute-start | bytes 1572872 | tf_op jit(solution)/shard_map/ppermute | solution.py:361
  31.1 6.1 %collective-permute-start.9 = (bf16[8,64,512]{2,1,0:T(8,128)(2,1)S(1)}, bf16[8,64,512]{2,1,0:T(8,128)(2,1)S(1)}, u32[]{:S(2)}, u32[]{:S(2)}) collective-permute-start(bf16[8,64,512]{2,1,0:T(8,128)(2,1)S(1)} %get-tuple-element.51.refs_5_), channel_id=1, source_target_pairs={{0,1},{1,0},{2,3},{3,2},{4,5},{5,4},{6,7},{7,6},{8,9},{9,8},{10,11... | collective-permute-start | bytes 1572872 | tf_op jit(solution)/shard_map/ppermute | solution.py:361
  35.2 12.1 %collective-permute-start.11 = (bf16[2,448,256]{2,1,0:T(8,128)(2,1)S(1)}, bf16[2,448,256]{2,1,0:T(8,128)(2,1)S(1)}, u32[]{:S(2)}, u32[]{:S(2)}) collective-permute-start(bf16[2,448,256]{2,1,0:T(8,128)(2,1)S(1)} %collective-permute-done.10.refs_11_), channel_id=1, source_target_pairs={{0,8},{8,16},{16,24},{24,28},{28,20},{20,12},{12,4},{4,0},{1,9},{9... | collective-permute-start | bytes 1376264 | tf_op jit(solution)/shard_map/ppermute | solution.py:364
  36.8 11.8 %collective-permute-start.13 = (bf16[2,448,256]{2,1,0:T(8,128)(2,1)S(1)}, bf16[2,448,256]{2,1,0:T(8,128)(2,1)S(1)}, u32[]{:S(2)}, u32[]{:S(2)}) collective-permute-start(bf16[2,448,256]{2,1,0:T(8,128)(2,1)S(1)} %collective-permute-done.12.refs_12_), channel_id=1, source_target_pairs={{0,4},{8,0},{16,8},{24,16},{28,24},{20,28},{12,20},{4,12},{1,5},{9... | collective-permute-start | bytes 1376264 | tf_op jit(solution)/shard_map/ppermute | solution.py:364
  49.2 6.1 %collective-permute-start.14 = (bf16[1,448,256]{2,1,0:T(8,128)(2,1)S(1)}, bf16[1,448,256]{2,1,0:T(8,128)(2,1)S(1)}, u32[]{:S(2)}, u32[]{:S(2)}) collective-permute-start(bf16[1,448,256]{2,1,0:T(8,128)(2,1)S(1)} %get-tuple-element.53), channel_id=1, source_target_pairs={{0,8},{8,16},{16,24},{24,28},{28,20},{20,12},{12,4},{4,0},{1,9},{9... | collective-permute-start | bytes 688136 | tf_op jit(solution)/shard_map/ppermute | solution.py:364
  50.8 6.0 %collective-permute-start.15 = (bf16[1,448,256]{2,1,0:T(8,128)(2,1)S(1)}, bf16[1,448,256]{2,1,0:T(8,128)(2,1)S(1)}, u32[]{:S(2)}, u32[]{:S(2)}) collective-permute-start(bf16[1,448,256]{2,1,0:T(8,128)(2,1)S(1)} %get-tuple-element.54), channel_id=1, source_target_pairs={{0,4},{8,0},{16,8},{24,16},{28,24},{20,28},{12,20},{4,12},{1,5},{9... | collective-permute-start | bytes 688136 | tf_op jit(solution)/shard_map/ppermute | solution.py:364
  58.4 24.9 %collective-permute-start.21 = (bf16[8,2,448,256]{3,2,1,0:T(8,128)(2,1)S(1)}, bf16[8,2,448,256]{3,2,1,0:T(8,128)(2,1)S(1)}, u32[]{:S(2)}, u32[]{:S(2)}) collective-permute-start(bf16[8,2,448,256]{3,2,1,0:T(8,128)(2,1)S(1)} %get-tuple-element.70.w_ref), channel_id=1, source_target_pairs={{0,1},{1,0},{2,3},{3,2},{4,5},{5,4},{6,7},{7,6},{8,9},{9,8},{10,11... | collective-permute-start | bytes 11010056 | tf_op jit(solution)/shard_map/ppermute | solution.py:361
  58.5 8.7 %collective-permute-start.16 = (bf16[512,256]{1,0:T(8,128)(2,1)S(1)}, bf16[512,256]{1,0:T(8,128)(2,1)S(1)}, u32[]{:S(2)}, u32[]{:S(2)}) collective-permute-start(bf16[512,256]{1,0:T(8,128)(2,1)S(1)} %get-tuple-element.58.kv_ref), channel_id=1, source_target_pairs={{0,2},{1,3},{2,0},{3,1},{4,6},{5,7},{6,4},{7,5},{8,10},{9,11},{10,... | collective-permute-start | bytes 786440 | tf_op jit(solution)/shard_map/ppermute | solution.py:361
  71.9 7.9 %collective-permute-start.19 = (bf16[512,256]{1,0:T(8,128)(2,1)S(1)}, bf16[512,256]{1,0:T(8,128)(2,1)S(1)}, u32[]{:S(2)}, u32[]{:S(2)}) collective-permute-start(bf16[512,256]{1,0:T(8,128)(2,1)S(1)} %get-tuple-element.61.refs_0_), channel_id=1, source_target_pairs={{0,2},{1,3},{2,0},{3,1},{4,6},{5,7},{6,4},{7,5},{8,10},{9,11},{10,... | collective-permute-start | bytes 786440 | tf_op jit(solution)/shard_map/ppermute | solution.py:361
  79.9 3.4 %collective-permute-start.20 = (bf16[512,256]{1,0:T(8,128)(2,1)S(1)}, bf16[512,256]{1,0:T(8,128)(2,1)S(1)}, u32[]{:S(2)}, u32[]{:S(2)}) collective-permute-start(bf16[512,256]{1,0:T(8,128)(2,1)S(1)} %add_convert_fusion.7.g_ref.refs_8_), channel_id=1, source_target_pairs={{0,1},{1,0},{2,3},{3,2},{4,5},{5,4},{6,7},{7,6},{8,9},{9,8},{10,11... | collective-permute-start | bytes 786440 | tf_op jit(solution)/shard_map/ppermute | solution.py:361
  81.2 8.1 %collective-permute-start.23 = (bf16[1,448,256]{2,1,0:T(8,128)(2,1)S(1)}, bf16[1,448,256]{2,1,0:T(8,128)(2,1)S(1)}, u32[]{:S(2)}, u32[]{:S(2)}) collective-permute-start(bf16[1,448,256]{2,1,0:T(8,128)(2,1)S(1)} %get-tuple-element.77), channel_id=1, source_target_pairs={{0,8},{8,16},{16,24},{24,28},{28,20},{20,12},{12,4},{4,0},{1,9},{9... | collective-permute-start | bytes 688136 | tf_op jit(solution)/shard_map/ppermute | solution.py:364
  82.8 8.1 %collective-permute-start.27 = (bf16[1,448,256]{2,1,0:T(8,128)(2,1)S(1)}, bf16[1,448,256]{2,1,0:T(8,128)(2,1)S(1)}, u32[]{:S(2)}, u32[]{:S(2)}) collective-permute-start(bf16[1,448,256]{2,1,0:T(8,128)(2,1)S(1)} %get-tuple-element.81), channel_id=1, source_target_pairs={{0,4},{8,0},{16,8},{24,16},{28,24},{20,28},{12,20},{4,12},{1,5},{9... | collective-permute-start | bytes 688136 | tf_op jit(solution)/shard_map/ppermute | solution.py:364
  89.3 12.2 %collective-permute-start.24 = (bf16[2,448,256]{2,1,0:T(8,128)(2,1)S(1)}, bf16[2,448,256]{2,1,0:T(8,128)(2,1)S(1)}, u32[]{:S(2)}, u32[]{:S(2)}) collective-permute-start(bf16[2,448,256]{2,1,0:T(8,128)(2,1)S(1)} %add_convert_fusion.6), channel_id=1, source_target_pairs={{0,8},{8,16},{16,24},{24,28},{28,20},{20,12},{12,4},{4,0},{1,9},{9... | collective-permute-start | bytes 1376264 | tf_op jit(solution)/shard_map/ppermute | solution.py:364
  91.0 12.2 %collective-permute-start.28 = (bf16[2,448,256]{2,1,0:T(8,128)(2,1)S(1)}, bf16[2,448,256]{2,1,0:T(8,128)(2,1)S(1)}, u32[]{:S(2)}, u32[]{:S(2)}) collective-permute-start(bf16[2,448,256]{2,1,0:T(8,128)(2,1)S(1)} %add_convert_fusion.3), channel_id=1, source_target_pairs={{0,4},{8,0},{16,8},{24,16},{28,24},{20,28},{12,20},{4,12},{1,5},{9... | collective-permute-start | bytes 1376264 | tf_op jit(solution)/shard_map/ppermute | solution.py:364
  91.6 12.4 %collective-permute-start.17 = (bf16[2,128,896]{2,1,0:T(8,128)(2,1)S(1)}, bf16[2,128,896]{2,1,0:T(8,128)(2,1)S(1)}, u32[]{:S(2)}, u32[]{:S(2)}) collective-permute-start(bf16[2,128,896]{2,1,0:T(8,128)(2,1)S(1)} %get-tuple-element.63), channel_id=1, source_target_pairs={{0,1},{1,0},{2,3},{3,2},{4,5},{5,4},{6,7},{7,6},{8,9},{9,8},{10,11... | collective-permute-start | bytes 1376264 | tf_op jit(solution)/shard_map/ppermute | solution.py:361
  91.6 12.4 %collective-permute-start.18 = (bf16[2,128,896]{2,1,0:T(8,128)(2,1)S(1)}, bf16[2,128,896]{2,1,0:T(8,128)(2,1)S(1)}, u32[]{:S(2)}, u32[]{:S(2)}) collective-permute-start(bf16[2,128,896]{2,1,0:T(8,128)(2,1)S(1)} %get-tuple-element.65), channel_id=1, source_target_pairs={{0,1},{1,0},{2,3},{3,2},{4,5},{5,4},{6,7},{7,6},{8,9},{9,8},{10,11... | collective-permute-start | bytes 1376264 | tf_op jit(solution)/shard_map/ppermute | solution.py:361
  94.4 22.3 %collective-permute-start.22 = (bf16[128,3584]{1,0:T(8,128)(2,1)S(1)}, bf16[128,3584]{1,0:T(8,128)(2,1)S(1)}, u32[]{:S(2)}, u32[]{:S(2)}) collective-permute-start(bf16[128,3584]{1,0:T(8,128)(2,1)S(1)} %get-tuple-element.72.refs_9_), channel_id=1, source_target_pairs={{0,2},{1,3},{2,0},{3,1},{4,6},{5,7},{6,4},{7,5},{8,10},{9,11},{10,... | collective-permute-start | bytes 2752520 | tf_op jit(solution)/shard_map/ppermute | solution.py:361
  101.7 11.3 %collective-permute-start.25 = (bf16[2,448,256]{2,1,0:T(8,128)(2,1)S(1)}, bf16[2,448,256]{2,1,0:T(8,128)(2,1)S(1)}, u32[]{:S(2)}, u32[]{:S(2)}) collective-permute-start(bf16[2,448,256]{2,1,0:T(8,128)(2,1)S(1)} %add_convert_fusion.5), channel_id=1, source_target_pairs={{0,8},{8,16},{16,24},{24,28},{28,20},{20,12},{12,4},{4,0},{1,9},{9... | collective-permute-start | bytes 1376264 | tf_op jit(solution)/shard_map/ppermute | solution.py:364
  103.3 11.3 %collective-permute-start.29 = (bf16[2,448,256]{2,1,0:T(8,128)(2,1)S(1)}, bf16[2,448,256]{2,1,0:T(8,128)(2,1)S(1)}, u32[]{:S(2)}, u32[]{:S(2)}) collective-permute-start(bf16[2,448,256]{2,1,0:T(8,128)(2,1)S(1)} %add_convert_fusion.2), channel_id=1, source_target_pairs={{0,4},{8,0},{16,8},{24,16},{28,24},{20,28},{12,20},{4,12},{1,5},{9... | collective-permute-start | bytes 1376264 | tf_op jit(solution)/shard_map/ppermute | solution.py:364
  113.1 10.4 %collective-permute-start.26 = (bf16[2,448,256]{2,1,0:T(8,128)(2,1)S(1)}, bf16[2,448,256]{2,1,0:T(8,128)(2,1)S(1)}, u32[]{:S(2)}, u32[]{:S(2)}) collective-permute-start(bf16[2,448,256]{2,1,0:T(8,128)(2,1)S(1)} %add_convert_fusion.4), channel_id=1, source_target_pairs={{0,8},{8,16},{16,24},{24,28},{28,20},{20,12},{12,4},{4,0},{1,9},{9... | collective-permute-start | bytes 1376264 | tf_op jit(solution)/shard_map/ppermute | solution.py:364
  114.7 10.1 %collective-permute-start.30 = (bf16[2,448,256]{2,1,0:T(8,128)(2,1)S(1)}, bf16[2,448,256]{2,1,0:T(8,128)(2,1)S(1)}, u32[]{:S(2)}, u32[]{:S(2)}) collective-permute-start(bf16[2,448,256]{2,1,0:T(8,128)(2,1)S(1)} %add_convert_fusion.1), channel_id=1, source_target_pairs={{0,4},{8,0},{16,8},{24,16},{28,24},{20,28},{12,20},{4,12},{1,5},{9... | collective-permute-start | bytes 1376264 | tf_op jit(solution)/shard_map/ppermute | solution.py:364
